TPU v7x, 32 devices: a whole 2x2x4 slice. The times are simulated.
32 devices in a mesh: seq: 8 (over z, x), head: 4 (over y, core).
Axes of the slice: x: 2, y: 2, z: 4, core: 2. Of those that a mesh axis runs over, the one named last changes fastest.
Arguments:
- queries: bfloat16 [4096, 4096], P('seq', 'head'), may hold values from -6 to 6
- key_input: bfloat16 [4096, 4096], P('seq', 'head'), may hold values from -6 to 6
- value_input: bfloat16 [4096, 4096], P('seq', 'head'), may hold values from -40 to 40
- gate_input: bfloat16 [4096, 4096], P('seq', 'head'), may hold values from -8 to 8
- kv_state: float32 [32, 128, 128], P('head'), may hold values from -512 to 512
- norm_gain: float32 [4096], replicated, may hold values from 0.25 to 1.75
- out_weight: bfloat16 [4096, 4096], P('head', 'seq'), may hold values from -0.09375 to 0.09375
Outputs:
- output: bfloat16 [4096, 4096], P(('seq', 'head'))
All inputs are finite; a program needn't handle non-finite values.
Results may differ from a plain program's by a relative error of at most 0.02.
Values may be sent and summed in bfloat16 or wider, within the bound.
No kernel may reach another device: no remote copies, remote signals or barrier semaphores. Data moves between devices by JAX's collectives and lax.ppermute only.
A program may use at most 128 MiB of HBM per device.

v0:
```python
import jax
import jax.numpy as jnp
from jax import lax
from jax.sharding import PartitionSpec as P

DH = 128
BLOCK = 512


epsilon = 1e-05


def entering(value, axis, join, neutral):
    place = lax.axis_index(axis)
    gathered = lax.all_gather(value.astype(jnp.bfloat16), axis)
    state = jnp.zeros_like(value) + jnp.asarray(neutral, value.dtype)

    def one(turn, state):
        return join(state, lax.dynamic_index_in_dim(gathered, turn, 0, False).astype(value.dtype))

    return lax.fori_loop(0, place, one, state)


def add_states(earlier, later):
    return earlier + later


def gated_norm(attn_rows, gate_rows, gain_part, total_width, square_sum):
    attn_float = attn_rows.astype(jnp.float32)
    scale = lax.rsqrt(square_sum / total_width + epsilon)
    normed = attn_float * scale[:, None] * gain_part[None, :]
    return (normed * jax.nn.sigmoid(gate_rows.astype(jnp.float32))).astype(jnp.bfloat16)


def shards(queries, key_input, value_input, gate_input, kv_state, norm_gain, out_weight):
    tok_rows = queries.shape[0]
    local_width = queries.shape[1]
    local_heads = local_width // DH
    num_blocks = tok_rows // BLOCK
    block_shape = (num_blocks, BLOCK, local_heads, DH)
    q_blocks = queries.reshape(block_shape)
    k_blocks = key_input.reshape(block_shape)
    v_blocks = value_input.reshape(block_shape)
    block_states = jnp.einsum(
        "nthd,nthe->nhde", k_blocks, v_blocks, preferred_element_type=jnp.float32
    )
    own_total = jnp.sum(block_states, axis=0)
    prefix = entering(own_total, "seq", add_states, jnp.zeros_like(own_total))
    start_state = kv_state + prefix
    running = jnp.cumsum(block_states, axis=0) - block_states
    before = start_state[None] + running
    carried_part = jnp.einsum(
        "nthd,nhde->nthe", q_blocks.astype(jnp.float32), before, precision=lax.Precision.HIGHEST
    )
    scores = jnp.einsum("nthd,nshd->nhts", q_blocks, k_blocks, preferred_element_type=jnp.float32)
    causal = jnp.arange(BLOCK)[:, None] >= jnp.arange(BLOCK)[None, :]
    weights = jnp.where(causal[None, None], scores, 0.0).astype(jnp.bfloat16)
    inner_part = jnp.einsum(
        "nhts,nshe->nthe", weights, v_blocks, preferred_element_type=jnp.float32
    )
    attn = (carried_part + inner_part).astype(jnp.bfloat16).reshape(tok_rows, local_width)
    total_width = local_width * lax.axis_size("head")
    tok_attn, tok_gate = (
        lax.all_to_all(attn, "head", split_axis=0, concat_axis=1, tiled=True),
        lax.all_to_all(gate_input, "head", split_axis=0, concat_axis=1, tiled=True),
    )
    tok_float = tok_attn.astype(jnp.float32)
    normed = gated_norm(
        tok_attn, tok_gate, norm_gain, total_width, jnp.sum(tok_float * tok_float, axis=1)
    )
    hidden = lax.all_to_all(normed, "head", split_axis=1, concat_axis=0, tiled=True)
    terms = jnp.dot(
        hidden,
        lax.all_gather(out_weight, "seq", axis=1, tiled=True),
        preferred_element_type=jnp.float32,
    )
    return lax.psum_scatter(terms.astype(jnp.bfloat16), "head", scatter_dimension=0, tiled=True)


def solution(mesh):
    in_specs = (
        P("seq", "head"),
        P("seq", "head"),
        P("seq", "head"),
        P("seq", "head"),
        P("head", None, None),
        P(),
        P("head", "seq"),
    )
    out_specs = P(("seq", "head"), None)
    return jax.shard_map(shards, mesh=mesh, in_specs=in_specs, out_specs=out_specs, check_vma=False)
```

profile of v0, /device:TPU:0, one launch (start us, length us, event | category | flops | bytes accessed | tf_op | source)
XLA Modules:
  0.0 246.4 jit_solution(3156137362572215742)
XLA Ops:
  6.5 0.0 copy-start
  6.5 0.0 all-gather.6.cloned.1.call-start
  6.5 2.9 %fusion.34 = (bf16[8,128,128]{2,1,0:T(8,128)(2,1)}, f32[8,128,128]{2,1,0:T(8,128)S(1)}) fusion(bf16[512,1024]{1,0:T(8,128)(2,1)} %param.11, bf16[512,1024]{1,0:T(8,128)(2,1)} %param.10), kind=kOutput, calls=%fused_computation.37 | convolution fusion | flops 134348800 | bytes 2883584 | tf_op jit(solution)/shard_map/nthd,nthe->nhde/dot_general | solution.py:44
  9.4 0.0 all-gather.6.cloned.1.call-update
  9.4 0.0 all-gather.4.cloned.1.call-start
  9.5 0.7 all-gather.4.cloned.1.call-update
  10.2 0.1 iota_compare_fusion
  10.3 51.3 %all-gather.6.cloned.1.call-done = bf16[64,128,128]{2,1,0:T(8,128)(2,1)} async-done(((bf16[8,128,128]{2,1,0:T(8,128)(2,1)}), bf16[64,128,128]{2,1,0:T(8,128)(2,1)}) %all-gather.6.cloned.1.call-update) | async-done | bytes 2097168 | tf_op jit(solution)/shard_map/all_gather | solution.py:15
  61.6 0.0 copy-start.2
  61.7 0.0 copy-done
  61.7 1.0 copy-done.2
  62.7 2.4 fusion.13
  65.1 4.8 %fusion.10 = bf16[1,512,8,128]{1,3,2,0:T(8,128)(2,1)S(1)} fusion(f32[8,128,512]{2,1,0:T(8,128)} %fusion.13, pred[512,512]{1,0:T(8,128)(4,1)S(1)} %iota_compare_fusion, bf16[512,1024]{1,0:T(8,128)(2,1)S(1)} %copy-done, bf16[512,1024]{1,0:T(8,128)(2,1)} %param.11, bf16[512,1024]{1,0:T(8,128)(2,1)} %param.10), kind=kOutput, calls=%fused_computation.15 | convolution fusion | flops 1078984704 | bytes 6553600 | tf_op jit(solution)/shard_map/nhts,nshe->nthe/dot_general | solution.py:58
  69.9 0.3 all_to_all.32
  70.2 0.0 copy-start.1
  70.2 1.2 copy.40
  71.4 3.5 %all-to-all-start = ((bf16[4,128,1024]{1,2,0:T(8,128)(2,1)}), bf16[4,128,1024]{1,2,0:T(8,128)(2,1)S(1)}, u32[]{:S(2)}, u32[]{:S(2)}) async-start(bf16[4,128,1024]{1,2,0:T(8,128)(2,1)} %copy.40), calls=%async_computation | async-start | bytes 2097152 | tf_op jit(solution)/shard_map/all_to_all | solution.py:64
  75.0 0.0 copy-done.1
  75.0 0.0 copy-start.3
  75.0 1.3 copy.41
  76.3 13.1 %all-to-all-done = bf16[4,128,1024]{1,2,0:T(8,128)(2,1)S(1)} async-done(((bf16[4,128,1024]{1,2,0:T(8,128)(2,1)}), bf16[4,128,1024]{1,2,0:T(8,128)(2,1)S(1)}, u32[]{:S(2)}, u32[]{:S(2)}) %all-to-all-start) | async-done | bytes 1048608 | tf_op jit(solution)/shard_map/all_to_all | solution.py:64
  89.4 3.5 %all-to-all-start.1 = ((bf16[4,128,1024]{1,2,0:T(8,128)(2,1)}), bf16[4,128,1024]{1,2,0:T(8,128)(2,1)S(1)}, u32[]{:S(2)}, u32[]{:S(2)}) async-start(bf16[4,128,1024]{1,2,0:T(8,128)(2,1)} %copy.41), calls=%async_computation.1 | async-start | bytes 2097152 | tf_op jit(solution)/shard_map/all_to_all | solution.py:65
  92.9 0.0 reduce-scatter.2.cloned.1.call-start
  93.0 0.0 copy-done.3
  93.0 0.6 fusion.5
  93.6 13.8 %all-to-all-done.1 = bf16[4,128,1024]{1,2,0:T(8,128)(2,1)S(1)} async-done(((bf16[4,128,1024]{1,2,0:T(8,128)(2,1)}), bf16[4,128,1024]{1,2,0:T(8,128)(2,1)S(1)}, u32[]{:S(2)}, u32[]{:S(2)}) %all-to-all-start.1) | async-done | bytes 1048608 | tf_op jit(solution)/shard_map/all_to_all | solution.py:65
  107.3 0.8 fusion.21
  108.1 16.9 %all_to_all.42 = bf16[128,4,1024]{0,2,1:T(8,128)(2,1)S(1)} all-to-all(bf16[128,4,1024]{0,2,1:T(8,128)(2,1)S(1)} %fusion.21), channel_id=1, replica_groups=mesh['seq'=8,'head'=4] {'head'}, dimensions={1} | all-to-all | bytes 2097152 | tf_op jit(solution)/shard_map/all_to_all | solution.py:71
  125.0 0.5 copy.42
  125.5 62.0 %all-gather.4.cloned.1.call-done = bf16[1024,4096]{1,0:T(8,128)(2,1)} async-done(((bf16[1024,512]{1,0:T(8,128)(2,1)}), bf16[1024,4096]{1,0:T(8,128)(2,1)}) %all-gather.4.cloned.1.call-update) | async-done | bytes 8388624 | tf_op jit(solution)/shard_map/all_gather | solution.py:74
  187.5 9.4 %convolution_convert_fusion = bf16[512,4096]{1,0:T(8,128)(2,1)} fusion(bf16[512,1024]{1,0:T(8,128)(2,1)S(1)} %bitcast.73, bf16[1024,4096]{1,0:T(8,128)(2,1)} %all-gather.4.cloned.1.call-done), kind=kOutput, calls=%fused_computation.2 | convolution fusion | flops 4297064448 | bytes 13631488 | tf_op jit(solution)/shard_map/dot_general | solution.py:72
  196.9 0.0 reduce-scatter.2.cloned.1.call-update
  197.0 42.9 %reduce-scatter.2.cloned.1.call-done = bf16[128,4096]{1,0:T(8,128)(2,1)} async-done(((bf16[512,4096]{1,0:T(8,128)(2,1)}), bf16[128,4096]{1,0:T(8,128)(2,1)}) %reduce-scatter.2.cloned.1.call-update) | async-done | bytes 1048592 | tf_op jit(solution)/shard_map/reduce_scatter | solution.py:77
  (4 shorter events, 0.1 us)
Async XLA Ops:
  6.5 55.1 %copy-start = (bf16[512,1024]{1,0:T(8,128)(2,1)S(1)}, bf16[512,1024]{1,0:T(8,128)(2,1)}, u32[]{:S(2)}) copy-start(bf16[512,1024]{1,0:T(8,128)(2,1)} %param.9) | copy-start | bytes 3145732
  6.5 55.0 %all-gather.6.cloned.1.call-start = ((), (), s32[]{:S(2)}) async-start(), calls=%async_computation.6 | async-start | bytes 2359296 | tf_op jit(solution)/shard_map/all_gather | solution.py:15
  9.4 178.1 %all-gather.4.cloned.1.call-start = ((), (), s32[]{:S(2)}) async-start(), calls=%async_computation.4 | async-start | bytes 9437184 | tf_op jit(solution)/shard_map/all_gather | solution.py:74
  61.6 1.0 copy-start.2
  70.2 4.8 %copy-start.1 = (bf16[512,1024]{1,0:T(8,128)(2,1)S(1)}, bf16[512,1024]{1,0:T(8,128)(2,1)}, u32[]{:S(2)}) copy-start(bf16[512,1024]{1,0:T(8,128)(2,1)} %param.12) | copy-start | bytes 3145732
  71.4 18.0 %all-to-all-start = ((bf16[4,128,1024]{1,2,0:T(8,128)(2,1)}), bf16[4,128,1024]{1,2,0:T(8,128)(2,1)S(1)}, u32[]{:S(2)}, u32[]{:S(2)}) async-start(bf16[4,128,1024]{1,2,0:T(8,128)(2,1)} %copy.40), calls=%async_computation | async-start | bytes 2097152 | tf_op jit(solution)/shard_map/all_to_all | solution.py:64
  75.0 18.0 %copy-start.3 = (f32[4096]{0:T(1024)S(1)}, f32[4096]{0:T(1024)}, u32[]{:S(2)}) copy-start(f32[4096]{0:T(1024)} %param.14) | copy-start | bytes 49156
  89.4 18.0 %all-to-all-start.1 = ((bf16[4,128,1024]{1,2,0:T(8,128)(2,1)}), bf16[4,128,1024]{1,2,0:T(8,128)(2,1)S(1)}, u32[]{:S(2)}, u32[]{:S(2)}) async-start(bf16[4,128,1024]{1,2,0:T(8,128)(2,1)} %copy.41), calls=%async_computation.1 | async-start | bytes 2097152 | tf_op jit(solution)/shard_map/all_to_all | solution.py:65
  92.9 146.9 %reduce-scatter.2.cloned.1.call-start = ((), (), s32[]{:S(2)}) async-start(), calls=%async_computation.5 | async-start | bytes 5242880 | tf_op jit(solution)/shard_map/reduce_scatter | solution.py:77
Sparse Core Ops, SparseCore 0:
  9.6 51.9 all-gather.5
  63.6 123.8 all-gather.3
  197.1 42.7 reduce-scatter.1
where the time goes:
time: 247 us; the launch traced here: 246 us
  waiting for transfers between devices  184 us (74%)
  matrix products  19.5 us (8%)
  blocking collectives  16.9 us (7%)
  between operations  13.2 us (5%)
  starting transfers between devices  7.12 us (3%)
  local copies, waits for them, and re-layouts  4.4 us (2%)
    all_gather x1, waiting for transfers between devices, shards(): lax.all_gather(out_weight, 'seq', axis=1, tiled=True)  62 us
    all_gather x1, waiting for transfers between devices, entering(): gathered = lax.all_gather(value.astype(jnp.bfloat16), axis)  51.3 us
    reduce_scatter x1, waiting for transfers between devices, shards(): lax.psum_scatter(terms.astype(jnp.bfloat16), 'head', scatter_dimension=0,...  42.9 us
    all_to_all x1, blocking collectives, shards(): lax.all_to_all(normed, 'head', split_axis=1, concat_axis=0, tiled=True)  16.9 us
    all_to_all x1, waiting for transfers between devices, shards(): lax.all_to_all(gate_input, 'head', split_axis=0, concat_axis=1, tiled=True)  13.8 us
    all_to_all x1, waiting for transfers between devices, shards(): lax.all_to_all(attn, 'head', split_axis=0, concat_axis=1, tiled=True)  13.1 us
    dot_general x1, matrix products, shards(): jnp.dot(hidden, lax.all_gather(out_weight, 'seq', axis=1, tiled=True), pr...  9.4 us
  transfers between devices with their start and end apart: 5, of which 5 were waited for; matrix products, arithmetic and copies ran while one was open for 5% of the time, Pallas kernels for 0%

commit v1 on v0

v1 whole, which is shorter than its diff:
```python
import jax
import jax.numpy as jnp
from jax import lax
from jax.sharding import PartitionSpec as P

DH = 128
BLOCK = 512
LINE = 4


epsilon = 1e-05


def line_pairs(n_seq, hops):
    inner = n_seq // LINE
    return [(a * inner + i, b * inner + i) for a, b in hops for i in range(inner)]


def turn_pairs(n_seq, turn):
    inner = n_seq // LINE
    return [(a * inner + i, a * inner + (i + turn) % inner) for a in range(LINE) for i in range(inner)]


def flip_pairs(n_head, bit):
    return [(h, h ^ bit) for h in range(n_head)]


SWAP_OUTER = [(0, 1), (1, 0), (2, 3), (3, 2)]
SWAP_MIDDLE = [(1, 2), (2, 1)]
TO_ENDS = [(1, 0), (2, 3)]


def state_prefix(own_total, n_seq, place):
    inner = n_seq // LINE
    i = place % inner
    shape = own_total.shape
    parts = own_total.reshape(inner, -1, DH)
    parts_low = parts.astype(jnp.bfloat16)
    from_member = [lax.dynamic_index_in_dim(parts, i, 0, False)]
    members = [i]
    for turn in range(1, inner):
        sent = lax.dynamic_index_in_dim(parts_low, (i + turn) % inner, 0, False)
        got = lax.ppermute(sent, "seq", turn_pairs(n_seq, turn))
        from_member.append(got.astype(jnp.float32))
        members.append((i - turn) % inner)
    group_sum = sum(from_member)
    from_left = lax.ppermute(group_sum.astype(jnp.bfloat16), "seq", line_pairs(n_seq, [(0, 1), (2, 3)]))
    from_left = from_left.astype(jnp.float32)
    pair_sum = (group_sum + from_left).astype(jnp.bfloat16)
    near = lax.ppermute(pair_sum, "seq", line_pairs(n_seq, [(1, 2)]))
    far = lax.ppermute(pair_sum, "seq", line_pairs(n_seq, [(1, 3)]))
    entering = from_left + near.astype(jnp.float32) + far.astype(jnp.float32)

    def before(member):
        total = entering
        for value, owner in zip(from_member, members):
            total = total + jnp.where(owner < member, value, 0.0)
        return total

    result = jnp.zeros_like(parts)
    result = lax.dynamic_update_index_in_dim(result, before(i), i, 0)
    for turn in range(1, inner):
        sent = before((i + turn) % inner).astype(jnp.bfloat16)
        got = lax.ppermute(sent, "seq", turn_pairs(n_seq, turn))
        result = lax.dynamic_update_index_in_dim(result, got.astype(jnp.float32), (i - turn) % inner, 0)
    return result.reshape(shape)


def shards(queries, key_input, value_input, gate_input, kv_state, norm_gain, out_weight):
    n_seq, n_head = lax.axis_size("seq"), lax.axis_size("head")
    inner = n_seq // LINE
    place, h = lax.axis_index("seq"), lax.axis_index("head")
    z, i = place // inner, place % inner
    tok_rows, local_width = queries.shape
    local_heads = local_width // DH
    num_blocks = tok_rows // BLOCK
    total_width = local_width * n_head

    def along(value, hops):
        return lax.ppermute(value, "seq", line_pairs(n_seq, hops))

    w_pair = along(out_weight, SWAP_OUTER)
    w_mid1 = along(out_weight, SWAP_MIDDLE)
    w_mid2 = along(w_pair, SWAP_MIDDLE)
    w_end1 = along(w_mid1, TO_ENDS)
    w_end2 = along(w_mid2, TO_ENDS)
    is_end = (z == 0) | (z == LINE - 1)
    weights = [
        out_weight,
        w_pair,
        jnp.where(is_end, w_end1, w_mid1),
        jnp.where(is_end, w_end2, w_mid2),
    ]
    low = z < 2
    weight_from = [z, z ^ 1, jnp.where(low, 2, 1), jnp.where(low, 3, 0)]

    block_shape = (num_blocks, BLOCK, local_heads, DH)
    q_blocks = queries.reshape(block_shape)
    k_blocks = key_input.reshape(block_shape)
    v_blocks = value_input.reshape(block_shape)
    block_states = jnp.einsum(
        "nthd,nthe->nhde", k_blocks, v_blocks, preferred_element_type=jnp.float32
    )
    own_total = jnp.sum(block_states, axis=0)
    start_state = kv_state + state_prefix(own_total, n_seq, place)
    running = jnp.cumsum(block_states, axis=0) - block_states
    before = start_state[None] + running
    carried_part = jnp.einsum(
        "nthd,nhde->nthe", q_blocks.astype(jnp.float32), before, precision=lax.Precision.HIGHEST
    )
    scores = jnp.einsum("nthd,nshd->nhts", q_blocks, k_blocks, preferred_element_type=jnp.float32)
    causal = jnp.arange(BLOCK)[:, None] >= jnp.arange(BLOCK)[None, :]
    masked = jnp.where(causal[None, None], scores, 0.0).astype(jnp.bfloat16)
    inner_part = jnp.einsum(
        "nhts,nshe->nthe", masked, v_blocks, preferred_element_type=jnp.float32
    )
    attn = (carried_part + inner_part).astype(jnp.bfloat16).reshape(tok_rows, local_width)
    attn_float = attn.astype(jnp.float32)

    squares = jnp.sum(attn_float * attn_float, axis=1)
    bit = 1
    while bit < n_head:
        squares = squares + lax.ppermute(squares, "head", flip_pairs(n_head, bit))
        bit *= 2
    out_rows = tok_rows // n_head
    own_squares = lax.dynamic_slice_in_dim(squares, h * out_rows, out_rows, 0)
    scale = lax.rsqrt(own_squares / total_width + epsilon)

    gain_part = lax.dynamic_slice_in_dim(norm_gain, h * local_width, local_width, 0)
    gated = attn_float * gain_part[None, :] * jax.nn.sigmoid(gate_input.astype(jnp.float32))
    gated = gated.astype(jnp.bfloat16).reshape(n_head, out_rows, local_width)
    bits = n_head.bit_length() - 1
    order = [int(format(j, "b").zfill(bits)[::-1], 2) for j in range(n_head)] if bits else [0]
    hidden = jnp.concatenate(
        [lax.dynamic_index_in_dim(gated, j ^ h, 0, False) for j in order], axis=0
    )
    hiddens = [hidden]
    for turn in range(1, inner):
        hiddens.append(lax.ppermute(hidden, "seq", turn_pairs(n_seq, turn)))

    def project(rows, weight):
        return jnp.dot(rows, weight, preferred_element_type=jnp.float32)

    width = out_weight.shape[1]
    output = jnp.zeros((out_rows, width * n_seq), jnp.bfloat16)
    for weight, owner in zip(weights, weight_from):
        half = tok_rows // 2
        sent = jnp.stack([project(rows[half:], weight).astype(jnp.bfloat16) for rows in hiddens])
        kept = jnp.stack([project(rows[:half], weight) for rows in hiddens])
        bit = 1
        while bit < n_head:
            kept = kept + lax.ppermute(sent, "head", flip_pairs(n_head, bit)).astype(jnp.float32)
            half = half // 2
            bit *= 2
            if bit < n_head:
                sent = kept[:, half:].astype(jnp.bfloat16)
                kept = kept[:, :half]
        pieces = [(kept[0], i)]
        for turn in range(1, inner):
            got = lax.ppermute(kept[turn].astype(jnp.bfloat16), "seq", turn_pairs(n_seq, -turn))
            pieces.append((got, (i + turn) % inner))
        for piece, member in pieces:
            scaled = (piece.astype(jnp.float32) * scale[:, None]).astype(jnp.bfloat16)
            output = lax.dynamic_update_slice_in_dim(
                output, scaled, (owner * inner + member) * width, 1
            )
    return output


def solution(mesh):
    in_specs = (
        P("seq", "head"),
        P("seq", "head"),
        P("seq", "head"),
        P("seq", "head"),
        P("head", None, None),
        P(),
        P("head", "seq"),
    )
    out_specs = P(("seq", "head"), None)
    return jax.shard_map(shards, mesh=mesh, in_specs=in_specs, out_specs=out_specs, check_vma=False)
```

time: 247 us -> 133 us (0.54)
  waiting for transfers between devices: 184 us -> 60 us
  starting transfers between devices: 7.12 us -> 33.9 us
  blocking collectives: 16.9 us -> 0 us
  between operations: 13.2 us -> 0.68 us
  other arithmetic: 1.4 us -> 9.23 us
  matrix products: 19.5 us -> 22.9 us
    all_gather x2 -> x0, waiting for transfers between devices: 113 us -> none  [the longest x1 62 us: shards(): lax.all_gather(out_weight, 'seq', axis=1, tiled=True)]
    ppermute x0 -> x25, waiting for transfers between devices: none -> 60 us  [the longest x8 17.4 us: shards(): lax.ppermute(sent, 'head', flip_pairs(n_head, bit)).astype(jnp.float32)]
    reduce_scatter x1 -> x0, waiting for transfers between devices: 42.9 us -> none  [shards(): lax.psum_scatter(terms.astype(jnp.bfloat16), 'head', scatter_dimension=0,...]
    ppermute x0 -> x25, starting transfers between devices: none -> 33.9 us  [the longest x5 11.4 us: along(): return lax.ppermute(value, 'seq', line_pairs(n_seq, hops))]
    all_to_all x2 -> x0, waiting for transfers between devices: 26.9 us -> none  [the longest x1 13.8 us: shards(): lax.all_to_all(gate_input, 'head', split_axis=0, concat_axis=1, tiled=True)]
    all_to_all x1 -> x0, blocking collectives: 16.9 us -> none  [shards(): lax.all_to_all(normed, 'head', split_axis=1, concat_axis=0, tiled=True)]
    all_to_all x2 -> x0, starting transfers between devices: 7.04 us -> none  [the longest x1 3.52 us: shards(): lax.all_to_all(attn, 'head', split_axis=0, concat_axis=1, tiled=True)]
    dot_general x2 -> x17, matrix products: 14.2 us -> 18.8 us  [the longest x16 13 us: project(): return jnp.dot(rows, weight, preferred_element_type=jnp.float32)]
  transfers between devices with their start and end apart: 5 -> 25, of which waited for: 5 -> 15; matrix products, arithmetic and copies ran while one was open for 5% -> 23% of each run, Pallas kernels for 0% -> 0%
where the time goes in v1:
time: 133 us
  waiting for transfers between devices  60 us (45%)
  starting transfers between devices  33.9 us (25%)
  matrix products  22.9 us (17%)
  other arithmetic  9.23 us (7%)
  local copies, waits for them, and re-layouts  6.09 us (5%)
    ppermute x8, waiting for transfers between devices, shards(): lax.ppermute(sent, 'head', flip_pairs(n_head, bit)).astype(jnp.float32)  17.4 us
    ppermute x5, waiting for transfers between devices, along(): return lax.ppermute(value, 'seq', line_pairs(n_seq, hops))  14.8 us
    dot_general x16, matrix products, project(): return jnp.dot(rows, weight, preferred_element_type=jnp.float32)  13 us
    ppermute x5, starting transfers between devices, along(): return lax.ppermute(value, 'seq', line_pairs(n_seq, hops))  11.4 us
    ppermute x1, waiting for transfers between devices, shards(): hiddens.append(lax.ppermute(hidden, 'seq', turn_pairs(n_seq, turn)))  9.56 us
    ppermute x4, waiting for transfers between devices, shards(): lax.ppermute(kept[turn].astype(jnp.bfloat16), 'seq', turn_pairs(n_seq, -t...  8.21 us
    ppermute x8, starting transfers between devices, shards(): lax.ppermute(sent, 'head', flip_pairs(n_head, bit)).astype(jnp.float32)  6.1 us
    ppermute x2, waiting for transfers between devices, state_prefix(): got = lax.ppermute(sent, 'seq', turn_pairs(n_seq, turn))  5.95 us
  transfers between devices with their start and end apart: 25, of which 15 were waited for; matrix products, arithmetic and copies ran while one was open for 23% of the time, Pallas kernels for 0%

profile of v1, /device:TPU:0, one launch (start us, length us, event | category | flops | bytes accessed | tf_op | source)
XLA Modules:
  0.0 132.8 jit_solution(550277959436357395)
XLA Ops:
  0.0 1.6 %copy.15 = bf16[512,1024]{0,1:T(8,128)(2,1)S(1)} copy(bf16[512,1024]{1,0:T(8,128)(2,1)} %param.8) | data formatting | bytes 2097152 | tf_op jit(solution)/shard_map/reshape
  1.7 1.3 copy.16
  3.0 1.6 %fusion.66 = f32[8,128,128]{2,1,0:T(8,128)S(1)} fusion(bf16[512,8,128]{0,2,1:T(8,128)(2,1)S(1)} %bitcast.157, bf16[512,8,128]{0,2,1:T(8,128)(2,1)} %bitcast.159), kind=kOutput, calls=%fused_computation.128 | convolution fusion | flops 134217728 | bytes 2621440 | tf_op jit(solution)/shard_map/nthd,nthe->nhde/dot_general | solution.py:101
  4.7 3.0 %collective-permute-start = (bf16[512,128]{1,0:T(8,128)(2,1)S(1)}, bf16[512,128]{1,0:T(8,128)(2,1)S(1)}, u32[]{:S(2)}, u32[]{:S(2)}) collective-permute-start(bf16[512,128]{1,0:T(8,128)(2,1)S(1)} %fusion.54), channel_id=1, source_target_pairs={{0,4},{4,0},{8,12},{12,8},{16,20},{20,16},{24,28},{28,24},{1,5},{5... | collective-permute-start | bytes 393224 | tf_op jit(solution)/shard_map/ppermute | solution.py:43
  7.7 3.5 %collective-permute-done = bf16[512,128]{1,0:T(8,128)(2,1)S(1)} collective-permute-done((bf16[512,128]{1,0:T(8,128)(2,1)S(1)}, bf16[512,128]{1,0:T(8,128)(2,1)S(1)}, u32[]{:S(2)}, u32[]{:S(2)}) %collective-permute-start) | collective-permute-done | bytes 131104 | tf_op jit(solution)/shard_map/ppermute | solution.py:43
  11.2 3.7 %collective-permute-start.1 = (bf16[512,128]{1,0:T(8,128)(2,1)S(1)}, bf16[512,128]{1,0:T(8,128)(2,1)S(1)}, u32[]{:S(2)}, u32[]{:S(2)}) collective-permute-start(bf16[512,128]{1,0:T(8,128)(2,1)S(1)} %fusion.49), channel_id=1, source_target_pairs={{0,8},{4,12},{16,24},{20,28},{1,9},{5,13},{17,25},{21,29},{2,10},{... | collective-permute-start | bytes 393224 | tf_op jit(solution)/shard_map/ppermute | solution.py:47
  15.0 2.5 %collective-permute-done.1 = bf16[512,128]{1,0:T(8,128)(2,1)S(1)} collective-permute-done((bf16[512,128]{1,0:T(8,128)(2,1)S(1)}, bf16[512,128]{1,0:T(8,128)(2,1)S(1)}, u32[]{:S(2)}, u32[]{:S(2)}) %collective-permute-start.1) | collective-permute-done | bytes 131104 | tf_op jit(solution)/shard_map/ppermute | solution.py:47
  17.5 0.7 fusion.33
  18.2 0.7 collective-permute-start.2
  18.8 1.3 collective-permute-start.3
  20.1 6.3 %collective-permute-start.11 = (bf16[1024,512]{1,0:T(8,128)(2,1)}, bf16[1024,512]{1,0:T(8,128)(2,1)}, u32[]{:S(2)}, u32[]{:S(2)}) collective-permute-start(bf16[1024,512]{1,0:T(8,128)(2,1)} %param.13), channel_id=1, source_target_pairs={{0,8},{4,12},{8,0},{12,4},{16,24},{20,28},{24,16},{28,20},{1,9},{5... | collective-permute-start | bytes 3145736 | tf_op jit(solution)/shard_map/ppermute | solution.py:80
  26.4 1.6 %collective-permute-start.15 = (bf16[1024,512]{1,0:T(8,128)(2,1)}, bf16[1024,512]{1,0:T(8,128)(2,1)}, u32[]{:S(2)}, u32[]{:S(2)}) collective-permute-start(bf16[1024,512]{1,0:T(8,128)(2,1)} %param.13), channel_id=1, source_target_pairs={{8,16},{12,20},{16,8},{20,12},{9,17},{13,21},{17,9},{21,13},{10,18... | collective-permute-start | bytes 3145736 | tf_op jit(solution)/shard_map/ppermute | solution.py:80
  28.1 0.8 iota_compare_fusion
  28.9 1.0 fusion.39
  29.9 1.6 %collective-permute-start.4 = (bf16[512,128]{1,0:T(8,128)(2,1)S(1)}, bf16[512,128]{1,0:T(8,128)(2,1)S(1)}, u32[]{:S(2)}, u32[]{:S(2)}) collective-permute-start(bf16[512,128]{1,0:T(8,128)(2,1)S(1)} %fusion.39), channel_id=1, source_target_pairs={{0,4},{4,0},{8,12},{12,8},{16,20},{20,16},{24,28},{28,24},{1,5},{5... | collective-permute-start | bytes 393224 | tf_op jit(solution)/shard_map/ppermute | solution.py:64
  31.5 1.0 fusion.37
  32.5 2.5 %collective-permute-done.4 = bf16[512,128]{1,0:T(8,128)(2,1)S(1)} collective-permute-done((bf16[512,128]{1,0:T(8,128)(2,1)S(1)}, bf16[512,128]{1,0:T(8,128)(2,1)S(1)}, u32[]{:S(2)}, u32[]{:S(2)}) %collective-permute-start.4) | collective-permute-done | bytes 131104 | tf_op jit(solution)/shard_map/ppermute | solution.py:64
  35.0 2.4 %fusion.17 = f32[8,128,512]{2,1,0:T(8,128)} fusion(f32[8,128,128]{2,1,0:T(8,128)S(1)} %fusion.66, f32[8,128,128]{2,1,0:T(8,128)S(1)} %copy-done.10, f32[8,128,128]{2,1,0:T(8,128)S(1)} %bitcast.161, bf16[512,1024]{1,0:T(8,128)(2,1)S(1)} %copy-done), kind=kOutput, calls=%fused_computation.35 | convolution fusion | flops 805699584 | bytes 4718592 | tf_op jit(solution)/shard_map/nthd,nhde->nthe/dot_general | solution.py:108
  37.4 5.9 %multiply_reduce_fusion = (f32[512]{0:T(512)S(1)}, f32[8,128,512]{2,1,0:T(8,128)}) fusion(f32[8,128,512]{2,1,0:T(8,128)} %fusion.17, bf16[512,8,128]{0,2,1:T(8,128)(2,1)} %bitcast.160, pred[512,512]{1,0:T(8,128)(4,1)S(1)} %copy-done.11, bf16[512,8,128]{0,2,1:T(8,128)(2,1)S(1)} %bitcast.158, bf16[512,1024]{1,0:T(8,128)(2,1)S(1)} %copy-done), kind=kOutput, calls=%fused_computation.7 | convolution fusion | flops 1080557056 | bytes 7604224 | tf_op jit(solution)/shard_map/nhts,nshe->nthe/dot_general | solution.py:114
  43.3 1.9 %copy.13 = f32[512,1024]{1,0:T(8,128)S(1)} copy(f32[512,1024]{0,1:T(8,128)} %bitcast.162) | data formatting | bytes 4194304 | tf_op jit(solution)/shard_map/convert_element_type | solution.py:118
  45.2 1.8 %multiply_convert_fusion = bf16[512,1024]{1,0:T(8,128)(2,1)S(1)} fusion(bf16[512,1024]{1,0:T(8,128)(2,1)} %param.10, f32[512,1024]{1,0:T(8,128)S(1)} %copy.13, f32[1024]{0:T(1024)S(1)} %dynamic-slice-done), kind=kLoop, calls=%fused_computation.8 | loop fusion | flops 3670016 | bytes 4198400 | tf_op jit(solution)/shard_map/convert_element_type | solution.py:131
  47.2 0.7 copy-done.4
  47.9 1.0 pad_maximum_fusion
  48.9 1.5 %collective-permute-start.5 = (bf16[512,1024]{1,0:T(8,128)(2,1)}, bf16[512,1024]{1,0:T(8,128)(2,1)S(1)}, u32[]{:S(2)}, u32[]{:S(2)}) collective-permute-start(bf16[512,1024]{1,0:T(8,128)(2,1)} %pad_maximum_fusion), channel_id=1, source_target_pairs={{0,4},{4,0},{8,12},{12,8},{16,20},{20,16},{24,28},{28,24},{1,5},{5... | collective-permute-start | bytes 3145736 | tf_op jit(solution)/shard_map/ppermute | solution.py:139
  50.4 1.5 %fusion.7 = bf16[1,256,512]{2,1,0:T(8,128)(2,1)S(1)} fusion(bf16[1024,512]{1,0:T(8,128)(2,1)S(1)} %copy-done.2, bf16[128,1024]{1,0:T(8,128)(2,1)} %copy-done.6, bf16[128,1024]{1,0:T(8,128)(2,1)} %copy-done.8), kind=kOutput, calls=%fused_computation.26 | convolution fusion | flops 269615104 | bytes 1835008 | tf_op jit(solution)/shard_map/dot_general | solution.py:142
  52.0 1.6 %collective-permute-start.9 = (f32[512]{0:T(512)S(1)}, f32[512]{0:T(512)S(1)}, u32[]{:S(2)}, u32[]{:S(2)}) collective-permute-start(f32[512]{0:T(512)S(1)} %add.207), channel_id=1, source_target_pairs={{0,2},{1,3},{2,0},{3,1},{4,6},{5,7},{6,4},{7,5},{8,10},{9,11},{10,... | collective-permute-start | bytes 6152 | tf_op jit(solution)/shard_map/ppermute | solution.py:123
  53.6 0.4 convolution_bitcast_fusion.7
  54.0 1.6 %collective-permute-done.9 = f32[512]{0:T(512)S(1)} collective-permute-done((f32[512]{0:T(512)S(1)}, f32[512]{0:T(512)S(1)}, u32[]{:S(2)}, u32[]{:S(2)}) %collective-permute-start.9) | collective-permute-done | bytes 2080 | tf_op jit(solution)/shard_map/ppermute | solution.py:123
  55.7 0.7 collective-permute-start.20
  56.5 1.3 collective-permute-start.16
  57.8 1.7 %fusion.9 = bf16[1,256,512]{2,1,0:T(8,128)(2,1)S(1)} fusion(bf16[1024,512]{1,0:T(8,128)(2,1)} %collective-permute-done.11, bf16[128,1024]{1,0:T(8,128)(2,1)S(1)} %copy-done.7, bf16[128,1024]{1,0:T(8,128)(2,1)S(1)} %copy-done.9), kind=kOutput, calls=%fused_computation.28 | convolution fusion | flops 269615104 | bytes 1835008 | tf_op jit(solution)/shard_map/dot_general | solution.py:142
  59.5 1.7 %convolution_bitcast_fusion.5 = f32[1,256,512]{2,1,0:T(8,128)S(1)} fusion(bf16[1024,512]{1,0:T(8,128)(2,1)} %collective-permute-done.11, bf16[128,1024]{1,0:T(8,128)(2,1)S(1)} %copy-done.5, bf16[128,1024]{1,0:T(8,128)(2,1)S(1)} %get-tuple-element.5), kind=kOutput, calls=%fused_computation.15 | convolution fusion | flops 269484032 | bytes 2097152 | tf_op jit(solution)/shard_map/dot_general | solution.py:142
  61.1 9.6 %collective-permute-done.5 = bf16[512,1024]{1,0:T(8,128)(2,1)S(1)} collective-permute-done((bf16[512,1024]{1,0:T(8,128)(2,1)}, bf16[512,1024]{1,0:T(8,128)(2,1)S(1)}, u32[]{:S(2)}, u32[]{:S(2)}) %collective-permute-start.5) | collective-permute-done | bytes 1048608 | tf_op jit(solution)/shard_map/ppermute | solution.py:139
  70.7 1.7 %fusion.10 = bf16[1,256,512]{2,1,0:T(8,128)(2,1)S(1)} fusion(bf16[1024,512]{1,0:T(8,128)(2,1)} %collective-permute-done.11, bf16[512,1024]{1,0:T(8,128)(2,1)S(1)} %collective-permute-done.5), kind=kOutput, calls=%fused_computation.29 | convolution fusion | flops 268566528 | bytes 1835008 | tf_op jit(solution)/shard_map/dot_general | solution.py:142
  72.5 0.4 fusion.8
  73.0 0.6 collective-permute-start.6
  73.5 1.7 %convolution_bitcast_fusion.4 = f32[1,256,512]{2,1,0:T(8,128)S(1)} fusion(bf16[1024,512]{1,0:T(8,128)(2,1)} %collective-permute-done.11, bf16[512,1024]{1,0:T(8,128)(2,1)S(1)} %collective-permute-done.5), kind=kOutput, calls=%fused_computation.14 | convolution fusion | flops 268435456 | bytes 2097152 | tf_op jit(solution)/shard_map/dot_general | solution.py:142
  75.6 8.5 %collective-permute-done.16 = bf16[1024,512]{1,0:T(8,128)(2,1)S(1)} collective-permute-done((bf16[1024,512]{1,0:T(8,128)(2,1)}, bf16[1024,512]{1,0:T(8,128)(2,1)S(1)}, u32[]{:S(2)}, u32[]{:S(2)}) %collective-permute-start.16) | collective-permute-done | bytes 1048608 | tf_op jit(solution)/shard_map/ppermute | solution.py:80
  84.2 0.4 fusion.11
  84.7 0.4 fusion.12
  85.5 1.6 %collective-permute-start.7 = (bf16[2,128,512]{2,1,0:T(8,128)(2,1)S(1)}, bf16[2,128,512]{2,1,0:T(8,128)(2,1)S(1)}, u32[]{:S(2)}, u32[]{:S(2)}) collective-permute-start(bf16[2,128,512]{2,1,0:T(8,128)(2,1)S(1)} %slice.181), channel_id=1, source_target_pairs={{0,2},{1,3},{2,0},{3,1},{4,6},{5,7},{6,4},{7,5},{8,10},{9,11},{10,... | collective-permute-start | bytes 786440 | tf_op jit(solution)/shard_map/ppermute | solution.py:152
  87.1 0.4 convolution_bitcast_fusion.3
  87.8 0.6 collective-permute-start.13
  88.3 1.5 %collective-permute-start.21 = (bf16[1024,512]{1,0:T(8,128)(2,1)S(1)}, bf16[1024,512]{1,0:T(8,128)(2,1)S(1)}, u32[]{:S(2)}, u32[]{:S(2)}) collective-permute-start(bf16[1024,512]{1,0:T(8,128)(2,1)S(1)} %collective-permute-done.20), channel_id=1, source_target_pairs={{8,0},{12,4},{16,24},{20,28},{9,1},{13,5},{17,25},{21,29},{10,2},{... | collective-permute-start | bytes 3145736 | tf_op jit(solution)/shard_map/ppermute | solution.py:80
  89.8 0.4 convolution_bitcast_fusion.2
  90.3 4.4 %collective-permute-done.7 = bf16[2,128,512]{2,1,0:T(8,128)(2,1)S(1)} collective-permute-done((bf16[2,128,512]{2,1,0:T(8,128)(2,1)S(1)}, bf16[2,128,512]{2,1,0:T(8,128)(2,1)S(1)}, u32[]{:S(2)}, u32[]{:S(2)}) %collective-permute-start.7) | collective-permute-done | bytes 262176 | tf_op jit(solution)/shard_map/ppermute | solution.py:152
  94.8 0.6 collective-permute-start.10
  95.4 4.5 %collective-permute-done.13 = bf16[2,128,512]{2,1,0:T(8,128)(2,1)S(1)} collective-permute-done((bf16[2,128,512]{2,1,0:T(8,128)(2,1)S(1)}, bf16[2,128,512]{2,1,0:T(8,128)(2,1)S(1)}, u32[]{:S(2)}, u32[]{:S(2)}) %collective-permute-start.13) | collective-permute-done | bytes 262176 | tf_op jit(solution)/shard_map/ppermute | solution.py:152
  100.0 0.6 collective-permute-start.14
  101.1 1.6 %collective-permute-start.18 = (bf16[2,128,512]{2,1,0:T(8,128)(2,1)S(1)}, bf16[2,128,512]{2,1,0:T(8,128)(2,1)S(1)}, u32[]{:S(2)}, u32[]{:S(2)}) collective-permute-start(bf16[2,128,512]{2,1,0:T(8,128)(2,1)S(1)} %slice.179), channel_id=1, source_target_pairs={{0,2},{1,3},{2,0},{3,1},{4,6},{5,7},{6,4},{7,5},{8,10},{9,11},{10,... | collective-permute-start | bytes 786440 | tf_op jit(solution)/shard_map/ppermute | solution.py:152
  102.8 2.4 %collective-permute-done.14 = bf16[128,512]{1,0:T(8,128)(2,1)S(1)} collective-permute-done((bf16[128,512]{1,0:T(8,128)(2,1)S(1)}, bf16[128,512]{1,0:T(8,128)(2,1)S(1)}, u32[]{:S(2)}, u32[]{:S(2)}) %collective-permute-start.14) | collective-permute-done | bytes 131104 | tf_op jit(solution)/shard_map/ppermute | solution.py:160
  105.3 3.6 %collective-permute-done.18 = bf16[2,128,512]{2,1,0:T(8,128)(2,1)S(1)} collective-permute-done((bf16[2,128,512]{2,1,0:T(8,128)(2,1)S(1)}, bf16[2,128,512]{2,1,0:T(8,128)(2,1)S(1)}, u32[]{:S(2)}, u32[]{:S(2)}) %collective-permute-start.18) | collective-permute-done | bytes 262176 | tf_op jit(solution)/shard_map/ppermute | solution.py:152
  108.9 6.3 %collective-permute-done.21 = bf16[1024,512]{1,0:T(8,128)(2,1)S(1)} collective-permute-done((bf16[1024,512]{1,0:T(8,128)(2,1)S(1)}, bf16[1024,512]{1,0:T(8,128)(2,1)S(1)}, u32[]{:S(2)}, u32[]{:S(2)}) %collective-permute-start.21) | collective-permute-done | bytes 1048608 | tf_op jit(solution)/shard_map/ppermute | solution.py:80
  115.3 0.4 fusion.13
  115.8 0.4 fusion.14
  116.4 0.6 collective-permute-start.19
  117.0 0.4 convolution_bitcast_fusion.1
  117.4 0.4 convolution_bitcast_fusion
  118.5 1.6 %collective-permute-start.23 = (bf16[2,128,512]{2,1,0:T(8,128)(2,1)S(1)}, bf16[2,128,512]{2,1,0:T(8,128)(2,1)S(1)}, u32[]{:S(2)}, u32[]{:S(2)}) collective-permute-start(bf16[2,128,512]{2,1,0:T(8,128)(2,1)S(1)} %slice.178), channel_id=1, source_target_pairs={{0,2},{1,3},{2,0},{3,1},{4,6},{5,7},{6,4},{7,5},{8,10},{9,11},{10,... | collective-permute-start | bytes 786440 | tf_op jit(solution)/shard_map/ppermute | solution.py:152
  120.2 2.2 %collective-permute-done.19 = bf16[128,512]{1,0:T(8,128)(2,1)S(1)} collective-permute-done((bf16[128,512]{1,0:T(8,128)(2,1)S(1)}, bf16[128,512]{1,0:T(8,128)(2,1)S(1)}, u32[]{:S(2)}, u32[]{:S(2)}) %collective-permute-start.19) | collective-permute-done | bytes 131104 | tf_op jit(solution)/shard_map/ppermute | solution.py:160
  122.4 4.5 %collective-permute-done.23 = bf16[2,128,512]{2,1,0:T(8,128)(2,1)S(1)} collective-permute-done((bf16[2,128,512]{2,1,0:T(8,128)(2,1)S(1)}, bf16[2,128,512]{2,1,0:T(8,128)(2,1)S(1)}, u32[]{:S(2)}, u32[]{:S(2)}) %collective-permute-start.23) | collective-permute-done | bytes 262176 | tf_op jit(solution)/shard_map/ppermute | solution.py:152
  127.0 1.3 collective-permute-start.24
  128.4 3.7 %collective-permute-done.24 = bf16[128,512]{1,0:T(8,128)(2,1)S(1)} collective-permute-done((bf16[128,512]{1,0:T(8,128)(2,1)S(1)}, bf16[128,512]{1,0:T(8,128)(2,1)S(1)}, u32[]{:S(2)}, u32[]{:S(2)}) %collective-permute-start.24) | collective-permute-done | bytes 131104 | tf_op jit(solution)/shard_map/ppermute | solution.py:160
  132.0 0.7 fusion.53
  (79 shorter events, 3.7 us)
Async XLA Ops:
  0.0 34.9 %copy-start = (bf16[512,1024]{1,0:T(8,128)(2,1)S(1)}, bf16[512,1024]{1,0:T(8,128)(2,1)}, u32[]{:S(2)}) copy-start(bf16[512,1024]{1,0:T(8,128)(2,1)} %param.7) | copy-start | bytes 3145732
  0.0 1.7 %copy-start.1 = (bf16[512,1024]{1,0:T(8,128)(2,1)S(1)}, bf16[512,1024]{1,0:T(8,128)(2,1)}, u32[]{:S(2)}) copy-start(bf16[512,1024]{1,0:T(8,128)(2,1)} %param.9) | copy-start | bytes 3145732
  4.7 30.3 %copy-start.10 = (f32[8,128,128]{2,1,0:T(8,128)S(1)}, f32[8,128,128]{2,1,0:T(8,128)}, u32[]{:S(2)}) copy-start(f32[8,128,128]{2,1,0:T(8,128)} %param.11) | copy-start | bytes 1572868
  4.7 6.5 %collective-permute-start = (bf16[512,128]{1,0:T(8,128)(2,1)S(1)}, bf16[512,128]{1,0:T(8,128)(2,1)S(1)}, u32[]{:S(2)}, u32[]{:S(2)}) collective-permute-start(bf16[512,128]{1,0:T(8,128)(2,1)S(1)} %fusion.54), channel_id=1, source_target_pairs={{0,4},{4,0},{8,12},{12,8},{16,20},{20,16},{24,28},{28,24},{1,5},{5... | collective-permute-start | bytes 393224 | tf_op jit(solution)/shard_map/ppermute | solution.py:43
  11.2 6.2 %collective-permute-start.1 = (bf16[512,128]{1,0:T(8,128)(2,1)S(1)}, bf16[512,128]{1,0:T(8,128)(2,1)S(1)}, u32[]{:S(2)}, u32[]{:S(2)}) collective-permute-start(bf16[512,128]{1,0:T(8,128)(2,1)S(1)} %fusion.49), channel_id=1, source_target_pairs={{0,8},{4,12},{16,24},{20,28},{1,9},{5,13},{17,25},{21,29},{2,10},{... | collective-permute-start | bytes 393224 | tf_op jit(solution)/shard_map/ppermute | solution.py:47
  18.2 10.7 %collective-permute-start.2 = (bf16[512,128]{1,0:T(8,128)(2,1)}, bf16[512,128]{1,0:T(8,128)(2,1)S(1)}, u32[]{:S(2)}, u32[]{:S(2)}) collective-permute-start(bf16[512,128]{1,0:T(8,128)(2,1)} %fusion.33), channel_id=1, source_target_pairs={{8,16},{12,20},{9,17},{13,21},{10,18},{14,22},{11,19},{15,23}} | collective-permute-start | bytes 393224 | tf_op jit(solution)/shard_map/ppermute | solution.py:50
  18.8 10.1 %collective-permute-start.3 = (bf16[512,128]{1,0:T(8,128)(2,1)}, bf16[512,128]{1,0:T(8,128)(2,1)}, u32[]{:S(2)}, u32[]{:S(2)}) collective-permute-start(bf16[512,128]{1,0:T(8,128)(2,1)} %fusion.33), channel_id=1, source_target_pairs={{8,24},{12,28},{9,25},{13,29},{10,26},{14,30},{11,27},{15,31}} | collective-permute-start | bytes 393224 | tf_op jit(solution)/shard_map/ppermute | solution.py:51
  20.1 35.6 %collective-permute-start.11 = (bf16[1024,512]{1,0:T(8,128)(2,1)}, bf16[1024,512]{1,0:T(8,128)(2,1)}, u32[]{:S(2)}, u32[]{:S(2)}) collective-permute-start(bf16[1024,512]{1,0:T(8,128)(2,1)} %param.13), channel_id=1, source_target_pairs={{0,8},{4,12},{8,0},{12,4},{16,24},{20,28},{24,16},{28,20},{1,9},{5... | collective-permute-start | bytes 3145736 | tf_op jit(solution)/shard_map/ppermute | solution.py:80
  26.4 30.0 %collective-permute-start.15 = (bf16[1024,512]{1,0:T(8,128)(2,1)}, bf16[1024,512]{1,0:T(8,128)(2,1)}, u32[]{:S(2)}, u32[]{:S(2)}) collective-permute-start(bf16[1024,512]{1,0:T(8,128)(2,1)} %param.13), channel_id=1, source_target_pairs={{8,16},{12,20},{16,8},{20,12},{9,17},{13,21},{17,9},{21,13},{10,18... | collective-permute-start | bytes 3145736 | tf_op jit(solution)/shard_map/ppermute | solution.py:80
  29.9 5.0 %collective-permute-start.4 = (bf16[512,128]{1,0:T(8,128)(2,1)S(1)}, bf16[512,128]{1,0:T(8,128)(2,1)S(1)}, u32[]{:S(2)}, u32[]{:S(2)}) collective-permute-start(bf16[512,128]{1,0:T(8,128)(2,1)S(1)} %fusion.39), channel_id=1, source_target_pairs={{0,4},{4,0},{8,12},{12,8},{16,20},{20,16},{24,28},{28,24},{1,5},{5... | collective-permute-start | bytes 393224 | tf_op jit(solution)/shard_map/ppermute | solution.py:64
  35.0 2.4 %copy-start.11 = (pred[512,512]{1,0:T(8,128)(4,1)S(1)}, pred[512,512]{1,0:T(8,128)(4,1)}, u32[]{:S(2)}) copy-start(pred[512,512]{1,0:T(8,128)(4,1)} %iota_compare_fusion) | copy-start | bytes 786436
  43.3 1.9 %dynamic-slice-start = ((f32[4096]{0:T(1024)}, s32[]{:T(128)}), f32[1024]{0:T(1024)S(1)}, s32[]{:S(2)}) async-start(f32[4096]{0:T(1024)} %param.12, s32[]{:T(128)} %select_n.148), calls=%async_computation | async-start | bytes 8704 | tf_op jit(solution)/shard_map/dynamic_slice | solution.py:129
  47.0 3.4 %copy-start.2 = (bf16[1024,512]{1,0:T(8,128)(2,1)S(1)}, bf16[1024,512]{1,0:T(8,128)(2,1)}, u32[]{:S(2)}) copy-start(bf16[1024,512]{1,0:T(8,128)(2,1)} %param.13) | copy-start | bytes 3145732
  47.2 0.7 copy-start.4
  47.2 1.7 %copy-start.6 = (bf16[128,1024]{1,0:T(8,128)(2,1)}, bf16[128,1024]{1,0:T(8,128)(2,1)S(1)}, u32[]{:S(2)}) copy-start(bf16[128,1024]{1,0:T(8,128)(2,1)S(1)} %get-tuple-element.6) | copy-start | bytes 786436
  47.2 1.7 %copy-start.8 = (bf16[128,1024]{1,0:T(8,128)(2,1)}, bf16[128,1024]{1,0:T(8,128)(2,1)S(1)}, u32[]{:S(2)}) copy-start(bf16[128,1024]{1,0:T(8,128)(2,1)S(1)} %get-tuple-element.7) | copy-start | bytes 786436
  48.9 21.8 %collective-permute-start.5 = (bf16[512,1024]{1,0:T(8,128)(2,1)}, bf16[512,1024]{1,0:T(8,128)(2,1)S(1)}, u32[]{:S(2)}, u32[]{:S(2)}) collective-permute-start(bf16[512,1024]{1,0:T(8,128)(2,1)} %pad_maximum_fusion), channel_id=1, source_target_pairs={{0,4},{4,0},{8,12},{12,8},{16,20},{20,16},{24,28},{28,24},{1,5},{5... | collective-permute-start | bytes 3145736 | tf_op jit(solution)/shard_map/ppermute | solution.py:139
  50.4 3.2 %copy-start.5 = (bf16[128,1024]{1,0:T(8,128)(2,1)S(1)}, bf16[128,1024]{1,0:T(8,128)(2,1)}, u32[]{:S(2)}) copy-start(bf16[128,1024]{1,0:T(8,128)(2,1)} %copy-done.4) | copy-start | bytes 786436
  50.4 7.4 %copy-start.7 = (bf16[128,1024]{1,0:T(8,128)(2,1)S(1)}, bf16[128,1024]{1,0:T(8,128)(2,1)}, u32[]{:S(2)}) copy-start(bf16[128,1024]{1,0:T(8,128)(2,1)} %copy-done.6) | copy-start | bytes 786436
  50.4 7.4 %copy-start.9 = (bf16[128,1024]{1,0:T(8,128)(2,1)S(1)}, bf16[128,1024]{1,0:T(8,128)(2,1)}, u32[]{:S(2)}) copy-start(bf16[128,1024]{1,0:T(8,128)(2,1)} %copy-done.8) | copy-start | bytes 786436
  50.4 1.6 %collective-permute-start.8 = (f32[512]{0:T(512)S(1)}, f32[512]{0:T(512)S(1)}, u32[]{:S(2)}, u32[]{:S(2)}) collective-permute-start(f32[512]{0:T(512)S(1)} %get-tuple-element.9), channel_id=1, source_target_pairs={{0,1},{1,0},{2,3},{3,2},{4,5},{5,4},{6,7},{7,6},{8,9},{9,8},{10,11... | collective-permute-start | bytes 6152 | tf_op jit(solution)/shard_map/ppermute | solution.py:123
  52.0 3.7 %collective-permute-start.9 = (f32[512]{0:T(512)S(1)}, f32[512]{0:T(512)S(1)}, u32[]{:S(2)}, u32[]{:S(2)}) collective-permute-start(f32[512]{0:T(512)S(1)} %add.207), channel_id=1, source_target_pairs={{0,2},{1,3},{2,0},{3,1},{4,6},{5,7},{6,4},{7,5},{8,10},{9,11},{10,... | collective-permute-start | bytes 6152 | tf_op jit(solution)/shard_map/ppermute | solution.py:123
  55.7 32.6 %collective-permute-start.20 = (bf16[1024,512]{1,0:T(8,128)(2,1)}, bf16[1024,512]{1,0:T(8,128)(2,1)S(1)}, u32[]{:S(2)}, u32[]{:S(2)}) collective-permute-start(bf16[1024,512]{1,0:T(8,128)(2,1)} %collective-permute-done.11), channel_id=1, source_target_pairs={{8,16},{12,20},{16,8},{20,12},{9,17},{13,21},{17,9},{21,13},{10,18... | collective-permute-start | bytes 3145736 | tf_op jit(solution)/shard_map/ppermute | solution.py:80
  56.5 27.6 %collective-permute-start.16 = (bf16[1024,512]{1,0:T(8,128)(2,1)}, bf16[1024,512]{1,0:T(8,128)(2,1)S(1)}, u32[]{:S(2)}, u32[]{:S(2)}) collective-permute-start(bf16[1024,512]{1,0:T(8,128)(2,1)} %collective-permute-done.15), channel_id=1, source_target_pairs={{8,0},{12,4},{16,24},{20,28},{9,1},{13,5},{17,25},{21,29},{10,2},{... | collective-permute-start | bytes 3145736 | tf_op jit(solution)/shard_map/ppermute | solution.py:80
  72.4 15.1 %collective-permute-start.12 = (bf16[2,256,512]{2,1,0:T(8,128)(2,1)S(1)}, bf16[2,256,512]{2,1,0:T(8,128)(2,1)S(1)}, u32[]{:S(2)}, u32[]{:S(2)}) collective-permute-start(bf16[2,256,512]{2,1,0:T(8,128)(2,1)S(1)} %pad_maximum_fusion.4), channel_id=1, source_target_pairs={{0,1},{1,0},{2,3},{3,2},{4,5},{5,4},{6,7},{7,6},{8,9},{9,8},{10,11... | collective-permute-start | bytes 1572872 | tf_op jit(solution)/shard_map/ppermute | solution.py:152
  73.0 12.3 %collective-permute-start.6 = (bf16[2,256,512]{2,1,0:T(8,128)(2,1)S(1)}, bf16[2,256,512]{2,1,0:T(8,128)(2,1)S(1)}, u32[]{:S(2)}, u32[]{:S(2)}) collective-permute-start(bf16[2,256,512]{2,1,0:T(8,128)(2,1)S(1)} %pad_maximum_fusion.3), channel_id=1, source_target_pairs={{0,1},{1,0},{2,3},{3,2},{4,5},{5,4},{6,7},{7,6},{8,9},{9,8},{10,11... | collective-permute-start | bytes 1572872 | tf_op jit(solution)/shard_map/ppermute | solution.py:152
  85.2 15.7 %collective-permute-start.17 = (bf16[2,256,512]{2,1,0:T(8,128)(2,1)S(1)}, bf16[2,256,512]{2,1,0:T(8,128)(2,1)S(1)}, u32[]{:S(2)}, u32[]{:S(2)}) collective-permute-start(bf16[2,256,512]{2,1,0:T(8,128)(2,1)S(1)} %pad_maximum_fusion.5), channel_id=1, source_target_pairs={{0,1},{1,0},{2,3},{3,2},{4,5},{5,4},{6,7},{7,6},{8,9},{9,8},{10,11... | collective-permute-start | bytes 1572872 | tf_op jit(solution)/shard_map/ppermute | solution.py:152
  85.5 9.2 %collective-permute-start.7 = (bf16[2,128,512]{2,1,0:T(8,128)(2,1)S(1)}, bf16[2,128,512]{2,1,0:T(8,128)(2,1)S(1)}, u32[]{:S(2)}, u32[]{:S(2)}) collective-permute-start(bf16[2,128,512]{2,1,0:T(8,128)(2,1)S(1)} %slice.181), channel_id=1, source_target_pairs={{0,2},{1,3},{2,0},{3,1},{4,6},{5,7},{6,4},{7,5},{8,10},{9,11},{10,... | collective-permute-start | bytes 786440 | tf_op jit(solution)/shard_map/ppermute | solution.py:152
  87.8 12.1 %collective-permute-start.13 = (bf16[2,128,512]{2,1,0:T(8,128)(2,1)S(1)}, bf16[2,128,512]{2,1,0:T(8,128)(2,1)S(1)}, u32[]{:S(2)}, u32[]{:S(2)}) collective-permute-start(bf16[2,128,512]{2,1,0:T(8,128)(2,1)S(1)} %slice.180), channel_id=1, source_target_pairs={{0,2},{1,3},{2,0},{3,1},{4,6},{5,7},{6,4},{7,5},{8,10},{9,11},{10,... | collective-permute-start | bytes 786440 | tf_op jit(solution)/shard_map/ppermute | solution.py:152
  88.3 26.9 %collective-permute-start.21 = (bf16[1024,512]{1,0:T(8,128)(2,1)S(1)}, bf16[1024,512]{1,0:T(8,128)(2,1)S(1)}, u32[]{:S(2)}, u32[]{:S(2)}) collective-permute-start(bf16[1024,512]{1,0:T(8,128)(2,1)S(1)} %collective-permute-done.20), channel_id=1, source_target_pairs={{8,0},{12,4},{16,24},{20,28},{9,1},{13,5},{17,25},{21,29},{10,2},{... | collective-permute-start | bytes 3145736 | tf_op jit(solution)/shard_map/ppermute | solution.py:80
  94.8 6.0 %collective-permute-start.10 = (bf16[128,512]{1,0:T(8,128)(2,1)S(1)}, bf16[128,512]{1,0:T(8,128)(2,1)S(1)}, u32[]{:S(2)}, u32[]{:S(2)}) collective-permute-start(bf16[128,512]{1,0:T(8,128)(2,1)S(1)} %fusion.56), channel_id=1, source_target_pairs={{0,4},{4,0},{8,12},{12,8},{16,20},{20,16},{24,28},{28,24},{1,5},{5... | collective-permute-start | bytes 393224 | tf_op jit(solution)/shard_map/ppermute | solution.py:160
  100.0 5.2 %collective-permute-start.14 = (bf16[128,512]{1,0:T(8,128)(2,1)S(1)}, bf16[128,512]{1,0:T(8,128)(2,1)S(1)}, u32[]{:S(2)}, u32[]{:S(2)}) collective-permute-start(bf16[128,512]{1,0:T(8,128)(2,1)S(1)} %fusion.58), channel_id=1, source_target_pairs={{0,4},{4,0},{8,12},{12,8},{16,20},{20,16},{24,28},{28,24},{1,5},{5... | collective-permute-start | bytes 393224 | tf_op jit(solution)/shard_map/ppermute | solution.py:160
  101.1 7.7 %collective-permute-start.18 = (bf16[2,128,512]{2,1,0:T(8,128)(2,1)S(1)}, bf16[2,128,512]{2,1,0:T(8,128)(2,1)S(1)}, u32[]{:S(2)}, u32[]{:S(2)}) collective-permute-start(bf16[2,128,512]{2,1,0:T(8,128)(2,1)S(1)} %slice.179), channel_id=1, source_target_pairs={{0,2},{1,3},{2,0},{3,1},{4,6},{5,7},{6,4},{7,5},{8,10},{9,11},{10,... | collective-permute-start | bytes 786440 | tf_op jit(solution)/shard_map/ppermute | solution.py:152
  116.3 2.0 %collective-permute-start.22 = (bf16[2,256,512]{2,1,0:T(8,128)(2,1)S(1)}, bf16[2,256,512]{2,1,0:T(8,128)(2,1)S(1)}, u32[]{:S(2)}, u32[]{:S(2)}) collective-permute-start(bf16[2,256,512]{2,1,0:T(8,128)(2,1)S(1)} %pad_maximum_fusion.6), channel_id=1, source_target_pairs={{0,1},{1,0},{2,3},{3,2},{4,5},{5,4},{6,7},{7,6},{8,9},{9,8},{10,11... | collective-permute-start | bytes 1572872 | tf_op jit(solution)/shard_map/ppermute | solution.py:152
  116.4 6.0 %collective-permute-start.19 = (bf16[128,512]{1,0:T(8,128)(2,1)S(1)}, bf16[128,512]{1,0:T(8,128)(2,1)S(1)}, u32[]{:S(2)}, u32[]{:S(2)}) collective-permute-start(bf16[128,512]{1,0:T(8,128)(2,1)S(1)} %fusion.60), channel_id=1, source_target_pairs={{0,4},{4,0},{8,12},{12,8},{16,20},{20,16},{24,28},{28,24},{1,5},{5... | collective-permute-start | bytes 393224 | tf_op jit(solution)/shard_map/ppermute | solution.py:160
  118.5 8.4 %collective-permute-start.23 = (bf16[2,128,512]{2,1,0:T(8,128)(2,1)S(1)}, bf16[2,128,512]{2,1,0:T(8,128)(2,1)S(1)}, u32[]{:S(2)}, u32[]{:S(2)}) collective-permute-start(bf16[2,128,512]{2,1,0:T(8,128)(2,1)S(1)} %slice.178), channel_id=1, source_target_pairs={{0,2},{1,3},{2,0},{3,1},{4,6},{5,7},{6,4},{7,5},{8,10},{9,11},{10,... | collective-permute-start | bytes 786440 | tf_op jit(solution)/shard_map/ppermute | solution.py:152
  127.0 5.0 %collective-permute-start.24 = (bf16[128,512]{1,0:T(8,128)(2,1)S(1)}, bf16[128,512]{1,0:T(8,128)(2,1)S(1)}, u32[]{:S(2)}, u32[]{:S(2)}) collective-permute-start(bf16[128,512]{1,0:T(8,128)(2,1)S(1)} %fusion.62), channel_id=1, source_target_pairs={{0,4},{4,0},{8,12},{12,8},{16,20},{20,16},{24,28},{28,24},{1,5},{5... | collective-permute-start | bytes 393224 | tf_op jit(solution)/shard_map/ppermute | solution.py:160
  128.4 3.7 %copy-start.3 = (bf16[128,4096]{1,0:T(8,128)(2,1)}, bf16[128,4096]{1,0:T(8,128)(2,1)S(1)}, u32[]{:S(2)}) copy-start(bf16[128,4096]{1,0:T(8,128)(2,1)S(1)} %fusion.61) | copy-start | bytes 3145732

commit v2 on v1

--- a/solution.py
+++ b/solution.py
@@ -1,6 +1,10 @@
+import functools
+
 import jax
 import jax.numpy as jnp
 from jax import lax
+from jax.experimental import pallas as pl
+from jax.experimental.pallas import tpu as pltpu
 from jax.sharding import PartitionSpec as P
 
 DH = 128
@@ -30,12 +34,161 @@
 TO_ENDS = [(1, 0), (2, 3)]
 
 
-def state_prefix(own_total, n_seq, place):
+def states_kernel(k_ref, v_ref, wide_ref, low_ref):
+    for index in range(wide_ref.shape[0]):
+        columns = pl.ds(index * DH, DH)
+        state = lax.dot_general(
+            k_ref[:, columns],
+            v_ref[:, columns],
+            (((0,), (0,)), ((), ())),
+            preferred_element_type=jnp.float32,
+        )
+        wide_ref[index] = state
+        low_ref[index] = state.astype(jnp.bfloat16)
+
+
+def block_states(key_input, value_input, heads_at_once=2):
+    rows, width = key_input.shape
+    heads = width // DH
+    steps = heads // heads_at_once
+    shape = (heads, DH, DH)
+    rows_spec = pl.BlockSpec((rows, heads_at_once * DH), lambda step: (0, step))
+    state_spec = pl.BlockSpec((heads_at_once, DH, DH), lambda step: (step, 0, 0))
+    return pl.pallas_call(
+        states_kernel,
+        grid=(steps,),
+        in_specs=[rows_spec, rows_spec],
+        out_specs=[state_spec, state_spec],
+        out_shape=[
+            jax.ShapeDtypeStruct(shape, jnp.float32),
+            jax.ShapeDtypeStruct(shape, jnp.bfloat16),
+        ],
+        cost_estimate=pl.CostEstimate(
+            flops=2 * rows * width * DH, bytes_accessed=4 * rows * width, transcendentals=0
+        ),
+    )(key_input, value_input)
+
+
+def causal_kernel(q_ref, k_ref, v_ref, *rest):
+    out_ref = rest[-1]
+    rows = q_ref.shape[0]
+    half = rows // 2
+    for index in range(q_ref.shape[1] // DH):
+        columns = pl.ds(index * DH, DH)
+        for first in (0, half):
+            seen = first + half
+            scores = lax.dot_general(
+                q_ref[pl.ds(first, half), columns],
+                k_ref[pl.ds(0, seen), columns],
+                (((1,), (1,)), ((), ())),
+                preferred_element_type=jnp.float32,
+            )
+            at_row = first + lax.broadcasted_iota(jnp.int32, scores.shape, 0)
+            at_column = lax.broadcasted_iota(jnp.int32, scores.shape, 1)
+            scores = jnp.where(at_row >= at_column, scores, 0.0).astype(jnp.bfloat16)
+            out_ref[pl.ds(first, half), columns] = jnp.dot(
+                scores, v_ref[pl.ds(0, seen), columns], preferred_element_type=jnp.float32
+            )
+
+
+def causal_part(queries, key_input, value_input, calls=2):
+    rows, width = queries.shape
+    heads = width // DH // calls
+    result = None
+    for call in range(calls):
+        spec = pl.BlockSpec((rows, DH), lambda head, base=call * heads: (0, base + head))
+        operands = [queries, key_input, value_input]
+        specs = [spec] * 3
+        aliases = {}
+        if result is not None:
+            operands.append(result)
+            specs.append(pl.BlockSpec(memory_space=pl.ANY))
+            aliases = {3: 0}
+        result = pl.pallas_call(
+            causal_kernel,
+            grid=(heads,),
+            in_specs=specs,
+            out_specs=spec,
+            out_shape=jax.ShapeDtypeStruct((rows, width), jnp.float32),
+            input_output_aliases=aliases,
+            cost_estimate=pl.CostEstimate(
+                flops=4 * rows * rows * heads * DH,
+                bytes_accessed=10 * rows * heads * DH,
+                transcendentals=0,
+            ),
+        )(*operands)
+    return result
+
+
+def hidden_kernel(order, h_ref, q_ref, inner_ref, state_ref, gate_ref, gain_ref, *rest):
+    hidden_ref, squares_ref = rest[-2:]
+    state = state_ref[0]
+    high = state.astype(jnp.bfloat16)
+    low = (state - high.astype(jnp.float32)).astype(jnp.bfloat16)
+    size = q_ref.shape[0] // len(order)
+    gain = gain_ref[0]
+
+    @pl.when(pl.program_id(0) == 0)
+    def _():
+        squares_ref[...] = jnp.zeros_like(squares_ref)
+
+    for position, block in enumerate(order):
+        start = pl.multiple_of((h_ref[0] ^ block) * size, size)
+        rows = pl.ds(start, size)
+        q_rows = q_ref[rows, :]
+        carried = jnp.dot(q_rows, high, preferred_element_type=jnp.float32) + jnp.dot(
+            q_rows, low, preferred_element_type=jnp.float32
+        )
+        attn = (carried + inner_ref[rows, :]).astype(jnp.bfloat16).astype(jnp.float32)
+        gate = jax.nn.sigmoid(gate_ref[rows, :].astype(jnp.float32))
+        placed = pl.ds(position * size, size)
+        hidden_ref[placed, :] = (attn * gain * gate).astype(jnp.bfloat16)
+        squares_ref[placed, :] += attn * attn
+
+
+def gated_hidden(queries, inner, state, gate_input, norm_gain, h, order, after):
+    rows, width = queries.shape
+    heads = width // DH
+    columns = pl.BlockSpec((rows, DH), lambda head, h_ref: (0, head))
+    return pl.pallas_call(
+        functools.partial(hidden_kernel, order),
+        grid_spec=pltpu.PrefetchScalarGridSpec(
+            num_scalar_prefetch=1,
+            grid=(heads,),
+            in_specs=[
+                columns,
+                columns,
+                pl.BlockSpec((1, DH, DH), lambda head, h_ref: (head, 0, 0)),
+                columns,
+                pl.BlockSpec((1, 1, DH), lambda head, h_ref: (h_ref[0] * heads + head, 0, 0)),
+            ]
+            + [pl.BlockSpec(memory_space=pl.ANY)] * len(after),
+            out_specs=[columns, pl.BlockSpec((rows, DH), lambda head, h_ref: (0, 0))],
+        ),
+        out_shape=[
+            jax.ShapeDtypeStruct((rows, width), jnp.bfloat16),
+            jax.ShapeDtypeStruct((rows, DH), jnp.float32),
+        ],
+        cost_estimate=pl.CostEstimate(
+            flops=4 * rows * width * DH, bytes_accessed=12 * rows * width, transcendentals=rows * width
+        ),
+    )(
+        jnp.reshape(h, (1,)).astype(jnp.int32),
+        queries,
+        inner,
+        state,
+        gate_input,
+        norm_gain.reshape(-1, 1, DH),
+        *after,
+    )
+
+
+def state_prefix(wide, low, n_seq, place):
     inner = n_seq // LINE
     i = place % inner
-    shape = own_total.shape
-    parts = own_total.reshape(inner, -1, DH)
-    parts_low = parts.astype(jnp.bfloat16)
+    shape = wide.shape
+    parts = wide.reshape(inner, -1, DH)
+    parts_low = low.reshape(inner, -1, DH)
     from_member = [lax.dynamic_index_in_dim(parts, i, 0, False)]
     members = [i]
     for turn in range(1, inner):
@@ -57,12 +210,12 @@
             total = total + jnp.where(owner < member, value, 0.0)
         return total
 
-    result = jnp.zeros_like(parts)
-    result = lax.dynamic_update_index_in_dim(result, before(i), i, 0)
+    index = jnp.arange(inner)[:, None, None]
+    result = jnp.where(index == i, before(i)[None], 0.0)
     for turn in range(1, inner):
         sent = before((i + turn) % inner).astype(jnp.bfloat16)
-        got = lax.ppermute(sent, "seq", turn_pairs(n_seq, turn))
-        result = lax.dynamic_update_index_in_dim(result, got.astype(jnp.float32), (i - turn) % inner, 0)
+        got = lax.ppermute(sent, "seq", turn_pairs(n_seq, turn)).astype(jnp.float32)
+        result = jnp.where(index == (i - turn) % inner, got[None], result)
     return result.reshape(shape)
 
 
@@ -72,8 +225,7 @@
     place, h = lax.axis_index("seq"), lax.axis_index("head")
     z, i = place // inner, place % inner
     tok_rows, local_width = queries.shape
-    local_heads = local_width // DH
-    num_blocks = tok_rows // BLOCK
+    assert tok_rows == BLOCK
     total_width = local_width * n_head
 
     def along(value, hops):
@@ -94,46 +246,24 @@
     low = z < 2
     weight_from = [z, z ^ 1, jnp.where(low, 2, 1), jnp.where(low, 3, 0)]
 
-    block_shape = (num_blocks, BLOCK, local_heads, DH)
-    q_blocks = queries.reshape(block_shape)
-    k_blocks = key_input.reshape(block_shape)
-    v_blocks = value_input.reshape(block_shape)
-    block_states = jnp.einsum(
-        "nthd,nthe->nhde", k_blocks, v_blocks, preferred_element_type=jnp.float32
-    )
-    own_total = jnp.sum(block_states, axis=0)
-    start_state = kv_state + state_prefix(own_total, n_seq, place)
-    running = jnp.cumsum(block_states, axis=0) - block_states
-    before = start_state[None] + running
-    carried_part = jnp.einsum(
-        "nthd,nhde->nthe", q_blocks.astype(jnp.float32), before, precision=lax.Precision.HIGHEST
-    )
-    scores = jnp.einsum("nthd,nshd->nhts", q_blocks, k_blocks, preferred_element_type=jnp.float32)
-    causal = jnp.arange(BLOCK)[:, None] >= jnp.arange(BLOCK)[None, :]
-    masked = jnp.where(causal[None, None], scores, 0.0).astype(jnp.bfloat16)
-    inner_part = jnp.einsum(
-        "nhts,nshe->nthe", masked, v_blocks, preferred_element_type=jnp.float32
-    )
-    attn = (carried_part + inner_part).astype(jnp.bfloat16).reshape(tok_rows, local_width)
-    attn_float = attn.astype(jnp.float32)
-
-    squares = jnp.sum(attn_float * attn_float, axis=1)
-    bit = 1
-    while bit < n_head:
-        squares = squares + lax.ppermute(squares, "head", flip_pairs(n_head, bit))
-        bit *= 2
-    out_rows = tok_rows // n_head
-    own_squares = lax.dynamic_slice_in_dim(squares, h * out_rows, out_rows, 0)
-    scale = lax.rsqrt(own_squares / total_width + epsilon)
-
-    gain_part = lax.dynamic_slice_in_dim(norm_gain, h * local_width, local_width, 0)
-    gated = attn_float * gain_part[None, :] * jax.nn.sigmoid(gate_input.astype(jnp.float32))
-    gated = gated.astype(jnp.bfloat16).reshape(n_head, out_rows, local_width)
+    wide, low_states = block_states(key_input, value_input)
+    state = kv_state + state_prefix(wide, low_states, n_seq, place)
+    inner_part = causal_part(queries, key_input, value_input)
     bits = n_head.bit_length() - 1
     order = [int(format(j, "b").zfill(bits)[::-1], 2) for j in range(n_head)] if bits else [0]
-    hidden = jnp.concatenate(
-        [lax.dynamic_index_in_dim(gated, j ^ h, 0, False) for j in order], axis=0
+    hidden, squares = gated_hidden(
+        queries, inner_part, state, gate_input, norm_gain, h, order, [w_pair, w_mid1]
     )
+
+    squares = jnp.sum(squares, axis=1)
+    out_rows = tok_rows // n_head
+    half, bit = tok_rows // 2, 1
+    while bit < n_head:
+        squares = squares[:half] + lax.ppermute(squares[half:], "head", flip_pairs(n_head, bit))
+        half //= 2
+        bit *= 2
+    scale = lax.rsqrt(squares / total_width + epsilon)
+
     hiddens = [hidden]
     for turn in range(1, inner):
         hiddens.append(lax.ppermute(hidden, "seq", turn_pairs(n_seq, turn)))

time: 133 us -> 161 us (1.21)
  Pallas kernels: 0 us -> 20.3 us
  waiting for transfers between devices: 60 us -> 78 us
  matrix products: 22.9 us -> 17.4 us
  starting transfers between devices: 33.9 us -> 29 us
  local copies, waits for them, and re-layouts: 6.09 us -> 3.62 us
    ppermute x5, waiting for transfers between devices: 14.8 us -> 45.1 us  [along(): return lax.ppermute(value, 'seq', line_pairs(n_seq, hops))]
    pallas_call x0 -> x4, Pallas kernels: none -> 20.3 us  [the longest x2 9.4 us: causal_part(): pl.pallas_call(causal_kernel, grid=(heads,), in_specs=specs, out_specs=sp...]
    dot_general x3 -> x0, matrix products: 9.95 us -> none  [the longest x1 5.88 us: shards(): jnp.einsum('nhts,nshe->nthe', masked, v_blocks, preferred_element_type=jn...]
    ppermute x1, waiting for transfers between devices: 9.56 us -> 0.01 us  [shards(): hiddens.append(lax.ppermute(hidden, 'seq', turn_pairs(n_seq, turn)))]
    ppermute x5, starting transfers between devices: 11.4 us -> 4.24 us  [along(): return lax.ppermute(value, 'seq', line_pairs(n_seq, hops))]
    ppermute x4, waiting for transfers between devices: 8.21 us -> 3.52 us  [shards(): lax.ppermute(kept[turn].astype(jnp.bfloat16), 'seq', turn_pairs(n_seq, -t...]
    dot_general x16, matrix products: 13 us -> 17.4 us  [project(): return jnp.dot(rows, weight, preferred_element_type=jnp.float32)]
    add x2 -> x3, other arithmetic: 0.01 us -> 3.95 us  [the longest x1 2.03 us: shards(): state = kv_state + state_prefix(wide, low_states, n_seq, place)]
  transfers between devices with their start and end apart: 25 -> 25, of which waited for: 15 -> 10; matrix products, arithmetic and copies ran while one was open for 23% -> 17% of each run, Pallas kernels for 0% -> 6%
where the time goes in v2:
time: 161 us; the launch traced here: 160 us
  waiting for transfers between devices  78 us (48%)
  starting transfers between devices  29 us (18%)
  Pallas kernels  20.3 us (13%)
  matrix products  17.4 us (11%)
  other arithmetic  10.5 us (7%)
  local copies, waits for them, and re-layouts  3.62 us (2%)
    ppermute x5, waiting for transfers between devices, along(): return lax.ppermute(value, 'seq', line_pairs(n_seq, hops))  45.1 us
    ppermute x8, waiting for transfers between devices, shards(): lax.ppermute(sent, 'head', flip_pairs(n_head, bit)).astype(jnp.float32)  21.2 us
    dot_general x16, matrix products, project(): return jnp.dot(rows, weight, preferred_element_type=jnp.float32)  17.4 us
    pallas_call x2, Pallas kernels, causal_part(): pl.pallas_call(causal_kernel, grid=(heads,), in_specs=specs, out_specs=sp...  9.4 us
    pallas_call x1, Pallas kernels, gated_hidden(): pl.pallas_call(functools.partial(hidden_kernel, order), grid_spec=pltpu.P...  6.87 us
    ppermute x8, starting transfers between devices, shards(): lax.ppermute(sent, 'head', flip_pairs(n_head, bit)).astype(jnp.float32)  6.1 us
    ppermute x4, starting transfers between devices, shards(): lax.ppermute(kept[turn].astype(jnp.bfloat16), 'seq', turn_pairs(n_seq, -t...  5.26 us
    ppermute x5, starting transfers between devices, along(): return lax.ppermute(value, 'seq', line_pairs(n_seq, hops))  4.24 us
  transfers between devices with their start and end apart: 25, of which 10 were waited for; matrix products, arithmetic and copies ran while one was open for 17% of the time, Pallas kernels for 6%

profile of v2, /device:TPU:0, one launch (start us, length us, event | category | flops | bytes accessed | tf_op | source)
XLA Modules:
  0.0 159.5 jit_solution(17906307160293450572)
XLA Ops:
  0.0 4.1 %shard_map.75 = (f32[8,128,128]{2,1,0:T(8,128)}, bf16[8,128,128]{2,1,0:T(8,128)(2,1)}) custom-call(bf16[512,1024]{1,0:T(8,128)(2,1)} %k_ref.5, bf16[512,1024]{1,0:T(8,128)(2,1)} %v_ref.5), custom_call_target="tpu_custom_call" | custom-call | flops 134217728 | bytes 2097152 | tf_op jit(solution)/shard_map/pallas_call | solution.py:57
  4.1 0.9 dynamic-slice_bitcast_fusion
  5.0 3.0 %collective-permute-start = (bf16[512,128]{1,0:T(8,128)(2,1)S(1)}, bf16[512,128]{1,0:T(8,128)(2,1)S(1)}, u32[]{:S(2)}, u32[]{:S(2)}) collective-permute-start(bf16[512,128]{1,0:T(8,128)(2,1)S(1)} %dynamic-slice_bitcast_fusion), channel_id=1, source_target_pairs={{0,4},{4,0},{8,12},{12,8},{16,20},{20,16},{24,28},{28,24},{1,5},{5... | collective-permute-start | bytes 393224 | tf_op jit(solution)/shard_map/ppermute | solution.py:196
  8.0 3.5 %collective-permute-done = bf16[512,128]{1,0:T(8,128)(2,1)S(1)} collective-permute-done((bf16[512,128]{1,0:T(8,128)(2,1)S(1)}, bf16[512,128]{1,0:T(8,128)(2,1)S(1)}, u32[]{:S(2)}, u32[]{:S(2)}) %collective-permute-start) | collective-permute-done | bytes 131104 | tf_op jit(solution)/shard_map/ppermute | solution.py:196
  11.5 1.0 fusion.38
  12.5 3.7 %collective-permute-start.1 = (bf16[512,128]{1,0:T(8,128)(2,1)S(1)}, bf16[512,128]{1,0:T(8,128)(2,1)S(1)}, u32[]{:S(2)}, u32[]{:S(2)}) collective-permute-start(bf16[512,128]{1,0:T(8,128)(2,1)S(1)} %fusion.38), channel_id=1, source_target_pairs={{0,8},{4,12},{16,24},{20,28},{1,9},{5,13},{17,25},{21,29},{2,10},{... | collective-permute-start | bytes 393224 | tf_op jit(solution)/shard_map/ppermute | solution.py:200
  16.3 0.7 collective-permute-start.6
  17.0 3.1 %collective-permute-done.1 = bf16[512,128]{1,0:T(8,128)(2,1)S(1)} collective-permute-done((bf16[512,128]{1,0:T(8,128)(2,1)S(1)}, bf16[512,128]{1,0:T(8,128)(2,1)S(1)}, u32[]{:S(2)}, u32[]{:S(2)}) %collective-permute-start.1) | collective-permute-done | bytes 131104 | tf_op jit(solution)/shard_map/ppermute | solution.py:200
  20.1 1.7 %fusion.24 = bf16[512,128]{1,0:T(8,128)(2,1)} fusion(bf16[512,128]{1,0:T(8,128)(2,1)S(1)} %collective-permute-done.1, bf16[512,128]{1,0:T(8,128)(2,1)S(1)} %collective-permute-done, f32[2,512,128]{2,1,0:T(8,128)} %bitcast.110, s32[]{:T(128)S(6)} %select_n.118), kind=kLoop, calls=%fused_computation.64 | loop fusion | flops 327680 | bytes 655364 | tf_op jit(solution)/shard_map/convert_element_type | solution.py:202
  21.9 0.7 collective-permute-start.2
  22.5 1.3 collective-permute-start.3
  23.9 0.6 copy-done.8
  24.5 1.9 %fusion.28 = (f32[512,128]{1,0:T(8,128)S(1)}, bf16[512,128]{1,0:T(8,128)(2,1)}) fusion(bf16[512,128]{1,0:T(8,128)(2,1)S(1)} %collective-permute-done, bf16[512,128]{1,0:T(8,128)(2,1)} %collective-permute-done.3, bf16[512,128]{1,0:T(8,128)(2,1)} %copy-done.8, bf16[512,128]{1,0:T(8,128)(2,1)} %copy-done.7, pred[]{:T(512)S(6)} %lt.79, pred[]{:T(512)S(6)} %lt.78, ...), kind=kLoop, calls=%fused_computation.68 | loop fusion | flops 851968 | bytes 1179655 | tf_op jit(solution)/shard_map/add | solution.py:210
  26.4 1.5 collective-permute-start.4
  28.2 4.7 %shard_map.73.rest_0_ = f32[512,1024]{1,0:T(8,128)} custom-call(bf16[512,1024]{1,0:T(8,128)(2,1)} %q_ref.5, bf16[512,1024]{1,0:T(8,128)(2,1)} %k_ref.5, bf16[512,1024]{1,0:T(8,128)(2,1)} %v_ref.5), custom_call_target="tpu_custom_call" | custom-call | flops 536870912 | bytes 2621440 | tf_op jit(solution)/shard_map/pallas_call | solution.py:107
  32.9 4.7 %shard_map.74.inner_ref = f32[512,1024]{1,0:T(8,128)} custom-call(bf16[512,1024]{1,0:T(8,128)(2,1)} %q_ref.5, bf16[512,1024]{1,0:T(8,128)(2,1)} %k_ref.5, bf16[512,1024]{1,0:T(8,128)(2,1)} %v_ref.5, f32[512,1024]{1,0:T(8,128)} %shard_map.73.rest_0_), custom_call_target="tpu_custom_call", output_to_operand_aliasing={{}: (3, {})} | custom-call | flops 536870912 | bytes 2621440 | tf_op jit(solution)/shard_map/pallas_call | solution.py:107
  37.7 2.0 %select_add_fusion.state_ref = f32[8,128,128]{2,1,0:T(8,128)} fusion(f32[8,128,128]{2,1,0:T(8,128)} %param.11, f32[8,128,128]{2,1,0:T(8,128)S(1)} %bitcast.107, f32[8,128,128]{2,1,0:T(8,128)S(1)} %bitcast.108, pred[8]{0:T(512)(128)(4,1)S(1)} %broadcast_in_dim.77, pred[8]{0:T(512)(128)(4,1)S(1)} %broadcast_in_dim.71), kind=kLoop, calls=%fused_computation.42 | loop fusion | flops 393216 | bytes 2097168 | tf_op jit(solution)/shard_map/add | solution.py:250
  39.7 0.8 collective-permute-done.5.rest_0_
  40.6 1.0 copy-done
  41.5 0.4 copy-done.3
  41.9 6.9 %shard_map.76 = (bf16[512,1024]{1,0:T(8,128)(2,1)}, f32[512,128]{1,0:T(8,128)}) custom-call(s32[1]{0:T(128)} %bitcast.h_ref, bf16[512,1024]{1,0:T(8,128)(2,1)} %q_ref.5, f32[512,1024]{1,0:T(8,128)} %shard_map.74.inner_ref, f32[8,128,128]{2,1,0:T(8,128)} %select_add_fusion.state_ref, bf16[512,1024]{1,0:T(8,128)(2,1)} %gate_ref.1, f32[32,1,128]{2,1,0:T(1,128)} %bitcast.113, ...), custom_call_target="tpu_custom_call" | custom-call | flops 268435456 | bytes 6291456 | tf_op jit(solution)/shard_map/pallas_call | solution.py:153
  48.8 1.5 collective-permute-start.7
  50.3 1.5 fusion
  51.8 1.1 reduce_sum.9
  53.1 0.9 collective-permute-start.20
  53.9 1.3 collective-permute-start.16
  55.2 1.5 convolution_bitcast_fusion.7
  56.7 0.5 fusion.2
  57.2 1.6 collective-permute-start.11
  58.8 0.4 convolution_bitcast_fusion.5
  59.2 1.6 collective-permute-done.11
  60.8 42.7 %collective-permute-done.16 = bf16[1024,512]{1,0:T(8,128)(2,1)S(1)} collective-permute-done((bf16[1024,512]{1,0:T(8,128)(2,1)S(1)}, bf16[1024,512]{1,0:T(8,128)(2,1)S(1)}, u32[]{:S(2)}, u32[]{:S(2)}) %collective-permute-start.16) | collective-permute-done | bytes 1048608 | tf_op jit(solution)/shard_map/ppermute | solution.py:232
  103.6 0.4 fusion.4
  104.1 1.5 fusion.5
  105.7 1.5 fusion.3
  107.3 0.6 collective-permute-start.13
  107.8 1.5 fusion.1
  109.4 0.4 convolution_bitcast_fusion.3
  109.9 1.5 convolution_bitcast_fusion.2
  111.4 1.5 convolution_bitcast_fusion.4
  112.9 1.3 collective-permute-start.21
  114.2 1.5 convolution_bitcast_fusion.6
  115.6 0.2 maximum_add_fusion.2
  115.9 1.6 collective-permute-start.18
  117.5 0.2 maximum_add_fusion
  117.7 0.6 collective-permute-start.9
  118.3 0.2 maximum_add_fusion.1
  118.5 1.6 collective-permute-start.14
  120.1 10.6 %collective-permute-done.9 = bf16[2,128,512]{2,1,0:T(8,128)(2,1)S(1)} collective-permute-done((bf16[2,128,512]{2,1,0:T(8,128)(2,1)S(1)}, bf16[2,128,512]{2,1,0:T(8,128)(2,1)S(1)}, u32[]{:S(2)}, u32[]{:S(2)}) %collective-permute-start.9) | collective-permute-done | bytes 262176 | tf_op jit(solution)/shard_map/ppermute | solution.py:282
  130.8 1.5 collective-permute-start.12
  132.3 3.6 %collective-permute-done.14 = bf16[2,128,512]{2,1,0:T(8,128)(2,1)S(1)} collective-permute-done((bf16[2,128,512]{2,1,0:T(8,128)(2,1)S(1)}, bf16[2,128,512]{2,1,0:T(8,128)(2,1)S(1)}, u32[]{:S(2)}, u32[]{:S(2)}) %collective-permute-start.14) | collective-permute-done | bytes 262176 | tf_op jit(solution)/shard_map/ppermute | solution.py:282
  136.0 1.6 collective-permute-start.15
  137.6 0.6 collective-permute-start.19
  138.6 1.7 %collective-permute-done.21 = bf16[1024,512]{1,0:T(8,128)(2,1)S(1)} collective-permute-done((bf16[1024,512]{1,0:T(8,128)(2,1)S(1)}, bf16[1024,512]{1,0:T(8,128)(2,1)S(1)}, u32[]{:S(2)}, u32[]{:S(2)}) %collective-permute-start.21) | collective-permute-done | bytes 1048608 | tf_op jit(solution)/shard_map/ppermute | solution.py:232
  140.4 0.4 fusion.6
  140.9 1.5 fusion.7
  142.6 0.4 convolution_bitcast_fusion.1
  143.0 1.5 convolution_bitcast_fusion
  144.5 0.2 maximum_add_fusion.3
  144.8 1.6 collective-permute-start.23
  146.5 7.0 %collective-permute-done.23 = bf16[2,128,512]{2,1,0:T(8,128)(2,1)S(1)} collective-permute-done((bf16[2,128,512]{2,1,0:T(8,128)(2,1)S(1)}, bf16[2,128,512]{2,1,0:T(8,128)(2,1)S(1)}, u32[]{:S(2)}, u32[]{:S(2)}) %collective-permute-start.23) | collective-permute-done | bytes 262176 | tf_op jit(solution)/shard_map/ppermute | solution.py:282
  153.6 1.6 collective-permute-start.24
  155.3 3.5 %collective-permute-done.24 = bf16[128,512]{1,0:T(8,128)(2,1)S(1)} collective-permute-done((bf16[128,512]{1,0:T(8,128)(2,1)S(1)}, bf16[128,512]{1,0:T(8,128)(2,1)S(1)}, u32[]{:S(2)}, u32[]{:S(2)}) %collective-permute-start.24) | collective-permute-done | bytes 131104 | tf_op jit(solution)/shard_map/ppermute | solution.py:290
  158.8 0.7 fusion.42
  (73 shorter events, 2.5 us)
Async XLA Ops:
  0.0 16.2 %copy-start.2 = (bf16[1024,512]{1,0:T(8,128)(2,1)S(1)}, bf16[1024,512]{1,0:T(8,128)(2,1)}, u32[]{:S(2)}) copy-start(bf16[1024,512]{1,0:T(8,128)(2,1)} %param.13) | copy-start | bytes 3145732
  5.0 6.5 %collective-permute-start = (bf16[512,128]{1,0:T(8,128)(2,1)S(1)}, bf16[512,128]{1,0:T(8,128)(2,1)S(1)}, u32[]{:S(2)}, u32[]{:S(2)}) collective-permute-start(bf16[512,128]{1,0:T(8,128)(2,1)S(1)} %dynamic-slice_bitcast_fusion), channel_id=1, source_target_pairs={{0,4},{4,0},{8,12},{12,8},{16,20},{20,16},{24,28},{28,24},{1,5},{5... | collective-permute-start | bytes 393224 | tf_op jit(solution)/shard_map/ppermute | solution.py:196
  12.5 7.7 %collective-permute-start.1 = (bf16[512,128]{1,0:T(8,128)(2,1)S(1)}, bf16[512,128]{1,0:T(8,128)(2,1)S(1)}, u32[]{:S(2)}, u32[]{:S(2)}) collective-permute-start(bf16[512,128]{1,0:T(8,128)(2,1)S(1)} %fusion.38), channel_id=1, source_target_pairs={{0,8},{4,12},{16,24},{20,28},{1,9},{5,13},{17,25},{21,29},{2,10},{... | collective-permute-start | bytes 393224 | tf_op jit(solution)/shard_map/ppermute | solution.py:200
  16.2 24.3 %collective-permute-start.5 = (bf16[1024,512]{1,0:T(8,128)(2,1)S(1)}, bf16[1024,512]{1,0:T(8,128)(2,1)S(1)}, u32[]{:S(2)}, u32[]{:S(2)}) collective-permute-start(bf16[1024,512]{1,0:T(8,128)(2,1)S(1)} %copy-done.2), channel_id=1, source_target_pairs={{0,8},{4,12},{8,0},{12,4},{16,24},{20,28},{24,16},{28,20},{1,9},{5... | collective-permute-start | bytes 3145736 | tf_op jit(solution)/shard_map/ppermute | solution.py:232
  16.3 24.2 %collective-permute-start.6 = (bf16[1024,512]{1,0:T(8,128)(2,1)S(1)}, bf16[1024,512]{1,0:T(8,128)(2,1)S(1)}, u32[]{:S(2)}, u32[]{:S(2)}) collective-permute-start(bf16[1024,512]{1,0:T(8,128)(2,1)S(1)} %copy-done.2), channel_id=1, source_target_pairs={{8,16},{12,20},{16,8},{20,12},{9,17},{13,21},{17,9},{21,13},{10,18... | collective-permute-start | bytes 3145736 | tf_op jit(solution)/shard_map/ppermute | solution.py:232
  20.1 3.7 %copy-start.7 = (bf16[512,128]{1,0:T(8,128)(2,1)}, bf16[512,128]{1,0:T(8,128)(2,1)S(1)}, u32[]{:S(2)}) copy-start(bf16[512,128]{1,0:T(8,128)(2,1)S(1)} %collective-permute-done.1) | copy-start | bytes 393220
  21.9 2.0 %collective-permute-start.2 = (bf16[512,128]{1,0:T(8,128)(2,1)}, bf16[512,128]{1,0:T(8,128)(2,1)S(1)}, u32[]{:S(2)}, u32[]{:S(2)}) collective-permute-start(bf16[512,128]{1,0:T(8,128)(2,1)} %fusion.24), channel_id=1, source_target_pairs={{8,16},{12,20},{9,17},{13,21},{10,18},{14,22},{11,19},{15,23}} | collective-permute-start | bytes 393224 | tf_op jit(solution)/shard_map/ppermute | solution.py:203
  22.5 2.0 %collective-permute-start.3 = (bf16[512,128]{1,0:T(8,128)(2,1)}, bf16[512,128]{1,0:T(8,128)(2,1)}, u32[]{:S(2)}, u32[]{:S(2)}) collective-permute-start(bf16[512,128]{1,0:T(8,128)(2,1)} %fusion.24), channel_id=1, source_target_pairs={{8,24},{12,28},{9,25},{13,29},{10,26},{14,30},{11,27},{15,31}} | collective-permute-start | bytes 393224 | tf_op jit(solution)/shard_map/ppermute | solution.py:204
  23.8 0.6 copy-start.8
  26.4 11.2 %collective-permute-start.4 = (bf16[512,128]{1,0:T(8,128)(2,1)}, bf16[512,128]{1,0:T(8,128)(2,1)S(1)}, u32[]{:S(2)}, u32[]{:S(2)}) collective-permute-start(bf16[512,128]{1,0:T(8,128)(2,1)} %get-tuple-element.14), channel_id=1, source_target_pairs={{0,4},{4,0},{8,12},{12,8},{16,20},{20,16},{24,28},{28,24},{1,5},{5... | collective-permute-start | bytes 393224 | tf_op jit(solution)/shard_map/ppermute | solution.py:217
  40.5 1.0 copy-start
  40.6 1.3 copy-start.3
  48.8 4.3 %copy-start.1 = (bf16[1024,512]{1,0:T(8,128)(2,1)S(1)}, bf16[1024,512]{1,0:T(8,128)(2,1)}, u32[]{:S(2)}) copy-start(bf16[1024,512]{1,0:T(8,128)(2,1)} %copy-done) | copy-start | bytes 3145732
  48.8 5.2 %copy-start.4 = (bf16[1024,512]{1,0:T(8,128)(2,1)S(1)}, bf16[1024,512]{1,0:T(8,128)(2,1)}, u32[]{:S(2)}) copy-start(bf16[1024,512]{1,0:T(8,128)(2,1)} %copy-done.3) | copy-start | bytes 3145732
  48.8 55.3 %collective-permute-start.7 = (bf16[512,1024]{1,0:T(8,128)(2,1)}, bf16[512,1024]{1,0:T(8,128)(2,1)}, u32[]{:S(2)}, u32[]{:S(2)}) collective-permute-start(bf16[512,1024]{1,0:T(8,128)(2,1)} %get-tuple-element.11), channel_id=1, source_target_pairs={{0,4},{4,0},{8,12},{12,8},{16,20},{20,16},{24,28},{28,24},{1,5},{5... | collective-permute-start | bytes 3145736 | tf_op jit(solution)/shard_map/ppermute | solution.py:269
  52.9 3.8 %copy-start.5 = (bf16[512,1024]{1,0:T(8,128)(2,1)S(1)}, bf16[512,1024]{1,0:T(8,128)(2,1)}, u32[]{:S(2)}) copy-start(bf16[512,1024]{1,0:T(8,128)(2,1)} %get-tuple-element.11) | copy-start | bytes 3145732
  53.0 4.2 %collective-permute-start.10 = (f32[256]{0:T(256)S(1)}, f32[256]{0:T(256)S(1)}, u32[]{:S(2)}, u32[]{:S(2)}) collective-permute-start(f32[256]{0:T(256)S(1)} %slice.100), channel_id=1, source_target_pairs={{0,1},{1,0},{2,3},{3,2},{4,5},{5,4},{6,7},{7,6},{8,9},{9,8},{10,11... | collective-permute-start | bytes 3080 | tf_op jit(solution)/shard_map/ppermute | solution.py:262
  53.1 59.8 %collective-permute-start.20 = (bf16[1024,512]{1,0:T(8,128)(2,1)S(1)}, bf16[1024,512]{1,0:T(8,128)(2,1)S(1)}, u32[]{:S(2)}, u32[]{:S(2)}) collective-permute-start(bf16[1024,512]{1,0:T(8,128)(2,1)S(1)} %copy-done.1), channel_id=1, source_target_pairs={{8,16},{12,20},{16,8},{20,12},{9,17},{13,21},{17,9},{21,13},{10,18... | collective-permute-start | bytes 3145736 | tf_op jit(solution)/shard_map/ppermute | solution.py:232
  53.9 49.6 %collective-permute-start.16 = (bf16[1024,512]{1,0:T(8,128)(2,1)S(1)}, bf16[1024,512]{1,0:T(8,128)(2,1)S(1)}, u32[]{:S(2)}, u32[]{:S(2)}) collective-permute-start(bf16[1024,512]{1,0:T(8,128)(2,1)S(1)} %copy-done.4), channel_id=1, source_target_pairs={{8,0},{12,4},{16,24},{20,28},{9,1},{13,5},{17,25},{21,29},{10,2},{... | collective-permute-start | bytes 3145736 | tf_op jit(solution)/shard_map/ppermute | solution.py:232
  57.2 3.6 %collective-permute-start.11 = (f32[128]{0:T(128)S(1)}, f32[128]{0:T(128)S(1)}, u32[]{:S(2)}, u32[]{:S(2)}) collective-permute-start(f32[128]{0:T(128)S(1)} %slice.102), channel_id=1, source_target_pairs={{0,2},{1,3},{2,0},{3,1},{4,6},{5,7},{6,4},{7,5},{8,10},{9,11},{10,... | collective-permute-start | bytes 1544 | tf_op jit(solution)/shard_map/ppermute | solution.py:262
  105.6 10.0 %collective-permute-start.17 = (bf16[2,256,512]{2,1,0:T(8,128)(2,1)S(1)}, bf16[2,256,512]{2,1,0:T(8,128)(2,1)S(1)}, u32[]{:S(2)}, u32[]{:S(2)}) collective-permute-start(bf16[2,256,512]{2,1,0:T(8,128)(2,1)S(1)} %pad_maximum_fusion.2), channel_id=1, source_target_pairs={{0,1},{1,0},{2,3},{3,2},{4,5},{5,4},{6,7},{7,6},{8,9},{9,8},{10,11... | collective-permute-start | bytes 1572872 | tf_op jit(solution)/shard_map/ppermute | solution.py:282
  107.3 11.0 %collective-permute-start.13 = (bf16[2,256,512]{2,1,0:T(8,128)(2,1)S(1)}, bf16[2,256,512]{2,1,0:T(8,128)(2,1)S(1)}, u32[]{:S(2)}, u32[]{:S(2)}) collective-permute-start(bf16[2,256,512]{2,1,0:T(8,128)(2,1)S(1)} %pad_maximum_fusion.1), channel_id=1, source_target_pairs={{0,1},{1,0},{2,3},{3,2},{4,5},{5,4},{6,7},{7,6},{8,9},{9,8},{10,11... | collective-permute-start | bytes 1572872 | tf_op jit(solution)/shard_map/ppermute | solution.py:282
  109.4 8.1 %collective-permute-start.8 = (bf16[2,256,512]{2,1,0:T(8,128)(2,1)S(1)}, bf16[2,256,512]{2,1,0:T(8,128)(2,1)S(1)}, u32[]{:S(2)}, u32[]{:S(2)}) collective-permute-start(bf16[2,256,512]{2,1,0:T(8,128)(2,1)S(1)} %pad_maximum_fusion), channel_id=1, source_target_pairs={{0,1},{1,0},{2,3},{3,2},{4,5},{5,4},{6,7},{7,6},{8,9},{9,8},{10,11... | collective-permute-start | bytes 1572872 | tf_op jit(solution)/shard_map/ppermute | solution.py:282
  112.9 27.4 %collective-permute-start.21 = (bf16[1024,512]{1,0:T(8,128)(2,1)S(1)}, bf16[1024,512]{1,0:T(8,128)(2,1)S(1)}, u32[]{:S(2)}, u32[]{:S(2)}) collective-permute-start(bf16[1024,512]{1,0:T(8,128)(2,1)S(1)} %collective-permute-done.20), channel_id=1, source_target_pairs={{8,0},{12,4},{16,24},{20,28},{9,1},{13,5},{17,25},{21,29},{10,2},{... | collective-permute-start | bytes 3145736 | tf_op jit(solution)/shard_map/ppermute | solution.py:232
  115.9 21.7 %collective-permute-start.18 = (bf16[2,128,512]{2,1,0:T(8,128)(2,1)S(1)}, bf16[2,128,512]{2,1,0:T(8,128)(2,1)S(1)}, u32[]{:S(2)}, u32[]{:S(2)}) collective-permute-start(bf16[2,128,512]{2,1,0:T(8,128)(2,1)S(1)} %slice.217), channel_id=1, source_target_pairs={{0,2},{1,3},{2,0},{3,1},{4,6},{5,7},{6,4},{7,5},{8,10},{9,11},{10,... | collective-permute-start | bytes 786440 | tf_op jit(solution)/shard_map/ppermute | solution.py:282
  117.7 13.0 %collective-permute-start.9 = (bf16[2,128,512]{2,1,0:T(8,128)(2,1)S(1)}, bf16[2,128,512]{2,1,0:T(8,128)(2,1)S(1)}, u32[]{:S(2)}, u32[]{:S(2)}) collective-permute-start(bf16[2,128,512]{2,1,0:T(8,128)(2,1)S(1)} %slice.219), channel_id=1, source_target_pairs={{0,2},{1,3},{2,0},{3,1},{4,6},{5,7},{6,4},{7,5},{8,10},{9,11},{10,... | collective-permute-start | bytes 786440 | tf_op jit(solution)/shard_map/ppermute | solution.py:282
  118.5 17.4 %collective-permute-start.14 = (bf16[2,128,512]{2,1,0:T(8,128)(2,1)S(1)}, bf16[2,128,512]{2,1,0:T(8,128)(2,1)S(1)}, u32[]{:S(2)}, u32[]{:S(2)}) collective-permute-start(bf16[2,128,512]{2,1,0:T(8,128)(2,1)S(1)} %slice.218), channel_id=1, source_target_pairs={{0,2},{1,3},{2,0},{3,1},{4,6},{5,7},{6,4},{7,5},{8,10},{9,11},{10,... | collective-permute-start | bytes 786440 | tf_op jit(solution)/shard_map/ppermute | solution.py:282
  130.8 7.7 %collective-permute-start.12 = (bf16[128,512]{1,0:T(8,128)(2,1)S(1)}, bf16[128,512]{1,0:T(8,128)(2,1)S(1)}, u32[]{:S(2)}, u32[]{:S(2)}) collective-permute-start(bf16[128,512]{1,0:T(8,128)(2,1)S(1)} %fusion.44), channel_id=1, source_target_pairs={{0,4},{4,0},{8,12},{12,8},{16,20},{20,16},{24,28},{28,24},{1,5},{5... | collective-permute-start | bytes 393224 | tf_op jit(solution)/shard_map/ppermute | solution.py:290
  136.0 6.5 %collective-permute-start.15 = (bf16[128,512]{1,0:T(8,128)(2,1)S(1)}, bf16[128,512]{1,0:T(8,128)(2,1)S(1)}, u32[]{:S(2)}, u32[]{:S(2)}) collective-permute-start(bf16[128,512]{1,0:T(8,128)(2,1)S(1)} %fusion.46), channel_id=1, source_target_pairs={{0,4},{4,0},{8,12},{12,8},{16,20},{20,16},{24,28},{28,24},{1,5},{5... | collective-permute-start | bytes 393224 | tf_op jit(solution)/shard_map/ppermute | solution.py:290
  137.6 8.8 %collective-permute-start.19 = (bf16[128,512]{1,0:T(8,128)(2,1)S(1)}, bf16[128,512]{1,0:T(8,128)(2,1)S(1)}, u32[]{:S(2)}, u32[]{:S(2)}) collective-permute-start(bf16[128,512]{1,0:T(8,128)(2,1)S(1)} %fusion.48), channel_id=1, source_target_pairs={{0,4},{4,0},{8,12},{12,8},{16,20},{20,16},{24,28},{28,24},{1,5},{5... | collective-permute-start | bytes 393224 | tf_op jit(solution)/shard_map/ppermute | solution.py:290
  142.4 2.1 %collective-permute-start.22 = (bf16[2,256,512]{2,1,0:T(8,128)(2,1)S(1)}, bf16[2,256,512]{2,1,0:T(8,128)(2,1)S(1)}, u32[]{:S(2)}, u32[]{:S(2)}) collective-permute-start(bf16[2,256,512]{2,1,0:T(8,128)(2,1)S(1)} %pad_maximum_fusion.3), channel_id=1, source_target_pairs={{0,1},{1,0},{2,3},{3,2},{4,5},{5,4},{6,7},{7,6},{8,9},{9,8},{10,11... | collective-permute-start | bytes 1572872 | tf_op jit(solution)/shard_map/ppermute | solution.py:282
  144.8 8.8 %collective-permute-start.23 = (bf16[2,128,512]{2,1,0:T(8,128)(2,1)S(1)}, bf16[2,128,512]{2,1,0:T(8,128)(2,1)S(1)}, u32[]{:S(2)}, u32[]{:S(2)}) collective-permute-start(bf16[2,128,512]{2,1,0:T(8,128)(2,1)S(1)} %slice.216), channel_id=1, source_target_pairs={{0,2},{1,3},{2,0},{3,1},{4,6},{5,7},{6,4},{7,5},{8,10},{9,11},{10,... | collective-permute-start | bytes 786440 | tf_op jit(solution)/shard_map/ppermute | solution.py:282
  153.6 5.2 %collective-permute-start.24 = (bf16[128,512]{1,0:T(8,128)(2,1)S(1)}, bf16[128,512]{1,0:T(8,128)(2,1)S(1)}, u32[]{:S(2)}, u32[]{:S(2)}) collective-permute-start(bf16[128,512]{1,0:T(8,128)(2,1)S(1)} %fusion.50), channel_id=1, source_target_pairs={{0,4},{4,0},{8,12},{12,8},{16,20},{20,16},{24,28},{28,24},{1,5},{5... | collective-permute-start | bytes 393224 | tf_op jit(solution)/shard_map/ppermute | solution.py:290
  155.3 3.5 %copy-start.6 = (bf16[128,4096]{1,0:T(8,128)(2,1)}, bf16[128,4096]{1,0:T(8,128)(2,1)S(1)}, u32[]{:S(2)}) copy-start(bf16[128,4096]{1,0:T(8,128)(2,1)S(1)} %fusion.49) | copy-start | bytes 3145732

commit v3 on v0

v3 whole, which is shorter than its diff:
```python
import functools

import jax
import jax.numpy as jnp
from jax import lax
from jax.experimental import pallas as pl
from jax.experimental.pallas import tpu as pltpu
from jax.sharding import PartitionSpec as P

DH = 128
BLOCK = 512
LINE = 4
VMEM_BYTES = 48 * 1024 * 1024


epsilon = 1e-05


def line_pairs(n_seq, hops):
    inner = n_seq // LINE
    return [(a * inner + i, b * inner + i) for a, b in hops for i in range(inner)]


def turn_pairs(n_seq, turn):
    inner = n_seq // LINE
    return [(a * inner + i, a * inner + (i + turn) % inner) for a in range(LINE) for i in range(inner)]


def flip_pairs(n_head, bit):
    return [(h, h ^ bit) for h in range(n_head)]


SWAP_OUTER = [(0, 1), (1, 0), (2, 3), (3, 2)]
SWAP_MIDDLE = [(1, 2), (2, 1)]
TO_ENDS = [(1, 0), (2, 3)]


def hold(value, *others):
    return lax.optimization_barrier((value, *others))[0]


def scalars(*values):
    return jnp.stack([jnp.asarray(value, jnp.int32) for value in values])


def states_kernel(part_ref, k_ref, v_ref, out_ref):
    for index in range(out_ref.shape[0]):
        columns = pl.ds(index * DH, DH)
        out_ref[index] = lax.dot_general(
            k_ref[:, columns],
            v_ref[:, columns],
            (((0,), (0,)), ((), ())),
            preferred_element_type=jnp.float32,
        ).astype(out_ref.dtype)


def block_states(key_input, value_input, part, heads, dtype):
    rows = key_input.shape[0]
    at_once = 2 if heads % 2 == 0 else 1
    steps = heads // at_once
    rows_spec = pl.BlockSpec((rows, at_once * DH), lambda step, part_ref: (0, part_ref[0] * steps + step))
    return pl.pallas_call(
        states_kernel,
        grid_spec=pltpu.PrefetchScalarGridSpec(
            num_scalar_prefetch=1,
            grid=(steps,),
            in_specs=[rows_spec, rows_spec],
            out_specs=pl.BlockSpec((at_once, DH, DH), lambda step, part_ref: (step, 0, 0)),
        ),
        out_shape=jax.ShapeDtypeStruct((heads, DH, DH), dtype),
        cost_estimate=pl.CostEstimate(
            flops=2 * rows * heads * DH * DH, bytes_accessed=4 * rows * heads * DH, transcendentals=0
        ),
    )(scalars(part), key_input, value_input)


def state_prefix(key_input, value_input, n_seq, place, early):
    inner = n_seq // LINE
    i = place % inner
    heads = key_input.shape[1] // DH
    split = heads % inner == 0
    share = heads // inner if split else heads
    sends = []
    if split:
        for turn in range(1, inner):
            sends.append(block_states(key_input, value_input, (i + turn) % inner, share, jnp.bfloat16))
        own = block_states(key_input, value_input, i, share, jnp.float32)
    else:
        own = block_states(key_input, value_input, 0, share, jnp.float32)
        sends = [own.astype(jnp.bfloat16)] * (inner - 1)
    members = [(i, own)]
    for turn in range(1, inner):
        got = lax.ppermute(sends[turn - 1], "seq", turn_pairs(n_seq, turn))
        members.append(((i - turn) % inner, got.astype(jnp.float32)))
    group_sum = sum(value for _, value in members)
    first = hold(group_sum.astype(jnp.bfloat16), *early)
    from_left = lax.ppermute(first, "seq", line_pairs(n_seq, [(0, 1), (2, 3)])).astype(jnp.float32)
    second = (group_sum + from_left).astype(jnp.bfloat16)
    near = lax.ppermute(second, "seq", line_pairs(n_seq, [(1, 2)]))
    far = lax.ppermute(second, "seq", line_pairs(n_seq, [(1, 3)]))
    entering = from_left + near.astype(jnp.float32) + far.astype(jnp.float32)

    def before(member):
        total = entering
        for owner, value in members:
            total = total + jnp.where(owner < member, value, 0.0)
        return total

    terms = [before(i)]
    if split:
        for turn in range(1, inner):
            sent = before((i + turn) % inner).astype(jnp.bfloat16)
            terms.append(lax.ppermute(sent, "seq", turn_pairs(n_seq, turn)))
    return terms, near


def causal_kernel(q_ref, k_ref, v_ref, *rest):
    out_ref = rest[-1]
    rows = q_ref.shape[0]
    half = rows // 2
    top, bottom = pl.ds(0, half), pl.ds(half, half)
    keep = lax.broadcasted_iota(jnp.int32, (half, half), 0) >= lax.broadcasted_iota(
        jnp.int32, (half, half), 1
    )

    def scores(q_rows, k_rows, columns):
        return lax.dot_general(
            q_ref[q_rows, columns],
            k_ref[k_rows, columns],
            (((1,), (1,)), ((), ())),
            preferred_element_type=jnp.float32,
        )

    for index in range(q_ref.shape[1] // DH):
        columns = pl.ds(index * DH, DH)
        first = jnp.where(keep, scores(top, top, columns), 0.0).astype(jnp.bfloat16)
        below = scores(bottom, top, columns).astype(jnp.bfloat16)
        last = jnp.where(keep, scores(bottom, bottom, columns), 0.0).astype(jnp.bfloat16)
        out_ref[top, columns] = jnp.dot(first, v_ref[top, columns], preferred_element_type=jnp.float32)
        out_ref[bottom, columns] = jnp.dot(
            jnp.concatenate([below, last], axis=1),
            v_ref[:, columns],
            preferred_element_type=jnp.float32,
        )


def causal_part(queries, key_input, value_input, first_head, heads, filled=None):
    rows, width = queries.shape
    at_once = 2 if heads % 2 == 0 and first_head % 2 == 0 else 1
    base = first_head // at_once
    spec = pl.BlockSpec((rows, at_once * DH), lambda step: (0, base + step))
    operands, specs, aliases = [queries, key_input, value_input], [spec] * 3, {}
    if filled is not None:
        operands.append(filled)
        specs.append(pl.BlockSpec(memory_space=pl.ANY))
        aliases = {3: 0}
    return pl.pallas_call(
        causal_kernel,
        grid=(heads // at_once,),
        in_specs=specs,
        out_specs=spec,
        out_shape=jax.ShapeDtypeStruct((rows, width), jnp.float32),
        input_output_aliases=aliases,
        cost_estimate=pl.CostEstimate(
            flops=4 * rows * rows * heads * DH,
            bytes_accessed=10 * rows * heads * DH,
            transcendentals=0,
        ),
    )(*operands)


def hidden_kernel(order, share, group, place_ref, q_ref, inner_ref, gate_ref, gain_ref, kv_ref, *rest):
    hidden_ref, squares_ref = rest[-2:]
    terms = rest[:group]
    state = kv_ref[0]
    if group == 1:
        state = state + terms[0][0]
    else:
        part = pl.program_id(0) // share
        for turn, term in enumerate(terms):
            covers = lax.rem(place_ref[1] - turn + group, group)
            state = state + jnp.where(part == covers, term[0].astype(jnp.float32), 0.0)
    high = state.astype(jnp.bfloat16)
    low = (state - high.astype(jnp.float32)).astype(jnp.bfloat16)
    both = jnp.concatenate([high, low], axis=0)
    size = q_ref.shape[0] // len(order)
    half_gain = gain_ref[0] * 0.5
    first = pl.program_id(0) == 0
    for position, block in enumerate(order):
        start = pl.multiple_of((place_ref[0] ^ block) * size, size)
        rows = pl.ds(start, size)
        q_rows = q_ref[rows, :]
        carried = jnp.dot(
            jnp.concatenate([q_rows, q_rows], axis=1), both, preferred_element_type=jnp.float32
        )
        attn = (carried + inner_ref[rows, :]).astype(jnp.bfloat16).astype(jnp.float32)
        gate = 1.0 + jnp.tanh(gate_ref[rows, :].astype(jnp.float32) * 0.5)
        placed = pl.ds(position * size, size)
        hidden_ref[placed, :] = (attn * (half_gain * gate)).astype(jnp.bfloat16)
        square = attn * attn
        squares_ref[placed, :] = jnp.where(first, square, squares_ref[placed, :] + square)


def gated_hidden(queries, inner_part, kv_state, terms, gate_input, norm_gain, h, i, order):
    rows, width = queries.shape
    heads = width // DH
    group = len(terms)
    share = heads // group
    columns = pl.BlockSpec((rows, DH), lambda head, place_ref: (0, head))
    return pl.pallas_call(
        functools.partial(hidden_kernel, order, share, group),
        grid_spec=pltpu.PrefetchScalarGridSpec(
            num_scalar_prefetch=1,
            grid=(heads,),
            in_specs=[
                columns,
                columns,
                columns,
                pl.BlockSpec((1, 1, DH), lambda head, place_ref: (place_ref[0] * heads + head, 0, 0)),
                pl.BlockSpec((1, DH, DH), lambda head, place_ref: (head, 0, 0)),
            ]
            + [pl.BlockSpec((1, DH, DH), lambda head, place_ref: (head % share, 0, 0))] * group,
            out_specs=[columns, pl.BlockSpec((rows, DH), lambda head, place_ref: (0, 0))],
        ),
        out_shape=[
            jax.ShapeDtypeStruct((rows, width), jnp.bfloat16),
            jax.ShapeDtypeStruct((rows, DH), jnp.float32),
        ],
        cost_estimate=pl.CostEstimate(
            flops=4 * rows * width * DH, bytes_accessed=12 * rows * width, transcendentals=rows * width
        ),
    )(
        scalars(h, i),
        queries,
        inner_part,
        gate_input,
        norm_gain.reshape(-1, 1, DH),
        kv_state,
        *terms,
    )


def project_kernel(groups, choices, flag_ref, *refs):
    rows_refs = refs[:groups]
    weight_refs = refs[groups : groups + sum(choices)]
    sent_ref, kept_ref, rows_buf, weight_buf, rows_sem, weight_sem = refs[groups + sum(choices) :]

    def rows_copy(group):
        return pltpu.make_async_copy(rows_refs[group], rows_buf.at[group % 2], rows_sem.at[group % 2])

    rows_copy(0).start()
    first = 0
    waits = []
    for index, number in enumerate(choices):
        copies = [
            pltpu.make_async_copy(weight_refs[first + k], weight_buf.at[index], weight_sem.at[index])
            for k in range(number)
        ]
        if number == 1:
            copies[0].start()
        else:
            for k in range(number):
                pl.when(flag_ref[0] == k)(copies[k].start)
        waits.append(copies[0])
        first += number
    half = sent_ref.shape[1]
    width = weight_buf.shape[2]
    for group in range(groups):
        if group + 1 < groups:
            rows_copy(group + 1).start()
        rows_copy(group).wait()
        for index in range(len(choices)):
            if group == 0:
                waits[index].wait()
            columns = pl.ds(index * width, width)
            product = jnp.dot(
                rows_buf[group % 2], weight_buf[index], preferred_element_type=jnp.float32
            )
            kept_ref[group, :, columns] = product[:half]
            sent_ref[group, :, columns] = product[half:].astype(jnp.bfloat16)


def project(rows_list, weights, flag):
    groups = len(rows_list)
    flat = [choice for weight in weights for choice in weight]
    choices = tuple(len(weight) for weight in weights)
    rows, depth = rows_list[0].shape
    width = flat[0].shape[1]
    shape = (groups, rows // 2, width * len(weights))
    return pl.pallas_call(
        functools.partial(project_kernel, groups, choices),
        in_specs=[pl.BlockSpec(memory_space=pltpu.SMEM)]
        + [pl.BlockSpec(memory_space=pl.ANY)] * (groups + len(flat)),
        out_specs=[pl.BlockSpec(memory_space=pltpu.VMEM)] * 2,
        out_shape=[
            jax.ShapeDtypeStruct(shape, jnp.bfloat16),
            jax.ShapeDtypeStruct(shape, jnp.float32),
        ],
        scratch_shapes=[
            pltpu.VMEM((2, rows, depth), jnp.bfloat16),
            pltpu.VMEM((len(weights), depth, width), jnp.bfloat16),
            pltpu.SemaphoreType.DMA((2,)),
            pltpu.SemaphoreType.DMA((len(weights),)),
        ],
        compiler_params=pltpu.CompilerParams(vmem_limit_bytes=VMEM_BYTES),
        cost_estimate=pl.CostEstimate(
            flops=2 * groups * rows * depth * width * len(weights),
            bytes_accessed=2 * depth * (groups * rows + width * len(weights)),
            transcendentals=0,
        ),
    )(flag, *rows_list, *flat)


def placed_kernel(counts, cut, starts_ref, scale_ref, *refs):
    pieces = refs[: len(counts)]
    out_ref = refs[-1]
    where = 0
    for piece, count in zip(pieces, counts):
        for index in range(count):
            part = piece[:, pl.ds(index * cut, cut)].astype(jnp.float32) * scale_ref[...]
            start = pl.multiple_of(starts_ref[where], DH)
            out_ref[:, pl.ds(start, cut)] = part.astype(out_ref.dtype)
            where += 1


def added_kernel(counts, cut, starts_ref, scale_ref, *refs):
    pieces = refs[: len(counts)]
    out_ref, buf, sem = refs[-3:]
    where = 0
    copies = []
    for piece, count in zip(pieces, counts):
        for index in range(count):
            part = piece[:, pl.ds(index * cut, cut)].astype(jnp.float32) * scale_ref[...]
            buf[where] = part.astype(out_ref.dtype)
            start = pl.multiple_of(starts_ref[where], DH)
            copy = pltpu.make_async_copy(buf.at[where], out_ref.at[:, pl.ds(start, cut)], sem.at[where])
            copy.start()
            copies.append(copy)
            where += 1
    for copy in copies:
        copy.wait()


def placed(filled, pieces, scale, cut, shape):
    counts = tuple(len(starts) for _, starts in pieces)
    starts = scalars(*[start for _, own in pieces for start in own])
    operands = [starts, scale[:, None]] + [piece for piece, _ in pieces]
    in_specs = [pl.BlockSpec(memory_space=pltpu.SMEM)] + [
        pl.BlockSpec(memory_space=pltpu.VMEM)
    ] * (len(operands) - 1)
    out_shape = jax.ShapeDtypeStruct(shape, jnp.bfloat16)
    params = pltpu.CompilerParams(vmem_limit_bytes=VMEM_BYTES)
    cost = pl.CostEstimate(
        flops=shape[0] * cut * sum(counts),
        bytes_accessed=6 * shape[0] * cut * sum(counts),
        transcendentals=0,
    )
    if filled is None:
        return pl.pallas_call(
            functools.partial(placed_kernel, counts, cut),
            in_specs=in_specs,
            out_specs=pl.BlockSpec(memory_space=pltpu.VMEM),
            out_shape=out_shape,
            compiler_params=params,
            cost_estimate=cost,
        )(*operands)
    return pl.pallas_call(
        functools.partial(added_kernel, counts, cut),
        in_specs=in_specs + [pl.BlockSpec(memory_space=pl.ANY)],
        out_specs=pl.BlockSpec(memory_space=pl.ANY),
        out_shape=out_shape,
        scratch_shapes=[
            pltpu.VMEM((sum(counts), shape[0], cut), jnp.bfloat16),
            pltpu.SemaphoreType.DMA((sum(counts),)),
        ],
        input_output_aliases={len(operands): 0},
        compiler_params=params,
        cost_estimate=cost,
    )(*operands, filled)


def shards(queries, key_input, value_input, gate_input, kv_state, norm_gain, out_weight):
    n_seq, n_head = lax.axis_size("seq"), lax.axis_size("head")
    inner = n_seq // LINE
    place, h = lax.axis_index("seq"), lax.axis_index("head")
    z, i = place // inner, place % inner
    tok_rows, local_width = queries.shape
    assert tok_rows == BLOCK
    heads = local_width // DH
    total_width = local_width * n_head
    width = out_weight.shape[1]
    cuts = 2 if width % (2 * DH) == 0 else 1
    cut = width // cuts

    def along(value, hops):
        return lax.ppermute(value, "seq", line_pairs(n_seq, hops))

    w_cuts = [out_weight[:, k * cut : (k + 1) * cut] for k in range(cuts)]
    w_pair = [along(w_cuts[0], SWAP_OUTER)]
    w_mid1 = [along(w_cuts[0], SWAP_MIDDLE)]
    terms, near = state_prefix(
        key_input, value_input, n_seq, place, [w_pair[0], w_mid1[0]]
    )
    some = heads // 2
    inner_part = causal_part(queries, key_input, value_input, 0, some)

    w_mid2, w_end1, w_end2 = [], [], []
    for k in range(cuts):
        if k:
            w_next = hold(w_cuts[k], near)
            w_pair.append(along(w_next, SWAP_OUTER))
            w_mid1.append(along(w_next, SWAP_MIDDLE))
        w_mid2.append(along(hold(w_pair[k], near), SWAP_MIDDLE))
        w_end1.append(along(hold(w_mid1[k], near), TO_ENDS))
    for k in range(cuts):
        w_end2.append(along(w_mid2[k], TO_ENDS))
    inner_part = causal_part(queries, key_input, value_input, some, heads - some, inner_part)

    bits = n_head.bit_length() - 1
    order = [int(format(j, "b").zfill(bits)[::-1], 2) for j in range(n_head)] if bits else [0]
    terms[0] = hold(terms[0], *w_pair[1:], *w_mid1[1:])
    hidden, squares = gated_hidden(
        queries, inner_part, kv_state, terms, gate_input, norm_gain, h, i, order
    )
    others = [lax.ppermute(hidden, "seq", turn_pairs(n_seq, turn)) for turn in range(1, inner)]

    squares = jnp.sum(squares, axis=1)
    out_rows = tok_rows // n_head
    half, bit = tok_rows // 2, 1
    while bit < n_head:
        squares = squares[:half] + lax.ppermute(squares[half:], "head", flip_pairs(n_head, bit))
        half //= 2
        bit *= 2
    scale = lax.rsqrt(squares / total_width + epsilon)

    is_end = (z == 0) | (z == LINE - 1)
    low = z < LINE // 2
    own_block, pair_block = z, z ^ 1
    third_block = jnp.where(low, 2, 1)
    fourth_block = jnp.where(low, 3, 0)
    flag = scalars(is_end)

    def summed(flag, rows_list, members, weights, blocks):
        sent, kept = project(rows_list, weights, flag)
        flag = hold(flag, sent)
        half, bit = tok_rows // 2, 1
        while bit < n_head:
            kept = kept + lax.ppermute(sent, "head", flip_pairs(n_head, bit)).astype(jnp.float32)
            half = half // 2
            bit *= 2
            if bit < n_head:
                sent = kept[:, half:].astype(jnp.bfloat16)
                kept = kept[:, :half]
        pieces = []
        for position, turn in enumerate(members):
            piece = kept[position]
            if turn:
                piece = lax.ppermute(piece.astype(jnp.bfloat16), "seq", turn_pairs(n_seq, -turn))
            starts = [(block * inner + (i + turn) % inner) * width + k * cut for block, k in blocks]
            pieces.append((piece, starts))
        return pieces, flag

    own_turn, other_turns = [0], list(range(1, inner))
    early_weights = [(w,) for w in w_cuts] + [(w,) for w in w_pair]
    early_blocks = [(own_block, k) for k in range(cuts)] + [(pair_block, k) for k in range(cuts)]
    third = [(w_mid1[k], w_end1[k]) for k in range(cuts)]
    fourth = [(w_mid2[k], w_end2[k]) for k in range(cuts)]
    rows_list, turns = [hidden] + others, own_turn + other_turns
    pieces, flag = summed(flag, [hidden], own_turn, early_weights, early_blocks)
    if others:
        more, flag = summed(flag, others, other_turns, early_weights, early_blocks)
        pieces += more
    more, flag = summed(flag, rows_list, turns, third, [(third_block, k) for k in range(cuts)])
    pieces += more
    for k in range(cuts):
        last, flag = summed(flag, rows_list, turns, [fourth[k]], [(fourth_block, k)])
        if k + 1 < cuts:
            pieces += last
    shape = (out_rows, width * n_seq)
    if cut % DH == 0:
        return placed(placed(None, pieces, scale, cut, shape), last, scale, cut, shape)
    output = jnp.zeros(shape, jnp.bfloat16)
    for piece, starts in pieces + last:
        piece = (piece.astype(jnp.float32) * scale[:, None]).astype(jnp.bfloat16)
        for index, start in enumerate(starts):
            part = piece[:, index * cut : (index + 1) * cut]
            output = lax.dynamic_update_slice_in_dim(output, part, start, 1)
    return output


def solution(mesh):
    in_specs = (
        P("seq", "head"),
        P("seq", "head"),
        P("seq", "head"),
        P("seq", "head"),
        P("head", None, None),
        P(),
        P("head", "seq"),
    )
    out_specs = P(("seq", "head"), None)
    return jax.shard_map(shards, mesh=mesh, in_specs=in_specs, out_specs=out_specs, check_vma=False)
```

time: 247 us -> 154 us (0.62)
  waiting for transfers between devices: 184 us -> 63.2 us
  Pallas kernels: 0 us -> 36.1 us
  starting transfers between devices: 7.12 us -> 42.1 us
  matrix products: 19.5 us -> 0 us
  blocking collectives: 16.9 us -> 0 us
  between operations: 13.2 us -> 0.67 us
  other arithmetic: 1.4 us -> 5.55 us
    all_gather x2 -> x0, waiting for transfers between devices: 113 us -> none  [the longest x1 62 us: shards(): lax.all_gather(out_weight, 'seq', axis=1, tiled=True)]
    ppermute x0 -> x32, waiting for transfers between devices: none -> 63.2 us  [the longest x10 38.7 us: along(): return lax.ppermute(value, 'seq', line_pairs(n_seq, hops))]
    reduce_scatter x1 -> x0, waiting for transfers between devices: 42.9 us -> none  [shards(): lax.psum_scatter(terms.astype(jnp.bfloat16), 'head', scatter_dimension=0,...]
    ppermute x0 -> x32, starting transfers between devices: none -> 42.1 us  [the longest x10 17.6 us: along(): return lax.ppermute(value, 'seq', line_pairs(n_seq, hops))]
    pallas_call x0 -> x12, Pallas kernels: none -> 36.1 us  [the longest x5 14.3 us: project(): pl.pallas_call(functools.partial(project_kernel, groups, choices), in_spe...]
    all_to_all x2 -> x0, waiting for transfers between devices: 26.9 us -> none  [the longest x1 13.8 us: shards(): lax.all_to_all(gate_input, 'head', split_axis=0, concat_axis=1, tiled=True)]
    dot_general x4 -> x0, matrix products: 19.5 us -> none  [the longest x1 9.4 us: shards(): jnp.dot(hidden, lax.all_gather(out_weight, 'seq', axis=1, tiled=True), pr...]
    all_to_all x1 -> x0, blocking collectives: 16.9 us -> none  [shards(): lax.all_to_all(normed, 'head', split_axis=1, concat_axis=0, tiled=True)]
  transfers between devices with their start and end apart: 5 -> 32, of which waited for: 5 -> 15; matrix products, arithmetic and copies ran while one was open for 5% -> 3% of each run, Pallas kernels for 0% -> 18%
where the time goes in v3:
time: 154 us; the launch traced here: 153 us
  waiting for transfers between devices  63.2 us (41%)
  starting transfers between devices  42.1 us (27%)
  Pallas kernels  36.1 us (23%)
  local copies, waits for them, and re-layouts  5.7 us (4%)
  other arithmetic  5.55 us (4%)
    ppermute x10, waiting for transfers between devices, along(): return lax.ppermute(value, 'seq', line_pairs(n_seq, hops))  38.7 us
    ppermute x10, starting transfers between devices, along(): return lax.ppermute(value, 'seq', line_pairs(n_seq, hops))  17.6 us
    ppermute x10, waiting for transfers between devices, summed(): lax.ppermute(sent, 'head', flip_pairs(n_head, bit)).astype(jnp.float32)  14.8 us
    pallas_call x5, Pallas kernels, project(): pl.pallas_call(functools.partial(project_kernel, groups, choices), in_spe...  14.3 us
    pallas_call x1, Pallas kernels, gated_hidden(): pl.pallas_call(functools.partial(hidden_kernel, order, share, group), gri...  7.68 us
    ppermute x10, starting transfers between devices, summed(): lax.ppermute(sent, 'head', flip_pairs(n_head, bit)).astype(jnp.float32)  6.59 us
    ppermute x1, starting transfers between devices, state_prefix(): lax.ppermute(first, 'seq', line_pairs(n_seq, [(0, 1), (2, 3)]))  6.55 us
    pallas_call x2, Pallas kernels, causal_part(): pl.pallas_call(causal_kernel, grid=(heads // at_once,), in_specs=specs, o...  6.51 us
  transfers between devices with their start and end apart: 32, of which 15 were waited for; matrix products, arithmetic and copies ran while one was open for 3% of the time, Pallas kernels for 18%

profile of v3, /device:TPU:0, one launch (start us, length us, event | category | flops | bytes accessed | tf_op | source)
XLA Modules:
  0.0 153.3 jit_solution(5897396189662898897)
XLA Ops:
  0.0 1.3 fusion.12
  1.3 3.1 %collective-permute-start.1 = (bf16[1024,256]{1,0:T(8,128)(2,1)S(1)}, bf16[1024,256]{1,0:T(8,128)(2,1)}, u32[]{:S(2)}, u32[]{:S(2)}) collective-permute-start(bf16[1024,256]{1,0:T(8,128)(2,1)S(1)} %get-tuple-element.52.refs_1_), channel_id=1, source_target_pairs={{0,8},{4,12},{8,0},{12,4},{16,24},{20,28},{24,16},{28,20},{1,9},{5... | collective-permute-start | bytes 1572872 | tf_op jit(solution)/shard_map/ppermute | solution.py:396
  4.4 0.7 collective-permute-start.2
  5.1 2.3 %shard_map.76 = bf16[4,128,128]{2,1,0:T(8,128)(2,1)} custom-call(s32[1]{0:T(128)} %bitcast.5.part_ref, bf16[512,1024]{1,0:T(8,128)(2,1)} %k_ref.7, bf16[512,1024]{1,0:T(8,128)(2,1)} %v_ref.7), custom_call_target="tpu_custom_call" | custom-call | flops 67108864 | bytes 1048576 | tf_op jit(solution)/shard_map/pallas_call | solution.py:62
  7.4 1.5 collective-permute-start
  8.8 2.3 %shard_map.75 = f32[4,128,128]{2,1,0:T(8,128)} custom-call(s32[1]{0:T(128)} %bitcast.3.part_ref, bf16[512,1024]{1,0:T(8,128)(2,1)} %k_ref.7, bf16[512,1024]{1,0:T(8,128)(2,1)} %v_ref.7), custom_call_target="tpu_custom_call" | custom-call | flops 67108864 | bytes 1048576 | tf_op jit(solution)/shard_map/pallas_call | solution.py:62
  11.1 1.4 collective-permute-done
  12.5 1.0 fusion.8
  13.5 2.9 %collective-permute-done.1.refs_3_ = bf16[1024,256]{1,0:T(8,128)(2,1)} collective-permute-done((bf16[1024,256]{1,0:T(8,128)(2,1)S(1)}, bf16[1024,256]{1,0:T(8,128)(2,1)}, u32[]{:S(2)}, u32[]{:S(2)}) %collective-permute-start.1) | collective-permute-done | bytes 524320 | tf_op jit(solution)/shard_map/ppermute | solution.py:396
  16.4 6.6 %collective-permute-start.3 = (bf16[4,128,128]{2,1,0:T(8,128)(2,1)S(1)}, bf16[4,128,128]{2,1,0:T(8,128)(2,1)S(1)}, u32[]{:S(2)}, u32[]{:S(2)}) collective-permute-start(bf16[4,128,128]{2,1,0:T(8,128)(2,1)S(1)} %fusion.8), channel_id=1, source_target_pairs={{0,8},{4,12},{16,24},{20,28},{1,9},{5,13},{17,25},{21,29},{2,10},{... | collective-permute-start | bytes 393224 | tf_op jit(solution)/shard_map/ppermute | solution.py:97
  23.0 2.5 %collective-permute-done.3 = bf16[4,128,128]{2,1,0:T(8,128)(2,1)S(1)} collective-permute-done((bf16[4,128,128]{2,1,0:T(8,128)(2,1)S(1)}, bf16[4,128,128]{2,1,0:T(8,128)(2,1)S(1)}, u32[]{:S(2)}, u32[]{:S(2)}) %collective-permute-start.3) | collective-permute-done | bytes 131104 | tf_op jit(solution)/shard_map/ppermute | solution.py:97
  25.5 1.0 fusion.2
  26.5 0.7 collective-permute-start.4
  27.1 0.7 collective-permute-start.5
  27.8 4.9 %collective-permute-start.6 = (bf16[1024,256]{1,0:T(8,128)(2,1)S(1)}, bf16[1024,256]{1,0:T(8,128)(2,1)}, u32[]{:S(2)}, u32[]{:S(2)}) collective-permute-start(bf16[1024,256]{1,0:T(8,128)(2,1)S(1)} %get-tuple-element.29.refs_2_), channel_id=1, source_target_pairs={{0,8},{4,12},{8,0},{12,4},{16,24},{20,28},{24,16},{28,20},{1,9},{5... | collective-permute-start | bytes 1572872 | tf_op jit(solution)/shard_map/ppermute | solution.py:396
  32.7 0.7 collective-permute-start.7
  33.5 3.3 %shard_map.73.rest_0_ = f32[512,1024]{1,0:T(8,128)} custom-call(bf16[512,1024]{1,0:T(8,128)(2,1)} %q_ref.5, bf16[512,1024]{1,0:T(8,128)(2,1)} %k_ref.7, bf16[512,1024]{1,0:T(8,128)(2,1)} %v_ref.7), custom_call_target="tpu_custom_call" | custom-call | flops 536870912 | bytes 2621440 | tf_op jit(solution)/shard_map/pallas_call | solution.py:157
  36.8 0.8 fusion.6
  37.6 1.5 collective-permute-start.8
  39.1 3.2 %shard_map.74.inner_ref = f32[512,1024]{1,0:T(8,128)} custom-call(bf16[512,1024]{1,0:T(8,128)(2,1)} %q_ref.5, bf16[512,1024]{1,0:T(8,128)(2,1)} %k_ref.7, bf16[512,1024]{1,0:T(8,128)(2,1)} %v_ref.7, f32[512,1024]{1,0:T(8,128)} %shard_map.73.rest_0_), custom_call_target="tpu_custom_call", output_to_operand_aliasing={{}: (3, {})} | custom-call | flops 536870912 | bytes 2621440 | tf_op jit(solution)/shard_map/pallas_call | solution.py:157
  42.3 0.6 pad_add_fusion.1.place_ref
  42.9 0.7 copy-done.10
  43.6 7.7 %shard_map.77 = (bf16[512,1024]{1,0:T(8,128)(2,1)}, f32[512,128]{1,0:T(8,128)}) custom-call(s32[2]{0:T(128)} %pad_add_fusion.1.place_ref, bf16[512,1024]{1,0:T(8,128)(2,1)} %q_ref.5, f32[512,1024]{1,0:T(8,128)} %shard_map.74.inner_ref, bf16[512,1024]{1,0:T(8,128)(2,1)} %gate_ref.1, f32[32,1,128]{2,1,0:T(1,128)} %bitcast.39, f32[8,128,128]{2,1,0:T(8,128)} %kv_ref.1, ...), custom_call_target="tpu_custom_call" | custom-call | flops 268435456 | bytes 6291456 | tf_op jit(solution)/shard_map/pallas_call | solution.py:210
  51.3 1.1 collective-permute-start.11
  52.4 1.5 collective-permute-start.14
  53.9 1.5 collective-permute-start.16
  55.4 1.2 copy-done
  56.6 1.0 copy-done.3
  57.6 1.0 copy-done.6
  58.7 3.8 %shard_map.78 = (bf16[1,256,1024]{2,1,0:T(8,128)(2,1)}, f32[1,256,1024]{2,1,0:T(8,128)S(1)}) custom-call(s32[1]{0:T(128)} %bitcast.7.flag_ref, bf16[512,1024]{1,0:T(8,128)(2,1)S(1)} %copy-done, bf16[1024,256]{1,0:T(8,128)(2,1)S(1)} %copy-done.6, bf16[1024,256]{1,0:T(8,128)(2,1)S(1)} %copy-done.3, bf16[1024,256]{1,0:T(8,128)(2,1)} %collective-permute-done.1.refs_3_, ...), custom_call_target="tpu_custom_call" | custom-call | flops 1073741824 | bytes 3145728 | tf_op jit(solution)/shard_map/pallas_call | solution.py:290
  62.8 0.6 collective-permute-start.9
  63.3 1.1 collective-permute-done.9
  64.4 1.5 collective-permute-start.10
  66.1 1.3 collective-permute-start.12
  67.4 0.6 collective-permute-done.10
  68.0 1.3 collective-permute-start.13
  69.3 1.3 collective-permute-start.15
  70.7 1.4 collective-permute-start.17
  72.2 1.2 convert_add_fusion.2
  73.4 1.6 %collective-permute-start.22 = (bf16[1,128,1024]{2,1,0:T(8,128)(2,1)S(1)}, bf16[1,128,1024]{2,1,0:T(8,128)(2,1)S(1)}, u32[]{:S(2)}, u32[]{:S(2)}) collective-permute-start(bf16[1,128,1024]{2,1,0:T(8,128)(2,1)S(1)} %slice.144), channel_id=1, source_target_pairs={{0,2},{1,3},{2,0},{3,1},{4,6},{5,7},{6,4},{7,5},{8,10},{9,11},{10,... | collective-permute-start | bytes 786440 | tf_op jit(solution)/shard_map/ppermute | solution.py:448
  75.0 3.0 %shard_map.79 = (bf16[1,256,1024]{2,1,0:T(8,128)(2,1)S(1)}, f32[1,256,1024]{2,1,0:T(8,128)S(1)}) custom-call(s32[1]{0:T(128)} %bitcast.7.flag_ref, bf16[512,1024]{1,0:T(8,128)(2,1)S(1)} %collective-permute-done.11.refs_0_.refs_1_, bf16[1024,256]{1,0:T(8,128)(2,1)S(1)} %copy-done.7, bf16[1024,256]{1,0:T(8,128)(2,1)S(1)} %copy-done.4, ...), custom_call_target="tpu_custom_call" | custom-call | flops 1073741824 | bytes 3145728 | tf_op jit(solution)/shard_map/pallas_call | solution.py:290
  78.0 9.4 %collective-permute-done.12.refs_3_ = bf16[1024,256]{1,0:T(8,128)(2,1)} collective-permute-done((bf16[1024,256]{1,0:T(8,128)(2,1)S(1)}, bf16[1024,256]{1,0:T(8,128)(2,1)}, u32[]{:S(2)}, u32[]{:S(2)}) %collective-permute-start.12) | collective-permute-done | bytes 524320 | tf_op jit(solution)/shard_map/ppermute | solution.py:396
  87.4 11.2 %collective-permute-done.13.refs_5_ = bf16[1024,256]{1,0:T(8,128)(2,1)} collective-permute-done((bf16[1024,256]{1,0:T(8,128)(2,1)S(1)}, bf16[1024,256]{1,0:T(8,128)(2,1)}, u32[]{:S(2)}, u32[]{:S(2)}) %collective-permute-start.13) | collective-permute-done | bytes 524320 | tf_op jit(solution)/shard_map/ppermute | solution.py:396
  98.6 3.2 %shard_map.80 = (bf16[2,256,512]{2,1,0:T(8,128)(2,1)S(1)}, f32[2,256,512]{2,1,0:T(8,128)S(1)}) custom-call(s32[1]{0:T(128)} %bitcast.7.flag_ref, bf16[512,1024]{1,0:T(8,128)(2,1)S(1)} %copy-done.1, bf16[512,1024]{1,0:T(8,128)(2,1)S(1)} %collective-permute-done.11.refs_0_.refs_1_, bf16[1024,256]{1,0:T(8,128)(2,1)S(1)} %collective-permute-done.2.refs_2_, ...), custom_call_target="tpu_custom_call" | custom-call | flops 1073741824 | bytes 3145728 | tf_op jit(solution)/shard_map/pallas_call | solution.py:290
  101.9 8.0 %collective-permute-done.15.refs_3_ = bf16[1024,256]{1,0:T(8,128)(2,1)} collective-permute-done((bf16[1024,256]{1,0:T(8,128)(2,1)}, bf16[1024,256]{1,0:T(8,128)(2,1)}, u32[]{:S(2)}, u32[]{:S(2)}) %collective-permute-start.15) | collective-permute-done | bytes 524320 | tf_op jit(solution)/shard_map/ppermute | solution.py:396
  109.8 2.5 %shard_map.81 = (bf16[2,256,256]{2,1,0:T(8,128)(2,1)S(1)}, f32[2,256,256]{2,1,0:T(8,128)S(1)}) custom-call(s32[1]{0:T(128)} %bitcast.7.flag_ref, bf16[512,1024]{1,0:T(8,128)(2,1)S(1)} %copy-done.1, bf16[512,1024]{1,0:T(8,128)(2,1)S(1)} %collective-permute-done.11.refs_0_.refs_1_, bf16[1024,256]{1,0:T(8,128)(2,1)} %collective-permute-done.14.refs_2_, ...), custom_call_target="tpu_custom_call" | custom-call | flops 536870912 | bytes 2621440 | tf_op jit(solution)/shard_map/pallas_call | solution.py:290
  112.4 7.2 %collective-permute-done.17.refs_3_ = bf16[1024,256]{1,0:T(8,128)(2,1)S(1)} collective-permute-done((bf16[1024,256]{1,0:T(8,128)(2,1)}, bf16[1024,256]{1,0:T(8,128)(2,1)S(1)}, u32[]{:S(2)}, u32[]{:S(2)}) %collective-permute-start.17) | collective-permute-done | bytes 524320 | tf_op jit(solution)/shard_map/ppermute | solution.py:396
  119.7 1.8 %shard_map.82 = (bf16[2,256,256]{2,1,0:T(8,128)(2,1)S(1)}, f32[2,256,256]{2,1,0:T(8,128)S(1)}) custom-call(s32[1]{0:T(128)} %bitcast.7.flag_ref, bf16[512,1024]{1,0:T(8,128)(2,1)S(1)} %copy-done.1, bf16[512,1024]{1,0:T(8,128)(2,1)S(1)} %collective-permute-done.11.refs_0_.refs_1_, bf16[1024,256]{1,0:T(8,128)(2,1)} %collective-permute-done.16.refs_2_, ...), custom_call_target="tpu_custom_call" | custom-call | flops 536870912 | bytes 2621440 | tf_op jit(solution)/shard_map/pallas_call | solution.py:290
  121.6 0.6 collective-permute-start.23
  122.3 0.6 collective-permute-start.30
  123.1 1.4 collective-permute-start.19
  124.6 4.1 %collective-permute-done.30 = bf16[2,128,256]{2,1,0:T(8,128)(2,1)S(1)} collective-permute-done((bf16[2,128,256]{2,1,0:T(8,128)(2,1)S(1)}, bf16[2,128,256]{2,1,0:T(8,128)(2,1)S(1)}, u32[]{:S(2)}, u32[]{:S(2)}) %collective-permute-start.30) | collective-permute-done | bytes 131104 | tf_op jit(solution)/shard_map/ppermute | solution.py:448
  128.8 1.0 collective-permute-start.31
  129.7 1.3 collective-permute-done.19
  131.4 0.6 collective-permute-start.24
  132.2 1.6 %collective-permute-start.27 = (bf16[2,128,512]{2,1,0:T(8,128)(2,1)S(1)}, bf16[2,128,512]{2,1,0:T(8,128)(2,1)S(1)}, u32[]{:S(2)}, u32[]{:S(2)}) collective-permute-start(bf16[2,128,512]{2,1,0:T(8,128)(2,1)S(1)} %slice.142), channel_id=1, source_target_pairs={{0,2},{1,3},{2,0},{3,1},{4,6},{5,7},{6,4},{7,5},{8,10},{9,11},{10,... | collective-permute-start | bytes 786440 | tf_op jit(solution)/shard_map/ppermute | solution.py:448
  133.8 1.0 collective-permute-start.20
  134.7 5.9 %collective-permute-done.24 = bf16[1,128,1024]{2,1,0:T(8,128)(2,1)S(1)} collective-permute-done((bf16[1,128,1024]{2,1,0:T(8,128)(2,1)S(1)}, bf16[1,128,1024]{2,1,0:T(8,128)(2,1)S(1)}, u32[]{:S(2)}, u32[]{:S(2)}) %collective-permute-start.24) | collective-permute-done | bytes 262176 | tf_op jit(solution)/shard_map/ppermute | solution.py:448
  140.7 1.0 collective-permute-start.25
  141.7 3.3 %collective-permute-done.27 = bf16[2,128,512]{2,1,0:T(8,128)(2,1)S(1)} collective-permute-done((bf16[2,128,512]{2,1,0:T(8,128)(2,1)S(1)}, bf16[2,128,512]{2,1,0:T(8,128)(2,1)S(1)}, u32[]{:S(2)}, u32[]{:S(2)}) %collective-permute-start.27) | collective-permute-done | bytes 262176 | tf_op jit(solution)/shard_map/ppermute | solution.py:448
  145.0 1.0 collective-permute-start.28
  146.0 4.0 %collective-permute-done.28.refs_3_ = bf16[128,512]{1,0:T(8,128)(2,1)S(1)} collective-permute-done((bf16[128,512]{1,0:T(8,128)(2,1)S(1)}, bf16[128,512]{1,0:T(8,128)(2,1)S(1)}, u32[]{:S(2)}, u32[]{:S(2)}) %collective-permute-start.28) | collective-permute-done | bytes 131104 | tf_op jit(solution)/shard_map/ppermute | solution.py:458
  150.1 1.8 %shard_map.83.refs_2_ = bf16[128,4096]{1,0:T(8,128)(2,1)} custom-call(s32[14]{0:T(128)S(1)} %stack.95.starts_ref, f32[128,1]{1,0:T(8,128)S(1)} %copy.11.scale_ref, f32[128,1024]{1,0:T(8,128)S(1)} %fusion.1.refs_0_, bf16[128,1024]{1,0:T(8,128)(2,1)S(1)} %collective-permute-done.25.refs_1_, f32[128,512]{1,0:T(8,128)S(1)} %slice_bitcast_fusion.refs_2_, ...), custom_call_target="tpu_custom_call" | custom-call | flops 458752 | bytes 2752512 | tf_op jit(solution)/shard_map/pallas_call | solution.py:359
  151.9 1.3 shard_map.84
  (68 shorter events, 1.9 us)
Async XLA Ops:
  1.3 9.8 %copy-start.5 = (bf16[1024,256]{1,0:T(8,128)(2,1)}, bf16[1024,256]{1,0:T(8,128)(2,1)S(1)}, u32[]{:S(2)}) copy-start(bf16[1024,256]{1,0:T(8,128)(2,1)S(1)} %get-tuple-element.52.refs_1_) | copy-start | bytes 1572868
  1.3 31.5 %copy-start.2 = (bf16[1024,256]{1,0:T(8,128)(2,1)}, bf16[1024,256]{1,0:T(8,128)(2,1)S(1)}, u32[]{:S(2)}) copy-start(bf16[1024,256]{1,0:T(8,128)(2,1)S(1)} %get-tuple-element.29.refs_2_) | copy-start | bytes 1572868
  1.3 15.1 %collective-permute-start.1 = (bf16[1024,256]{1,0:T(8,128)(2,1)S(1)}, bf16[1024,256]{1,0:T(8,128)(2,1)}, u32[]{:S(2)}, u32[]{:S(2)}) collective-permute-start(bf16[1024,256]{1,0:T(8,128)(2,1)S(1)} %get-tuple-element.52.refs_1_), channel_id=1, source_target_pairs={{0,8},{4,12},{8,0},{12,4},{16,24},{20,28},{24,16},{28,20},{1,9},{5... | collective-permute-start | bytes 1572872 | tf_op jit(solution)/shard_map/ppermute | solution.py:396
  4.4 12.0 %collective-permute-start.2 = (bf16[1024,256]{1,0:T(8,128)(2,1)S(1)}, bf16[1024,256]{1,0:T(8,128)(2,1)S(1)}, u32[]{:S(2)}, u32[]{:S(2)}) collective-permute-start(bf16[1024,256]{1,0:T(8,128)(2,1)S(1)} %get-tuple-element.52.refs_1_), channel_id=1, source_target_pairs={{8,16},{12,20},{16,8},{20,12},{9,17},{13,21},{17,9},{21,13},{10,18... | collective-permute-start | bytes 1572872 | tf_op jit(solution)/shard_map/ppermute | solution.py:396
  7.4 5.2 %collective-permute-start = (bf16[4,128,128]{2,1,0:T(8,128)(2,1)}, bf16[4,128,128]{2,1,0:T(8,128)(2,1)S(1)}, u32[]{:S(2)}, u32[]{:S(2)}) collective-permute-start(bf16[4,128,128]{2,1,0:T(8,128)(2,1)} %shard_map.76), channel_id=1, source_target_pairs={{0,4},{4,0},{8,12},{12,8},{16,20},{20,16},{24,28},{28,24},{1,5},{5... | collective-permute-start | bytes 393224 | tf_op jit(solution)/shard_map/ppermute | solution.py:93
  16.4 9.1 %collective-permute-start.3 = (bf16[4,128,128]{2,1,0:T(8,128)(2,1)S(1)}, bf16[4,128,128]{2,1,0:T(8,128)(2,1)S(1)}, u32[]{:S(2)}, u32[]{:S(2)}) collective-permute-start(bf16[4,128,128]{2,1,0:T(8,128)(2,1)S(1)} %fusion.8), channel_id=1, source_target_pairs={{0,8},{4,12},{16,24},{20,28},{1,9},{5,13},{17,25},{21,29},{2,10},{... | collective-permute-start | bytes 393224 | tf_op jit(solution)/shard_map/ppermute | solution.py:97
  26.5 1.4 collective-permute-start.4
  27.1 9.6 %collective-permute-start.5 = (bf16[4,128,128]{2,1,0:T(8,128)(2,1)S(1)}, bf16[4,128,128]{2,1,0:T(8,128)(2,1)S(1)}, u32[]{:S(2)}, u32[]{:S(2)}) collective-permute-start(bf16[4,128,128]{2,1,0:T(8,128)(2,1)S(1)} %fusion.2), channel_id=1, source_target_pairs={{8,24},{12,28},{9,25},{13,29},{10,26},{14,30},{11,27},{15,31}} | collective-permute-start | bytes 393224 | tf_op jit(solution)/shard_map/ppermute | solution.py:100
  27.8 15.1 %collective-permute-start.6 = (bf16[1024,256]{1,0:T(8,128)(2,1)S(1)}, bf16[1024,256]{1,0:T(8,128)(2,1)}, u32[]{:S(2)}, u32[]{:S(2)}) collective-permute-start(bf16[1024,256]{1,0:T(8,128)(2,1)S(1)} %get-tuple-element.29.refs_2_), channel_id=1, source_target_pairs={{0,8},{4,12},{8,0},{12,4},{16,24},{20,28},{24,16},{28,20},{1,9},{5... | collective-permute-start | bytes 1572872 | tf_op jit(solution)/shard_map/ppermute | solution.py:396
  32.7 10.2 %collective-permute-start.7 = (bf16[1024,256]{1,0:T(8,128)(2,1)S(1)}, bf16[1024,256]{1,0:T(8,128)(2,1)S(1)}, u32[]{:S(2)}, u32[]{:S(2)}) collective-permute-start(bf16[1024,256]{1,0:T(8,128)(2,1)S(1)} %get-tuple-element.29.refs_2_), channel_id=1, source_target_pairs={{8,16},{12,20},{16,8},{20,12},{9,17},{13,21},{17,9},{21,13},{10,18... | collective-permute-start | bytes 1572872 | tf_op jit(solution)/shard_map/ppermute | solution.py:396
  33.5 3.3 %copy-start.8 = (f32[4,128,128]{2,1,0:T(8,128)S(1)}, f32[4,128,128]{2,1,0:T(8,128)}, u32[]{:S(2)}) copy-start(f32[4,128,128]{2,1,0:T(8,128)} %shard_map.75) | copy-start | bytes 786436
  37.6 5.3 %collective-permute-start.8 = (bf16[4,128,128]{2,1,0:T(8,128)(2,1)S(1)}, bf16[4,128,128]{2,1,0:T(8,128)(2,1)S(1)}, u32[]{:S(2)}, u32[]{:S(2)}) collective-permute-start(bf16[4,128,128]{2,1,0:T(8,128)(2,1)S(1)} %get-tuple-element.53), channel_id=1, source_target_pairs={{0,4},{4,0},{8,12},{12,8},{16,20},{20,16},{24,28},{28,24},{1,5},{5... | collective-permute-start | bytes 393224 | tf_op jit(solution)/shard_map/ppermute | solution.py:113
  42.9 0.7 copy-start.10
  51.3 22.1 %collective-permute-start.11 = (bf16[512,1024]{1,0:T(8,128)(2,1)}, bf16[512,1024]{1,0:T(8,128)(2,1)S(1)}, u32[]{:S(2)}, u32[]{:S(2)}) collective-permute-start(bf16[512,1024]{1,0:T(8,128)(2,1)} %get-tuple-element.32.refs_0_), channel_id=1, source_target_pairs={{0,4},{4,0},{8,12},{12,8},{16,20},{20,16},{24,28},{28,24},{1,5},{5... | collective-permute-start | bytes 3145736 | tf_op jit(solution)/shard_map/ppermute | solution.py:425
  52.4 13.6 %collective-permute-start.14 = (bf16[1024,256]{1,0:T(8,128)(2,1)}, bf16[1024,256]{1,0:T(8,128)(2,1)}, u32[]{:S(2)}, u32[]{:S(2)}) collective-permute-start(bf16[1024,256]{1,0:T(8,128)(2,1)} %collective-permute-done.1.refs_3_), channel_id=1, source_target_pairs={{8,16},{12,20},{16,8},{20,12},{9,17},{13,21},{17,9},{21,13},{10,18... | collective-permute-start | bytes 1572872 | tf_op jit(solution)/shard_map/ppermute | solution.py:396
  53.9 15.4 %collective-permute-start.16 = (bf16[1024,256]{1,0:T(8,128)(2,1)}, bf16[1024,256]{1,0:T(8,128)(2,1)}, u32[]{:S(2)}, u32[]{:S(2)}) collective-permute-start(bf16[1024,256]{1,0:T(8,128)(2,1)} %collective-permute-done.6.refs_4_), channel_id=1, source_target_pairs={{8,16},{12,20},{16,8},{20,12},{9,17},{13,21},{17,9},{21,13},{10,18... | collective-permute-start | bytes 1572872 | tf_op jit(solution)/shard_map/ppermute | solution.py:396
  55.4 1.2 copy-start
  56.6 1.0 copy-start.3
  57.6 1.0 copy-start.6
  58.7 4.0 %copy-start.9 = (f32[512,128]{1,0:T(8,128)S(1)}, f32[512,128]{1,0:T(8,128)}, u32[]{:S(2)}) copy-start(f32[512,128]{1,0:T(8,128)} %get-tuple-element.31) | copy-start | bytes 786436
  62.5 8.3 %collective-permute-start.21 = (bf16[1,256,1024]{2,1,0:T(8,128)(2,1)}, bf16[1,256,1024]{2,1,0:T(8,128)(2,1)}, u32[]{:S(2)}, u32[]{:S(2)}) collective-permute-start(bf16[1,256,1024]{2,1,0:T(8,128)(2,1)} %get-tuple-element.33), channel_id=1, source_target_pairs={{0,1},{1,0},{2,3},{3,2},{4,5},{5,4},{6,7},{7,6},{8,9},{9,8},{10,11... | collective-permute-start | bytes 1572872 | tf_op jit(solution)/shard_map/ppermute | solution.py:448
  62.8 1.6 %collective-permute-start.9 = (f32[256]{0:T(256)S(1)}, f32[256]{0:T(256)S(1)}, u32[]{:S(2)}, u32[]{:S(2)}) collective-permute-start(f32[256]{0:T(256)S(1)} %slice.77), channel_id=1, source_target_pairs={{0,1},{1,0},{2,3},{3,2},{4,5},{5,4},{6,7},{7,6},{8,9},{9,8},{10,11... | collective-permute-start | bytes 3080 | tf_op jit(solution)/shard_map/ppermute | solution.py:431
  64.4 3.5 %collective-permute-start.10 = (f32[128]{0:T(128)S(1)}, f32[128]{0:T(128)S(1)}, u32[]{:S(2)}, u32[]{:S(2)}) collective-permute-start(f32[128]{0:T(128)S(1)} %slice.79), channel_id=1, source_target_pairs={{0,2},{1,3},{2,0},{3,1},{4,6},{5,7},{6,4},{7,5},{8,10},{9,11},{10,... | collective-permute-start | bytes 1544 | tf_op jit(solution)/shard_map/ppermute | solution.py:431
  66.1 21.3 %collective-permute-start.12 = (bf16[1024,256]{1,0:T(8,128)(2,1)S(1)}, bf16[1024,256]{1,0:T(8,128)(2,1)}, u32[]{:S(2)}, u32[]{:S(2)}) collective-permute-start(bf16[1024,256]{1,0:T(8,128)(2,1)S(1)} %collective-permute-done.2.refs_2_), channel_id=1, source_target_pairs={{8,0},{12,4},{16,24},{20,28},{9,1},{13,5},{17,25},{21,29},{10,2},{... | collective-permute-start | bytes 1572872 | tf_op jit(solution)/shard_map/ppermute | solution.py:396
  68.0 30.6 %collective-permute-start.13 = (bf16[1024,256]{1,0:T(8,128)(2,1)S(1)}, bf16[1024,256]{1,0:T(8,128)(2,1)}, u32[]{:S(2)}, u32[]{:S(2)}) collective-permute-start(bf16[1024,256]{1,0:T(8,128)(2,1)S(1)} %collective-permute-done.7.refs_4_), channel_id=1, source_target_pairs={{8,0},{12,4},{16,24},{20,28},{9,1},{13,5},{17,25},{21,29},{10,2},{... | collective-permute-start | bytes 1572872 | tf_op jit(solution)/shard_map/ppermute | solution.py:396
  69.3 40.6 %collective-permute-start.15 = (bf16[1024,256]{1,0:T(8,128)(2,1)}, bf16[1024,256]{1,0:T(8,128)(2,1)}, u32[]{:S(2)}, u32[]{:S(2)}) collective-permute-start(bf16[1024,256]{1,0:T(8,128)(2,1)} %collective-permute-done.14.refs_2_), channel_id=1, source_target_pairs={{8,0},{12,4},{16,24},{20,28},{9,1},{13,5},{17,25},{21,29},{10,2},{... | collective-permute-start | bytes 1572872 | tf_op jit(solution)/shard_map/ppermute | solution.py:396
  70.7 4.3 %copy-start.4 = (bf16[1024,256]{1,0:T(8,128)(2,1)S(1)}, bf16[1024,256]{1,0:T(8,128)(2,1)}, u32[]{:S(2)}) copy-start(bf16[1024,256]{1,0:T(8,128)(2,1)} %copy-done.2) | copy-start | bytes 1572868
  70.7 4.3 %copy-start.7 = (bf16[1024,256]{1,0:T(8,128)(2,1)S(1)}, bf16[1024,256]{1,0:T(8,128)(2,1)}, u32[]{:S(2)}) copy-start(bf16[1024,256]{1,0:T(8,128)(2,1)} %copy-done.5) | copy-start | bytes 1572868
  70.7 49.0 %collective-permute-start.17 = (bf16[1024,256]{1,0:T(8,128)(2,1)}, bf16[1024,256]{1,0:T(8,128)(2,1)S(1)}, u32[]{:S(2)}, u32[]{:S(2)}) collective-permute-start(bf16[1024,256]{1,0:T(8,128)(2,1)} %collective-permute-done.16.refs_2_), channel_id=1, source_target_pairs={{8,0},{12,4},{16,24},{20,28},{9,1},{13,5},{17,25},{21,29},{10,2},{... | collective-permute-start | bytes 1572872 | tf_op jit(solution)/shard_map/ppermute | solution.py:396
  73.4 25.2 %copy-start.1 = (bf16[512,1024]{1,0:T(8,128)(2,1)S(1)}, bf16[512,1024]{1,0:T(8,128)(2,1)}, u32[]{:S(2)}) copy-start(bf16[512,1024]{1,0:T(8,128)(2,1)} %get-tuple-element.32.refs_0_) | copy-start | bytes 3145732
  73.4 48.1 %collective-permute-start.22 = (bf16[1,128,1024]{2,1,0:T(8,128)(2,1)S(1)}, bf16[1,128,1024]{2,1,0:T(8,128)(2,1)S(1)}, u32[]{:S(2)}, u32[]{:S(2)}) collective-permute-start(bf16[1,128,1024]{2,1,0:T(8,128)(2,1)S(1)} %slice.144), channel_id=1, source_target_pairs={{0,2},{1,3},{2,0},{3,1},{4,6},{5,7},{6,4},{7,5},{8,10},{9,11},{10,... | collective-permute-start | bytes 786440 | tf_op jit(solution)/shard_map/ppermute | solution.py:448
  112.4 9.9 %collective-permute-start.29 = (bf16[2,256,256]{2,1,0:T(8,128)(2,1)S(1)}, bf16[2,256,256]{2,1,0:T(8,128)(2,1)S(1)}, u32[]{:S(2)}, u32[]{:S(2)}) collective-permute-start(bf16[2,256,256]{2,1,0:T(8,128)(2,1)S(1)} %get-tuple-element.42), channel_id=1, source_target_pairs={{0,1},{1,0},{2,3},{3,2},{4,5},{5,4},{6,7},{7,6},{8,9},{9,8},{10,11... | collective-permute-start | bytes 786440 | tf_op jit(solution)/shard_map/ppermute | solution.py:448
  121.5 1.6 %collective-permute-start.18 = (bf16[2,256,256]{2,1,0:T(8,128)(2,1)S(1)}, bf16[2,256,256]{2,1,0:T(8,128)(2,1)S(1)}, u32[]{:S(2)}, u32[]{:S(2)}) collective-permute-start(bf16[2,256,256]{2,1,0:T(8,128)(2,1)S(1)} %get-tuple-element.46), channel_id=1, source_target_pairs={{0,1},{1,0},{2,3},{3,2},{4,5},{5,4},{6,7},{7,6},{8,9},{9,8},{10,11... | collective-permute-start | bytes 786440 | tf_op jit(solution)/shard_map/ppermute | solution.py:448
  121.6 9.5 %collective-permute-start.23 = (bf16[1,256,1024]{2,1,0:T(8,128)(2,1)S(1)}, bf16[1,256,1024]{2,1,0:T(8,128)(2,1)S(1)}, u32[]{:S(2)}, u32[]{:S(2)}) collective-permute-start(bf16[1,256,1024]{2,1,0:T(8,128)(2,1)S(1)} %get-tuple-element.35), channel_id=1, source_target_pairs={{0,1},{1,0},{2,3},{3,2},{4,5},{5,4},{6,7},{7,6},{8,9},{9,8},{10,11... | collective-permute-start | bytes 1572872 | tf_op jit(solution)/shard_map/ppermute | solution.py:448
  122.2 9.8 %collective-permute-start.26 = (bf16[2,256,512]{2,1,0:T(8,128)(2,1)S(1)}, bf16[2,256,512]{2,1,0:T(8,128)(2,1)S(1)}, u32[]{:S(2)}, u32[]{:S(2)}) collective-permute-start(bf16[2,256,512]{2,1,0:T(8,128)(2,1)S(1)} %get-tuple-element.39), channel_id=1, source_target_pairs={{0,1},{1,0},{2,3},{3,2},{4,5},{5,4},{6,7},{7,6},{8,9},{9,8},{10,11... | collective-permute-start | bytes 1572872 | tf_op jit(solution)/shard_map/ppermute | solution.py:448
  122.3 6.4 %collective-permute-start.30 = (bf16[2,128,256]{2,1,0:T(8,128)(2,1)S(1)}, bf16[2,128,256]{2,1,0:T(8,128)(2,1)S(1)}, u32[]{:S(2)}, u32[]{:S(2)}) collective-permute-start(bf16[2,128,256]{2,1,0:T(8,128)(2,1)S(1)} %slice.145), channel_id=1, source_target_pairs={{0,2},{1,3},{2,0},{3,1},{4,6},{5,7},{6,4},{7,5},{8,10},{9,11},{10,... | collective-permute-start | bytes 393224 | tf_op jit(solution)/shard_map/ppermute | solution.py:448
  123.1 7.9 %collective-permute-start.19 = (bf16[2,128,256]{2,1,0:T(8,128)(2,1)S(1)}, bf16[2,128,256]{2,1,0:T(8,128)(2,1)S(1)}, u32[]{:S(2)}, u32[]{:S(2)}) collective-permute-start(bf16[2,128,256]{2,1,0:T(8,128)(2,1)S(1)} %slice.146), channel_id=1, source_target_pairs={{0,2},{1,3},{2,0},{3,1},{4,6},{5,7},{6,4},{7,5},{8,10},{9,11},{10,... | collective-permute-start | bytes 393224 | tf_op jit(solution)/shard_map/ppermute | solution.py:448
  128.8 17.2 %collective-permute-start.31 = (bf16[128,256]{1,0:T(8,128)(2,1)S(1)}, bf16[128,256]{1,0:T(8,128)(2,1)S(1)}, u32[]{:S(2)}, u32[]{:S(2)}) collective-permute-start(bf16[128,256]{1,0:T(8,128)(2,1)S(1)} %fusion.11), channel_id=1, source_target_pairs={{0,4},{4,0},{8,12},{12,8},{16,20},{20,16},{24,28},{28,24},{1,5},{5... | collective-permute-start | bytes 196616 | tf_op jit(solution)/shard_map/ppermute | solution.py:458
  131.4 9.3 %collective-permute-start.24 = (bf16[1,128,1024]{2,1,0:T(8,128)(2,1)S(1)}, bf16[1,128,1024]{2,1,0:T(8,128)(2,1)S(1)}, u32[]{:S(2)}, u32[]{:S(2)}) collective-permute-start(bf16[1,128,1024]{2,1,0:T(8,128)(2,1)S(1)} %slice.143), channel_id=1, source_target_pairs={{0,2},{1,3},{2,0},{3,1},{4,6},{5,7},{6,4},{7,5},{8,10},{9,11},{10,... | collective-permute-start | bytes 786440 | tf_op jit(solution)/shard_map/ppermute | solution.py:448
  132.2 12.7 %collective-permute-start.27 = (bf16[2,128,512]{2,1,0:T(8,128)(2,1)S(1)}, bf16[2,128,512]{2,1,0:T(8,128)(2,1)S(1)}, u32[]{:S(2)}, u32[]{:S(2)}) collective-permute-start(bf16[2,128,512]{2,1,0:T(8,128)(2,1)S(1)} %slice.142), channel_id=1, source_target_pairs={{0,2},{1,3},{2,0},{3,1},{4,6},{5,7},{6,4},{7,5},{8,10},{9,11},{10,... | collective-permute-start | bytes 786440 | tf_op jit(solution)/shard_map/ppermute | solution.py:448
  133.8 18.1 %collective-permute-start.20 = (bf16[128,256]{1,0:T(8,128)(2,1)S(1)}, bf16[128,256]{1,0:T(8,128)(2,1)S(1)}, u32[]{:S(2)}, u32[]{:S(2)}) collective-permute-start(bf16[128,256]{1,0:T(8,128)(2,1)S(1)} %fusion.10), channel_id=1, source_target_pairs={{0,4},{4,0},{8,12},{12,8},{16,20},{20,16},{24,28},{28,24},{1,5},{5... | collective-permute-start | bytes 196616 | tf_op jit(solution)/shard_map/ppermute | solution.py:458
  140.7 9.4 %collective-permute-start.25 = (bf16[128,1024]{1,0:T(8,128)(2,1)S(1)}, bf16[128,1024]{1,0:T(8,128)(2,1)S(1)}, u32[]{:S(2)}, u32[]{:S(2)}) collective-permute-start(bf16[128,1024]{1,0:T(8,128)(2,1)S(1)} %fusion.7), channel_id=1, source_target_pairs={{0,4},{4,0},{8,12},{12,8},{16,20},{20,16},{24,28},{28,24},{1,5},{5... | collective-permute-start | bytes 786440 | tf_op jit(solution)/shard_map/ppermute | solution.py:458
  145.0 5.0 %collective-permute-start.28 = (bf16[128,512]{1,0:T(8,128)(2,1)S(1)}, bf16[128,512]{1,0:T(8,128)(2,1)S(1)}, u32[]{:S(2)}, u32[]{:S(2)}) collective-permute-start(bf16[128,512]{1,0:T(8,128)(2,1)S(1)} %fusion.9), channel_id=1, source_target_pairs={{0,4},{4,0},{8,12},{12,8},{16,20},{20,16},{24,28},{28,24},{1,5},{5... | collective-permute-start | bytes 393224 | tf_op jit(solution)/shard_map/ppermute | solution.py:458

commit v4 on v0

v4 whole, which is shorter than its diff:
```python
import functools

import jax
import jax.numpy as jnp
from jax import lax
from jax.experimental import pallas as pl
from jax.experimental.pallas import tpu as pltpu
from jax.sharding import PartitionSpec as P

DH = 128
BLOCK = 512
LINE = 4
VMEM_BYTES = 48 * 1024 * 1024


epsilon = 1e-05


def line_pairs(n_seq, hops):
    inner = n_seq // LINE
    return [(a * inner + i, b * inner + i) for a, b in hops for i in range(inner)]


def turn_pairs(n_seq, turn):
    inner = n_seq // LINE
    return [(a * inner + i, a * inner + (i + turn) % inner) for a in range(LINE) for i in range(inner)]


def flip_pairs(n_head, bit):
    return [(h, h ^ bit) for h in range(n_head)]


SWAP_OUTER = [(0, 1), (1, 0), (2, 3), (3, 2)]
SWAP_MIDDLE = [(1, 2), (2, 1)]
TO_ENDS = [(1, 0), (2, 3)]


def hold(value, *others):
    return lax.optimization_barrier((value, *others))[0]


def scalars(*values):
    return jnp.stack([jnp.asarray(value, jnp.int32) for value in values])


def local_call(kernel, places, operands, out_shapes, scratch=()):
    return pl.pallas_call(
        kernel,
        in_specs=[pl.BlockSpec(memory_space=pltpu.SMEM)]
        + [pl.BlockSpec(memory_space=pltpu.VMEM)] * len(operands),
        out_specs=[pl.BlockSpec(memory_space=pltpu.VMEM)] * len(out_shapes),
        out_shape=out_shapes,
        scratch_shapes=list(scratch),
        compiler_params=pltpu.CompilerParams(vmem_limit_bytes=VMEM_BYTES),
        cost_estimate=pl.CostEstimate(flops=1, bytes_accessed=1, transcendentals=0),
    )(places, *operands)


def combine_kernel(count, always, masks_ref, *refs):
    values, outs = refs[:count], refs[count:]
    total = values[0][...].astype(jnp.float32)
    for value in values[1:always]:
        total = total + value[...].astype(jnp.float32)
    for position, out in enumerate(outs):
        own = total
        for k in range(always, count):
            mask = masks_ref[position * (count - always) + k - always]
            own = own + jnp.where(mask != 0, values[k][...].astype(jnp.float32), 0.0)
        out[...] = own.astype(out.dtype)


def combine(values, dtypes, sometimes=(), masks=None):
    operands = list(values) + list(sometimes)
    masks = scalars(0) if masks is None else scalars(*masks)
    return local_call(
        functools.partial(combine_kernel, len(operands), len(values)),
        masks,
        operands,
        [jax.ShapeDtypeStruct(values[0].shape, dtype) for dtype in dtypes],
    )


def states_kernel(part_ref, k_ref, v_ref, out_ref):
    heads = out_ref.shape[0]
    for index in range(heads):
        columns = pl.ds(pl.multiple_of((part_ref[0] * heads + index) * DH, DH), DH)
        out_ref[index] = lax.dot_general(
            k_ref[:, columns],
            v_ref[:, columns],
            (((0,), (0,)), ((), ())),
            preferred_element_type=jnp.float32,
        ).astype(out_ref.dtype)


def block_states(key_input, value_input, part, heads, dtype):
    return local_call(
        states_kernel,
        scalars(part),
        [key_input, value_input],
        [jax.ShapeDtypeStruct((heads, DH, DH), dtype)],
    )[0]


def state_prefix(key_input, value_input, n_seq, place, early, later):
    inner = n_seq // LINE
    i = place % inner
    heads = key_input.shape[1] // DH
    split = heads % inner == 0
    share = heads // inner if split else heads
    if split:
        sends = [
            block_states(key_input, value_input, (i + turn) % inner, share, jnp.bfloat16)
            for turn in range(1, inner)
        ]
        own = block_states(key_input, value_input, i, share, jnp.float32)
    else:
        own = block_states(key_input, value_input, 0, share, jnp.float32)
        sends = [own.astype(jnp.bfloat16)] * (inner - 1)
    values, members = [own], [i]
    for turn in range(1, inner):
        values.append(lax.ppermute(sends[turn - 1], "seq", turn_pairs(n_seq, turn)))
        members.append((i - turn) % inner)
    (first,) = combine(values, [jnp.bfloat16])
    from_left = lax.ppermute(hold(first, *early), "seq", line_pairs(n_seq, [(0, 1), (2, 3)]))
    (second,) = combine(values + [from_left], [jnp.bfloat16])
    near = lax.ppermute(second, "seq", line_pairs(n_seq, [(1, 2)]))
    far = lax.ppermute(second, "seq", line_pairs(n_seq, [(1, 3)]))
    targets = [i] + [(i + turn) % inner for turn in range(1, inner)] if split else [i]
    masks = [owner < target for target in targets for owner in members]
    dtypes = [jnp.float32] + [jnp.bfloat16] * (len(targets) - 1)
    near = hold(near, *later(from_left))
    befores = combine([from_left, near, far], dtypes, values, masks)
    terms = [befores[0]]
    for turn in range(1, len(targets)):
        terms.append(lax.ppermute(befores[turn], "seq", turn_pairs(n_seq, turn)))
    return terms, far


def causal_kernel(first_head, place_ref, q_ref, k_ref, v_ref, out_ref):
    rows = q_ref.shape[0]
    half = rows // 2
    top, bottom = pl.ds(0, half), pl.ds(half, half)
    keep = lax.broadcasted_iota(jnp.int32, (half, half), 0) >= lax.broadcasted_iota(
        jnp.int32, (half, half), 1
    )

    def scores(q_rows, k_rows, columns):
        return lax.dot_general(
            q_ref[q_rows, columns],
            k_ref[k_rows, columns],
            (((1,), (1,)), ((), ())),
            preferred_element_type=jnp.float32,
        )

    for index in range(out_ref.shape[1] // DH):
        columns = pl.ds((first_head + index) * DH, DH)
        placed = pl.ds(index * DH, DH)
        first = jnp.where(keep, scores(top, top, columns), 0.0).astype(jnp.bfloat16)
        below = scores(bottom, top, columns).astype(jnp.bfloat16)
        last = jnp.where(keep, scores(bottom, bottom, columns), 0.0).astype(jnp.bfloat16)
        out_ref[top, placed] = jnp.dot(first, v_ref[top, columns], preferred_element_type=jnp.float32)
        out_ref[bottom, placed] = jnp.dot(
            jnp.concatenate([below, last], axis=1),
            v_ref[:, columns],
            preferred_element_type=jnp.float32,
        )


def causal_part(queries, key_input, value_input, first_head, heads):
    return local_call(
        functools.partial(causal_kernel, first_head),
        scalars(0),
        [queries, key_input, value_input],
        [jax.ShapeDtypeStruct((queries.shape[0], heads * DH), jnp.float32)],
    )[0]


def hidden_kernel(order, group, calls, place_ref, q_ref, gate_ref, gain_ref, kv_ref, *refs):
    terms, inners = refs[:group], refs[group : group + calls]
    hidden_ref, squares_ref = refs[group + calls :]
    heads = kv_ref.shape[0]
    share = heads // group
    size = q_ref.shape[0] // len(order)
    states = []
    for head in range(heads):
        state = kv_ref[head]
        for turn, term in enumerate(terms):
            value = term[head % share].astype(jnp.float32)
            if group > 1:
                covers = lax.rem(place_ref[1] - turn + group, group)
                value = jnp.where(covers == head // share, value, 0.0)
            state = state + value
        high = state.astype(jnp.bfloat16)
        low = (state - high.astype(jnp.float32)).astype(jnp.bfloat16)
        states.append(jnp.concatenate([high, low], axis=0))
    for position, block in enumerate(order):
        start = pl.multiple_of((place_ref[0] ^ block) * size, size)
        rows = pl.ds(start, size)
        placed = pl.ds(position * size, size)
        squares = jnp.zeros((size, DH), jnp.float32)
        for head in range(heads):
            columns = pl.ds(head * DH, DH)
            q_rows = q_ref[rows, columns]
            carried = jnp.dot(
                jnp.concatenate([q_rows, q_rows], axis=1),
                states[head],
                preferred_element_type=jnp.float32,
            )
            per_call = inners[0].shape[1] // DH
            inner = inners[head // per_call][rows, pl.ds(head % per_call * DH, DH)]
            attn = (carried + inner).astype(jnp.bfloat16).astype(jnp.float32)
            gate = 1.0 + jnp.tanh(gate_ref[rows, columns].astype(jnp.float32) * 0.5)
            gain = gain_ref[place_ref[0] * heads + head] * 0.5
            hidden_ref[placed, columns] = (attn * (gain * gate)).astype(jnp.bfloat16)
            squares = squares + attn * attn
        squares_ref[pl.ds(position, 1), :] = jnp.sum(jnp.transpose(squares), axis=0, keepdims=True)


def gated_hidden(queries, inners, kv_state, terms, gate_input, norm_gain, h, i, order):
    rows, width = queries.shape
    return local_call(
        functools.partial(hidden_kernel, order, len(terms), len(inners)),
        scalars(h, i),
        [queries, gate_input, norm_gain.reshape(-1, 1, DH), kv_state, *terms, *inners],
        [
            jax.ShapeDtypeStruct((rows, width), jnp.bfloat16),
            jax.ShapeDtypeStruct((len(order), rows // len(order)), jnp.float32),
        ],
    )


def project_kernel(groups, choices, flag_ref, *refs):
    rows_refs = refs[:groups]
    weight_refs = refs[groups : groups + sum(choices)]
    sent_ref, kept_ref = refs[groups + sum(choices) :]
    half = sent_ref.shape[1]
    width = weight_refs[0].shape[1]

    def products(index, weight_ref):
        columns = pl.ds(index * width, width)
        for group in range(groups):
            product = jnp.dot(
                rows_refs[group][...], weight_ref[...], preferred_element_type=jnp.float32
            )
            kept_ref[group, :, columns] = product[:half]
            sent_ref[group, :, columns] = product[half:].astype(jnp.bfloat16)

    first = 0
    for index, number in enumerate(choices):
        for k in range(number):
            one = functools.partial(products, index, weight_refs[first + k])
            if number == 1:
                one()
            else:
                pl.when(flag_ref[0] == k)(one)
        first += number


def project(rows_list, weights, flag):
    flat = [choice for weight in weights for choice in weight]
    choices = tuple(len(weight) for weight in weights)
    shape = (len(rows_list), rows_list[0].shape[0] // 2, flat[0].shape[1] * len(weights))
    return local_call(
        functools.partial(project_kernel, len(rows_list), choices),
        flag,
        [*rows_list, *flat],
        [jax.ShapeDtypeStruct(shape, jnp.bfloat16), jax.ShapeDtypeStruct(shape, jnp.float32)],
    )


def fold_kernel(flag_ref, kept_ref, got_ref, *outs):
    if len(outs) == 2 and len(outs[0].shape) == 3:
        sent_ref, left_ref = outs
        half = left_ref.shape[1]
        left_ref[...] = kept_ref[:, :half] + got_ref[:, :half].astype(jnp.float32)
        sent_ref[...] = (kept_ref[:, half:] + got_ref[:, half:].astype(jnp.float32)).astype(jnp.bfloat16)
        return
    for group, out in enumerate(outs):
        out[...] = (kept_ref[group] + got_ref[group].astype(jnp.float32)).astype(out.dtype)


def fold(kept, got, more):
    groups, rows, width = kept.shape
    if more:
        shape = (groups, rows // 2, width)
        outs = [jax.ShapeDtypeStruct(shape, jnp.bfloat16), jax.ShapeDtypeStruct(shape, jnp.float32)]
    else:
        outs = [jax.ShapeDtypeStruct((rows, width), jnp.bfloat16)] * groups
    return local_call(fold_kernel, scalars(0), [kept, got], outs)


def column(row):
    return jnp.transpose(jnp.broadcast_to(row, (row.shape[1], row.shape[1])))


def scaled_parts(counts, cut, squares_ref, pieces, total_width):
    scale = lax.rsqrt(column(squares_ref[...]) / total_width + epsilon)
    for piece, count in zip(pieces, counts):
        for index in range(count):
            for first in range(index * cut, (index + 1) * cut, DH):
                yield piece[:, pl.ds(first, DH)].astype(jnp.float32) * scale


def placed_kernel(counts, cut, total_width, starts_ref, squares_ref, *refs):
    out_ref = refs[-1]
    steps = cut // DH
    for at, part in enumerate(scaled_parts(counts, cut, squares_ref, refs[:-1], total_width)):
        start = pl.multiple_of(starts_ref[at // steps] + at % steps * DH, DH)
        out_ref[:, pl.ds(start, DH)] = part.astype(out_ref.dtype)


def added_kernel(counts, cut, total_width, starts_ref, squares_ref, *refs):
    pieces = refs[: len(counts)]
    out_ref, buf, sem = refs[-3:]
    steps = cut // DH
    copies = []
    for at, part in enumerate(scaled_parts(counts, cut, squares_ref, pieces, total_width)):
        where = at // steps
        buf[where, :, pl.ds(at % steps * DH, DH)] = part.astype(out_ref.dtype)
        if at % steps == steps - 1:
            start = pl.multiple_of(starts_ref[where], DH)
            copy = pltpu.make_async_copy(buf.at[where], out_ref.at[:, pl.ds(start, cut)], sem.at[where])
            copy.start()
            copies.append(copy)
    for copy in copies:
        copy.wait()


def placed(filled, pieces, squares, cut, shape, total_width):
    counts = tuple(len(starts) for _, starts in pieces)
    starts = scalars(*[start for _, own in pieces for start in own])
    operands = [squares] + [piece for piece, _ in pieces]
    out_shape = jax.ShapeDtypeStruct(shape, jnp.bfloat16)
    if filled is None:
        kernel = functools.partial(placed_kernel, counts, cut, total_width)
        return local_call(kernel, starts, operands, [out_shape])[0]
    return pl.pallas_call(
        functools.partial(added_kernel, counts, cut, total_width),
        in_specs=[pl.BlockSpec(memory_space=pltpu.SMEM)]
        + [pl.BlockSpec(memory_space=pltpu.VMEM)] * len(operands)
        + [pl.BlockSpec(memory_space=pl.ANY)],
        out_specs=pl.BlockSpec(memory_space=pl.ANY),
        out_shape=out_shape,
        scratch_shapes=[
            pltpu.VMEM((sum(counts), shape[0], cut), jnp.bfloat16),
            pltpu.SemaphoreType.DMA((sum(counts),)),
        ],
        input_output_aliases={len(operands) + 1: 0},
        compiler_params=pltpu.CompilerParams(vmem_limit_bytes=VMEM_BYTES),
        cost_estimate=pl.CostEstimate(flops=1, bytes_accessed=1, transcendentals=0),
    )(starts, *operands, filled)


def shards(queries, key_input, value_input, gate_input, kv_state, norm_gain, out_weight):
    n_seq, n_head = lax.axis_size("seq"), lax.axis_size("head")
    inner = n_seq // LINE
    place, h = lax.axis_index("seq"), lax.axis_index("head")
    z, i = place // inner, place % inner
    tok_rows, local_width = queries.shape
    assert tok_rows == BLOCK
    heads = local_width // DH
    total_width = local_width * n_head
    width = out_weight.shape[1]
    cuts = 2 if width % (2 * DH) == 0 else 1
    cut = width // cuts

    def along(value, hops):
        return lax.ppermute(value, "seq", line_pairs(n_seq, hops))

    w_cuts = [out_weight[:, k * cut : (k + 1) * cut] for k in range(cuts)]
    w_pair = [along(w_cuts[0], SWAP_OUTER)]
    w_mid1 = [along(w_cuts[0], SWAP_MIDDLE)]

    def later(from_left):
        for cut_columns in w_cuts[1:]:
            cut_columns = hold(cut_columns, from_left)
            w_pair.append(along(cut_columns, SWAP_OUTER))
            w_mid1.append(along(cut_columns, SWAP_MIDDLE))
        return w_pair[1:] + w_mid1[1:]

    terms, far = state_prefix(
        key_input, value_input, n_seq, place, [w_pair[0], w_mid1[0]], later
    )
    some = heads // 2
    inners = [
        causal_part(queries, key_input, value_input, 0, some),
        causal_part(queries, key_input, value_input, some, heads - some),
    ]

    w_mid2 = [along(hold(w_pair[k], far), SWAP_MIDDLE) for k in range(cuts)]
    w_end1 = [along(hold(w_mid1[k], far), TO_ENDS) for k in range(cuts)]
    w_end2 = [along(w_mid2[k], TO_ENDS) for k in range(cuts)]

    bits = n_head.bit_length() - 1
    order = [int(format(j, "b").zfill(bits)[::-1], 2) for j in range(n_head)] if bits else [0]
    hidden, squares = gated_hidden(
        queries, inners, kv_state, terms, gate_input, norm_gain, h, i, order
    )
    others = [lax.ppermute(hidden, "seq", turn_pairs(n_seq, turn)) for turn in range(1, inner)]

    out_rows = tok_rows // n_head
    half, bit, square_steps = n_head // 2, 1, []
    while bit < n_head:
        square_steps.append(lax.ppermute(squares[half:], "head", flip_pairs(n_head, bit)))
        squares = squares[:half] + square_steps[-1]
        half //= 2
        bit *= 2

    is_end = (z == 0) | (z == LINE - 1)
    low = z < LINE // 2
    flag = scalars(is_end)

    def summed(flag, rows_list, members, weights, blocks):
        sent, kept = project(rows_list, weights, flag)
        bit, steps = 1, []
        while bit < n_head:
            steps.append(lax.ppermute(sent, "head", flip_pairs(n_head, bit)))
            bit *= 2
            if bit < n_head:
                sent, kept = fold(kept, steps[-1], True)
            else:
                kept = fold(kept, steps[-1], False)
        pieces = []
        for position, turn in enumerate(members):
            piece = kept[position]
            if turn:
                piece = lax.ppermute(piece, "seq", turn_pairs(n_seq, -turn))
            starts = [(block * inner + (i + turn) % inner) * width + k * cut for block, k in blocks]
            pieces.append((piece, starts))
        return pieces, steps

    own_turn, other_turns = [0], list(range(1, inner))
    early = [(w,) for w in w_cuts] + [(w,) for w in w_pair]
    early_blocks = [(z, k) for k in range(cuts)] + [(z ^ 1, k) for k in range(cuts)]
    third = [(w_mid1[k], w_end1[k]) for k in range(cuts)]
    third_blocks = [(jnp.where(low, 2, 1), k) for k in range(cuts)]
    fourth = [(w_mid2[k], w_end2[k]) for k in range(cuts)]
    fourth_block = jnp.where(low, 3, 0)
    rows_list, turns = [hidden] + others, own_turn + other_turns
    flag = hold(flag, w_end1[0], w_mid2[0], *square_steps[:1])
    pieces, steps = summed(flag, [hidden], own_turn, early, early_blocks)
    flag = hold(flag, squares, *steps, *w_end1, *w_mid2)
    more, steps = summed(flag, [hidden], own_turn, third, third_blocks)
    pieces += more
    flag = hold(flag, *steps, w_end2[0])
    partner_steps = []
    if others:
        more, partner_steps = summed(flag, others, other_turns, early + third, early_blocks + third_blocks)
        pieces += more
    for k in range(cuts):
        flag = hold(flag, *(partner_steps if k else partner_steps[:1]))
        last, steps = summed(flag, rows_list, turns, [fourth[k]], [(fourth_block, k)])
        flag = hold(flag, *steps[:1])
        if k + 1 < cuts:
            pieces += last
    shape = (out_rows, width * n_seq)
    if cut % DH == 0 and out_rows == DH:
        filled = placed(None, pieces, squares, cut, shape, total_width)
        return placed(filled, last, squares, cut, shape, total_width)
    scale = lax.rsqrt(squares.reshape(out_rows, 1) / total_width + epsilon)
    output = jnp.zeros(shape, jnp.bfloat16)
    for piece, starts in pieces + last:
        piece = (piece.astype(jnp.float32) * scale).astype(jnp.bfloat16)
        for index, start in enumerate(starts):
            part = piece[:, index * cut : (index + 1) * cut]
            output = lax.dynamic_update_slice_in_dim(output, part, start, 1)
    return output


def solution(mesh):
    in_specs = (
        P("seq", "head"),
        P("seq", "head"),
        P("seq", "head"),
        P("seq", "head"),
        P("head", None, None),
        P(),
        P("head", "seq"),
    )
    out_specs = P(("seq", "head"), None)
    return jax.shard_map(shards, mesh=mesh, in_specs=in_specs, out_specs=out_specs, check_vma=False)
```

time: 247 us -> 152 us (0.62)
  waiting for transfers between devices: 184 us -> 72.5 us
  starting transfers between devices: 7.12 us -> 39 us
  Pallas kernels: 0 us -> 23.8 us
  matrix products: 19.5 us -> 0 us
  blocking collectives: 16.9 us -> 0 us
  between operations: 13.2 us -> 0.5 us
  local copies, waits for them, and re-layouts: 4.4 us -> 15.1 us
    all_gather x2 -> x0, waiting for transfers between devices: 113 us -> none  [the longest x1 62 us: shards(): lax.all_gather(out_weight, 'seq', axis=1, tiled=True)]
    ppermute x0 -> x31, waiting for transfers between devices: none -> 72.5 us  [the longest x10 41.7 us: along(): return lax.ppermute(value, 'seq', line_pairs(n_seq, hops))]
    reduce_scatter x1 -> x0, waiting for transfers between devices: 42.9 us -> none  [shards(): lax.psum_scatter(terms.astype(jnp.bfloat16), 'head', scatter_dimension=0,...]
    ppermute x0 -> x31, starting transfers between devices: none -> 39 us  [the longest x10 18.3 us: along(): return lax.ppermute(value, 'seq', line_pairs(n_seq, hops))]
    all_to_all x2 -> x0, waiting for transfers between devices: 26.9 us -> none  [the longest x1 13.8 us: shards(): lax.all_to_all(gate_input, 'head', split_axis=0, concat_axis=1, tiled=True)]
    pallas_call x0 -> x25, Pallas kernels: none -> 23.8 us  [the longest x24 22.5 us: local_call(): pl.pallas_call(kernel, in_specs=[pl.BlockSpec(memory_space=pltpu.SMEM)] +...]
    dot_general x4 -> x0, matrix products: 19.5 us -> none  [the longest x1 9.4 us: shards(): jnp.dot(hidden, lax.all_gather(out_weight, 'seq', axis=1, tiled=True), pr...]
    all_to_all x1 -> x0, blocking collectives: 16.9 us -> none  [shards(): lax.all_to_all(normed, 'head', split_axis=1, concat_axis=0, tiled=True)]
  transfers between devices with their start and end apart: 5 -> 31, of which waited for: 5 -> 16; matrix products, arithmetic and copies ran while one was open for 5% -> 0% of each run, Pallas kernels for 0% -> 9%
where the time goes in v4:
time: 152 us; the launch traced here: 151 us
  waiting for transfers between devices  72.5 us (48%)
  starting transfers between devices  39 us (26%)
  Pallas kernels  23.8 us (16%)
  local copies, waits for them, and re-layouts  15.1 us (10%)
    ppermute x10, waiting for transfers between devices, along(): return lax.ppermute(value, 'seq', line_pairs(n_seq, hops))  41.7 us
    pallas_call x24, Pallas kernels, local_call(): pl.pallas_call(kernel, in_specs=[pl.BlockSpec(memory_space=pltpu.SMEM)] +...  22.5 us
    ppermute x10, starting transfers between devices, along(): return lax.ppermute(value, 'seq', line_pairs(n_seq, hops))  18.3 us
    ppermute x10, waiting for transfers between devices, summed(): steps.append(lax.ppermute(sent, 'head', flip_pairs(n_head, bit)))  15.5 us
    unnamed x38, local copies, waits for them, and re-layouts  12.6 us
    ppermute x10, starting transfers between devices, summed(): steps.append(lax.ppermute(sent, 'head', flip_pairs(n_head, bit)))  7.39 us
    ppermute x2, waiting for transfers between devices, shards(): lax.ppermute(squares[half:], 'head', flip_pairs(n_head, bit))  7.33 us
    ppermute x1, starting transfers between devices, state_prefix(): lax.ppermute(hold(first, *early), 'seq', line_pairs(n_seq, [(0, 1), (2, 3...  3.64 us
  transfers between devices with their start and end apart: 31, of which 16 were waited for; matrix products, arithmetic and copies ran while one was open for 0% of the time, Pallas kernels for 9%

profile of v4, /device:TPU:0, one launch (start us, length us, event | category | flops | bytes accessed | tf_op | source)
XLA Modules:
  0.0 151.1 jit_solution(2895095190215232279)
XLA Ops:
  0.0 2.4 %fusion = (bf16[1024,256]{1,0:T(8,128)(2,1)}, bf16[1024,256]{1,0:T(8,128)(2,1)}) fusion(bf16[1024,512]{1,0:T(8,128)(2,1)} %param.13), kind=kLoop, calls=%fused_computation.5 | loop fusion | bytes 2097152 | tf_op jit(solution)/shard_map/slice | solution.py:370
  2.4 1.4 collective-permute-start.2
  3.9 5.1 %collective-permute-start.1 = (bf16[1024,256]{1,0:T(8,128)(2,1)}, bf16[1024,256]{1,0:T(8,128)(2,1)}, u32[]{:S(2)}, u32[]{:S(2)}) collective-permute-start(bf16[1024,256]{1,0:T(8,128)(2,1)} %get-tuple-element.88.refs_1_), channel_id=1, source_target_pairs={{0,8},{4,12},{8,0},{12,4},{16,24},{20,28},{24,16},{28,20},{1,9},{5... | collective-permute-start | bytes 1572872 | tf_op jit(solution)/shard_map/ppermute | solution.py:368
  9.5 1.6 %collective-permute-start = (bf16[4,128,128]{2,1,0:T(8,128)(2,1)S(1)}, bf16[4,128,128]{2,1,0:T(8,128)(2,1)S(1)}, u32[]{:S(2)}, u32[]{:S(2)}) collective-permute-start(bf16[4,128,128]{2,1,0:T(8,128)(2,1)S(1)} %shard_map.74), channel_id=1, source_target_pairs={{0,4},{4,0},{8,12},{12,8},{16,20},{20,16},{24,28},{28,24},{1,5},{5... | collective-permute-start | bytes 393224 | tf_op jit(solution)/shard_map/ppermute | solution.py:121
  11.5 3.0 %collective-permute-done.refs_1_.refs_4_ = bf16[4,128,128]{2,1,0:T(8,128)(2,1)S(1)} collective-permute-done((bf16[4,128,128]{2,1,0:T(8,128)(2,1)S(1)}, bf16[4,128,128]{2,1,0:T(8,128)(2,1)S(1)}, u32[]{:S(2)}, u32[]{:S(2)}) %collective-permute-start) | collective-permute-done | bytes 131104 | tf_op jit(solution)/shard_map/ppermute | solution.py:121
  14.5 6.4 %collective-permute-done.1.refs_3_ = bf16[1024,256]{1,0:T(8,128)(2,1)} collective-permute-done((bf16[1024,256]{1,0:T(8,128)(2,1)}, bf16[1024,256]{1,0:T(8,128)(2,1)}, u32[]{:S(2)}, u32[]{:S(2)}) %collective-permute-start.1) | collective-permute-done | bytes 524320 | tf_op jit(solution)/shard_map/ppermute | solution.py:368
  20.9 3.6 %collective-permute-start.3 = (bf16[4,128,128]{2,1,0:T(8,128)(2,1)S(1)}, bf16[4,128,128]{2,1,0:T(8,128)(2,1)S(1)}, u32[]{:S(2)}, u32[]{:S(2)}) collective-permute-start(bf16[4,128,128]{2,1,0:T(8,128)(2,1)S(1)} %shard_map.75), channel_id=1, source_target_pairs={{0,8},{4,12},{16,24},{20,28},{1,9},{5,13},{17,25},{21,29},{2,10},{... | collective-permute-start | bytes 393224 | tf_op jit(solution)/shard_map/ppermute | solution.py:124
  24.6 2.5 %collective-permute-done.3.refs_2_.refs_0_ = bf16[4,128,128]{2,1,0:T(8,128)(2,1)S(1)} collective-permute-done((bf16[4,128,128]{2,1,0:T(8,128)(2,1)S(1)}, bf16[4,128,128]{2,1,0:T(8,128)(2,1)S(1)}, u32[]{:S(2)}, u32[]{:S(2)}) %collective-permute-start.3) | collective-permute-done | bytes 131104 | tf_op jit(solution)/shard_map/ppermute | solution.py:124
  27.1 1.5 collective-permute-start.6
  28.5 3.0 %collective-permute-start.5 = (bf16[1024,256]{1,0:T(8,128)(2,1)}, bf16[1024,256]{1,0:T(8,128)(2,1)}, u32[]{:S(2)}, u32[]{:S(2)}) collective-permute-start(bf16[1024,256]{1,0:T(8,128)(2,1)} %get-tuple-element.47.refs_2_), channel_id=1, source_target_pairs={{0,8},{4,12},{8,0},{12,4},{16,24},{20,28},{24,16},{28,20},{1,9},{5... | collective-permute-start | bytes 1572872 | tf_op jit(solution)/shard_map/ppermute | solution.py:368
  31.5 0.7 shard_map.76
  32.2 0.7 copy-done.9
  32.9 0.7 collective-permute-start.7
  33.6 0.7 copy-done.14
  34.2 1.3 collective-permute-start.11
  35.5 1.5 collective-permute-start.12
  37.0 1.3 collective-permute-start.4
  38.4 3.0 %collective-permute-done.5.refs_4_ = bf16[1024,256]{1,0:T(8,128)(2,1)} collective-permute-done((bf16[1024,256]{1,0:T(8,128)(2,1)}, bf16[1024,256]{1,0:T(8,128)(2,1)}, u32[]{:S(2)}, u32[]{:S(2)}) %collective-permute-start.5) | collective-permute-done | bytes 524320 | tf_op jit(solution)/shard_map/ppermute | solution.py:368
  41.4 0.9 copy-done.10
  42.3 0.9 copy-done.15
  43.2 1.7 %shard_map.77 = (f32[4,128,128]{2,1,0:T(8,128)S(1)}, bf16[4,128,128]{2,1,0:T(8,128)(2,1)}) custom-call(s32[4]{0:T(128)S(1)} %add_convert_fusion.masks_ref, bf16[4,128,128]{2,1,0:T(8,128)(2,1)S(1)} %copy-done.10, bf16[4,128,128]{2,1,0:T(8,128)(2,1)} %collective-permute-done.4.refs_1_, bf16[4,128,128]{2,1,0:T(8,128)(2,1)S(1)} %copy-done.15, ...), custom_call_target="tpu_custom_call" | custom-call | flops 1 | bytes 1 | tf_op jit(solution)/shard_map/pallas_call | solution.py:47
  44.9 0.7 copy-done.12
  45.6 1.5 collective-permute-start.8
  47.1 1.1 shard_map.78.refs_2_
  48.2 1.0 copy-done.3
  49.2 1.1 shard_map.79.refs_3_
  50.3 1.0 copy-done.5
  51.4 1.2 copy-done.4
  52.6 1.2 copy-done.6
  53.9 1.2 copy-done.8
  55.1 1.0 copy-done.11
  56.1 1.7 %shard_map.80 = (bf16[512,1024]{1,0:T(8,128)(2,1)S(1)}, f32[4,128]{1,0:T(4,128)S(1)}) custom-call(s32[2]{0:T(128)S(1)} %pad_add_fusion.1.place_ref, bf16[512,1024]{1,0:T(8,128)(2,1)S(1)} %copy-done.2, bf16[512,1024]{1,0:T(8,128)(2,1)S(1)} %copy-done.8, f32[32,1,128]{2,1,0:T(1,128)S(1)} %bitcast.24, f32[8,128,128]{2,1,0:T(8,128)S(1)} %copy-done.11, ...), custom_call_target="tpu_custom_call" | custom-call | flops 1 | bytes 1 | tf_op jit(solution)/shard_map/pallas_call | solution.py:47
  58.5 1.1 collective-permute-done.9
  59.6 2.8 %shard_map.81 = (bf16[1,256,1024]{2,1,0:T(8,128)(2,1)S(1)}, f32[1,256,1024]{2,1,0:T(8,128)S(1)}) custom-call(s32[1]{0:T(128)} %bitcast.9.flag_ref, bf16[512,1024]{1,0:T(8,128)(2,1)S(1)} %get-tuple-element.55.refs_0_, bf16[1024,256]{1,0:T(8,128)(2,1)} %get-tuple-element.88.refs_1_, bf16[1024,256]{1,0:T(8,128)(2,1)} %get-tuple-element.47.refs_2_, ...), custom_call_target="tpu_custom_call" | custom-call | flops 1 | bytes 1 | tf_op jit(solution)/shard_map/pallas_call | solution.py:47
  62.6 0.9 collective-permute-start.20
  63.5 1.3 collective-permute-start.15
  64.8 0.7 collective-permute-start.16
  65.6 1.6 %collective-permute-start.14 = (bf16[1,128,1024]{2,1,0:T(8,128)(2,1)S(1)}, bf16[1,128,1024]{2,1,0:T(8,128)(2,1)S(1)}, u32[]{:S(2)}, u32[]{:S(2)}) collective-permute-start(bf16[1,128,1024]{2,1,0:T(8,128)(2,1)S(1)} %get-tuple-element.58), channel_id=1, source_target_pairs={{0,2},{1,3},{2,0},{3,1},{4,6},{5,7},{6,4},{7,5},{8,10},{9,11},{10,... | collective-permute-start | bytes 786440 | tf_op jit(solution)/shard_map/ppermute | solution.py:417
  67.8 6.2 %collective-permute-done.10 = f32[1,128]{1,0:T(1,128)S(1)} collective-permute-done((f32[1,128]{1,0:T(1,128)S(1)}, f32[1,128]{1,0:T(1,128)S(1)}, u32[]{:S(2)}, u32[]{:S(2)}) %collective-permute-start.10) | collective-permute-done | bytes 544 | tf_op jit(solution)/shard_map/ppermute | solution.py:404
  74.0 1.3 collective-permute-start.19
  75.3 23.9 %collective-permute-done.15.refs_4_.refs_8_ = bf16[1024,256]{1,0:T(8,128)(2,1)S(1)} collective-permute-done((bf16[1024,256]{1,0:T(8,128)(2,1)}, bf16[1024,256]{1,0:T(8,128)(2,1)S(1)}, u32[]{:S(2)}, u32[]{:S(2)}) %collective-permute-start.15) | collective-permute-done | bytes 524320 | tf_op jit(solution)/shard_map/ppermute | solution.py:368
  99.2 2.2 %shard_map.83 = (bf16[1,256,512]{2,1,0:T(8,128)(2,1)S(1)}, f32[1,256,512]{2,1,0:T(8,128)S(1)}) custom-call(s32[1]{0:T(128)} %bitcast.9.flag_ref, bf16[512,1024]{1,0:T(8,128)(2,1)S(1)} %get-tuple-element.55.refs_0_, bf16[1024,256]{1,0:T(8,128)(2,1)} %collective-permute-done.2.refs_1_.refs_5_, bf16[1024,256]{1,0:T(8,128)(2,1)} %collective-permute-done.11.refs_2_.refs_6_, ...), custom_call_target="tpu_custom_call" | custom-call | flops 1 | bytes 1 | tf_op jit(solution)/shard_map/pallas_call | solution.py:47
  101.6 1.5 %collective-permute-done.17.got_ref = bf16[1,256,512]{2,1,0:T(8,128)(2,1)S(1)} collective-permute-done((bf16[1,256,512]{2,1,0:T(8,128)(2,1)S(1)}, bf16[1,256,512]{2,1,0:T(8,128)(2,1)S(1)}, u32[]{:S(2)}, u32[]{:S(2)}) %collective-permute-start.17) | collective-permute-done | bytes 262176 | tf_op jit(solution)/shard_map/ppermute | solution.py:417
  103.1 1.6 %collective-permute-start.18 = (bf16[1,128,512]{2,1,0:T(8,128)(2,1)S(1)}, bf16[1,128,512]{2,1,0:T(8,128)(2,1)S(1)}, u32[]{:S(2)}, u32[]{:S(2)}) collective-permute-start(bf16[1,128,512]{2,1,0:T(8,128)(2,1)S(1)} %get-tuple-element.64), channel_id=1, source_target_pairs={{0,2},{1,3},{2,0},{3,1},{4,6},{5,7},{6,4},{7,5},{8,10},{9,11},{10,... | collective-permute-start | bytes 393224 | tf_op jit(solution)/shard_map/ppermute | solution.py:417
  104.7 7.2 %collective-permute-done.19.refs_3_ = bf16[1024,256]{1,0:T(8,128)(2,1)S(1)} collective-permute-done((bf16[1024,256]{1,0:T(8,128)(2,1)}, bf16[1024,256]{1,0:T(8,128)(2,1)S(1)}, u32[]{:S(2)}, u32[]{:S(2)}) %collective-permute-start.19) | collective-permute-done | bytes 524320 | tf_op jit(solution)/shard_map/ppermute | solution.py:368
  111.9 5.3 %shard_map.85 = (bf16[1,256,1536]{2,1,0:T(8,128)(2,1)S(1)}, f32[1,256,1536]{2,1,0:T(8,128)}) custom-call(s32[1]{0:T(128)} %bitcast.9.flag_ref, bf16[512,1024]{1,0:T(8,128)(2,1)S(1)} %collective-permute-done.20.refs_0_.refs_1_, bf16[1024,256]{1,0:T(8,128)(2,1)} %get-tuple-element.88.refs_1_, bf16[1024,256]{1,0:T(8,128)(2,1)} %get-tuple-element.47.refs_2_, ...), custom_call_target="tpu_custom_call" | custom-call | flops 1 | bytes 1 | tf_op jit(solution)/shard_map/pallas_call | solution.py:47
  117.3 1.3 collective-permute-start.24
  118.5 1.0 collective-permute-done.21.got_ref
  119.5 1.4 copy-done.7
  121.1 1.6 %collective-permute-start.23 = (bf16[1,128,1536]{2,1,0:T(8,128)(2,1)S(1)}, bf16[1,128,1536]{2,1,0:T(8,128)(2,1)S(1)}, u32[]{:S(2)}, u32[]{:S(2)}) collective-permute-start(bf16[1,128,1536]{2,1,0:T(8,128)(2,1)S(1)} %get-tuple-element.71), channel_id=1, source_target_pairs={{0,2},{1,3},{2,0},{3,1},{4,6},{5,7},{6,4},{7,5},{8,10},{9,11},{10,... | collective-permute-start | bytes 1179656 | tf_op jit(solution)/shard_map/ppermute | solution.py:417
  122.7 1.7 %shard_map.86 = (bf16[2,256,256]{2,1,0:T(8,128)(2,1)S(1)}, f32[2,256,256]{2,1,0:T(8,128)S(1)}) custom-call(s32[1]{0:T(128)} %bitcast.9.flag_ref, bf16[512,1024]{1,0:T(8,128)(2,1)S(1)} %get-tuple-element.55.refs_0_, bf16[512,1024]{1,0:T(8,128)(2,1)S(1)} %collective-permute-done.20.refs_0_.refs_1_, bf16[1024,256]{1,0:T(8,128)(2,1)} %collective-permute-done.12.refs_2_, ...), custom_call_target="tpu_custom_call" | custom-call | flops 1 | bytes 1 | tf_op jit(solution)/shard_map/pallas_call | solution.py:47
  124.5 1.5 %collective-permute-done.22.got_ref = bf16[2,256,256]{2,1,0:T(8,128)(2,1)S(1)} collective-permute-done((bf16[2,256,256]{2,1,0:T(8,128)(2,1)S(1)}, bf16[2,256,256]{2,1,0:T(8,128)(2,1)S(1)}, u32[]{:S(2)}, u32[]{:S(2)}) %collective-permute-start.22) | collective-permute-done | bytes 262176 | tf_op jit(solution)/shard_map/ppermute | solution.py:417
  126.0 6.3 %collective-permute-done.23.got_ref = bf16[1,128,1536]{2,1,0:T(8,128)(2,1)S(1)} collective-permute-done((bf16[1,128,1536]{2,1,0:T(8,128)(2,1)S(1)}, bf16[1,128,1536]{2,1,0:T(8,128)(2,1)S(1)}, u32[]{:S(2)}, u32[]{:S(2)}) %collective-permute-start.23) | collective-permute-done | bytes 393248 | tf_op jit(solution)/shard_map/ppermute | solution.py:417
  132.3 1.2 collective-permute-done.24.refs_3_
  133.5 0.7 shard_map.88
  134.3 1.2 collective-permute-start.28
  135.6 1.6 %collective-permute-start.29 = (bf16[2,128,256]{2,1,0:T(8,128)(2,1)S(1)}, bf16[2,128,256]{2,1,0:T(8,128)(2,1)S(1)}, u32[]{:S(2)}, u32[]{:S(2)}) collective-permute-start(bf16[2,128,256]{2,1,0:T(8,128)(2,1)S(1)} %get-tuple-element.84), channel_id=1, source_target_pairs={{0,2},{1,3},{2,0},{3,1},{4,6},{5,7},{6,4},{7,5},{8,10},{9,11},{10,... | collective-permute-start | bytes 393224 | tf_op jit(solution)/shard_map/ppermute | solution.py:417
  137.9 4.1 %collective-permute-done.29.got_ref = bf16[2,128,256]{2,1,0:T(8,128)(2,1)S(1)} collective-permute-done((bf16[2,128,256]{2,1,0:T(8,128)(2,1)S(1)}, bf16[2,128,256]{2,1,0:T(8,128)(2,1)S(1)}, u32[]{:S(2)}, u32[]{:S(2)}) %collective-permute-start.29) | collective-permute-done | bytes 131104 | tf_op jit(solution)/shard_map/ppermute | solution.py:417
  142.0 1.0 collective-permute-start.30
  143.0 1.1 collective-permute-done.26.got_ref
  144.1 1.0 collective-permute-start.27
  145.2 2.5 %collective-permute-done.30.refs_4_ = bf16[128,256]{1,0:T(8,128)(2,1)S(1)} collective-permute-done((bf16[128,256]{1,0:T(8,128)(2,1)S(1)}, bf16[128,256]{1,0:T(8,128)(2,1)S(1)}, u32[]{:S(2)}, u32[]{:S(2)}) %collective-permute-start.30) | collective-permute-done | bytes 65568 | tf_op jit(solution)/shard_map/ppermute | solution.py:427
  147.7 1.9 %shard_map.96.refs_2_ = bf16[128,4096]{1,0:T(8,128)(2,1)} custom-call(s32[14]{0:T(128)S(1)} %stack.118.starts_ref, f32[1,128]{1,0:T(1,128)S(1)} %slice_add_fusion.1.squares_ref, bf16[128,1024]{1,0:T(8,128)(2,1)S(1)} %shard_map.91.refs_0_, bf16[128,512]{1,0:T(8,128)(2,1)S(1)} %shard_map.92.refs_1_, bf16[128,1536]{1,0:T(8,128)(2,1)S(1)} %collective-permute-done.28.refs_2_, ...), custom_call_target="tpu_custom_call" | custom-call | flops 1 | bytes 1 | tf_op jit(solution)/shard_map/pallas_call | solution.py:47
  149.6 1.3 shard_map.97
  (70 shorter events, 4.2 us)
Async XLA Ops:
  0.0 9.0 %copy-start.1 = (bf16[512,1024]{1,0:T(8,128)(2,1)S(1)}, bf16[512,1024]{1,0:T(8,128)(2,1)}, u32[]{:S(2)}) copy-start(bf16[512,1024]{1,0:T(8,128)(2,1)} %v_ref.7) | copy-start | bytes 3145732
  0.0 9.0 %copy-start = (bf16[512,1024]{1,0:T(8,128)(2,1)S(1)}, bf16[512,1024]{1,0:T(8,128)(2,1)}, u32[]{:S(2)}) copy-start(bf16[512,1024]{1,0:T(8,128)(2,1)} %k_ref.7) | copy-start | bytes 3145732
  2.4 12.1 %collective-permute-start.2 = (bf16[1024,256]{1,0:T(8,128)(2,1)}, bf16[1024,256]{1,0:T(8,128)(2,1)}, u32[]{:S(2)}, u32[]{:S(2)}) collective-permute-start(bf16[1024,256]{1,0:T(8,128)(2,1)} %get-tuple-element.88.refs_1_), channel_id=1, source_target_pairs={{8,16},{12,20},{16,8},{20,12},{9,17},{13,21},{17,9},{21,13},{10,18... | collective-permute-start | bytes 1572872 | tf_op jit(solution)/shard_map/ppermute | solution.py:368
  3.9 17.1 %collective-permute-start.1 = (bf16[1024,256]{1,0:T(8,128)(2,1)}, bf16[1024,256]{1,0:T(8,128)(2,1)}, u32[]{:S(2)}, u32[]{:S(2)}) collective-permute-start(bf16[1024,256]{1,0:T(8,128)(2,1)} %get-tuple-element.88.refs_1_), channel_id=1, source_target_pairs={{0,8},{4,12},{8,0},{12,4},{16,24},{20,28},{24,16},{28,20},{1,9},{5... | collective-permute-start | bytes 1572872 | tf_op jit(solution)/shard_map/ppermute | solution.py:368
  9.5 5.0 %collective-permute-start = (bf16[4,128,128]{2,1,0:T(8,128)(2,1)S(1)}, bf16[4,128,128]{2,1,0:T(8,128)(2,1)S(1)}, u32[]{:S(2)}, u32[]{:S(2)}) collective-permute-start(bf16[4,128,128]{2,1,0:T(8,128)(2,1)S(1)} %shard_map.74), channel_id=1, source_target_pairs={{0,4},{4,0},{8,12},{12,8},{16,20},{20,16},{24,28},{28,24},{1,5},{5... | collective-permute-start | bytes 393224 | tf_op jit(solution)/shard_map/ppermute | solution.py:121
  11.5 35.6 %copy-start.2 = (bf16[512,1024]{1,0:T(8,128)(2,1)S(1)}, bf16[512,1024]{1,0:T(8,128)(2,1)}, u32[]{:S(2)}) copy-start(bf16[512,1024]{1,0:T(8,128)(2,1)} %q_ref.5) | copy-start | bytes 3145732
  20.9 6.1 %collective-permute-start.3 = (bf16[4,128,128]{2,1,0:T(8,128)(2,1)S(1)}, bf16[4,128,128]{2,1,0:T(8,128)(2,1)S(1)}, u32[]{:S(2)}, u32[]{:S(2)}) collective-permute-start(bf16[4,128,128]{2,1,0:T(8,128)(2,1)S(1)} %shard_map.75), channel_id=1, source_target_pairs={{0,8},{4,12},{16,24},{20,28},{1,9},{5,13},{17,25},{21,29},{2,10},{... | collective-permute-start | bytes 393224 | tf_op jit(solution)/shard_map/ppermute | solution.py:124
  27.1 11.3 %collective-permute-start.6 = (bf16[1024,256]{1,0:T(8,128)(2,1)}, bf16[1024,256]{1,0:T(8,128)(2,1)}, u32[]{:S(2)}, u32[]{:S(2)}) collective-permute-start(bf16[1024,256]{1,0:T(8,128)(2,1)} %get-tuple-element.47.refs_2_), channel_id=1, source_target_pairs={{8,16},{12,20},{16,8},{20,12},{9,17},{13,21},{17,9},{21,13},{10,18... | collective-permute-start | bytes 1572872 | tf_op jit(solution)/shard_map/ppermute | solution.py:368
  28.5 12.9 %collective-permute-start.5 = (bf16[1024,256]{1,0:T(8,128)(2,1)}, bf16[1024,256]{1,0:T(8,128)(2,1)}, u32[]{:S(2)}, u32[]{:S(2)}) collective-permute-start(bf16[1024,256]{1,0:T(8,128)(2,1)} %get-tuple-element.47.refs_2_), channel_id=1, source_target_pairs={{0,8},{4,12},{8,0},{12,4},{16,24},{20,28},{24,16},{28,20},{1,9},{5... | collective-permute-start | bytes 1572872 | tf_op jit(solution)/shard_map/ppermute | solution.py:368
  32.2 0.7 copy-start.9
  32.9 0.7 collective-permute-start.7
  33.5 0.7 copy-start.14
  34.2 24.2 %collective-permute-start.11 = (bf16[1024,256]{1,0:T(8,128)(2,1)}, bf16[1024,256]{1,0:T(8,128)(2,1)}, u32[]{:S(2)}, u32[]{:S(2)}) collective-permute-start(bf16[1024,256]{1,0:T(8,128)(2,1)} %collective-permute-done.2.refs_1_.refs_5_), channel_id=1, source_target_pairs={{8,0},{12,4},{16,24},{20,28},{9,1},{13,5},{17,25},{21,29},{10,2},{... | collective-permute-start | bytes 1572872 | tf_op jit(solution)/shard_map/ppermute | solution.py:368
  35.5 22.9 %collective-permute-start.12 = (bf16[1024,256]{1,0:T(8,128)(2,1)}, bf16[1024,256]{1,0:T(8,128)(2,1)}, u32[]{:S(2)}, u32[]{:S(2)}) collective-permute-start(bf16[1024,256]{1,0:T(8,128)(2,1)} %collective-permute-done.1.refs_3_), channel_id=1, source_target_pairs={{8,16},{12,20},{16,8},{20,12},{9,17},{13,21},{17,9},{21,13},{10,18... | collective-permute-start | bytes 1572872 | tf_op jit(solution)/shard_map/ppermute | solution.py:368
  37.0 1.4 collective-permute-start.4
  41.4 0.9 copy-start.10
  42.3 0.9 copy-start.15
  44.9 0.7 copy-start.12
  45.6 5.8 %collective-permute-start.8 = (bf16[4,128,128]{2,1,0:T(8,128)(2,1)}, bf16[4,128,128]{2,1,0:T(8,128)(2,1)S(1)}, u32[]{:S(2)}, u32[]{:S(2)}) collective-permute-start(bf16[4,128,128]{2,1,0:T(8,128)(2,1)} %get-tuple-element.50), channel_id=1, source_target_pairs={{0,4},{4,0},{8,12},{12,8},{16,20},{20,16},{24,28},{28,24},{1,5},{5... | collective-permute-start | bytes 393224 | tf_op jit(solution)/shard_map/ppermute | solution.py:135
  48.2 1.0 copy-start.3
  49.2 2.2 %copy-start.13 = (f32[4,128,128]{2,1,0:T(8,128)S(1)}, f32[4,128,128]{2,1,0:T(8,128)}, u32[]{:S(2)}) copy-start(f32[4,128,128]{2,1,0:T(8,128)} %copy-done.12) | copy-start | bytes 786436
  49.2 2.2 %copy-start.16 = (f32[4096]{0:T(1024)S(1)}, f32[4096]{0:T(1024)}, u32[]{:S(2)}) copy-start(f32[4096]{0:T(1024)} %param.12) | copy-start | bytes 49156
  50.3 1.0 copy-start.5
  51.4 1.2 copy-start.4
  52.6 1.2 copy-start.6
  53.8 1.2 copy-start.8
  55.1 1.0 copy-start.11
  57.8 0.6 copy-start.17
  58.4 1.1 collective-permute-start.9
  62.3 4.9 %copy-start.18 = (f32[4,128]{1,0:T(4,128)S(1)}, f32[4,128]{1,0:T(4,128)}, u32[]{:S(2)}) copy-start(f32[4,128]{1,0:T(4,128)} %copy-done.17) | copy-start | bytes 6148
  62.4 3.2 %collective-permute-start.13 = (bf16[1,256,1024]{2,1,0:T(8,128)(2,1)S(1)}, bf16[1,256,1024]{2,1,0:T(8,128)(2,1)S(1)}, u32[]{:S(2)}, u32[]{:S(2)}) collective-permute-start(bf16[1,256,1024]{2,1,0:T(8,128)(2,1)S(1)} %get-tuple-element.56), channel_id=1, source_target_pairs={{0,1},{1,0},{2,3},{3,2},{4,5},{5,4},{6,7},{7,6},{8,9},{9,8},{10,11... | collective-permute-start | bytes 1572872 | tf_op jit(solution)/shard_map/ppermute | solution.py:417
  62.6 49.3 %collective-permute-start.20 = (bf16[512,1024]{1,0:T(8,128)(2,1)S(1)}, bf16[512,1024]{1,0:T(8,128)(2,1)S(1)}, u32[]{:S(2)}, u32[]{:S(2)}) collective-permute-start(bf16[512,1024]{1,0:T(8,128)(2,1)S(1)} %get-tuple-element.55.refs_0_), channel_id=1, source_target_pairs={{0,4},{4,0},{8,12},{12,8},{16,20},{20,16},{24,28},{28,24},{1,5},{5... | collective-permute-start | bytes 3145736 | tf_op jit(solution)/shard_map/ppermute | solution.py:399
  63.5 35.7 %collective-permute-start.15 = (bf16[1024,256]{1,0:T(8,128)(2,1)}, bf16[1024,256]{1,0:T(8,128)(2,1)S(1)}, u32[]{:S(2)}, u32[]{:S(2)}) collective-permute-start(bf16[1024,256]{1,0:T(8,128)(2,1)} %collective-permute-done.6.refs_3_.refs_7_), channel_id=1, source_target_pairs={{8,0},{12,4},{16,24},{20,28},{9,1},{13,5},{17,25},{21,29},{10,2},{... | collective-permute-start | bytes 1572872 | tf_op jit(solution)/shard_map/ppermute | solution.py:368
  64.8 34.4 %collective-permute-start.16 = (bf16[1024,256]{1,0:T(8,128)(2,1)}, bf16[1024,256]{1,0:T(8,128)(2,1)S(1)}, u32[]{:S(2)}, u32[]{:S(2)}) collective-permute-start(bf16[1024,256]{1,0:T(8,128)(2,1)} %collective-permute-done.5.refs_4_), channel_id=1, source_target_pairs={{8,16},{12,20},{16,8},{20,12},{9,17},{13,21},{17,9},{21,13},{10,18... | collective-permute-start | bytes 1572872 | tf_op jit(solution)/shard_map/ppermute | solution.py:368
  65.6 33.6 %collective-permute-start.14 = (bf16[1,128,1024]{2,1,0:T(8,128)(2,1)S(1)}, bf16[1,128,1024]{2,1,0:T(8,128)(2,1)S(1)}, u32[]{:S(2)}, u32[]{:S(2)}) collective-permute-start(bf16[1,128,1024]{2,1,0:T(8,128)(2,1)S(1)} %get-tuple-element.58), channel_id=1, source_target_pairs={{0,2},{1,3},{2,0},{3,1},{4,6},{5,7},{6,4},{7,5},{8,10},{9,11},{10,... | collective-permute-start | bytes 786440 | tf_op jit(solution)/shard_map/ppermute | solution.py:417
  67.2 6.8 %collective-permute-start.10 = (f32[1,128]{1,0:T(1,128)S(1)}, f32[1,128]{1,0:T(1,128)S(1)}, u32[]{:S(2)}, u32[]{:S(2)}) collective-permute-start(f32[1,128]{1,0:T(1,128)S(1)} %slice.23), channel_id=1, source_target_pairs={{0,2},{1,3},{2,0},{3,1},{4,6},{5,7},{6,4},{7,5},{8,10},{9,11},{10,... | collective-permute-start | bytes 1544 | tf_op jit(solution)/shard_map/ppermute | solution.py:404
  74.0 37.9 %collective-permute-start.19 = (bf16[1024,256]{1,0:T(8,128)(2,1)}, bf16[1024,256]{1,0:T(8,128)(2,1)S(1)}, u32[]{:S(2)}, u32[]{:S(2)}) collective-permute-start(bf16[1024,256]{1,0:T(8,128)(2,1)} %collective-permute-done.12.refs_2_), channel_id=1, source_target_pairs={{8,0},{12,4},{16,24},{20,28},{9,1},{13,5},{17,25},{21,29},{10,2},{... | collective-permute-start | bytes 1572872 | tf_op jit(solution)/shard_map/ppermute | solution.py:368
  101.5 1.6 %collective-permute-start.17 = (bf16[1,256,512]{2,1,0:T(8,128)(2,1)S(1)}, bf16[1,256,512]{2,1,0:T(8,128)(2,1)S(1)}, u32[]{:S(2)}, u32[]{:S(2)}) collective-permute-start(bf16[1,256,512]{2,1,0:T(8,128)(2,1)S(1)} %get-tuple-element.62), channel_id=1, source_target_pairs={{0,1},{1,0},{2,3},{3,2},{4,5},{5,4},{6,7},{7,6},{8,9},{9,8},{10,11... | collective-permute-start | bytes 786440 | tf_op jit(solution)/shard_map/ppermute | solution.py:417
  103.1 8.8 %collective-permute-start.18 = (bf16[1,128,512]{2,1,0:T(8,128)(2,1)S(1)}, bf16[1,128,512]{2,1,0:T(8,128)(2,1)S(1)}, u32[]{:S(2)}, u32[]{:S(2)}) collective-permute-start(bf16[1,128,512]{2,1,0:T(8,128)(2,1)S(1)} %get-tuple-element.64), channel_id=1, source_target_pairs={{0,2},{1,3},{2,0},{3,1},{4,6},{5,7},{6,4},{7,5},{8,10},{9,11},{10,... | collective-permute-start | bytes 393224 | tf_op jit(solution)/shard_map/ppermute | solution.py:417
  117.3 2.3 %collective-permute-start.21 = (bf16[1,256,1536]{2,1,0:T(8,128)(2,1)S(1)}, bf16[1,256,1536]{2,1,0:T(8,128)(2,1)S(1)}, u32[]{:S(2)}, u32[]{:S(2)}) collective-permute-start(bf16[1,256,1536]{2,1,0:T(8,128)(2,1)S(1)} %get-tuple-element.66), channel_id=1, source_target_pairs={{0,1},{1,0},{2,3},{3,2},{4,5},{5,4},{6,7},{7,6},{8,9},{9,8},{10,11... | collective-permute-start | bytes 2359304 | tf_op jit(solution)/shard_map/ppermute | solution.py:417
  117.3 16.2 %collective-permute-start.24 = (bf16[1024,256]{1,0:T(8,128)(2,1)S(1)}, bf16[1024,256]{1,0:T(8,128)(2,1)S(1)}, u32[]{:S(2)}, u32[]{:S(2)}) collective-permute-start(bf16[1024,256]{1,0:T(8,128)(2,1)S(1)} %collective-permute-done.16.refs_2_), channel_id=1, source_target_pairs={{8,0},{12,4},{16,24},{20,28},{9,1},{13,5},{17,25},{21,29},{10,2},{... | collective-permute-start | bytes 1572872 | tf_op jit(solution)/shard_map/ppermute | solution.py:368
  119.5 1.4 copy-start.7
  121.1 11.2 %collective-permute-start.23 = (bf16[1,128,1536]{2,1,0:T(8,128)(2,1)S(1)}, bf16[1,128,1536]{2,1,0:T(8,128)(2,1)S(1)}, u32[]{:S(2)}, u32[]{:S(2)}) collective-permute-start(bf16[1,128,1536]{2,1,0:T(8,128)(2,1)S(1)} %get-tuple-element.71), channel_id=1, source_target_pairs={{0,2},{1,3},{2,0},{3,1},{4,6},{5,7},{6,4},{7,5},{8,10},{9,11},{10,... | collective-permute-start | bytes 1179656 | tf_op jit(solution)/shard_map/ppermute | solution.py:417
  124.4 1.6 %collective-permute-start.22 = (bf16[2,256,256]{2,1,0:T(8,128)(2,1)S(1)}, bf16[2,256,256]{2,1,0:T(8,128)(2,1)S(1)}, u32[]{:S(2)}, u32[]{:S(2)}) collective-permute-start(bf16[2,256,256]{2,1,0:T(8,128)(2,1)S(1)} %get-tuple-element.68), channel_id=1, source_target_pairs={{0,1},{1,0},{2,3},{3,2},{4,5},{5,4},{6,7},{7,6},{8,9},{9,8},{10,11... | collective-permute-start | bytes 786440 | tf_op jit(solution)/shard_map/ppermute | solution.py:417
  134.2 3.0 %collective-permute-start.25 = (bf16[2,256,256]{2,1,0:T(8,128)(2,1)S(1)}, bf16[2,256,256]{2,1,0:T(8,128)(2,1)S(1)}, u32[]{:S(2)}, u32[]{:S(2)}) collective-permute-start(bf16[2,256,256]{2,1,0:T(8,128)(2,1)S(1)} %get-tuple-element.74), channel_id=1, source_target_pairs={{0,1},{1,0},{2,3},{3,2},{4,5},{5,4},{6,7},{7,6},{8,9},{9,8},{10,11... | collective-permute-start | bytes 786440 | tf_op jit(solution)/shard_map/ppermute | solution.py:417
  134.3 13.4 %collective-permute-start.28 = (bf16[128,1536]{1,0:T(8,128)(2,1)S(1)}, bf16[128,1536]{1,0:T(8,128)(2,1)S(1)}, u32[]{:S(2)}, u32[]{:S(2)}) collective-permute-start(bf16[128,1536]{1,0:T(8,128)(2,1)S(1)} %shard_map.93), channel_id=1, source_target_pairs={{0,4},{4,0},{8,12},{12,8},{16,20},{20,16},{24,28},{28,24},{1,5},{5... | collective-permute-start | bytes 1179656 | tf_op jit(solution)/shard_map/ppermute | solution.py:427
  135.6 6.4 %collective-permute-start.29 = (bf16[2,128,256]{2,1,0:T(8,128)(2,1)S(1)}, bf16[2,128,256]{2,1,0:T(8,128)(2,1)S(1)}, u32[]{:S(2)}, u32[]{:S(2)}) collective-permute-start(bf16[2,128,256]{2,1,0:T(8,128)(2,1)S(1)} %get-tuple-element.84), channel_id=1, source_target_pairs={{0,2},{1,3},{2,0},{3,1},{4,6},{5,7},{6,4},{7,5},{8,10},{9,11},{10,... | collective-permute-start | bytes 393224 | tf_op jit(solution)/shard_map/ppermute | solution.py:417
  137.2 6.8 %collective-permute-start.26 = (bf16[2,128,256]{2,1,0:T(8,128)(2,1)S(1)}, bf16[2,128,256]{2,1,0:T(8,128)(2,1)S(1)}, u32[]{:S(2)}, u32[]{:S(2)}) collective-permute-start(bf16[2,128,256]{2,1,0:T(8,128)(2,1)S(1)} %get-tuple-element.76), channel_id=1, source_target_pairs={{0,2},{1,3},{2,0},{3,1},{4,6},{5,7},{6,4},{7,5},{8,10},{9,11},{10,... | collective-permute-start | bytes 393224 | tf_op jit(solution)/shard_map/ppermute | solution.py:417
  142.0 5.7 %collective-permute-start.30 = (bf16[128,256]{1,0:T(8,128)(2,1)S(1)}, bf16[128,256]{1,0:T(8,128)(2,1)S(1)}, u32[]{:S(2)}, u32[]{:S(2)}) collective-permute-start(bf16[128,256]{1,0:T(8,128)(2,1)S(1)} %get-tuple-element.86), channel_id=1, source_target_pairs={{0,4},{4,0},{8,12},{12,8},{16,20},{20,16},{24,28},{28,24},{1,5},{5... | collective-permute-start | bytes 196616 | tf_op jit(solution)/shard_map/ppermute | solution.py:427
  144.1 5.5 %collective-permute-start.27 = (bf16[128,256]{1,0:T(8,128)(2,1)S(1)}, bf16[128,256]{1,0:T(8,128)(2,1)S(1)}, u32[]{:S(2)}, u32[]{:S(2)}) collective-permute-start(bf16[128,256]{1,0:T(8,128)(2,1)S(1)} %get-tuple-element.78), channel_id=1, source_target_pairs={{0,4},{4,0},{8,12},{12,8},{16,20},{20,16},{24,28},{28,24},{1,5},{5... | collective-permute-start | bytes 196616 | tf_op jit(solution)/shard_map/ppermute | solution.py:427

commit v5 on v4

--- a/solution.py
+++ b/solution.py
@@ -10,7 +10,7 @@
 DH = 128
 BLOCK = 512
 LINE = 4
-VMEM_BYTES = 48 * 1024 * 1024
+VMEM_BYTES = 16 * 1024 * 1024
 
 
 epsilon = 1e-05
@@ -44,6 +44,7 @@
 
 
 def local_call(kernel, places, operands, out_shapes, scratch=()):
+    held = sum(value.size * value.dtype.itemsize for value in [*operands, *out_shapes])
     return pl.pallas_call(
         kernel,
         in_specs=[pl.BlockSpec(memory_space=pltpu.SMEM)]
@@ -51,22 +52,23 @@
         out_specs=[pl.BlockSpec(memory_space=pltpu.VMEM)] * len(out_shapes),
         out_shape=out_shapes,
         scratch_shapes=list(scratch),
-        compiler_params=pltpu.CompilerParams(vmem_limit_bytes=VMEM_BYTES),
+        compiler_params=pltpu.CompilerParams(vmem_limit_bytes=max(VMEM_BYTES, held + held // 2)),
         cost_estimate=pl.CostEstimate(flops=1, bytes_accessed=1, transcendentals=0),
     )(places, *operands)
 
 
 def combine_kernel(count, always, masks_ref, *refs):
     values, outs = refs[:count], refs[count:]
-    total = values[0][...].astype(jnp.float32)
-    for value in values[1:always]:
-        total = total + value[...].astype(jnp.float32)
-    for position, out in enumerate(outs):
-        own = total
-        for k in range(always, count):
-            mask = masks_ref[position * (count - always) + k - always]
-            own = own + jnp.where(mask != 0, values[k][...].astype(jnp.float32), 0.0)
-        out[...] = own.astype(out.dtype)
+    for index in range(values[0].shape[0]):
+        total = values[0][index].astype(jnp.float32)
+        for value in values[1:always]:
+            total = total + value[index].astype(jnp.float32)
+        for position, out in enumerate(outs):
+            own = total
+            for k in range(always, count):
+                mask = masks_ref[position * (count - always) + k - always]
+                own = own + jnp.where(mask != 0, values[k][index].astype(jnp.float32), 0.0)
+            out[index] = own.astype(out.dtype)
 
 
 def combine(values, dtypes, sometimes=(), masks=None):
@@ -78,6 +80,26 @@
         operands,
         [jax.ShapeDtypeStruct(values[0].shape, dtype) for dtype in dtypes],
     )
+
+
+def cut_kernel(first, w_ref, out_ref, sem):
+    copy = pltpu.make_async_copy(w_ref.at[:, pl.ds(first, out_ref.shape[1])], out_ref, sem)
+    copy.start()
+    copy.wait()
+
+
+def cut_columns(weight, first, width):
+    if width % DH:
+        return weight[:, first : first + width]
+    return pl.pallas_call(
+        functools.partial(cut_kernel, first),
+        in_specs=[pl.BlockSpec(memory_space=pl.ANY)],
+        out_specs=pl.BlockSpec(memory_space=pltpu.VMEM),
+        out_shape=jax.ShapeDtypeStruct((weight.shape[0], width), weight.dtype),
+        scratch_shapes=[pltpu.SemaphoreType.DMA],
+        compiler_params=pltpu.CompilerParams(vmem_limit_bytes=VMEM_BYTES),
+        cost_estimate=pl.CostEstimate(flops=1, bytes_accessed=1, transcendentals=0),
+    )(weight)
 
 
 def states_kernel(part_ref, k_ref, v_ref, out_ref):
@@ -101,7 +123,7 @@
     )[0]
 
 
-def state_prefix(key_input, value_input, n_seq, place, early, later):
+def state_prefix(key_input, value_input, n_seq, place, early):
     inner = n_seq // LINE
     i = place % inner
     heads = key_input.shape[1] // DH
@@ -121,19 +143,19 @@
         values.append(lax.ppermute(sends[turn - 1], "seq", turn_pairs(n_seq, turn)))
         members.append((i - turn) % inner)
     (first,) = combine(values, [jnp.bfloat16])
-    from_left = lax.ppermute(hold(first, *early), "seq", line_pairs(n_seq, [(0, 1), (2, 3)]))
+    from_left = lax.ppermute(first, "seq", line_pairs(n_seq, [(0, 1), (2, 3)]))
+    from_left = hold(from_left, *early)
     (second,) = combine(values + [from_left], [jnp.bfloat16])
     near = lax.ppermute(second, "seq", line_pairs(n_seq, [(1, 2)]))
     far = lax.ppermute(second, "seq", line_pairs(n_seq, [(1, 3)]))
     targets = [i] + [(i + turn) % inner for turn in range(1, inner)] if split else [i]
     masks = [owner < target for target in targets for owner in members]
     dtypes = [jnp.float32] + [jnp.bfloat16] * (len(targets) - 1)
-    near = hold(near, *later(from_left))
     befores = combine([from_left, near, far], dtypes, values, masks)
     terms = [befores[0]]
     for turn in range(1, len(targets)):
         terms.append(lax.ppermute(befores[turn], "seq", turn_pairs(n_seq, turn)))
-    return terms, far
+    return terms, [near, far]
 
 
 def causal_kernel(first_head, place_ref, q_ref, k_ref, v_ref, out_ref):
@@ -229,21 +251,22 @@
     )
 
 
-def project_kernel(groups, choices, flag_ref, *refs):
-    rows_refs = refs[:groups]
-    weight_refs = refs[groups : groups + sum(choices)]
-    sent_ref, kept_ref = refs[groups + sum(choices) :]
-    half = sent_ref.shape[1]
+def project_kernel(jobs, n_rows, choices, flag_ref, *refs):
+    rows_refs = refs[:n_rows]
+    weight_refs = refs[n_rows : n_rows + sum(choices)]
+    sent_ref, kept_ref = refs[n_rows + sum(choices) :]
+    half = sent_ref.shape[0]
     width = weight_refs[0].shape[1]
 
     def products(index, weight_ref):
-        columns = pl.ds(index * width, width)
-        for group in range(groups):
-            product = jnp.dot(
-                rows_refs[group][...], weight_ref[...], preferred_element_type=jnp.float32
-            )
-            kept_ref[group, :, columns] = product[:half]
-            sent_ref[group, :, columns] = product[half:].astype(jnp.bfloat16)
+        for position, (rows, weight) in enumerate(jobs):
+            if weight == index:
+                columns = pl.ds(position * width, width)
+                product = jnp.dot(
+                    rows_refs[rows][...], weight_ref[...], preferred_element_type=jnp.float32
+                )
+                kept_ref[:, columns] = product[:half]
+                sent_ref[:, columns] = product[half:].astype(jnp.bfloat16)
 
     first = 0
     for index, number in enumerate(choices):
@@ -256,37 +279,40 @@
         first += number
 
 
-def project(rows_list, weights, flag):
+def project(jobs, rows_list, weights, flag):
     flat = [choice for weight in weights for choice in weight]
     choices = tuple(len(weight) for weight in weights)
-    shape = (len(rows_list), rows_list[0].shape[0] // 2, flat[0].shape[1] * len(weights))
+    shape = (rows_list[0].shape[0] // 2, flat[0].shape[1] * len(jobs))
     return local_call(
-        functools.partial(project_kernel, len(rows_list), choices),
+        functools.partial(project_kernel, tuple(jobs), len(rows_list), choices),
         flag,
         [*rows_list, *flat],
         [jax.ShapeDtypeStruct(shape, jnp.bfloat16), jax.ShapeDtypeStruct(shape, jnp.float32)],
     )
 
 
-def fold_kernel(flag_ref, kept_ref, got_ref, *outs):
-    if len(outs) == 2 and len(outs[0].shape) == 3:
+def fold_kernel(more, flag_ref, kept_ref, got_ref, *outs):
+    if more:
         sent_ref, left_ref = outs
-        half = left_ref.shape[1]
-        left_ref[...] = kept_ref[:, :half] + got_ref[:, :half].astype(jnp.float32)
-        sent_ref[...] = (kept_ref[:, half:] + got_ref[:, half:].astype(jnp.float32)).astype(jnp.bfloat16)
+        half = left_ref.shape[0]
+        left_ref[...] = kept_ref[:half] + got_ref[:half].astype(jnp.float32)
+        sent_ref[...] = (kept_ref[half:] + got_ref[half:].astype(jnp.float32)).astype(jnp.bfloat16)
         return
-    for group, out in enumerate(outs):
-        out[...] = (kept_ref[group] + got_ref[group].astype(jnp.float32)).astype(out.dtype)
-
-
-def fold(kept, got, more):
-    groups, rows, width = kept.shape
-    if more:
-        shape = (groups, rows // 2, width)
+    first = 0
+    for out in outs:
+        columns = pl.ds(first, out.shape[1])
+        out[...] = (kept_ref[:, columns] + got_ref[:, columns].astype(jnp.float32)).astype(out.dtype)
+        first += out.shape[1]
+
+
+def fold(kept, got, widths=None):
+    rows, width = kept.shape
+    if widths is None:
+        shape = (rows // 2, width)
         outs = [jax.ShapeDtypeStruct(shape, jnp.bfloat16), jax.ShapeDtypeStruct(shape, jnp.float32)]
     else:
-        outs = [jax.ShapeDtypeStruct((rows, width), jnp.bfloat16)] * groups
-    return local_call(fold_kernel, scalars(0), [kept, got], outs)
+        outs = [jax.ShapeDtypeStruct((rows, some), jnp.bfloat16) for some in widths]
+    return local_call(functools.partial(fold_kernel, widths is None), scalars(0), [kept, got], outs)
 
 
 def column(row):
@@ -367,28 +393,21 @@
     def along(value, hops):
         return lax.ppermute(value, "seq", line_pairs(n_seq, hops))
 
-    w_cuts = [out_weight[:, k * cut : (k + 1) * cut] for k in range(cuts)]
+    w_cuts = [cut_columns(out_weight, k * cut, cut) for k in range(cuts)]
     w_pair = [along(w_cuts[0], SWAP_OUTER)]
     w_mid1 = [along(w_cuts[0], SWAP_MIDDLE)]
-
-    def later(from_left):
-        for cut_columns in w_cuts[1:]:
-            cut_columns = hold(cut_columns, from_left)
-            w_pair.append(along(cut_columns, SWAP_OUTER))
-            w_mid1.append(along(cut_columns, SWAP_MIDDLE))
-        return w_pair[1:] + w_mid1[1:]
-
-    terms, far = state_prefix(
-        key_input, value_input, n_seq, place, [w_pair[0], w_mid1[0]], later
-    )
+    terms, steps = state_prefix(key_input, value_input, n_seq, place, [w_pair[0], w_mid1[0]])
     some = heads // 2
     inners = [
         causal_part(queries, key_input, value_input, 0, some),
         causal_part(queries, key_input, value_input, some, heads - some),
     ]
 
-    w_mid2 = [along(hold(w_pair[k], far), SWAP_MIDDLE) for k in range(cuts)]
-    w_end1 = [along(hold(w_mid1[k], far), TO_ENDS) for k in range(cuts)]
+    for k in range(1, cuts):
+        w_pair.append(along(hold(w_cuts[k], *steps), SWAP_OUTER))
+        w_mid1.append(along(hold(w_cuts[k], *steps), SWAP_MIDDLE))
+    w_mid2 = [along(hold(w_pair[k], *steps), SWAP_MIDDLE) for k in range(cuts)]
+    w_end1 = [along(hold(w_mid1[k], *steps), TO_ENDS) for k in range(cuts)]
     w_end2 = [along(w_mid2[k], TO_ENDS) for k in range(cuts)]
 
     bits = n_head.bit_length() - 1
@@ -399,10 +418,9 @@
     others = [lax.ppermute(hidden, "seq", turn_pairs(n_seq, turn)) for turn in range(1, inner)]
 
     out_rows = tok_rows // n_head
-    half, bit, square_steps = n_head // 2, 1, []
+    half, bit = n_head // 2, 1
     while bit < n_head:
-        square_steps.append(lax.ppermute(squares[half:], "head", flip_pairs(n_head, bit)))
-        squares = squares[:half] + square_steps[-1]
+        squares = squares[:half] + lax.ppermute(squares[half:], "head", flip_pairs(n_head, bit))
         half //= 2
         bit *= 2
 
@@ -410,47 +428,54 @@
     low = z < LINE // 2
     flag = scalars(is_end)
 
-    def summed(flag, rows_list, members, weights, blocks):
-        sent, kept = project(rows_list, weights, flag)
+    rows_list = [hidden] + others
+
+    def summed(flag, parts):
+        blocks = sorted({block for _, own in parts for block in own})
+        turns = [turn for turn, _ in parts]
+        jobs = [(p, blocks.index(block)) for p, (_, own) in enumerate(parts) for block in own]
+        sent, kept = project(
+            jobs, [rows_list[turn] for turn in turns], [weights[block] for block in blocks], flag
+        )
+        widths = [cut * len(own) for _, own in parts]
         bit, steps = 1, []
         while bit < n_head:
             steps.append(lax.ppermute(sent, "head", flip_pairs(n_head, bit)))
             bit *= 2
             if bit < n_head:
-                sent, kept = fold(kept, steps[-1], True)
+                sent, kept = fold(kept, steps[-1])
             else:
-                kept = fold(kept, steps[-1], False)
+                kept = fold(kept, steps[-1], widths)
         pieces = []
-        for position, turn in enumerate(members):
-            piece = kept[position]
+        for piece, (turn, own) in zip(kept, parts):
             if turn:
                 piece = lax.ppermute(piece, "seq", turn_pairs(n_seq, -turn))
-            starts = [(block * inner + (i + turn) % inner) * width + k * cut for block, k in blocks]
+            starts = [
+                (owners[block] * inner + (i + turn) % inner) * width + k * cut for block, k in own
+            ]
             pieces.append((piece, starts))
         return pieces, steps
 
-    own_turn, other_turns = [0], list(range(1, inner))
-    early = [(w,) for w in w_cuts] + [(w,) for w in w_pair]
-    early_blocks = [(z, k) for k in range(cuts)] + [(z ^ 1, k) for k in range(cuts)]
-    third = [(w_mid1[k], w_end1[k]) for k in range(cuts)]
-    third_blocks = [(jnp.where(low, 2, 1), k) for k in range(cuts)]
-    fourth = [(w_mid2[k], w_end2[k]) for k in range(cuts)]
-    fourth_block = jnp.where(low, 3, 0)
-    rows_list, turns = [hidden] + others, own_turn + other_turns
-    flag = hold(flag, w_end1[0], w_mid2[0], *square_steps[:1])
-    pieces, steps = summed(flag, [hidden], own_turn, early, early_blocks)
+    owners = [z, z ^ 1, jnp.where(low, 2, 1), jnp.where(low, 3, 0)]
+    weights = {}
+    for k in range(cuts):
+        weights[0, k] = (w_cuts[k],)
+        weights[1, k] = (w_pair[k],)
+        weights[2, k] = (w_mid1[k], w_end1[k])
+        weights[3, k] = (w_mid2[k], w_end2[k])
+    cut_range = range(cuts)
+    early = [(block, k) for block in (0, 1) for k in cut_range]
+    third = [(2, k) for k in cut_range]
+    other_turns = list(range(1, inner))
+    flag = hold(flag, w_end1[0], w_mid2[0])
+    pieces, steps = summed(flag, [(0, early)])
     flag = hold(flag, squares, *steps, *w_end1, *w_mid2)
-    more, steps = summed(flag, [hidden], own_turn, third, third_blocks)
+    more, late_steps = summed(flag, [(0, third)] + [(turn, early + third) for turn in other_turns])
     pieces += more
-    flag = hold(flag, *steps, w_end2[0])
-    partner_steps = []
-    if others:
-        more, partner_steps = summed(flag, others, other_turns, early + third, early_blocks + third_blocks)
-        pieces += more
-    for k in range(cuts):
-        flag = hold(flag, *(partner_steps if k else partner_steps[:1]))
-        last, steps = summed(flag, rows_list, turns, [fourth[k]], [(fourth_block, k)])
-        flag = hold(flag, *steps[:1])
+    flag = hold(flag, late_steps[0])
+    for k in cut_range:
+        last, steps = summed(flag, [(turn, [(3, k)]) for turn in [0] + other_turns])
+        flag = hold(flag, steps[0], *late_steps)
         if k + 1 < cuts:
             pieces += last
     shape = (out_rows, width * n_seq)

time: 152 us -> 129 us (0.85)
  waiting for transfers between devices: 72.5 us -> 55.4 us
  local copies, waits for them, and re-layouts: 15.1 us -> 7.65 us
  starting transfers between devices: 39 us -> 42.9 us
  Pallas kernels: 23.8 us -> 21.5 us
    ppermute x10, waiting for transfers between devices: 41.7 us -> 32.8 us  [along(): return lax.ppermute(value, 'seq', line_pairs(n_seq, hops))]
    ppermute x10 -> x8, waiting for transfers between devices: 15.5 us -> 8.45 us  [summed(): steps.append(lax.ppermute(sent, 'head', flip_pairs(n_head, bit)))]
    unnamed x38 -> x34, local copies, waits for them, and re-layouts: 12.6 us -> 7.55 us
    pallas_call x24 -> x21, Pallas kernels: 22.5 us -> 18.5 us  [local_call(): pl.pallas_call(kernel, in_specs=[pl.BlockSpec(memory_space=pltpu.SMEM)] +...]
    ppermute x10, starting transfers between devices: 18.3 us -> 22.2 us  [along(): return lax.ppermute(value, 'seq', line_pairs(n_seq, hops))]
    slice x1 -> x0, local copies, waits for them, and re-layouts: 2.4 us -> none  [shards(): w_cuts = [out_weight[:, k * cut:(k + 1) * cut] for k in range(cuts)]]
    ppermute x1, starting transfers between devices: 3.64 us -> 5.55 us  [state_prefix(): from_left = lax.ppermute(first, 'seq', line_pairs(n_seq, [(0, 1), (2, 3)]))]
    ppermute x10 -> x8, starting transfers between devices: 7.39 us -> 5.61 us  [summed(): steps.append(lax.ppermute(sent, 'head', flip_pairs(n_head, bit)))]
  transfers between devices with their start and end apart: 31 -> 29, of which waited for: 16 -> 12; matrix products, arithmetic and copies ran while one was open for 0% -> 0% of each run, Pallas kernels for 9% -> 11%
where the time goes in v5:
time: 129 us; the launch traced here: 128 us
  waiting for transfers between devices  55.4 us (43%)
  starting transfers between devices  42.9 us (33%)
  Pallas kernels  21.5 us (17%)
  local copies, waits for them, and re-layouts  7.65 us (6%)
    ppermute x10, waiting for transfers between devices, along(): return lax.ppermute(value, 'seq', line_pairs(n_seq, hops))  32.8 us
    ppermute x10, starting transfers between devices, along(): return lax.ppermute(value, 'seq', line_pairs(n_seq, hops))  22.2 us
    pallas_call x21, Pallas kernels, local_call(): pl.pallas_call(kernel, in_specs=[pl.BlockSpec(memory_space=pltpu.SMEM)] +...  18.5 us
    ppermute x8, waiting for transfers between devices, summed(): steps.append(lax.ppermute(sent, 'head', flip_pairs(n_head, bit)))  8.45 us
    unnamed x34, local copies, waits for them, and re-layouts  7.55 us
    ppermute x2, waiting for transfers between devices, shards(): lax.ppermute(squares[half:], 'head', flip_pairs(n_head, bit))  6.12 us
    ppermute x8, starting transfers between devices, summed(): steps.append(lax.ppermute(sent, 'head', flip_pairs(n_head, bit)))  5.61 us
    ppermute x1, starting transfers between devices, state_prefix(): from_left = lax.ppermute(first, 'seq', line_pairs(n_seq, [(0, 1), (2, 3)]))  5.55 us
  transfers between devices with their start and end apart: 29, of which 12 were waited for; matrix products, arithmetic and copies ran while one was open for 0% of the time, Pallas kernels for 11%

profile of v5, /device:TPU:0, one launch (start us, length us, event | category | flops | bytes accessed | tf_op | source)
XLA Modules:
  0.0 128.1 jit_solution(5477104875767124387)
XLA Ops:
  0.0 1.3 %copy-done.4 = bf16[1024,512]{1,0:T(8,128)(2,1)S(1)} copy-done((bf16[1024,512]{1,0:T(8,128)(2,1)S(1)}, bf16[1024,512]{1,0:T(8,128)(2,1)}, u32[]{:S(2)}) %copy-start.4) | copy-done | bytes 1048600
  1.3 0.8 shard_map.76.refs_1_.refs_2_
  2.2 3.1 %collective-permute-start.2 = (bf16[1024,256]{1,0:T(8,128)(2,1)}, bf16[1024,256]{1,0:T(8,128)(2,1)}, u32[]{:S(2)}, u32[]{:S(2)}) collective-permute-start(bf16[1024,256]{1,0:T(8,128)(2,1)} %shard_map.76.refs_1_.refs_2_), channel_id=1, source_target_pairs={{0,8},{4,12},{8,0},{12,4},{16,24},{20,28},{24,16},{28,20},{1,9},{5... | collective-permute-start | bytes 1572872 | tf_op jit(solution)/shard_map/ppermute | solution.py:394
  5.3 1.5 %collective-permute-start.3 = (bf16[1024,256]{1,0:T(8,128)(2,1)}, bf16[1024,256]{1,0:T(8,128)(2,1)}, u32[]{:S(2)}, u32[]{:S(2)}) collective-permute-start(bf16[1024,256]{1,0:T(8,128)(2,1)} %shard_map.76.refs_1_.refs_2_), channel_id=1, source_target_pairs={{8,16},{12,20},{16,8},{20,12},{9,17},{13,21},{17,9},{21,13},{10,18... | collective-permute-start | bytes 1572872 | tf_op jit(solution)/shard_map/ppermute | solution.py:394
  6.7 1.2 copy-done.1
  7.9 0.5 shard_map.74
  8.4 1.6 %collective-permute-start = (bf16[4,128,128]{2,1,0:T(8,128)(2,1)S(1)}, bf16[4,128,128]{2,1,0:T(8,128)(2,1)S(1)}, u32[]{:S(2)}, u32[]{:S(2)}) collective-permute-start(bf16[4,128,128]{2,1,0:T(8,128)(2,1)S(1)} %shard_map.74), channel_id=1, source_target_pairs={{0,4},{4,0},{8,12},{12,8},{16,20},{20,16},{24,28},{28,24},{1,5},{5... | collective-permute-start | bytes 393224 | tf_op jit(solution)/shard_map/ppermute | solution.py:143
  10.0 0.5 shard_map.73.refs_0_.refs_3_
  10.5 3.0 %collective-permute-done.refs_1_.refs_4_ = bf16[4,128,128]{2,1,0:T(8,128)(2,1)S(1)} collective-permute-done((bf16[4,128,128]{2,1,0:T(8,128)(2,1)S(1)}, bf16[4,128,128]{2,1,0:T(8,128)(2,1)S(1)}, u32[]{:S(2)}, u32[]{:S(2)}) %collective-permute-start) | collective-permute-done | bytes 131104 | tf_op jit(solution)/shard_map/ppermute | solution.py:143
  13.5 5.5 %collective-permute-start.1 = (bf16[4,128,128]{2,1,0:T(8,128)(2,1)S(1)}, bf16[4,128,128]{2,1,0:T(8,128)(2,1)S(1)}, u32[]{:S(2)}, u32[]{:S(2)}) collective-permute-start(bf16[4,128,128]{2,1,0:T(8,128)(2,1)S(1)} %shard_map.75), channel_id=1, source_target_pairs={{0,8},{4,12},{16,24},{20,28},{1,9},{5,13},{17,25},{21,29},{2,10},{... | collective-permute-start | bytes 393224 | tf_op jit(solution)/shard_map/ppermute | solution.py:146
  19.1 2.5 %collective-permute-done.1.refs_2_.refs_0_ = bf16[4,128,128]{2,1,0:T(8,128)(2,1)S(1)} collective-permute-done((bf16[4,128,128]{2,1,0:T(8,128)(2,1)S(1)}, bf16[4,128,128]{2,1,0:T(8,128)(2,1)S(1)}, u32[]{:S(2)}, u32[]{:S(2)}) %collective-permute-start.1) | collective-permute-done | bytes 131104 | tf_op jit(solution)/shard_map/ppermute | solution.py:146
  21.6 0.7 collective-permute-start.4
  22.3 0.7 collective-permute-start.5
  23.0 0.8 shard_map.82.refs_2_.refs_3_
  23.9 0.6 copy-done.12
  24.5 0.6 copy-done.14
  25.1 1.5 %collective-permute-start.10 = (bf16[1024,256]{1,0:T(8,128)(2,1)}, bf16[1024,256]{1,0:T(8,128)(2,1)}, u32[]{:S(2)}, u32[]{:S(2)}) collective-permute-start(bf16[1024,256]{1,0:T(8,128)(2,1)} %collective-permute-done.2.refs_3_.refs_4_), channel_id=1, source_target_pairs={{8,16},{12,20},{16,8},{20,12},{9,17},{13,21},{17,9},{21,13},{10,18... | collective-permute-start | bytes 1572872 | tf_op jit(solution)/shard_map/ppermute | solution.py:394
  26.6 1.3 collective-permute-start.9
  27.9 8.9 %collective-permute-start.11 = (bf16[1024,256]{1,0:T(8,128)(2,1)}, bf16[1024,256]{1,0:T(8,128)(2,1)}, u32[]{:S(2)}, u32[]{:S(2)}) collective-permute-start(bf16[1024,256]{1,0:T(8,128)(2,1)} %shard_map.82.refs_2_.refs_3_), channel_id=1, source_target_pairs={{0,8},{4,12},{8,0},{12,4},{16,24},{20,28},{24,16},{28,20},{1,9},{5... | collective-permute-start | bytes 1572872 | tf_op jit(solution)/shard_map/ppermute | solution.py:394
  36.9 0.9 copy-done.8
  37.8 0.9 copy-done.13
  38.7 0.9 copy-done.15
  39.6 1.3 %shard_map.78 = (f32[4,128,128]{2,1,0:T(8,128)S(1)}, bf16[4,128,128]{2,1,0:T(8,128)(2,1)}) custom-call(s32[4]{0:T(128)S(1)} %add_convert_fusion.masks_ref, bf16[4,128,128]{2,1,0:T(8,128)(2,1)S(1)} %copy-done.8, bf16[4,128,128]{2,1,0:T(8,128)(2,1)S(1)} %copy-done.13, bf16[4,128,128]{2,1,0:T(8,128)(2,1)S(1)} %copy-done.15, ...), custom_call_target="tpu_custom_call" | custom-call | flops 1 | bytes 1 | tf_op jit(solution)/shard_map/pallas_call | solution.py:48
  40.9 0.7 copy-done.10
  41.6 1.5 %collective-permute-start.6 = (bf16[4,128,128]{2,1,0:T(8,128)(2,1)}, bf16[4,128,128]{2,1,0:T(8,128)(2,1)S(1)}, u32[]{:S(2)}, u32[]{:S(2)}) collective-permute-start(bf16[4,128,128]{2,1,0:T(8,128)(2,1)} %get-tuple-element.43), channel_id=1, source_target_pairs={{0,4},{4,0},{8,12},{12,8},{16,20},{20,16},{24,28},{28,24},{1,5},{5... | collective-permute-start | bytes 393224 | tf_op jit(solution)/shard_map/ppermute | solution.py:157
  43.1 1.4 %collective-permute-start.14 = (bf16[1024,256]{1,0:T(8,128)(2,1)}, bf16[1024,256]{1,0:T(8,128)(2,1)}, u32[]{:S(2)}, u32[]{:S(2)}) collective-permute-start(bf16[1024,256]{1,0:T(8,128)(2,1)} %shard_map.82.refs_2_.refs_3_), channel_id=1, source_target_pairs={{8,16},{12,20},{16,8},{20,12},{9,17},{13,21},{17,9},{21,13},{10,18... | collective-permute-start | bytes 1572872 | tf_op jit(solution)/shard_map/ppermute | solution.py:394
  44.6 1.1 shard_map.79.refs_2_
  45.8 1.1 shard_map.80.refs_3_
  47.0 0.1 copy-done.9
  47.2 1.7 %shard_map.81 = (bf16[512,1024]{1,0:T(8,128)(2,1)S(1)}, f32[4,128]{1,0:T(4,128)S(1)}) custom-call(s32[2]{0:T(128)S(1)} %pad_add_fusion.1.place_ref, bf16[512,1024]{1,0:T(8,128)(2,1)S(1)} %copy-done.3, bf16[512,1024]{1,0:T(8,128)(2,1)S(1)} %copy-done.6, f32[32,1,128]{2,1,0:T(1,128)S(1)} %bitcast.24, f32[8,128,128]{2,1,0:T(8,128)S(1)} %copy-done.9, ...), custom_call_target="tpu_custom_call" | custom-call | flops 1 | bytes 1 | tf_op jit(solution)/shard_map/pallas_call | solution.py:48
  48.9 1.2 collective-permute-start.17
  50.2 6.1 %collective-permute-done.11.refs_4_.refs_5_ = bf16[1024,256]{1,0:T(8,128)(2,1)} collective-permute-done((bf16[1024,256]{1,0:T(8,128)(2,1)}, bf16[1024,256]{1,0:T(8,128)(2,1)}, u32[]{:S(2)}, u32[]{:S(2)}) %collective-permute-start.11) | collective-permute-done | bytes 524320 | tf_op jit(solution)/shard_map/ppermute | solution.py:394
  56.2 2.8 %shard_map.83 = (bf16[256,1024]{1,0:T(8,128)(2,1)S(1)}, f32[256,1024]{1,0:T(8,128)S(1)}) custom-call(s32[1]{0:T(128)} %bitcast.9.flag_ref, bf16[512,1024]{1,0:T(8,128)(2,1)S(1)} %get-tuple-element.48.refs_0_, bf16[1024,256]{1,0:T(8,128)(2,1)} %shard_map.76.refs_1_.refs_2_, bf16[1024,256]{1,0:T(8,128)(2,1)} %shard_map.82.refs_2_.refs_3_, ...), custom_call_target="tpu_custom_call" | custom-call | flops 1 | bytes 1 | tf_op jit(solution)/shard_map/pallas_call | solution.py:48
  59.1 1.3 %collective-permute-start.15 = (bf16[1024,256]{1,0:T(8,128)(2,1)}, bf16[1024,256]{1,0:T(8,128)(2,1)S(1)}, u32[]{:S(2)}, u32[]{:S(2)}) collective-permute-start(bf16[1024,256]{1,0:T(8,128)(2,1)} %collective-permute-done.14.refs_8_), channel_id=1, source_target_pairs={{8,0},{12,4},{16,24},{20,28},{9,1},{13,5},{17,25},{21,29},{10,2},{... | collective-permute-start | bytes 1572872 | tf_op jit(solution)/shard_map/ppermute | solution.py:394
  60.4 0.7 collective-permute-start.16
  61.1 0.5 collective-permute-start.7
  61.7 0.1 shard_map.84
  61.8 1.6 %collective-permute-start.13 = (bf16[128,1024]{1,0:T(8,128)(2,1)S(1)}, bf16[128,1024]{1,0:T(8,128)(2,1)S(1)}, u32[]{:S(2)}, u32[]{:S(2)}) collective-permute-start(bf16[128,1024]{1,0:T(8,128)(2,1)S(1)} %get-tuple-element.52), channel_id=1, source_target_pairs={{0,2},{1,3},{2,0},{3,1},{4,6},{5,7},{6,4},{7,5},{8,10},{9,11},{10,... | collective-permute-start | bytes 786440 | tf_op jit(solution)/shard_map/ppermute | solution.py:443
  63.4 0.7 collective-permute-start.8
  64.0 6.1 %collective-permute-done.8 = f32[1,128]{1,0:T(1,128)S(1)} collective-permute-done((f32[1,128]{1,0:T(1,128)S(1)}, f32[1,128]{1,0:T(1,128)S(1)}, u32[]{:S(2)}, u32[]{:S(2)}) %collective-permute-start.8) | collective-permute-done | bytes 544 | tf_op jit(solution)/shard_map/ppermute | solution.py:423
  70.1 5.4 %collective-permute-done.15.refs_9_ = bf16[1024,256]{1,0:T(8,128)(2,1)S(1)} collective-permute-done((bf16[1024,256]{1,0:T(8,128)(2,1)}, bf16[1024,256]{1,0:T(8,128)(2,1)S(1)}, u32[]{:S(2)}, u32[]{:S(2)}) %collective-permute-start.15) | collective-permute-done | bytes 524320 | tf_op jit(solution)/shard_map/ppermute | solution.py:394
  75.5 4.7 %shard_map.85 = (bf16[256,2048]{1,0:T(8,128)(2,1)S(1)}, f32[256,2048]{1,0:T(8,128)S(1)}) custom-call(s32[1]{0:T(128)} %bitcast.9.flag_ref, bf16[512,1024]{1,0:T(8,128)(2,1)S(1)} %get-tuple-element.48.refs_0_, bf16[512,1024]{1,0:T(8,128)(2,1)S(1)} %collective-permute-done.17.refs_1_, bf16[1024,256]{1,0:T(8,128)(2,1)} %shard_map.76.refs_1_.refs_2_, ...), custom_call_target="tpu_custom_call" | custom-call | flops 1 | bytes 1 | tf_op jit(solution)/shard_map/pallas_call | solution.py:48
  80.3 1.3 %collective-permute-start.19 = (bf16[1024,256]{1,0:T(8,128)(2,1)}, bf16[1024,256]{1,0:T(8,128)(2,1)S(1)}, u32[]{:S(2)}, u32[]{:S(2)}) collective-permute-start(bf16[1024,256]{1,0:T(8,128)(2,1)} %collective-permute-done.10.refs_2_), channel_id=1, source_target_pairs={{8,0},{12,4},{16,24},{20,28},{9,1},{13,5},{17,25},{21,29},{10,2},{... | collective-permute-start | bytes 1572872 | tf_op jit(solution)/shard_map/ppermute | solution.py:394
  81.6 1.3 %collective-permute-done.18.got_ref = bf16[256,2048]{1,0:T(8,128)(2,1)S(1)} collective-permute-done((bf16[256,2048]{1,0:T(8,128)(2,1)S(1)}, bf16[256,2048]{1,0:T(8,128)(2,1)S(1)}, u32[]{:S(2)}, u32[]{:S(2)}) %collective-permute-start.18) | collective-permute-done | bytes 1048608 | tf_op jit(solution)/shard_map/ppermute | solution.py:443
  82.9 0.2 shard_map.87
  83.1 1.6 %collective-permute-start.21 = (bf16[128,2048]{1,0:T(8,128)(2,1)S(1)}, bf16[128,2048]{1,0:T(8,128)(2,1)S(1)}, u32[]{:S(2)}, u32[]{:S(2)}) collective-permute-start(bf16[128,2048]{1,0:T(8,128)(2,1)S(1)} %get-tuple-element.60), channel_id=1, source_target_pairs={{0,2},{1,3},{2,0},{3,1},{4,6},{5,7},{6,4},{7,5},{8,10},{9,11},{10,... | collective-permute-start | bytes 1572872 | tf_op jit(solution)/shard_map/ppermute | solution.py:443
  84.7 1.3 collective-permute-start.22
  86.0 13.7 %collective-permute-done.19.refs_3_ = bf16[1024,256]{1,0:T(8,128)(2,1)S(1)} collective-permute-done((bf16[1024,256]{1,0:T(8,128)(2,1)}, bf16[1024,256]{1,0:T(8,128)(2,1)S(1)}, u32[]{:S(2)}, u32[]{:S(2)}) %collective-permute-start.19) | collective-permute-done | bytes 524320 | tf_op jit(solution)/shard_map/ppermute | solution.py:394
  99.6 1.7 %shard_map.86 = (bf16[256,512]{1,0:T(8,128)(2,1)S(1)}, f32[256,512]{1,0:T(8,128)S(1)}) custom-call(s32[1]{0:T(128)} %bitcast.9.flag_ref, bf16[512,1024]{1,0:T(8,128)(2,1)S(1)} %get-tuple-element.48.refs_0_, bf16[512,1024]{1,0:T(8,128)(2,1)S(1)} %collective-permute-done.17.refs_1_, bf16[1024,256]{1,0:T(8,128)(2,1)} %collective-permute-done.10.refs_2_, ...), custom_call_target="tpu_custom_call" | custom-call | flops 1 | bytes 1 | tf_op jit(solution)/shard_map/pallas_call | solution.py:48
  101.5 1.5 %collective-permute-done.20.got_ref = bf16[256,512]{1,0:T(8,128)(2,1)S(1)} collective-permute-done((bf16[256,512]{1,0:T(8,128)(2,1)S(1)}, bf16[256,512]{1,0:T(8,128)(2,1)S(1)}, u32[]{:S(2)}, u32[]{:S(2)}) %collective-permute-start.20) | collective-permute-done | bytes 262176 | tf_op jit(solution)/shard_map/ppermute | solution.py:443
  103.0 7.7 %collective-permute-done.22.refs_3_ = bf16[1024,256]{1,0:T(8,128)(2,1)S(1)} collective-permute-done((bf16[1024,256]{1,0:T(8,128)(2,1)S(1)}, bf16[1024,256]{1,0:T(8,128)(2,1)S(1)}, u32[]{:S(2)}, u32[]{:S(2)}) %collective-permute-start.22) | collective-permute-done | bytes 524320 | tf_op jit(solution)/shard_map/ppermute | solution.py:394
  110.7 0.7 shard_map.88
  111.5 0.1 shard_map.92
  111.6 1.6 %collective-permute-start.26 = (bf16[128,1536]{1,0:T(8,128)(2,1)S(1)}, bf16[128,1536]{1,0:T(8,128)(2,1)S(1)}, u32[]{:S(2)}, u32[]{:S(2)}) collective-permute-start(bf16[128,1536]{1,0:T(8,128)(2,1)S(1)} %get-tuple-element.71), channel_id=1, source_target_pairs={{0,4},{4,0},{8,12},{12,8},{16,20},{20,16},{24,28},{28,24},{1,5},{5... | collective-permute-start | bytes 1179656 | tf_op jit(solution)/shard_map/ppermute | solution.py:452
  113.2 1.6 %collective-permute-start.27 = (bf16[128,512]{1,0:T(8,128)(2,1)S(1)}, bf16[128,512]{1,0:T(8,128)(2,1)S(1)}, u32[]{:S(2)}, u32[]{:S(2)}) collective-permute-start(bf16[128,512]{1,0:T(8,128)(2,1)S(1)} %get-tuple-element.74), channel_id=1, source_target_pairs={{0,2},{1,3},{2,0},{3,1},{4,6},{5,7},{6,4},{7,5},{8,10},{9,11},{10,... | collective-permute-start | bytes 393224 | tf_op jit(solution)/shard_map/ppermute | solution.py:443
  114.8 0.6 collective-permute-start.24
  115.4 0.1 stack.118.starts_ref
  115.5 4.1 %collective-permute-done.27.got_ref = bf16[128,512]{1,0:T(8,128)(2,1)S(1)} collective-permute-done((bf16[128,512]{1,0:T(8,128)(2,1)S(1)}, bf16[128,512]{1,0:T(8,128)(2,1)S(1)}, u32[]{:S(2)}, u32[]{:S(2)}) %collective-permute-start.27) | collective-permute-done | bytes 131104 | tf_op jit(solution)/shard_map/ppermute | solution.py:443
  119.6 0.6 collective-permute-start.28
  120.2 1.5 %collective-permute-done.24.got_ref = bf16[128,512]{1,0:T(8,128)(2,1)S(1)} collective-permute-done((bf16[128,512]{1,0:T(8,128)(2,1)S(1)}, bf16[128,512]{1,0:T(8,128)(2,1)S(1)}, u32[]{:S(2)}, u32[]{:S(2)}) %collective-permute-start.24) | collective-permute-done | bytes 131104 | tf_op jit(solution)/shard_map/ppermute | solution.py:443
  121.7 0.6 collective-permute-start.25
  122.4 2.5 %collective-permute-done.28.refs_4_ = bf16[128,256]{1,0:T(8,128)(2,1)S(1)} collective-permute-done((bf16[128,256]{1,0:T(8,128)(2,1)S(1)}, bf16[128,256]{1,0:T(8,128)(2,1)S(1)}, u32[]{:S(2)}, u32[]{:S(2)}) %collective-permute-start.28) | collective-permute-done | bytes 65568 | tf_op jit(solution)/shard_map/ppermute | solution.py:452
  124.9 1.9 %shard_map.95.refs_2_ = bf16[128,4096]{1,0:T(8,128)(2,1)} custom-call(s32[14]{0:T(128)S(1)} %stack.118.starts_ref, f32[1,128]{1,0:T(1,128)S(1)} %slice_add_fusion.1.squares_ref, bf16[128,1024]{1,0:T(8,128)(2,1)S(1)} %shard_map.91.refs_0_, bf16[128,512]{1,0:T(8,128)(2,1)S(1)} %get-tuple-element.70.refs_1_, ...), custom_call_target="tpu_custom_call" | custom-call | flops 1 | bytes 1 | tf_op jit(solution)/shard_map/pallas_call | solution.py:48
  126.8 1.3 %shard_map.96 = bf16[128,4096]{1,0:T(8,128)(2,1)} custom-call(s32[2]{0:T(128)S(1)} %pad_add_fusion.starts_ref, f32[1,128]{1,0:T(1,128)S(1)} %slice_add_fusion.1.squares_ref, bf16[128,256]{1,0:T(8,128)(2,1)S(1)} %get-tuple-element.66.refs_0_, bf16[128,256]{1,0:T(8,128)(2,1)S(1)} %collective-permute-done.25.refs_1_, ...), custom_call_target="tpu_custom_call", output_to_operand_aliasing={{}: (4, {})} | custom-call | flops 1 | bytes 1 | tf_op jit(solution)/shard_map/pallas_call | solution.py:363
  (60 shorter events, 1.0 us)
Async XLA Ops:
  0.0 6.7 %copy-start = (bf16[512,1024]{1,0:T(8,128)(2,1)S(1)}, bf16[512,1024]{1,0:T(8,128)(2,1)}, u32[]{:S(2)}) copy-start(bf16[512,1024]{1,0:T(8,128)(2,1)} %k_ref.7) | copy-start | bytes 3145732
  0.0 1.3 %copy-start.4 = (bf16[1024,512]{1,0:T(8,128)(2,1)S(1)}, bf16[1024,512]{1,0:T(8,128)(2,1)}, u32[]{:S(2)}) copy-start(bf16[1024,512]{1,0:T(8,128)(2,1)} %w_ref.3) | copy-start | bytes 3145732
  2.2 19.4 %collective-permute-start.2 = (bf16[1024,256]{1,0:T(8,128)(2,1)}, bf16[1024,256]{1,0:T(8,128)(2,1)}, u32[]{:S(2)}, u32[]{:S(2)}) collective-permute-start(bf16[1024,256]{1,0:T(8,128)(2,1)} %shard_map.76.refs_1_.refs_2_), channel_id=1, source_target_pairs={{0,8},{4,12},{8,0},{12,4},{16,24},{20,28},{24,16},{28,20},{1,9},{5... | collective-permute-start | bytes 1572872 | tf_op jit(solution)/shard_map/ppermute | solution.py:394
  5.3 16.3 %collective-permute-start.3 = (bf16[1024,256]{1,0:T(8,128)(2,1)}, bf16[1024,256]{1,0:T(8,128)(2,1)}, u32[]{:S(2)}, u32[]{:S(2)}) collective-permute-start(bf16[1024,256]{1,0:T(8,128)(2,1)} %shard_map.76.refs_1_.refs_2_), channel_id=1, source_target_pairs={{8,16},{12,20},{16,8},{20,12},{9,17},{13,21},{17,9},{21,13},{10,18... | collective-permute-start | bytes 1572872 | tf_op jit(solution)/shard_map/ppermute | solution.py:394
  6.7 1.2 copy-start.1
  7.9 2.1 %copy-start.2 = (bf16[512,1024]{1,0:T(8,128)(2,1)S(1)}, bf16[512,1024]{1,0:T(8,128)(2,1)}, u32[]{:S(2)}) copy-start(bf16[512,1024]{1,0:T(8,128)(2,1)} %v_ref.7) | copy-start | bytes 3145732
  8.4 14.6 %copy-start.5 = (bf16[1024,512]{1,0:T(8,128)(2,1)S(1)}, bf16[1024,512]{1,0:T(8,128)(2,1)}, u32[]{:S(2)}) copy-start(bf16[1024,512]{1,0:T(8,128)(2,1)} %w_ref.3) | copy-start | bytes 3145732
  8.4 5.0 %collective-permute-start = (bf16[4,128,128]{2,1,0:T(8,128)(2,1)S(1)}, bf16[4,128,128]{2,1,0:T(8,128)(2,1)S(1)}, u32[]{:S(2)}, u32[]{:S(2)}) collective-permute-start(bf16[4,128,128]{2,1,0:T(8,128)(2,1)S(1)} %shard_map.74), channel_id=1, source_target_pairs={{0,4},{4,0},{8,12},{12,8},{16,20},{20,16},{24,28},{28,24},{1,5},{5... | collective-permute-start | bytes 393224 | tf_op jit(solution)/shard_map/ppermute | solution.py:143
  10.5 34.2 %copy-start.3 = (bf16[512,1024]{1,0:T(8,128)(2,1)S(1)}, bf16[512,1024]{1,0:T(8,128)(2,1)}, u32[]{:S(2)}) copy-start(bf16[512,1024]{1,0:T(8,128)(2,1)} %q_ref.5) | copy-start | bytes 3145732
  13.5 8.1 %collective-permute-start.1 = (bf16[4,128,128]{2,1,0:T(8,128)(2,1)S(1)}, bf16[4,128,128]{2,1,0:T(8,128)(2,1)S(1)}, u32[]{:S(2)}, u32[]{:S(2)}) collective-permute-start(bf16[4,128,128]{2,1,0:T(8,128)(2,1)S(1)} %shard_map.75), channel_id=1, source_target_pairs={{0,8},{4,12},{16,24},{20,28},{1,9},{5,13},{17,25},{21,29},{2,10},{... | collective-permute-start | bytes 393224 | tf_op jit(solution)/shard_map/ppermute | solution.py:146
  21.6 2.3 %copy-start.7 = (bf16[4,128,128]{2,1,0:T(8,128)(2,1)}, bf16[4,128,128]{2,1,0:T(8,128)(2,1)S(1)}, u32[]{:S(2)}) copy-start(bf16[4,128,128]{2,1,0:T(8,128)(2,1)S(1)} %collective-permute-done.1.refs_2_.refs_0_) | copy-start | bytes 393220
  21.6 2.2 %collective-permute-start.4 = (bf16[4,128,128]{2,1,0:T(8,128)(2,1)S(1)}, bf16[4,128,128]{2,1,0:T(8,128)(2,1)S(1)}, u32[]{:S(2)}, u32[]{:S(2)}) collective-permute-start(bf16[4,128,128]{2,1,0:T(8,128)(2,1)S(1)} %shard_map.77), channel_id=1, source_target_pairs={{8,16},{12,20},{9,17},{13,21},{10,18},{14,22},{11,19},{15,23}} | collective-permute-start | bytes 393224 | tf_op jit(solution)/shard_map/ppermute | solution.py:149
  22.3 2.2 %collective-permute-start.5 = (bf16[4,128,128]{2,1,0:T(8,128)(2,1)S(1)}, bf16[4,128,128]{2,1,0:T(8,128)(2,1)S(1)}, u32[]{:S(2)}, u32[]{:S(2)}) collective-permute-start(bf16[4,128,128]{2,1,0:T(8,128)(2,1)S(1)} %shard_map.77), channel_id=1, source_target_pairs={{8,24},{12,28},{9,25},{13,29},{10,26},{14,30},{11,27},{15,31}} | collective-permute-start | bytes 393224 | tf_op jit(solution)/shard_map/ppermute | solution.py:150
  23.9 0.6 copy-start.12
  24.5 0.6 copy-start.14
  25.1 25.0 %collective-permute-start.10 = (bf16[1024,256]{1,0:T(8,128)(2,1)}, bf16[1024,256]{1,0:T(8,128)(2,1)}, u32[]{:S(2)}, u32[]{:S(2)}) collective-permute-start(bf16[1024,256]{1,0:T(8,128)(2,1)} %collective-permute-done.2.refs_3_.refs_4_), channel_id=1, source_target_pairs={{8,16},{12,20},{16,8},{20,12},{9,17},{13,21},{17,9},{21,13},{10,18... | collective-permute-start | bytes 1572872 | tf_op jit(solution)/shard_map/ppermute | solution.py:394
  26.6 23.5 %collective-permute-start.9 = (bf16[1024,256]{1,0:T(8,128)(2,1)}, bf16[1024,256]{1,0:T(8,128)(2,1)}, u32[]{:S(2)}, u32[]{:S(2)}) collective-permute-start(bf16[1024,256]{1,0:T(8,128)(2,1)} %collective-permute-done.3.refs_6_), channel_id=1, source_target_pairs={{8,0},{12,4},{16,24},{20,28},{9,1},{13,5},{17,25},{21,29},{10,2},{... | collective-permute-start | bytes 1572872 | tf_op jit(solution)/shard_map/ppermute | solution.py:394
  27.9 28.3 %collective-permute-start.11 = (bf16[1024,256]{1,0:T(8,128)(2,1)}, bf16[1024,256]{1,0:T(8,128)(2,1)}, u32[]{:S(2)}, u32[]{:S(2)}) collective-permute-start(bf16[1024,256]{1,0:T(8,128)(2,1)} %shard_map.82.refs_2_.refs_3_), channel_id=1, source_target_pairs={{0,8},{4,12},{8,0},{12,4},{16,24},{20,28},{24,16},{28,20},{1,9},{5... | collective-permute-start | bytes 1572872 | tf_op jit(solution)/shard_map/ppermute | solution.py:394
  36.9 0.9 copy-start.8
  37.8 0.9 copy-start.13
  38.7 0.9 copy-start.15
  40.9 0.7 copy-start.10
  41.6 5.2 %collective-permute-start.6 = (bf16[4,128,128]{2,1,0:T(8,128)(2,1)}, bf16[4,128,128]{2,1,0:T(8,128)(2,1)S(1)}, u32[]{:S(2)}, u32[]{:S(2)}) collective-permute-start(bf16[4,128,128]{2,1,0:T(8,128)(2,1)} %get-tuple-element.43), channel_id=1, source_target_pairs={{0,4},{4,0},{8,12},{12,8},{16,20},{20,16},{24,28},{28,24},{1,5},{5... | collective-permute-start | bytes 393224 | tf_op jit(solution)/shard_map/ppermute | solution.py:157
  43.1 16.0 %collective-permute-start.14 = (bf16[1024,256]{1,0:T(8,128)(2,1)}, bf16[1024,256]{1,0:T(8,128)(2,1)}, u32[]{:S(2)}, u32[]{:S(2)}) collective-permute-start(bf16[1024,256]{1,0:T(8,128)(2,1)} %shard_map.82.refs_2_.refs_3_), channel_id=1, source_target_pairs={{8,16},{12,20},{16,8},{20,12},{9,17},{13,21},{17,9},{21,13},{10,18... | collective-permute-start | bytes 1572872 | tf_op jit(solution)/shard_map/ppermute | solution.py:394
  45.7 1.2 copy-start.6
  45.7 1.3 %copy-start.9 = (f32[8,128,128]{2,1,0:T(8,128)S(1)}, f32[8,128,128]{2,1,0:T(8,128)}, u32[]{:S(2)}) copy-start(f32[8,128,128]{2,1,0:T(8,128)} %kv_ref.1) | copy-start | bytes 1572868
  45.8 1.4 %copy-start.11 = (f32[4,128,128]{2,1,0:T(8,128)S(1)}, f32[4,128,128]{2,1,0:T(8,128)}, u32[]{:S(2)}) copy-start(f32[4,128,128]{2,1,0:T(8,128)} %copy-done.10) | copy-start | bytes 786436
  45.8 1.4 %copy-start.16 = (f32[4096]{0:T(1024)S(1)}, f32[4096]{0:T(1024)}, u32[]{:S(2)}) copy-start(f32[4096]{0:T(1024)} %param.12) | copy-start | bytes 49156
  48.9 26.6 %collective-permute-start.17 = (bf16[512,1024]{1,0:T(8,128)(2,1)S(1)}, bf16[512,1024]{1,0:T(8,128)(2,1)S(1)}, u32[]{:S(2)}, u32[]{:S(2)}) collective-permute-start(bf16[512,1024]{1,0:T(8,128)(2,1)S(1)} %get-tuple-element.48.refs_0_), channel_id=1, source_target_pairs={{0,4},{4,0},{8,12},{12,8},{16,20},{20,16},{24,28},{28,24},{1,5},{5... | collective-permute-start | bytes 3145736 | tf_op jit(solution)/shard_map/ppermute | solution.py:418
  59.0 2.6 %collective-permute-start.12 = (bf16[256,1024]{1,0:T(8,128)(2,1)S(1)}, bf16[256,1024]{1,0:T(8,128)(2,1)S(1)}, u32[]{:S(2)}, u32[]{:S(2)}) collective-permute-start(bf16[256,1024]{1,0:T(8,128)(2,1)S(1)} %get-tuple-element.50), channel_id=1, source_target_pairs={{0,1},{1,0},{2,3},{3,2},{4,5},{5,4},{6,7},{7,6},{8,9},{9,8},{10,11... | collective-permute-start | bytes 1572872 | tf_op jit(solution)/shard_map/ppermute | solution.py:443
  59.1 16.4 %collective-permute-start.15 = (bf16[1024,256]{1,0:T(8,128)(2,1)}, bf16[1024,256]{1,0:T(8,128)(2,1)S(1)}, u32[]{:S(2)}, u32[]{:S(2)}) collective-permute-start(bf16[1024,256]{1,0:T(8,128)(2,1)} %collective-permute-done.14.refs_8_), channel_id=1, source_target_pairs={{8,0},{12,4},{16,24},{20,28},{9,1},{13,5},{17,25},{21,29},{10,2},{... | collective-permute-start | bytes 1572872 | tf_op jit(solution)/shard_map/ppermute | solution.py:394
  60.4 15.1 %collective-permute-start.16 = (bf16[1024,256]{1,0:T(8,128)(2,1)}, bf16[1024,256]{1,0:T(8,128)(2,1)S(1)}, u32[]{:S(2)}, u32[]{:S(2)}) collective-permute-start(bf16[1024,256]{1,0:T(8,128)(2,1)} %collective-permute-done.11.refs_4_.refs_5_), channel_id=1, source_target_pairs={{8,16},{12,20},{16,8},{20,12},{9,17},{13,21},{17,9},{21,13},{10,18... | collective-permute-start | bytes 1572872 | tf_op jit(solution)/shard_map/ppermute | solution.py:394
  61.1 2.2 %collective-permute-start.7 = (f32[2,128]{1,0:T(2,128)S(1)}, f32[2,128]{1,0:T(2,128)S(1)}, u32[]{:S(2)}, u32[]{:S(2)}) collective-permute-start(f32[2,128]{1,0:T(2,128)S(1)} %slice.13), channel_id=1, source_target_pairs={{0,1},{1,0},{2,3},{3,2},{4,5},{5,4},{6,7},{7,6},{8,9},{9,8},{10,11... | collective-permute-start | bytes 3080 | tf_op jit(solution)/shard_map/ppermute | solution.py:423
  61.8 13.8 %collective-permute-start.13 = (bf16[128,1024]{1,0:T(8,128)(2,1)S(1)}, bf16[128,1024]{1,0:T(8,128)(2,1)S(1)}, u32[]{:S(2)}, u32[]{:S(2)}) collective-permute-start(bf16[128,1024]{1,0:T(8,128)(2,1)S(1)} %get-tuple-element.52), channel_id=1, source_target_pairs={{0,2},{1,3},{2,0},{3,1},{4,6},{5,7},{6,4},{7,5},{8,10},{9,11},{10,... | collective-permute-start | bytes 786440 | tf_op jit(solution)/shard_map/ppermute | solution.py:443
  63.4 6.8 %collective-permute-start.8 = (f32[1,128]{1,0:T(1,128)S(1)}, f32[1,128]{1,0:T(1,128)S(1)}, u32[]{:S(2)}, u32[]{:S(2)}) collective-permute-start(f32[1,128]{1,0:T(1,128)S(1)} %slice.15), channel_id=1, source_target_pairs={{0,2},{1,3},{2,0},{3,1},{4,6},{5,7},{6,4},{7,5},{8,10},{9,11},{10,... | collective-permute-start | bytes 1544 | tf_op jit(solution)/shard_map/ppermute | solution.py:423
  80.2 2.7 %collective-permute-start.18 = (bf16[256,2048]{1,0:T(8,128)(2,1)S(1)}, bf16[256,2048]{1,0:T(8,128)(2,1)S(1)}, u32[]{:S(2)}, u32[]{:S(2)}) collective-permute-start(bf16[256,2048]{1,0:T(8,128)(2,1)S(1)} %get-tuple-element.56), channel_id=1, source_target_pairs={{0,1},{1,0},{2,3},{3,2},{4,5},{5,4},{6,7},{7,6},{8,9},{9,8},{10,11... | collective-permute-start | bytes 3145736 | tf_op jit(solution)/shard_map/ppermute | solution.py:443
  80.3 19.4 %collective-permute-start.19 = (bf16[1024,256]{1,0:T(8,128)(2,1)}, bf16[1024,256]{1,0:T(8,128)(2,1)S(1)}, u32[]{:S(2)}, u32[]{:S(2)}) collective-permute-start(bf16[1024,256]{1,0:T(8,128)(2,1)} %collective-permute-done.10.refs_2_), channel_id=1, source_target_pairs={{8,0},{12,4},{16,24},{20,28},{9,1},{13,5},{17,25},{21,29},{10,2},{... | collective-permute-start | bytes 1572872 | tf_op jit(solution)/shard_map/ppermute | solution.py:394
  83.1 19.9 %collective-permute-start.21 = (bf16[128,2048]{1,0:T(8,128)(2,1)S(1)}, bf16[128,2048]{1,0:T(8,128)(2,1)S(1)}, u32[]{:S(2)}, u32[]{:S(2)}) collective-permute-start(bf16[128,2048]{1,0:T(8,128)(2,1)S(1)} %get-tuple-element.60), channel_id=1, source_target_pairs={{0,2},{1,3},{2,0},{3,1},{4,6},{5,7},{6,4},{7,5},{8,10},{9,11},{10,... | collective-permute-start | bytes 1572872 | tf_op jit(solution)/shard_map/ppermute | solution.py:443
  84.7 26.0 %collective-permute-start.22 = (bf16[1024,256]{1,0:T(8,128)(2,1)S(1)}, bf16[1024,256]{1,0:T(8,128)(2,1)S(1)}, u32[]{:S(2)}, u32[]{:S(2)}) collective-permute-start(bf16[1024,256]{1,0:T(8,128)(2,1)S(1)} %collective-permute-done.16.refs_2_), channel_id=1, source_target_pairs={{8,0},{12,4},{16,24},{20,28},{9,1},{13,5},{17,25},{21,29},{10,2},{... | collective-permute-start | bytes 1572872 | tf_op jit(solution)/shard_map/ppermute | solution.py:394
  101.4 1.6 %collective-permute-start.20 = (bf16[256,512]{1,0:T(8,128)(2,1)S(1)}, bf16[256,512]{1,0:T(8,128)(2,1)S(1)}, u32[]{:S(2)}, u32[]{:S(2)}) collective-permute-start(bf16[256,512]{1,0:T(8,128)(2,1)S(1)} %get-tuple-element.58), channel_id=1, source_target_pairs={{0,1},{1,0},{2,3},{3,2},{4,5},{5,4},{6,7},{7,6},{8,9},{9,8},{10,11... | collective-permute-start | bytes 786440 | tf_op jit(solution)/shard_map/ppermute | solution.py:443
  111.4 3.4 %collective-permute-start.23 = (bf16[256,512]{1,0:T(8,128)(2,1)S(1)}, bf16[256,512]{1,0:T(8,128)(2,1)S(1)}, u32[]{:S(2)}, u32[]{:S(2)}) collective-permute-start(bf16[256,512]{1,0:T(8,128)(2,1)S(1)} %get-tuple-element.63), channel_id=1, source_target_pairs={{0,1},{1,0},{2,3},{3,2},{4,5},{5,4},{6,7},{7,6},{8,9},{9,8},{10,11... | collective-permute-start | bytes 786440 | tf_op jit(solution)/shard_map/ppermute | solution.py:443
  111.6 13.4 %collective-permute-start.26 = (bf16[128,1536]{1,0:T(8,128)(2,1)S(1)}, bf16[128,1536]{1,0:T(8,128)(2,1)S(1)}, u32[]{:S(2)}, u32[]{:S(2)}) collective-permute-start(bf16[128,1536]{1,0:T(8,128)(2,1)S(1)} %get-tuple-element.71), channel_id=1, source_target_pairs={{0,4},{4,0},{8,12},{12,8},{16,20},{20,16},{24,28},{28,24},{1,5},{5... | collective-permute-start | bytes 1179656 | tf_op jit(solution)/shard_map/ppermute | solution.py:452
  113.2 6.4 %collective-permute-start.27 = (bf16[128,512]{1,0:T(8,128)(2,1)S(1)}, bf16[128,512]{1,0:T(8,128)(2,1)S(1)}, u32[]{:S(2)}, u32[]{:S(2)}) collective-permute-start(bf16[128,512]{1,0:T(8,128)(2,1)S(1)} %get-tuple-element.74), channel_id=1, source_target_pairs={{0,2},{1,3},{2,0},{3,1},{4,6},{5,7},{6,4},{7,5},{8,10},{9,11},{10,... | collective-permute-start | bytes 393224 | tf_op jit(solution)/shard_map/ppermute | solution.py:443
  114.8 6.8 %collective-permute-start.24 = (bf16[128,512]{1,0:T(8,128)(2,1)S(1)}, bf16[128,512]{1,0:T(8,128)(2,1)S(1)}, u32[]{:S(2)}, u32[]{:S(2)}) collective-permute-start(bf16[128,512]{1,0:T(8,128)(2,1)S(1)} %get-tuple-element.65), channel_id=1, source_target_pairs={{0,2},{1,3},{2,0},{3,1},{4,6},{5,7},{6,4},{7,5},{8,10},{9,11},{10,... | collective-permute-start | bytes 393224 | tf_op jit(solution)/shard_map/ppermute | solution.py:443
  119.6 5.3 %collective-permute-start.28 = (bf16[128,256]{1,0:T(8,128)(2,1)S(1)}, bf16[128,256]{1,0:T(8,128)(2,1)S(1)}, u32[]{:S(2)}, u32[]{:S(2)}) collective-permute-start(bf16[128,256]{1,0:T(8,128)(2,1)S(1)} %get-tuple-element.76), channel_id=1, source_target_pairs={{0,4},{4,0},{8,12},{12,8},{16,20},{20,16},{24,28},{28,24},{1,5},{5... | collective-permute-start | bytes 196616 | tf_op jit(solution)/shard_map/ppermute | solution.py:452
  121.7 5.1 %collective-permute-start.25 = (bf16[128,256]{1,0:T(8,128)(2,1)S(1)}, bf16[128,256]{1,0:T(8,128)(2,1)S(1)}, u32[]{:S(2)}, u32[]{:S(2)}) collective-permute-start(bf16[128,256]{1,0:T(8,128)(2,1)S(1)} %get-tuple-element.67), channel_id=1, source_target_pairs={{0,4},{4,0},{8,12},{12,8},{16,20},{20,16},{24,28},{28,24},{1,5},{5... | collective-permute-start | bytes 196616 | tf_op jit(solution)/shard_map/ppermute | solution.py:452

commit v6 on v5

--- a/solution.py
+++ b/solution.py
@@ -102,25 +102,44 @@
     )(weight)
 
 
-def states_kernel(part_ref, k_ref, v_ref, out_ref):
+def states_kernel(part_ref, k_ref, v_ref, out_ref, k_buf, v_buf, sems):
     heads = out_ref.shape[0]
+    copies = []
     for index in range(heads):
-        columns = pl.ds(pl.multiple_of((part_ref[0] * heads + index) * DH, DH), DH)
+        source = pl.ds(pl.multiple_of((part_ref[0] * heads + index) * DH, DH), DH)
+        target = pl.ds(index * DH, DH)
+        for which, (ref, buf) in enumerate(((k_ref, k_buf), (v_ref, v_buf))):
+            copies.append(
+                pltpu.make_async_copy(ref.at[:, source], buf.at[:, target], sems.at[which, index])
+            )
+            copies[-1].start()
+    for index in range(heads):
+        columns = pl.ds(index * DH, DH)
+        copies[2 * index].wait()
+        copies[2 * index + 1].wait()
         out_ref[index] = lax.dot_general(
-            k_ref[:, columns],
-            v_ref[:, columns],
+            k_buf[:, columns],
+            v_buf[:, columns],
             (((0,), (0,)), ((), ())),
             preferred_element_type=jnp.float32,
         ).astype(out_ref.dtype)
 
 
 def block_states(key_input, value_input, part, heads, dtype):
-    return local_call(
+    rows = key_input.shape[0]
+    return pl.pallas_call(
         states_kernel,
-        scalars(part),
-        [key_input, value_input],
-        [jax.ShapeDtypeStruct((heads, DH, DH), dtype)],
-    )[0]
+        in_specs=[pl.BlockSpec(memory_space=pltpu.SMEM)] + [pl.BlockSpec(memory_space=pl.ANY)] * 2,
+        out_specs=pl.BlockSpec(memory_space=pltpu.VMEM),
+        out_shape=jax.ShapeDtypeStruct((heads, DH, DH), dtype),
+        scratch_shapes=[
+            pltpu.VMEM((rows, heads * DH), key_input.dtype),
+            pltpu.VMEM((rows, heads * DH), value_input.dtype),
+            pltpu.SemaphoreType.DMA((2, heads)),
+        ],
+        compiler_params=pltpu.CompilerParams(vmem_limit_bytes=VMEM_BYTES),
+        cost_estimate=pl.CostEstimate(flops=1, bytes_accessed=1, transcendentals=0),
+    )(scalars(part), key_input, value_input)
 
 
 def state_prefix(key_input, value_input, n_seq, place, early):
@@ -155,7 +174,7 @@
     terms = [befores[0]]
     for turn in range(1, len(targets)):
         terms.append(lax.ppermute(befores[turn], "seq", turn_pairs(n_seq, turn)))
-    return terms, [near, far]
+    return terms, befores[0]
 
 
 def causal_kernel(first_head, place_ref, q_ref, k_ref, v_ref, out_ref):
@@ -396,7 +415,7 @@
     w_cuts = [cut_columns(out_weight, k * cut, cut) for k in range(cuts)]
     w_pair = [along(w_cuts[0], SWAP_OUTER)]
     w_mid1 = [along(w_cuts[0], SWAP_MIDDLE)]
-    terms, steps = state_prefix(key_input, value_input, n_seq, place, [w_pair[0], w_mid1[0]])
+    terms, stepped = state_prefix(key_input, value_input, n_seq, place, [w_pair[0], w_mid1[0]])
     some = heads // 2
     inners = [
         causal_part(queries, key_input, value_input, 0, some),
@@ -404,14 +423,15 @@
     ]
 
     for k in range(1, cuts):
-        w_pair.append(along(hold(w_cuts[k], *steps), SWAP_OUTER))
-        w_mid1.append(along(hold(w_cuts[k], *steps), SWAP_MIDDLE))
-    w_mid2 = [along(hold(w_pair[k], *steps), SWAP_MIDDLE) for k in range(cuts)]
-    w_end1 = [along(hold(w_mid1[k], *steps), TO_ENDS) for k in range(cuts)]
+        w_pair.append(along(hold(w_cuts[k], stepped), SWAP_OUTER))
+        w_mid1.append(along(hold(w_cuts[k], stepped), SWAP_MIDDLE))
+    w_mid2 = [along(hold(w_pair[k], stepped), SWAP_MIDDLE) for k in range(cuts)]
+    w_end1 = [along(hold(w_mid1[k], stepped), TO_ENDS) for k in range(cuts)]
     w_end2 = [along(w_mid2[k], TO_ENDS) for k in range(cuts)]
 
     bits = n_head.bit_length() - 1
     order = [int(format(j, "b").zfill(bits)[::-1], 2) for j in range(n_head)] if bits else [0]
+    terms[0] = hold(terms[0], *w_pair[1:], *w_mid1[1:])
     hidden, squares = gated_hidden(
         queries, inners, kv_state, terms, gate_input, norm_gain, h, i, order
     )
@@ -437,6 +457,7 @@
         sent, kept = project(
             jobs, [rows_list[turn] for turn in turns], [weights[block] for block in blocks], flag
         )
+        sent_first = sent
         widths = [cut * len(own) for _, own in parts]
         bit, steps = 1, []
         while bit < n_head:
@@ -454,7 +475,7 @@
                 (owners[block] * inner + (i + turn) % inner) * width + k * cut for block, k in own
             ]
             pieces.append((piece, starts))
-        return pieces, steps
+        return pieces, sent_first, steps
 
     owners = [z, z ^ 1, jnp.where(low, 2, 1), jnp.where(low, 3, 0)]
     weights = {}
@@ -463,24 +484,41 @@
         weights[1, k] = (w_pair[k],)
         weights[2, k] = (w_mid1[k], w_end1[k])
         weights[3, k] = (w_mid2[k], w_end2[k])
-    cut_range = range(cuts)
-    early = [(block, k) for block in (0, 1) for k in cut_range]
-    third = [(2, k) for k in cut_range]
-    other_turns = list(range(1, inner))
-    flag = hold(flag, w_end1[0], w_mid2[0])
-    pieces, steps = summed(flag, [(0, early)])
-    flag = hold(flag, squares, *steps, *w_end1, *w_mid2)
-    more, late_steps = summed(flag, [(0, third)] + [(turn, early + third) for turn in other_turns])
-    pieces += more
-    flag = hold(flag, late_steps[0])
-    for k in cut_range:
-        last, steps = summed(flag, [(turn, [(3, k)]) for turn in [0] + other_turns])
-        flag = hold(flag, steps[0], *late_steps)
+    turns = list(range(inner))
+    pieces = []
+
+    def group(members, block, pins):
+        more, sent, steps = summed(
+            hold(flag, *pins), [(turn, [(block, k) for k in range(cuts)]) for turn in members]
+        )
+        pieces.extend(more)
+        return sent, steps
+
+    shape = (out_rows, width * n_seq)
+    in_kernel = cut % DH == 0 and out_rows == DH
+
+    pins = [w_end1[0], w_mid2[0]]
+    sent, steps_own = group(turns[:1], 0, pins)
+    sent, steps_pair = group(turns[:1], 1, [sent])
+    steps_other = []
+    for block in (0, 1) if inner > 1 else ():
+        sent, steps = group(turns[1:], block, [sent, squares])
+        steps_other += steps
+    sent, steps_third = group(turns[:1], 2, [sent, *w_end1, *w_mid2, *steps_own, *steps_pair])
+    if inner > 1:
+        sent, steps = group(turns[1:], 2, [sent])
+        steps_third += steps
+    pins = [sent, *steps_other]
+    filled = None
+    for k in range(cuts):
+        if k + 1 == cuts and in_kernel:
+            filled = placed(None, pieces, squares, cut, shape, total_width)
+            pins = [filled]
+        last, sent, steps = summed(hold(flag, *pins), [(turn, [(3, k)]) for turn in turns])
         if k + 1 < cuts:
             pieces += last
-    shape = (out_rows, width * n_seq)
-    if cut % DH == 0 and out_rows == DH:
-        filled = placed(None, pieces, squares, cut, shape, total_width)
+            pins = [sent]
+    if in_kernel:
         return placed(filled, last, squares, cut, shape, total_width)
     scale = lax.rsqrt(squares.reshape(out_rows, 1) / total_width + epsilon)
     output = jnp.zeros(shape, jnp.bfloat16)

time: 129 us -> 140 us (1.085)
  waiting for transfers between devices: 55.4 us -> 42.9 us
  local copies, waits for them, and re-layouts: 7.65 us -> 18 us
  Pallas kernels: 21.5 us -> 29.8 us
  starting transfers between devices: 42.9 us -> 47.4 us
    ppermute x10, waiting for transfers between devices: 32.8 us -> 19.6 us  [along(): return lax.ppermute(value, 'seq', line_pairs(n_seq, hops))]
    unnamed x34 -> x68, local copies, waits for them, and re-layouts: 7.55 us -> 17.9 us
    pallas_call x21 -> x31, Pallas kernels: 18.5 us -> 25 us  [local_call(): pl.pallas_call(kernel, in_specs=[pl.BlockSpec(memory_space=pltpu.SMEM)] +...]
    ppermute x8 -> x16, waiting for transfers between devices: 8.45 us -> 14.1 us  [summed(): steps.append(lax.ppermute(sent, 'head', flip_pairs(n_head, bit)))]
    ppermute x2, waiting for transfers between devices: 6.12 us -> 0.71 us  [shards(): lax.ppermute(squares[half:], 'head', flip_pairs(n_head, bit))]
    ppermute x8 -> x16, starting transfers between devices: 5.61 us -> 11 us  [summed(): steps.append(lax.ppermute(sent, 'head', flip_pairs(n_head, bit)))]
    ppermute x10, starting transfers between devices: 22.2 us -> 17.5 us  [along(): return lax.ppermute(value, 'seq', line_pairs(n_seq, hops))]
    pallas_call x0 -> x2, Pallas kernels: none -> 2.57 us  [block_states(): pl.pallas_call(states_kernel, in_specs=[pl.BlockSpec(memory_space=pltpu.S...]
  transfers between devices with their start and end apart: 29 -> 39, of which waited for: 12 -> 15; matrix products, arithmetic and copies ran while one was open for 0% -> 0% of each run, Pallas kernels for 11% -> 17%
where the time goes in v6:
time: 140 us; the launch traced here: 139 us
  starting transfers between devices  47.4 us (34%)
  waiting for transfers between devices  42.9 us (31%)
  Pallas kernels  29.8 us (21%)
  local copies, waits for them, and re-layouts  18 us (13%)
    pallas_call x31, Pallas kernels, local_call(): pl.pallas_call(kernel, in_specs=[pl.BlockSpec(memory_space=pltpu.SMEM)] +...  25 us
    ppermute x10, waiting for transfers between devices, along(): return lax.ppermute(value, 'seq', line_pairs(n_seq, hops))  19.6 us
    unnamed x68, local copies, waits for them, and re-layouts  17.9 us
    ppermute x10, starting transfers between devices, along(): return lax.ppermute(value, 'seq', line_pairs(n_seq, hops))  17.5 us
    ppermute x16, waiting for transfers between devices, summed(): steps.append(lax.ppermute(sent, 'head', flip_pairs(n_head, bit)))  14.1 us
    ppermute x16, starting transfers between devices, summed(): steps.append(lax.ppermute(sent, 'head', flip_pairs(n_head, bit)))  11 us
    ppermute x1, starting transfers between devices, state_prefix(): from_left = lax.ppermute(first, 'seq', line_pairs(n_seq, [(0, 1), (2, 3)]))  5.54 us
    ppermute x5, starting transfers between devices, summed(): piece = lax.ppermute(piece, 'seq', turn_pairs(n_seq, -turn))  4.51 us
  transfers between devices with their start and end apart: 39, of which 15 were waited for; matrix products, arithmetic and copies ran while one was open for 0% of the time, Pallas kernels for 17%

profile of v6, /device:TPU:0, one launch (start us, length us, event | category | flops | bytes accessed | tf_op | source)
XLA Modules:
  0.0 139.1 jit_solution(17397790221421620647)
XLA Ops:
  0.0 1.3 copy-done.7
  1.4 3.1 %collective-permute-start.2 = (bf16[1024,256]{1,0:T(8,128)(2,1)S(1)}, bf16[1024,256]{1,0:T(8,128)(2,1)}, u32[]{:S(2)}, u32[]{:S(2)}) collective-permute-start(bf16[1024,256]{1,0:T(8,128)(2,1)S(1)} %shard_map.76.refs_1_), channel_id=1, source_target_pairs={{0,8},{4,12},{8,0},{12,4},{16,24},{20,28},{24,16},{28,20},{1,9},{5... | collective-permute-start | bytes 1572872 | tf_op jit(solution)/shard_map/ppermute | solution.py:413
  4.5 1.5 %collective-permute-start.3 = (bf16[1024,256]{1,0:T(8,128)(2,1)S(1)}, bf16[1024,256]{1,0:T(8,128)(2,1)}, u32[]{:S(2)}, u32[]{:S(2)}) collective-permute-start(bf16[1024,256]{1,0:T(8,128)(2,1)S(1)} %shard_map.76.refs_1_), channel_id=1, source_target_pairs={{8,16},{12,20},{16,8},{20,12},{9,17},{13,21},{17,9},{21,13},{10,18... | collective-permute-start | bytes 1572872 | tf_op jit(solution)/shard_map/ppermute | solution.py:413
  5.9 1.2 copy-done.1
  7.2 1.3 shard_map.74
  8.5 1.6 %collective-permute-start = (bf16[4,128,128]{2,1,0:T(8,128)(2,1)S(1)}, bf16[4,128,128]{2,1,0:T(8,128)(2,1)S(1)}, u32[]{:S(2)}, u32[]{:S(2)}) collective-permute-start(bf16[4,128,128]{2,1,0:T(8,128)(2,1)S(1)} %shard_map.74), channel_id=1, source_target_pairs={{0,4},{4,0},{8,12},{12,8},{16,20},{20,16},{24,28},{28,24},{1,5},{5... | collective-permute-start | bytes 393224 | tf_op jit(solution)/shard_map/ppermute | solution.py:162
  10.0 1.3 shard_map.73.refs_0_.refs_3_
  11.3 2.2 %collective-permute-done.refs_1_.refs_4_ = bf16[4,128,128]{2,1,0:T(8,128)(2,1)S(1)} collective-permute-done((bf16[4,128,128]{2,1,0:T(8,128)(2,1)S(1)}, bf16[4,128,128]{2,1,0:T(8,128)(2,1)S(1)}, u32[]{:S(2)}, u32[]{:S(2)}) %collective-permute-start) | collective-permute-done | bytes 131104 | tf_op jit(solution)/shard_map/ppermute | solution.py:162
  13.5 5.5 %collective-permute-start.1 = (bf16[4,128,128]{2,1,0:T(8,128)(2,1)S(1)}, bf16[4,128,128]{2,1,0:T(8,128)(2,1)S(1)}, u32[]{:S(2)}, u32[]{:S(2)}) collective-permute-start(bf16[4,128,128]{2,1,0:T(8,128)(2,1)S(1)} %shard_map.75), channel_id=1, source_target_pairs={{0,8},{4,12},{16,24},{20,28},{1,9},{5,13},{17,25},{21,29},{2,10},{... | collective-permute-start | bytes 393224 | tf_op jit(solution)/shard_map/ppermute | solution.py:165
  19.1 2.5 %collective-permute-done.1.refs_2_.refs_0_ = bf16[4,128,128]{2,1,0:T(8,128)(2,1)S(1)} collective-permute-done((bf16[4,128,128]{2,1,0:T(8,128)(2,1)S(1)}, bf16[4,128,128]{2,1,0:T(8,128)(2,1)S(1)}, u32[]{:S(2)}, u32[]{:S(2)}) %collective-permute-start.1) | collective-permute-done | bytes 131104 | tf_op jit(solution)/shard_map/ppermute | solution.py:165
  22.3 1.4 %collective-permute-start.4 = (bf16[4,128,128]{2,1,0:T(8,128)(2,1)}, bf16[4,128,128]{2,1,0:T(8,128)(2,1)}, u32[]{:S(2)}, u32[]{:S(2)}) collective-permute-start(bf16[4,128,128]{2,1,0:T(8,128)(2,1)} %shard_map.77), channel_id=1, source_target_pairs={{8,16},{12,20},{9,17},{13,21},{10,18},{14,22},{11,19},{15,23}} | collective-permute-start | bytes 393224 | tf_op jit(solution)/shard_map/ppermute | solution.py:168
  23.7 1.3 collective-permute-start.5
  25.0 0.8 shard_map.79.refs_2_
  26.0 0.9 copy-done.17
  26.9 1.7 %shard_map.78 = (f32[4,128,128]{2,1,0:T(8,128)S(1)}, bf16[4,128,128]{2,1,0:T(8,128)(2,1)}) custom-call(s32[4]{0:T(128)S(1)} %add_convert_fusion.masks_ref, bf16[4,128,128]{2,1,0:T(8,128)(2,1)S(1)} %copy-done.17, bf16[4,128,128]{2,1,0:T(8,128)(2,1)} %collective-permute-done.4.refs_1_, bf16[4,128,128]{2,1,0:T(8,128)(2,1)} %collective-permute-done.5.refs_2_, ...), custom_call_target="tpu_custom_call" | custom-call | flops 1 | bytes 1 | tf_op jit(solution)/shard_map/pallas_call | solution.py:48
  28.6 0.7 copy-done.23
  29.4 5.0 %collective-permute-start.6 = (bf16[1024,256]{1,0:T(8,128)(2,1)}, bf16[1024,256]{1,0:T(8,128)(2,1)}, u32[]{:S(2)}, u32[]{:S(2)}) collective-permute-start(bf16[1024,256]{1,0:T(8,128)(2,1)} %shard_map.79.refs_2_), channel_id=1, source_target_pairs={{0,8},{4,12},{8,0},{12,4},{16,24},{20,28},{24,16},{28,20},{1,9},{5... | collective-permute-start | bytes 1572872 | tf_op jit(solution)/shard_map/ppermute | solution.py:413
  34.3 1.5 %collective-permute-start.7 = (bf16[1024,256]{1,0:T(8,128)(2,1)}, bf16[1024,256]{1,0:T(8,128)(2,1)}, u32[]{:S(2)}, u32[]{:S(2)}) collective-permute-start(bf16[1024,256]{1,0:T(8,128)(2,1)} %shard_map.79.refs_2_), channel_id=1, source_target_pairs={{8,16},{12,20},{16,8},{20,12},{9,17},{13,21},{17,9},{21,13},{10,18... | collective-permute-start | bytes 1572872 | tf_op jit(solution)/shard_map/ppermute | solution.py:413
  35.8 1.5 %collective-permute-start.8 = (bf16[4,128,128]{2,1,0:T(8,128)(2,1)}, bf16[4,128,128]{2,1,0:T(8,128)(2,1)S(1)}, u32[]{:S(2)}, u32[]{:S(2)}) collective-permute-start(bf16[4,128,128]{2,1,0:T(8,128)(2,1)} %get-tuple-element.64), channel_id=1, source_target_pairs={{0,4},{4,0},{8,12},{12,8},{16,20},{20,16},{24,28},{28,24},{1,5},{5... | collective-permute-start | bytes 393224 | tf_op jit(solution)/shard_map/ppermute | solution.py:176
  37.3 1.1 shard_map.80.refs_2_
  38.4 1.0 copy-done.9
  39.3 1.1 shard_map.81.refs_3_
  40.4 0.9 copy-done.11
  41.5 3.2 %collective-permute-done.6.refs_2_ = bf16[1024,256]{1,0:T(8,128)(2,1)} collective-permute-done((bf16[1024,256]{1,0:T(8,128)(2,1)}, bf16[1024,256]{1,0:T(8,128)(2,1)}, u32[]{:S(2)}, u32[]{:S(2)}) %collective-permute-start.6) | collective-permute-done | bytes 524320 | tf_op jit(solution)/shard_map/ppermute | solution.py:413
  44.7 1.2 copy-done.10
  45.9 1.2 copy-done.12
  47.1 1.2 copy-done.13
  48.3 1.0 copy-done.18
  49.4 1.7 %shard_map.82 = (bf16[512,1024]{1,0:T(8,128)(2,1)S(1)}, f32[4,128]{1,0:T(4,128)S(1)}) custom-call(s32[2]{0:T(128)S(1)} %pad_add_fusion.1.place_ref, bf16[512,1024]{1,0:T(8,128)(2,1)S(1)} %copy-done.3, bf16[512,1024]{1,0:T(8,128)(2,1)S(1)} %copy-done.13, f32[32,1,128]{2,1,0:T(1,128)S(1)} %bitcast.24, f32[8,128,128]{2,1,0:T(8,128)S(1)} %copy-done.18, ...), custom_call_target="tpu_custom_call" | custom-call | flops 1 | bytes 1 | tf_op jit(solution)/shard_map/pallas_call | solution.py:48
  51.7 1.5 %collective-permute-start.17 = (bf16[512,1024]{1,0:T(8,128)(2,1)S(1)}, bf16[512,1024]{1,0:T(8,128)(2,1)S(1)}, u32[]{:S(2)}, u32[]{:S(2)}) collective-permute-start(bf16[512,1024]{1,0:T(8,128)(2,1)S(1)} %get-tuple-element.69.refs_0_), channel_id=1, source_target_pairs={{0,4},{4,0},{8,12},{12,8},{16,20},{20,16},{24,28},{28,24},{1,5},{5... | collective-permute-start | bytes 3145736 | tf_op jit(solution)/shard_map/ppermute | solution.py:438
  53.2 1.3 collective-permute-start.11
  55.9 12.5 %collective-permute-done.11.refs_2_ = bf16[1024,256]{1,0:T(8,128)(2,1)S(1)} collective-permute-done((bf16[1024,256]{1,0:T(8,128)(2,1)}, bf16[1024,256]{1,0:T(8,128)(2,1)S(1)}, u32[]{:S(2)}, u32[]{:S(2)}) %collective-permute-start.11) | collective-permute-done | bytes 524320 | tf_op jit(solution)/shard_map/ppermute | solution.py:413
  68.4 1.2 copy-done.5
  69.6 1.8 %shard_map.83 = (bf16[256,512]{1,0:T(8,128)(2,1)S(1)}, f32[256,512]{1,0:T(8,128)S(1)}) custom-call(s32[1]{0:T(128)} %bitcast.9.flag_ref, bf16[512,1024]{1,0:T(8,128)(2,1)S(1)} %get-tuple-element.69.refs_0_, bf16[1024,256]{1,0:T(8,128)(2,1)S(1)} %copy-done.5, bf16[1024,256]{1,0:T(8,128)(2,1)} %shard_map.79.refs_2_), custom_call_target="tpu_custom_call" | custom-call | flops 1 | bytes 1 | tf_op jit(solution)/shard_map/pallas_call | solution.py:48
  71.5 2.0 %shard_map.86 = (bf16[256,512]{1,0:T(8,128)(2,1)S(1)}, f32[256,512]{1,0:T(8,128)S(1)}) custom-call(s32[1]{0:T(128)} %bitcast.9.flag_ref, bf16[512,1024]{1,0:T(8,128)(2,1)S(1)} %get-tuple-element.69.refs_0_, bf16[1024,256]{1,0:T(8,128)(2,1)} %collective-permute-done.2.refs_1_, bf16[1024,256]{1,0:T(8,128)(2,1)} %collective-permute-done.6.refs_2_), custom_call_target="tpu_custom_call" | custom-call | flops 1 | bytes 1 | tf_op jit(solution)/shard_map/pallas_call | solution.py:48
  74.0 1.6 %collective-permute-start.10 = (f32[1,128]{1,0:T(1,128)S(1)}, f32[1,128]{1,0:T(1,128)S(1)}, u32[]{:S(2)}, u32[]{:S(2)}) collective-permute-start(f32[1,128]{1,0:T(1,128)S(1)} %slice.15), channel_id=1, source_target_pairs={{0,2},{1,3},{2,0},{3,1},{4,6},{5,7},{6,4},{7,5},{8,10},{9,11},{10,... | collective-permute-start | bytes 1544 | tf_op jit(solution)/shard_map/ppermute | solution.py:443
  75.6 1.3 collective-permute-start.24
  76.9 0.7 collective-permute-done.10
  78.3 1.8 %shard_map.89 = (bf16[256,512]{1,0:T(8,128)(2,1)S(1)}, f32[256,512]{1,0:T(8,128)S(1)}) custom-call(s32[1]{0:T(128)} %bitcast.9.flag_ref, bf16[512,1024]{1,0:T(8,128)(2,1)S(1)} %collective-permute-done.17.refs_0_.refs_1_, bf16[1024,256]{1,0:T(8,128)(2,1)S(1)} %copy-done.6, bf16[1024,256]{1,0:T(8,128)(2,1)} %shard_map.79.refs_2_), custom_call_target="tpu_custom_call" | custom-call | flops 1 | bytes 1 | tf_op jit(solution)/shard_map/pallas_call | solution.py:48
  80.2 2.0 %shard_map.92 = (bf16[256,512]{1,0:T(8,128)(2,1)S(1)}, f32[256,512]{1,0:T(8,128)S(1)}) custom-call(s32[1]{0:T(128)} %bitcast.9.flag_ref, bf16[512,1024]{1,0:T(8,128)(2,1)S(1)} %collective-permute-done.17.refs_0_.refs_1_, bf16[1024,256]{1,0:T(8,128)(2,1)} %collective-permute-done.2.refs_1_, bf16[1024,256]{1,0:T(8,128)(2,1)} %collective-permute-done.6.refs_2_), custom_call_target="tpu_custom_call" | custom-call | flops 1 | bytes 1 | tf_op jit(solution)/shard_map/pallas_call | solution.py:48
  82.7 1.3 collective-permute-start.31
  84.8 1.5 %collective-permute-start.14 = (bf16[128,512]{1,0:T(8,128)(2,1)S(1)}, bf16[128,512]{1,0:T(8,128)(2,1)S(1)}, u32[]{:S(2)}, u32[]{:S(2)}) collective-permute-start(bf16[128,512]{1,0:T(8,128)(2,1)S(1)} %get-tuple-element.73), channel_id=1, source_target_pairs={{0,2},{1,3},{2,0},{3,1},{4,6},{5,7},{6,4},{7,5},{8,10},{9,11},{10,... | collective-permute-start | bytes 393224 | tf_op jit(solution)/shard_map/ppermute | solution.py:464
  86.9 4.2 %collective-permute-done.14.got_ref = bf16[128,512]{1,0:T(8,128)(2,1)S(1)} collective-permute-done((bf16[128,512]{1,0:T(8,128)(2,1)S(1)}, bf16[128,512]{1,0:T(8,128)(2,1)S(1)}, u32[]{:S(2)}, u32[]{:S(2)}) %collective-permute-start.14) | collective-permute-done | bytes 131104 | tf_op jit(solution)/shard_map/ppermute | solution.py:464
  91.2 1.5 %collective-permute-start.19 = (bf16[128,512]{1,0:T(8,128)(2,1)S(1)}, bf16[128,512]{1,0:T(8,128)(2,1)S(1)}, u32[]{:S(2)}, u32[]{:S(2)}) collective-permute-start(bf16[128,512]{1,0:T(8,128)(2,1)S(1)} %get-tuple-element.83), channel_id=1, source_target_pairs={{0,2},{1,3},{2,0},{3,1},{4,6},{5,7},{6,4},{7,5},{8,10},{9,11},{10,... | collective-permute-start | bytes 393224 | tf_op jit(solution)/shard_map/ppermute | solution.py:464
  92.7 1.3 collective-permute-done.16.got_ref
  94.0 1.5 %collective-permute-start.22 = (bf16[128,512]{1,0:T(8,128)(2,1)S(1)}, bf16[128,512]{1,0:T(8,128)(2,1)S(1)}, u32[]{:S(2)}, u32[]{:S(2)}) collective-permute-start(bf16[128,512]{1,0:T(8,128)(2,1)S(1)} %get-tuple-element.88), channel_id=1, source_target_pairs={{0,2},{1,3},{2,0},{3,1},{4,6},{5,7},{6,4},{7,5},{8,10},{9,11},{10,... | collective-permute-start | bytes 393224 | tf_op jit(solution)/shard_map/ppermute | solution.py:464
  95.5 2.1 %shard_map.95 = (bf16[256,512]{1,0:T(8,128)(2,1)S(1)}, f32[256,512]{1,0:T(8,128)S(1)}) custom-call(s32[1]{0:T(128)} %bitcast.9.flag_ref, bf16[512,1024]{1,0:T(8,128)(2,1)S(1)} %get-tuple-element.69.refs_0_, bf16[1024,256]{1,0:T(8,128)(2,1)} %collective-permute-done.3.refs_1_, bf16[1024,256]{1,0:T(8,128)(2,1)S(1)} %collective-permute-done.11.refs_2_, ...), custom_call_target="tpu_custom_call" | custom-call | flops 1 | bytes 1 | tf_op jit(solution)/shard_map/pallas_call | solution.py:48
  97.6 2.3 %shard_map.98 = (bf16[256,512]{1,0:T(8,128)(2,1)S(1)}, f32[256,512]{1,0:T(8,128)S(1)}) custom-call(s32[1]{0:T(128)} %bitcast.9.flag_ref, bf16[512,1024]{1,0:T(8,128)(2,1)S(1)} %collective-permute-done.17.refs_0_.refs_1_, bf16[1024,256]{1,0:T(8,128)(2,1)} %collective-permute-done.3.refs_1_, bf16[1024,256]{1,0:T(8,128)(2,1)S(1)} %collective-permute-done.11.refs_2_, ...), custom_call_target="tpu_custom_call" | custom-call | flops 1 | bytes 1 | tf_op jit(solution)/shard_map/pallas_call | solution.py:48
  100.0 3.9 %collective-permute-done.31.refs_3_ = bf16[1024,256]{1,0:T(8,128)(2,1)S(1)} collective-permute-done((bf16[1024,256]{1,0:T(8,128)(2,1)S(1)}, bf16[1024,256]{1,0:T(8,128)(2,1)S(1)}, u32[]{:S(2)}, u32[]{:S(2)}) %collective-permute-start.31) | collective-permute-done | bytes 524320 | tf_op jit(solution)/shard_map/ppermute | solution.py:413
  104.7 1.3 collective-permute-start.35
  107.2 1.6 %collective-permute-start.33 = (bf16[128,512]{1,0:T(8,128)(2,1)S(1)}, bf16[128,512]{1,0:T(8,128)(2,1)S(1)}, u32[]{:S(2)}, u32[]{:S(2)}) collective-permute-start(bf16[128,512]{1,0:T(8,128)(2,1)S(1)} %get-tuple-element.105), channel_id=1, source_target_pairs={{0,2},{1,3},{2,0},{3,1},{4,6},{5,7},{6,4},{7,5},{8,10},{9,11},{10,... | collective-permute-start | bytes 393224 | tf_op jit(solution)/shard_map/ppermute | solution.py:464
  111.9 1.1 collective-permute-done.29.got_ref
  114.2 1.6 %collective-permute-done.33.got_ref = bf16[128,512]{1,0:T(8,128)(2,1)S(1)} collective-permute-done((bf16[128,512]{1,0:T(8,128)(2,1)S(1)}, bf16[128,512]{1,0:T(8,128)(2,1)S(1)}, u32[]{:S(2)}, u32[]{:S(2)}) %collective-permute-start.33) | collective-permute-done | bytes 131104 | tf_op jit(solution)/shard_map/ppermute | solution.py:464
  118.3 1.4 %collective-permute-start.34 = (bf16[128,256]{1,0:T(8,128)(2,1)}, bf16[128,256]{1,0:T(8,128)(2,1)}, u32[]{:S(2)}, u32[]{:S(2)}) collective-permute-start(bf16[128,256]{1,0:T(8,128)(2,1)} %get-tuple-element.107), channel_id=1, source_target_pairs={{0,4},{4,0},{8,12},{12,8},{16,20},{20,16},{24,28},{28,24},{1,5},{5... | collective-permute-start | bytes 196616 | tf_op jit(solution)/shard_map/ppermute | solution.py:473
  119.9 0.9 copy-done.20
  120.9 0.9 copy-done.22
  121.9 1.1 collective-permute-done.34.refs_7_
  122.9 2.4 %shard_map.104.refs_2_ = bf16[128,4096]{1,0:T(8,128)(2,1)} custom-call(s32[14]{0:T(128)S(1)} %stack.118.starts_ref, f32[1,128]{1,0:T(1,128)S(1)} %slice_add_fusion.1.squares_ref, bf16[128,512]{1,0:T(8,128)(2,1)S(1)} %shard_map.85.refs_0_, bf16[128,512]{1,0:T(8,128)(2,1)S(1)} %shard_map.88.refs_1_, bf16[128,512]{1,0:T(8,128)(2,1)} %collective-permute-done.20.refs_2_, ...), custom_call_target="tpu_custom_call" | custom-call | flops 1 | bytes 1 | tf_op jit(solution)/shard_map/pallas_call | solution.py:48
  126.1 1.5 %collective-permute-done.36.got_ref = bf16[256,512]{1,0:T(8,128)(2,1)S(1)} collective-permute-done((bf16[256,512]{1,0:T(8,128)(2,1)S(1)}, bf16[256,512]{1,0:T(8,128)(2,1)S(1)}, u32[]{:S(2)}, u32[]{:S(2)}) %collective-permute-start.36) | collective-permute-done | bytes 262176 | tf_op jit(solution)/shard_map/ppermute | solution.py:464
  127.7 1.3 collective-permute-start.37
  129.0 4.3 %collective-permute-done.37.got_ref = bf16[128,512]{1,0:T(8,128)(2,1)S(1)} collective-permute-done((bf16[128,512]{1,0:T(8,128)(2,1)S(1)}, bf16[128,512]{1,0:T(8,128)(2,1)S(1)}, u32[]{:S(2)}, u32[]{:S(2)}) %collective-permute-start.37) | collective-permute-done | bytes 131104 | tf_op jit(solution)/shard_map/ppermute | solution.py:464
  133.3 1.5 %collective-permute-start.38 = (bf16[128,256]{1,0:T(8,128)(2,1)S(1)}, bf16[128,256]{1,0:T(8,128)(2,1)S(1)}, u32[]{:S(2)}, u32[]{:S(2)}) collective-permute-start(bf16[128,256]{1,0:T(8,128)(2,1)S(1)} %get-tuple-element.114), channel_id=1, source_target_pairs={{0,4},{4,0},{8,12},{12,8},{16,20},{20,16},{24,28},{28,24},{1,5},{5... | collective-permute-start | bytes 196616 | tf_op jit(solution)/shard_map/ppermute | solution.py:473
  134.8 2.8 %collective-permute-done.38.refs_1_ = bf16[128,256]{1,0:T(8,128)(2,1)S(1)} collective-permute-done((bf16[128,256]{1,0:T(8,128)(2,1)S(1)}, bf16[128,256]{1,0:T(8,128)(2,1)S(1)}, u32[]{:S(2)}, u32[]{:S(2)}) %collective-permute-start.38) | collective-permute-done | bytes 65568 | tf_op jit(solution)/shard_map/ppermute | solution.py:473
  137.6 1.3 shard_map.108
  (126 shorter events, 16.3 us)
Async XLA Ops:
  0.0 5.9 %copy-start = (bf16[512,1024]{1,0:T(8,128)(2,1)S(1)}, bf16[512,1024]{1,0:T(8,128)(2,1)}, u32[]{:S(2)}) copy-start(bf16[512,1024]{1,0:T(8,128)(2,1)} %k_ref.7) | copy-start | bytes 3145732
  0.0 1.3 copy-start.7
  1.4 7.1 %copy-start.4 = (bf16[1024,256]{1,0:T(8,128)(2,1)}, bf16[1024,256]{1,0:T(8,128)(2,1)S(1)}, u32[]{:S(2)}) copy-start(bf16[1024,256]{1,0:T(8,128)(2,1)S(1)} %shard_map.76.refs_1_) | copy-start | bytes 1572868
  1.4 20.2 %collective-permute-start.2 = (bf16[1024,256]{1,0:T(8,128)(2,1)S(1)}, bf16[1024,256]{1,0:T(8,128)(2,1)}, u32[]{:S(2)}, u32[]{:S(2)}) collective-permute-start(bf16[1024,256]{1,0:T(8,128)(2,1)S(1)} %shard_map.76.refs_1_), channel_id=1, source_target_pairs={{0,8},{4,12},{8,0},{12,4},{16,24},{20,28},{24,16},{28,20},{1,9},{5... | collective-permute-start | bytes 1572872 | tf_op jit(solution)/shard_map/ppermute | solution.py:413
  4.5 17.1 %collective-permute-start.3 = (bf16[1024,256]{1,0:T(8,128)(2,1)S(1)}, bf16[1024,256]{1,0:T(8,128)(2,1)}, u32[]{:S(2)}, u32[]{:S(2)}) collective-permute-start(bf16[1024,256]{1,0:T(8,128)(2,1)S(1)} %shard_map.76.refs_1_), channel_id=1, source_target_pairs={{8,16},{12,20},{16,8},{20,12},{9,17},{13,21},{17,9},{21,13},{10,18... | collective-permute-start | bytes 1572872 | tf_op jit(solution)/shard_map/ppermute | solution.py:413
  5.9 1.2 copy-start.1
  7.2 2.9 %copy-start.2 = (bf16[512,1024]{1,0:T(8,128)(2,1)S(1)}, bf16[512,1024]{1,0:T(8,128)(2,1)}, u32[]{:S(2)}) copy-start(bf16[512,1024]{1,0:T(8,128)(2,1)} %v_ref.7) | copy-start | bytes 3145732
  8.5 5.0 %collective-permute-start = (bf16[4,128,128]{2,1,0:T(8,128)(2,1)S(1)}, bf16[4,128,128]{2,1,0:T(8,128)(2,1)S(1)}, u32[]{:S(2)}, u32[]{:S(2)}) collective-permute-start(bf16[4,128,128]{2,1,0:T(8,128)(2,1)S(1)} %shard_map.74), channel_id=1, source_target_pairs={{0,4},{4,0},{8,12},{12,8},{16,20},{20,16},{24,28},{28,24},{1,5},{5... | collective-permute-start | bytes 393224 | tf_op jit(solution)/shard_map/ppermute | solution.py:162
  11.3 13.7 %copy-start.8 = (bf16[1024,512]{1,0:T(8,128)(2,1)S(1)}, bf16[1024,512]{1,0:T(8,128)(2,1)}, u32[]{:S(2)}) copy-start(bf16[1024,512]{1,0:T(8,128)(2,1)} %w_ref.3) | copy-start | bytes 3145732
  13.5 8.0 %collective-permute-start.1 = (bf16[4,128,128]{2,1,0:T(8,128)(2,1)S(1)}, bf16[4,128,128]{2,1,0:T(8,128)(2,1)S(1)}, u32[]{:S(2)}, u32[]{:S(2)}) collective-permute-start(bf16[4,128,128]{2,1,0:T(8,128)(2,1)S(1)} %shard_map.75), channel_id=1, source_target_pairs={{0,8},{4,12},{16,24},{20,28},{1,9},{5,13},{17,25},{21,29},{2,10},{... | collective-permute-start | bytes 393224 | tf_op jit(solution)/shard_map/ppermute | solution.py:165
  22.3 15.0 %copy-start.3 = (bf16[512,1024]{1,0:T(8,128)(2,1)S(1)}, bf16[512,1024]{1,0:T(8,128)(2,1)}, u32[]{:S(2)}) copy-start(bf16[512,1024]{1,0:T(8,128)(2,1)} %q_ref.5) | copy-start | bytes 3145732
  22.3 3.7 %collective-permute-start.4 = (bf16[4,128,128]{2,1,0:T(8,128)(2,1)}, bf16[4,128,128]{2,1,0:T(8,128)(2,1)}, u32[]{:S(2)}, u32[]{:S(2)}) collective-permute-start(bf16[4,128,128]{2,1,0:T(8,128)(2,1)} %shard_map.77), channel_id=1, source_target_pairs={{8,16},{12,20},{9,17},{13,21},{10,18},{14,22},{11,19},{15,23}} | collective-permute-start | bytes 393224 | tf_op jit(solution)/shard_map/ppermute | solution.py:168
  23.7 2.3 %collective-permute-start.5 = (bf16[4,128,128]{2,1,0:T(8,128)(2,1)}, bf16[4,128,128]{2,1,0:T(8,128)(2,1)}, u32[]{:S(2)}, u32[]{:S(2)}) collective-permute-start(bf16[4,128,128]{2,1,0:T(8,128)(2,1)} %shard_map.77), channel_id=1, source_target_pairs={{8,24},{12,28},{9,25},{13,29},{10,26},{14,30},{11,27},{15,31}} | collective-permute-start | bytes 393224 | tf_op jit(solution)/shard_map/ppermute | solution.py:169
  29.4 15.3 %collective-permute-start.6 = (bf16[1024,256]{1,0:T(8,128)(2,1)}, bf16[1024,256]{1,0:T(8,128)(2,1)}, u32[]{:S(2)}, u32[]{:S(2)}) collective-permute-start(bf16[1024,256]{1,0:T(8,128)(2,1)} %shard_map.79.refs_2_), channel_id=1, source_target_pairs={{0,8},{4,12},{8,0},{12,4},{16,24},{20,28},{24,16},{28,20},{1,9},{5... | collective-permute-start | bytes 1572872 | tf_op jit(solution)/shard_map/ppermute | solution.py:413
  34.3 10.3 %collective-permute-start.7 = (bf16[1024,256]{1,0:T(8,128)(2,1)}, bf16[1024,256]{1,0:T(8,128)(2,1)}, u32[]{:S(2)}, u32[]{:S(2)}) collective-permute-start(bf16[1024,256]{1,0:T(8,128)(2,1)} %shard_map.79.refs_2_), channel_id=1, source_target_pairs={{8,16},{12,20},{16,8},{20,12},{9,17},{13,21},{17,9},{21,13},{10,18... | collective-permute-start | bytes 1572872 | tf_op jit(solution)/shard_map/ppermute | solution.py:413
  35.8 8.9 %collective-permute-start.8 = (bf16[4,128,128]{2,1,0:T(8,128)(2,1)}, bf16[4,128,128]{2,1,0:T(8,128)(2,1)S(1)}, u32[]{:S(2)}, u32[]{:S(2)}) collective-permute-start(bf16[4,128,128]{2,1,0:T(8,128)(2,1)} %get-tuple-element.64), channel_id=1, source_target_pairs={{0,4},{4,0},{8,12},{12,8},{16,20},{20,16},{24,28},{28,24},{1,5},{5... | collective-permute-start | bytes 393224 | tf_op jit(solution)/shard_map/ppermute | solution.py:176
  38.4 1.0 copy-start.9
  39.3 5.3 %copy-start.24 = (f32[4,128,128]{2,1,0:T(8,128)S(1)}, f32[4,128,128]{2,1,0:T(8,128)}, u32[]{:S(2)}) copy-start(f32[4,128,128]{2,1,0:T(8,128)} %copy-done.23) | copy-start | bytes 786436
  39.3 5.3 %copy-start.31 = (f32[4096]{0:T(1024)S(1)}, f32[4096]{0:T(1024)}, u32[]{:S(2)}) copy-start(f32[4096]{0:T(1024)} %param.12) | copy-start | bytes 49156
  40.4 1.0 copy-start.11
  44.7 1.2 copy-start.10
  45.9 1.2 copy-start.12
  47.1 1.2 copy-start.13
  48.3 1.0 copy-start.18
  51.7 26.6 %collective-permute-start.17 = (bf16[512,1024]{1,0:T(8,128)(2,1)S(1)}, bf16[512,1024]{1,0:T(8,128)(2,1)S(1)}, u32[]{:S(2)}, u32[]{:S(2)}) collective-permute-start(bf16[512,1024]{1,0:T(8,128)(2,1)S(1)} %get-tuple-element.69.refs_0_), channel_id=1, source_target_pairs={{0,4},{4,0},{8,12},{12,8},{16,20},{20,16},{24,28},{28,24},{1,5},{5... | collective-permute-start | bytes 3145736 | tf_op jit(solution)/shard_map/ppermute | solution.py:438
  53.2 15.2 %collective-permute-start.11 = (bf16[1024,256]{1,0:T(8,128)(2,1)}, bf16[1024,256]{1,0:T(8,128)(2,1)S(1)}, u32[]{:S(2)}, u32[]{:S(2)}) collective-permute-start(bf16[1024,256]{1,0:T(8,128)(2,1)} %collective-permute-done.3.refs_1_), channel_id=1, source_target_pairs={{8,0},{12,4},{16,24},{20,28},{9,1},{13,5},{17,25},{21,29},{10,2},{... | collective-permute-start | bytes 1572872 | tf_op jit(solution)/shard_map/ppermute | solution.py:413
  54.5 13.9 %collective-permute-start.12 = (bf16[1024,256]{1,0:T(8,128)(2,1)}, bf16[1024,256]{1,0:T(8,128)(2,1)S(1)}, u32[]{:S(2)}, u32[]{:S(2)}) collective-permute-start(bf16[1024,256]{1,0:T(8,128)(2,1)} %collective-permute-done.2.refs_1_), channel_id=1, source_target_pairs={{8,16},{12,20},{16,8},{20,12},{9,17},{13,21},{17,9},{21,13},{10,18... | collective-permute-start | bytes 1572872 | tf_op jit(solution)/shard_map/ppermute | solution.py:413
  55.9 18.1 %collective-permute-start.9 = (f32[2,128]{1,0:T(2,128)S(1)}, f32[2,128]{1,0:T(2,128)S(1)}, u32[]{:S(2)}, u32[]{:S(2)}) collective-permute-start(f32[2,128]{1,0:T(2,128)S(1)} %slice.13), channel_id=1, source_target_pairs={{0,1},{1,0},{2,3},{3,2},{4,5},{5,4},{6,7},{7,6},{8,9},{9,8},{10,11... | collective-permute-start | bytes 3080 | tf_op jit(solution)/shard_map/ppermute | solution.py:443
  68.4 3.0 %copy-start.14 = (bf16[1024,256]{1,0:T(8,128)(2,1)}, bf16[1024,256]{1,0:T(8,128)(2,1)S(1)}, u32[]{:S(2)}) copy-start(bf16[1024,256]{1,0:T(8,128)(2,1)S(1)} %collective-permute-done.12.refs_2_) | copy-start | bytes 1572868
  68.4 1.2 copy-start.5
  71.4 6.9 %copy-start.6 = (bf16[1024,256]{1,0:T(8,128)(2,1)S(1)}, bf16[1024,256]{1,0:T(8,128)(2,1)}, u32[]{:S(2)}) copy-start(bf16[1024,256]{1,0:T(8,128)(2,1)} %copy-done.4) | copy-start | bytes 1572868
  71.4 10.7 %collective-permute-start.13 = (bf16[256,512]{1,0:T(8,128)(2,1)S(1)}, bf16[256,512]{1,0:T(8,128)(2,1)S(1)}, u32[]{:S(2)}, u32[]{:S(2)}) collective-permute-start(bf16[256,512]{1,0:T(8,128)(2,1)S(1)} %get-tuple-element.71), channel_id=1, source_target_pairs={{0,1},{1,0},{2,3},{3,2},{4,5},{5,4},{6,7},{7,6},{8,9},{9,8},{10,11... | collective-permute-start | bytes 786440 | tf_op jit(solution)/shard_map/ppermute | solution.py:464
  73.5 9.2 %collective-permute-start.15 = (bf16[256,512]{1,0:T(8,128)(2,1)S(1)}, bf16[256,512]{1,0:T(8,128)(2,1)S(1)}, u32[]{:S(2)}, u32[]{:S(2)}) collective-permute-start(bf16[256,512]{1,0:T(8,128)(2,1)S(1)} %get-tuple-element.76), channel_id=1, source_target_pairs={{0,1},{1,0},{2,3},{3,2},{4,5},{5,4},{6,7},{7,6},{8,9},{9,8},{10,11... | collective-permute-start | bytes 786440 | tf_op jit(solution)/shard_map/ppermute | solution.py:464
  74.0 3.6 %collective-permute-start.10 = (f32[1,128]{1,0:T(1,128)S(1)}, f32[1,128]{1,0:T(1,128)S(1)}, u32[]{:S(2)}, u32[]{:S(2)}) collective-permute-start(f32[1,128]{1,0:T(1,128)S(1)} %slice.15), channel_id=1, source_target_pairs={{0,2},{1,3},{2,0},{3,1},{4,6},{5,7},{6,4},{7,5},{8,10},{9,11},{10,... | collective-permute-start | bytes 1544 | tf_op jit(solution)/shard_map/ppermute | solution.py:443
  75.6 19.9 %collective-permute-start.24 = (bf16[1024,256]{1,0:T(8,128)(2,1)}, bf16[1024,256]{1,0:T(8,128)(2,1)S(1)}, u32[]{:S(2)}, u32[]{:S(2)}) collective-permute-start(bf16[1024,256]{1,0:T(8,128)(2,1)} %collective-permute-done.7.refs_3_), channel_id=1, source_target_pairs={{8,0},{12,4},{16,24},{20,28},{9,1},{13,5},{17,25},{21,29},{10,2},{... | collective-permute-start | bytes 1572872 | tf_op jit(solution)/shard_map/ppermute | solution.py:413
  77.6 17.9 %collective-permute-start.25 = (bf16[1024,256]{1,0:T(8,128)(2,1)}, bf16[1024,256]{1,0:T(8,128)(2,1)S(1)}, u32[]{:S(2)}, u32[]{:S(2)}) collective-permute-start(bf16[1024,256]{1,0:T(8,128)(2,1)} %collective-permute-done.6.refs_2_), channel_id=1, source_target_pairs={{8,16},{12,20},{16,8},{20,12},{9,17},{13,21},{17,9},{21,13},{10,18... | collective-permute-start | bytes 1572872 | tf_op jit(solution)/shard_map/ppermute | solution.py:413
  80.1 2.6 %copy-start.15 = (bf16[1024,256]{1,0:T(8,128)(2,1)S(1)}, bf16[1024,256]{1,0:T(8,128)(2,1)}, u32[]{:S(2)}) copy-start(bf16[1024,256]{1,0:T(8,128)(2,1)} %copy-done.14) | copy-start | bytes 1572868
  80.1 4.7 %collective-permute-start.18 = (bf16[256,512]{1,0:T(8,128)(2,1)S(1)}, bf16[256,512]{1,0:T(8,128)(2,1)S(1)}, u32[]{:S(2)}, u32[]{:S(2)}) collective-permute-start(bf16[256,512]{1,0:T(8,128)(2,1)S(1)} %get-tuple-element.81), channel_id=1, source_target_pairs={{0,1},{1,0},{2,3},{3,2},{4,5},{5,4},{6,7},{7,6},{8,9},{9,8},{10,11... | collective-permute-start | bytes 786440 | tf_op jit(solution)/shard_map/ppermute | solution.py:464
  82.2 4.2 %collective-permute-start.21 = (bf16[256,512]{1,0:T(8,128)(2,1)S(1)}, bf16[256,512]{1,0:T(8,128)(2,1)S(1)}, u32[]{:S(2)}, u32[]{:S(2)}) collective-permute-start(bf16[256,512]{1,0:T(8,128)(2,1)S(1)} %get-tuple-element.86), channel_id=1, source_target_pairs={{0,1},{1,0},{2,3},{3,2},{4,5},{5,4},{6,7},{7,6},{8,9},{9,8},{10,11... | collective-permute-start | bytes 786440 | tf_op jit(solution)/shard_map/ppermute | solution.py:464
  82.7 21.2 %collective-permute-start.31 = (bf16[1024,256]{1,0:T(8,128)(2,1)S(1)}, bf16[1024,256]{1,0:T(8,128)(2,1)S(1)}, u32[]{:S(2)}, u32[]{:S(2)}) collective-permute-start(bf16[1024,256]{1,0:T(8,128)(2,1)S(1)} %copy-done.15), channel_id=1, source_target_pairs={{8,0},{12,4},{16,24},{20,28},{9,1},{13,5},{17,25},{21,29},{10,2},{... | collective-permute-start | bytes 1572872 | tf_op jit(solution)/shard_map/ppermute | solution.py:413
  84.8 6.4 %collective-permute-start.14 = (bf16[128,512]{1,0:T(8,128)(2,1)S(1)}, bf16[128,512]{1,0:T(8,128)(2,1)S(1)}, u32[]{:S(2)}, u32[]{:S(2)}) collective-permute-start(bf16[128,512]{1,0:T(8,128)(2,1)S(1)} %get-tuple-element.73), channel_id=1, source_target_pairs={{0,2},{1,3},{2,0},{3,1},{4,6},{5,7},{6,4},{7,5},{8,10},{9,11},{10,... | collective-permute-start | bytes 393224 | tf_op jit(solution)/shard_map/ppermute | solution.py:464
  86.4 7.6 %collective-permute-start.16 = (bf16[128,512]{1,0:T(8,128)(2,1)S(1)}, bf16[128,512]{1,0:T(8,128)(2,1)S(1)}, u32[]{:S(2)}, u32[]{:S(2)}) collective-permute-start(bf16[128,512]{1,0:T(8,128)(2,1)S(1)} %get-tuple-element.78), channel_id=1, source_target_pairs={{0,2},{1,3},{2,0},{3,1},{4,6},{5,7},{6,4},{7,5},{8,10},{9,11},{10,... | collective-permute-start | bytes 393224 | tf_op jit(solution)/shard_map/ppermute | solution.py:464
  91.2 8.8 %collective-permute-start.19 = (bf16[128,512]{1,0:T(8,128)(2,1)S(1)}, bf16[128,512]{1,0:T(8,128)(2,1)S(1)}, u32[]{:S(2)}, u32[]{:S(2)}) collective-permute-start(bf16[128,512]{1,0:T(8,128)(2,1)S(1)} %get-tuple-element.83), channel_id=1, source_target_pairs={{0,2},{1,3},{2,0},{3,1},{4,6},{5,7},{6,4},{7,5},{8,10},{9,11},{10,... | collective-permute-start | bytes 393224 | tf_op jit(solution)/shard_map/ppermute | solution.py:464
  94.0 3.6 %copy-start.25 = (bf16[128,512]{1,0:T(8,128)(2,1)}, bf16[128,512]{1,0:T(8,128)(2,1)S(1)}, u32[]{:S(2)}) copy-start(bf16[128,512]{1,0:T(8,128)(2,1)S(1)} %collective-permute-done.16.got_ref) | copy-start | bytes 393220
  94.0 6.0 %collective-permute-start.22 = (bf16[128,512]{1,0:T(8,128)(2,1)S(1)}, bf16[128,512]{1,0:T(8,128)(2,1)S(1)}, u32[]{:S(2)}, u32[]{:S(2)}) collective-permute-start(bf16[128,512]{1,0:T(8,128)(2,1)S(1)} %get-tuple-element.88), channel_id=1, source_target_pairs={{0,2},{1,3},{2,0},{3,1},{4,6},{5,7},{6,4},{7,5},{8,10},{9,11},{10,... | collective-permute-start | bytes 393224 | tf_op jit(solution)/shard_map/ppermute | solution.py:464
  99.9 6.6 %collective-permute-start.28 = (bf16[256,512]{1,0:T(8,128)(2,1)S(1)}, bf16[256,512]{1,0:T(8,128)(2,1)S(1)}, u32[]{:S(2)}, u32[]{:S(2)}) collective-permute-start(bf16[256,512]{1,0:T(8,128)(2,1)S(1)} %get-tuple-element.98), channel_id=1, source_target_pairs={{0,1},{1,0},{2,3},{3,2},{4,5},{5,4},{6,7},{7,6},{8,9},{9,8},{10,11... | collective-permute-start | bytes 786440 | tf_op jit(solution)/shard_map/ppermute | solution.py:464
  104.6 2.5 %collective-permute-start.32 = (bf16[256,512]{1,0:T(8,128)(2,1)S(1)}, bf16[256,512]{1,0:T(8,128)(2,1)S(1)}, u32[]{:S(2)}, u32[]{:S(2)}) collective-permute-start(bf16[256,512]{1,0:T(8,128)(2,1)S(1)} %get-tuple-element.103), channel_id=1, source_target_pairs={{0,1},{1,0},{2,3},{3,2},{4,5},{5,4},{6,7},{7,6},{8,9},{9,8},{10,11... | collective-permute-start | bytes 786440 | tf_op jit(solution)/shard_map/ppermute | solution.py:464
  104.7 20.6 %collective-permute-start.35 = (bf16[1024,256]{1,0:T(8,128)(2,1)S(1)}, bf16[1024,256]{1,0:T(8,128)(2,1)S(1)}, u32[]{:S(2)}, u32[]{:S(2)}) collective-permute-start(bf16[1024,256]{1,0:T(8,128)(2,1)S(1)} %collective-permute-done.25.refs_2_), channel_id=1, source_target_pairs={{8,0},{12,4},{16,24},{20,28},{9,1},{13,5},{17,25},{21,29},{10,2},{... | collective-permute-start | bytes 1572872 | tf_op jit(solution)/shard_map/ppermute | solution.py:413
  106.0 2.8 %collective-permute-start.26 = (bf16[256,512]{1,0:T(8,128)(2,1)S(1)}, bf16[256,512]{1,0:T(8,128)(2,1)S(1)}, u32[]{:S(2)}, u32[]{:S(2)}) collective-permute-start(bf16[256,512]{1,0:T(8,128)(2,1)S(1)} %get-tuple-element.93), channel_id=1, source_target_pairs={{0,1},{1,0},{2,3},{3,2},{4,5},{5,4},{6,7},{7,6},{8,9},{9,8},{10,11... | collective-permute-start | bytes 786440 | tf_op jit(solution)/shard_map/ppermute | solution.py:464
  106.6 6.4 %collective-permute-start.29 = (bf16[128,512]{1,0:T(8,128)(2,1)S(1)}, bf16[128,512]{1,0:T(8,128)(2,1)S(1)}, u32[]{:S(2)}, u32[]{:S(2)}) collective-permute-start(bf16[128,512]{1,0:T(8,128)(2,1)S(1)} %get-tuple-element.100), channel_id=1, source_target_pairs={{0,2},{1,3},{2,0},{3,1},{4,6},{5,7},{6,4},{7,5},{8,10},{9,11},{10,... | collective-permute-start | bytes 393224 | tf_op jit(solution)/shard_map/ppermute | solution.py:464
  107.2 8.6 %collective-permute-start.33 = (bf16[128,512]{1,0:T(8,128)(2,1)S(1)}, bf16[128,512]{1,0:T(8,128)(2,1)S(1)}, u32[]{:S(2)}, u32[]{:S(2)}) collective-permute-start(bf16[128,512]{1,0:T(8,128)(2,1)S(1)} %get-tuple-element.105), channel_id=1, source_target_pairs={{0,2},{1,3},{2,0},{3,1},{4,6},{5,7},{6,4},{7,5},{8,10},{9,11},{10,... | collective-permute-start | bytes 393224 | tf_op jit(solution)/shard_map/ppermute | solution.py:464
  109.5 8.1 %collective-permute-start.27 = (bf16[128,512]{1,0:T(8,128)(2,1)S(1)}, bf16[128,512]{1,0:T(8,128)(2,1)S(1)}, u32[]{:S(2)}, u32[]{:S(2)}) collective-permute-start(bf16[128,512]{1,0:T(8,128)(2,1)S(1)} %get-tuple-element.95), channel_id=1, source_target_pairs={{0,2},{1,3},{2,0},{3,1},{4,6},{5,7},{6,4},{7,5},{8,10},{9,11},{10,... | collective-permute-start | bytes 393224 | tf_op jit(solution)/shard_map/ppermute | solution.py:464
  110.7 11.1 %collective-permute-start.20 = (bf16[128,512]{1,0:T(8,128)(2,1)}, bf16[128,512]{1,0:T(8,128)(2,1)}, u32[]{:S(2)}, u32[]{:S(2)}) collective-permute-start(bf16[128,512]{1,0:T(8,128)(2,1)} %shard_map.91), channel_id=1, source_target_pairs={{0,4},{4,0},{8,12},{12,8},{16,20},{20,16},{24,28},{28,24},{1,5},{5... | collective-permute-start | bytes 393224 | tf_op jit(solution)/shard_map/ppermute | solution.py:473
  113.0 8.9 %collective-permute-start.23 = (bf16[128,512]{1,0:T(8,128)(2,1)}, bf16[128,512]{1,0:T(8,128)(2,1)}, u32[]{:S(2)}, u32[]{:S(2)}) collective-permute-start(bf16[128,512]{1,0:T(8,128)(2,1)} %shard_map.94), channel_id=1, source_target_pairs={{0,4},{4,0},{8,12},{12,8},{16,20},{20,16},{24,28},{28,24},{1,5},{5... | collective-permute-start | bytes 393224 | tf_op jit(solution)/shard_map/ppermute | solution.py:473
  115.8 6.1 %collective-permute-start.30 = (bf16[128,512]{1,0:T(8,128)(2,1)}, bf16[128,512]{1,0:T(8,128)(2,1)}, u32[]{:S(2)}, u32[]{:S(2)}) collective-permute-start(bf16[128,512]{1,0:T(8,128)(2,1)} %shard_map.100), channel_id=1, source_target_pairs={{0,4},{4,0},{8,12},{12,8},{16,20},{20,16},{24,28},{28,24},{1,5},{5... | collective-permute-start | bytes 393224 | tf_op jit(solution)/shard_map/ppermute | solution.py:473
  118.3 4.6 %collective-permute-start.34 = (bf16[128,256]{1,0:T(8,128)(2,1)}, bf16[128,256]{1,0:T(8,128)(2,1)}, u32[]{:S(2)}, u32[]{:S(2)}) collective-permute-start(bf16[128,256]{1,0:T(8,128)(2,1)} %get-tuple-element.107), channel_id=1, source_target_pairs={{0,4},{4,0},{8,12},{12,8},{16,20},{20,16},{24,28},{28,24},{1,5},{5... | collective-permute-start | bytes 196616 | tf_op jit(solution)/shard_map/ppermute | solution.py:473
  119.8 1.0 copy-start.20
  119.9 1.0 copy-start.26
  120.8 0.9 copy-start.22
  120.8 1.0 copy-start.28
  121.8 1.1 copy-start.30
  126.0 1.6 %collective-permute-start.36 = (bf16[256,512]{1,0:T(8,128)(2,1)S(1)}, bf16[256,512]{1,0:T(8,128)(2,1)S(1)}, u32[]{:S(2)}, u32[]{:S(2)}) collective-permute-start(bf16[256,512]{1,0:T(8,128)(2,1)S(1)} %get-tuple-element.110), channel_id=1, source_target_pairs={{0,1},{1,0},{2,3},{3,2},{4,5},{5,4},{6,7},{7,6},{8,9},{9,8},{10,11... | collective-permute-start | bytes 786440 | tf_op jit(solution)/shard_map/ppermute | solution.py:464
  127.7 5.6 %collective-permute-start.37 = (bf16[128,512]{1,0:T(8,128)(2,1)S(1)}, bf16[128,512]{1,0:T(8,128)(2,1)S(1)}, u32[]{:S(2)}, u32[]{:S(2)}) collective-permute-start(bf16[128,512]{1,0:T(8,128)(2,1)S(1)} %get-tuple-element.112), channel_id=1, source_target_pairs={{0,2},{1,3},{2,0},{3,1},{4,6},{5,7},{6,4},{7,5},{8,10},{9,11},{10,... | collective-permute-start | bytes 393224 | tf_op jit(solution)/shard_map/ppermute | solution.py:464
  133.3 4.3 %collective-permute-start.38 = (bf16[128,256]{1,0:T(8,128)(2,1)S(1)}, bf16[128,256]{1,0:T(8,128)(2,1)S(1)}, u32[]{:S(2)}, u32[]{:S(2)}) collective-permute-start(bf16[128,256]{1,0:T(8,128)(2,1)S(1)} %get-tuple-element.114), channel_id=1, source_target_pairs={{0,4},{4,0},{8,12},{12,8},{16,20},{20,16},{24,28},{28,24},{1,5},{5... | collective-permute-start | bytes 196616 | tf_op jit(solution)/shard_map/ppermute | solution.py:473
  (9 other events, 6.3 us)

commit v7 on v6

--- a/solution.py
+++ b/solution.py
@@ -43,7 +43,7 @@
     return jnp.stack([jnp.asarray(value, jnp.int32) for value in values])
 
 
-def local_call(kernel, places, operands, out_shapes, scratch=()):
+def local_call(kernel, places, operands, out_shapes, flops=0):
     held = sum(value.size * value.dtype.itemsize for value in [*operands, *out_shapes])
     return pl.pallas_call(
         kernel,
@@ -51,9 +51,8 @@
         + [pl.BlockSpec(memory_space=pltpu.VMEM)] * len(operands),
         out_specs=[pl.BlockSpec(memory_space=pltpu.VMEM)] * len(out_shapes),
         out_shape=out_shapes,
-        scratch_shapes=list(scratch),
         compiler_params=pltpu.CompilerParams(vmem_limit_bytes=max(VMEM_BYTES, held + held // 2)),
-        cost_estimate=pl.CostEstimate(flops=1, bytes_accessed=1, transcendentals=0),
+        cost_estimate=pl.CostEstimate(flops=flops, bytes_accessed=held, transcendentals=0),
     )(places, *operands)
 
 
@@ -93,12 +92,14 @@
         return weight[:, first : first + width]
     return pl.pallas_call(
         functools.partial(cut_kernel, first),
-        in_specs=[pl.BlockSpec(memory_space=pl.ANY)],
+        in_specs=[pl.BlockSpec(memory_space=pltpu.HBM)],
         out_specs=pl.BlockSpec(memory_space=pltpu.VMEM),
         out_shape=jax.ShapeDtypeStruct((weight.shape[0], width), weight.dtype),
         scratch_shapes=[pltpu.SemaphoreType.DMA],
         compiler_params=pltpu.CompilerParams(vmem_limit_bytes=VMEM_BYTES),
-        cost_estimate=pl.CostEstimate(flops=1, bytes_accessed=1, transcendentals=0),
+        cost_estimate=pl.CostEstimate(
+            flops=0, bytes_accessed=4 * weight.shape[0] * width, transcendentals=0
+        ),
     )(weight)
 
 
@@ -129,7 +130,7 @@
     rows = key_input.shape[0]
     return pl.pallas_call(
         states_kernel,
-        in_specs=[pl.BlockSpec(memory_space=pltpu.SMEM)] + [pl.BlockSpec(memory_space=pl.ANY)] * 2,
+        in_specs=[pl.BlockSpec(memory_space=pltpu.SMEM)] + [pl.BlockSpec(memory_space=pltpu.HBM)] * 2,
         out_specs=pl.BlockSpec(memory_space=pltpu.VMEM),
         out_shape=jax.ShapeDtypeStruct((heads, DH, DH), dtype),
         scratch_shapes=[
@@ -138,7 +139,9 @@
             pltpu.SemaphoreType.DMA((2, heads)),
         ],
         compiler_params=pltpu.CompilerParams(vmem_limit_bytes=VMEM_BYTES),
-        cost_estimate=pl.CostEstimate(flops=1, bytes_accessed=1, transcendentals=0),
+        cost_estimate=pl.CostEstimate(
+            flops=2 * rows * heads * DH * DH, bytes_accessed=4 * rows * heads * DH, transcendentals=0
+        ),
     )(scalars(part), key_input, value_input)
 
 
@@ -213,6 +216,7 @@
         scalars(0),
         [queries, key_input, value_input],
         [jax.ShapeDtypeStruct((queries.shape[0], heads * DH), jnp.float32)],
+        3 * queries.shape[0] ** 2 * heads * DH,
     )[0]
 
 
@@ -267,6 +271,7 @@
             jax.ShapeDtypeStruct((rows, width), jnp.bfloat16),
             jax.ShapeDtypeStruct((len(order), rows // len(order)), jnp.float32),
         ],
+        4 * rows * width * DH,
     )
 
 
@@ -275,12 +280,11 @@
     weight_refs = refs[n_rows : n_rows + sum(choices)]
     sent_ref, kept_ref = refs[n_rows + sum(choices) :]
     half = sent_ref.shape[0]
-    width = weight_refs[0].shape[1]
 
     def products(index, weight_ref):
-        for position, (rows, weight) in enumerate(jobs):
+        for rows, weight, first in jobs:
             if weight == index:
-                columns = pl.ds(position * width, width)
+                columns = pl.ds(first, weight_ref.shape[1])
                 product = jnp.dot(
                     rows_refs[rows][...], weight_ref[...], preferred_element_type=jnp.float32
                 )
@@ -301,12 +305,18 @@
 def project(jobs, rows_list, weights, flag):
     flat = [choice for weight in weights for choice in weight]
     choices = tuple(len(weight) for weight in weights)
-    shape = (rows_list[0].shape[0] // 2, flat[0].shape[1] * len(jobs))
+    placed_jobs, total = [], 0
+    for rows, weight in jobs:
+        placed_jobs.append((rows, weight, total))
+        total += weights[weight][0].shape[1]
+    height, depth = rows_list[0].shape
+    shape = (height // 2, total)
     return local_call(
-        functools.partial(project_kernel, tuple(jobs), len(rows_list), choices),
+        functools.partial(project_kernel, tuple(placed_jobs), len(rows_list), choices),
         flag,
         [*rows_list, *flat],
         [jax.ShapeDtypeStruct(shape, jnp.bfloat16), jax.ShapeDtypeStruct(shape, jnp.float32)],
+        2 * height * depth * total,
     )
 
 
@@ -338,61 +348,62 @@
     return jnp.transpose(jnp.broadcast_to(row, (row.shape[1], row.shape[1])))
 
 
-def scaled_parts(counts, cut, squares_ref, pieces, total_width):
+def scaled_parts(widths, starts_ref, squares_ref, pieces, total_width):
     scale = lax.rsqrt(column(squares_ref[...]) / total_width + epsilon)
-    for piece, count in zip(pieces, counts):
-        for index in range(count):
-            for first in range(index * cut, (index + 1) * cut, DH):
-                yield piece[:, pl.ds(first, DH)].astype(jnp.float32) * scale
-
-
-def placed_kernel(counts, cut, total_width, starts_ref, squares_ref, *refs):
+    where = 0
+    for piece, own in zip(pieces, widths):
+        first = 0
+        for width in own:
+            for at in range(0, width, DH):
+                part = piece[:, pl.ds(first + at, DH)].astype(jnp.float32) * scale
+                yield part, pl.multiple_of(starts_ref[where] + at, DH)
+            first += width
+            where += 1
+
+
+def placed_kernel(widths, total_width, starts_ref, squares_ref, *refs):
     out_ref = refs[-1]
-    steps = cut // DH
-    for at, part in enumerate(scaled_parts(counts, cut, squares_ref, refs[:-1], total_width)):
-        start = pl.multiple_of(starts_ref[at // steps] + at % steps * DH, DH)
+    for part, start in scaled_parts(widths, starts_ref, squares_ref, refs[:-1], total_width):
         out_ref[:, pl.ds(start, DH)] = part.astype(out_ref.dtype)
 
 
-def added_kernel(counts, cut, total_width, starts_ref, squares_ref, *refs):
-    pieces = refs[: len(counts)]
+def added_kernel(widths, total_width, starts_ref, squares_ref, *refs):
     out_ref, buf, sem = refs[-3:]
-    steps = cut // DH
     copies = []
-    for at, part in enumerate(scaled_parts(counts, cut, squares_ref, pieces, total_width)):
-        where = at // steps
-        buf[where, :, pl.ds(at % steps * DH, DH)] = part.astype(out_ref.dtype)
-        if at % steps == steps - 1:
-            start = pl.multiple_of(starts_ref[where], DH)
-            copy = pltpu.make_async_copy(buf.at[where], out_ref.at[:, pl.ds(start, cut)], sem.at[where])
-            copy.start()
-            copies.append(copy)
+    parts = scaled_parts(widths, starts_ref, squares_ref, refs[: len(widths)], total_width)
+    for at, (part, start) in enumerate(parts):
+        buf[at] = part.astype(out_ref.dtype)
+        copies.append(pltpu.make_async_copy(buf.at[at], out_ref.at[:, pl.ds(start, DH)], sem.at[at]))
+        copies[-1].start()
     for copy in copies:
         copy.wait()
 
 
-def placed(filled, pieces, squares, cut, shape, total_width):
-    counts = tuple(len(starts) for _, starts in pieces)
-    starts = scalars(*[start for _, own in pieces for start in own])
-    operands = [squares] + [piece for piece, _ in pieces]
+def placed(filled, pieces, squares, shape, total_width):
+    widths = tuple(tuple(own) for _, _, own in pieces)
+    starts = scalars(*[start for _, own, _ in pieces for start in own])
+    operands = [squares] + [piece for piece, _, _ in pieces]
     out_shape = jax.ShapeDtypeStruct(shape, jnp.bfloat16)
+    columns = sum(sum(own) for own in widths)
     if filled is None:
-        kernel = functools.partial(placed_kernel, counts, cut, total_width)
+        kernel = functools.partial(placed_kernel, widths, total_width)
         return local_call(kernel, starts, operands, [out_shape])[0]
     return pl.pallas_call(
-        functools.partial(added_kernel, counts, cut, total_width),
+        functools.partial(added_kernel, widths, total_width),
         in_specs=[pl.BlockSpec(memory_space=pltpu.SMEM)]
         + [pl.BlockSpec(memory_space=pltpu.VMEM)] * len(operands)
         + [pl.BlockSpec(memory_space=pl.ANY)],
         out_specs=pl.BlockSpec(memory_space=pl.ANY),
         out_shape=out_shape,
         scratch_shapes=[
-            pltpu.VMEM((sum(counts), shape[0], cut), jnp.bfloat16),
-            pltpu.SemaphoreType.DMA((sum(counts),)),
+            pltpu.VMEM((columns // DH, shape[0], DH), jnp.bfloat16),
+            pltpu.SemaphoreType.DMA((columns // DH,)),
         ],
         input_output_aliases={len(operands) + 1: 0},
         compiler_params=pltpu.CompilerParams(vmem_limit_bytes=VMEM_BYTES),
-        cost_estimate=pl.CostEstimate(flops=1, bytes_accessed=1, transcendentals=0),
+        cost_estimate=pl.CostEstimate(
+            flops=0, bytes_accessed=4 * shape[0] * columns, transcendentals=0
+        ),
     )(starts, *operands, filled)
 
 
@@ -412,26 +423,22 @@
     def along(value, hops):
         return lax.ppermute(value, "seq", line_pairs(n_seq, hops))
 
-    w_cuts = [cut_columns(out_weight, k * cut, cut) for k in range(cuts)]
-    w_pair = [along(w_cuts[0], SWAP_OUTER)]
-    w_mid1 = [along(w_cuts[0], SWAP_MIDDLE)]
-    terms, stepped = state_prefix(key_input, value_input, n_seq, place, [w_pair[0], w_mid1[0]])
+    w_mid1 = along(out_weight, SWAP_MIDDLE)
+    w_pair = along(out_weight, SWAP_OUTER)
+    terms, stepped = state_prefix(key_input, value_input, n_seq, place, [w_mid1, w_pair])
     some = heads // 2
     inners = [
         causal_part(queries, key_input, value_input, 0, some),
         causal_part(queries, key_input, value_input, some, heads - some),
     ]
 
-    for k in range(1, cuts):
-        w_pair.append(along(hold(w_cuts[k], stepped), SWAP_OUTER))
-        w_mid1.append(along(hold(w_cuts[k], stepped), SWAP_MIDDLE))
-    w_mid2 = [along(hold(w_pair[k], stepped), SWAP_MIDDLE) for k in range(cuts)]
-    w_end1 = [along(hold(w_mid1[k], stepped), TO_ENDS) for k in range(cuts)]
-    w_end2 = [along(w_mid2[k], TO_ENDS) for k in range(cuts)]
+    w_end1 = along(hold(w_mid1, stepped), TO_ENDS)
+    w_cuts = [cut_columns(w_pair, k * cut, cut) for k in range(cuts)]
+    w_mid2 = [along(hold(w_cut, stepped), SWAP_MIDDLE) for w_cut in w_cuts]
+    w_end2 = [along(w, TO_ENDS) for w in w_mid2]
 
     bits = n_head.bit_length() - 1
     order = [int(format(j, "b").zfill(bits)[::-1], 2) for j in range(n_head)] if bits else [0]
-    terms[0] = hold(terms[0], *w_pair[1:], *w_mid1[1:])
     hidden, squares = gated_hidden(
         queries, inners, kv_state, terms, gate_input, norm_gain, h, i, order
     )
@@ -450,83 +457,74 @@
 
     rows_list = [hidden] + others
 
-    def summed(flag, parts):
-        blocks = sorted({block for _, own in parts for block in own})
-        turns = [turn for turn, _ in parts]
-        jobs = [(p, blocks.index(block)) for p, (_, own) in enumerate(parts) for block in own]
-        sent, kept = project(
-            jobs, [rows_list[turn] for turn in turns], [weights[block] for block in blocks], flag
-        )
-        sent_first = sent
-        widths = [cut * len(own) for _, own in parts]
-        bit, steps = 1, []
+    owners = [z, z ^ 1, jnp.where(low, 2, 1), jnp.where(low, 3, 0)]
+    blocks = {"own": [(out_weight,)], "pair": [(w_pair,)], "third": [(w_mid1, w_end1)]}
+    blocks["last"] = list(zip(w_mid2, w_end2))
+    places = {name: owners[k] for k, name in enumerate(blocks)}
+
+    def summed(parts, pins, pin_end=None):
+        weights, jobs, widths, starts = [], [], [], []
+        for p, (turn, own) in enumerate(parts):
+            member = (i + turn) % inner
+            widths.append([])
+            starts.append([])
+            for name, first, last in own:
+                for k in range(first, last):
+                    weight = blocks[name][k]
+                    known = [n for n, other in enumerate(weights) if other[0] is weight[0]]
+                    if not known:
+                        weights.append(weight)
+                    jobs.append((p, known[0] if known else len(weights) - 1))
+                    size = weight[0].shape[1]
+                    widths[-1].append(size)
+                    starts[-1].append((places[name] * inner + member) * width + k * size)
+        sent, kept = project(jobs, [rows_list[turn] for turn, _ in parts], weights, hold(flag, *pins))
+        first_sent, steps, bit = sent, [], 1
         while bit < n_head:
             steps.append(lax.ppermute(sent, "head", flip_pairs(n_head, bit)))
             bit *= 2
             if bit < n_head:
                 sent, kept = fold(kept, steps[-1])
             else:
-                kept = fold(kept, steps[-1], widths)
+                got = steps[-1] if pin_end is None else hold(steps[-1], pin_end)
+                kept = fold(kept, got, [sum(own) for own in widths])
         pieces = []
-        for piece, (turn, own) in zip(kept, parts):
+        for piece, (turn, _), own_starts, own_widths in zip(kept, parts, starts, widths):
             if turn:
                 piece = lax.ppermute(piece, "seq", turn_pairs(n_seq, -turn))
-            starts = [
-                (owners[block] * inner + (i + turn) % inner) * width + k * cut for block, k in own
-            ]
-            pieces.append((piece, starts))
-        return pieces, sent_first, steps
-
-    owners = [z, z ^ 1, jnp.where(low, 2, 1), jnp.where(low, 3, 0)]
-    weights = {}
-    for k in range(cuts):
-        weights[0, k] = (w_cuts[k],)
-        weights[1, k] = (w_pair[k],)
-        weights[2, k] = (w_mid1[k], w_end1[k])
-        weights[3, k] = (w_mid2[k], w_end2[k])
+            pieces.append((piece, own_starts, own_widths))
+        return pieces, first_sent, steps
+
     turns = list(range(inner))
-    pieces = []
-
-    def group(members, block, pins):
-        more, sent, steps = summed(
-            hold(flag, *pins), [(turn, [(block, k) for k in range(cuts)]) for turn in members]
-        )
-        pieces.extend(more)
-        return sent, steps
-
     shape = (out_rows, width * n_seq)
     in_kernel = cut % DH == 0 and out_rows == DH
-
-    pins = [w_end1[0], w_mid2[0]]
-    sent, steps_own = group(turns[:1], 0, pins)
-    sent, steps_pair = group(turns[:1], 1, [sent])
-    steps_other = []
-    for block in (0, 1) if inner > 1 else ():
-        sent, steps = group(turns[1:], block, [sent, squares])
-        steps_other += steps
-    sent, steps_third = group(turns[:1], 2, [sent, *w_end1, *w_mid2, *steps_own, *steps_pair])
-    if inner > 1:
-        sent, steps = group(turns[1:], 2, [sent])
-        steps_third += steps
-    pins = [sent, *steps_other]
+    ahead = [("own", 0, 1), ("pair", 0, 1)]
+
+    pieces, sent, steps_own = summed([(0, ahead + [("third", 0, 1)])], [w_end1, *w_mid2])
+    pins = [sent, squares, w_end2[0]]
+    for some in (ahead, [("third", 0, 1)]) if inner > 1 else ():
+        more, sent, steps = summed([(turn, some) for turn in turns[1:]], pins)
+        pieces += more
+        pins = [sent]
+    pins += steps_own
     filled = None
     for k in range(cuts):
         if k + 1 == cuts and in_kernel:
-            filled = placed(None, pieces, squares, cut, shape, total_width)
-            pins = [filled]
-        last, sent, steps = summed(hold(flag, *pins), [(turn, [(3, k)]) for turn in turns])
+            filled = placed(None, pieces, squares, shape, total_width)
+        last, sent, _ = summed([(turn, [("last", k, k + 1)]) for turn in turns], pins, filled)
+        pins = [sent]
         if k + 1 < cuts:
             pieces += last
-            pins = [sent]
     if in_kernel:
-        return placed(filled, last, squares, cut, shape, total_width)
+        return placed(filled, last, squares, shape, total_width)
     scale = lax.rsqrt(squares.reshape(out_rows, 1) / total_width + epsilon)
     output = jnp.zeros(shape, jnp.bfloat16)
-    for piece, starts in pieces + last:
+    for piece, starts, widths in pieces + last:
         piece = (piece.astype(jnp.float32) * scale).astype(jnp.bfloat16)
-        for index, start in enumerate(starts):
-            part = piece[:, index * cut : (index + 1) * cut]
-            output = lax.dynamic_update_slice_in_dim(output, part, start, 1)
+        first = 0
+        for start, size in zip(starts, widths):
+            output = lax.dynamic_update_slice_in_dim(output, piece[:, first : first + size], start, 1)
+            first += size
     return output
 
 

time: 140 us -> 143 us (1.021)
  waiting for transfers between devices: 42.9 us -> 68.8 us
  local copies, waits for them, and re-layouts: 18 us -> 6.74 us
  starting transfers between devices: 47.4 us -> 38.3 us
  Pallas kernels: 29.8 us -> 27.9 us
    ppermute x10 -> x7, waiting for transfers between devices: 19.6 us -> 35.9 us  [along(): return lax.ppermute(value, 'seq', line_pairs(n_seq, hops))]
    unnamed x68 -> x32, local copies, waits for them, and re-layouts: 17.9 us -> 6.64 us
    ppermute x1, waiting for transfers between devices: 2.5 us -> 9.63 us  [state_prefix(): from_left = lax.ppermute(first, 'seq', line_pairs(n_seq, [(0, 1), (2, 3)]))]
    ppermute x10 -> x7, starting transfers between devices: 17.5 us -> 11.4 us  [along(): return lax.ppermute(value, 'seq', line_pairs(n_seq, hops))]
    pallas_call x31 -> x22, Pallas kernels: 25 us -> 20.3 us  [local_call(): pl.pallas_call(kernel, in_specs=[pl.BlockSpec(memory_space=pltpu.SMEM)] +...]
    ppermute x16 -> x10, waiting for transfers between devices: 14.1 us -> 9.41 us  [summed(): steps.append(lax.ppermute(sent, 'head', flip_pairs(n_head, bit)))]
    ppermute x16 -> x10, starting transfers between devices: 11 us -> 6.45 us  [summed(): steps.append(lax.ppermute(sent, 'head', flip_pairs(n_head, bit)))]
    pallas_call x2, Pallas kernels: 0.87 us -> 3.73 us  [cut_columns(): pl.pallas_call(functools.partial(cut_kernel, first), in_specs=[pl.BlockSp...]
  transfers between devices with their start and end apart: 39 -> 29, of which waited for: 15 -> 13; matrix products, arithmetic and copies ran while one was open for 0% -> 0% of each run, Pallas kernels for 17% -> 17%
where the time goes in v7:
time: 143 us; the launch traced here: 142 us
  waiting for transfers between devices  68.8 us (48%)
  starting transfers between devices  38.3 us (27%)
  Pallas kernels  27.9 us (20%)
  local copies, waits for them, and re-layouts  6.74 us (5%)
    ppermute x7, waiting for transfers between devices, along(): return lax.ppermute(value, 'seq', line_pairs(n_seq, hops))  35.9 us
    pallas_call x22, Pallas kernels, local_call(): pl.pallas_call(kernel, in_specs=[pl.BlockSpec(memory_space=pltpu.SMEM)] +...  20.3 us
    ppermute x7, starting transfers between devices, along(): return lax.ppermute(value, 'seq', line_pairs(n_seq, hops))  11.4 us
    ppermute x1, waiting for transfers between devices, state_prefix(): from_left = lax.ppermute(first, 'seq', line_pairs(n_seq, [(0, 1), (2, 3)]))  9.63 us
    ppermute x10, waiting for transfers between devices, summed(): steps.append(lax.ppermute(sent, 'head', flip_pairs(n_head, bit)))  9.41 us
    unnamed x32, local copies, waits for them, and re-layouts  6.64 us
    ppermute x4, waiting for transfers between devices, summed(): piece = lax.ppermute(piece, 'seq', turn_pairs(n_seq, -turn))  6.52 us
    ppermute x10, starting transfers between devices, summed(): steps.append(lax.ppermute(sent, 'head', flip_pairs(n_head, bit)))  6.45 us
  transfers between devices with their start and end apart: 29, of which 13 were waited for; matrix products, arithmetic and copies ran while one was open for 0% of the time, Pallas kernels for 17%

profile of v7, /device:TPU:0, one launch (start us, length us, event | category | flops | bytes accessed | tf_op | source)
XLA Modules:
  0.0 142.3 jit_solution(3304021946799011997)
XLA Ops:
  0.0 3.0 %collective-permute-start.3 = (bf16[1024,512]{1,0:T(8,128)(2,1)}, bf16[1024,512]{1,0:T(8,128)(2,1)}, u32[]{:S(2)}, u32[]{:S(2)}) collective-permute-start(bf16[1024,512]{1,0:T(8,128)(2,1)} %refs_1_.3), channel_id=1, source_target_pairs={{0,8},{4,12},{8,0},{12,4},{16,24},{20,28},{24,16},{28,20},{1,9},{5... | collective-permute-start | bytes 3145736 | tf_op jit(solution)/shard_map/ppermute | solution.py:424
  3.0 1.6 %collective-permute-start.2 = (bf16[1024,512]{1,0:T(8,128)(2,1)}, bf16[1024,512]{1,0:T(8,128)(2,1)}, u32[]{:S(2)}, u32[]{:S(2)}) collective-permute-start(bf16[1024,512]{1,0:T(8,128)(2,1)} %refs_1_.3), channel_id=1, source_target_pairs={{8,16},{12,20},{16,8},{20,12},{9,17},{13,21},{17,9},{21,13},{10,18... | collective-permute-start | bytes 3145736 | tf_op jit(solution)/shard_map/ppermute | solution.py:424
  4.7 1.2 copy-done
  5.9 1.2 copy-done.2
  7.1 1.3 shard_map.74
  8.4 1.6 %collective-permute-start = (bf16[4,128,128]{2,1,0:T(8,128)(2,1)S(1)}, bf16[4,128,128]{2,1,0:T(8,128)(2,1)S(1)}, u32[]{:S(2)}, u32[]{:S(2)}) collective-permute-start(bf16[4,128,128]{2,1,0:T(8,128)(2,1)S(1)} %shard_map.74), channel_id=1, source_target_pairs={{0,4},{4,0},{8,12},{12,8},{16,20},{20,16},{24,28},{28,24},{1,5},{5... | collective-permute-start | bytes 393224 | tf_op jit(solution)/shard_map/ppermute | solution.py:165
  10.0 1.3 shard_map.73.refs_0_.refs_3_
  11.3 2.2 %collective-permute-done.refs_1_.refs_4_ = bf16[4,128,128]{2,1,0:T(8,128)(2,1)S(1)} collective-permute-done((bf16[4,128,128]{2,1,0:T(8,128)(2,1)S(1)}, bf16[4,128,128]{2,1,0:T(8,128)(2,1)S(1)}, u32[]{:S(2)}, u32[]{:S(2)}) %collective-permute-start) | collective-permute-done | bytes 131104 | tf_op jit(solution)/shard_map/ppermute | solution.py:165
  13.5 5.4 %collective-permute-start.1 = (bf16[4,128,128]{2,1,0:T(8,128)(2,1)S(1)}, bf16[4,128,128]{2,1,0:T(8,128)(2,1)S(1)}, u32[]{:S(2)}, u32[]{:S(2)}) collective-permute-start(bf16[4,128,128]{2,1,0:T(8,128)(2,1)S(1)} %shard_map.75), channel_id=1, source_target_pairs={{0,8},{4,12},{16,24},{20,28},{1,9},{5,13},{17,25},{21,29},{2,10},{... | collective-permute-start | bytes 393224 | tf_op jit(solution)/shard_map/ppermute | solution.py:168
  18.8 9.6 %collective-permute-done.1.refs_2_.refs_0_ = bf16[4,128,128]{2,1,0:T(8,128)(2,1)S(1)} collective-permute-done((bf16[4,128,128]{2,1,0:T(8,128)(2,1)S(1)}, bf16[4,128,128]{2,1,0:T(8,128)(2,1)S(1)}, u32[]{:S(2)}, u32[]{:S(2)}) %collective-permute-start.1) | collective-permute-done | bytes 131104 | tf_op jit(solution)/shard_map/ppermute | solution.py:168
  28.5 0.7 shard_map.76
  29.2 0.7 copy-done.6
  29.8 1.3 collective-permute-start.4
  31.1 1.3 collective-permute-start.5
  32.5 0.9 copy-done.7
  33.4 1.1 shard_map.77
  34.6 0.7 copy-done.9
  35.3 0.7 copy-done.14
  35.9 1.3 collective-permute-start.9
  37.3 1.1 shard_map.78.refs_2_
  38.4 1.9 %shard_map.81 = bf16[1024,256]{1,0:T(8,128)(2,1)} custom-call(bf16[1024,512]{1,0:T(8,128)(2,1)} %collective-permute-done.3.w_ref.refs_2_), custom_call_target="tpu_custom_call" | custom-call | bytes 1048576 | tf_op jit(solution)/shard_map/pallas_call | solution.py:93
  40.2 1.8 %shard_map.82 = bf16[1024,256]{1,0:T(8,128)(2,1)} custom-call(bf16[1024,512]{1,0:T(8,128)(2,1)} %collective-permute-done.3.w_ref.refs_2_), custom_call_target="tpu_custom_call" | custom-call | bytes 1048576 | tf_op jit(solution)/shard_map/pallas_call | solution.py:93
  42.1 1.5 %collective-permute-start.10 = (bf16[1024,256]{1,0:T(8,128)(2,1)}, bf16[1024,256]{1,0:T(8,128)(2,1)}, u32[]{:S(2)}, u32[]{:S(2)}) collective-permute-start(bf16[1024,256]{1,0:T(8,128)(2,1)} %shard_map.81), channel_id=1, source_target_pairs={{8,16},{12,20},{16,8},{20,12},{9,17},{13,21},{17,9},{21,13},{10,18... | collective-permute-start | bytes 1572872 | tf_op jit(solution)/shard_map/ppermute | solution.py:424
  43.6 1.4 %collective-permute-start.11 = (bf16[1024,256]{1,0:T(8,128)(2,1)}, bf16[1024,256]{1,0:T(8,128)(2,1)}, u32[]{:S(2)}, u32[]{:S(2)}) collective-permute-start(bf16[1024,256]{1,0:T(8,128)(2,1)} %shard_map.82), channel_id=1, source_target_pairs={{8,16},{12,20},{16,8},{20,12},{9,17},{13,21},{17,9},{21,13},{10,18... | collective-permute-start | bytes 1572872 | tf_op jit(solution)/shard_map/ppermute | solution.py:424
  45.0 1.6 %collective-permute-start.6 = (bf16[4,128,128]{2,1,0:T(8,128)(2,1)S(1)}, bf16[4,128,128]{2,1,0:T(8,128)(2,1)S(1)}, u32[]{:S(2)}, u32[]{:S(2)}) collective-permute-start(bf16[4,128,128]{2,1,0:T(8,128)(2,1)S(1)} %copy-done.15), channel_id=1, source_target_pairs={{0,4},{4,0},{8,12},{12,8},{16,20},{20,16},{24,28},{28,24},{1,5},{5... | collective-permute-start | bytes 393224 | tf_op jit(solution)/shard_map/ppermute | solution.py:179
  46.6 1.1 shard_map.79.refs_3_
  47.8 2.3 %collective-permute-done.6.refs_1_ = bf16[4,128,128]{2,1,0:T(8,128)(2,1)S(1)} collective-permute-done((bf16[4,128,128]{2,1,0:T(8,128)(2,1)S(1)}, bf16[4,128,128]{2,1,0:T(8,128)(2,1)S(1)}, u32[]{:S(2)}, u32[]{:S(2)}) %collective-permute-start.6) | collective-permute-done | bytes 131104 | tf_op jit(solution)/shard_map/ppermute | solution.py:179
  50.1 1.8 %shard_map.80 = (bf16[512,1024]{1,0:T(8,128)(2,1)S(1)}, f32[4,128]{1,0:T(4,128)S(1)}) custom-call(s32[2]{0:T(128)S(1)} %pad_add_fusion.1.place_ref, bf16[512,1024]{1,0:T(8,128)(2,1)S(1)} %copy-done.4, bf16[512,1024]{1,0:T(8,128)(2,1)S(1)} %copy-done.5, f32[32,1,128]{2,1,0:T(1,128)S(1)} %bitcast.18, f32[8,128,128]{2,1,0:T(8,128)S(1)} %copy-done.8, ...), custom_call_target="tpu_custom_call" | custom-call | flops 268435456 | bytes 6178816 | tf_op jit(solution)/shard_map/pallas_call | solution.py:48
  51.8 1.6 %collective-permute-start.13 = (bf16[512,1024]{1,0:T(8,128)(2,1)S(1)}, bf16[512,1024]{1,0:T(8,128)(2,1)S(1)}, u32[]{:S(2)}, u32[]{:S(2)}) collective-permute-start(bf16[512,1024]{1,0:T(8,128)(2,1)S(1)} %get-tuple-element.51.refs_0_), channel_id=1, source_target_pairs={{0,4},{4,0},{8,12},{12,8},{16,20},{20,16},{24,28},{28,24},{1,5},{5... | collective-permute-start | bytes 3145736 | tf_op jit(solution)/shard_map/ppermute | solution.py:445
  53.4 15.2 %collective-permute-done.9.refs_4_.refs_2_ = bf16[1024,512]{1,0:T(8,128)(2,1)} collective-permute-done((bf16[1024,512]{1,0:T(8,128)(2,1)}, bf16[1024,512]{1,0:T(8,128)(2,1)}, u32[]{:S(2)}, u32[]{:S(2)}) %collective-permute-start.9) | collective-permute-done | bytes 1048608 | tf_op jit(solution)/shard_map/ppermute | solution.py:424
  68.6 1.2 copy-done.12
  69.8 3.9 %shard_map.83 = (bf16[256,1536]{1,0:T(8,128)(2,1)S(1)}, f32[256,1536]{1,0:T(8,128)S(1)}) custom-call(s32[1]{0:T(128)} %bitcast.9.flag_ref, bf16[512,1024]{1,0:T(8,128)(2,1)S(1)} %get-tuple-element.51.refs_0_, bf16[1024,512]{1,0:T(8,128)(2,1)S(1)} %copy-done.12, bf16[1024,512]{1,0:T(8,128)(2,1)} %collective-permute-done.3.w_ref.refs_2_, ...), custom_call_target="tpu_custom_call" | custom-call | flops 1610612736 | bytes 7602176 | tf_op jit(solution)/shard_map/pallas_call | solution.py:48
  73.8 1.3 collective-permute-start.12
  75.1 0.6 collective-permute-start.7
  75.6 0.8 collective-permute-done.7
  76.5 1.5 %collective-permute-start.8 = (f32[1,128]{1,0:T(1,128)S(1)}, f32[1,128]{1,0:T(1,128)S(1)}, u32[]{:S(2)}, u32[]{:S(2)}) collective-permute-start(f32[1,128]{1,0:T(1,128)S(1)} %slice.15), channel_id=1, source_target_pairs={{0,2},{1,3},{2,0},{3,1},{4,6},{5,7},{6,4},{7,5},{8,10},{9,11},{10,... | collective-permute-start | bytes 1544 | tf_op jit(solution)/shard_map/ppermute | solution.py:450
  78.0 2.0 %collective-permute-done.8 = f32[1,128]{1,0:T(1,128)S(1)} collective-permute-done((f32[1,128]{1,0:T(1,128)S(1)}, f32[1,128]{1,0:T(1,128)S(1)}, u32[]{:S(2)}, u32[]{:S(2)}) %collective-permute-start.8) | collective-permute-done | bytes 544 | tf_op jit(solution)/shard_map/ppermute | solution.py:450
  80.0 19.6 %collective-permute-done.12.refs_3_ = bf16[1024,256]{1,0:T(8,128)(2,1)S(1)} collective-permute-done((bf16[1024,256]{1,0:T(8,128)(2,1)}, bf16[1024,256]{1,0:T(8,128)(2,1)S(1)}, u32[]{:S(2)}, u32[]{:S(2)}) %collective-permute-start.12) | collective-permute-done | bytes 524320 | tf_op jit(solution)/shard_map/ppermute | solution.py:424
  99.6 2.5 %shard_map.84 = (bf16[256,1024]{1,0:T(8,128)(2,1)S(1)}, f32[256,1024]{1,0:T(8,128)S(1)}) custom-call(s32[1]{0:T(128)} %bitcast.9.flag_ref, bf16[512,1024]{1,0:T(8,128)(2,1)S(1)} %collective-permute-done.13.refs_0_.refs_1_, bf16[1024,512]{1,0:T(8,128)(2,1)S(1)} %copy-done.13, bf16[1024,512]{1,0:T(8,128)(2,1)} %collective-permute-done.3.w_ref.refs_2_), custom_call_target="tpu_custom_call" | custom-call | flops 1073741824 | bytes 4718592 | tf_op jit(solution)/shard_map/pallas_call | solution.py:48
  102.1 1.3 collective-permute-start.16
  103.4 0.1 shard_map.86
  103.6 1.6 %collective-permute-start.15 = (bf16[128,1536]{1,0:T(8,128)(2,1)S(1)}, bf16[128,1536]{1,0:T(8,128)(2,1)S(1)}, u32[]{:S(2)}, u32[]{:S(2)}) collective-permute-start(bf16[128,1536]{1,0:T(8,128)(2,1)S(1)} %get-tuple-element.58), channel_id=1, source_target_pairs={{0,2},{1,3},{2,0},{3,1},{4,6},{5,7},{6,4},{7,5},{8,10},{9,11},{10,... | collective-permute-start | bytes 1179656 | tf_op jit(solution)/shard_map/ppermute | solution.py:484
  105.2 2.2 %shard_map.85 = (bf16[256,512]{1,0:T(8,128)(2,1)S(1)}, f32[256,512]{1,0:T(8,128)S(1)}) custom-call(s32[1]{0:T(128)} %bitcast.9.flag_ref, bf16[512,1024]{1,0:T(8,128)(2,1)S(1)} %collective-permute-done.13.refs_0_.refs_1_, bf16[1024,512]{1,0:T(8,128)(2,1)} %collective-permute-done.2.refs_3_.refs_1_, bf16[1024,512]{1,0:T(8,128)(2,1)} %collective-permute-done.9.refs_4_.refs_2_), custom_call_target="tpu_custom_call" | custom-call | flops 536870912 | bytes 3932160 | tf_op jit(solution)/shard_map/pallas_call | solution.py:48
  107.4 0.3 collective-permute-start.22
  107.7 0.1 shard_map.91
  107.8 0.6 collective-permute-start.20
  108.3 7.2 %collective-permute-done.15.got_ref = bf16[128,1536]{1,0:T(8,128)(2,1)S(1)} collective-permute-done((bf16[128,1536]{1,0:T(8,128)(2,1)S(1)}, bf16[128,1536]{1,0:T(8,128)(2,1)S(1)}, u32[]{:S(2)}, u32[]{:S(2)}) %collective-permute-start.15) | collective-permute-done | bytes 393248 | tf_op jit(solution)/shard_map/ppermute | solution.py:484
  115.6 1.7 %shard_map.87 = (bf16[256,512]{1,0:T(8,128)(2,1)S(1)}, f32[256,512]{1,0:T(8,128)S(1)}) custom-call(s32[1]{0:T(128)} %bitcast.9.flag_ref, bf16[512,1024]{1,0:T(8,128)(2,1)S(1)} %get-tuple-element.51.refs_0_, bf16[512,1024]{1,0:T(8,128)(2,1)S(1)} %collective-permute-done.13.refs_0_.refs_1_, bf16[1024,256]{1,0:T(8,128)(2,1)} %collective-permute-done.10.refs_2_, ...), custom_call_target="tpu_custom_call" | custom-call | flops 536870912 | bytes 3932160 | tf_op jit(solution)/shard_map/pallas_call | solution.py:48
  117.4 1.2 collective-permute-done.16.refs_3_
  118.5 1.7 %shard_map.88 = (bf16[256,512]{1,0:T(8,128)(2,1)S(1)}, f32[256,512]{1,0:T(8,128)S(1)}) custom-call(s32[1]{0:T(128)} %bitcast.9.flag_ref, bf16[512,1024]{1,0:T(8,128)(2,1)S(1)} %get-tuple-element.51.refs_0_, bf16[512,1024]{1,0:T(8,128)(2,1)S(1)} %collective-permute-done.13.refs_0_.refs_1_, bf16[1024,256]{1,0:T(8,128)(2,1)} %collective-permute-done.11.refs_2_, ...), custom_call_target="tpu_custom_call" | custom-call | flops 536870912 | bytes 3932160 | tf_op jit(solution)/shard_map/pallas_call | solution.py:48
  120.4 1.6 %collective-permute-start.23 = (bf16[128,512]{1,0:T(8,128)(2,1)S(1)}, bf16[128,512]{1,0:T(8,128)(2,1)S(1)}, u32[]{:S(2)}, u32[]{:S(2)}) collective-permute-start(bf16[128,512]{1,0:T(8,128)(2,1)S(1)} %get-tuple-element.72), channel_id=1, source_target_pairs={{0,2},{1,3},{2,0},{3,1},{4,6},{5,7},{6,4},{7,5},{8,10},{9,11},{10,... | collective-permute-start | bytes 393224 | tf_op jit(solution)/shard_map/ppermute | solution.py:484
  122.1 1.6 %collective-permute-start.21 = (bf16[128,1024]{1,0:T(8,128)(2,1)S(1)}, bf16[128,1024]{1,0:T(8,128)(2,1)S(1)}, u32[]{:S(2)}, u32[]{:S(2)}) collective-permute-start(bf16[128,1024]{1,0:T(8,128)(2,1)S(1)} %shard_map.92), channel_id=1, source_target_pairs={{0,4},{4,0},{8,12},{12,8},{16,20},{20,16},{24,28},{28,24},{1,5},{5... | collective-permute-start | bytes 786440 | tf_op jit(solution)/shard_map/ppermute | solution.py:494
  123.7 0.6 collective-permute-start.26
  124.3 2.2 %collective-permute-done.23.got_ref = bf16[128,512]{1,0:T(8,128)(2,1)S(1)} collective-permute-done((bf16[128,512]{1,0:T(8,128)(2,1)S(1)}, bf16[128,512]{1,0:T(8,128)(2,1)S(1)}, u32[]{:S(2)}, u32[]{:S(2)}) %collective-permute-start.23) | collective-permute-done | bytes 131104 | tf_op jit(solution)/shard_map/ppermute | solution.py:484
  126.5 1.9 %collective-permute-start.24 = (bf16[128,512]{1,0:T(8,128)(2,1)S(1)}, bf16[128,512]{1,0:T(8,128)(2,1)S(1)}, u32[]{:S(2)}, u32[]{:S(2)}) collective-permute-start(bf16[128,512]{1,0:T(8,128)(2,1)S(1)} %shard_map.94), channel_id=1, source_target_pairs={{0,4},{4,0},{8,12},{12,8},{16,20},{20,16},{24,28},{28,24},{1,5},{5... | collective-permute-start | bytes 393224 | tf_op jit(solution)/shard_map/ppermute | solution.py:494
  128.4 1.6 %collective-permute-start.18 = (bf16[128,512]{1,0:T(8,128)(2,1)S(1)}, bf16[128,512]{1,0:T(8,128)(2,1)S(1)}, u32[]{:S(2)}, u32[]{:S(2)}) collective-permute-start(bf16[128,512]{1,0:T(8,128)(2,1)S(1)} %get-tuple-element.65), channel_id=1, source_target_pairs={{0,2},{1,3},{2,0},{3,1},{4,6},{5,7},{6,4},{7,5},{8,10},{9,11},{10,... | collective-permute-start | bytes 393224 | tf_op jit(solution)/shard_map/ppermute | solution.py:484
  130.1 0.7 collective-permute-start.27
  130.8 0.1 stack.94.starts_ref
  130.9 3.1 %collective-permute-done.24.refs_2_ = bf16[128,512]{1,0:T(8,128)(2,1)S(1)} collective-permute-done((bf16[128,512]{1,0:T(8,128)(2,1)S(1)}, bf16[128,512]{1,0:T(8,128)(2,1)S(1)}, u32[]{:S(2)}, u32[]{:S(2)}) %collective-permute-start.24) | collective-permute-done | bytes 131104 | tf_op jit(solution)/shard_map/ppermute | solution.py:494
  134.1 0.7 collective-permute-done.27.refs_4_
  134.8 1.8 %shard_map.97.refs_2_ = bf16[128,4096]{1,0:T(8,128)(2,1)} custom-call(s32[8]{0:T(128)S(1)} %stack.94.starts_ref, f32[1,128]{1,0:T(1,128)S(1)} %slice_add_fusion.1.squares_ref, bf16[128,1536]{1,0:T(8,128)(2,1)S(1)} %shard_map.90.refs_0_, bf16[128,1024]{1,0:T(8,128)(2,1)S(1)} %collective-permute-done.21.refs_1_, ...), custom_call_target="tpu_custom_call" | custom-call | bytes 1966592 | tf_op jit(solution)/shard_map/pallas_call | solution.py:48
  136.7 1.6 %collective-permute-start.28 = (bf16[128,256]{1,0:T(8,128)(2,1)S(1)}, bf16[128,256]{1,0:T(8,128)(2,1)S(1)}, u32[]{:S(2)}, u32[]{:S(2)}) collective-permute-start(bf16[128,256]{1,0:T(8,128)(2,1)S(1)} %get-tuple-element.80), channel_id=1, source_target_pairs={{0,4},{4,0},{8,12},{12,8},{16,20},{20,16},{24,28},{28,24},{1,5},{5... | collective-permute-start | bytes 196616 | tf_op jit(solution)/shard_map/ppermute | solution.py:494
  138.3 2.7 %collective-permute-done.28.refs_1_ = bf16[128,256]{1,0:T(8,128)(2,1)S(1)} collective-permute-done((bf16[128,256]{1,0:T(8,128)(2,1)S(1)}, bf16[128,256]{1,0:T(8,128)(2,1)S(1)}, u32[]{:S(2)}, u32[]{:S(2)}) %collective-permute-start.28) | collective-permute-done | bytes 65568 | tf_op jit(solution)/shard_map/ppermute | solution.py:494
  141.0 1.3 shard_map.99
  (61 shorter events, 1.0 us)
Async XLA Ops:
  0.0 28.5 %collective-permute-start.3 = (bf16[1024,512]{1,0:T(8,128)(2,1)}, bf16[1024,512]{1,0:T(8,128)(2,1)}, u32[]{:S(2)}, u32[]{:S(2)}) collective-permute-start(bf16[1024,512]{1,0:T(8,128)(2,1)} %refs_1_.3), channel_id=1, source_target_pairs={{0,8},{4,12},{8,0},{12,4},{16,24},{20,28},{24,16},{28,20},{1,9},{5... | collective-permute-start | bytes 3145736 | tf_op jit(solution)/shard_map/ppermute | solution.py:424
  3.0 25.4 %collective-permute-start.2 = (bf16[1024,512]{1,0:T(8,128)(2,1)}, bf16[1024,512]{1,0:T(8,128)(2,1)}, u32[]{:S(2)}, u32[]{:S(2)}) collective-permute-start(bf16[1024,512]{1,0:T(8,128)(2,1)} %refs_1_.3), channel_id=1, source_target_pairs={{8,16},{12,20},{16,8},{20,12},{9,17},{13,21},{17,9},{21,13},{10,18... | collective-permute-start | bytes 3145736 | tf_op jit(solution)/shard_map/ppermute | solution.py:424
  4.7 1.2 copy-start
  5.9 1.2 copy-start.2
  7.1 2.9 %copy-start.1 = (bf16[512,1024]{1,0:T(8,128)(2,1)S(1)}, bf16[512,1024]{1,0:T(8,128)(2,1)}, u32[]{:S(2)}) copy-start(bf16[512,1024]{1,0:T(8,128)(2,1)} %k_ref.7) | copy-start | bytes 3145732
  8.4 5.0 %collective-permute-start = (bf16[4,128,128]{2,1,0:T(8,128)(2,1)S(1)}, bf16[4,128,128]{2,1,0:T(8,128)(2,1)S(1)}, u32[]{:S(2)}, u32[]{:S(2)}) collective-permute-start(bf16[4,128,128]{2,1,0:T(8,128)(2,1)S(1)} %shard_map.74), channel_id=1, source_target_pairs={{0,4},{4,0},{8,12},{12,8},{16,20},{20,16},{24,28},{28,24},{1,5},{5... | collective-permute-start | bytes 393224 | tf_op jit(solution)/shard_map/ppermute | solution.py:165
  10.0 27.3 %copy-start.4 = (bf16[512,1024]{1,0:T(8,128)(2,1)S(1)}, bf16[512,1024]{1,0:T(8,128)(2,1)}, u32[]{:S(2)}) copy-start(bf16[512,1024]{1,0:T(8,128)(2,1)} %q_ref.5) | copy-start | bytes 3145732
  11.2 26.0 %copy-start.3 = (bf16[512,1024]{1,0:T(8,128)(2,1)S(1)}, bf16[512,1024]{1,0:T(8,128)(2,1)}, u32[]{:S(2)}) copy-start(bf16[512,1024]{1,0:T(8,128)(2,1)} %v_ref.7) | copy-start | bytes 3145732
  13.5 15.0 %collective-permute-start.1 = (bf16[4,128,128]{2,1,0:T(8,128)(2,1)S(1)}, bf16[4,128,128]{2,1,0:T(8,128)(2,1)S(1)}, u32[]{:S(2)}, u32[]{:S(2)}) collective-permute-start(bf16[4,128,128]{2,1,0:T(8,128)(2,1)S(1)} %shard_map.75), channel_id=1, source_target_pairs={{0,8},{4,12},{16,24},{20,28},{1,9},{5,13},{17,25},{21,29},{2,10},{... | collective-permute-start | bytes 393224 | tf_op jit(solution)/shard_map/ppermute | solution.py:168
  29.2 0.7 copy-start.6
  29.8 2.7 %collective-permute-start.4 = (bf16[4,128,128]{2,1,0:T(8,128)(2,1)}, bf16[4,128,128]{2,1,0:T(8,128)(2,1)}, u32[]{:S(2)}, u32[]{:S(2)}) collective-permute-start(bf16[4,128,128]{2,1,0:T(8,128)(2,1)} %shard_map.76), channel_id=1, source_target_pairs={{8,16},{12,20},{9,17},{13,21},{10,18},{14,22},{11,19},{15,23}} | collective-permute-start | bytes 393224 | tf_op jit(solution)/shard_map/ppermute | solution.py:171
  31.1 1.4 collective-permute-start.5
  32.5 0.9 copy-start.7
  34.6 0.7 copy-start.9
  35.3 0.7 copy-start.14
  35.9 32.6 %collective-permute-start.9 = (bf16[1024,512]{1,0:T(8,128)(2,1)}, bf16[1024,512]{1,0:T(8,128)(2,1)}, u32[]{:S(2)}, u32[]{:S(2)}) collective-permute-start(bf16[1024,512]{1,0:T(8,128)(2,1)} %collective-permute-done.2.refs_3_.refs_1_), channel_id=1, source_target_pairs={{8,0},{12,4},{16,24},{20,28},{9,1},{13,5},{17,25},{21,29},{10,2},{... | collective-permute-start | bytes 3145736 | tf_op jit(solution)/shard_map/ppermute | solution.py:424
  38.3 6.7 %copy-start.15 = (bf16[4,128,128]{2,1,0:T(8,128)(2,1)S(1)}, bf16[4,128,128]{2,1,0:T(8,128)(2,1)}, u32[]{:S(2)}) copy-start(bf16[4,128,128]{2,1,0:T(8,128)(2,1)} %copy-done.14) | copy-start | bytes 393220
  42.1 11.3 %collective-permute-start.10 = (bf16[1024,256]{1,0:T(8,128)(2,1)}, bf16[1024,256]{1,0:T(8,128)(2,1)}, u32[]{:S(2)}, u32[]{:S(2)}) collective-permute-start(bf16[1024,256]{1,0:T(8,128)(2,1)} %shard_map.81), channel_id=1, source_target_pairs={{8,16},{12,20},{16,8},{20,12},{9,17},{13,21},{17,9},{21,13},{10,18... | collective-permute-start | bytes 1572872 | tf_op jit(solution)/shard_map/ppermute | solution.py:424
  43.6 9.8 %collective-permute-start.11 = (bf16[1024,256]{1,0:T(8,128)(2,1)}, bf16[1024,256]{1,0:T(8,128)(2,1)}, u32[]{:S(2)}, u32[]{:S(2)}) collective-permute-start(bf16[1024,256]{1,0:T(8,128)(2,1)} %shard_map.82), channel_id=1, source_target_pairs={{8,16},{12,20},{16,8},{20,12},{9,17},{13,21},{17,9},{21,13},{10,18... | collective-permute-start | bytes 1572872 | tf_op jit(solution)/shard_map/ppermute | solution.py:424
  45.0 5.1 %copy-start.5 = (bf16[512,1024]{1,0:T(8,128)(2,1)S(1)}, bf16[512,1024]{1,0:T(8,128)(2,1)}, u32[]{:S(2)}) copy-start(bf16[512,1024]{1,0:T(8,128)(2,1)} %gate_ref.1) | copy-start | bytes 3145732
  45.0 5.1 %copy-start.8 = (f32[8,128,128]{2,1,0:T(8,128)S(1)}, f32[8,128,128]{2,1,0:T(8,128)}, u32[]{:S(2)}) copy-start(f32[8,128,128]{2,1,0:T(8,128)} %kv_ref.1) | copy-start | bytes 1572868
  45.0 5.1 %copy-start.10 = (f32[4,128,128]{2,1,0:T(8,128)S(1)}, f32[4,128,128]{2,1,0:T(8,128)}, u32[]{:S(2)}) copy-start(f32[4,128,128]{2,1,0:T(8,128)} %copy-done.9) | copy-start | bytes 786436
  45.0 5.1 %copy-start.11 = (f32[4096]{0:T(1024)S(1)}, f32[4096]{0:T(1024)}, u32[]{:S(2)}) copy-start(f32[4096]{0:T(1024)} %param.12) | copy-start | bytes 49156
  45.0 5.0 %collective-permute-start.6 = (bf16[4,128,128]{2,1,0:T(8,128)(2,1)S(1)}, bf16[4,128,128]{2,1,0:T(8,128)(2,1)S(1)}, u32[]{:S(2)}, u32[]{:S(2)}) collective-permute-start(bf16[4,128,128]{2,1,0:T(8,128)(2,1)S(1)} %copy-done.15), channel_id=1, source_target_pairs={{0,4},{4,0},{8,12},{12,8},{16,20},{20,16},{24,28},{28,24},{1,5},{5... | collective-permute-start | bytes 393224 | tf_op jit(solution)/shard_map/ppermute | solution.py:179
  51.8 47.7 %collective-permute-start.13 = (bf16[512,1024]{1,0:T(8,128)(2,1)S(1)}, bf16[512,1024]{1,0:T(8,128)(2,1)S(1)}, u32[]{:S(2)}, u32[]{:S(2)}) collective-permute-start(bf16[512,1024]{1,0:T(8,128)(2,1)S(1)} %get-tuple-element.51.refs_0_), channel_id=1, source_target_pairs={{0,4},{4,0},{8,12},{12,8},{16,20},{20,16},{24,28},{28,24},{1,5},{5... | collective-permute-start | bytes 3145736 | tf_op jit(solution)/shard_map/ppermute | solution.py:445
  68.6 1.2 copy-start.12
  69.8 29.8 %copy-start.13 = (bf16[1024,512]{1,0:T(8,128)(2,1)S(1)}, bf16[1024,512]{1,0:T(8,128)(2,1)}, u32[]{:S(2)}) copy-start(bf16[1024,512]{1,0:T(8,128)(2,1)} %refs_1_.3) | copy-start | bytes 3145732
  73.7 29.7 %collective-permute-start.14 = (bf16[256,1536]{1,0:T(8,128)(2,1)S(1)}, bf16[256,1536]{1,0:T(8,128)(2,1)S(1)}, u32[]{:S(2)}, u32[]{:S(2)}) collective-permute-start(bf16[256,1536]{1,0:T(8,128)(2,1)S(1)} %get-tuple-element.52), channel_id=1, source_target_pairs={{0,1},{1,0},{2,3},{3,2},{4,5},{5,4},{6,7},{7,6},{8,9},{9,8},{10,11... | collective-permute-start | bytes 2359304 | tf_op jit(solution)/shard_map/ppermute | solution.py:484
  73.8 25.8 %collective-permute-start.12 = (bf16[1024,256]{1,0:T(8,128)(2,1)}, bf16[1024,256]{1,0:T(8,128)(2,1)S(1)}, u32[]{:S(2)}, u32[]{:S(2)}) collective-permute-start(bf16[1024,256]{1,0:T(8,128)(2,1)} %collective-permute-done.10.refs_2_), channel_id=1, source_target_pairs={{8,0},{12,4},{16,24},{20,28},{9,1},{13,5},{17,25},{21,29},{10,2},{... | collective-permute-start | bytes 1572872 | tf_op jit(solution)/shard_map/ppermute | solution.py:424
  75.1 1.4 collective-permute-start.7
  76.5 3.5 %collective-permute-start.8 = (f32[1,128]{1,0:T(1,128)S(1)}, f32[1,128]{1,0:T(1,128)S(1)}, u32[]{:S(2)}, u32[]{:S(2)}) collective-permute-start(f32[1,128]{1,0:T(1,128)S(1)} %slice.15), channel_id=1, source_target_pairs={{0,2},{1,3},{2,0},{3,1},{4,6},{5,7},{6,4},{7,5},{8,10},{9,11},{10,... | collective-permute-start | bytes 1544 | tf_op jit(solution)/shard_map/ppermute | solution.py:450
  102.0 5.6 %collective-permute-start.19 = (bf16[256,1024]{1,0:T(8,128)(2,1)S(1)}, bf16[256,1024]{1,0:T(8,128)(2,1)S(1)}, u32[]{:S(2)}, u32[]{:S(2)}) collective-permute-start(bf16[256,1024]{1,0:T(8,128)(2,1)S(1)} %get-tuple-element.54), channel_id=1, source_target_pairs={{0,1},{1,0},{2,3},{3,2},{4,5},{5,4},{6,7},{7,6},{8,9},{9,8},{10,11... | collective-permute-start | bytes 1572872 | tf_op jit(solution)/shard_map/ppermute | solution.py:484
  102.1 16.4 %collective-permute-start.16 = (bf16[1024,256]{1,0:T(8,128)(2,1)}, bf16[1024,256]{1,0:T(8,128)(2,1)S(1)}, u32[]{:S(2)}, u32[]{:S(2)}) collective-permute-start(bf16[1024,256]{1,0:T(8,128)(2,1)} %collective-permute-done.11.refs_2_), channel_id=1, source_target_pairs={{8,0},{12,4},{16,24},{20,28},{9,1},{13,5},{17,25},{21,29},{10,2},{... | collective-permute-start | bytes 1572872 | tf_op jit(solution)/shard_map/ppermute | solution.py:424
  103.6 12.0 %collective-permute-start.15 = (bf16[128,1536]{1,0:T(8,128)(2,1)S(1)}, bf16[128,1536]{1,0:T(8,128)(2,1)S(1)}, u32[]{:S(2)}, u32[]{:S(2)}) collective-permute-start(bf16[128,1536]{1,0:T(8,128)(2,1)S(1)} %get-tuple-element.58), channel_id=1, source_target_pairs={{0,2},{1,3},{2,0},{3,1},{4,6},{5,7},{6,4},{7,5},{8,10},{9,11},{10,... | collective-permute-start | bytes 1179656 | tf_op jit(solution)/shard_map/ppermute | solution.py:484
  107.4 13.0 %collective-permute-start.22 = (bf16[256,512]{1,0:T(8,128)(2,1)S(1)}, bf16[256,512]{1,0:T(8,128)(2,1)S(1)}, u32[]{:S(2)}, u32[]{:S(2)}) collective-permute-start(bf16[256,512]{1,0:T(8,128)(2,1)S(1)} %get-tuple-element.56), channel_id=1, source_target_pairs={{0,1},{1,0},{2,3},{3,2},{4,5},{5,4},{6,7},{7,6},{8,9},{9,8},{10,11... | collective-permute-start | bytes 786440 | tf_op jit(solution)/shard_map/ppermute | solution.py:484
  107.8 14.2 %collective-permute-start.20 = (bf16[128,1024]{1,0:T(8,128)(2,1)S(1)}, bf16[128,1024]{1,0:T(8,128)(2,1)S(1)}, u32[]{:S(2)}, u32[]{:S(2)}) collective-permute-start(bf16[128,1024]{1,0:T(8,128)(2,1)S(1)} %get-tuple-element.69), channel_id=1, source_target_pairs={{0,2},{1,3},{2,0},{3,1},{4,6},{5,7},{6,4},{7,5},{8,10},{9,11},{10,... | collective-permute-start | bytes 786440 | tf_op jit(solution)/shard_map/ppermute | solution.py:484
  117.3 6.3 %collective-permute-start.25 = (bf16[256,512]{1,0:T(8,128)(2,1)S(1)}, bf16[256,512]{1,0:T(8,128)(2,1)S(1)}, u32[]{:S(2)}, u32[]{:S(2)}) collective-permute-start(bf16[256,512]{1,0:T(8,128)(2,1)S(1)} %get-tuple-element.60), channel_id=1, source_target_pairs={{0,1},{1,0},{2,3},{3,2},{4,5},{5,4},{6,7},{7,6},{8,9},{9,8},{10,11... | collective-permute-start | bytes 786440 | tf_op jit(solution)/shard_map/ppermute | solution.py:484
  120.3 8.1 %collective-permute-start.17 = (bf16[256,512]{1,0:T(8,128)(2,1)S(1)}, bf16[256,512]{1,0:T(8,128)(2,1)S(1)}, u32[]{:S(2)}, u32[]{:S(2)}) collective-permute-start(bf16[256,512]{1,0:T(8,128)(2,1)S(1)} %get-tuple-element.63), channel_id=1, source_target_pairs={{0,1},{1,0},{2,3},{3,2},{4,5},{5,4},{6,7},{7,6},{8,9},{9,8},{10,11... | collective-permute-start | bytes 786440 | tf_op jit(solution)/shard_map/ppermute | solution.py:484
  120.4 6.0 %collective-permute-start.23 = (bf16[128,512]{1,0:T(8,128)(2,1)S(1)}, bf16[128,512]{1,0:T(8,128)(2,1)S(1)}, u32[]{:S(2)}, u32[]{:S(2)}) collective-permute-start(bf16[128,512]{1,0:T(8,128)(2,1)S(1)} %get-tuple-element.72), channel_id=1, source_target_pairs={{0,2},{1,3},{2,0},{3,1},{4,6},{5,7},{6,4},{7,5},{8,10},{9,11},{10,... | collective-permute-start | bytes 393224 | tf_op jit(solution)/shard_map/ppermute | solution.py:484
  122.1 12.0 %collective-permute-start.21 = (bf16[128,1024]{1,0:T(8,128)(2,1)S(1)}, bf16[128,1024]{1,0:T(8,128)(2,1)S(1)}, u32[]{:S(2)}, u32[]{:S(2)}) collective-permute-start(bf16[128,1024]{1,0:T(8,128)(2,1)S(1)} %shard_map.92), channel_id=1, source_target_pairs={{0,4},{4,0},{8,12},{12,8},{16,20},{20,16},{24,28},{28,24},{1,5},{5... | collective-permute-start | bytes 786440 | tf_op jit(solution)/shard_map/ppermute | solution.py:494
  123.7 6.3 %collective-permute-start.26 = (bf16[128,512]{1,0:T(8,128)(2,1)S(1)}, bf16[128,512]{1,0:T(8,128)(2,1)S(1)}, u32[]{:S(2)}, u32[]{:S(2)}) collective-permute-start(bf16[128,512]{1,0:T(8,128)(2,1)S(1)} %get-tuple-element.75), channel_id=1, source_target_pairs={{0,2},{1,3},{2,0},{3,1},{4,6},{5,7},{6,4},{7,5},{8,10},{9,11},{10,... | collective-permute-start | bytes 393224 | tf_op jit(solution)/shard_map/ppermute | solution.py:484
  126.5 7.6 %collective-permute-start.24 = (bf16[128,512]{1,0:T(8,128)(2,1)S(1)}, bf16[128,512]{1,0:T(8,128)(2,1)S(1)}, u32[]{:S(2)}, u32[]{:S(2)}) collective-permute-start(bf16[128,512]{1,0:T(8,128)(2,1)S(1)} %shard_map.94), channel_id=1, source_target_pairs={{0,4},{4,0},{8,12},{12,8},{16,20},{20,16},{24,28},{28,24},{1,5},{5... | collective-permute-start | bytes 393224 | tf_op jit(solution)/shard_map/ppermute | solution.py:494
  128.4 8.2 %collective-permute-start.18 = (bf16[128,512]{1,0:T(8,128)(2,1)S(1)}, bf16[128,512]{1,0:T(8,128)(2,1)S(1)}, u32[]{:S(2)}, u32[]{:S(2)}) collective-permute-start(bf16[128,512]{1,0:T(8,128)(2,1)S(1)} %get-tuple-element.65), channel_id=1, source_target_pairs={{0,2},{1,3},{2,0},{3,1},{4,6},{5,7},{6,4},{7,5},{8,10},{9,11},{10,... | collective-permute-start | bytes 393224 | tf_op jit(solution)/shard_map/ppermute | solution.py:484
  130.1 4.7 %collective-permute-start.27 = (bf16[128,256]{1,0:T(8,128)(2,1)S(1)}, bf16[128,256]{1,0:T(8,128)(2,1)S(1)}, u32[]{:S(2)}, u32[]{:S(2)}) collective-permute-start(bf16[128,256]{1,0:T(8,128)(2,1)S(1)} %get-tuple-element.77), channel_id=1, source_target_pairs={{0,4},{4,0},{8,12},{12,8},{16,20},{20,16},{24,28},{28,24},{1,5},{5... | collective-permute-start | bytes 196616 | tf_op jit(solution)/shard_map/ppermute | solution.py:494
  136.7 4.3 %collective-permute-start.28 = (bf16[128,256]{1,0:T(8,128)(2,1)S(1)}, bf16[128,256]{1,0:T(8,128)(2,1)S(1)}, u32[]{:S(2)}, u32[]{:S(2)}) collective-permute-start(bf16[128,256]{1,0:T(8,128)(2,1)S(1)} %get-tuple-element.80), channel_id=1, source_target_pairs={{0,4},{4,0},{8,12},{12,8},{16,20},{20,16},{24,28},{28,24},{1,5},{5... | collective-permute-start | bytes 196616 | tf_op jit(solution)/shard_map/ppermute | solution.py:494

commit v8 on v5

--- a/solution.py
+++ b/solution.py
@@ -43,7 +43,7 @@
     return jnp.stack([jnp.asarray(value, jnp.int32) for value in values])
 
 
-def local_call(kernel, places, operands, out_shapes, scratch=()):
+def local_call(kernel, places, operands, out_shapes, flops=0):
     held = sum(value.size * value.dtype.itemsize for value in [*operands, *out_shapes])
     return pl.pallas_call(
         kernel,
@@ -51,9 +51,8 @@
         + [pl.BlockSpec(memory_space=pltpu.VMEM)] * len(operands),
         out_specs=[pl.BlockSpec(memory_space=pltpu.VMEM)] * len(out_shapes),
         out_shape=out_shapes,
-        scratch_shapes=list(scratch),
         compiler_params=pltpu.CompilerParams(vmem_limit_bytes=max(VMEM_BYTES, held + held // 2)),
-        cost_estimate=pl.CostEstimate(flops=1, bytes_accessed=1, transcendentals=0),
+        cost_estimate=pl.CostEstimate(flops=flops, bytes_accessed=held, transcendentals=0),
     )(places, *operands)
 
 
@@ -82,26 +81,6 @@
     )
 
 
-def cut_kernel(first, w_ref, out_ref, sem):
-    copy = pltpu.make_async_copy(w_ref.at[:, pl.ds(first, out_ref.shape[1])], out_ref, sem)
-    copy.start()
-    copy.wait()
-
-
-def cut_columns(weight, first, width):
-    if width % DH:
-        return weight[:, first : first + width]
-    return pl.pallas_call(
-        functools.partial(cut_kernel, first),
-        in_specs=[pl.BlockSpec(memory_space=pl.ANY)],
-        out_specs=pl.BlockSpec(memory_space=pltpu.VMEM),
-        out_shape=jax.ShapeDtypeStruct((weight.shape[0], width), weight.dtype),
-        scratch_shapes=[pltpu.SemaphoreType.DMA],
-        compiler_params=pltpu.CompilerParams(vmem_limit_bytes=VMEM_BYTES),
-        cost_estimate=pl.CostEstimate(flops=1, bytes_accessed=1, transcendentals=0),
-    )(weight)
-
-
 def states_kernel(part_ref, k_ref, v_ref, out_ref):
     heads = out_ref.shape[0]
     for index in range(heads):
@@ -120,6 +99,7 @@
         scalars(part),
         [key_input, value_input],
         [jax.ShapeDtypeStruct((heads, DH, DH), dtype)],
+        2 * key_input.shape[0] * heads * DH * DH,
     )[0]
 
 
@@ -194,6 +174,7 @@
         scalars(0),
         [queries, key_input, value_input],
         [jax.ShapeDtypeStruct((queries.shape[0], heads * DH), jnp.float32)],
+        3 * queries.shape[0] ** 2 * heads * DH,
     )[0]
 
 
@@ -248,6 +229,7 @@
             jax.ShapeDtypeStruct((rows, width), jnp.bfloat16),
             jax.ShapeDtypeStruct((len(order), rows // len(order)), jnp.float32),
         ],
+        4 * rows * width * DH,
     )
 
 
@@ -256,12 +238,11 @@
     weight_refs = refs[n_rows : n_rows + sum(choices)]
     sent_ref, kept_ref = refs[n_rows + sum(choices) :]
     half = sent_ref.shape[0]
-    width = weight_refs[0].shape[1]
 
     def products(index, weight_ref):
-        for position, (rows, weight) in enumerate(jobs):
+        for rows, weight, first in jobs:
             if weight == index:
-                columns = pl.ds(position * width, width)
+                columns = pl.ds(first, weight_ref.shape[1])
                 product = jnp.dot(
                     rows_refs[rows][...], weight_ref[...], preferred_element_type=jnp.float32
                 )
@@ -282,12 +263,18 @@
 def project(jobs, rows_list, weights, flag):
     flat = [choice for weight in weights for choice in weight]
     choices = tuple(len(weight) for weight in weights)
-    shape = (rows_list[0].shape[0] // 2, flat[0].shape[1] * len(jobs))
+    placed_jobs, total = [], 0
+    for rows, weight in jobs:
+        placed_jobs.append((rows, weight, total))
+        total += weights[weight][0].shape[1]
+    height, depth = rows_list[0].shape
+    shape = (height // 2, total)
     return local_call(
-        functools.partial(project_kernel, tuple(jobs), len(rows_list), choices),
+        functools.partial(project_kernel, tuple(placed_jobs), len(rows_list), choices),
         flag,
         [*rows_list, *flat],
         [jax.ShapeDtypeStruct(shape, jnp.bfloat16), jax.ShapeDtypeStruct(shape, jnp.float32)],
+        2 * height * depth * total,
     )
 
 
@@ -319,61 +306,60 @@
     return jnp.transpose(jnp.broadcast_to(row, (row.shape[1], row.shape[1])))
 
 
-def scaled_parts(counts, cut, squares_ref, pieces, total_width):
+def scaled_parts(counts, width, starts_ref, squares_ref, pieces, total_width):
     scale = lax.rsqrt(column(squares_ref[...]) / total_width + epsilon)
+    where = 0
     for piece, count in zip(pieces, counts):
         for index in range(count):
-            for first in range(index * cut, (index + 1) * cut, DH):
-                yield piece[:, pl.ds(first, DH)].astype(jnp.float32) * scale
-
-
-def placed_kernel(counts, cut, total_width, starts_ref, squares_ref, *refs):
+            for at in range(0, width, DH):
+                part = piece[:, pl.ds(index * width + at, DH)].astype(jnp.float32) * scale
+                yield part, pl.multiple_of(starts_ref[where] + at, DH)
+            where += 1
+
+
+def placed_kernel(counts, width, total_width, starts_ref, squares_ref, *refs):
     out_ref = refs[-1]
-    steps = cut // DH
-    for at, part in enumerate(scaled_parts(counts, cut, squares_ref, refs[:-1], total_width)):
-        start = pl.multiple_of(starts_ref[at // steps] + at % steps * DH, DH)
+    for part, start in scaled_parts(counts, width, starts_ref, squares_ref, refs[:-1], total_width):
         out_ref[:, pl.ds(start, DH)] = part.astype(out_ref.dtype)
 
 
-def added_kernel(counts, cut, total_width, starts_ref, squares_ref, *refs):
-    pieces = refs[: len(counts)]
+def added_kernel(counts, width, total_width, starts_ref, squares_ref, *refs):
     out_ref, buf, sem = refs[-3:]
-    steps = cut // DH
     copies = []
-    for at, part in enumerate(scaled_parts(counts, cut, squares_ref, pieces, total_width)):
-        where = at // steps
-        buf[where, :, pl.ds(at % steps * DH, DH)] = part.astype(out_ref.dtype)
-        if at % steps == steps - 1:
-            start = pl.multiple_of(starts_ref[where], DH)
-            copy = pltpu.make_async_copy(buf.at[where], out_ref.at[:, pl.ds(start, cut)], sem.at[where])
-            copy.start()
-            copies.append(copy)
+    parts = scaled_parts(counts, width, starts_ref, squares_ref, refs[: len(counts)], total_width)
+    for at, (part, start) in enumerate(parts):
+        buf[at] = part.astype(out_ref.dtype)
+        copies.append(pltpu.make_async_copy(buf.at[at], out_ref.at[:, pl.ds(start, DH)], sem.at[at]))
+        copies[-1].start()
     for copy in copies:
         copy.wait()
 
 
-def placed(filled, pieces, squares, cut, shape, total_width):
+def placed(filled, pieces, squares, width, shape, total_width):
     counts = tuple(len(starts) for _, starts in pieces)
     starts = scalars(*[start for _, own in pieces for start in own])
     operands = [squares] + [piece for piece, _ in pieces]
     out_shape = jax.ShapeDtypeStruct(shape, jnp.bfloat16)
+    columns = width * sum(counts)
     if filled is None:
-        kernel = functools.partial(placed_kernel, counts, cut, total_width)
+        kernel = functools.partial(placed_kernel, counts, width, total_width)
         return local_call(kernel, starts, operands, [out_shape])[0]
     return pl.pallas_call(
-        functools.partial(added_kernel, counts, cut, total_width),
+        functools.partial(added_kernel, counts, width, total_width),
         in_specs=[pl.BlockSpec(memory_space=pltpu.SMEM)]
         + [pl.BlockSpec(memory_space=pltpu.VMEM)] * len(operands)
         + [pl.BlockSpec(memory_space=pl.ANY)],
         out_specs=pl.BlockSpec(memory_space=pl.ANY),
         out_shape=out_shape,
         scratch_shapes=[
-            pltpu.VMEM((sum(counts), shape[0], cut), jnp.bfloat16),
-            pltpu.SemaphoreType.DMA((sum(counts),)),
+            pltpu.VMEM((columns // DH, shape[0], DH), jnp.bfloat16),
+            pltpu.SemaphoreType.DMA((columns // DH,)),
         ],
         input_output_aliases={len(operands) + 1: 0},
         compiler_params=pltpu.CompilerParams(vmem_limit_bytes=VMEM_BYTES),
-        cost_estimate=pl.CostEstimate(flops=1, bytes_accessed=1, transcendentals=0),
+        cost_estimate=pl.CostEstimate(
+            flops=0, bytes_accessed=4 * shape[0] * columns, transcendentals=0
+        ),
     )(starts, *operands, filled)
 
 
@@ -387,28 +373,22 @@
     heads = local_width // DH
     total_width = local_width * n_head
     width = out_weight.shape[1]
-    cuts = 2 if width % (2 * DH) == 0 else 1
-    cut = width // cuts
 
     def along(value, hops):
         return lax.ppermute(value, "seq", line_pairs(n_seq, hops))
 
-    w_cuts = [cut_columns(out_weight, k * cut, cut) for k in range(cuts)]
-    w_pair = [along(w_cuts[0], SWAP_OUTER)]
-    w_mid1 = [along(w_cuts[0], SWAP_MIDDLE)]
-    terms, steps = state_prefix(key_input, value_input, n_seq, place, [w_pair[0], w_mid1[0]])
+    w_mid1 = along(out_weight, SWAP_MIDDLE)
+    w_pair = along(out_weight, SWAP_OUTER)
+    terms, stepped = state_prefix(key_input, value_input, n_seq, place, [w_mid1, w_pair])
     some = heads // 2
     inners = [
         causal_part(queries, key_input, value_input, 0, some),
         causal_part(queries, key_input, value_input, some, heads - some),
     ]
 
-    for k in range(1, cuts):
-        w_pair.append(along(hold(w_cuts[k], *steps), SWAP_OUTER))
-        w_mid1.append(along(hold(w_cuts[k], *steps), SWAP_MIDDLE))
-    w_mid2 = [along(hold(w_pair[k], *steps), SWAP_MIDDLE) for k in range(cuts)]
-    w_end1 = [along(hold(w_mid1[k], *steps), TO_ENDS) for k in range(cuts)]
-    w_end2 = [along(w_mid2[k], TO_ENDS) for k in range(cuts)]
+    w_end1 = along(hold(w_mid1, *stepped), TO_ENDS)
+    w_mid2 = along(hold(w_pair, *stepped), SWAP_MIDDLE)
+    w_end2 = along(w_mid2, TO_ENDS)
 
     bits = n_head.bit_length() - 1
     order = [int(format(j, "b").zfill(bits)[::-1], 2) for j in range(n_head)] if bits else [0]
@@ -430,64 +410,57 @@
 
     rows_list = [hidden] + others
 
-    def summed(flag, parts):
-        blocks = sorted({block for _, own in parts for block in own})
-        turns = [turn for turn, _ in parts]
-        jobs = [(p, blocks.index(block)) for p, (_, own) in enumerate(parts) for block in own]
+    owners = [z, z ^ 1, jnp.where(low, 2, 1), jnp.where(low, 3, 0)]
+    blocks = [(out_weight,), (w_pair,), (w_mid1, w_end1), (w_mid2, w_end2)]
+
+    def summed(parts, pins, pin_end=None):
+        weights = sorted({block for _, own in parts for block in own})
+        jobs = [(p, weights.index(block)) for p, (_, own) in enumerate(parts) for block in own]
         sent, kept = project(
-            jobs, [rows_list[turn] for turn in turns], [weights[block] for block in blocks], flag
+            jobs,
+            [rows_list[turn] for turn, _ in parts],
+            [blocks[block] for block in weights],
+            hold(flag, *pins),
         )
-        widths = [cut * len(own) for _, own in parts]
-        bit, steps = 1, []
+        first_sent, bit = sent, 1
         while bit < n_head:
-            steps.append(lax.ppermute(sent, "head", flip_pairs(n_head, bit)))
+            got = lax.ppermute(sent, "head", flip_pairs(n_head, bit))
             bit *= 2
             if bit < n_head:
-                sent, kept = fold(kept, steps[-1])
+                sent, kept = fold(kept, got)
             else:
-                kept = fold(kept, steps[-1], widths)
+                got = got if pin_end is None else hold(got, pin_end)
+                kept = fold(kept, got, [width * len(own) for _, own in parts])
         pieces = []
         for piece, (turn, own) in zip(kept, parts):
             if turn:
                 piece = lax.ppermute(piece, "seq", turn_pairs(n_seq, -turn))
-            starts = [
-                (owners[block] * inner + (i + turn) % inner) * width + k * cut for block, k in own
-            ]
+            starts = [(owners[block] * inner + (i + turn) % inner) * width for block in own]
             pieces.append((piece, starts))
-        return pieces, steps
-
-    owners = [z, z ^ 1, jnp.where(low, 2, 1), jnp.where(low, 3, 0)]
-    weights = {}
-    for k in range(cuts):
-        weights[0, k] = (w_cuts[k],)
-        weights[1, k] = (w_pair[k],)
-        weights[2, k] = (w_mid1[k], w_end1[k])
-        weights[3, k] = (w_mid2[k], w_end2[k])
-    cut_range = range(cuts)
-    early = [(block, k) for block in (0, 1) for k in cut_range]
-    third = [(2, k) for k in cut_range]
-    other_turns = list(range(1, inner))
-    flag = hold(flag, w_end1[0], w_mid2[0])
-    pieces, steps = summed(flag, [(0, early)])
-    flag = hold(flag, squares, *steps, *w_end1, *w_mid2)
-    more, late_steps = summed(flag, [(0, third)] + [(turn, early + third) for turn in other_turns])
-    pieces += more
-    flag = hold(flag, late_steps[0])
-    for k in cut_range:
-        last, steps = summed(flag, [(turn, [(3, k)]) for turn in [0] + other_turns])
-        flag = hold(flag, steps[0], *late_steps)
-        if k + 1 < cuts:
-            pieces += last
+        return pieces, first_sent, got
+
+    turns = list(range(inner))
     shape = (out_rows, width * n_seq)
-    if cut % DH == 0 and out_rows == DH:
-        filled = placed(None, pieces, squares, cut, shape, total_width)
-        return placed(filled, last, squares, cut, shape, total_width)
+    in_kernel = width % DH == 0 and out_rows == DH
+
+    pieces, pins, ends = [], [], []
+    groups = [(turns[:1], [0, 1]), (turns[:1], [2]), (turns[1:], [0, 1]), (turns[1:], [2])]
+    for members, some in groups:
+        if members:
+            more, sent, end = summed([(turn, some) for turn in members], pins)
+            pieces += more
+            ends.append(end)
+            pins = [sent, squares, w_mid2]
+    filled = placed(None, pieces, squares, width, shape, total_width) if in_kernel else None
+    last, _, _ = summed([(turn, [3]) for turn in turns], [sent, *ends], filled)
+    if in_kernel:
+        return placed(filled, last, squares, width, shape, total_width)
     scale = lax.rsqrt(squares.reshape(out_rows, 1) / total_width + epsilon)
     output = jnp.zeros(shape, jnp.bfloat16)
     for piece, starts in pieces + last:
         piece = (piece.astype(jnp.float32) * scale).astype(jnp.bfloat16)
         for index, start in enumerate(starts):
-            part = piece[:, index * cut : (index + 1) * cut]
+            part = piece[:, index * width : (index + 1) * width]
             output = lax.dynamic_update_slice_in_dim(output, part, start, 1)
     return output
 

time: 129 us -> 126 us (0.977)
  waiting for transfers between devices: 55.4 us -> 67.6 us
  starting transfers between devices: 42.9 us -> 30.8 us
  local copies, waits for them, and re-layouts: 7.65 us -> 3.8 us
    ppermute x10 -> x5, starting transfers between devices: 22.2 us -> 9.01 us  [along(): return lax.ppermute(value, 'seq', line_pairs(n_seq, hops))]
    ppermute x10 -> x5, waiting for transfers between devices: 32.8 us -> 22.8 us  [along(): return lax.ppermute(value, 'seq', line_pairs(n_seq, hops))]
    ppermute x3, waiting for transfers between devices: 2.54 us -> 12.3 us  [summed(): piece = lax.ppermute(piece, 'seq', turn_pairs(n_seq, -turn))]
    ppermute x8 -> x10, waiting for transfers between devices: 8.45 us -> 17.1 us  [summed(): got = lax.ppermute(sent, 'head', flip_pairs(n_head, bit))]
    ppermute x1, waiting for transfers between devices: 2.5 us -> 10.4 us  [state_prefix(): from_left = lax.ppermute(first, 'seq', line_pairs(n_seq, [(0, 1), (2, 3)]))]
    ppermute x2, waiting for transfers between devices: 6.12 us -> 1.14 us  [shards(): lax.ppermute(squares[half:], 'head', flip_pairs(n_head, bit))]
    unnamed x34 -> x24, local copies, waits for them, and re-layouts: 7.55 us -> 3.71 us
    pallas_call x21 -> x24, Pallas kernels: 18.5 us -> 21 us  [local_call(): pl.pallas_call(kernel, in_specs=[pl.BlockSpec(memory_space=pltpu.SMEM)] +...]
  transfers between devices with their start and end apart: 29 -> 26, of which waited for: 12 -> 11; matrix products, arithmetic and copies ran while one was open for 0% -> 0% of each run, Pallas kernels for 11% -> 14%
where the time goes in v8:
time: 126 us; the launch traced here: 125 us
  waiting for transfers between devices  67.6 us (54%)
  starting transfers between devices  30.8 us (24%)
  Pallas kernels  22.4 us (18%)
  local copies, waits for them, and re-layouts  3.8 us (3%)
    ppermute x5, waiting for transfers between devices, along(): return lax.ppermute(value, 'seq', line_pairs(n_seq, hops))  22.8 us
    pallas_call x24, Pallas kernels, local_call(): pl.pallas_call(kernel, in_specs=[pl.BlockSpec(memory_space=pltpu.SMEM)] +...  21 us
    ppermute x10, waiting for transfers between devices, summed(): got = lax.ppermute(sent, 'head', flip_pairs(n_head, bit))  17.1 us
    ppermute x3, waiting for transfers between devices, summed(): piece = lax.ppermute(piece, 'seq', turn_pairs(n_seq, -turn))  12.3 us
    ppermute x1, waiting for transfers between devices, state_prefix(): from_left = lax.ppermute(first, 'seq', line_pairs(n_seq, [(0, 1), (2, 3)]))  10.4 us
    ppermute x5, starting transfers between devices, along(): return lax.ppermute(value, 'seq', line_pairs(n_seq, hops))  9.01 us
    ppermute x10, starting transfers between devices, summed(): got = lax.ppermute(sent, 'head', flip_pairs(n_head, bit))  6.75 us
    ppermute x1, starting transfers between devices, state_prefix(): from_left = lax.ppermute(first, 'seq', line_pairs(n_seq, [(0, 1), (2, 3)]))  5.34 us
  transfers between devices with their start and end apart: 26, of which 11 were waited for; matrix products, arithmetic and copies ran while one was open for 0% of the time, Pallas kernels for 14%

profile of v8, /device:TPU:0, one launch (start us, length us, event | category | flops | bytes accessed | tf_op | source)
XLA Modules:
  0.0 125.1 jit_solution(5353900393464449052)
XLA Ops:
  0.0 3.0 %collective-permute-start.3 = (bf16[1024,512]{1,0:T(8,128)(2,1)}, bf16[1024,512]{1,0:T(8,128)(2,1)}, u32[]{:S(2)}, u32[]{:S(2)}) collective-permute-start(bf16[1024,512]{1,0:T(8,128)(2,1)} %refs_1_.3), channel_id=1, source_target_pairs={{0,8},{4,12},{8,0},{12,4},{16,24},{20,28},{24,16},{28,20},{1,9},{5... | collective-permute-start | bytes 3145736 | tf_op jit(solution)/shard_map/ppermute | solution.py:378
  3.0 1.7 %collective-permute-start.2 = (bf16[1024,512]{1,0:T(8,128)(2,1)}, bf16[1024,512]{1,0:T(8,128)(2,1)}, u32[]{:S(2)}, u32[]{:S(2)}) collective-permute-start(bf16[1024,512]{1,0:T(8,128)(2,1)} %refs_1_.3), channel_id=1, source_target_pairs={{8,16},{12,20},{16,8},{20,12},{9,17},{13,21},{17,9},{21,13},{10,18... | collective-permute-start | bytes 3145736 | tf_op jit(solution)/shard_map/ppermute | solution.py:378
  4.7 1.2 copy-done
  5.9 1.2 copy-done.2
  7.1 0.5 shard_map.74
  7.6 1.6 %collective-permute-start = (bf16[4,128,128]{2,1,0:T(8,128)(2,1)S(1)}, bf16[4,128,128]{2,1,0:T(8,128)(2,1)S(1)}, u32[]{:S(2)}, u32[]{:S(2)}) collective-permute-start(bf16[4,128,128]{2,1,0:T(8,128)(2,1)S(1)} %shard_map.74), channel_id=1, source_target_pairs={{0,4},{4,0},{8,12},{12,8},{16,20},{20,16},{24,28},{28,24},{1,5},{5... | collective-permute-start | bytes 393224 | tf_op jit(solution)/shard_map/ppermute | solution.py:123
  9.2 0.5 shard_map.73.refs_0_.refs_3_
  9.7 0.0 copy-start.3
  9.7 3.0 %collective-permute-done.refs_1_.refs_4_ = bf16[4,128,128]{2,1,0:T(8,128)(2,1)S(1)} collective-permute-done((bf16[4,128,128]{2,1,0:T(8,128)(2,1)S(1)}, bf16[4,128,128]{2,1,0:T(8,128)(2,1)S(1)}, u32[]{:S(2)}, u32[]{:S(2)}) %collective-permute-start) | collective-permute-done | bytes 131104 | tf_op jit(solution)/shard_map/ppermute | solution.py:123
  12.7 5.3 %collective-permute-start.1 = (bf16[4,128,128]{2,1,0:T(8,128)(2,1)S(1)}, bf16[4,128,128]{2,1,0:T(8,128)(2,1)S(1)}, u32[]{:S(2)}, u32[]{:S(2)}) collective-permute-start(bf16[4,128,128]{2,1,0:T(8,128)(2,1)S(1)} %shard_map.75), channel_id=1, source_target_pairs={{0,8},{4,12},{16,24},{20,28},{1,9},{5,13},{17,25},{21,29},{2,10},{... | collective-permute-start | bytes 393224 | tf_op jit(solution)/shard_map/ppermute | solution.py:126
  18.0 10.4 %collective-permute-done.1.refs_2_.refs_0_ = bf16[4,128,128]{2,1,0:T(8,128)(2,1)S(1)} collective-permute-done((bf16[4,128,128]{2,1,0:T(8,128)(2,1)S(1)}, bf16[4,128,128]{2,1,0:T(8,128)(2,1)S(1)}, u32[]{:S(2)}, u32[]{:S(2)}) %collective-permute-start.1) | collective-permute-done | bytes 131104 | tf_op jit(solution)/shard_map/ppermute | solution.py:126
  28.5 0.0 collective-permute-done.3.refs_2_
  28.5 0.0 collective-permute-done.2.refs_1_
  28.5 0.7 shard_map.76
  29.2 1.3 %collective-permute-start.5 = (bf16[4,128,128]{2,1,0:T(8,128)(2,1)}, bf16[4,128,128]{2,1,0:T(8,128)(2,1)}, u32[]{:S(2)}, u32[]{:S(2)}) collective-permute-start(bf16[4,128,128]{2,1,0:T(8,128)(2,1)} %shard_map.76), channel_id=1, source_target_pairs={{8,24},{12,28},{9,25},{13,29},{10,26},{14,30},{11,27},{15,31}} | collective-permute-start | bytes 393224 | tf_op jit(solution)/shard_map/ppermute | solution.py:130
  30.5 1.3 %collective-permute-start.4 = (bf16[4,128,128]{2,1,0:T(8,128)(2,1)}, bf16[4,128,128]{2,1,0:T(8,128)(2,1)}, u32[]{:S(2)}, u32[]{:S(2)}) collective-permute-start(bf16[4,128,128]{2,1,0:T(8,128)(2,1)} %shard_map.76), channel_id=1, source_target_pairs={{8,16},{12,20},{9,17},{13,21},{10,18},{14,22},{11,19},{15,23}} | collective-permute-start | bytes 393224 | tf_op jit(solution)/shard_map/ppermute | solution.py:129
  31.8 1.1 shard_map.78.refs_2_
  32.9 1.6 %collective-permute-start.9 = (bf16[1024,512]{1,0:T(8,128)(2,1)}, bf16[1024,512]{1,0:T(8,128)(2,1)}, u32[]{:S(2)}, u32[]{:S(2)}) collective-permute-start(bf16[1024,512]{1,0:T(8,128)(2,1)} %collective-permute-done.3.refs_2_), channel_id=1, source_target_pairs={{8,16},{12,20},{16,8},{20,12},{9,17},{13,21},{17,9},{21,13},{10,18... | collective-permute-start | bytes 3145736 | tf_op jit(solution)/shard_map/ppermute | solution.py:378
  34.6 0.1 add_convert_fusion.masks_ref
  34.6 1.1 shard_map.77
  35.8 1.6 %collective-permute-start.6 = (bf16[4,128,128]{2,1,0:T(8,128)(2,1)S(1)}, bf16[4,128,128]{2,1,0:T(8,128)(2,1)S(1)}, u32[]{:S(2)}, u32[]{:S(2)}) collective-permute-start(bf16[4,128,128]{2,1,0:T(8,128)(2,1)S(1)} %get-tuple-element.41), channel_id=1, source_target_pairs={{0,4},{4,0},{8,12},{12,8},{16,20},{20,16},{24,28},{28,24},{1,5},{5... | collective-permute-start | bytes 393224 | tf_op jit(solution)/shard_map/ppermute | solution.py:137
  37.3 0.1 pad_add_fusion.1.place_ref
  37.4 1.4 %collective-permute-start.10 = (bf16[1024,512]{1,0:T(8,128)(2,1)}, bf16[1024,512]{1,0:T(8,128)(2,1)}, u32[]{:S(2)}, u32[]{:S(2)}) collective-permute-start(bf16[1024,512]{1,0:T(8,128)(2,1)} %collective-permute-done.2.refs_1_), channel_id=1, source_target_pairs={{8,0},{12,4},{16,24},{20,28},{9,1},{13,5},{17,25},{21,29},{10,2},{... | collective-permute-start | bytes 3145736 | tf_op jit(solution)/shard_map/ppermute | solution.py:378
  38.8 1.1 shard_map.79.refs_3_
  39.9 0.9 collective-permute-done.6.refs_1_
  40.8 1.8 %shard_map.80 = (bf16[512,1024]{1,0:T(8,128)(2,1)S(1)}, f32[4,128]{1,0:T(4,128)S(1)}) custom-call(s32[2]{0:T(128)S(1)} %pad_add_fusion.1.place_ref, bf16[512,1024]{1,0:T(8,128)(2,1)S(1)} %copy-done.4, bf16[512,1024]{1,0:T(8,128)(2,1)S(1)} %copy-done.5, f32[32,1,128]{2,1,0:T(1,128)S(1)} %bitcast.16, f32[8,128,128]{2,1,0:T(8,128)S(1)} %copy-done.8, ...), custom_call_target="tpu_custom_call" | custom-call | flops 268435456 | bytes 6178816 | tf_op jit(solution)/shard_map/pallas_call | solution.py:48
  42.6 1.6 %collective-permute-start.11 = (bf16[512,1024]{1,0:T(8,128)(2,1)S(1)}, bf16[512,1024]{1,0:T(8,128)(2,1)S(1)}, u32[]{:S(2)}, u32[]{:S(2)}) collective-permute-start(bf16[512,1024]{1,0:T(8,128)(2,1)S(1)} %get-tuple-element.43.refs_0_), channel_id=1, source_target_pairs={{0,4},{4,0},{8,12},{12,8},{16,20},{20,16},{24,28},{28,24},{1,5},{5... | collective-permute-start | bytes 3145736 | tf_op jit(solution)/shard_map/ppermute | solution.py:398
  44.1 1.1 collective-permute-done.7
  45.3 1.5 %collective-permute-start.8 = (f32[1,128]{1,0:T(1,128)S(1)}, f32[1,128]{1,0:T(1,128)S(1)}, u32[]{:S(2)}, u32[]{:S(2)}) collective-permute-start(f32[1,128]{1,0:T(1,128)S(1)} %slice.15), channel_id=1, source_target_pairs={{0,2},{1,3},{2,0},{3,1},{4,6},{5,7},{6,4},{7,5},{8,10},{9,11},{10,... | collective-permute-start | bytes 1544 | tf_op jit(solution)/shard_map/ppermute | solution.py:403
  46.8 1.2 copy-done.10
  48.0 2.5 %shard_map.81 = (bf16[256,1024]{1,0:T(8,128)(2,1)S(1)}, f32[256,1024]{1,0:T(8,128)S(1)}) custom-call(s32[1]{0:T(128)} %bitcast.9.flag_ref, bf16[512,1024]{1,0:T(8,128)(2,1)S(1)} %get-tuple-element.43.refs_0_, bf16[1024,512]{1,0:T(8,128)(2,1)S(1)} %copy-done.10, bf16[1024,512]{1,0:T(8,128)(2,1)} %collective-permute-done.3.refs_2_), custom_call_target="tpu_custom_call" | custom-call | flops 1073741824 | bytes 4718592 | tf_op jit(solution)/shard_map/pallas_call | solution.py:48
  50.5 0.1 collective-permute-start.12
  50.6 1.3 %collective-permute-start.20 = (bf16[1024,512]{1,0:T(8,128)(2,1)}, bf16[1024,512]{1,0:T(8,128)(2,1)S(1)}, u32[]{:S(2)}, u32[]{:S(2)}) collective-permute-start(bf16[1024,512]{1,0:T(8,128)(2,1)} %collective-permute-done.9.refs_2_), channel_id=1, source_target_pairs={{8,0},{12,4},{16,24},{20,28},{9,1},{13,5},{17,25},{21,29},{10,2},{... | collective-permute-start | bytes 3145736 | tf_op jit(solution)/shard_map/ppermute | solution.py:378
  51.9 0.0 copy-start.11
  51.9 22.8 %collective-permute-done.10.refs_2_ = bf16[1024,512]{1,0:T(8,128)(2,1)} collective-permute-done((bf16[1024,512]{1,0:T(8,128)(2,1)}, bf16[1024,512]{1,0:T(8,128)(2,1)}, u32[]{:S(2)}, u32[]{:S(2)}) %collective-permute-start.10) | collective-permute-done | bytes 1048608 | tf_op jit(solution)/shard_map/ppermute | solution.py:378
  74.7 2.2 %shard_map.82 = (bf16[256,512]{1,0:T(8,128)(2,1)S(1)}, f32[256,512]{1,0:T(8,128)S(1)}) custom-call(s32[1]{0:T(128)} %bitcast.9.flag_ref, bf16[512,1024]{1,0:T(8,128)(2,1)S(1)} %get-tuple-element.43.refs_0_, bf16[1024,512]{1,0:T(8,128)(2,1)} %collective-permute-done.2.refs_1_, bf16[1024,512]{1,0:T(8,128)(2,1)} %collective-permute-done.10.refs_2_), custom_call_target="tpu_custom_call" | custom-call | flops 536870912 | bytes 3932160 | tf_op jit(solution)/shard_map/pallas_call | solution.py:48
  77.0 2.5 %shard_map.83 = (bf16[256,1024]{1,0:T(8,128)(2,1)S(1)}, f32[256,1024]{1,0:T(8,128)S(1)}) custom-call(s32[1]{0:T(128)} %bitcast.9.flag_ref, bf16[512,1024]{1,0:T(8,128)(2,1)S(1)} %collective-permute-done.11.refs_0_.refs_1_, bf16[1024,512]{1,0:T(8,128)(2,1)S(1)} %copy-done.11, bf16[1024,512]{1,0:T(8,128)(2,1)} %collective-permute-done.3.refs_2_), custom_call_target="tpu_custom_call" | custom-call | flops 1073741824 | bytes 4718592 | tf_op jit(solution)/shard_map/pallas_call | solution.py:48
  79.4 0.1 collective-permute-start.16
  79.5 0.5 collective-permute-start.14
  80.0 2.2 %shard_map.84 = (bf16[256,512]{1,0:T(8,128)(2,1)S(1)}, f32[256,512]{1,0:T(8,128)S(1)}) custom-call(s32[1]{0:T(128)} %bitcast.9.flag_ref, bf16[512,1024]{1,0:T(8,128)(2,1)S(1)} %collective-permute-done.11.refs_0_.refs_1_, bf16[1024,512]{1,0:T(8,128)(2,1)} %collective-permute-done.2.refs_1_, bf16[1024,512]{1,0:T(8,128)(2,1)} %collective-permute-done.10.refs_2_), custom_call_target="tpu_custom_call" | custom-call | flops 536870912 | bytes 3932160 | tf_op jit(solution)/shard_map/pallas_call | solution.py:48
  82.3 0.1 collective-permute-start.18
  82.4 0.1 shard_map.85
  82.5 1.6 %collective-permute-start.13 = (bf16[128,1024]{1,0:T(8,128)(2,1)S(1)}, bf16[128,1024]{1,0:T(8,128)(2,1)S(1)}, u32[]{:S(2)}, u32[]{:S(2)}) collective-permute-start(bf16[128,1024]{1,0:T(8,128)(2,1)S(1)} %get-tuple-element.54), channel_id=1, source_target_pairs={{0,2},{1,3},{2,0},{3,1},{4,6},{5,7},{6,4},{7,5},{8,10},{9,11},{10,... | collective-permute-start | bytes 786440 | tf_op jit(solution)/shard_map/ppermute | solution.py:427
  84.1 0.1 shard_map.87
  84.2 0.6 collective-permute-start.17
  84.8 1.6 %collective-permute-start.15 = (bf16[128,512]{1,0:T(8,128)(2,1)S(1)}, bf16[128,512]{1,0:T(8,128)(2,1)S(1)}, u32[]{:S(2)}, u32[]{:S(2)}) collective-permute-start(bf16[128,512]{1,0:T(8,128)(2,1)S(1)} %get-tuple-element.56), channel_id=1, source_target_pairs={{0,2},{1,3},{2,0},{3,1},{4,6},{5,7},{6,4},{7,5},{8,10},{9,11},{10,... | collective-permute-start | bytes 393224 | tf_op jit(solution)/shard_map/ppermute | solution.py:427
  86.5 0.6 collective-permute-start.19
  87.0 4.7 %collective-permute-done.13.got_ref = bf16[128,1024]{1,0:T(8,128)(2,1)S(1)} collective-permute-done((bf16[128,1024]{1,0:T(8,128)(2,1)S(1)}, bf16[128,1024]{1,0:T(8,128)(2,1)S(1)}, u32[]{:S(2)}, u32[]{:S(2)}) %collective-permute-start.13) | collective-permute-done | bytes 262176 | tf_op jit(solution)/shard_map/ppermute | solution.py:427
  91.7 8.4 %collective-permute-done.15.got_ref = bf16[128,512]{1,0:T(8,128)(2,1)S(1)} collective-permute-done((bf16[128,512]{1,0:T(8,128)(2,1)S(1)}, bf16[128,512]{1,0:T(8,128)(2,1)S(1)}, u32[]{:S(2)}, u32[]{:S(2)}) %collective-permute-start.15) | collective-permute-done | bytes 131104 | tf_op jit(solution)/shard_map/ppermute | solution.py:427
  100.1 2.4 %collective-permute-done.19.got_ref = bf16[128,512]{1,0:T(8,128)(2,1)S(1)} collective-permute-done((bf16[128,512]{1,0:T(8,128)(2,1)S(1)}, bf16[128,512]{1,0:T(8,128)(2,1)S(1)}, u32[]{:S(2)}, u32[]{:S(2)}) %collective-permute-start.19) | collective-permute-done | bytes 131104 | tf_op jit(solution)/shard_map/ppermute | solution.py:427
  102.5 2.5 %shard_map.89 = (bf16[256,1024]{1,0:T(8,128)(2,1)S(1)}, f32[256,1024]{1,0:T(8,128)S(1)}) custom-call(s32[1]{0:T(128)} %bitcast.9.flag_ref, bf16[512,1024]{1,0:T(8,128)(2,1)S(1)} %get-tuple-element.43.refs_0_, bf16[512,1024]{1,0:T(8,128)(2,1)S(1)} %collective-permute-done.11.refs_0_.refs_1_, bf16[1024,512]{1,0:T(8,128)(2,1)} %collective-permute-done.9.refs_2_, ...), custom_call_target="tpu_custom_call" | custom-call | flops 1073741824 | bytes 5767168 | tf_op jit(solution)/shard_map/pallas_call | solution.py:48
  105.0 0.1 collective-permute-start.21
  105.1 0.2 collective-permute-start.23
  105.3 1.7 %collective-permute-done.21.got_ref = bf16[256,1024]{1,0:T(8,128)(2,1)S(1)} collective-permute-done((bf16[256,1024]{1,0:T(8,128)(2,1)S(1)}, bf16[256,1024]{1,0:T(8,128)(2,1)S(1)}, u32[]{:S(2)}, u32[]{:S(2)}) %collective-permute-start.21) | collective-permute-done | bytes 524320 | tf_op jit(solution)/shard_map/ppermute | solution.py:427
  106.9 0.1 shard_map.90
  107.0 1.6 %collective-permute-start.22 = (bf16[128,1024]{1,0:T(8,128)(2,1)S(1)}, bf16[128,1024]{1,0:T(8,128)(2,1)S(1)}, u32[]{:S(2)}, u32[]{:S(2)}) collective-permute-start(bf16[128,1024]{1,0:T(8,128)(2,1)S(1)} %get-tuple-element.65), channel_id=1, source_target_pairs={{0,2},{1,3},{2,0},{3,1},{4,6},{5,7},{6,4},{7,5},{8,10},{9,11},{10,... | collective-permute-start | bytes 786440 | tf_op jit(solution)/shard_map/ppermute | solution.py:427
  108.7 0.3 collective-permute-start.24
  109.0 0.1 stack.86.starts_ref
  109.1 7.5 %collective-permute-done.24.refs_3_ = bf16[128,512]{1,0:T(8,128)(2,1)S(1)} collective-permute-done((bf16[128,512]{1,0:T(8,128)(2,1)S(1)}, bf16[128,512]{1,0:T(8,128)(2,1)S(1)}, u32[]{:S(2)}, u32[]{:S(2)}) %collective-permute-start.24) | collective-permute-done | bytes 131104 | tf_op jit(solution)/shard_map/ppermute | solution.py:437
  116.7 1.8 %shard_map.95.refs_2_ = bf16[128,4096]{1,0:T(8,128)(2,1)} custom-call(s32[6]{0:T(128)S(1)} %stack.86.starts_ref, f32[1,128]{1,0:T(1,128)S(1)} %slice_add_fusion.1.squares_ref, bf16[128,1024]{1,0:T(8,128)(2,1)S(1)} %shard_map.91.refs_0_, bf16[128,512]{1,0:T(8,128)(2,1)S(1)} %shard_map.92.refs_1_, bf16[128,1024]{1,0:T(8,128)(2,1)S(1)} %collective-permute-done.23.refs_2_, ...), custom_call_target="tpu_custom_call" | custom-call | bytes 1835520 | tf_op jit(solution)/shard_map/pallas_call | solution.py:48
  118.6 0.4 collective-permute-start.25
  118.9 0.1 pad_add_fusion.starts_ref
  119.0 4.7 %collective-permute-done.25.refs_1_ = bf16[128,512]{1,0:T(8,128)(2,1)S(1)} collective-permute-done((bf16[128,512]{1,0:T(8,128)(2,1)S(1)}, bf16[128,512]{1,0:T(8,128)(2,1)S(1)}, u32[]{:S(2)}, u32[]{:S(2)}) %collective-permute-start.25) | collective-permute-done | bytes 131104 | tf_op jit(solution)/shard_map/ppermute | solution.py:437
  123.7 1.4 %shard_map.97 = bf16[128,4096]{1,0:T(8,128)(2,1)} custom-call(s32[2]{0:T(128)S(1)} %pad_add_fusion.starts_ref, f32[1,128]{1,0:T(1,128)S(1)} %slice_add_fusion.1.squares_ref, bf16[128,512]{1,0:T(8,128)(2,1)S(1)} %get-tuple-element.71.refs_0_, bf16[128,512]{1,0:T(8,128)(2,1)S(1)} %collective-permute-done.25.refs_1_, ...), custom_call_target="tpu_custom_call", output_to_operand_aliasing={{}: (4, {})} | custom-call | bytes 524288 | tf_op jit(solution)/shard_map/pallas_call | solution.py:347
  (45 shorter events, 0.4 us)
Async XLA Ops:
  0.0 28.5 %collective-permute-start.3 = (bf16[1024,512]{1,0:T(8,128)(2,1)}, bf16[1024,512]{1,0:T(8,128)(2,1)}, u32[]{:S(2)}, u32[]{:S(2)}) collective-permute-start(bf16[1024,512]{1,0:T(8,128)(2,1)} %refs_1_.3), channel_id=1, source_target_pairs={{0,8},{4,12},{8,0},{12,4},{16,24},{20,28},{24,16},{28,20},{1,9},{5... | collective-permute-start | bytes 3145736 | tf_op jit(solution)/shard_map/ppermute | solution.py:378
  3.0 25.4 %collective-permute-start.2 = (bf16[1024,512]{1,0:T(8,128)(2,1)}, bf16[1024,512]{1,0:T(8,128)(2,1)}, u32[]{:S(2)}, u32[]{:S(2)}) collective-permute-start(bf16[1024,512]{1,0:T(8,128)(2,1)} %refs_1_.3), channel_id=1, source_target_pairs={{8,16},{12,20},{16,8},{20,12},{9,17},{13,21},{17,9},{21,13},{10,18... | collective-permute-start | bytes 3145736 | tf_op jit(solution)/shard_map/ppermute | solution.py:378
  4.7 1.2 copy-start
  5.9 1.2 copy-start.2
  7.1 2.0 %copy-start.1 = (bf16[512,1024]{1,0:T(8,128)(2,1)S(1)}, bf16[512,1024]{1,0:T(8,128)(2,1)}, u32[]{:S(2)}) copy-start(bf16[512,1024]{1,0:T(8,128)(2,1)} %k_ref.7) | copy-start | bytes 3145732
  7.6 5.0 %collective-permute-start = (bf16[4,128,128]{2,1,0:T(8,128)(2,1)S(1)}, bf16[4,128,128]{2,1,0:T(8,128)(2,1)S(1)}, u32[]{:S(2)}, u32[]{:S(2)}) collective-permute-start(bf16[4,128,128]{2,1,0:T(8,128)(2,1)S(1)} %shard_map.74), channel_id=1, source_target_pairs={{0,4},{4,0},{8,12},{12,8},{16,20},{20,16},{24,28},{28,24},{1,5},{5... | collective-permute-start | bytes 393224 | tf_op jit(solution)/shard_map/ppermute | solution.py:123
  9.2 22.6 %copy-start.4 = (bf16[512,1024]{1,0:T(8,128)(2,1)S(1)}, bf16[512,1024]{1,0:T(8,128)(2,1)}, u32[]{:S(2)}) copy-start(bf16[512,1024]{1,0:T(8,128)(2,1)} %q_ref.5) | copy-start | bytes 3145732
  9.7 22.2 %copy-start.3 = (bf16[512,1024]{1,0:T(8,128)(2,1)S(1)}, bf16[512,1024]{1,0:T(8,128)(2,1)}, u32[]{:S(2)}) copy-start(bf16[512,1024]{1,0:T(8,128)(2,1)} %v_ref.7) | copy-start | bytes 3145732
  12.7 15.8 %collective-permute-start.1 = (bf16[4,128,128]{2,1,0:T(8,128)(2,1)S(1)}, bf16[4,128,128]{2,1,0:T(8,128)(2,1)S(1)}, u32[]{:S(2)}, u32[]{:S(2)}) collective-permute-start(bf16[4,128,128]{2,1,0:T(8,128)(2,1)S(1)} %shard_map.75), channel_id=1, source_target_pairs={{0,8},{4,12},{16,24},{20,28},{1,9},{5,13},{17,25},{21,29},{2,10},{... | collective-permute-start | bytes 393224 | tf_op jit(solution)/shard_map/ppermute | solution.py:126
  28.5 0.7 copy-start.6
  29.2 3.7 %collective-permute-start.5 = (bf16[4,128,128]{2,1,0:T(8,128)(2,1)}, bf16[4,128,128]{2,1,0:T(8,128)(2,1)}, u32[]{:S(2)}, u32[]{:S(2)}) collective-permute-start(bf16[4,128,128]{2,1,0:T(8,128)(2,1)} %shard_map.76), channel_id=1, source_target_pairs={{8,24},{12,28},{9,25},{13,29},{10,26},{14,30},{11,27},{15,31}} | collective-permute-start | bytes 393224 | tf_op jit(solution)/shard_map/ppermute | solution.py:130
  30.5 2.4 %collective-permute-start.4 = (bf16[4,128,128]{2,1,0:T(8,128)(2,1)}, bf16[4,128,128]{2,1,0:T(8,128)(2,1)}, u32[]{:S(2)}, u32[]{:S(2)}) collective-permute-start(bf16[4,128,128]{2,1,0:T(8,128)(2,1)} %shard_map.76), channel_id=1, source_target_pairs={{8,16},{12,20},{9,17},{13,21},{10,18},{14,22},{11,19},{15,23}} | collective-permute-start | bytes 393224 | tf_op jit(solution)/shard_map/ppermute | solution.py:129
  31.8 2.8 %copy-start.7 = (bf16[4,128,128]{2,1,0:T(8,128)(2,1)S(1)}, bf16[4,128,128]{2,1,0:T(8,128)(2,1)}, u32[]{:S(2)}) copy-start(bf16[4,128,128]{2,1,0:T(8,128)(2,1)} %copy-done.6) | copy-start | bytes 393220
  32.9 17.6 %collective-permute-start.9 = (bf16[1024,512]{1,0:T(8,128)(2,1)}, bf16[1024,512]{1,0:T(8,128)(2,1)}, u32[]{:S(2)}, u32[]{:S(2)}) collective-permute-start(bf16[1024,512]{1,0:T(8,128)(2,1)} %collective-permute-done.3.refs_2_), channel_id=1, source_target_pairs={{8,16},{12,20},{16,8},{20,12},{9,17},{13,21},{17,9},{21,13},{10,18... | collective-permute-start | bytes 3145736 | tf_op jit(solution)/shard_map/ppermute | solution.py:378
  35.8 5.0 %collective-permute-start.6 = (bf16[4,128,128]{2,1,0:T(8,128)(2,1)S(1)}, bf16[4,128,128]{2,1,0:T(8,128)(2,1)S(1)}, u32[]{:S(2)}, u32[]{:S(2)}) collective-permute-start(bf16[4,128,128]{2,1,0:T(8,128)(2,1)S(1)} %get-tuple-element.41), channel_id=1, source_target_pairs={{0,4},{4,0},{8,12},{12,8},{16,20},{20,16},{24,28},{28,24},{1,5},{5... | collective-permute-start | bytes 393224 | tf_op jit(solution)/shard_map/ppermute | solution.py:137
  37.4 3.4 %copy-start.5 = (bf16[512,1024]{1,0:T(8,128)(2,1)S(1)}, bf16[512,1024]{1,0:T(8,128)(2,1)}, u32[]{:S(2)}) copy-start(bf16[512,1024]{1,0:T(8,128)(2,1)} %gate_ref.1) | copy-start | bytes 3145732
  37.4 3.4 %copy-start.8 = (f32[8,128,128]{2,1,0:T(8,128)S(1)}, f32[8,128,128]{2,1,0:T(8,128)}, u32[]{:S(2)}) copy-start(f32[8,128,128]{2,1,0:T(8,128)} %kv_ref.1) | copy-start | bytes 1572868
  37.4 3.4 %copy-start.9 = (f32[4096]{0:T(1024)S(1)}, f32[4096]{0:T(1024)}, u32[]{:S(2)}) copy-start(f32[4096]{0:T(1024)} %param.12) | copy-start | bytes 49156
  37.4 37.3 %collective-permute-start.10 = (bf16[1024,512]{1,0:T(8,128)(2,1)}, bf16[1024,512]{1,0:T(8,128)(2,1)}, u32[]{:S(2)}, u32[]{:S(2)}) collective-permute-start(bf16[1024,512]{1,0:T(8,128)(2,1)} %collective-permute-done.2.refs_1_), channel_id=1, source_target_pairs={{8,0},{12,4},{16,24},{20,28},{9,1},{13,5},{17,25},{21,29},{10,2},{... | collective-permute-start | bytes 3145736 | tf_op jit(solution)/shard_map/ppermute | solution.py:378
  42.6 34.4 %collective-permute-start.11 = (bf16[512,1024]{1,0:T(8,128)(2,1)S(1)}, bf16[512,1024]{1,0:T(8,128)(2,1)S(1)}, u32[]{:S(2)}, u32[]{:S(2)}) collective-permute-start(bf16[512,1024]{1,0:T(8,128)(2,1)S(1)} %get-tuple-element.43.refs_0_), channel_id=1, source_target_pairs={{0,4},{4,0},{8,12},{12,8},{16,20},{20,16},{24,28},{28,24},{1,5},{5... | collective-permute-start | bytes 3145736 | tf_op jit(solution)/shard_map/ppermute | solution.py:398
  44.1 1.1 collective-permute-start.7
  45.3 6.6 %collective-permute-start.8 = (f32[1,128]{1,0:T(1,128)S(1)}, f32[1,128]{1,0:T(1,128)S(1)}, u32[]{:S(2)}, u32[]{:S(2)}) collective-permute-start(f32[1,128]{1,0:T(1,128)S(1)} %slice.15), channel_id=1, source_target_pairs={{0,2},{1,3},{2,0},{3,1},{4,6},{5,7},{6,4},{7,5},{8,10},{9,11},{10,... | collective-permute-start | bytes 1544 | tf_op jit(solution)/shard_map/ppermute | solution.py:403
  46.8 1.2 copy-start.10
  50.5 31.9 %collective-permute-start.12 = (bf16[256,1024]{1,0:T(8,128)(2,1)S(1)}, bf16[256,1024]{1,0:T(8,128)(2,1)S(1)}, u32[]{:S(2)}, u32[]{:S(2)}) collective-permute-start(bf16[256,1024]{1,0:T(8,128)(2,1)S(1)} %get-tuple-element.44), channel_id=1, source_target_pairs={{0,1},{1,0},{2,3},{3,2},{4,5},{5,4},{6,7},{7,6},{8,9},{9,8},{10,11... | collective-permute-start | bytes 1572872 | tf_op jit(solution)/shard_map/ppermute | solution.py:427
  50.6 51.9 %collective-permute-start.20 = (bf16[1024,512]{1,0:T(8,128)(2,1)}, bf16[1024,512]{1,0:T(8,128)(2,1)S(1)}, u32[]{:S(2)}, u32[]{:S(2)}) collective-permute-start(bf16[1024,512]{1,0:T(8,128)(2,1)} %collective-permute-done.9.refs_2_), channel_id=1, source_target_pairs={{8,0},{12,4},{16,24},{20,28},{9,1},{13,5},{17,25},{21,29},{10,2},{... | collective-permute-start | bytes 3145736 | tf_op jit(solution)/shard_map/ppermute | solution.py:378
  51.9 25.1 %copy-start.11 = (bf16[1024,512]{1,0:T(8,128)(2,1)S(1)}, bf16[1024,512]{1,0:T(8,128)(2,1)}, u32[]{:S(2)}) copy-start(bf16[1024,512]{1,0:T(8,128)(2,1)} %refs_1_.3) | copy-start | bytes 3145732
  79.4 4.7 %collective-permute-start.16 = (bf16[256,1024]{1,0:T(8,128)(2,1)S(1)}, bf16[256,1024]{1,0:T(8,128)(2,1)S(1)}, u32[]{:S(2)}, u32[]{:S(2)}) collective-permute-start(bf16[256,1024]{1,0:T(8,128)(2,1)S(1)} %get-tuple-element.50), channel_id=1, source_target_pairs={{0,1},{1,0},{2,3},{3,2},{4,5},{5,4},{6,7},{7,6},{8,9},{9,8},{10,11... | collective-permute-start | bytes 1572872 | tf_op jit(solution)/shard_map/ppermute | solution.py:427
  79.5 5.2 %collective-permute-start.14 = (bf16[256,512]{1,0:T(8,128)(2,1)S(1)}, bf16[256,512]{1,0:T(8,128)(2,1)S(1)}, u32[]{:S(2)}, u32[]{:S(2)}) collective-permute-start(bf16[256,512]{1,0:T(8,128)(2,1)S(1)} %get-tuple-element.48), channel_id=1, source_target_pairs={{0,1},{1,0},{2,3},{3,2},{4,5},{5,4},{6,7},{7,6},{8,9},{9,8},{10,11... | collective-permute-start | bytes 786440 | tf_op jit(solution)/shard_map/ppermute | solution.py:427
  82.3 4.1 %collective-permute-start.18 = (bf16[256,512]{1,0:T(8,128)(2,1)S(1)}, bf16[256,512]{1,0:T(8,128)(2,1)S(1)}, u32[]{:S(2)}, u32[]{:S(2)}) collective-permute-start(bf16[256,512]{1,0:T(8,128)(2,1)S(1)} %get-tuple-element.52), channel_id=1, source_target_pairs={{0,1},{1,0},{2,3},{3,2},{4,5},{5,4},{6,7},{7,6},{8,9},{9,8},{10,11... | collective-permute-start | bytes 786440 | tf_op jit(solution)/shard_map/ppermute | solution.py:427
  82.5 9.2 %collective-permute-start.13 = (bf16[128,1024]{1,0:T(8,128)(2,1)S(1)}, bf16[128,1024]{1,0:T(8,128)(2,1)S(1)}, u32[]{:S(2)}, u32[]{:S(2)}) collective-permute-start(bf16[128,1024]{1,0:T(8,128)(2,1)S(1)} %get-tuple-element.54), channel_id=1, source_target_pairs={{0,2},{1,3},{2,0},{3,1},{4,6},{5,7},{6,4},{7,5},{8,10},{9,11},{10,... | collective-permute-start | bytes 786440 | tf_op jit(solution)/shard_map/ppermute | solution.py:427
  84.2 18.3 %collective-permute-start.17 = (bf16[128,1024]{1,0:T(8,128)(2,1)S(1)}, bf16[128,1024]{1,0:T(8,128)(2,1)S(1)}, u32[]{:S(2)}, u32[]{:S(2)}) collective-permute-start(bf16[128,1024]{1,0:T(8,128)(2,1)S(1)} %get-tuple-element.58), channel_id=1, source_target_pairs={{0,2},{1,3},{2,0},{3,1},{4,6},{5,7},{6,4},{7,5},{8,10},{9,11},{10,... | collective-permute-start | bytes 786440 | tf_op jit(solution)/shard_map/ppermute | solution.py:427
  84.8 15.3 %collective-permute-start.15 = (bf16[128,512]{1,0:T(8,128)(2,1)S(1)}, bf16[128,512]{1,0:T(8,128)(2,1)S(1)}, u32[]{:S(2)}, u32[]{:S(2)}) collective-permute-start(bf16[128,512]{1,0:T(8,128)(2,1)S(1)} %get-tuple-element.56), channel_id=1, source_target_pairs={{0,2},{1,3},{2,0},{3,1},{4,6},{5,7},{6,4},{7,5},{8,10},{9,11},{10,... | collective-permute-start | bytes 393224 | tf_op jit(solution)/shard_map/ppermute | solution.py:427
  86.5 16.0 %collective-permute-start.19 = (bf16[128,512]{1,0:T(8,128)(2,1)S(1)}, bf16[128,512]{1,0:T(8,128)(2,1)S(1)}, u32[]{:S(2)}, u32[]{:S(2)}) collective-permute-start(bf16[128,512]{1,0:T(8,128)(2,1)S(1)} %get-tuple-element.60), channel_id=1, source_target_pairs={{0,2},{1,3},{2,0},{3,1},{4,6},{5,7},{6,4},{7,5},{8,10},{9,11},{10,... | collective-permute-start | bytes 393224 | tf_op jit(solution)/shard_map/ppermute | solution.py:427
  105.0 2.0 %collective-permute-start.21 = (bf16[256,1024]{1,0:T(8,128)(2,1)S(1)}, bf16[256,1024]{1,0:T(8,128)(2,1)S(1)}, u32[]{:S(2)}, u32[]{:S(2)}) collective-permute-start(bf16[256,1024]{1,0:T(8,128)(2,1)S(1)} %get-tuple-element.63), channel_id=1, source_target_pairs={{0,1},{1,0},{2,3},{3,2},{4,5},{5,4},{6,7},{7,6},{8,9},{9,8},{10,11... | collective-permute-start | bytes 1572872 | tf_op jit(solution)/shard_map/ppermute | solution.py:427
  105.1 11.6 %collective-permute-start.23 = (bf16[128,1024]{1,0:T(8,128)(2,1)S(1)}, bf16[128,1024]{1,0:T(8,128)(2,1)S(1)}, u32[]{:S(2)}, u32[]{:S(2)}) collective-permute-start(bf16[128,1024]{1,0:T(8,128)(2,1)S(1)} %shard_map.93), channel_id=1, source_target_pairs={{0,4},{4,0},{8,12},{12,8},{16,20},{20,16},{24,28},{28,24},{1,5},{5... | collective-permute-start | bytes 786440 | tf_op jit(solution)/shard_map/ppermute | solution.py:437
  107.0 11.5 %collective-permute-start.22 = (bf16[128,1024]{1,0:T(8,128)(2,1)S(1)}, bf16[128,1024]{1,0:T(8,128)(2,1)S(1)}, u32[]{:S(2)}, u32[]{:S(2)}) collective-permute-start(bf16[128,1024]{1,0:T(8,128)(2,1)S(1)} %get-tuple-element.65), channel_id=1, source_target_pairs={{0,2},{1,3},{2,0},{3,1},{4,6},{5,7},{6,4},{7,5},{8,10},{9,11},{10,... | collective-permute-start | bytes 786440 | tf_op jit(solution)/shard_map/ppermute | solution.py:427
  108.7 8.0 %collective-permute-start.24 = (bf16[128,512]{1,0:T(8,128)(2,1)S(1)}, bf16[128,512]{1,0:T(8,128)(2,1)S(1)}, u32[]{:S(2)}, u32[]{:S(2)}) collective-permute-start(bf16[128,512]{1,0:T(8,128)(2,1)S(1)} %shard_map.94), channel_id=1, source_target_pairs={{0,4},{4,0},{8,12},{12,8},{16,20},{20,16},{24,28},{28,24},{1,5},{5... | collective-permute-start | bytes 393224 | tf_op jit(solution)/shard_map/ppermute | solution.py:437
  118.6 5.2 %collective-permute-start.25 = (bf16[128,512]{1,0:T(8,128)(2,1)S(1)}, bf16[128,512]{1,0:T(8,128)(2,1)S(1)}, u32[]{:S(2)}, u32[]{:S(2)}) collective-permute-start(bf16[128,512]{1,0:T(8,128)(2,1)S(1)} %get-tuple-element.72), channel_id=1, source_target_pairs={{0,4},{4,0},{8,12},{12,8},{16,20},{20,16},{24,28},{28,24},{1,5},{5... | collective-permute-start | bytes 393224 | tf_op jit(solution)/shard_map/ppermute | solution.py:437

commit v9 on v8

--- a/solution.py
+++ b/solution.py
@@ -30,7 +30,8 @@
     return [(h, h ^ bit) for h in range(n_head)]
 
 
-SWAP_OUTER = [(0, 1), (1, 0), (2, 3), (3, 2)]
+SWAP_NEXT = [(z, z ^ 1) for z in range(LINE)]
+SWAP_HALVES = [(z, z ^ 2) for z in range(LINE)]
 SWAP_MIDDLE = [(1, 2), (2, 1)]
 TO_ENDS = [(1, 0), (2, 3)]
 
@@ -103,7 +104,7 @@
     )[0]
 
 
-def state_prefix(key_input, value_input, n_seq, place, early):
+def state_prefix(key_input, value_input, n_seq, place):
     inner = n_seq // LINE
     i = place % inner
     heads = key_input.shape[1] // DH
@@ -124,7 +125,6 @@
         members.append((i - turn) % inner)
     (first,) = combine(values, [jnp.bfloat16])
     from_left = lax.ppermute(first, "seq", line_pairs(n_seq, [(0, 1), (2, 3)]))
-    from_left = hold(from_left, *early)
     (second,) = combine(values + [from_left], [jnp.bfloat16])
     near = lax.ppermute(second, "seq", line_pairs(n_seq, [(1, 2)]))
     far = lax.ppermute(second, "seq", line_pairs(n_seq, [(1, 3)]))
@@ -377,18 +377,17 @@
     def along(value, hops):
         return lax.ppermute(value, "seq", line_pairs(n_seq, hops))
 
-    w_mid1 = along(out_weight, SWAP_MIDDLE)
-    w_pair = along(out_weight, SWAP_OUTER)
-    terms, stepped = state_prefix(key_input, value_input, n_seq, place, [w_mid1, w_pair])
+    terms, stepped = state_prefix(key_input, value_input, n_seq, place)
     some = heads // 2
     inners = [
         causal_part(queries, key_input, value_input, 0, some),
         causal_part(queries, key_input, value_input, some, heads - some),
     ]
 
-    w_end1 = along(hold(w_mid1, *stepped), TO_ENDS)
-    w_mid2 = along(hold(w_pair, *stepped), SWAP_MIDDLE)
-    w_end2 = along(w_mid2, TO_ENDS)
+    own_columns = hold(out_weight, *stepped)
+    w_halves = along(own_columns, SWAP_HALVES)
+    w_next = along(own_columns, SWAP_NEXT)
+    w_middle = along(own_columns, SWAP_MIDDLE)
 
     bits = n_head.bit_length() - 1
     order = [int(format(j, "b").zfill(bits)[::-1], 2) for j in range(n_head)] if bits else [0]
@@ -405,13 +404,12 @@
         bit *= 2
 
     is_end = (z == 0) | (z == LINE - 1)
-    low = z < LINE // 2
     flag = scalars(is_end)
 
     rows_list = [hidden] + others
 
-    owners = [z, z ^ 1, jnp.where(low, 2, 1), jnp.where(low, 3, 0)]
-    blocks = [(out_weight,), (w_pair,), (w_mid1, w_end1), (w_mid2, w_end2)]
+    owners = [z ^ block for block in range(LINE)]
+    blocks = [(out_weight,), (w_next,), (w_halves,)]
 
     def summed(parts, pins, pin_end=None):
         weights = sorted({block for _, own in parts for block in own})
@@ -444,15 +442,22 @@
     in_kernel = width % DH == 0 and out_rows == DH
 
     pieces, pins, ends = [], [], []
-    groups = [(turns[:1], [0, 1]), (turns[:1], [2]), (turns[1:], [0, 1]), (turns[1:], [2])]
-    for members, some in groups:
+
+    def group(members, some):
         if members:
             more, sent, end = summed([(turn, some) for turn in members], pins)
-            pieces += more
+            pieces.extend(more)
             ends.append(end)
-            pins = [sent, squares, w_mid2]
+            pins[:] = [sent, squares]
+
+    group(turns[:1], [0])
+    group(turns[1:], [0])
+    w_ends = along(hold(w_halves, *ends), TO_ENDS)
+    blocks.append((w_middle, w_ends))
+    group(turns[:1], [1, 2])
+    group(turns[1:], [1, 2])
     filled = placed(None, pieces, squares, width, shape, total_width) if in_kernel else None
-    last, _, _ = summed([(turn, [3]) for turn in turns], [sent, *ends], filled)
+    last, _, _ = summed([(turn, [3]) for turn in turns], [*pins, *ends], filled)
     if in_kernel:
         return placed(filled, last, squares, width, shape, total_width)
     scale = lax.rsqrt(squares.reshape(out_rows, 1) / total_width + epsilon)

time: 126 us -> 127 us (level)
  starting transfers between devices: 30.8 us -> 35.9 us
  waiting for transfers between devices: 67.6 us -> 64.5 us
    ppermute x1, waiting for transfers between devices: 10.4 us -> 2.5 us  [state_prefix(): from_left = lax.ppermute(first, 'seq', line_pairs(n_seq, [(0, 1), (2, 3)]))]
    ppermute x1, waiting for transfers between devices: 0.01 us -> 6.17 us  [shards(): lax.ppermute(hidden, 'seq', turn_pairs(n_seq, turn))]
    ppermute x5 -> x4, starting transfers between devices: 9.01 us -> 11.6 us  [along(): return lax.ppermute(value, 'seq', line_pairs(n_seq, hops))]
    ppermute x10, waiting for transfers between devices: 17.1 us -> 14.6 us  [summed(): got = lax.ppermute(sent, 'head', flip_pairs(n_head, bit))]
    ppermute x10, starting transfers between devices: 6.75 us -> 8.48 us  [summed(): got = lax.ppermute(sent, 'head', flip_pairs(n_head, bit))]
    ppermute x1, starting transfers between devices: 5.34 us -> 3.74 us  [state_prefix(): from_left = lax.ppermute(first, 'seq', line_pairs(n_seq, [(0, 1), (2, 3)]))]
    ppermute x1, starting transfers between devices: 1.55 us -> 3 us  [state_prefix(): values.append(lax.ppermute(sends[turn - 1], 'seq', turn_pairs(n_seq, turn)))]
    ppermute x1, waiting for transfers between devices: 0.89 us -> 2.31 us  [state_prefix(): terms.append(lax.ppermute(befores[turn], 'seq', turn_pairs(n_seq, turn)))]
  transfers between devices with their start and end apart: 26 -> 25, of which waited for: 11 -> 12; matrix products, arithmetic and copies ran while one was open for 0% -> 0% of each run, Pallas kernels for 14% -> 11%
where the time goes in v9:
time: 127 us
  waiting for transfers between devices  64.5 us (51%)
  starting transfers between devices  35.9 us (28%)
  Pallas kernels  21.2 us (17%)
  local copies, waits for them, and re-layouts  4.45 us (4%)
    ppermute x4, waiting for transfers between devices, along(): return lax.ppermute(value, 'seq', line_pairs(n_seq, hops))  23 us
    pallas_call x24, Pallas kernels, local_call(): pl.pallas_call(kernel, in_specs=[pl.BlockSpec(memory_space=pltpu.SMEM)] +...  19.8 us
    ppermute x10, waiting for transfers between devices, summed(): got = lax.ppermute(sent, 'head', flip_pairs(n_head, bit))  14.6 us
    ppermute x3, waiting for transfers between devices, summed(): piece = lax.ppermute(piece, 'seq', turn_pairs(n_seq, -turn))  11.8 us
    ppermute x4, starting transfers between devices, along(): return lax.ppermute(value, 'seq', line_pairs(n_seq, hops))  11.6 us
    ppermute x10, starting transfers between devices, summed(): got = lax.ppermute(sent, 'head', flip_pairs(n_head, bit))  8.48 us
    ppermute x1, waiting for transfers between devices, shards(): lax.ppermute(hidden, 'seq', turn_pairs(n_seq, turn))  6.17 us
    unnamed x24, local copies, waits for them, and re-layouts  4.36 us
  transfers between devices with their start and end apart: 25, of which 12 were waited for; matrix products, arithmetic and copies ran while one was open for 0% of the time, Pallas kernels for 11%

profile of v9, /device:TPU:0, one launch (start us, length us, event | category | flops | bytes accessed | tf_op | source)
XLA Modules:
  0.0 126.6 jit_solution(796171913872346734)
XLA Ops:
  0.0 1.2 copy-done
  1.2 1.2 copy-done.2
  2.5 0.5 shard_map.74
  2.9 3.0 %collective-permute-start = (bf16[4,128,128]{2,1,0:T(8,128)(2,1)S(1)}, bf16[4,128,128]{2,1,0:T(8,128)(2,1)S(1)}, u32[]{:S(2)}, u32[]{:S(2)}) collective-permute-start(bf16[4,128,128]{2,1,0:T(8,128)(2,1)S(1)} %shard_map.74), channel_id=1, source_target_pairs={{0,4},{4,0},{8,12},{12,8},{16,20},{20,16},{24,28},{28,24},{1,5},{5... | collective-permute-start | bytes 393224 | tf_op jit(solution)/shard_map/ppermute | solution.py:124
  5.9 0.5 shard_map.73.refs_0_.refs_3_
  6.4 3.0 %collective-permute-done.refs_1_.refs_4_ = bf16[4,128,128]{2,1,0:T(8,128)(2,1)S(1)} collective-permute-done((bf16[4,128,128]{2,1,0:T(8,128)(2,1)S(1)}, bf16[4,128,128]{2,1,0:T(8,128)(2,1)S(1)}, u32[]{:S(2)}, u32[]{:S(2)}) %collective-permute-start) | collective-permute-done | bytes 131104 | tf_op jit(solution)/shard_map/ppermute | solution.py:124
  9.5 3.7 %collective-permute-start.1 = (bf16[4,128,128]{2,1,0:T(8,128)(2,1)S(1)}, bf16[4,128,128]{2,1,0:T(8,128)(2,1)S(1)}, u32[]{:S(2)}, u32[]{:S(2)}) collective-permute-start(bf16[4,128,128]{2,1,0:T(8,128)(2,1)S(1)} %shard_map.75), channel_id=1, source_target_pairs={{0,8},{4,12},{16,24},{20,28},{1,9},{5,13},{17,25},{21,29},{2,10},{... | collective-permute-start | bytes 393224 | tf_op jit(solution)/shard_map/ppermute | solution.py:127
  13.2 2.5 %collective-permute-done.1.refs_2_.refs_0_ = bf16[4,128,128]{2,1,0:T(8,128)(2,1)S(1)} collective-permute-done((bf16[4,128,128]{2,1,0:T(8,128)(2,1)S(1)}, bf16[4,128,128]{2,1,0:T(8,128)(2,1)S(1)}, u32[]{:S(2)}, u32[]{:S(2)}) %collective-permute-start.1) | collective-permute-done | bytes 131104 | tf_op jit(solution)/shard_map/ppermute | solution.py:127
  15.7 0.7 shard_map.76
  16.4 1.3 %collective-permute-start.2 = (bf16[4,128,128]{2,1,0:T(8,128)(2,1)}, bf16[4,128,128]{2,1,0:T(8,128)(2,1)}, u32[]{:S(2)}, u32[]{:S(2)}) collective-permute-start(bf16[4,128,128]{2,1,0:T(8,128)(2,1)} %shard_map.76), channel_id=1, source_target_pairs={{8,16},{12,20},{9,17},{13,21},{10,18},{14,22},{11,19},{15,23}} | collective-permute-start | bytes 393224 | tf_op jit(solution)/shard_map/ppermute | solution.py:129
  17.7 1.3 %collective-permute-start.3 = (bf16[4,128,128]{2,1,0:T(8,128)(2,1)}, bf16[4,128,128]{2,1,0:T(8,128)(2,1)}, u32[]{:S(2)}, u32[]{:S(2)}) collective-permute-start(bf16[4,128,128]{2,1,0:T(8,128)(2,1)} %shard_map.76), channel_id=1, source_target_pairs={{8,24},{12,28},{9,25},{13,29},{10,26},{14,30},{11,27},{15,31}} | collective-permute-start | bytes 393224 | tf_op jit(solution)/shard_map/ppermute | solution.py:130
  19.0 1.1 shard_map.78.refs_2_
  20.1 1.0 copy-done.5
  21.1 0.1 add_convert_fusion.masks_ref
  21.2 0.9 copy-done.9
  22.1 1.1 shard_map.77
  23.3 1.6 %collective-permute-start.4 = (bf16[4,128,128]{2,1,0:T(8,128)(2,1)S(1)}, bf16[4,128,128]{2,1,0:T(8,128)(2,1)S(1)}, u32[]{:S(2)}, u32[]{:S(2)}) collective-permute-start(bf16[4,128,128]{2,1,0:T(8,128)(2,1)S(1)} %get-tuple-element.39), channel_id=1, source_target_pairs={{0,4},{4,0},{8,12},{12,8},{16,20},{20,16},{24,28},{28,24},{1,5},{5... | collective-permute-start | bytes 393224 | tf_op jit(solution)/shard_map/ppermute | solution.py:137
  24.8 1.1 shard_map.79.refs_3_
  25.9 0.1 pad_add_fusion.1.place_ref
  26.0 2.3 %collective-permute-done.4.refs_1_ = bf16[4,128,128]{2,1,0:T(8,128)(2,1)S(1)} collective-permute-done((bf16[4,128,128]{2,1,0:T(8,128)(2,1)S(1)}, bf16[4,128,128]{2,1,0:T(8,128)(2,1)S(1)}, u32[]{:S(2)}, u32[]{:S(2)}) %collective-permute-start.4) | collective-permute-done | bytes 131104 | tf_op jit(solution)/shard_map/ppermute | solution.py:137
  28.3 1.8 %shard_map.80 = (bf16[512,1024]{1,0:T(8,128)(2,1)S(1)}, f32[4,128]{1,0:T(4,128)S(1)}) custom-call(s32[2]{0:T(128)S(1)} %pad_add_fusion.1.place_ref, bf16[512,1024]{1,0:T(8,128)(2,1)S(1)} %copy-done.4, bf16[512,1024]{1,0:T(8,128)(2,1)S(1)} %copy-done.7, f32[32,1,128]{2,1,0:T(1,128)S(1)} %bitcast.16, f32[8,128,128]{2,1,0:T(8,128)S(1)} %copy-done.10, ...), custom_call_target="tpu_custom_call" | custom-call | flops 268435456 | bytes 6178816 | tf_op jit(solution)/shard_map/pallas_call | solution.py:49
  30.1 1.6 %collective-permute-start.7 = (bf16[512,1024]{1,0:T(8,128)(2,1)S(1)}, bf16[512,1024]{1,0:T(8,128)(2,1)S(1)}, u32[]{:S(2)}, u32[]{:S(2)}) collective-permute-start(bf16[512,1024]{1,0:T(8,128)(2,1)S(1)} %get-tuple-element.41.refs_0_), channel_id=1, source_target_pairs={{0,4},{4,0},{8,12},{12,8},{16,20},{20,16},{24,28},{28,24},{1,5},{5... | collective-permute-start | bytes 3145736 | tf_op jit(solution)/shard_map/ppermute | solution.py:397
  31.6 7.5 %collective-permute-start.9 = (bf16[1024,512]{1,0:T(8,128)(2,1)}, bf16[1024,512]{1,0:T(8,128)(2,1)}, u32[]{:S(2)}, u32[]{:S(2)}) collective-permute-start(bf16[1024,512]{1,0:T(8,128)(2,1)} %refs_1_.3), channel_id=1, source_target_pairs={{0,16},{4,20},{8,24},{12,28},{16,0},{20,4},{24,8},{28,12},{1,17},{... | collective-permute-start | bytes 3145736 | tf_op jit(solution)/shard_map/ppermute | solution.py:378
  39.1 2.1 %collective-permute-start.8 = (bf16[1024,512]{1,0:T(8,128)(2,1)}, bf16[1024,512]{1,0:T(8,128)(2,1)}, u32[]{:S(2)}, u32[]{:S(2)}) collective-permute-start(bf16[1024,512]{1,0:T(8,128)(2,1)} %refs_1_.3), channel_id=1, source_target_pairs={{0,8},{4,12},{8,0},{12,4},{16,24},{20,28},{24,16},{28,20},{1,9},{5... | collective-permute-start | bytes 3145736 | tf_op jit(solution)/shard_map/ppermute | solution.py:378
  41.3 1.1 collective-permute-done.5
  42.4 1.5 %collective-permute-start.6 = (f32[1,128]{1,0:T(1,128)S(1)}, f32[1,128]{1,0:T(1,128)S(1)}, u32[]{:S(2)}, u32[]{:S(2)}) collective-permute-start(f32[1,128]{1,0:T(1,128)S(1)} %slice.15), channel_id=1, source_target_pairs={{0,2},{1,3},{2,0},{3,1},{4,6},{5,7},{6,4},{7,5},{8,10},{9,11},{10,... | collective-permute-start | bytes 1544 | tf_op jit(solution)/shard_map/ppermute | solution.py:402
  43.9 1.9 %shard_map.81 = (bf16[256,512]{1,0:T(8,128)(2,1)S(1)}, f32[256,512]{1,0:T(8,128)S(1)}) custom-call(s32[1]{0:T(128)} %bitcast.9.flag_ref, bf16[512,1024]{1,0:T(8,128)(2,1)S(1)} %get-tuple-element.41.refs_0_, bf16[1024,512]{1,0:T(8,128)(2,1)} %refs_1_.3), custom_call_target="tpu_custom_call" | custom-call | flops 536870912 | bytes 2883584 | tf_op jit(solution)/shard_map/pallas_call | solution.py:49
  45.9 0.1 collective-permute-start.10
  46.0 0.0 collective-permute-done.6
  46.0 6.2 %collective-permute-done.7.refs_0_.refs_1_ = bf16[512,1024]{1,0:T(8,128)(2,1)S(1)} collective-permute-done((bf16[512,1024]{1,0:T(8,128)(2,1)S(1)}, bf16[512,1024]{1,0:T(8,128)(2,1)S(1)}, u32[]{:S(2)}, u32[]{:S(2)}) %collective-permute-start.7) | collective-permute-done | bytes 1048608 | tf_op jit(solution)/shard_map/ppermute | solution.py:397
  52.1 1.9 %shard_map.82 = (bf16[256,512]{1,0:T(8,128)(2,1)S(1)}, f32[256,512]{1,0:T(8,128)S(1)}) custom-call(s32[1]{0:T(128)} %bitcast.9.flag_ref, bf16[512,1024]{1,0:T(8,128)(2,1)S(1)} %collective-permute-done.7.refs_0_.refs_1_, bf16[1024,512]{1,0:T(8,128)(2,1)} %refs_1_.3), custom_call_target="tpu_custom_call" | custom-call | flops 536870912 | bytes 2883584 | tf_op jit(solution)/shard_map/pallas_call | solution.py:49
  54.1 0.1 collective-permute-start.12
  54.2 0.1 shard_map.85
  54.2 1.6 %collective-permute-start.11 = (bf16[128,512]{1,0:T(8,128)(2,1)S(1)}, bf16[128,512]{1,0:T(8,128)(2,1)S(1)}, u32[]{:S(2)}, u32[]{:S(2)}) collective-permute-start(bf16[128,512]{1,0:T(8,128)(2,1)S(1)} %get-tuple-element.51), channel_id=1, source_target_pairs={{0,2},{1,3},{2,0},{3,1},{4,6},{5,7},{6,4},{7,5},{8,10},{9,11},{10,... | collective-permute-start | bytes 393224 | tf_op jit(solution)/shard_map/ppermute | solution.py:425
  55.8 0.1 shard_map.86
  55.9 1.4 %collective-permute-start.13 = (bf16[128,512]{1,0:T(8,128)(2,1)S(1)}, bf16[128,512]{1,0:T(8,128)(2,1)S(1)}, u32[]{:S(2)}, u32[]{:S(2)}) collective-permute-start(bf16[128,512]{1,0:T(8,128)(2,1)S(1)} %get-tuple-element.53), channel_id=1, source_target_pairs={{0,2},{1,3},{2,0},{3,1},{4,6},{5,7},{6,4},{7,5},{8,10},{9,11},{10,... | collective-permute-start | bytes 393224 | tf_op jit(solution)/shard_map/ppermute | solution.py:425
  57.3 0.7 collective-permute-start.18
  58.0 2.5 %collective-permute-done.11.got_ref = bf16[128,512]{1,0:T(8,128)(2,1)S(1)} collective-permute-done((bf16[128,512]{1,0:T(8,128)(2,1)S(1)}, bf16[128,512]{1,0:T(8,128)(2,1)S(1)}, u32[]{:S(2)}, u32[]{:S(2)}) %collective-permute-start.11) | collective-permute-done | bytes 131104 | tf_op jit(solution)/shard_map/ppermute | solution.py:425
  60.6 23.0 %collective-permute-done.9.refs_2_ = bf16[1024,512]{1,0:T(8,128)(2,1)} collective-permute-done((bf16[1024,512]{1,0:T(8,128)(2,1)}, bf16[1024,512]{1,0:T(8,128)(2,1)}, u32[]{:S(2)}, u32[]{:S(2)}) %collective-permute-start.9) | collective-permute-done | bytes 1048608 | tf_op jit(solution)/shard_map/ppermute | solution.py:378
  83.6 1.3 %collective-permute-start.19 = (bf16[1024,512]{1,0:T(8,128)(2,1)}, bf16[1024,512]{1,0:T(8,128)(2,1)S(1)}, u32[]{:S(2)}, u32[]{:S(2)}) collective-permute-start(bf16[1024,512]{1,0:T(8,128)(2,1)} %collective-permute-done.9.refs_2_), channel_id=1, source_target_pairs={{8,0},{12,4},{16,24},{20,28},{9,1},{13,5},{17,25},{21,29},{10,2},{... | collective-permute-start | bytes 3145736 | tf_op jit(solution)/shard_map/ppermute | solution.py:378
  84.9 2.8 %shard_map.83 = (bf16[256,1024]{1,0:T(8,128)(2,1)S(1)}, f32[256,1024]{1,0:T(8,128)S(1)}) custom-call(s32[1]{0:T(128)} %bitcast.9.flag_ref, bf16[512,1024]{1,0:T(8,128)(2,1)S(1)} %get-tuple-element.41.refs_0_, bf16[1024,512]{1,0:T(8,128)(2,1)} %collective-permute-done.8.refs_1_, bf16[1024,512]{1,0:T(8,128)(2,1)} %collective-permute-done.9.refs_2_), custom_call_target="tpu_custom_call" | custom-call | flops 1073741824 | bytes 4718592 | tf_op jit(solution)/shard_map/pallas_call | solution.py:49
  87.7 0.1 collective-permute-start.14
  87.8 2.8 %shard_map.84 = (bf16[256,1024]{1,0:T(8,128)(2,1)S(1)}, f32[256,1024]{1,0:T(8,128)S(1)}) custom-call(s32[1]{0:T(128)} %bitcast.9.flag_ref, bf16[512,1024]{1,0:T(8,128)(2,1)S(1)} %collective-permute-done.7.refs_0_.refs_1_, bf16[1024,512]{1,0:T(8,128)(2,1)} %collective-permute-done.8.refs_1_, bf16[1024,512]{1,0:T(8,128)(2,1)} %collective-permute-done.9.refs_2_), custom_call_target="tpu_custom_call" | custom-call | flops 1073741824 | bytes 4718592 | tf_op jit(solution)/shard_map/pallas_call | solution.py:49
  90.6 0.6 collective-permute-start.16
  91.2 0.1 shard_map.87
  91.2 1.6 %collective-permute-start.15 = (bf16[128,1024]{1,0:T(8,128)(2,1)S(1)}, bf16[128,1024]{1,0:T(8,128)(2,1)S(1)}, u32[]{:S(2)}, u32[]{:S(2)}) collective-permute-start(bf16[128,1024]{1,0:T(8,128)(2,1)S(1)} %get-tuple-element.55), channel_id=1, source_target_pairs={{0,2},{1,3},{2,0},{3,1},{4,6},{5,7},{6,4},{7,5},{8,10},{9,11},{10,... | collective-permute-start | bytes 786440 | tf_op jit(solution)/shard_map/ppermute | solution.py:425
  92.8 0.1 shard_map.88
  92.9 1.5 %collective-permute-start.17 = (bf16[128,1024]{1,0:T(8,128)(2,1)S(1)}, bf16[128,1024]{1,0:T(8,128)(2,1)S(1)}, u32[]{:S(2)}, u32[]{:S(2)}) collective-permute-start(bf16[128,1024]{1,0:T(8,128)(2,1)S(1)} %get-tuple-element.57), channel_id=1, source_target_pairs={{0,2},{1,3},{2,0},{3,1},{4,6},{5,7},{6,4},{7,5},{8,10},{9,11},{10,... | collective-permute-start | bytes 786440 | tf_op jit(solution)/shard_map/ppermute | solution.py:425
  94.4 6.1 %collective-permute-done.15.got_ref = bf16[128,1024]{1,0:T(8,128)(2,1)S(1)} collective-permute-done((bf16[128,1024]{1,0:T(8,128)(2,1)S(1)}, bf16[128,1024]{1,0:T(8,128)(2,1)S(1)}, u32[]{:S(2)}, u32[]{:S(2)}) %collective-permute-start.15) | collective-permute-done | bytes 262176 | tf_op jit(solution)/shard_map/ppermute | solution.py:425
  100.5 4.7 %collective-permute-done.17.got_ref = bf16[128,1024]{1,0:T(8,128)(2,1)S(1)} collective-permute-done((bf16[128,1024]{1,0:T(8,128)(2,1)S(1)}, bf16[128,1024]{1,0:T(8,128)(2,1)S(1)}, u32[]{:S(2)}, u32[]{:S(2)}) %collective-permute-start.17) | collective-permute-done | bytes 262176 | tf_op jit(solution)/shard_map/ppermute | solution.py:425
  105.2 1.3 shard_map.89
  106.4 0.1 collective-permute-start.20
  106.6 0.6 collective-permute-start.23
  107.2 1.2 collective-permute-done.20.got_ref
  108.4 0.1 shard_map.90
  108.5 1.6 %collective-permute-start.21 = (bf16[128,1024]{1,0:T(8,128)(2,1)S(1)}, bf16[128,1024]{1,0:T(8,128)(2,1)S(1)}, u32[]{:S(2)}, u32[]{:S(2)}) collective-permute-start(bf16[128,1024]{1,0:T(8,128)(2,1)S(1)} %get-tuple-element.63), channel_id=1, source_target_pairs={{0,2},{1,3},{2,0},{3,1},{4,6},{5,7},{6,4},{7,5},{8,10},{9,11},{10,... | collective-permute-start | bytes 786440 | tf_op jit(solution)/shard_map/ppermute | solution.py:425
  110.1 0.6 collective-permute-start.22
  110.7 0.1 stack.86.starts_ref
  110.9 7.3 %collective-permute-done.22.refs_1_ = bf16[128,512]{1,0:T(8,128)(2,1)S(1)} collective-permute-done((bf16[128,512]{1,0:T(8,128)(2,1)S(1)}, bf16[128,512]{1,0:T(8,128)(2,1)S(1)}, u32[]{:S(2)}, u32[]{:S(2)}) %collective-permute-start.22) | collective-permute-done | bytes 131104 | tf_op jit(solution)/shard_map/ppermute | solution.py:435
  118.2 1.8 %shard_map.95.refs_2_ = bf16[128,4096]{1,0:T(8,128)(2,1)} custom-call(s32[6]{0:T(128)S(1)} %stack.86.starts_ref, f32[1,128]{1,0:T(1,128)S(1)} %slice_add_fusion.1.squares_ref, bf16[128,512]{1,0:T(8,128)(2,1)S(1)} %shard_map.91.refs_0_, bf16[128,512]{1,0:T(8,128)(2,1)S(1)} %collective-permute-done.22.refs_1_, bf16[128,1024]{1,0:T(8,128)(2,1)S(1)} %shard_map.93.refs_2_, ...), custom_call_target="tpu_custom_call" | custom-call | bytes 1835520 | tf_op jit(solution)/shard_map/pallas_call | solution.py:49
  120.0 0.6 collective-permute-start.24
  120.6 0.1 pad_add_fusion.starts_ref
  120.7 4.5 %collective-permute-done.24.refs_1_ = bf16[128,512]{1,0:T(8,128)(2,1)S(1)} collective-permute-done((bf16[128,512]{1,0:T(8,128)(2,1)S(1)}, bf16[128,512]{1,0:T(8,128)(2,1)S(1)}, u32[]{:S(2)}, u32[]{:S(2)}) %collective-permute-start.24) | collective-permute-done | bytes 131104 | tf_op jit(solution)/shard_map/ppermute | solution.py:435
  125.2 1.4 %shard_map.97 = bf16[128,4096]{1,0:T(8,128)(2,1)} custom-call(s32[2]{0:T(128)S(1)} %pad_add_fusion.starts_ref, f32[1,128]{1,0:T(1,128)S(1)} %slice_add_fusion.1.squares_ref, bf16[128,512]{1,0:T(8,128)(2,1)S(1)} %get-tuple-element.69.refs_0_, bf16[128,512]{1,0:T(8,128)(2,1)S(1)} %collective-permute-done.24.refs_1_, ...), custom_call_target="tpu_custom_call", output_to_operand_aliasing={{}: (4, {})} | custom-call | bytes 524288 | tf_op jit(solution)/shard_map/pallas_call | solution.py:347
  (43 shorter events, 0.3 us)
Async XLA Ops:
  0.0 1.2 copy-start
  1.2 1.2 copy-start.2
  2.5 3.5 %copy-start.1 = (bf16[512,1024]{1,0:T(8,128)(2,1)S(1)}, bf16[512,1024]{1,0:T(8,128)(2,1)}, u32[]{:S(2)}) copy-start(bf16[512,1024]{1,0:T(8,128)(2,1)} %k_ref.7) | copy-start | bytes 3145732
  2.9 6.5 %collective-permute-start = (bf16[4,128,128]{2,1,0:T(8,128)(2,1)S(1)}, bf16[4,128,128]{2,1,0:T(8,128)(2,1)S(1)}, u32[]{:S(2)}, u32[]{:S(2)}) collective-permute-start(bf16[4,128,128]{2,1,0:T(8,128)(2,1)S(1)} %shard_map.74), channel_id=1, source_target_pairs={{0,4},{4,0},{8,12},{12,8},{16,20},{20,16},{24,28},{28,24},{1,5},{5... | collective-permute-start | bytes 393224 | tf_op jit(solution)/shard_map/ppermute | solution.py:124
  6.4 12.6 %copy-start.4 = (bf16[512,1024]{1,0:T(8,128)(2,1)S(1)}, bf16[512,1024]{1,0:T(8,128)(2,1)}, u32[]{:S(2)}) copy-start(bf16[512,1024]{1,0:T(8,128)(2,1)} %q_ref.5) | copy-start | bytes 3145732
  9.5 6.2 %collective-permute-start.1 = (bf16[4,128,128]{2,1,0:T(8,128)(2,1)S(1)}, bf16[4,128,128]{2,1,0:T(8,128)(2,1)S(1)}, u32[]{:S(2)}, u32[]{:S(2)}) collective-permute-start(bf16[4,128,128]{2,1,0:T(8,128)(2,1)S(1)} %shard_map.75), channel_id=1, source_target_pairs={{0,8},{4,12},{16,24},{20,28},{1,9},{5,13},{17,25},{21,29},{2,10},{... | collective-permute-start | bytes 393224 | tf_op jit(solution)/shard_map/ppermute | solution.py:127
  15.7 0.7 copy-start.8
  16.4 4.8 %collective-permute-start.2 = (bf16[4,128,128]{2,1,0:T(8,128)(2,1)}, bf16[4,128,128]{2,1,0:T(8,128)(2,1)}, u32[]{:S(2)}, u32[]{:S(2)}) collective-permute-start(bf16[4,128,128]{2,1,0:T(8,128)(2,1)} %shard_map.76), channel_id=1, source_target_pairs={{8,16},{12,20},{9,17},{13,21},{10,18},{14,22},{11,19},{15,23}} | collective-permute-start | bytes 393224 | tf_op jit(solution)/shard_map/ppermute | solution.py:129
  17.7 3.5 %collective-permute-start.3 = (bf16[4,128,128]{2,1,0:T(8,128)(2,1)}, bf16[4,128,128]{2,1,0:T(8,128)(2,1)}, u32[]{:S(2)}, u32[]{:S(2)}) collective-permute-start(bf16[4,128,128]{2,1,0:T(8,128)(2,1)} %shard_map.76), channel_id=1, source_target_pairs={{8,24},{12,28},{9,25},{13,29},{10,26},{14,30},{11,27},{15,31}} | collective-permute-start | bytes 393224 | tf_op jit(solution)/shard_map/ppermute | solution.py:130
  19.0 5.8 %copy-start.3 = (bf16[512,1024]{1,0:T(8,128)(2,1)S(1)}, bf16[512,1024]{1,0:T(8,128)(2,1)}, u32[]{:S(2)}) copy-start(bf16[512,1024]{1,0:T(8,128)(2,1)} %v_ref.7) | copy-start | bytes 3145732
  20.1 1.0 copy-start.5
  21.2 0.9 copy-start.9
  23.2 5.1 %copy-start.6 = (f32[512,512]{1,0:T(8,128)S(1)}, f32[512,512]{1,0:T(8,128)}, u32[]{:S(2)}) copy-start(f32[512,512]{1,0:T(8,128)} %copy-done.5) | copy-start | bytes 3145732
  23.2 5.1 %copy-start.7 = (bf16[512,1024]{1,0:T(8,128)(2,1)S(1)}, bf16[512,1024]{1,0:T(8,128)(2,1)}, u32[]{:S(2)}) copy-start(bf16[512,1024]{1,0:T(8,128)(2,1)} %gate_ref.1) | copy-start | bytes 3145732
  23.2 5.1 %copy-start.10 = (f32[8,128,128]{2,1,0:T(8,128)S(1)}, f32[8,128,128]{2,1,0:T(8,128)}, u32[]{:S(2)}) copy-start(f32[8,128,128]{2,1,0:T(8,128)} %kv_ref.1) | copy-start | bytes 1572868
  23.3 5.0 %collective-permute-start.4 = (bf16[4,128,128]{2,1,0:T(8,128)(2,1)S(1)}, bf16[4,128,128]{2,1,0:T(8,128)(2,1)S(1)}, u32[]{:S(2)}, u32[]{:S(2)}) collective-permute-start(bf16[4,128,128]{2,1,0:T(8,128)(2,1)S(1)} %get-tuple-element.39), channel_id=1, source_target_pairs={{0,4},{4,0},{8,12},{12,8},{16,20},{20,16},{24,28},{28,24},{1,5},{5... | collective-permute-start | bytes 393224 | tf_op jit(solution)/shard_map/ppermute | solution.py:137
  24.8 3.5 %copy-start.11 = (f32[4096]{0:T(1024)S(1)}, f32[4096]{0:T(1024)}, u32[]{:S(2)}) copy-start(f32[4096]{0:T(1024)} %param.12) | copy-start | bytes 49156
  30.1 22.1 %collective-permute-start.7 = (bf16[512,1024]{1,0:T(8,128)(2,1)S(1)}, bf16[512,1024]{1,0:T(8,128)(2,1)S(1)}, u32[]{:S(2)}, u32[]{:S(2)}) collective-permute-start(bf16[512,1024]{1,0:T(8,128)(2,1)S(1)} %get-tuple-element.41.refs_0_), channel_id=1, source_target_pairs={{0,4},{4,0},{8,12},{12,8},{16,20},{20,16},{24,28},{28,24},{1,5},{5... | collective-permute-start | bytes 3145736 | tf_op jit(solution)/shard_map/ppermute | solution.py:397
  31.6 52.0 %collective-permute-start.9 = (bf16[1024,512]{1,0:T(8,128)(2,1)}, bf16[1024,512]{1,0:T(8,128)(2,1)}, u32[]{:S(2)}, u32[]{:S(2)}) collective-permute-start(bf16[1024,512]{1,0:T(8,128)(2,1)} %refs_1_.3), channel_id=1, source_target_pairs={{0,16},{4,20},{8,24},{12,28},{16,0},{20,4},{24,8},{28,12},{1,17},{... | collective-permute-start | bytes 3145736 | tf_op jit(solution)/shard_map/ppermute | solution.py:378
  39.1 45.8 %collective-permute-start.8 = (bf16[1024,512]{1,0:T(8,128)(2,1)}, bf16[1024,512]{1,0:T(8,128)(2,1)}, u32[]{:S(2)}, u32[]{:S(2)}) collective-permute-start(bf16[1024,512]{1,0:T(8,128)(2,1)} %refs_1_.3), channel_id=1, source_target_pairs={{0,8},{4,12},{8,0},{12,4},{16,24},{20,28},{24,16},{28,20},{1,9},{5... | collective-permute-start | bytes 3145736 | tf_op jit(solution)/shard_map/ppermute | solution.py:378
  41.3 1.1 collective-permute-start.5
  42.4 3.5 %collective-permute-start.6 = (f32[1,128]{1,0:T(1,128)S(1)}, f32[1,128]{1,0:T(1,128)S(1)}, u32[]{:S(2)}, u32[]{:S(2)}) collective-permute-start(f32[1,128]{1,0:T(1,128)S(1)} %slice.15), channel_id=1, source_target_pairs={{0,2},{1,3},{2,0},{3,1},{4,6},{5,7},{6,4},{7,5},{8,10},{9,11},{10,... | collective-permute-start | bytes 1544 | tf_op jit(solution)/shard_map/ppermute | solution.py:402
  45.9 8.3 %collective-permute-start.10 = (bf16[256,512]{1,0:T(8,128)(2,1)S(1)}, bf16[256,512]{1,0:T(8,128)(2,1)S(1)}, u32[]{:S(2)}, u32[]{:S(2)}) collective-permute-start(bf16[256,512]{1,0:T(8,128)(2,1)S(1)} %get-tuple-element.42), channel_id=1, source_target_pairs={{0,1},{1,0},{2,3},{3,2},{4,5},{5,4},{6,7},{7,6},{8,9},{9,8},{10,11... | collective-permute-start | bytes 786440 | tf_op jit(solution)/shard_map/ppermute | solution.py:425
  54.1 1.7 %collective-permute-start.12 = (bf16[256,512]{1,0:T(8,128)(2,1)S(1)}, bf16[256,512]{1,0:T(8,128)(2,1)S(1)}, u32[]{:S(2)}, u32[]{:S(2)}) collective-permute-start(bf16[256,512]{1,0:T(8,128)(2,1)S(1)} %get-tuple-element.44), channel_id=1, source_target_pairs={{0,1},{1,0},{2,3},{3,2},{4,5},{5,4},{6,7},{7,6},{8,9},{9,8},{10,11... | collective-permute-start | bytes 786440 | tf_op jit(solution)/shard_map/ppermute | solution.py:425
  54.2 6.4 %collective-permute-start.11 = (bf16[128,512]{1,0:T(8,128)(2,1)S(1)}, bf16[128,512]{1,0:T(8,128)(2,1)S(1)}, u32[]{:S(2)}, u32[]{:S(2)}) collective-permute-start(bf16[128,512]{1,0:T(8,128)(2,1)S(1)} %get-tuple-element.51), channel_id=1, source_target_pairs={{0,2},{1,3},{2,0},{3,1},{4,6},{5,7},{6,4},{7,5},{8,10},{9,11},{10,... | collective-permute-start | bytes 393224 | tf_op jit(solution)/shard_map/ppermute | solution.py:425
  55.9 27.7 %collective-permute-start.13 = (bf16[128,512]{1,0:T(8,128)(2,1)S(1)}, bf16[128,512]{1,0:T(8,128)(2,1)S(1)}, u32[]{:S(2)}, u32[]{:S(2)}) collective-permute-start(bf16[128,512]{1,0:T(8,128)(2,1)S(1)} %get-tuple-element.53), channel_id=1, source_target_pairs={{0,2},{1,3},{2,0},{3,1},{4,6},{5,7},{6,4},{7,5},{8,10},{9,11},{10,... | collective-permute-start | bytes 393224 | tf_op jit(solution)/shard_map/ppermute | solution.py:425
  57.3 47.8 %collective-permute-start.18 = (bf16[1024,512]{1,0:T(8,128)(2,1)}, bf16[1024,512]{1,0:T(8,128)(2,1)S(1)}, u32[]{:S(2)}, u32[]{:S(2)}) collective-permute-start(bf16[1024,512]{1,0:T(8,128)(2,1)} %refs_1_.3), channel_id=1, source_target_pairs={{8,16},{12,20},{16,8},{20,12},{9,17},{13,21},{17,9},{21,13},{10,18... | collective-permute-start | bytes 3145736 | tf_op jit(solution)/shard_map/ppermute | solution.py:378
  83.6 21.6 %collective-permute-start.19 = (bf16[1024,512]{1,0:T(8,128)(2,1)}, bf16[1024,512]{1,0:T(8,128)(2,1)S(1)}, u32[]{:S(2)}, u32[]{:S(2)}) collective-permute-start(bf16[1024,512]{1,0:T(8,128)(2,1)} %collective-permute-done.9.refs_2_), channel_id=1, source_target_pairs={{8,0},{12,4},{16,24},{20,28},{9,1},{13,5},{17,25},{21,29},{10,2},{... | collective-permute-start | bytes 3145736 | tf_op jit(solution)/shard_map/ppermute | solution.py:378
  87.7 3.4 %collective-permute-start.14 = (bf16[256,1024]{1,0:T(8,128)(2,1)S(1)}, bf16[256,1024]{1,0:T(8,128)(2,1)S(1)}, u32[]{:S(2)}, u32[]{:S(2)}) collective-permute-start(bf16[256,1024]{1,0:T(8,128)(2,1)S(1)} %get-tuple-element.47), channel_id=1, source_target_pairs={{0,1},{1,0},{2,3},{3,2},{4,5},{5,4},{6,7},{7,6},{8,9},{9,8},{10,11... | collective-permute-start | bytes 1572872 | tf_op jit(solution)/shard_map/ppermute | solution.py:425
  90.6 2.2 %collective-permute-start.16 = (bf16[256,1024]{1,0:T(8,128)(2,1)S(1)}, bf16[256,1024]{1,0:T(8,128)(2,1)S(1)}, u32[]{:S(2)}, u32[]{:S(2)}) collective-permute-start(bf16[256,1024]{1,0:T(8,128)(2,1)S(1)} %get-tuple-element.49), channel_id=1, source_target_pairs={{0,1},{1,0},{2,3},{3,2},{4,5},{5,4},{6,7},{7,6},{8,9},{9,8},{10,11... | collective-permute-start | bytes 1572872 | tf_op jit(solution)/shard_map/ppermute | solution.py:425
  91.2 9.2 %collective-permute-start.15 = (bf16[128,1024]{1,0:T(8,128)(2,1)S(1)}, bf16[128,1024]{1,0:T(8,128)(2,1)S(1)}, u32[]{:S(2)}, u32[]{:S(2)}) collective-permute-start(bf16[128,1024]{1,0:T(8,128)(2,1)S(1)} %get-tuple-element.55), channel_id=1, source_target_pairs={{0,2},{1,3},{2,0},{3,1},{4,6},{5,7},{6,4},{7,5},{8,10},{9,11},{10,... | collective-permute-start | bytes 786440 | tf_op jit(solution)/shard_map/ppermute | solution.py:425
  92.9 12.2 %collective-permute-start.17 = (bf16[128,1024]{1,0:T(8,128)(2,1)S(1)}, bf16[128,1024]{1,0:T(8,128)(2,1)S(1)}, u32[]{:S(2)}, u32[]{:S(2)}) collective-permute-start(bf16[128,1024]{1,0:T(8,128)(2,1)S(1)} %get-tuple-element.57), channel_id=1, source_target_pairs={{0,2},{1,3},{2,0},{3,1},{4,6},{5,7},{6,4},{7,5},{8,10},{9,11},{10,... | collective-permute-start | bytes 786440 | tf_op jit(solution)/shard_map/ppermute | solution.py:425
  106.4 2.0 %collective-permute-start.20 = (bf16[256,1024]{1,0:T(8,128)(2,1)S(1)}, bf16[256,1024]{1,0:T(8,128)(2,1)S(1)}, u32[]{:S(2)}, u32[]{:S(2)}) collective-permute-start(bf16[256,1024]{1,0:T(8,128)(2,1)S(1)} %get-tuple-element.61), channel_id=1, source_target_pairs={{0,1},{1,0},{2,3},{3,2},{4,5},{5,4},{6,7},{7,6},{8,9},{9,8},{10,11... | collective-permute-start | bytes 1572872 | tf_op jit(solution)/shard_map/ppermute | solution.py:425
  106.6 11.6 %collective-permute-start.23 = (bf16[128,1024]{1,0:T(8,128)(2,1)S(1)}, bf16[128,1024]{1,0:T(8,128)(2,1)S(1)}, u32[]{:S(2)}, u32[]{:S(2)}) collective-permute-start(bf16[128,1024]{1,0:T(8,128)(2,1)S(1)} %shard_map.94), channel_id=1, source_target_pairs={{0,4},{4,0},{8,12},{12,8},{16,20},{20,16},{24,28},{28,24},{1,5},{5... | collective-permute-start | bytes 786440 | tf_op jit(solution)/shard_map/ppermute | solution.py:435
  108.5 11.5 %collective-permute-start.21 = (bf16[128,1024]{1,0:T(8,128)(2,1)S(1)}, bf16[128,1024]{1,0:T(8,128)(2,1)S(1)}, u32[]{:S(2)}, u32[]{:S(2)}) collective-permute-start(bf16[128,1024]{1,0:T(8,128)(2,1)S(1)} %get-tuple-element.63), channel_id=1, source_target_pairs={{0,2},{1,3},{2,0},{3,1},{4,6},{5,7},{6,4},{7,5},{8,10},{9,11},{10,... | collective-permute-start | bytes 786440 | tf_op jit(solution)/shard_map/ppermute | solution.py:425
  110.1 8.0 %collective-permute-start.22 = (bf16[128,512]{1,0:T(8,128)(2,1)S(1)}, bf16[128,512]{1,0:T(8,128)(2,1)S(1)}, u32[]{:S(2)}, u32[]{:S(2)}) collective-permute-start(bf16[128,512]{1,0:T(8,128)(2,1)S(1)} %shard_map.92), channel_id=1, source_target_pairs={{0,4},{4,0},{8,12},{12,8},{16,20},{20,16},{24,28},{28,24},{1,5},{5... | collective-permute-start | bytes 393224 | tf_op jit(solution)/shard_map/ppermute | solution.py:435
  120.0 5.2 %collective-permute-start.24 = (bf16[128,512]{1,0:T(8,128)(2,1)S(1)}, bf16[128,512]{1,0:T(8,128)(2,1)S(1)}, u32[]{:S(2)}, u32[]{:S(2)}) collective-permute-start(bf16[128,512]{1,0:T(8,128)(2,1)S(1)} %get-tuple-element.70), channel_id=1, source_target_pairs={{0,4},{4,0},{8,12},{12,8},{16,20},{20,16},{24,28},{28,24},{1,5},{5... | collective-permute-start | bytes 393224 | tf_op jit(solution)/shard_map/ppermute | solution.py:435

commit v10 on v9

--- a/solution.py
+++ b/solution.py
@@ -441,23 +441,26 @@
     shape = (out_rows, width * n_seq)
     in_kernel = width % DH == 0 and out_rows == DH
 
-    pieces, pins, ends = [], [], []
+    pieces, pins, ends = [], [w_halves, w_next], []
 
     def group(members, some):
-        if members:
-            more, sent, end = summed([(turn, some) for turn in members], pins)
-            pieces.extend(more)
-            ends.append(end)
-            pins[:] = [sent, squares]
+        more, sent, end = summed([(turn, some) for turn in members], pins)
+        pieces.extend(more)
+        ends.append(end)
+        pins[:] = [sent, squares]
+        return [piece for piece, _ in more]
 
     group(turns[:1], [0])
-    group(turns[1:], [0])
-    w_ends = along(hold(w_halves, *ends), TO_ENDS)
+    returned = group(turns[1:], [0]) if inner > 1 else []
+    w_ends = along(w_halves, TO_ENDS)
     blocks.append((w_middle, w_ends))
     group(turns[:1], [1, 2])
-    group(turns[1:], [1, 2])
+    if inner > 1:
+        group(turns[1:], [1, 2])
     filled = placed(None, pieces, squares, width, shape, total_width) if in_kernel else None
-    last, _, _ = summed([(turn, [3]) for turn in turns], [*pins, *ends], filled)
+    last, _, _ = summed(
+        [(turn, [3]) for turn in turns], [*pins, *ends, *returned], filled
+    )
     if in_kernel:
         return placed(filled, last, squares, width, shape, total_width)
     scale = lax.rsqrt(squares.reshape(out_rows, 1) / total_width + epsilon)

time: 127 us -> 128 us (level)
  waiting for transfers between devices: 64.5 us -> 68.6 us
  Pallas kernels: 21.2 us -> 18.8 us
  starting transfers between devices: 35.9 us -> 34.5 us
    ppermute x4, waiting for transfers between devices: 23 us -> 35.3 us  [along(): return lax.ppermute(value, 'seq', line_pairs(n_seq, hops))]
    ppermute x1, waiting for transfers between devices: 6.17 us -> 0.01 us  [shards(): lax.ppermute(hidden, 'seq', turn_pairs(n_seq, turn))]
    ppermute x10, waiting for transfers between devices: 14.6 us -> 11.4 us  [summed(): got = lax.ppermute(sent, 'head', flip_pairs(n_head, bit))]
    pallas_call x24, Pallas kernels: 19.8 us -> 17.4 us  [local_call(): pl.pallas_call(kernel, in_specs=[pl.BlockSpec(memory_space=pltpu.SMEM)] +...]
    ppermute x1, waiting for transfers between devices: 2.31 us -> 0.01 us  [state_prefix(): terms.append(lax.ppermute(befores[turn], 'seq', turn_pairs(n_seq, turn)))]
    ppermute x3, waiting for transfers between devices: 11.8 us -> 13.9 us  [summed(): piece = lax.ppermute(piece, 'seq', turn_pairs(n_seq, -turn))]
    ppermute x2, waiting for transfers between devices: 1.14 us -> 2.43 us  [shards(): lax.ppermute(squares[half:], 'head', flip_pairs(n_head, bit))]
    unnamed x24 -> x38, local copies, waits for them, and re-layouts: 4.36 us -> 5.03 us
  transfers between devices with their start and end apart: 25 -> 25, of which waited for: 12 -> 13; matrix products, arithmetic and copies ran while one was open for 0% -> 0% of each run, Pallas kernels for 11% -> 11%
where the time goes in v10:
time: 128 us
  waiting for transfers between devices  68.6 us (54%)
  starting transfers between devices  34.5 us (27%)
  Pallas kernels  18.8 us (15%)
  local copies, waits for them, and re-layouts  5.12 us (4%)
    ppermute x4, waiting for transfers between devices, along(): return lax.ppermute(value, 'seq', line_pairs(n_seq, hops))  35.3 us
    pallas_call x24, Pallas kernels, local_call(): pl.pallas_call(kernel, in_specs=[pl.BlockSpec(memory_space=pltpu.SMEM)] +...  17.4 us
    ppermute x3, waiting for transfers between devices, summed(): piece = lax.ppermute(piece, 'seq', turn_pairs(n_seq, -turn))  13.9 us
    ppermute x4, starting transfers between devices, along(): return lax.ppermute(value, 'seq', line_pairs(n_seq, hops))  11.7 us
    ppermute x10, waiting for transfers between devices, summed(): got = lax.ppermute(sent, 'head', flip_pairs(n_head, bit))  11.4 us
    ppermute x10, starting transfers between devices, summed(): got = lax.ppermute(sent, 'head', flip_pairs(n_head, bit))  8.05 us
    unnamed x38, local copies, waits for them, and re-layouts  5.03 us
    ppermute x1, starting transfers between devices, state_prefix(): from_left = lax.ppermute(first, 'seq', line_pairs(n_seq, [(0, 1), (2, 3)]))  3.74 us
  transfers between devices with their start and end apart: 25, of which 13 were waited for; matrix products, arithmetic and copies ran while one was open for 0% of the time, Pallas kernels for 11%

profile of v10, /device:TPU:0, one launch (start us, length us, event | category | flops | bytes accessed | tf_op | source)
XLA Modules:
  0.0 127.6 jit_solution(14832054859653085594)
XLA Ops:
  0.0 1.2 copy-done
  1.2 1.2 copy-done.2
  2.5 0.5 shard_map.74
  2.9 3.0 %collective-permute-start = (bf16[4,128,128]{2,1,0:T(8,128)(2,1)S(1)}, bf16[4,128,128]{2,1,0:T(8,128)(2,1)S(1)}, u32[]{:S(2)}, u32[]{:S(2)}) collective-permute-start(bf16[4,128,128]{2,1,0:T(8,128)(2,1)S(1)} %shard_map.74), channel_id=1, source_target_pairs={{0,4},{4,0},{8,12},{12,8},{16,20},{20,16},{24,28},{28,24},{1,5},{5... | collective-permute-start | bytes 393224 | tf_op jit(solution)/shard_map/ppermute | solution.py:124
  5.9 0.5 shard_map.73.refs_0_.refs_3_
  6.4 3.0 %collective-permute-done.refs_1_.refs_4_ = bf16[4,128,128]{2,1,0:T(8,128)(2,1)S(1)} collective-permute-done((bf16[4,128,128]{2,1,0:T(8,128)(2,1)S(1)}, bf16[4,128,128]{2,1,0:T(8,128)(2,1)S(1)}, u32[]{:S(2)}, u32[]{:S(2)}) %collective-permute-start) | collective-permute-done | bytes 131104 | tf_op jit(solution)/shard_map/ppermute | solution.py:124
  9.5 3.7 %collective-permute-start.1 = (bf16[4,128,128]{2,1,0:T(8,128)(2,1)S(1)}, bf16[4,128,128]{2,1,0:T(8,128)(2,1)S(1)}, u32[]{:S(2)}, u32[]{:S(2)}) collective-permute-start(bf16[4,128,128]{2,1,0:T(8,128)(2,1)S(1)} %shard_map.75), channel_id=1, source_target_pairs={{0,8},{4,12},{16,24},{20,28},{1,9},{5,13},{17,25},{21,29},{2,10},{... | collective-permute-start | bytes 393224 | tf_op jit(solution)/shard_map/ppermute | solution.py:127
  13.2 2.5 %collective-permute-done.1.refs_2_.refs_0_ = bf16[4,128,128]{2,1,0:T(8,128)(2,1)S(1)} collective-permute-done((bf16[4,128,128]{2,1,0:T(8,128)(2,1)S(1)}, bf16[4,128,128]{2,1,0:T(8,128)(2,1)S(1)}, u32[]{:S(2)}, u32[]{:S(2)}) %collective-permute-start.1) | collective-permute-done | bytes 131104 | tf_op jit(solution)/shard_map/ppermute | solution.py:127
  15.7 0.7 shard_map.76
  16.4 1.3 %collective-permute-start.2 = (bf16[4,128,128]{2,1,0:T(8,128)(2,1)}, bf16[4,128,128]{2,1,0:T(8,128)(2,1)}, u32[]{:S(2)}, u32[]{:S(2)}) collective-permute-start(bf16[4,128,128]{2,1,0:T(8,128)(2,1)} %shard_map.76), channel_id=1, source_target_pairs={{8,16},{12,20},{9,17},{13,21},{10,18},{14,22},{11,19},{15,23}} | collective-permute-start | bytes 393224 | tf_op jit(solution)/shard_map/ppermute | solution.py:129
  17.7 1.3 %collective-permute-start.3 = (bf16[4,128,128]{2,1,0:T(8,128)(2,1)}, bf16[4,128,128]{2,1,0:T(8,128)(2,1)}, u32[]{:S(2)}, u32[]{:S(2)}) collective-permute-start(bf16[4,128,128]{2,1,0:T(8,128)(2,1)} %shard_map.76), channel_id=1, source_target_pairs={{8,24},{12,28},{9,25},{13,29},{10,26},{14,30},{11,27},{15,31}} | collective-permute-start | bytes 393224 | tf_op jit(solution)/shard_map/ppermute | solution.py:130
  19.1 1.1 shard_map.78.refs_2_
  20.2 1.0 copy-done.6
  21.1 0.1 add_convert_fusion.masks_ref
  21.2 0.9 copy-done.12
  22.1 1.1 shard_map.77
  23.2 1.6 %collective-permute-start.4 = (bf16[4,128,128]{2,1,0:T(8,128)(2,1)S(1)}, bf16[4,128,128]{2,1,0:T(8,128)(2,1)S(1)}, u32[]{:S(2)}, u32[]{:S(2)}) collective-permute-start(bf16[4,128,128]{2,1,0:T(8,128)(2,1)S(1)} %get-tuple-element.39), channel_id=1, source_target_pairs={{0,4},{4,0},{8,12},{12,8},{16,20},{20,16},{24,28},{28,24},{1,5},{5... | collective-permute-start | bytes 393224 | tf_op jit(solution)/shard_map/ppermute | solution.py:137
  24.8 0.1 pad_add_fusion.1.place_ref
  24.9 6.4 %collective-permute-start.7 = (bf16[1024,512]{1,0:T(8,128)(2,1)}, bf16[1024,512]{1,0:T(8,128)(2,1)}, u32[]{:S(2)}, u32[]{:S(2)}) collective-permute-start(bf16[1024,512]{1,0:T(8,128)(2,1)} %refs_1_.3), channel_id=1, source_target_pairs={{0,16},{4,20},{8,24},{12,28},{16,0},{20,4},{24,8},{28,12},{1,17},{... | collective-permute-start | bytes 3145736 | tf_op jit(solution)/shard_map/ppermute | solution.py:378
  31.3 3.3 %collective-permute-start.8 = (bf16[1024,512]{1,0:T(8,128)(2,1)}, bf16[1024,512]{1,0:T(8,128)(2,1)}, u32[]{:S(2)}, u32[]{:S(2)}) collective-permute-start(bf16[1024,512]{1,0:T(8,128)(2,1)} %refs_1_.3), channel_id=1, source_target_pairs={{0,8},{4,12},{8,0},{12,4},{16,24},{20,28},{24,16},{28,20},{1,9},{5... | collective-permute-start | bytes 3145736 | tf_op jit(solution)/shard_map/ppermute | solution.py:378
  34.6 1.1 shard_map.79.refs_3_
  35.7 1.7 %shard_map.80 = (bf16[512,1024]{1,0:T(8,128)(2,1)S(1)}, f32[4,128]{1,0:T(4,128)S(1)}) custom-call(s32[2]{0:T(128)S(1)} %pad_add_fusion.1.place_ref, bf16[512,1024]{1,0:T(8,128)(2,1)S(1)} %copy-done.4, bf16[512,1024]{1,0:T(8,128)(2,1)S(1)} %copy-done.8, f32[32,1,128]{2,1,0:T(1,128)S(1)} %bitcast.16, f32[8,128,128]{2,1,0:T(8,128)S(1)} %copy-done.13, ...), custom_call_target="tpu_custom_call" | custom-call | flops 268435456 | bytes 6178816 | tf_op jit(solution)/shard_map/pallas_call | solution.py:49
  37.5 0.6 collective-permute-start.9
  38.1 1.1 collective-permute-done.5
  39.2 1.5 %collective-permute-start.6 = (f32[1,128]{1,0:T(1,128)S(1)}, f32[1,128]{1,0:T(1,128)S(1)}, u32[]{:S(2)}, u32[]{:S(2)}) collective-permute-start(f32[1,128]{1,0:T(1,128)S(1)} %slice.15), channel_id=1, source_target_pairs={{0,2},{1,3},{2,0},{3,1},{4,6},{5,7},{6,4},{7,5},{8,10},{9,11},{10,... | collective-permute-start | bytes 1544 | tf_op jit(solution)/shard_map/ppermute | solution.py:402
  40.7 0.7 collective-permute-start.19
  41.5 1.3 %collective-permute-done.6 = f32[1,128]{1,0:T(1,128)S(1)} collective-permute-done((f32[1,128]{1,0:T(1,128)S(1)}, f32[1,128]{1,0:T(1,128)S(1)}, u32[]{:S(2)}, u32[]{:S(2)}) %collective-permute-start.6) | collective-permute-done | bytes 544 | tf_op jit(solution)/shard_map/ppermute | solution.py:402
  42.8 35.3 %collective-permute-done.7.refs_2_ = bf16[1024,512]{1,0:T(8,128)(2,1)} collective-permute-done((bf16[1024,512]{1,0:T(8,128)(2,1)}, bf16[1024,512]{1,0:T(8,128)(2,1)}, u32[]{:S(2)}, u32[]{:S(2)}) %collective-permute-start.7) | collective-permute-done | bytes 1048608 | tf_op jit(solution)/shard_map/ppermute | solution.py:378
  78.1 1.3 %collective-permute-start.20 = (bf16[1024,512]{1,0:T(8,128)(2,1)}, bf16[1024,512]{1,0:T(8,128)(2,1)S(1)}, u32[]{:S(2)}, u32[]{:S(2)}) collective-permute-start(bf16[1024,512]{1,0:T(8,128)(2,1)} %collective-permute-done.7.refs_2_), channel_id=1, source_target_pairs={{8,0},{12,4},{16,24},{20,28},{9,1},{13,5},{17,25},{21,29},{10,2},{... | collective-permute-start | bytes 3145736 | tf_op jit(solution)/shard_map/ppermute | solution.py:378
  79.4 0.7 shard_map.81
  80.1 0.7 shard_map.82
  80.8 0.1 collective-permute-start.12
  80.9 2.8 %shard_map.83 = (bf16[256,1024]{1,0:T(8,128)(2,1)S(1)}, f32[256,1024]{1,0:T(8,128)S(1)}) custom-call(s32[1]{0:T(128)} %bitcast.9.flag_ref, bf16[512,1024]{1,0:T(8,128)(2,1)S(1)} %get-tuple-element.43.refs_0_, bf16[1024,512]{1,0:T(8,128)(2,1)} %collective-permute-done.8.refs_1_, bf16[1024,512]{1,0:T(8,128)(2,1)} %collective-permute-done.7.refs_2_), custom_call_target="tpu_custom_call" | custom-call | flops 1073741824 | bytes 4718592 | tf_op jit(solution)/shard_map/pallas_call | solution.py:49
  83.7 0.6 collective-permute-start.14
  84.2 2.8 %shard_map.84 = (bf16[256,1024]{1,0:T(8,128)(2,1)S(1)}, f32[256,1024]{1,0:T(8,128)S(1)}) custom-call(s32[1]{0:T(128)} %bitcast.9.flag_ref, bf16[512,1024]{1,0:T(8,128)(2,1)S(1)} %collective-permute-done.9.refs_0_.refs_1_, bf16[1024,512]{1,0:T(8,128)(2,1)} %collective-permute-done.8.refs_1_, bf16[1024,512]{1,0:T(8,128)(2,1)} %collective-permute-done.7.refs_2_), custom_call_target="tpu_custom_call" | custom-call | flops 1073741824 | bytes 4718592 | tf_op jit(solution)/shard_map/pallas_call | solution.py:49
  87.0 0.1 collective-permute-start.16
  87.1 0.5 collective-permute-start.10
  87.7 1.7 %collective-permute-done.10.got_ref = bf16[256,512]{1,0:T(8,128)(2,1)S(1)} collective-permute-done((bf16[256,512]{1,0:T(8,128)(2,1)S(1)}, bf16[256,512]{1,0:T(8,128)(2,1)S(1)}, u32[]{:S(2)}, u32[]{:S(2)}) %collective-permute-start.10) | collective-permute-done | bytes 262176 | tf_op jit(solution)/shard_map/ppermute | solution.py:425
  89.4 1.5 %collective-permute-start.13 = (bf16[128,512]{1,0:T(8,128)(2,1)S(1)}, bf16[128,512]{1,0:T(8,128)(2,1)S(1)}, u32[]{:S(2)}, u32[]{:S(2)}) collective-permute-start(bf16[128,512]{1,0:T(8,128)(2,1)S(1)} %get-tuple-element.54), channel_id=1, source_target_pairs={{0,2},{1,3},{2,0},{3,1},{4,6},{5,7},{6,4},{7,5},{8,10},{9,11},{10,... | collective-permute-start | bytes 393224 | tf_op jit(solution)/shard_map/ppermute | solution.py:425
  90.9 0.1 shard_map.85
  91.0 0.6 collective-permute-start.11
  91.5 0.1 shard_map.87
  91.7 1.6 %collective-permute-start.15 = (bf16[128,1024]{1,0:T(8,128)(2,1)S(1)}, bf16[128,1024]{1,0:T(8,128)(2,1)S(1)}, u32[]{:S(2)}, u32[]{:S(2)}) collective-permute-start(bf16[128,1024]{1,0:T(8,128)(2,1)S(1)} %get-tuple-element.56), channel_id=1, source_target_pairs={{0,2},{1,3},{2,0},{3,1},{4,6},{5,7},{6,4},{7,5},{8,10},{9,11},{10,... | collective-permute-start | bytes 786440 | tf_op jit(solution)/shard_map/ppermute | solution.py:425
  93.2 0.1 shard_map.88
  93.3 2.4 %collective-permute-done.13.got_ref = bf16[128,512]{1,0:T(8,128)(2,1)S(1)} collective-permute-done((bf16[128,512]{1,0:T(8,128)(2,1)S(1)}, bf16[128,512]{1,0:T(8,128)(2,1)S(1)}, u32[]{:S(2)}, u32[]{:S(2)}) %collective-permute-start.13) | collective-permute-done | bytes 131104 | tf_op jit(solution)/shard_map/ppermute | solution.py:425
  95.7 1.5 %collective-permute-start.17 = (bf16[128,1024]{1,0:T(8,128)(2,1)S(1)}, bf16[128,1024]{1,0:T(8,128)(2,1)S(1)}, u32[]{:S(2)}, u32[]{:S(2)}) collective-permute-start(bf16[128,1024]{1,0:T(8,128)(2,1)S(1)} %get-tuple-element.58), channel_id=1, source_target_pairs={{0,2},{1,3},{2,0},{3,1},{4,6},{5,7},{6,4},{7,5},{8,10},{9,11},{10,... | collective-permute-start | bytes 786440 | tf_op jit(solution)/shard_map/ppermute | solution.py:425
  97.3 1.3 collective-permute-done.11.got_ref
  98.5 0.5 collective-permute-start.18
  99.1 4.4 %collective-permute-done.18.refs_1_ = bf16[128,512]{1,0:T(8,128)(2,1)S(1)} collective-permute-done((bf16[128,512]{1,0:T(8,128)(2,1)S(1)}, bf16[128,512]{1,0:T(8,128)(2,1)S(1)}, u32[]{:S(2)}, u32[]{:S(2)}) %collective-permute-start.18) | collective-permute-done | bytes 131104 | tf_op jit(solution)/shard_map/ppermute | solution.py:435
  103.5 0.6 copy-done.16
  104.2 4.8 %collective-permute-done.17.got_ref = bf16[128,1024]{1,0:T(8,128)(2,1)S(1)} collective-permute-done((bf16[128,1024]{1,0:T(8,128)(2,1)S(1)}, bf16[128,1024]{1,0:T(8,128)(2,1)S(1)}, u32[]{:S(2)}, u32[]{:S(2)}) %collective-permute-start.17) | collective-permute-done | bytes 262176 | tf_op jit(solution)/shard_map/ppermute | solution.py:425
  109.0 1.3 shard_map.90
  110.2 0.1 collective-permute-start.21
  110.4 0.6 collective-permute-start.23
  111.0 1.2 collective-permute-done.21.got_ref
  112.2 0.1 shard_map.91
  112.4 1.6 %collective-permute-start.22 = (bf16[128,1024]{1,0:T(8,128)(2,1)S(1)}, bf16[128,1024]{1,0:T(8,128)(2,1)S(1)}, u32[]{:S(2)}, u32[]{:S(2)}) collective-permute-start(bf16[128,1024]{1,0:T(8,128)(2,1)S(1)} %get-tuple-element.64), channel_id=1, source_target_pairs={{0,2},{1,3},{2,0},{3,1},{4,6},{5,7},{6,4},{7,5},{8,10},{9,11},{10,... | collective-permute-start | bytes 786440 | tf_op jit(solution)/shard_map/ppermute | solution.py:425
  113.9 0.1 stack.86.starts_ref
  114.1 5.0 %collective-permute-done.23.refs_3_ = bf16[128,1024]{1,0:T(8,128)(2,1)S(1)} collective-permute-done((bf16[128,1024]{1,0:T(8,128)(2,1)S(1)}, bf16[128,1024]{1,0:T(8,128)(2,1)S(1)}, u32[]{:S(2)}, u32[]{:S(2)}) %collective-permute-start.23) | collective-permute-done | bytes 262176 | tf_op jit(solution)/shard_map/ppermute | solution.py:435
  119.2 1.8 %shard_map.95.refs_2_ = bf16[128,4096]{1,0:T(8,128)(2,1)} custom-call(s32[6]{0:T(128)S(1)} %stack.86.starts_ref, f32[1,128]{1,0:T(1,128)S(1)} %slice_add_fusion.1.squares_ref, bf16[128,512]{1,0:T(8,128)(2,1)S(1)} %shard_map.92.refs_0_, bf16[128,512]{1,0:T(8,128)(2,1)S(1)} %copy-done.17, bf16[128,1024]{1,0:T(8,128)(2,1)S(1)} %shard_map.93.refs_2_, ...), custom_call_target="tpu_custom_call" | custom-call | bytes 1835520 | tf_op jit(solution)/shard_map/pallas_call | solution.py:49
  121.0 0.6 collective-permute-start.24
  121.6 0.1 pad_add_fusion.starts_ref
  121.7 4.5 %collective-permute-done.24.refs_1_ = bf16[128,512]{1,0:T(8,128)(2,1)S(1)} collective-permute-done((bf16[128,512]{1,0:T(8,128)(2,1)S(1)}, bf16[128,512]{1,0:T(8,128)(2,1)S(1)}, u32[]{:S(2)}, u32[]{:S(2)}) %collective-permute-start.24) | collective-permute-done | bytes 131104 | tf_op jit(solution)/shard_map/ppermute | solution.py:435
  126.2 1.4 %shard_map.97 = bf16[128,4096]{1,0:T(8,128)(2,1)} custom-call(s32[2]{0:T(128)S(1)} %pad_add_fusion.starts_ref, f32[1,128]{1,0:T(1,128)S(1)} %slice_add_fusion.1.squares_ref, bf16[128,512]{1,0:T(8,128)(2,1)S(1)} %get-tuple-element.69.refs_0_, bf16[128,512]{1,0:T(8,128)(2,1)S(1)} %collective-permute-done.24.refs_1_, ...), custom_call_target="tpu_custom_call", output_to_operand_aliasing={{}: (4, {})} | custom-call | bytes 524288 | tf_op jit(solution)/shard_map/pallas_call | solution.py:347
  (57 shorter events, 0.4 us)
Async XLA Ops:
  0.0 1.2 copy-start
  1.2 1.2 copy-start.2
  2.5 3.5 %copy-start.1 = (bf16[512,1024]{1,0:T(8,128)(2,1)S(1)}, bf16[512,1024]{1,0:T(8,128)(2,1)}, u32[]{:S(2)}) copy-start(bf16[512,1024]{1,0:T(8,128)(2,1)} %k_ref.7) | copy-start | bytes 3145732
  2.9 6.5 %collective-permute-start = (bf16[4,128,128]{2,1,0:T(8,128)(2,1)S(1)}, bf16[4,128,128]{2,1,0:T(8,128)(2,1)S(1)}, u32[]{:S(2)}, u32[]{:S(2)}) collective-permute-start(bf16[4,128,128]{2,1,0:T(8,128)(2,1)S(1)} %shard_map.74), channel_id=1, source_target_pairs={{0,4},{4,0},{8,12},{12,8},{16,20},{20,16},{24,28},{28,24},{1,5},{5... | collective-permute-start | bytes 393224 | tf_op jit(solution)/shard_map/ppermute | solution.py:124
  6.4 12.6 %copy-start.4 = (bf16[512,1024]{1,0:T(8,128)(2,1)S(1)}, bf16[512,1024]{1,0:T(8,128)(2,1)}, u32[]{:S(2)}) copy-start(bf16[512,1024]{1,0:T(8,128)(2,1)} %q_ref.5) | copy-start | bytes 3145732
  9.5 6.2 %collective-permute-start.1 = (bf16[4,128,128]{2,1,0:T(8,128)(2,1)S(1)}, bf16[4,128,128]{2,1,0:T(8,128)(2,1)S(1)}, u32[]{:S(2)}, u32[]{:S(2)}) collective-permute-start(bf16[4,128,128]{2,1,0:T(8,128)(2,1)S(1)} %shard_map.75), channel_id=1, source_target_pairs={{0,8},{4,12},{16,24},{20,28},{1,9},{5,13},{17,25},{21,29},{2,10},{... | collective-permute-start | bytes 393224 | tf_op jit(solution)/shard_map/ppermute | solution.py:127
  15.7 0.7 copy-start.11
  16.4 4.8 %collective-permute-start.2 = (bf16[4,128,128]{2,1,0:T(8,128)(2,1)}, bf16[4,128,128]{2,1,0:T(8,128)(2,1)}, u32[]{:S(2)}, u32[]{:S(2)}) collective-permute-start(bf16[4,128,128]{2,1,0:T(8,128)(2,1)} %shard_map.76), channel_id=1, source_target_pairs={{8,16},{12,20},{9,17},{13,21},{10,18},{14,22},{11,19},{15,23}} | collective-permute-start | bytes 393224 | tf_op jit(solution)/shard_map/ppermute | solution.py:129
  17.7 3.5 %collective-permute-start.3 = (bf16[4,128,128]{2,1,0:T(8,128)(2,1)}, bf16[4,128,128]{2,1,0:T(8,128)(2,1)}, u32[]{:S(2)}, u32[]{:S(2)}) collective-permute-start(bf16[4,128,128]{2,1,0:T(8,128)(2,1)} %shard_map.76), channel_id=1, source_target_pairs={{8,24},{12,28},{9,25},{13,29},{10,26},{14,30},{11,27},{15,31}} | collective-permute-start | bytes 393224 | tf_op jit(solution)/shard_map/ppermute | solution.py:130
  19.1 15.5 %copy-start.3 = (bf16[512,1024]{1,0:T(8,128)(2,1)S(1)}, bf16[512,1024]{1,0:T(8,128)(2,1)}, u32[]{:S(2)}) copy-start(bf16[512,1024]{1,0:T(8,128)(2,1)} %v_ref.7) | copy-start | bytes 3145732
  20.1 1.0 copy-start.6
  21.2 0.9 copy-start.12
  23.2 12.4 %collective-permute-start.4 = (bf16[4,128,128]{2,1,0:T(8,128)(2,1)S(1)}, bf16[4,128,128]{2,1,0:T(8,128)(2,1)S(1)}, u32[]{:S(2)}, u32[]{:S(2)}) collective-permute-start(bf16[4,128,128]{2,1,0:T(8,128)(2,1)S(1)} %get-tuple-element.39), channel_id=1, source_target_pairs={{0,4},{4,0},{8,12},{12,8},{16,20},{20,16},{24,28},{28,24},{1,5},{5... | collective-permute-start | bytes 393224 | tf_op jit(solution)/shard_map/ppermute | solution.py:137
  24.9 10.8 %copy-start.7 = (f32[512,512]{1,0:T(8,128)S(1)}, f32[512,512]{1,0:T(8,128)}, u32[]{:S(2)}) copy-start(f32[512,512]{1,0:T(8,128)} %copy-done.6) | copy-start | bytes 3145732
  24.9 10.8 %copy-start.8 = (bf16[512,1024]{1,0:T(8,128)(2,1)S(1)}, bf16[512,1024]{1,0:T(8,128)(2,1)}, u32[]{:S(2)}) copy-start(bf16[512,1024]{1,0:T(8,128)(2,1)} %gate_ref.1) | copy-start | bytes 3145732
  24.9 10.8 %copy-start.13 = (f32[8,128,128]{2,1,0:T(8,128)S(1)}, f32[8,128,128]{2,1,0:T(8,128)}, u32[]{:S(2)}) copy-start(f32[8,128,128]{2,1,0:T(8,128)} %kv_ref.1) | copy-start | bytes 1572868
  24.9 10.8 %copy-start.18 = (f32[4096]{0:T(1024)S(1)}, f32[4096]{0:T(1024)}, u32[]{:S(2)}) copy-start(f32[4096]{0:T(1024)} %param.12) | copy-start | bytes 49156
  24.9 53.2 %collective-permute-start.7 = (bf16[1024,512]{1,0:T(8,128)(2,1)}, bf16[1024,512]{1,0:T(8,128)(2,1)}, u32[]{:S(2)}, u32[]{:S(2)}) collective-permute-start(bf16[1024,512]{1,0:T(8,128)(2,1)} %refs_1_.3), channel_id=1, source_target_pairs={{0,16},{4,20},{8,24},{12,28},{16,0},{20,4},{24,8},{28,12},{1,17},{... | collective-permute-start | bytes 3145736 | tf_op jit(solution)/shard_map/ppermute | solution.py:378
  31.3 46.8 %collective-permute-start.8 = (bf16[1024,512]{1,0:T(8,128)(2,1)}, bf16[1024,512]{1,0:T(8,128)(2,1)}, u32[]{:S(2)}, u32[]{:S(2)}) collective-permute-start(bf16[1024,512]{1,0:T(8,128)(2,1)} %refs_1_.3), channel_id=1, source_target_pairs={{0,8},{4,12},{8,0},{12,4},{16,24},{20,28},{24,16},{28,20},{1,9},{5... | collective-permute-start | bytes 3145736 | tf_op jit(solution)/shard_map/ppermute | solution.py:378
  35.7 5.0 %copy-start.5 = (bf16[1024,512]{1,0:T(8,128)(2,1)S(1)}, bf16[1024,512]{1,0:T(8,128)(2,1)}, u32[]{:S(2)}) copy-start(bf16[1024,512]{1,0:T(8,128)(2,1)} %refs_1_.3) | copy-start | bytes 3145732
  37.5 42.6 %collective-permute-start.9 = (bf16[512,1024]{1,0:T(8,128)(2,1)S(1)}, bf16[512,1024]{1,0:T(8,128)(2,1)S(1)}, u32[]{:S(2)}, u32[]{:S(2)}) collective-permute-start(bf16[512,1024]{1,0:T(8,128)(2,1)S(1)} %get-tuple-element.43.refs_0_), channel_id=1, source_target_pairs={{0,4},{4,0},{8,12},{12,8},{16,20},{20,16},{24,28},{28,24},{1,5},{5... | collective-permute-start | bytes 3145736 | tf_op jit(solution)/shard_map/ppermute | solution.py:397
  38.1 1.1 collective-permute-start.5
  39.2 3.5 %collective-permute-start.6 = (f32[1,128]{1,0:T(1,128)S(1)}, f32[1,128]{1,0:T(1,128)S(1)}, u32[]{:S(2)}, u32[]{:S(2)}) collective-permute-start(f32[1,128]{1,0:T(1,128)S(1)} %slice.15), channel_id=1, source_target_pairs={{0,2},{1,3},{2,0},{3,1},{4,6},{5,7},{6,4},{7,5},{8,10},{9,11},{10,... | collective-permute-start | bytes 1544 | tf_op jit(solution)/shard_map/ppermute | solution.py:402
  40.7 68.2 %collective-permute-start.19 = (bf16[1024,512]{1,0:T(8,128)(2,1)S(1)}, bf16[1024,512]{1,0:T(8,128)(2,1)S(1)}, u32[]{:S(2)}, u32[]{:S(2)}) collective-permute-start(bf16[1024,512]{1,0:T(8,128)(2,1)S(1)} %copy-done.5), channel_id=1, source_target_pairs={{8,16},{12,20},{16,8},{20,12},{9,17},{13,21},{17,9},{21,13},{10,18... | collective-permute-start | bytes 3145736 | tf_op jit(solution)/shard_map/ppermute | solution.py:378
  78.1 30.9 %collective-permute-start.20 = (bf16[1024,512]{1,0:T(8,128)(2,1)}, bf16[1024,512]{1,0:T(8,128)(2,1)S(1)}, u32[]{:S(2)}, u32[]{:S(2)}) collective-permute-start(bf16[1024,512]{1,0:T(8,128)(2,1)} %collective-permute-done.7.refs_2_), channel_id=1, source_target_pairs={{8,0},{12,4},{16,24},{20,28},{9,1},{13,5},{17,25},{21,29},{10,2},{... | collective-permute-start | bytes 3145736 | tf_op jit(solution)/shard_map/ppermute | solution.py:378
  80.8 6.3 %collective-permute-start.12 = (bf16[256,512]{1,0:T(8,128)(2,1)S(1)}, bf16[256,512]{1,0:T(8,128)(2,1)S(1)}, u32[]{:S(2)}, u32[]{:S(2)}) collective-permute-start(bf16[256,512]{1,0:T(8,128)(2,1)S(1)} %get-tuple-element.46), channel_id=1, source_target_pairs={{0,1},{1,0},{2,3},{3,2},{4,5},{5,4},{6,7},{7,6},{8,9},{9,8},{10,11... | collective-permute-start | bytes 786440 | tf_op jit(solution)/shard_map/ppermute | solution.py:425
  83.7 7.3 %collective-permute-start.14 = (bf16[256,1024]{1,0:T(8,128)(2,1)S(1)}, bf16[256,1024]{1,0:T(8,128)(2,1)S(1)}, u32[]{:S(2)}, u32[]{:S(2)}) collective-permute-start(bf16[256,1024]{1,0:T(8,128)(2,1)S(1)} %get-tuple-element.48), channel_id=1, source_target_pairs={{0,1},{1,0},{2,3},{3,2},{4,5},{5,4},{6,7},{7,6},{8,9},{9,8},{10,11... | collective-permute-start | bytes 1572872 | tf_op jit(solution)/shard_map/ppermute | solution.py:425
  87.0 4.6 %collective-permute-start.16 = (bf16[256,1024]{1,0:T(8,128)(2,1)S(1)}, bf16[256,1024]{1,0:T(8,128)(2,1)S(1)}, u32[]{:S(2)}, u32[]{:S(2)}) collective-permute-start(bf16[256,1024]{1,0:T(8,128)(2,1)S(1)} %get-tuple-element.50), channel_id=1, source_target_pairs={{0,1},{1,0},{2,3},{3,2},{4,5},{5,4},{6,7},{7,6},{8,9},{9,8},{10,11... | collective-permute-start | bytes 1572872 | tf_op jit(solution)/shard_map/ppermute | solution.py:425
  87.1 2.3 %collective-permute-start.10 = (bf16[256,512]{1,0:T(8,128)(2,1)S(1)}, bf16[256,512]{1,0:T(8,128)(2,1)S(1)}, u32[]{:S(2)}, u32[]{:S(2)}) collective-permute-start(bf16[256,512]{1,0:T(8,128)(2,1)S(1)} %get-tuple-element.44), channel_id=1, source_target_pairs={{0,1},{1,0},{2,3},{3,2},{4,5},{5,4},{6,7},{7,6},{8,9},{9,8},{10,11... | collective-permute-start | bytes 786440 | tf_op jit(solution)/shard_map/ppermute | solution.py:425
  89.4 6.3 %collective-permute-start.13 = (bf16[128,512]{1,0:T(8,128)(2,1)S(1)}, bf16[128,512]{1,0:T(8,128)(2,1)S(1)}, u32[]{:S(2)}, u32[]{:S(2)}) collective-permute-start(bf16[128,512]{1,0:T(8,128)(2,1)S(1)} %get-tuple-element.54), channel_id=1, source_target_pairs={{0,2},{1,3},{2,0},{3,1},{4,6},{5,7},{6,4},{7,5},{8,10},{9,11},{10,... | collective-permute-start | bytes 393224 | tf_op jit(solution)/shard_map/ppermute | solution.py:425
  91.0 7.6 %collective-permute-start.11 = (bf16[128,512]{1,0:T(8,128)(2,1)S(1)}, bf16[128,512]{1,0:T(8,128)(2,1)S(1)}, u32[]{:S(2)}, u32[]{:S(2)}) collective-permute-start(bf16[128,512]{1,0:T(8,128)(2,1)S(1)} %get-tuple-element.52), channel_id=1, source_target_pairs={{0,2},{1,3},{2,0},{3,1},{4,6},{5,7},{6,4},{7,5},{8,10},{9,11},{10,... | collective-permute-start | bytes 393224 | tf_op jit(solution)/shard_map/ppermute | solution.py:425
  91.6 1.7 %copy-start.9 = (f32[128,1024]{1,0:T(8,128)}, f32[128,1024]{1,0:T(8,128)S(1)}, u32[]{:S(2)}) copy-start(f32[128,1024]{1,0:T(8,128)S(1)} %get-tuple-element.66.kept_ref) | copy-start | bytes 1572868
  91.7 12.5 %collective-permute-start.15 = (bf16[128,1024]{1,0:T(8,128)(2,1)S(1)}, bf16[128,1024]{1,0:T(8,128)(2,1)S(1)}, u32[]{:S(2)}, u32[]{:S(2)}) collective-permute-start(bf16[128,1024]{1,0:T(8,128)(2,1)S(1)} %get-tuple-element.56), channel_id=1, source_target_pairs={{0,2},{1,3},{2,0},{3,1},{4,6},{5,7},{6,4},{7,5},{8,10},{9,11},{10,... | collective-permute-start | bytes 786440 | tf_op jit(solution)/shard_map/ppermute | solution.py:425
  95.7 13.2 %collective-permute-start.17 = (bf16[128,1024]{1,0:T(8,128)(2,1)S(1)}, bf16[128,1024]{1,0:T(8,128)(2,1)S(1)}, u32[]{:S(2)}, u32[]{:S(2)}) collective-permute-start(bf16[128,1024]{1,0:T(8,128)(2,1)S(1)} %get-tuple-element.58), channel_id=1, source_target_pairs={{0,2},{1,3},{2,0},{3,1},{4,6},{5,7},{6,4},{7,5},{8,10},{9,11},{10,... | collective-permute-start | bytes 786440 | tf_op jit(solution)/shard_map/ppermute | solution.py:425
  98.5 5.0 %collective-permute-start.18 = (bf16[128,512]{1,0:T(8,128)(2,1)S(1)}, bf16[128,512]{1,0:T(8,128)(2,1)S(1)}, u32[]{:S(2)}, u32[]{:S(2)}) collective-permute-start(bf16[128,512]{1,0:T(8,128)(2,1)S(1)} %shard_map.89), channel_id=1, source_target_pairs={{0,4},{4,0},{8,12},{12,8},{16,20},{20,16},{24,28},{28,24},{1,5},{5... | collective-permute-start | bytes 393224 | tf_op jit(solution)/shard_map/ppermute | solution.py:435
  103.5 0.7 copy-start.16
  104.2 6.1 %copy-start.14 = (bf16[128,1024]{1,0:T(8,128)(2,1)}, bf16[128,1024]{1,0:T(8,128)(2,1)S(1)}, u32[]{:S(2)}) copy-start(bf16[128,1024]{1,0:T(8,128)(2,1)S(1)} %collective-permute-done.15.got_ref) | copy-start | bytes 786436
  110.2 2.0 %collective-permute-start.21 = (bf16[256,1024]{1,0:T(8,128)(2,1)S(1)}, bf16[256,1024]{1,0:T(8,128)(2,1)S(1)}, u32[]{:S(2)}, u32[]{:S(2)}) collective-permute-start(bf16[256,1024]{1,0:T(8,128)(2,1)S(1)} %get-tuple-element.62), channel_id=1, source_target_pairs={{0,1},{1,0},{2,3},{3,2},{4,5},{5,4},{6,7},{7,6},{8,9},{9,8},{10,11... | collective-permute-start | bytes 1572872 | tf_op jit(solution)/shard_map/ppermute | solution.py:425
  110.4 8.8 %collective-permute-start.23 = (bf16[128,1024]{1,0:T(8,128)(2,1)S(1)}, bf16[128,1024]{1,0:T(8,128)(2,1)S(1)}, u32[]{:S(2)}, u32[]{:S(2)}) collective-permute-start(bf16[128,1024]{1,0:T(8,128)(2,1)S(1)} %shard_map.94), channel_id=1, source_target_pairs={{0,4},{4,0},{8,12},{12,8},{16,20},{20,16},{24,28},{28,24},{1,5},{5... | collective-permute-start | bytes 786440 | tf_op jit(solution)/shard_map/ppermute | solution.py:435
  112.2 1.8 %copy-start.15 = (bf16[128,1024]{1,0:T(8,128)(2,1)S(1)}, bf16[128,1024]{1,0:T(8,128)(2,1)}, u32[]{:S(2)}) copy-start(bf16[128,1024]{1,0:T(8,128)(2,1)} %copy-done.14) | copy-start | bytes 786436
  112.3 1.7 %copy-start.10 = (f32[128,1024]{1,0:T(8,128)S(1)}, f32[128,1024]{1,0:T(8,128)}, u32[]{:S(2)}) copy-start(f32[128,1024]{1,0:T(8,128)} %copy-done.9) | copy-start | bytes 1572868
  112.4 8.6 %collective-permute-start.22 = (bf16[128,1024]{1,0:T(8,128)(2,1)S(1)}, bf16[128,1024]{1,0:T(8,128)(2,1)S(1)}, u32[]{:S(2)}, u32[]{:S(2)}) collective-permute-start(bf16[128,1024]{1,0:T(8,128)(2,1)S(1)} %get-tuple-element.64), channel_id=1, source_target_pairs={{0,2},{1,3},{2,0},{3,1},{4,6},{5,7},{6,4},{7,5},{8,10},{9,11},{10,... | collective-permute-start | bytes 786440 | tf_op jit(solution)/shard_map/ppermute | solution.py:425
  114.1 5.1 %copy-start.17 = (bf16[128,512]{1,0:T(8,128)(2,1)S(1)}, bf16[128,512]{1,0:T(8,128)(2,1)}, u32[]{:S(2)}) copy-start(bf16[128,512]{1,0:T(8,128)(2,1)} %copy-done.16) | copy-start | bytes 393220
  121.0 5.2 %collective-permute-start.24 = (bf16[128,512]{1,0:T(8,128)(2,1)S(1)}, bf16[128,512]{1,0:T(8,128)(2,1)S(1)}, u32[]{:S(2)}, u32[]{:S(2)}) collective-permute-start(bf16[128,512]{1,0:T(8,128)(2,1)S(1)} %get-tuple-element.70), channel_id=1, source_target_pairs={{0,4},{4,0},{8,12},{12,8},{16,20},{20,16},{24,28},{28,24},{1,5},{5... | collective-permute-start | bytes 393224 | tf_op jit(solution)/shard_map/ppermute | solution.py:435

commit v11 on v10

--- a/solution.py
+++ b/solution.py
@@ -80,6 +80,18 @@
         operands,
         [jax.ShapeDtypeStruct(values[0].shape, dtype) for dtype in dtypes],
     )
+
+
+def cut_kernel(places_ref, weight_ref, *outs):
+    first = 0
+    for out in outs:
+        out[...] = weight_ref[:, pl.ds(first, out.shape[1])]
+        first += out.shape[1]
+
+
+def cut_columns(weight, widths):
+    shapes = [jax.ShapeDtypeStruct((weight.shape[0], width), weight.dtype) for width in widths]
+    return local_call(cut_kernel, scalars(0), [weight], shapes)
 
 
 def states_kernel(part_ref, k_ref, v_ref, out_ref):
@@ -235,44 +247,48 @@
 
 def project_kernel(jobs, n_rows, choices, flag_ref, *refs):
     rows_refs = refs[:n_rows]
-    weight_refs = refs[n_rows : n_rows + sum(choices)]
-    sent_ref, kept_ref = refs[n_rows + sum(choices) :]
+    weight_refs = refs[n_rows:-2]
+    sent_ref, kept_ref = refs[-2:]
     half = sent_ref.shape[0]
 
-    def products(index, weight_ref):
-        for rows, weight, first in jobs:
-            if weight == index:
-                columns = pl.ds(first, weight_ref.shape[1])
-                product = jnp.dot(
-                    rows_refs[rows][...], weight_ref[...], preferred_element_type=jnp.float32
-                )
-                kept_ref[:, columns] = product[:half]
-                sent_ref[:, columns] = product[half:].astype(jnp.bfloat16)
-
-    first = 0
-    for index, number in enumerate(choices):
-        for k in range(number):
-            one = functools.partial(products, index, weight_refs[first + k])
-            if number == 1:
+    def products(rows, ref, source, target, width):
+        columns = pl.ds(target, width)
+        product = jnp.dot(
+            rows_refs[rows][...],
+            weight_refs[ref][:, pl.ds(source, width)],
+            preferred_element_type=jnp.float32,
+        )
+        kept_ref[:, columns] = product[:half]
+        sent_ref[:, columns] = product[half:].astype(jnp.bfloat16)
+
+    target = 0
+    for rows, weight in jobs:
+        width = choices[weight][0][2]
+        for k, (ref, source, _) in enumerate(choices[weight]):
+            one = functools.partial(products, rows, ref, source, target, width)
+            if len(choices[weight]) == 1:
                 one()
             else:
                 pl.when(flag_ref[0] == k)(one)
-        first += number
+        target += width
 
 
 def project(jobs, rows_list, weights, flag):
-    flat = [choice for weight in weights for choice in weight]
-    choices = tuple(len(weight) for weight in weights)
-    placed_jobs, total = [], 0
-    for rows, weight in jobs:
-        placed_jobs.append((rows, weight, total))
-        total += weights[weight][0].shape[1]
+    arrays, choices = [], []
+    for weight in weights:
+        choices.append([])
+        for array, first, width in weight:
+            known = [n for n, other in enumerate(arrays) if other is array]
+            if not known:
+                arrays.append(array)
+            choices[-1].append((known[0] if known else len(arrays) - 1, first, width))
     height, depth = rows_list[0].shape
+    total = sum(choices[weight][0][2] for _, weight in jobs)
     shape = (height // 2, total)
     return local_call(
-        functools.partial(project_kernel, tuple(placed_jobs), len(rows_list), choices),
+        functools.partial(project_kernel, tuple(jobs), len(rows_list), choices),
         flag,
-        [*rows_list, *flat],
+        [*rows_list, *arrays],
         [jax.ShapeDtypeStruct(shape, jnp.bfloat16), jax.ShapeDtypeStruct(shape, jnp.float32)],
         2 * height * depth * total,
     )
@@ -384,16 +400,27 @@
         causal_part(queries, key_input, value_input, some, heads - some),
     ]
 
-    own_columns = hold(out_weight, *stepped)
-    w_halves = along(own_columns, SWAP_HALVES)
-    w_next = along(own_columns, SWAP_NEXT)
-    w_middle = along(own_columns, SWAP_MIDDLE)
+    if width % DH == 0 and width > DH:
+        cuts = [(0, DH), (DH, width - DH)]
+        w_cuts = list(cut_columns(out_weight, [size for _, size in cuts]))
+    else:
+        cuts, w_cuts = [(0, width)], [out_weight]
+    w_cuts[0] = hold(w_cuts[0], *stepped)
+    w_halves = [along(w_cuts[0], SWAP_HALVES)]
+    w_next = [along(w_cuts[0], SWAP_NEXT)]
+    if len(cuts) > 1:
+        terms[0] = hold(terms[0], w_halves[0], w_next[0])
 
     bits = n_head.bit_length() - 1
     order = [int(format(j, "b").zfill(bits)[::-1], 2) for j in range(n_head)] if bits else [0]
     hidden, squares = gated_hidden(
         queries, inners, kv_state, terms, gate_input, norm_gain, h, i, order
     )
+    for w_cut in w_cuts[1:]:
+        w_cut = hold(w_cut, *w_halves, *w_next)
+        w_next.append(along(w_cut, SWAP_NEXT))
+        w_halves.append(along(w_cut, SWAP_HALVES))
+    w_middle = along(hold(out_weight, *stepped), SWAP_MIDDLE)
     others = [lax.ppermute(hidden, "seq", turn_pairs(n_seq, turn)) for turn in range(1, inner)]
 
     out_rows = tok_rows // n_head
@@ -409,20 +436,26 @@
     rows_list = [hidden] + others
 
     owners = [z ^ block for block in range(LINE)]
-    blocks = [(out_weight,), (w_next,), (w_halves,)]
+    blocks = [
+        [((out_weight, 0, width),)],
+        [((w, 0, size),) for w, (_, size) in zip(w_next, cuts)],
+        [((w, 0, size),) for w, (_, size) in zip(w_halves, cuts)],
+    ]
 
     def summed(parts, pins, pin_end=None):
-        weights = sorted({block for _, own in parts for block in own})
-        jobs = [(p, weights.index(block)) for p, (_, own) in enumerate(parts) for block in own]
-        sent, kept = project(
-            jobs,
-            [rows_list[turn] for turn, _ in parts],
-            [blocks[block] for block in weights],
-            hold(flag, *pins),
-        )
-        first_sent, bit = sent, 1
+        weights, jobs = [], []
+        where = {}
+        for p, (_, own) in enumerate(parts):
+            for block in own:
+                if block not in where:
+                    where[block] = range(len(weights), len(weights) + len(blocks[block]))
+                    weights += blocks[block]
+                jobs += [(p, n) for n in where[block]]
+        sent, kept = project(jobs, [rows_list[turn] for turn, _ in parts], weights, hold(flag, *pins))
+        first_sent, steps, bit = sent, [], 1
         while bit < n_head:
             got = lax.ppermute(sent, "head", flip_pairs(n_head, bit))
+            steps.append(got)
             bit *= 2
             if bit < n_head:
                 sent, kept = fold(kept, got)
@@ -435,28 +468,31 @@
                 piece = lax.ppermute(piece, "seq", turn_pairs(n_seq, -turn))
             starts = [(owners[block] * inner + (i + turn) % inner) * width for block in own]
             pieces.append((piece, starts))
-        return pieces, first_sent, got
+        return pieces, first_sent, steps
 
     turns = list(range(inner))
     shape = (out_rows, width * n_seq)
     in_kernel = width % DH == 0 and out_rows == DH
 
-    pieces, pins, ends = [], [w_halves, w_next], []
+    pieces, pins, ends = [], [], []
 
     def group(members, some):
-        more, sent, end = summed([(turn, some) for turn in members], pins)
+        more, sent, steps = summed([(turn, some) for turn in members], pins)
         pieces.extend(more)
-        ends.append(end)
+        ends.append(steps[-1])
         pins[:] = [sent, squares]
         return [piece for piece, _ in more]
 
+    w_ends = [along(w, TO_ENDS) for w in w_halves[:-1]]
     group(turns[:1], [0])
+    pins += w_ends
     returned = group(turns[1:], [0]) if inner > 1 else []
-    w_ends = along(w_halves, TO_ENDS)
-    blocks.append((w_middle, w_ends))
-    group(turns[:1], [1, 2])
-    if inner > 1:
-        group(turns[1:], [1, 2])
+    w_ends.append(along(hold(w_halves[-1], *ends), TO_ENDS))
+    blocks.append([((w_middle, first, size), (w, 0, size)) for w, (first, size) in zip(w_ends, cuts)])
+    for block in (1, 2):
+        group(turns[:1], [block])
+        if inner > 1:
+            group(turns[1:], [block])
     filled = placed(None, pieces, squares, width, shape, total_width) if in_kernel else None
     last, _, _ = summed(
         [(turn, [3]) for turn in turns], [*pins, *ends, *returned], filled

time: 128 us -> 154 us (1.20)
  Pallas kernels: 18.8 us -> 27 us
  waiting for transfers between devices: 68.6 us -> 75.8 us
  local copies, waits for them, and re-layouts: 5.12 us -> 12.1 us
  starting transfers between devices: 34.5 us -> 38.2 us
    ppermute x4 -> x7, waiting for transfers between devices: 35.3 us -> 43.6 us  [along(): return lax.ppermute(value, 'seq', line_pairs(n_seq, hops))]
    pallas_call x24 -> x31, Pallas kernels: 17.4 us -> 25.6 us  [local_call(): pl.pallas_call(kernel, in_specs=[pl.BlockSpec(memory_space=pltpu.SMEM)] +...]
    unnamed x38, local copies, waits for them, and re-layouts: 5.03 us -> 12 us
    ppermute x10 -> x14, waiting for transfers between devices: 11.4 us -> 16.3 us  [summed(): got = lax.ppermute(sent, 'head', flip_pairs(n_head, bit))]
    ppermute x3 -> x4, waiting for transfers between devices: 13.9 us -> 10.3 us  [summed(): piece = lax.ppermute(piece, 'seq', turn_pairs(n_seq, -turn))]
    ppermute x10 -> x14, starting transfers between devices: 8.05 us -> 10.5 us  [summed(): got = lax.ppermute(sent, 'head', flip_pairs(n_head, bit))]
    ppermute x2, waiting for transfers between devices: 2.43 us -> 0.09 us  [shards(): lax.ppermute(squares[half:], 'head', flip_pairs(n_head, bit))]
    ppermute x3 -> x4, starting transfers between devices: 1.74 us -> 3.3 us  [summed(): piece = lax.ppermute(piece, 'seq', turn_pairs(n_seq, -turn))]
  transfers between devices with their start and end apart: 25 -> 33, of which waited for: 13 -> 17; matrix products, arithmetic and copies ran while one was open for 0% -> 0% of each run, Pallas kernels for 11% -> 13%
where the time goes in v11:
time: 154 us
  waiting for transfers between devices  75.8 us (49%)
  starting transfers between devices  38.2 us (25%)
  Pallas kernels  27 us (18%)
  local copies, waits for them, and re-layouts  12.1 us (8%)
    ppermute x7, waiting for transfers between devices, along(): return lax.ppermute(value, 'seq', line_pairs(n_seq, hops))  43.6 us
    pallas_call x31, Pallas kernels, local_call(): pl.pallas_call(kernel, in_specs=[pl.BlockSpec(memory_space=pltpu.SMEM)] +...  25.6 us
    ppermute x14, waiting for transfers between devices, summed(): got = lax.ppermute(sent, 'head', flip_pairs(n_head, bit))  16.3 us
    unnamed x38, local copies, waits for them, and re-layouts  12 us
    ppermute x14, starting transfers between devices, summed(): got = lax.ppermute(sent, 'head', flip_pairs(n_head, bit))  10.5 us
    ppermute x7, starting transfers between devices, along(): return lax.ppermute(value, 'seq', line_pairs(n_seq, hops))  10.4 us
    ppermute x4, waiting for transfers between devices, summed(): piece = lax.ppermute(piece, 'seq', turn_pairs(n_seq, -turn))  10.3 us
    ppermute x1, starting transfers between devices, state_prefix(): from_left = lax.ppermute(first, 'seq', line_pairs(n_seq, [(0, 1), (2, 3)]))  3.74 us
  transfers between devices with their start and end apart: 33, of which 17 were waited for; matrix products, arithmetic and copies ran while one was open for 0% of the time, Pallas kernels for 13%

profile of v11, /device:TPU:0, one launch (start us, length us, event | category | flops | bytes accessed | tf_op | source)
XLA Modules:
  0.0 153.7 jit_solution(10097189189349743007)
XLA Ops:
  0.0 1.2 copy-done
  1.2 1.2 copy-done.2
  2.9 3.0 %collective-permute-start = (bf16[4,128,128]{2,1,0:T(8,128)(2,1)S(1)}, bf16[4,128,128]{2,1,0:T(8,128)(2,1)S(1)}, u32[]{:S(2)}, u32[]{:S(2)}) collective-permute-start(bf16[4,128,128]{2,1,0:T(8,128)(2,1)S(1)} %shard_map.74), channel_id=1, source_target_pairs={{0,4},{4,0},{8,12},{12,8},{16,20},{20,16},{24,28},{28,24},{1,5},{5... | collective-permute-start | bytes 393224 | tf_op jit(solution)/shard_map/ppermute | solution.py:136
  6.5 3.0 %collective-permute-done.refs_1_.refs_4_ = bf16[4,128,128]{2,1,0:T(8,128)(2,1)S(1)} collective-permute-done((bf16[4,128,128]{2,1,0:T(8,128)(2,1)S(1)}, bf16[4,128,128]{2,1,0:T(8,128)(2,1)S(1)}, u32[]{:S(2)}, u32[]{:S(2)}) %collective-permute-start) | collective-permute-done | bytes 131104 | tf_op jit(solution)/shard_map/ppermute | solution.py:136
  9.5 3.7 %collective-permute-start.1 = (bf16[4,128,128]{2,1,0:T(8,128)(2,1)S(1)}, bf16[4,128,128]{2,1,0:T(8,128)(2,1)S(1)}, u32[]{:S(2)}, u32[]{:S(2)}) collective-permute-start(bf16[4,128,128]{2,1,0:T(8,128)(2,1)S(1)} %shard_map.75), channel_id=1, source_target_pairs={{0,8},{4,12},{16,24},{20,28},{1,9},{5,13},{17,25},{21,29},{2,10},{... | collective-permute-start | bytes 393224 | tf_op jit(solution)/shard_map/ppermute | solution.py:139
  13.2 2.5 %collective-permute-done.1.refs_2_.refs_0_ = bf16[4,128,128]{2,1,0:T(8,128)(2,1)S(1)} collective-permute-done((bf16[4,128,128]{2,1,0:T(8,128)(2,1)S(1)}, bf16[4,128,128]{2,1,0:T(8,128)(2,1)S(1)}, u32[]{:S(2)}, u32[]{:S(2)}) %collective-permute-start.1) | collective-permute-done | bytes 131104 | tf_op jit(solution)/shard_map/ppermute | solution.py:139
  15.7 0.7 shard_map.76
  16.4 1.3 collective-permute-start.3
  17.7 1.3 collective-permute-start.2
  19.0 2.0 %shard_map.78 = (bf16[1024,128]{1,0:T(8,128)(2,1)}, bf16[1024,384]{1,0:T(8,128)(2,1)S(1)}) custom-call(s32[1]{0:T(128)} %constant.73.clone.1.masks_ref.places_ref.place_ref.flag_ref, bf16[1024,512]{1,0:T(8,128)(2,1)} %refs_1_.3), custom_call_target="tpu_custom_call" | custom-call | bytes 2097152 | tf_op jit(solution)/shard_map/pallas_call | solution.py:49
  21.0 0.9 copy-done.18
  21.9 1.1 shard_map.79.refs_2_
  23.0 1.0 copy-done.5
  24.0 6.9 %collective-permute-start.5 = (bf16[1024,128]{1,0:T(8,128)(2,1)}, bf16[1024,128]{1,0:T(8,128)(2,1)}, u32[]{:S(2)}, u32[]{:S(2)}) collective-permute-start(bf16[1024,128]{1,0:T(8,128)(2,1)} %get-tuple-element.55), channel_id=1, source_target_pairs={{0,8},{4,12},{8,0},{12,4},{16,24},{20,28},{24,16},{28,20},{1,9},{5... | collective-permute-start | bytes 786440 | tf_op jit(solution)/shard_map/ppermute | solution.py:394
  30.9 1.7 %shard_map.77 = (f32[4,128,128]{2,1,0:T(8,128)S(1)}, bf16[4,128,128]{2,1,0:T(8,128)(2,1)}) custom-call(s32[4]{0:T(128)S(1)} %add_convert_fusion.masks_ref, bf16[4,128,128]{2,1,0:T(8,128)(2,1)S(1)} %copy-done.11, bf16[4,128,128]{2,1,0:T(8,128)(2,1)} %collective-permute-done.2.refs_1_, bf16[4,128,128]{2,1,0:T(8,128)(2,1)} %collective-permute-done.3.refs_2_, ...), custom_call_target="tpu_custom_call" | custom-call | bytes 1179648 | tf_op jit(solution)/shard_map/pallas_call | solution.py:49
  32.7 0.7 copy-done.13
  33.4 1.5 collective-permute-start.6
  34.9 1.1 shard_map.80.refs_3_
  36.0 1.0 copy-done.7
  37.1 1.3 collective-permute-done.5.refs_1_
  38.3 4.9 %collective-permute-done.4.refs_1_ = bf16[1024,128]{1,0:T(8,128)(2,1)} collective-permute-done((bf16[1024,128]{1,0:T(8,128)(2,1)}, bf16[1024,128]{1,0:T(8,128)(2,1)}, u32[]{:S(2)}, u32[]{:S(2)}) %collective-permute-start.4) | collective-permute-done | bytes 262176 | tf_op jit(solution)/shard_map/ppermute | solution.py:394
  43.2 1.2 copy-done.6
  44.5 1.2 copy-done.8
  45.7 1.2 copy-done.9
  46.9 1.0 copy-done.12
  47.9 1.7 %shard_map.81 = (bf16[512,1024]{1,0:T(8,128)(2,1)S(1)}, f32[4,128]{1,0:T(4,128)S(1)}) custom-call(s32[2]{0:T(128)S(1)} %pad_add_fusion.1.place_ref, bf16[512,1024]{1,0:T(8,128)(2,1)S(1)} %copy-done.4, bf16[512,1024]{1,0:T(8,128)(2,1)S(1)} %copy-done.9, f32[32,1,128]{2,1,0:T(1,128)S(1)} %bitcast.16, f32[8,128,128]{2,1,0:T(8,128)S(1)} %copy-done.12, ...), custom_call_target="tpu_custom_call" | custom-call | flops 268435456 | bytes 6178816 | tf_op jit(solution)/shard_map/pallas_call | solution.py:49
  49.7 0.6 copy-done.16
  50.3 1.5 collective-permute-start.10
  51.7 0.7 copy-done.17
  52.7 1.3 collective-permute-start.9
  54.0 1.6 %collective-permute-start.8 = (f32[1,128]{1,0:T(1,128)S(1)}, f32[1,128]{1,0:T(1,128)S(1)}, u32[]{:S(2)}, u32[]{:S(2)}) collective-permute-start(f32[1,128]{1,0:T(1,128)S(1)} %slice.15), channel_id=1, source_target_pairs={{0,2},{1,3},{2,0},{3,1},{4,6},{5,7},{6,4},{7,5},{8,10},{9,11},{10,... | collective-permute-start | bytes 1544 | tf_op jit(solution)/shard_map/ppermute | solution.py:429
  55.6 1.9 %shard_map.82 = (bf16[256,512]{1,0:T(8,128)(2,1)S(1)}, f32[256,512]{1,0:T(8,128)S(1)}) custom-call(s32[1]{0:T(128)} %bitcast.9.flag_ref, bf16[512,1024]{1,0:T(8,128)(2,1)S(1)} %get-tuple-element.59.refs_0_, bf16[1024,512]{1,0:T(8,128)(2,1)} %refs_1_.3), custom_call_target="tpu_custom_call" | custom-call | flops 536870912 | bytes 2883584 | tf_op jit(solution)/shard_map/pallas_call | solution.py:49
  57.6 37.5 %collective-permute-done.9.refs_3_ = bf16[1024,128]{1,0:T(8,128)(2,1)S(1)} collective-permute-done((bf16[1024,128]{1,0:T(8,128)(2,1)}, bf16[1024,128]{1,0:T(8,128)(2,1)S(1)}, u32[]{:S(2)}, u32[]{:S(2)}) %collective-permute-start.9) | collective-permute-done | bytes 262176 | tf_op jit(solution)/shard_map/ppermute | solution.py:394
  95.1 1.9 %shard_map.83 = (bf16[256,512]{1,0:T(8,128)(2,1)S(1)}, f32[256,512]{1,0:T(8,128)S(1)}) custom-call(s32[1]{0:T(128)} %bitcast.9.flag_ref, bf16[512,1024]{1,0:T(8,128)(2,1)S(1)} %collective-permute-done.10.refs_0_.refs_1_, bf16[1024,512]{1,0:T(8,128)(2,1)} %refs_1_.3), custom_call_target="tpu_custom_call" | custom-call | flops 536870912 | bytes 2883584 | tf_op jit(solution)/shard_map/pallas_call | solution.py:49
  97.1 0.7 collective-permute-start.26
  97.9 1.6 %collective-permute-start.14 = (bf16[128,512]{1,0:T(8,128)(2,1)S(1)}, bf16[128,512]{1,0:T(8,128)(2,1)S(1)}, u32[]{:S(2)}, u32[]{:S(2)}) collective-permute-start(bf16[128,512]{1,0:T(8,128)(2,1)S(1)} %get-tuple-element.74), channel_id=1, source_target_pairs={{0,2},{1,3},{2,0},{3,1},{4,6},{5,7},{6,4},{7,5},{8,10},{9,11},{10,... | collective-permute-start | bytes 393224 | tf_op jit(solution)/shard_map/ppermute | solution.py:457
  99.5 0.7 collective-permute-start.16
  100.2 4.0 %collective-permute-done.14.got_ref = bf16[128,512]{1,0:T(8,128)(2,1)S(1)} collective-permute-done((bf16[128,512]{1,0:T(8,128)(2,1)S(1)}, bf16[128,512]{1,0:T(8,128)(2,1)S(1)}, u32[]{:S(2)}, u32[]{:S(2)}) %collective-permute-start.14) | collective-permute-done | bytes 131104 | tf_op jit(solution)/shard_map/ppermute | solution.py:457
  104.3 2.4 %collective-permute-done.16.got_ref = bf16[128,512]{1,0:T(8,128)(2,1)S(1)} collective-permute-done((bf16[128,512]{1,0:T(8,128)(2,1)S(1)}, bf16[128,512]{1,0:T(8,128)(2,1)S(1)}, u32[]{:S(2)}, u32[]{:S(2)}) %collective-permute-start.16) | collective-permute-done | bytes 131104 | tf_op jit(solution)/shard_map/ppermute | solution.py:457
  106.7 1.3 collective-permute-start.27
  107.9 1.9 %shard_map.84 = (bf16[256,512]{1,0:T(8,128)(2,1)S(1)}, f32[256,512]{1,0:T(8,128)S(1)}) custom-call(s32[1]{0:T(128)} %bitcast.9.flag_ref, bf16[512,1024]{1,0:T(8,128)(2,1)S(1)} %get-tuple-element.59.refs_0_, bf16[1024,128]{1,0:T(8,128)(2,1)} %collective-permute-done.5.refs_1_, bf16[1024,384]{1,0:T(8,128)(2,1)S(1)} %collective-permute-done.11.refs_2_), custom_call_target="tpu_custom_call" | custom-call | flops 536870912 | bytes 2883584 | tf_op jit(solution)/shard_map/pallas_call | solution.py:49
  109.9 1.9 %shard_map.85 = (bf16[256,512]{1,0:T(8,128)(2,1)S(1)}, f32[256,512]{1,0:T(8,128)S(1)}) custom-call(s32[1]{0:T(128)} %bitcast.9.flag_ref, bf16[512,1024]{1,0:T(8,128)(2,1)S(1)} %collective-permute-done.10.refs_0_.refs_1_, bf16[1024,128]{1,0:T(8,128)(2,1)} %collective-permute-done.5.refs_1_, bf16[1024,384]{1,0:T(8,128)(2,1)S(1)} %collective-permute-done.11.refs_2_), custom_call_target="tpu_custom_call" | custom-call | flops 536870912 | bytes 2883584 | tf_op jit(solution)/shard_map/pallas_call | solution.py:49
  112.4 1.9 %shard_map.86 = (bf16[256,512]{1,0:T(8,128)(2,1)S(1)}, f32[256,512]{1,0:T(8,128)S(1)}) custom-call(s32[1]{0:T(128)} %bitcast.9.flag_ref, bf16[512,1024]{1,0:T(8,128)(2,1)S(1)} %get-tuple-element.59.refs_0_, bf16[1024,128]{1,0:T(8,128)(2,1)} %collective-permute-done.4.refs_1_, bf16[1024,384]{1,0:T(8,128)(2,1)S(1)} %collective-permute-done.12.refs_2_), custom_call_target="tpu_custom_call" | custom-call | flops 536870912 | bytes 2883584 | tf_op jit(solution)/shard_map/pallas_call | solution.py:49
  114.5 1.9 %shard_map.87 = (bf16[256,512]{1,0:T(8,128)(2,1)S(1)}, f32[256,512]{1,0:T(8,128)S(1)}) custom-call(s32[1]{0:T(128)} %bitcast.9.flag_ref, bf16[512,1024]{1,0:T(8,128)(2,1)S(1)} %collective-permute-done.10.refs_0_.refs_1_, bf16[1024,128]{1,0:T(8,128)(2,1)} %collective-permute-done.4.refs_1_, bf16[1024,384]{1,0:T(8,128)(2,1)S(1)} %collective-permute-done.12.refs_2_), custom_call_target="tpu_custom_call" | custom-call | flops 536870912 | bytes 2883584 | tf_op jit(solution)/shard_map/pallas_call | solution.py:49
  117.0 1.6 %collective-permute-start.20 = (bf16[128,512]{1,0:T(8,128)(2,1)S(1)}, bf16[128,512]{1,0:T(8,128)(2,1)S(1)}, u32[]{:S(2)}, u32[]{:S(2)}) collective-permute-start(bf16[128,512]{1,0:T(8,128)(2,1)S(1)} %get-tuple-element.80), channel_id=1, source_target_pairs={{0,2},{1,3},{2,0},{3,1},{4,6},{5,7},{6,4},{7,5},{8,10},{9,11},{10,... | collective-permute-start | bytes 393224 | tf_op jit(solution)/shard_map/ppermute | solution.py:457
  118.6 0.6 collective-permute-start.18
  119.3 1.6 %collective-permute-start.22 = (bf16[128,512]{1,0:T(8,128)(2,1)S(1)}, bf16[128,512]{1,0:T(8,128)(2,1)S(1)}, u32[]{:S(2)}, u32[]{:S(2)}) collective-permute-start(bf16[128,512]{1,0:T(8,128)(2,1)S(1)} %get-tuple-element.82), channel_id=1, source_target_pairs={{0,2},{1,3},{2,0},{3,1},{4,6},{5,7},{6,4},{7,5},{8,10},{9,11},{10,... | collective-permute-start | bytes 393224 | tf_op jit(solution)/shard_map/ppermute | solution.py:457
  120.9 2.5 %collective-permute-done.20.got_ref = bf16[128,512]{1,0:T(8,128)(2,1)S(1)} collective-permute-done((bf16[128,512]{1,0:T(8,128)(2,1)S(1)}, bf16[128,512]{1,0:T(8,128)(2,1)S(1)}, u32[]{:S(2)}, u32[]{:S(2)}) %collective-permute-start.20) | collective-permute-done | bytes 131104 | tf_op jit(solution)/shard_map/ppermute | solution.py:457
  123.4 1.5 collective-permute-start.24
  124.9 1.3 collective-permute-done.18.got_ref
  126.2 0.5 collective-permute-start.25
  126.8 2.3 %collective-permute-done.22.got_ref = bf16[128,512]{1,0:T(8,128)(2,1)S(1)} collective-permute-done((bf16[128,512]{1,0:T(8,128)(2,1)S(1)}, bf16[128,512]{1,0:T(8,128)(2,1)S(1)}, u32[]{:S(2)}, u32[]{:S(2)}) %collective-permute-start.22) | collective-permute-done | bytes 131104 | tf_op jit(solution)/shard_map/ppermute | solution.py:457
  129.0 1.9 %collective-permute-done.24.got_ref = bf16[128,512]{1,0:T(8,128)(2,1)S(1)} collective-permute-done((bf16[128,512]{1,0:T(8,128)(2,1)S(1)}, bf16[128,512]{1,0:T(8,128)(2,1)S(1)}, u32[]{:S(2)}, u32[]{:S(2)}) %collective-permute-start.24) | collective-permute-done | bytes 131104 | tf_op jit(solution)/shard_map/ppermute | solution.py:457
  131.2 2.3 %shard_map.95 = (bf16[256,1024]{1,0:T(8,128)(2,1)S(1)}, f32[256,1024]{1,0:T(8,128)S(1)}) custom-call(s32[1]{0:T(128)} %bitcast.9.flag_ref, bf16[512,1024]{1,0:T(8,128)(2,1)S(1)} %get-tuple-element.59.refs_0_, bf16[512,1024]{1,0:T(8,128)(2,1)S(1)} %collective-permute-done.10.refs_0_.refs_1_, bf16[1024,512]{1,0:T(8,128)(2,1)S(1)} %collective-permute-done.26.refs_2_, ...), custom_call_target="tpu_custom_call" | custom-call | flops 1073741824 | bytes 5767168 | tf_op jit(solution)/shard_map/pallas_call | solution.py:49
  133.6 1.9 %collective-permute-done.28.got_ref = bf16[256,1024]{1,0:T(8,128)(2,1)S(1)} collective-permute-done((bf16[256,1024]{1,0:T(8,128)(2,1)S(1)}, bf16[256,1024]{1,0:T(8,128)(2,1)S(1)}, u32[]{:S(2)}, u32[]{:S(2)}) %collective-permute-start.28) | collective-permute-done | bytes 524320 | tf_op jit(solution)/shard_map/ppermute | solution.py:457
  135.6 1.6 %collective-permute-start.29 = (bf16[128,1024]{1,0:T(8,128)(2,1)S(1)}, bf16[128,1024]{1,0:T(8,128)(2,1)S(1)}, u32[]{:S(2)}, u32[]{:S(2)}) collective-permute-start(bf16[128,1024]{1,0:T(8,128)(2,1)S(1)} %get-tuple-element.92), channel_id=1, source_target_pairs={{0,2},{1,3},{2,0},{3,1},{4,6},{5,7},{6,4},{7,5},{8,10},{9,11},{10,... | collective-permute-start | bytes 786440 | tf_op jit(solution)/shard_map/ppermute | solution.py:457
  137.2 0.6 collective-permute-start.30
  137.9 1.6 %collective-permute-start.31 = (bf16[128,512]{1,0:T(8,128)(2,1)S(1)}, bf16[128,512]{1,0:T(8,128)(2,1)S(1)}, u32[]{:S(2)}, u32[]{:S(2)}) collective-permute-start(bf16[128,512]{1,0:T(8,128)(2,1)S(1)} %shard_map.101), channel_id=1, source_target_pairs={{0,4},{4,0},{8,12},{12,8},{16,20},{20,16},{24,28},{28,24},{1,5},{5... | collective-permute-start | bytes 393224 | tf_op jit(solution)/shard_map/ppermute | solution.py:468
  139.6 4.1 %collective-permute-done.30.refs_3_ = bf16[128,512]{1,0:T(8,128)(2,1)S(1)} collective-permute-done((bf16[128,512]{1,0:T(8,128)(2,1)S(1)}, bf16[128,512]{1,0:T(8,128)(2,1)S(1)}, u32[]{:S(2)}, u32[]{:S(2)}) %collective-permute-start.30) | collective-permute-done | bytes 131104 | tf_op jit(solution)/shard_map/ppermute | solution.py:468
  143.7 1.7 %collective-permute-done.31.refs_5_ = bf16[128,512]{1,0:T(8,128)(2,1)S(1)} collective-permute-done((bf16[128,512]{1,0:T(8,128)(2,1)S(1)}, bf16[128,512]{1,0:T(8,128)(2,1)S(1)}, u32[]{:S(2)}, u32[]{:S(2)}) %collective-permute-start.31) | collective-permute-done | bytes 131104 | tf_op jit(solution)/shard_map/ppermute | solution.py:468
  145.4 1.8 %shard_map.102.refs_2_ = bf16[128,4096]{1,0:T(8,128)(2,1)} custom-call(s32[6]{0:T(128)S(1)} %stack.86.starts_ref, f32[1,128]{1,0:T(1,128)S(1)} %slice_add_fusion.1.squares_ref, bf16[128,512]{1,0:T(8,128)(2,1)S(1)} %shard_map.97.refs_0_, bf16[128,512]{1,0:T(8,128)(2,1)S(1)} %collective-permute-done.25.refs_1_, bf16[128,512]{1,0:T(8,128)(2,1)S(1)} %shard_map.98.refs_2_, ...), custom_call_target="tpu_custom_call" | custom-call | bytes 1835520 | tf_op jit(solution)/shard_map/pallas_call | solution.py:49
  147.2 0.6 collective-permute-start.32
  147.9 4.4 %collective-permute-done.32.refs_1_ = bf16[128,512]{1,0:T(8,128)(2,1)S(1)} collective-permute-done((bf16[128,512]{1,0:T(8,128)(2,1)S(1)}, bf16[128,512]{1,0:T(8,128)(2,1)S(1)}, u32[]{:S(2)}, u32[]{:S(2)}) %collective-permute-start.32) | collective-permute-done | bytes 131104 | tf_op jit(solution)/shard_map/ppermute | solution.py:468
  152.3 1.4 shard_map.104
  (80 shorter events, 3.9 us)
Async XLA Ops:
  0.0 1.2 copy-start
  1.2 1.2 copy-start.2
  2.5 3.5 %copy-start.1 = (bf16[512,1024]{1,0:T(8,128)(2,1)S(1)}, bf16[512,1024]{1,0:T(8,128)(2,1)}, u32[]{:S(2)}) copy-start(bf16[512,1024]{1,0:T(8,128)(2,1)} %k_ref.7) | copy-start | bytes 3145732
  2.9 6.5 %collective-permute-start = (bf16[4,128,128]{2,1,0:T(8,128)(2,1)S(1)}, bf16[4,128,128]{2,1,0:T(8,128)(2,1)S(1)}, u32[]{:S(2)}, u32[]{:S(2)}) collective-permute-start(bf16[4,128,128]{2,1,0:T(8,128)(2,1)S(1)} %shard_map.74), channel_id=1, source_target_pairs={{0,4},{4,0},{8,12},{12,8},{16,20},{20,16},{24,28},{28,24},{1,5},{5... | collective-permute-start | bytes 393224 | tf_op jit(solution)/shard_map/ppermute | solution.py:136
  6.4 15.4 %copy-start.3 = (bf16[512,1024]{1,0:T(8,128)(2,1)S(1)}, bf16[512,1024]{1,0:T(8,128)(2,1)}, u32[]{:S(2)}) copy-start(bf16[512,1024]{1,0:T(8,128)(2,1)} %v_ref.7) | copy-start | bytes 3145732
  6.4 15.4 %copy-start.4 = (bf16[512,1024]{1,0:T(8,128)(2,1)S(1)}, bf16[512,1024]{1,0:T(8,128)(2,1)}, u32[]{:S(2)}) copy-start(bf16[512,1024]{1,0:T(8,128)(2,1)} %q_ref.5) | copy-start | bytes 3145732
  9.5 6.2 %collective-permute-start.1 = (bf16[4,128,128]{2,1,0:T(8,128)(2,1)S(1)}, bf16[4,128,128]{2,1,0:T(8,128)(2,1)S(1)}, u32[]{:S(2)}, u32[]{:S(2)}) collective-permute-start(bf16[4,128,128]{2,1,0:T(8,128)(2,1)S(1)} %shard_map.75), channel_id=1, source_target_pairs={{0,8},{4,12},{16,24},{20,28},{1,9},{5,13},{17,25},{21,29},{2,10},{... | collective-permute-start | bytes 393224 | tf_op jit(solution)/shard_map/ppermute | solution.py:139
  15.7 0.7 copy-start.10
  16.4 7.5 %collective-permute-start.3 = (bf16[4,128,128]{2,1,0:T(8,128)(2,1)}, bf16[4,128,128]{2,1,0:T(8,128)(2,1)}, u32[]{:S(2)}, u32[]{:S(2)}) collective-permute-start(bf16[4,128,128]{2,1,0:T(8,128)(2,1)} %shard_map.76), channel_id=1, source_target_pairs={{8,24},{12,28},{9,25},{13,29},{10,26},{14,30},{11,27},{15,31}} | collective-permute-start | bytes 393224 | tf_op jit(solution)/shard_map/ppermute | solution.py:142
  17.7 6.2 %collective-permute-start.2 = (bf16[4,128,128]{2,1,0:T(8,128)(2,1)}, bf16[4,128,128]{2,1,0:T(8,128)(2,1)}, u32[]{:S(2)}, u32[]{:S(2)}) collective-permute-start(bf16[4,128,128]{2,1,0:T(8,128)(2,1)} %shard_map.76), channel_id=1, source_target_pairs={{8,16},{12,20},{9,17},{13,21},{10,18},{14,22},{11,19},{15,23}} | collective-permute-start | bytes 393224 | tf_op jit(solution)/shard_map/ppermute | solution.py:141
  21.0 0.9 copy-start.18
  21.9 9.1 %copy-start.11 = (bf16[4,128,128]{2,1,0:T(8,128)(2,1)S(1)}, bf16[4,128,128]{2,1,0:T(8,128)(2,1)}, u32[]{:S(2)}) copy-start(bf16[4,128,128]{2,1,0:T(8,128)(2,1)} %copy-done.10) | copy-start | bytes 393220
  23.0 1.0 copy-start.5
  24.0 14.4 %collective-permute-start.5 = (bf16[1024,128]{1,0:T(8,128)(2,1)}, bf16[1024,128]{1,0:T(8,128)(2,1)}, u32[]{:S(2)}, u32[]{:S(2)}) collective-permute-start(bf16[1024,128]{1,0:T(8,128)(2,1)} %get-tuple-element.55), channel_id=1, source_target_pairs={{0,8},{4,12},{8,0},{12,4},{16,24},{20,28},{24,16},{28,20},{1,9},{5... | collective-permute-start | bytes 786440 | tf_op jit(solution)/shard_map/ppermute | solution.py:394
  30.9 12.3 %collective-permute-start.4 = (bf16[1024,128]{1,0:T(8,128)(2,1)}, bf16[1024,128]{1,0:T(8,128)(2,1)}, u32[]{:S(2)}, u32[]{:S(2)}) collective-permute-start(bf16[1024,128]{1,0:T(8,128)(2,1)} %get-tuple-element.55), channel_id=1, source_target_pairs={{0,16},{4,20},{8,24},{12,28},{16,0},{20,4},{24,8},{28,12},{1,17},{... | collective-permute-start | bytes 786440 | tf_op jit(solution)/shard_map/ppermute | solution.py:394
  32.7 0.7 copy-start.13
  33.4 9.8 %copy-start.14 = (f32[4,128,128]{2,1,0:T(8,128)S(1)}, f32[4,128,128]{2,1,0:T(8,128)}, u32[]{:S(2)}) copy-start(f32[4,128,128]{2,1,0:T(8,128)} %copy-done.13) | copy-start | bytes 786436
  33.4 9.8 %collective-permute-start.6 = (bf16[4,128,128]{2,1,0:T(8,128)(2,1)}, bf16[4,128,128]{2,1,0:T(8,128)(2,1)S(1)}, u32[]{:S(2)}, u32[]{:S(2)}) collective-permute-start(bf16[4,128,128]{2,1,0:T(8,128)(2,1)} %get-tuple-element.57), channel_id=1, source_target_pairs={{0,4},{4,0},{8,12},{12,8},{16,20},{20,16},{24,28},{28,24},{1,5},{5... | collective-permute-start | bytes 393224 | tf_op jit(solution)/shard_map/ppermute | solution.py:149
  34.9 8.3 %copy-start.15 = (f32[4096]{0:T(1024)S(1)}, f32[4096]{0:T(1024)}, u32[]{:S(2)}) copy-start(f32[4096]{0:T(1024)} %param.12) | copy-start | bytes 49156
  36.0 1.0 copy-start.7
  43.2 1.2 copy-start.6
  44.5 1.2 copy-start.8
  45.7 1.2 copy-start.9
  46.9 1.0 copy-start.12
  49.7 0.6 copy-start.16
  50.3 44.8 %collective-permute-start.10 = (bf16[512,1024]{1,0:T(8,128)(2,1)S(1)}, bf16[512,1024]{1,0:T(8,128)(2,1)S(1)}, u32[]{:S(2)}, u32[]{:S(2)}) collective-permute-start(bf16[512,1024]{1,0:T(8,128)(2,1)S(1)} %get-tuple-element.59.refs_0_), channel_id=1, source_target_pairs={{0,4},{4,0},{8,12},{12,8},{16,20},{20,16},{24,28},{28,24},{1,5},{5... | collective-permute-start | bytes 3145736 | tf_op jit(solution)/shard_map/ppermute | solution.py:424
  51.7 0.7 copy-start.17
  52.4 1.5 collective-permute-start.7
  52.4 51.8 %collective-permute-start.12 = (bf16[1024,384]{1,0:T(8,128)(2,1)}, bf16[1024,384]{1,0:T(8,128)(2,1)S(1)}, u32[]{:S(2)}, u32[]{:S(2)}) collective-permute-start(bf16[1024,384]{1,0:T(8,128)(2,1)} %copy-done.18), channel_id=1, source_target_pairs={{0,16},{4,20},{8,24},{12,28},{16,0},{20,4},{24,8},{28,12},{1,17},{... | collective-permute-start | bytes 2359304 | tf_op jit(solution)/shard_map/ppermute | solution.py:394
  52.7 55.3 %collective-permute-start.11 = (bf16[1024,384]{1,0:T(8,128)(2,1)}, bf16[1024,384]{1,0:T(8,128)(2,1)S(1)}, u32[]{:S(2)}, u32[]{:S(2)}) collective-permute-start(bf16[1024,384]{1,0:T(8,128)(2,1)} %copy-done.18), channel_id=1, source_target_pairs={{0,8},{4,12},{8,0},{12,4},{16,24},{20,28},{24,16},{28,20},{1,9},{5... | collective-permute-start | bytes 2359304 | tf_op jit(solution)/shard_map/ppermute | solution.py:394
  52.7 42.4 %collective-permute-start.9 = (bf16[1024,128]{1,0:T(8,128)(2,1)}, bf16[1024,128]{1,0:T(8,128)(2,1)S(1)}, u32[]{:S(2)}, u32[]{:S(2)}) collective-permute-start(bf16[1024,128]{1,0:T(8,128)(2,1)} %collective-permute-done.4.refs_1_), channel_id=1, source_target_pairs={{8,0},{12,4},{16,24},{20,28},{9,1},{13,5},{17,25},{21,29},{10,2},{... | collective-permute-start | bytes 786440 | tf_op jit(solution)/shard_map/ppermute | solution.py:394
  54.0 3.6 %collective-permute-start.8 = (f32[1,128]{1,0:T(1,128)S(1)}, f32[1,128]{1,0:T(1,128)S(1)}, u32[]{:S(2)}, u32[]{:S(2)}) collective-permute-start(f32[1,128]{1,0:T(1,128)S(1)} %slice.15), channel_id=1, source_target_pairs={{0,2},{1,3},{2,0},{3,1},{4,6},{5,7},{6,4},{7,5},{8,10},{9,11},{10,... | collective-permute-start | bytes 1544 | tf_op jit(solution)/shard_map/ppermute | solution.py:429
  57.6 40.2 %collective-permute-start.13 = (bf16[256,512]{1,0:T(8,128)(2,1)S(1)}, bf16[256,512]{1,0:T(8,128)(2,1)S(1)}, u32[]{:S(2)}, u32[]{:S(2)}) collective-permute-start(bf16[256,512]{1,0:T(8,128)(2,1)S(1)} %get-tuple-element.60), channel_id=1, source_target_pairs={{0,1},{1,0},{2,3},{3,2},{4,5},{5,4},{6,7},{7,6},{8,9},{9,8},{10,11... | collective-permute-start | bytes 786440 | tf_op jit(solution)/shard_map/ppermute | solution.py:457
  97.0 2.5 %collective-permute-start.15 = (bf16[256,512]{1,0:T(8,128)(2,1)S(1)}, bf16[256,512]{1,0:T(8,128)(2,1)S(1)}, u32[]{:S(2)}, u32[]{:S(2)}) collective-permute-start(bf16[256,512]{1,0:T(8,128)(2,1)S(1)} %get-tuple-element.62), channel_id=1, source_target_pairs={{0,1},{1,0},{2,3},{3,2},{4,5},{5,4},{6,7},{7,6},{8,9},{9,8},{10,11... | collective-permute-start | bytes 786440 | tf_op jit(solution)/shard_map/ppermute | solution.py:457
  97.1 34.1 %collective-permute-start.26 = (bf16[1024,512]{1,0:T(8,128)(2,1)}, bf16[1024,512]{1,0:T(8,128)(2,1)S(1)}, u32[]{:S(2)}, u32[]{:S(2)}) collective-permute-start(bf16[1024,512]{1,0:T(8,128)(2,1)} %refs_1_.3), channel_id=1, source_target_pairs={{8,16},{12,20},{16,8},{20,12},{9,17},{13,21},{17,9},{21,13},{10,18... | collective-permute-start | bytes 3145736 | tf_op jit(solution)/shard_map/ppermute | solution.py:394
  97.9 6.4 %collective-permute-start.14 = (bf16[128,512]{1,0:T(8,128)(2,1)S(1)}, bf16[128,512]{1,0:T(8,128)(2,1)S(1)}, u32[]{:S(2)}, u32[]{:S(2)}) collective-permute-start(bf16[128,512]{1,0:T(8,128)(2,1)S(1)} %get-tuple-element.74), channel_id=1, source_target_pairs={{0,2},{1,3},{2,0},{3,1},{4,6},{5,7},{6,4},{7,5},{8,10},{9,11},{10,... | collective-permute-start | bytes 393224 | tf_op jit(solution)/shard_map/ppermute | solution.py:457
  99.5 7.1 %collective-permute-start.16 = (bf16[128,512]{1,0:T(8,128)(2,1)S(1)}, bf16[128,512]{1,0:T(8,128)(2,1)S(1)}, u32[]{:S(2)}, u32[]{:S(2)}) collective-permute-start(bf16[128,512]{1,0:T(8,128)(2,1)S(1)} %get-tuple-element.76), channel_id=1, source_target_pairs={{0,2},{1,3},{2,0},{3,1},{4,6},{5,7},{6,4},{7,5},{8,10},{9,11},{10,... | collective-permute-start | bytes 393224 | tf_op jit(solution)/shard_map/ppermute | solution.py:457
  106.7 24.5 %collective-permute-start.27 = (bf16[1024,384]{1,0:T(8,128)(2,1)S(1)}, bf16[1024,384]{1,0:T(8,128)(2,1)S(1)}, u32[]{:S(2)}, u32[]{:S(2)}) collective-permute-start(bf16[1024,384]{1,0:T(8,128)(2,1)S(1)} %collective-permute-done.12.refs_2_), channel_id=1, source_target_pairs={{8,0},{12,4},{16,24},{20,28},{9,1},{13,5},{17,25},{21,29},{10,2},{... | collective-permute-start | bytes 2359304 | tf_op jit(solution)/shard_map/ppermute | solution.py:394
  111.8 4.6 %collective-permute-start.19 = (bf16[256,512]{1,0:T(8,128)(2,1)S(1)}, bf16[256,512]{1,0:T(8,128)(2,1)S(1)}, u32[]{:S(2)}, u32[]{:S(2)}) collective-permute-start(bf16[256,512]{1,0:T(8,128)(2,1)S(1)} %get-tuple-element.68), channel_id=1, source_target_pairs={{0,1},{1,0},{2,3},{3,2},{4,5},{5,4},{6,7},{7,6},{8,9},{9,8},{10,11... | collective-permute-start | bytes 786440 | tf_op jit(solution)/shard_map/ppermute | solution.py:457
  111.9 5.1 %collective-permute-start.17 = (bf16[256,512]{1,0:T(8,128)(2,1)S(1)}, bf16[256,512]{1,0:T(8,128)(2,1)S(1)}, u32[]{:S(2)}, u32[]{:S(2)}) collective-permute-start(bf16[256,512]{1,0:T(8,128)(2,1)S(1)} %get-tuple-element.66), channel_id=1, source_target_pairs={{0,1},{1,0},{2,3},{3,2},{4,5},{5,4},{6,7},{7,6},{8,9},{9,8},{10,11... | collective-permute-start | bytes 786440 | tf_op jit(solution)/shard_map/ppermute | solution.py:457
  114.3 4.3 %collective-permute-start.21 = (bf16[256,512]{1,0:T(8,128)(2,1)S(1)}, bf16[256,512]{1,0:T(8,128)(2,1)S(1)}, u32[]{:S(2)}, u32[]{:S(2)}) collective-permute-start(bf16[256,512]{1,0:T(8,128)(2,1)S(1)} %get-tuple-element.70), channel_id=1, source_target_pairs={{0,1},{1,0},{2,3},{3,2},{4,5},{5,4},{6,7},{7,6},{8,9},{9,8},{10,11... | collective-permute-start | bytes 786440 | tf_op jit(solution)/shard_map/ppermute | solution.py:457
  116.4 2.8 %collective-permute-start.23 = (bf16[256,512]{1,0:T(8,128)(2,1)S(1)}, bf16[256,512]{1,0:T(8,128)(2,1)S(1)}, u32[]{:S(2)}, u32[]{:S(2)}) collective-permute-start(bf16[256,512]{1,0:T(8,128)(2,1)S(1)} %get-tuple-element.72), channel_id=1, source_target_pairs={{0,1},{1,0},{2,3},{3,2},{4,5},{5,4},{6,7},{7,6},{8,9},{9,8},{10,11... | collective-permute-start | bytes 786440 | tf_op jit(solution)/shard_map/ppermute | solution.py:457
  117.0 6.4 %collective-permute-start.20 = (bf16[128,512]{1,0:T(8,128)(2,1)S(1)}, bf16[128,512]{1,0:T(8,128)(2,1)S(1)}, u32[]{:S(2)}, u32[]{:S(2)}) collective-permute-start(bf16[128,512]{1,0:T(8,128)(2,1)S(1)} %get-tuple-element.80), channel_id=1, source_target_pairs={{0,2},{1,3},{2,0},{3,1},{4,6},{5,7},{6,4},{7,5},{8,10},{9,11},{10,... | collective-permute-start | bytes 393224 | tf_op jit(solution)/shard_map/ppermute | solution.py:457
  118.6 7.6 %collective-permute-start.18 = (bf16[128,512]{1,0:T(8,128)(2,1)S(1)}, bf16[128,512]{1,0:T(8,128)(2,1)S(1)}, u32[]{:S(2)}, u32[]{:S(2)}) collective-permute-start(bf16[128,512]{1,0:T(8,128)(2,1)S(1)} %get-tuple-element.78), channel_id=1, source_target_pairs={{0,2},{1,3},{2,0},{3,1},{4,6},{5,7},{6,4},{7,5},{8,10},{9,11},{10,... | collective-permute-start | bytes 393224 | tf_op jit(solution)/shard_map/ppermute | solution.py:457
  119.3 9.8 %collective-permute-start.22 = (bf16[128,512]{1,0:T(8,128)(2,1)S(1)}, bf16[128,512]{1,0:T(8,128)(2,1)S(1)}, u32[]{:S(2)}, u32[]{:S(2)}) collective-permute-start(bf16[128,512]{1,0:T(8,128)(2,1)S(1)} %get-tuple-element.82), channel_id=1, source_target_pairs={{0,2},{1,3},{2,0},{3,1},{4,6},{5,7},{6,4},{7,5},{8,10},{9,11},{10,... | collective-permute-start | bytes 393224 | tf_op jit(solution)/shard_map/ppermute | solution.py:457
  123.4 7.6 %collective-permute-start.24 = (bf16[128,512]{1,0:T(8,128)(2,1)S(1)}, bf16[128,512]{1,0:T(8,128)(2,1)S(1)}, u32[]{:S(2)}, u32[]{:S(2)}) collective-permute-start(bf16[128,512]{1,0:T(8,128)(2,1)S(1)} %get-tuple-element.84), channel_id=1, source_target_pairs={{0,2},{1,3},{2,0},{3,1},{4,6},{5,7},{6,4},{7,5},{8,10},{9,11},{10,... | collective-permute-start | bytes 393224 | tf_op jit(solution)/shard_map/ppermute | solution.py:457
  126.2 5.0 %collective-permute-start.25 = (bf16[128,512]{1,0:T(8,128)(2,1)S(1)}, bf16[128,512]{1,0:T(8,128)(2,1)S(1)}, u32[]{:S(2)}, u32[]{:S(2)}) collective-permute-start(bf16[128,512]{1,0:T(8,128)(2,1)S(1)} %shard_map.94), channel_id=1, source_target_pairs={{0,4},{4,0},{8,12},{12,8},{16,20},{20,16},{24,28},{28,24},{1,5},{5... | collective-permute-start | bytes 393224 | tf_op jit(solution)/shard_map/ppermute | solution.py:468
  133.5 2.0 %collective-permute-start.28 = (bf16[256,1024]{1,0:T(8,128)(2,1)S(1)}, bf16[256,1024]{1,0:T(8,128)(2,1)S(1)}, u32[]{:S(2)}, u32[]{:S(2)}) collective-permute-start(bf16[256,1024]{1,0:T(8,128)(2,1)S(1)} %get-tuple-element.90), channel_id=1, source_target_pairs={{0,1},{1,0},{2,3},{3,2},{4,5},{5,4},{6,7},{7,6},{8,9},{9,8},{10,11... | collective-permute-start | bytes 1572872 | tf_op jit(solution)/shard_map/ppermute | solution.py:457
  135.6 11.6 %collective-permute-start.29 = (bf16[128,1024]{1,0:T(8,128)(2,1)S(1)}, bf16[128,1024]{1,0:T(8,128)(2,1)S(1)}, u32[]{:S(2)}, u32[]{:S(2)}) collective-permute-start(bf16[128,1024]{1,0:T(8,128)(2,1)S(1)} %get-tuple-element.92), channel_id=1, source_target_pairs={{0,2},{1,3},{2,0},{3,1},{4,6},{5,7},{6,4},{7,5},{8,10},{9,11},{10,... | collective-permute-start | bytes 786440 | tf_op jit(solution)/shard_map/ppermute | solution.py:457
  137.2 6.4 %collective-permute-start.30 = (bf16[128,512]{1,0:T(8,128)(2,1)S(1)}, bf16[128,512]{1,0:T(8,128)(2,1)S(1)}, u32[]{:S(2)}, u32[]{:S(2)}) collective-permute-start(bf16[128,512]{1,0:T(8,128)(2,1)S(1)} %shard_map.99), channel_id=1, source_target_pairs={{0,4},{4,0},{8,12},{12,8},{16,20},{20,16},{24,28},{28,24},{1,5},{5... | collective-permute-start | bytes 393224 | tf_op jit(solution)/shard_map/ppermute | solution.py:468
  137.9 7.5 %collective-permute-start.31 = (bf16[128,512]{1,0:T(8,128)(2,1)S(1)}, bf16[128,512]{1,0:T(8,128)(2,1)S(1)}, u32[]{:S(2)}, u32[]{:S(2)}) collective-permute-start(bf16[128,512]{1,0:T(8,128)(2,1)S(1)} %shard_map.101), channel_id=1, source_target_pairs={{0,4},{4,0},{8,12},{12,8},{16,20},{20,16},{24,28},{28,24},{1,5},{5... | collective-permute-start | bytes 393224 | tf_op jit(solution)/shard_map/ppermute | solution.py:468
  147.2 5.0 %collective-permute-start.32 = (bf16[128,512]{1,0:T(8,128)(2,1)S(1)}, bf16[128,512]{1,0:T(8,128)(2,1)S(1)}, u32[]{:S(2)}, u32[]{:S(2)}) collective-permute-start(bf16[128,512]{1,0:T(8,128)(2,1)S(1)} %get-tuple-element.100), channel_id=1, source_target_pairs={{0,4},{4,0},{8,12},{12,8},{16,20},{20,16},{24,28},{28,24},{1,5},{5... | collective-permute-start | bytes 393224 | tf_op jit(solution)/shard_map/ppermute | solution.py:468

commit v12 on v10

--- a/solution.py
+++ b/solution.py
@@ -180,7 +180,8 @@
 
 def hidden_kernel(order, group, calls, place_ref, q_ref, gate_ref, gain_ref, kv_ref, *refs):
     terms, inners = refs[:group], refs[group : group + calls]
-    hidden_ref, squares_ref = refs[group + calls :]
+    kept_ref, sent_ref, squares_ref = refs[group + calls :]
+    half = kept_ref.shape[0]
     heads = kv_ref.shape[0]
     share = heads // group
     size = q_ref.shape[0] // len(order)
@@ -199,7 +200,8 @@
     for position, block in enumerate(order):
         start = pl.multiple_of((place_ref[0] ^ block) * size, size)
         rows = pl.ds(start, size)
-        placed = pl.ds(position * size, size)
+        hidden_ref = kept_ref if position * size < half else sent_ref
+        placed = pl.ds(position * size % half, size)
         squares = jnp.zeros((size, DH), jnp.float32)
         for head in range(heads):
             columns = pl.ds(head * DH, DH)
@@ -221,12 +223,14 @@
 
 def gated_hidden(queries, inners, kv_state, terms, gate_input, norm_gain, h, i, order):
     rows, width = queries.shape
+    half = jax.ShapeDtypeStruct((rows // 2, width), jnp.bfloat16)
     return local_call(
         functools.partial(hidden_kernel, order, len(terms), len(inners)),
         scalars(h, i),
         [queries, gate_input, norm_gain.reshape(-1, 1, DH), kv_state, *terms, *inners],
         [
-            jax.ShapeDtypeStruct((rows, width), jnp.bfloat16),
+            half,
+            half,
             jax.ShapeDtypeStruct((len(order), rows // len(order)), jnp.float32),
         ],
         4 * rows * width * DH,
@@ -234,20 +238,21 @@
 
 
 def project_kernel(jobs, n_rows, choices, flag_ref, *refs):
-    rows_refs = refs[:n_rows]
-    weight_refs = refs[n_rows : n_rows + sum(choices)]
-    sent_ref, kept_ref = refs[n_rows + sum(choices) :]
-    half = sent_ref.shape[0]
+    rows_refs = refs[: 2 * n_rows]
+    weight_refs = refs[2 * n_rows : -2]
+    sent_ref, kept_ref = refs[-2:]
 
     def products(index, weight_ref):
         for rows, weight, first in jobs:
             if weight == index:
                 columns = pl.ds(first, weight_ref.shape[1])
-                product = jnp.dot(
-                    rows_refs[rows][...], weight_ref[...], preferred_element_type=jnp.float32
+                kept_rows, sent_rows = rows_refs[2 * rows : 2 * rows + 2]
+                sent_ref[:, columns] = jnp.dot(
+                    sent_rows[...], weight_ref[...], preferred_element_type=jnp.float32
+                ).astype(jnp.bfloat16)
+                kept_ref[:, columns] = jnp.dot(
+                    kept_rows[...], weight_ref[...], preferred_element_type=jnp.float32
                 )
-                kept_ref[:, columns] = product[:half]
-                sent_ref[:, columns] = product[half:].astype(jnp.bfloat16)
 
     first = 0
     for index, number in enumerate(choices):
@@ -267,14 +272,14 @@
     for rows, weight in jobs:
         placed_jobs.append((rows, weight, total))
         total += weights[weight][0].shape[1]
-    height, depth = rows_list[0].shape
-    shape = (height // 2, total)
+    height, depth = rows_list[0][0].shape
+    shape = (height, total)
     return local_call(
         functools.partial(project_kernel, tuple(placed_jobs), len(rows_list), choices),
         flag,
-        [*rows_list, *flat],
+        [*[half for pair in rows_list for half in pair], *flat],
         [jax.ShapeDtypeStruct(shape, jnp.bfloat16), jax.ShapeDtypeStruct(shape, jnp.float32)],
-        2 * height * depth * total,
+        4 * height * depth * total,
     )
 
 
@@ -391,10 +396,13 @@
 
     bits = n_head.bit_length() - 1
     order = [int(format(j, "b").zfill(bits)[::-1], 2) for j in range(n_head)] if bits else [0]
-    hidden, squares = gated_hidden(
+    kept_rows, sent_rows, squares = gated_hidden(
         queries, inners, kv_state, terms, gate_input, norm_gain, h, i, order
     )
-    others = [lax.ppermute(hidden, "seq", turn_pairs(n_seq, turn)) for turn in range(1, inner)]
+    rows_list = [(kept_rows, sent_rows)]
+    for turn in range(1, inner):
+        pairs = turn_pairs(n_seq, turn)
+        rows_list.append((lax.ppermute(kept_rows, "seq", pairs), lax.ppermute(sent_rows, "seq", pairs)))
 
     out_rows = tok_rows // n_head
     half, bit = n_head // 2, 1
@@ -406,7 +414,6 @@
     is_end = (z == 0) | (z == LINE - 1)
     flag = scalars(is_end)
 
-    rows_list = [hidden] + others
 
     owners = [z ^ block for block in range(LINE)]
     blocks = [(out_weight,), (w_next,), (w_halves,)]
@@ -441,7 +448,7 @@
     shape = (out_rows, width * n_seq)
     in_kernel = width % DH == 0 and out_rows == DH
 
-    pieces, pins, ends = [], [w_halves, w_next], []
+    pieces, pins, ends = [], [], []
 
     def group(members, some):
         more, sent, end = summed([(turn, some) for turn in members], pins)
@@ -452,7 +459,7 @@
 
     group(turns[:1], [0])
     returned = group(turns[1:], [0]) if inner > 1 else []
-    w_ends = along(w_halves, TO_ENDS)
+    w_ends = along(hold(w_halves, *ends), TO_ENDS)
     blocks.append((w_middle, w_ends))
     group(turns[:1], [1, 2])
     if inner > 1:

time: 128 us -> 118 us (0.922)
  waiting for transfers between devices: 68.6 us -> 52.8 us
  starting transfers between devices: 34.5 us -> 39.3 us
  Pallas kernels: 18.8 us -> 21.2 us
  local copies, waits for them, and re-layouts: 5.12 us -> 3.48 us
    ppermute x4, waiting for transfers between devices: 35.3 us -> 7.26 us  [along(): return lax.ppermute(value, 'seq', line_pairs(n_seq, hops))]
    ppermute x1 -> x2, waiting for transfers between devices: 0.01 us -> 15.5 us  [the longest x1 8.12 us: shards(): lax.ppermute(kept_rows, 'seq', pairs)]
    ppermute x10, waiting for transfers between devices: 11.4 us -> 8.8 us  [summed(): got = lax.ppermute(sent, 'head', flip_pairs(n_head, bit))]
    pallas_call x24, Pallas kernels: 17.4 us -> 19.8 us  [local_call(): pl.pallas_call(kernel, in_specs=[pl.BlockSpec(memory_space=pltpu.SMEM)] +...]
    ppermute x4, starting transfers between devices: 11.7 us -> 13.8 us  [along(): return lax.ppermute(value, 'seq', line_pairs(n_seq, hops))]
    unnamed x38 -> x20, local copies, waits for them, and re-layouts: 5.03 us -> 3.39 us
    ppermute x1 -> x2, starting transfers between devices: 0.6 us -> 2.09 us  [the longest x1 1.5 us: shards(): lax.ppermute(sent_rows, 'seq', pairs)]
  transfers between devices with their start and end apart: 25 -> 26, of which waited for: 13 -> 14; matrix products, arithmetic and copies ran while one was open for 0% -> 0% of each run, Pallas kernels for 11% -> 14%
where the time goes in v12:
time: 118 us; the launch traced here: 117 us
  waiting for transfers between devices  52.8 us (45%)
  starting transfers between devices  39.3 us (33%)
  Pallas kernels  21.2 us (18%)
  local copies, waits for them, and re-layouts  3.48 us (3%)
    pallas_call x24, Pallas kernels, local_call(): pl.pallas_call(kernel, in_specs=[pl.BlockSpec(memory_space=pltpu.SMEM)] +...  19.8 us
    ppermute x3, waiting for transfers between devices, summed(): piece = lax.ppermute(piece, 'seq', turn_pairs(n_seq, -turn))  14.5 us
    ppermute x4, starting transfers between devices, along(): return lax.ppermute(value, 'seq', line_pairs(n_seq, hops))  13.8 us
    ppermute x10, starting transfers between devices, summed(): got = lax.ppermute(sent, 'head', flip_pairs(n_head, bit))  9.21 us
    ppermute x10, waiting for transfers between devices, summed(): got = lax.ppermute(sent, 'head', flip_pairs(n_head, bit))  8.8 us
    ppermute x1, waiting for transfers between devices, shards(): lax.ppermute(kept_rows, 'seq', pairs)  8.12 us
    ppermute x1, waiting for transfers between devices, shards(): lax.ppermute(sent_rows, 'seq', pairs)  7.38 us
    ppermute x4, waiting for transfers between devices, along(): return lax.ppermute(value, 'seq', line_pairs(n_seq, hops))  7.26 us
  transfers between devices with their start and end apart: 26, of which 14 were waited for; matrix products, arithmetic and copies ran while one was open for 0% of the time, Pallas kernels for 14%

profile of v12, /device:TPU:0, one launch (start us, length us, event | category | flops | bytes accessed | tf_op | source)
XLA Modules:
  0.0 117.4 jit_solution(2816873007032785764)
XLA Ops:
  0.0 1.2 %copy-done = bf16[512,1024]{1,0:T(8,128)(2,1)S(1)} copy-done((bf16[512,1024]{1,0:T(8,128)(2,1)S(1)}, bf16[512,1024]{1,0:T(8,128)(2,1)}, u32[]{:S(2)}) %copy-start) | copy-done | bytes 1048600
  1.2 1.2 %copy-done.2 = bf16[512,1024]{1,0:T(8,128)(2,1)S(1)} copy-done((bf16[512,1024]{1,0:T(8,128)(2,1)S(1)}, bf16[512,1024]{1,0:T(8,128)(2,1)}, u32[]{:S(2)}) %copy-start.2) | copy-done | bytes 1048600
  2.5 0.5 shard_map.74
  2.9 3.0 %collective-permute-start = (bf16[4,128,128]{2,1,0:T(8,128)(2,1)S(1)}, bf16[4,128,128]{2,1,0:T(8,128)(2,1)S(1)}, u32[]{:S(2)}, u32[]{:S(2)}) collective-permute-start(bf16[4,128,128]{2,1,0:T(8,128)(2,1)S(1)} %shard_map.74), channel_id=1, source_target_pairs={{0,4},{4,0},{8,12},{12,8},{16,20},{20,16},{24,28},{28,24},{1,5},{5... | collective-permute-start | bytes 393224 | tf_op jit(solution)/shard_map/ppermute | solution.py:124
  6.0 0.5 shard_map.73.refs_0_.refs_3_
  6.4 3.0 %collective-permute-done.refs_1_.refs_4_ = bf16[4,128,128]{2,1,0:T(8,128)(2,1)S(1)} collective-permute-done((bf16[4,128,128]{2,1,0:T(8,128)(2,1)S(1)}, bf16[4,128,128]{2,1,0:T(8,128)(2,1)S(1)}, u32[]{:S(2)}, u32[]{:S(2)}) %collective-permute-start) | collective-permute-done | bytes 131104 | tf_op jit(solution)/shard_map/ppermute | solution.py:124
  9.5 3.7 %collective-permute-start.1 = (bf16[4,128,128]{2,1,0:T(8,128)(2,1)S(1)}, bf16[4,128,128]{2,1,0:T(8,128)(2,1)S(1)}, u32[]{:S(2)}, u32[]{:S(2)}) collective-permute-start(bf16[4,128,128]{2,1,0:T(8,128)(2,1)S(1)} %shard_map.75), channel_id=1, source_target_pairs={{0,8},{4,12},{16,24},{20,28},{1,9},{5,13},{17,25},{21,29},{2,10},{... | collective-permute-start | bytes 393224 | tf_op jit(solution)/shard_map/ppermute | solution.py:127
  13.2 2.5 %collective-permute-done.1.refs_2_.refs_0_ = bf16[4,128,128]{2,1,0:T(8,128)(2,1)S(1)} collective-permute-done((bf16[4,128,128]{2,1,0:T(8,128)(2,1)S(1)}, bf16[4,128,128]{2,1,0:T(8,128)(2,1)S(1)}, u32[]{:S(2)}, u32[]{:S(2)}) %collective-permute-start.1) | collective-permute-done | bytes 131104 | tf_op jit(solution)/shard_map/ppermute | solution.py:127
  15.7 0.7 shard_map.76
  16.4 1.3 %collective-permute-start.2 = (bf16[4,128,128]{2,1,0:T(8,128)(2,1)}, bf16[4,128,128]{2,1,0:T(8,128)(2,1)}, u32[]{:S(2)}, u32[]{:S(2)}) collective-permute-start(bf16[4,128,128]{2,1,0:T(8,128)(2,1)} %shard_map.76), channel_id=1, source_target_pairs={{8,16},{12,20},{9,17},{13,21},{10,18},{14,22},{11,19},{15,23}} | collective-permute-start | bytes 393224 | tf_op jit(solution)/shard_map/ppermute | solution.py:129
  17.8 1.3 %collective-permute-start.3 = (bf16[4,128,128]{2,1,0:T(8,128)(2,1)}, bf16[4,128,128]{2,1,0:T(8,128)(2,1)}, u32[]{:S(2)}, u32[]{:S(2)}) collective-permute-start(bf16[4,128,128]{2,1,0:T(8,128)(2,1)} %shard_map.76), channel_id=1, source_target_pairs={{8,24},{12,28},{9,25},{13,29},{10,26},{14,30},{11,27},{15,31}} | collective-permute-start | bytes 393224 | tf_op jit(solution)/shard_map/ppermute | solution.py:130
  19.1 0.1 add_convert_fusion.masks_ref
  19.2 0.9 copy-done.7
  20.1 1.1 shard_map.77
  21.2 1.6 %collective-permute-start.4 = (bf16[4,128,128]{2,1,0:T(8,128)(2,1)S(1)}, bf16[4,128,128]{2,1,0:T(8,128)(2,1)S(1)}, u32[]{:S(2)}, u32[]{:S(2)}) collective-permute-start(bf16[4,128,128]{2,1,0:T(8,128)(2,1)S(1)} %get-tuple-element.40), channel_id=1, source_target_pairs={{0,4},{4,0},{8,12},{12,8},{16,20},{20,16},{24,28},{28,24},{1,5},{5... | collective-permute-start | bytes 393224 | tf_op jit(solution)/shard_map/ppermute | solution.py:137
  22.7 0.1 pad_add_fusion.1.place_ref
  22.8 8.4 %collective-permute-start.10 = (bf16[1024,512]{1,0:T(8,128)(2,1)}, bf16[1024,512]{1,0:T(8,128)(2,1)}, u32[]{:S(2)}, u32[]{:S(2)}) collective-permute-start(bf16[1024,512]{1,0:T(8,128)(2,1)} %refs_2_.3), channel_id=1, source_target_pairs={{0,16},{4,20},{8,24},{12,28},{16,0},{20,4},{24,8},{28,12},{1,17},{... | collective-permute-start | bytes 3145736 | tf_op jit(solution)/shard_map/ppermute | solution.py:383
  31.2 1.1 shard_map.78.refs_2_
  32.4 1.1 shard_map.79.refs_3_
  33.4 3.4 %collective-permute-start.9 = (bf16[1024,512]{1,0:T(8,128)(2,1)}, bf16[1024,512]{1,0:T(8,128)(2,1)}, u32[]{:S(2)}, u32[]{:S(2)}) collective-permute-start(bf16[1024,512]{1,0:T(8,128)(2,1)} %refs_2_.3), channel_id=1, source_target_pairs={{0,8},{4,12},{8,0},{12,4},{16,24},{20,28},{24,16},{28,20},{1,9},{5... | collective-permute-start | bytes 3145736 | tf_op jit(solution)/shard_map/ppermute | solution.py:383
  36.8 1.7 %shard_map.80 = (bf16[256,1024]{1,0:T(8,128)(2,1)S(1)}, bf16[256,1024]{1,0:T(8,128)(2,1)S(1)}, f32[4,128]{1,0:T(4,128)S(1)}) custom-call(s32[2]{0:T(128)S(1)} %pad_add_fusion.1.place_ref, bf16[512,1024]{1,0:T(8,128)(2,1)S(1)} %copy-done.4, bf16[512,1024]{1,0:T(8,128)(2,1)S(1)} %copy-done.5, f32[32,1,128]{2,1,0:T(1,128)S(1)} %bitcast.16, ...), custom_call_target="tpu_custom_call" | custom-call | flops 268435456 | bytes 6178816 | tf_op jit(solution)/shard_map/pallas_call | solution.py:49
  38.6 0.6 collective-permute-start.7
  39.2 1.5 %collective-permute-start.8 = (bf16[256,1024]{1,0:T(8,128)(2,1)S(1)}, bf16[256,1024]{1,0:T(8,128)(2,1)S(1)}, u32[]{:S(2)}, u32[]{:S(2)}) collective-permute-start(bf16[256,1024]{1,0:T(8,128)(2,1)S(1)} %get-tuple-element.43.refs_1_), channel_id=1, source_target_pairs={{0,4},{4,0},{8,12},{12,8},{16,20},{20,16},{24,28},{28,24},{1,5},{5... | collective-permute-start | bytes 1572872 | tf_op jit(solution)/shard_map/ppermute | solution.py:405
  40.7 1.1 collective-permute-done.5
  41.8 1.5 %collective-permute-start.6 = (f32[1,128]{1,0:T(1,128)S(1)}, f32[1,128]{1,0:T(1,128)S(1)}, u32[]{:S(2)}, u32[]{:S(2)}) collective-permute-start(f32[1,128]{1,0:T(1,128)S(1)} %slice.15), channel_id=1, source_target_pairs={{0,2},{1,3},{2,0},{3,1},{4,6},{5,7},{6,4},{7,5},{8,10},{9,11},{10,... | collective-permute-start | bytes 1544 | tf_op jit(solution)/shard_map/ppermute | solution.py:410
  43.4 1.9 %shard_map.81 = (bf16[256,512]{1,0:T(8,128)(2,1)S(1)}, f32[256,512]{1,0:T(8,128)S(1)}) custom-call(s32[1]{0:T(128)} %bitcast.9.flag_ref, bf16[256,1024]{1,0:T(8,128)(2,1)S(1)} %get-tuple-element.42.refs_0_, bf16[256,1024]{1,0:T(8,128)(2,1)S(1)} %get-tuple-element.43.refs_1_, bf16[1024,512]{1,0:T(8,128)(2,1)} %refs_2_.3), custom_call_target="tpu_custom_call" | custom-call | flops 536870912 | bytes 2883584 | tf_op jit(solution)/shard_map/pallas_call | solution.py:49
  45.3 0.1 collective-permute-done.6
  45.4 8.1 %collective-permute-done.7.refs_0_.refs_2_ = bf16[256,1024]{1,0:T(8,128)(2,1)S(1)} collective-permute-done((bf16[256,1024]{1,0:T(8,128)(2,1)S(1)}, bf16[256,1024]{1,0:T(8,128)(2,1)S(1)}, u32[]{:S(2)}, u32[]{:S(2)}) %collective-permute-start.7) | collective-permute-done | bytes 524320 | tf_op jit(solution)/shard_map/ppermute | solution.py:405
  53.5 7.4 %collective-permute-done.8.refs_1_.refs_3_ = bf16[256,1024]{1,0:T(8,128)(2,1)S(1)} collective-permute-done((bf16[256,1024]{1,0:T(8,128)(2,1)S(1)}, bf16[256,1024]{1,0:T(8,128)(2,1)S(1)}, u32[]{:S(2)}, u32[]{:S(2)}) %collective-permute-start.8) | collective-permute-done | bytes 524320 | tf_op jit(solution)/shard_map/ppermute | solution.py:405
  60.9 1.9 %shard_map.82 = (bf16[256,512]{1,0:T(8,128)(2,1)S(1)}, f32[256,512]{1,0:T(8,128)S(1)}) custom-call(s32[1]{0:T(128)} %bitcast.9.flag_ref, bf16[256,1024]{1,0:T(8,128)(2,1)S(1)} %collective-permute-done.7.refs_0_.refs_2_, bf16[256,1024]{1,0:T(8,128)(2,1)S(1)} %collective-permute-done.8.refs_1_.refs_3_, bf16[1024,512]{1,0:T(8,128)(2,1)} %refs_2_.3), custom_call_target="tpu_custom_call" | custom-call | flops 536870912 | bytes 2883584 | tf_op jit(solution)/shard_map/pallas_call | solution.py:49
  62.8 0.1 collective-permute-start.13
  62.9 0.1 shard_map.85
  63.0 1.6 %collective-permute-start.12 = (bf16[128,512]{1,0:T(8,128)(2,1)S(1)}, bf16[128,512]{1,0:T(8,128)(2,1)S(1)}, u32[]{:S(2)}, u32[]{:S(2)}) collective-permute-start(bf16[128,512]{1,0:T(8,128)(2,1)S(1)} %get-tuple-element.53), channel_id=1, source_target_pairs={{0,2},{1,3},{2,0},{3,1},{4,6},{5,7},{6,4},{7,5},{8,10},{9,11},{10,... | collective-permute-start | bytes 393224 | tf_op jit(solution)/shard_map/ppermute | solution.py:432
  64.6 0.1 shard_map.86
  64.6 1.4 %collective-permute-start.14 = (bf16[128,512]{1,0:T(8,128)(2,1)S(1)}, bf16[128,512]{1,0:T(8,128)(2,1)S(1)}, u32[]{:S(2)}, u32[]{:S(2)}) collective-permute-start(bf16[128,512]{1,0:T(8,128)(2,1)S(1)} %get-tuple-element.55), channel_id=1, source_target_pairs={{0,2},{1,3},{2,0},{3,1},{4,6},{5,7},{6,4},{7,5},{8,10},{9,11},{10,... | collective-permute-start | bytes 393224 | tf_op jit(solution)/shard_map/ppermute | solution.py:432
  66.1 0.7 collective-permute-start.20
  66.8 2.5 %collective-permute-done.12.got_ref = bf16[128,512]{1,0:T(8,128)(2,1)S(1)} collective-permute-done((bf16[128,512]{1,0:T(8,128)(2,1)S(1)}, bf16[128,512]{1,0:T(8,128)(2,1)S(1)}, u32[]{:S(2)}, u32[]{:S(2)}) %collective-permute-start.12) | collective-permute-done | bytes 131104 | tf_op jit(solution)/shard_map/ppermute | solution.py:432
  69.3 5.4 %collective-permute-done.10.refs_3_ = bf16[1024,512]{1,0:T(8,128)(2,1)} collective-permute-done((bf16[1024,512]{1,0:T(8,128)(2,1)}, bf16[1024,512]{1,0:T(8,128)(2,1)}, u32[]{:S(2)}, u32[]{:S(2)}) %collective-permute-start.10) | collective-permute-done | bytes 1048608 | tf_op jit(solution)/shard_map/ppermute | solution.py:383
  74.7 1.3 %collective-permute-start.21 = (bf16[1024,512]{1,0:T(8,128)(2,1)}, bf16[1024,512]{1,0:T(8,128)(2,1)S(1)}, u32[]{:S(2)}, u32[]{:S(2)}) collective-permute-start(bf16[1024,512]{1,0:T(8,128)(2,1)} %collective-permute-done.10.refs_3_), channel_id=1, source_target_pairs={{8,0},{12,4},{16,24},{20,28},{9,1},{13,5},{17,25},{21,29},{10,2},{... | collective-permute-start | bytes 3145736 | tf_op jit(solution)/shard_map/ppermute | solution.py:383
  76.0 2.8 %shard_map.83 = (bf16[256,1024]{1,0:T(8,128)(2,1)S(1)}, f32[256,1024]{1,0:T(8,128)S(1)}) custom-call(s32[1]{0:T(128)} %bitcast.9.flag_ref, bf16[256,1024]{1,0:T(8,128)(2,1)S(1)} %get-tuple-element.42.refs_0_, bf16[256,1024]{1,0:T(8,128)(2,1)S(1)} %get-tuple-element.43.refs_1_, bf16[1024,512]{1,0:T(8,128)(2,1)} %collective-permute-done.9.refs_2_, ...), custom_call_target="tpu_custom_call" | custom-call | flops 1073741824 | bytes 4718592 | tf_op jit(solution)/shard_map/pallas_call | solution.py:49
  78.8 0.1 collective-permute-start.15
  78.9 2.8 %shard_map.84 = (bf16[256,1024]{1,0:T(8,128)(2,1)S(1)}, f32[256,1024]{1,0:T(8,128)S(1)}) custom-call(s32[1]{0:T(128)} %bitcast.9.flag_ref, bf16[256,1024]{1,0:T(8,128)(2,1)S(1)} %collective-permute-done.7.refs_0_.refs_2_, bf16[256,1024]{1,0:T(8,128)(2,1)S(1)} %collective-permute-done.8.refs_1_.refs_3_, bf16[1024,512]{1,0:T(8,128)(2,1)} %collective-permute-done.9.refs_2_, ...), custom_call_target="tpu_custom_call" | custom-call | flops 1073741824 | bytes 4718592 | tf_op jit(solution)/shard_map/pallas_call | solution.py:49
  81.7 0.6 collective-permute-start.17
  82.3 0.1 shard_map.87
  82.4 2.4 %collective-permute-start.16 = (bf16[128,1024]{1,0:T(8,128)(2,1)S(1)}, bf16[128,1024]{1,0:T(8,128)(2,1)S(1)}, u32[]{:S(2)}, u32[]{:S(2)}) collective-permute-start(bf16[128,1024]{1,0:T(8,128)(2,1)S(1)} %get-tuple-element.57), channel_id=1, source_target_pairs={{0,2},{1,3},{2,0},{3,1},{4,6},{5,7},{6,4},{7,5},{8,10},{9,11},{10,... | collective-permute-start | bytes 786440 | tf_op jit(solution)/shard_map/ppermute | solution.py:432
  84.7 0.1 shard_map.88
  84.8 1.5 %collective-permute-start.18 = (bf16[128,1024]{1,0:T(8,128)(2,1)S(1)}, bf16[128,1024]{1,0:T(8,128)(2,1)S(1)}, u32[]{:S(2)}, u32[]{:S(2)}) collective-permute-start(bf16[128,1024]{1,0:T(8,128)(2,1)S(1)} %get-tuple-element.59), channel_id=1, source_target_pairs={{0,2},{1,3},{2,0},{3,1},{4,6},{5,7},{6,4},{7,5},{8,10},{9,11},{10,... | collective-permute-start | bytes 786440 | tf_op jit(solution)/shard_map/ppermute | solution.py:432
  86.3 0.6 collective-permute-start.19
  86.9 5.0 %collective-permute-done.19.refs_1_ = bf16[128,512]{1,0:T(8,128)(2,1)S(1)} collective-permute-done((bf16[128,512]{1,0:T(8,128)(2,1)S(1)}, bf16[128,512]{1,0:T(8,128)(2,1)S(1)}, u32[]{:S(2)}, u32[]{:S(2)}) %collective-permute-start.19) | collective-permute-done | bytes 131104 | tf_op jit(solution)/shard_map/ppermute | solution.py:442
  91.9 5.0 %collective-permute-done.18.got_ref = bf16[128,1024]{1,0:T(8,128)(2,1)S(1)} collective-permute-done((bf16[128,1024]{1,0:T(8,128)(2,1)S(1)}, bf16[128,1024]{1,0:T(8,128)(2,1)S(1)}, u32[]{:S(2)}, u32[]{:S(2)}) %collective-permute-start.18) | collective-permute-done | bytes 262176 | tf_op jit(solution)/shard_map/ppermute | solution.py:432
  96.9 1.9 %collective-permute-done.21.refs_5_ = bf16[1024,512]{1,0:T(8,128)(2,1)S(1)} collective-permute-done((bf16[1024,512]{1,0:T(8,128)(2,1)}, bf16[1024,512]{1,0:T(8,128)(2,1)S(1)}, u32[]{:S(2)}, u32[]{:S(2)}) %collective-permute-start.21) | collective-permute-done | bytes 1048608 | tf_op jit(solution)/shard_map/ppermute | solution.py:383
  98.7 1.3 %shard_map.90 = (bf16[256,1024]{1,0:T(8,128)(2,1)S(1)}, f32[256,1024]{1,0:T(8,128)S(1)}) custom-call(s32[1]{0:T(128)} %bitcast.9.flag_ref, bf16[256,1024]{1,0:T(8,128)(2,1)S(1)} %get-tuple-element.42.refs_0_, bf16[256,1024]{1,0:T(8,128)(2,1)S(1)} %get-tuple-element.43.refs_1_, bf16[256,1024]{1,0:T(8,128)(2,1)S(1)} %collective-permute-done.7.refs_0_.refs_2_, ...), custom_call_target="tpu_custom_call" | custom-call | flops 1073741824 | bytes 5767168 | tf_op jit(solution)/shard_map/pallas_call | solution.py:49
  100.0 0.1 collective-permute-start.22
  100.1 0.6 collective-permute-start.24
  100.7 1.2 %collective-permute-done.22.got_ref = bf16[256,1024]{1,0:T(8,128)(2,1)S(1)} collective-permute-done((bf16[256,1024]{1,0:T(8,128)(2,1)S(1)}, bf16[256,1024]{1,0:T(8,128)(2,1)S(1)}, u32[]{:S(2)}, u32[]{:S(2)}) %collective-permute-start.22) | collective-permute-done | bytes 524320 | tf_op jit(solution)/shard_map/ppermute | solution.py:432
  102.0 0.1 shard_map.91
  102.1 1.6 %collective-permute-start.23 = (bf16[128,1024]{1,0:T(8,128)(2,1)S(1)}, bf16[128,1024]{1,0:T(8,128)(2,1)S(1)}, u32[]{:S(2)}, u32[]{:S(2)}) collective-permute-start(bf16[128,1024]{1,0:T(8,128)(2,1)S(1)} %get-tuple-element.66), channel_id=1, source_target_pairs={{0,2},{1,3},{2,0},{3,1},{4,6},{5,7},{6,4},{7,5},{8,10},{9,11},{10,... | collective-permute-start | bytes 786440 | tf_op jit(solution)/shard_map/ppermute | solution.py:432
  103.7 0.1 stack.86.starts_ref
  103.8 5.1 %collective-permute-done.24.refs_3_ = bf16[128,1024]{1,0:T(8,128)(2,1)S(1)} collective-permute-done((bf16[128,1024]{1,0:T(8,128)(2,1)S(1)}, bf16[128,1024]{1,0:T(8,128)(2,1)S(1)}, u32[]{:S(2)}, u32[]{:S(2)}) %collective-permute-start.24) | collective-permute-done | bytes 262176 | tf_op jit(solution)/shard_map/ppermute | solution.py:442
  108.9 1.8 %shard_map.95.refs_2_ = bf16[128,4096]{1,0:T(8,128)(2,1)} custom-call(s32[6]{0:T(128)S(1)} %stack.86.starts_ref, f32[1,128]{1,0:T(1,128)S(1)} %slice_add_fusion.1.squares_ref, bf16[128,512]{1,0:T(8,128)(2,1)S(1)} %shard_map.92.refs_0_, bf16[128,512]{1,0:T(8,128)(2,1)S(1)} %collective-permute-done.19.refs_1_, bf16[128,1024]{1,0:T(8,128)(2,1)S(1)} %shard_map.93.refs_2_, ...), custom_call_target="tpu_custom_call" | custom-call | bytes 1835520 | tf_op jit(solution)/shard_map/pallas_call | solution.py:49
  110.8 0.6 collective-permute-start.25
  111.4 0.1 pad_add_fusion.starts_ref
  111.4 4.5 %collective-permute-done.25.refs_1_ = bf16[128,512]{1,0:T(8,128)(2,1)S(1)} collective-permute-done((bf16[128,512]{1,0:T(8,128)(2,1)S(1)}, bf16[128,512]{1,0:T(8,128)(2,1)S(1)}, u32[]{:S(2)}, u32[]{:S(2)}) %collective-permute-start.25) | collective-permute-done | bytes 131104 | tf_op jit(solution)/shard_map/ppermute | solution.py:442
  116.0 1.4 %shard_map.97 = bf16[128,4096]{1,0:T(8,128)(2,1)} custom-call(s32[2]{0:T(128)S(1)} %pad_add_fusion.starts_ref, f32[1,128]{1,0:T(1,128)S(1)} %slice_add_fusion.1.squares_ref, bf16[128,512]{1,0:T(8,128)(2,1)S(1)} %get-tuple-element.71.refs_0_, bf16[128,512]{1,0:T(8,128)(2,1)S(1)} %collective-permute-done.25.refs_1_, ...), custom_call_target="tpu_custom_call", output_to_operand_aliasing={{}: (4, {})} | custom-call | bytes 524288 | tf_op jit(solution)/shard_map/pallas_call | solution.py:352
  (41 shorter events, 0.3 us)
Async XLA Ops:
  0.0 1.2 %copy-start = (bf16[512,1024]{1,0:T(8,128)(2,1)S(1)}, bf16[512,1024]{1,0:T(8,128)(2,1)}, u32[]{:S(2)}) copy-start(bf16[512,1024]{1,0:T(8,128)(2,1)} %k_ref.7) | copy-start | bytes 3145732
  1.2 1.2 %copy-start.2 = (bf16[512,1024]{1,0:T(8,128)(2,1)S(1)}, bf16[512,1024]{1,0:T(8,128)(2,1)}, u32[]{:S(2)}) copy-start(bf16[512,1024]{1,0:T(8,128)(2,1)} %v_ref.7) | copy-start | bytes 3145732
  2.5 3.5 %copy-start.1 = (bf16[512,1024]{1,0:T(8,128)(2,1)S(1)}, bf16[512,1024]{1,0:T(8,128)(2,1)}, u32[]{:S(2)}) copy-start(bf16[512,1024]{1,0:T(8,128)(2,1)} %k_ref.7) | copy-start | bytes 3145732
  2.9 6.5 %collective-permute-start = (bf16[4,128,128]{2,1,0:T(8,128)(2,1)S(1)}, bf16[4,128,128]{2,1,0:T(8,128)(2,1)S(1)}, u32[]{:S(2)}, u32[]{:S(2)}) collective-permute-start(bf16[4,128,128]{2,1,0:T(8,128)(2,1)S(1)} %shard_map.74), channel_id=1, source_target_pairs={{0,4},{4,0},{8,12},{12,8},{16,20},{20,16},{24,28},{28,24},{1,5},{5... | collective-permute-start | bytes 393224 | tf_op jit(solution)/shard_map/ppermute | solution.py:124
  5.9 25.3 %copy-start.4 = (bf16[512,1024]{1,0:T(8,128)(2,1)S(1)}, bf16[512,1024]{1,0:T(8,128)(2,1)}, u32[]{:S(2)}) copy-start(bf16[512,1024]{1,0:T(8,128)(2,1)} %q_ref.5) | copy-start | bytes 3145732
  6.4 24.8 %copy-start.3 = (bf16[512,1024]{1,0:T(8,128)(2,1)S(1)}, bf16[512,1024]{1,0:T(8,128)(2,1)}, u32[]{:S(2)}) copy-start(bf16[512,1024]{1,0:T(8,128)(2,1)} %v_ref.7) | copy-start | bytes 3145732
  9.5 6.2 %collective-permute-start.1 = (bf16[4,128,128]{2,1,0:T(8,128)(2,1)S(1)}, bf16[4,128,128]{2,1,0:T(8,128)(2,1)S(1)}, u32[]{:S(2)}, u32[]{:S(2)}) collective-permute-start(bf16[4,128,128]{2,1,0:T(8,128)(2,1)S(1)} %shard_map.75), channel_id=1, source_target_pairs={{0,8},{4,12},{16,24},{20,28},{1,9},{5,13},{17,25},{21,29},{2,10},{... | collective-permute-start | bytes 393224 | tf_op jit(solution)/shard_map/ppermute | solution.py:127
  15.7 0.7 copy-start.6
  16.4 2.7 %collective-permute-start.2 = (bf16[4,128,128]{2,1,0:T(8,128)(2,1)}, bf16[4,128,128]{2,1,0:T(8,128)(2,1)}, u32[]{:S(2)}, u32[]{:S(2)}) collective-permute-start(bf16[4,128,128]{2,1,0:T(8,128)(2,1)} %shard_map.76), channel_id=1, source_target_pairs={{8,16},{12,20},{9,17},{13,21},{10,18},{14,22},{11,19},{15,23}} | collective-permute-start | bytes 393224 | tf_op jit(solution)/shard_map/ppermute | solution.py:129
  17.8 1.4 %collective-permute-start.3 = (bf16[4,128,128]{2,1,0:T(8,128)(2,1)}, bf16[4,128,128]{2,1,0:T(8,128)(2,1)}, u32[]{:S(2)}, u32[]{:S(2)}) collective-permute-start(bf16[4,128,128]{2,1,0:T(8,128)(2,1)} %shard_map.76), channel_id=1, source_target_pairs={{8,24},{12,28},{9,25},{13,29},{10,26},{14,30},{11,27},{15,31}} | collective-permute-start | bytes 393224 | tf_op jit(solution)/shard_map/ppermute | solution.py:130
  19.1 0.9 copy-start.7
  21.2 15.6 %collective-permute-start.4 = (bf16[4,128,128]{2,1,0:T(8,128)(2,1)S(1)}, bf16[4,128,128]{2,1,0:T(8,128)(2,1)S(1)}, u32[]{:S(2)}, u32[]{:S(2)}) collective-permute-start(bf16[4,128,128]{2,1,0:T(8,128)(2,1)S(1)} %get-tuple-element.40), channel_id=1, source_target_pairs={{0,4},{4,0},{8,12},{12,8},{16,20},{20,16},{24,28},{28,24},{1,5},{5... | collective-permute-start | bytes 393224 | tf_op jit(solution)/shard_map/ppermute | solution.py:137
  22.8 51.9 %collective-permute-start.10 = (bf16[1024,512]{1,0:T(8,128)(2,1)}, bf16[1024,512]{1,0:T(8,128)(2,1)}, u32[]{:S(2)}, u32[]{:S(2)}) collective-permute-start(bf16[1024,512]{1,0:T(8,128)(2,1)} %refs_2_.3), channel_id=1, source_target_pairs={{0,16},{4,20},{8,24},{12,28},{16,0},{20,4},{24,8},{28,12},{1,17},{... | collective-permute-start | bytes 3145736 | tf_op jit(solution)/shard_map/ppermute | solution.py:383
  32.3 4.5 %copy-start.5 = (bf16[512,1024]{1,0:T(8,128)(2,1)S(1)}, bf16[512,1024]{1,0:T(8,128)(2,1)}, u32[]{:S(2)}) copy-start(bf16[512,1024]{1,0:T(8,128)(2,1)} %gate_ref.1) | copy-start | bytes 3145732
  32.3 4.5 %copy-start.8 = (f32[8,128,128]{2,1,0:T(8,128)S(1)}, f32[8,128,128]{2,1,0:T(8,128)}, u32[]{:S(2)}) copy-start(f32[8,128,128]{2,1,0:T(8,128)} %kv_ref.1) | copy-start | bytes 1572868
  32.3 4.5 %copy-start.9 = (f32[4096]{0:T(1024)S(1)}, f32[4096]{0:T(1024)}, u32[]{:S(2)}) copy-start(f32[4096]{0:T(1024)} %param.12) | copy-start | bytes 49156
  33.4 42.6 %collective-permute-start.9 = (bf16[1024,512]{1,0:T(8,128)(2,1)}, bf16[1024,512]{1,0:T(8,128)(2,1)}, u32[]{:S(2)}, u32[]{:S(2)}) collective-permute-start(bf16[1024,512]{1,0:T(8,128)(2,1)} %refs_2_.3), channel_id=1, source_target_pairs={{0,8},{4,12},{8,0},{12,4},{16,24},{20,28},{24,16},{28,20},{1,9},{5... | collective-permute-start | bytes 3145736 | tf_op jit(solution)/shard_map/ppermute | solution.py:383
  38.6 14.9 %collective-permute-start.7 = (bf16[256,1024]{1,0:T(8,128)(2,1)S(1)}, bf16[256,1024]{1,0:T(8,128)(2,1)S(1)}, u32[]{:S(2)}, u32[]{:S(2)}) collective-permute-start(bf16[256,1024]{1,0:T(8,128)(2,1)S(1)} %get-tuple-element.42.refs_0_), channel_id=1, source_target_pairs={{0,4},{4,0},{8,12},{12,8},{16,20},{20,16},{24,28},{28,24},{1,5},{5... | collective-permute-start | bytes 1572872 | tf_op jit(solution)/shard_map/ppermute | solution.py:405
  39.2 21.7 %collective-permute-start.8 = (bf16[256,1024]{1,0:T(8,128)(2,1)S(1)}, bf16[256,1024]{1,0:T(8,128)(2,1)S(1)}, u32[]{:S(2)}, u32[]{:S(2)}) collective-permute-start(bf16[256,1024]{1,0:T(8,128)(2,1)S(1)} %get-tuple-element.43.refs_1_), channel_id=1, source_target_pairs={{0,4},{4,0},{8,12},{12,8},{16,20},{20,16},{24,28},{28,24},{1,5},{5... | collective-permute-start | bytes 1572872 | tf_op jit(solution)/shard_map/ppermute | solution.py:405
  40.7 1.1 collective-permute-start.5
  41.8 3.5 %collective-permute-start.6 = (f32[1,128]{1,0:T(1,128)S(1)}, f32[1,128]{1,0:T(1,128)S(1)}, u32[]{:S(2)}, u32[]{:S(2)}) collective-permute-start(f32[1,128]{1,0:T(1,128)S(1)} %slice.15), channel_id=1, source_target_pairs={{0,2},{1,3},{2,0},{3,1},{4,6},{5,7},{6,4},{7,5},{8,10},{9,11},{10,... | collective-permute-start | bytes 1544 | tf_op jit(solution)/shard_map/ppermute | solution.py:410
  45.4 17.5 %collective-permute-start.11 = (bf16[256,512]{1,0:T(8,128)(2,1)S(1)}, bf16[256,512]{1,0:T(8,128)(2,1)S(1)}, u32[]{:S(2)}, u32[]{:S(2)}) collective-permute-start(bf16[256,512]{1,0:T(8,128)(2,1)S(1)} %get-tuple-element.44), channel_id=1, source_target_pairs={{0,1},{1,0},{2,3},{3,2},{4,5},{5,4},{6,7},{7,6},{8,9},{9,8},{10,11... | collective-permute-start | bytes 786440 | tf_op jit(solution)/shard_map/ppermute | solution.py:432
  62.8 1.7 %collective-permute-start.13 = (bf16[256,512]{1,0:T(8,128)(2,1)S(1)}, bf16[256,512]{1,0:T(8,128)(2,1)S(1)}, u32[]{:S(2)}, u32[]{:S(2)}) collective-permute-start(bf16[256,512]{1,0:T(8,128)(2,1)S(1)} %get-tuple-element.46), channel_id=1, source_target_pairs={{0,1},{1,0},{2,3},{3,2},{4,5},{5,4},{6,7},{7,6},{8,9},{9,8},{10,11... | collective-permute-start | bytes 786440 | tf_op jit(solution)/shard_map/ppermute | solution.py:432
  63.0 6.4 %collective-permute-start.12 = (bf16[128,512]{1,0:T(8,128)(2,1)S(1)}, bf16[128,512]{1,0:T(8,128)(2,1)S(1)}, u32[]{:S(2)}, u32[]{:S(2)}) collective-permute-start(bf16[128,512]{1,0:T(8,128)(2,1)S(1)} %get-tuple-element.53), channel_id=1, source_target_pairs={{0,2},{1,3},{2,0},{3,1},{4,6},{5,7},{6,4},{7,5},{8,10},{9,11},{10,... | collective-permute-start | bytes 393224 | tf_op jit(solution)/shard_map/ppermute | solution.py:432
  64.6 10.1 %collective-permute-start.14 = (bf16[128,512]{1,0:T(8,128)(2,1)S(1)}, bf16[128,512]{1,0:T(8,128)(2,1)S(1)}, u32[]{:S(2)}, u32[]{:S(2)}) collective-permute-start(bf16[128,512]{1,0:T(8,128)(2,1)S(1)} %get-tuple-element.55), channel_id=1, source_target_pairs={{0,2},{1,3},{2,0},{3,1},{4,6},{5,7},{6,4},{7,5},{8,10},{9,11},{10,... | collective-permute-start | bytes 393224 | tf_op jit(solution)/shard_map/ppermute | solution.py:432
  66.1 30.8 %collective-permute-start.20 = (bf16[1024,512]{1,0:T(8,128)(2,1)}, bf16[1024,512]{1,0:T(8,128)(2,1)S(1)}, u32[]{:S(2)}, u32[]{:S(2)}) collective-permute-start(bf16[1024,512]{1,0:T(8,128)(2,1)} %refs_2_.3), channel_id=1, source_target_pairs={{8,16},{12,20},{16,8},{20,12},{9,17},{13,21},{17,9},{21,13},{10,18... | collective-permute-start | bytes 3145736 | tf_op jit(solution)/shard_map/ppermute | solution.py:383
  74.7 24.0 %collective-permute-start.21 = (bf16[1024,512]{1,0:T(8,128)(2,1)}, bf16[1024,512]{1,0:T(8,128)(2,1)S(1)}, u32[]{:S(2)}, u32[]{:S(2)}) collective-permute-start(bf16[1024,512]{1,0:T(8,128)(2,1)} %collective-permute-done.10.refs_3_), channel_id=1, source_target_pairs={{8,0},{12,4},{16,24},{20,28},{9,1},{13,5},{17,25},{21,29},{10,2},{... | collective-permute-start | bytes 3145736 | tf_op jit(solution)/shard_map/ppermute | solution.py:383
  78.8 3.4 %collective-permute-start.15 = (bf16[256,1024]{1,0:T(8,128)(2,1)S(1)}, bf16[256,1024]{1,0:T(8,128)(2,1)S(1)}, u32[]{:S(2)}, u32[]{:S(2)}) collective-permute-start(bf16[256,1024]{1,0:T(8,128)(2,1)S(1)} %get-tuple-element.49), channel_id=1, source_target_pairs={{0,1},{1,0},{2,3},{3,2},{4,5},{5,4},{6,7},{7,6},{8,9},{9,8},{10,11... | collective-permute-start | bytes 1572872 | tf_op jit(solution)/shard_map/ppermute | solution.py:432
  81.7 3.0 %collective-permute-start.17 = (bf16[256,1024]{1,0:T(8,128)(2,1)S(1)}, bf16[256,1024]{1,0:T(8,128)(2,1)S(1)}, u32[]{:S(2)}, u32[]{:S(2)}) collective-permute-start(bf16[256,1024]{1,0:T(8,128)(2,1)S(1)} %get-tuple-element.51), channel_id=1, source_target_pairs={{0,1},{1,0},{2,3},{3,2},{4,5},{5,4},{6,7},{7,6},{8,9},{9,8},{10,11... | collective-permute-start | bytes 1572872 | tf_op jit(solution)/shard_map/ppermute | solution.py:432
  82.4 9.5 %collective-permute-start.16 = (bf16[128,1024]{1,0:T(8,128)(2,1)S(1)}, bf16[128,1024]{1,0:T(8,128)(2,1)S(1)}, u32[]{:S(2)}, u32[]{:S(2)}) collective-permute-start(bf16[128,1024]{1,0:T(8,128)(2,1)S(1)} %get-tuple-element.57), channel_id=1, source_target_pairs={{0,2},{1,3},{2,0},{3,1},{4,6},{5,7},{6,4},{7,5},{8,10},{9,11},{10,... | collective-permute-start | bytes 786440 | tf_op jit(solution)/shard_map/ppermute | solution.py:432
  84.8 12.0 %collective-permute-start.18 = (bf16[128,1024]{1,0:T(8,128)(2,1)S(1)}, bf16[128,1024]{1,0:T(8,128)(2,1)S(1)}, u32[]{:S(2)}, u32[]{:S(2)}) collective-permute-start(bf16[128,1024]{1,0:T(8,128)(2,1)S(1)} %get-tuple-element.59), channel_id=1, source_target_pairs={{0,2},{1,3},{2,0},{3,1},{4,6},{5,7},{6,4},{7,5},{8,10},{9,11},{10,... | collective-permute-start | bytes 786440 | tf_op jit(solution)/shard_map/ppermute | solution.py:432
  86.3 5.5 %collective-permute-start.19 = (bf16[128,512]{1,0:T(8,128)(2,1)S(1)}, bf16[128,512]{1,0:T(8,128)(2,1)S(1)}, u32[]{:S(2)}, u32[]{:S(2)}) collective-permute-start(bf16[128,512]{1,0:T(8,128)(2,1)S(1)} %shard_map.89), channel_id=1, source_target_pairs={{0,4},{4,0},{8,12},{12,8},{16,20},{20,16},{24,28},{28,24},{1,5},{5... | collective-permute-start | bytes 393224 | tf_op jit(solution)/shard_map/ppermute | solution.py:442
  100.0 2.0 %collective-permute-start.22 = (bf16[256,1024]{1,0:T(8,128)(2,1)S(1)}, bf16[256,1024]{1,0:T(8,128)(2,1)S(1)}, u32[]{:S(2)}, u32[]{:S(2)}) collective-permute-start(bf16[256,1024]{1,0:T(8,128)(2,1)S(1)} %get-tuple-element.64), channel_id=1, source_target_pairs={{0,1},{1,0},{2,3},{3,2},{4,5},{5,4},{6,7},{7,6},{8,9},{9,8},{10,11... | collective-permute-start | bytes 1572872 | tf_op jit(solution)/shard_map/ppermute | solution.py:432
  100.1 8.8 %collective-permute-start.24 = (bf16[128,1024]{1,0:T(8,128)(2,1)S(1)}, bf16[128,1024]{1,0:T(8,128)(2,1)S(1)}, u32[]{:S(2)}, u32[]{:S(2)}) collective-permute-start(bf16[128,1024]{1,0:T(8,128)(2,1)S(1)} %shard_map.94), channel_id=1, source_target_pairs={{0,4},{4,0},{8,12},{12,8},{16,20},{20,16},{24,28},{28,24},{1,5},{5... | collective-permute-start | bytes 786440 | tf_op jit(solution)/shard_map/ppermute | solution.py:442
  102.1 8.7 %collective-permute-start.23 = (bf16[128,1024]{1,0:T(8,128)(2,1)S(1)}, bf16[128,1024]{1,0:T(8,128)(2,1)S(1)}, u32[]{:S(2)}, u32[]{:S(2)}) collective-permute-start(bf16[128,1024]{1,0:T(8,128)(2,1)S(1)} %get-tuple-element.66), channel_id=1, source_target_pairs={{0,2},{1,3},{2,0},{3,1},{4,6},{5,7},{6,4},{7,5},{8,10},{9,11},{10,... | collective-permute-start | bytes 786440 | tf_op jit(solution)/shard_map/ppermute | solution.py:432
  110.8 5.2 %collective-permute-start.25 = (bf16[128,512]{1,0:T(8,128)(2,1)S(1)}, bf16[128,512]{1,0:T(8,128)(2,1)S(1)}, u32[]{:S(2)}, u32[]{:S(2)}) collective-permute-start(bf16[128,512]{1,0:T(8,128)(2,1)S(1)} %get-tuple-element.72), channel_id=1, source_target_pairs={{0,4},{4,0},{8,12},{12,8},{16,20},{20,16},{24,28},{28,24},{1,5},{5... | collective-permute-start | bytes 393224 | tf_op jit(solution)/shard_map/ppermute | solution.py:442

commit v13 on v12

--- a/solution.py
+++ b/solution.py
@@ -391,7 +391,7 @@
 
     own_columns = hold(out_weight, *stepped)
     w_halves = along(own_columns, SWAP_HALVES)
-    w_next = along(own_columns, SWAP_NEXT)
+    w_next = along(hold(own_columns, terms[0]), SWAP_NEXT)
     w_middle = along(own_columns, SWAP_MIDDLE)
 
     bits = n_head.bit_length() - 1
@@ -461,13 +461,13 @@
     returned = group(turns[1:], [0]) if inner > 1 else []
     w_ends = along(hold(w_halves, *ends), TO_ENDS)
     blocks.append((w_middle, w_ends))
-    group(turns[:1], [1, 2])
-    if inner > 1:
-        group(turns[1:], [1, 2])
-    filled = placed(None, pieces, squares, width, shape, total_width) if in_kernel else None
-    last, _, _ = summed(
-        [(turn, [3]) for turn in turns], [*pins, *ends, *returned], filled
-    )
+    for block in (2, 1) if inner > 1 else ():
+        returned += group(turns[1:], [block])
+    group(turns[:1], [2, 1])
+    if in_kernel:
+        filled = placed(None, pieces, squares, width, shape, total_width)
+        pins.append(filled)
+    last, _, _ = summed([(turn, [3]) for turn in turns], [*pins, *ends, *returned])
     if in_kernel:
         return placed(filled, last, squares, width, shape, total_width)
     scale = lax.rsqrt(squares.reshape(out_rows, 1) / total_width + epsilon)

time: 118 us -> 134 us (1.14)
  waiting for transfers between devices: 52.8 us -> 59.2 us
  Pallas kernels: 21.2 us -> 25.9 us
  local copies, waits for them, and re-layouts: 3.48 us -> 7.08 us
    ppermute x10 -> x12, waiting for transfers between devices: 8.8 us -> 23.3 us  [summed(): got = lax.ppermute(sent, 'head', flip_pairs(n_head, bit))]
    ppermute x3 -> x4, waiting for transfers between devices: 14.5 us -> 7.68 us  [summed(): piece = lax.ppermute(piece, 'seq', turn_pairs(n_seq, -turn))]
    pallas_call x24 -> x27, Pallas kernels: 19.8 us -> 24.5 us  [local_call(): pl.pallas_call(kernel, in_specs=[pl.BlockSpec(memory_space=pltpu.SMEM)] +...]
    unnamed x20 -> x28, local copies, waits for them, and re-layouts: 3.39 us -> 6.99 us
    ppermute x3 -> x4, starting transfers between devices: 1.77 us -> 3.18 us  [summed(): piece = lax.ppermute(piece, 'seq', turn_pairs(n_seq, -turn))]
    ppermute x10 -> x12, starting transfers between devices: 9.21 us -> 9.07 us  [summed(): got = lax.ppermute(sent, 'head', flip_pairs(n_head, bit))]
  transfers between devices with their start and end apart: 26 -> 29, of which waited for: 14 -> 17; matrix products, arithmetic and copies ran while one was open for 0% -> 0% of each run, Pallas kernels for 14% -> 15%
where the time goes in v13:
time: 134 us; the launch traced here: 132 us
  waiting for transfers between devices  59.2 us (44%)
  starting transfers between devices  39.7 us (30%)
  Pallas kernels  25.9 us (19%)
  local copies, waits for them, and re-layouts  7.08 us (5%)
    pallas_call x27, Pallas kernels, local_call(): pl.pallas_call(kernel, in_specs=[pl.BlockSpec(memory_space=pltpu.SMEM)] +...  24.5 us
    ppermute x12, waiting for transfers between devices, summed(): got = lax.ppermute(sent, 'head', flip_pairs(n_head, bit))  23.3 us
    ppermute x4, starting transfers between devices, along(): return lax.ppermute(value, 'seq', line_pairs(n_seq, hops))  13 us
    ppermute x12, starting transfers between devices, summed(): got = lax.ppermute(sent, 'head', flip_pairs(n_head, bit))  9.07 us
    ppermute x1, waiting for transfers between devices, shards(): lax.ppermute(kept_rows, 'seq', pairs)  8.12 us
    ppermute x4, waiting for transfers between devices, summed(): piece = lax.ppermute(piece, 'seq', turn_pairs(n_seq, -turn))  7.68 us
    unnamed x28, local copies, waits for them, and re-layouts  6.99 us
    ppermute x4, waiting for transfers between devices, along(): return lax.ppermute(value, 'seq', line_pairs(n_seq, hops))  6.88 us
  transfers between devices with their start and end apart: 29, of which 17 were waited for; matrix products, arithmetic and copies ran while one was open for 0% of the time, Pallas kernels for 15%

profile of v13, /device:TPU:0, one launch (start us, length us, event | category | flops | bytes accessed | tf_op | source)
XLA Modules:
  0.0 132.4 jit_solution(4263839246751152731)
XLA Ops:
  0.0 1.2 copy-done
  1.2 1.2 copy-done.2
  2.5 0.5 shard_map.74
  2.9 3.0 %collective-permute-start = (bf16[4,128,128]{2,1,0:T(8,128)(2,1)S(1)}, bf16[4,128,128]{2,1,0:T(8,128)(2,1)S(1)}, u32[]{:S(2)}, u32[]{:S(2)}) collective-permute-start(bf16[4,128,128]{2,1,0:T(8,128)(2,1)S(1)} %shard_map.74), channel_id=1, source_target_pairs={{0,4},{4,0},{8,12},{12,8},{16,20},{20,16},{24,28},{28,24},{1,5},{5... | collective-permute-start | bytes 393224 | tf_op jit(solution)/shard_map/ppermute | solution.py:124
  6.0 0.5 shard_map.73.refs_0_.refs_3_
  6.4 3.0 %collective-permute-done.refs_1_.refs_4_ = bf16[4,128,128]{2,1,0:T(8,128)(2,1)S(1)} collective-permute-done((bf16[4,128,128]{2,1,0:T(8,128)(2,1)S(1)}, bf16[4,128,128]{2,1,0:T(8,128)(2,1)S(1)}, u32[]{:S(2)}, u32[]{:S(2)}) %collective-permute-start) | collective-permute-done | bytes 131104 | tf_op jit(solution)/shard_map/ppermute | solution.py:124
  9.5 3.7 %collective-permute-start.1 = (bf16[4,128,128]{2,1,0:T(8,128)(2,1)S(1)}, bf16[4,128,128]{2,1,0:T(8,128)(2,1)S(1)}, u32[]{:S(2)}, u32[]{:S(2)}) collective-permute-start(bf16[4,128,128]{2,1,0:T(8,128)(2,1)S(1)} %shard_map.75), channel_id=1, source_target_pairs={{0,8},{4,12},{16,24},{20,28},{1,9},{5,13},{17,25},{21,29},{2,10},{... | collective-permute-start | bytes 393224 | tf_op jit(solution)/shard_map/ppermute | solution.py:127
  13.2 2.5 %collective-permute-done.1.refs_2_.refs_0_ = bf16[4,128,128]{2,1,0:T(8,128)(2,1)S(1)} collective-permute-done((bf16[4,128,128]{2,1,0:T(8,128)(2,1)S(1)}, bf16[4,128,128]{2,1,0:T(8,128)(2,1)S(1)}, u32[]{:S(2)}, u32[]{:S(2)}) %collective-permute-start.1) | collective-permute-done | bytes 131104 | tf_op jit(solution)/shard_map/ppermute | solution.py:127
  15.7 0.7 shard_map.76
  16.4 1.3 collective-permute-start.3
  17.7 1.3 collective-permute-start.2
  19.1 0.9 copy-done.9
  20.0 1.1 shard_map.77
  21.1 1.6 %collective-permute-start.4 = (bf16[4,128,128]{2,1,0:T(8,128)(2,1)S(1)}, bf16[4,128,128]{2,1,0:T(8,128)(2,1)S(1)}, u32[]{:S(2)}, u32[]{:S(2)}) collective-permute-start(bf16[4,128,128]{2,1,0:T(8,128)(2,1)S(1)} %get-tuple-element.45), channel_id=1, source_target_pairs={{0,4},{4,0},{8,12},{12,8},{16,20},{20,16},{24,28},{28,24},{1,5},{5... | collective-permute-start | bytes 393224 | tf_op jit(solution)/shard_map/ppermute | solution.py:137
  22.8 10.9 %collective-permute-start.9 = (bf16[1024,512]{1,0:T(8,128)(2,1)}, bf16[1024,512]{1,0:T(8,128)(2,1)}, u32[]{:S(2)}, u32[]{:S(2)}) collective-permute-start(bf16[1024,512]{1,0:T(8,128)(2,1)} %refs_2_.3), channel_id=1, source_target_pairs={{0,16},{4,20},{8,24},{12,28},{16,0},{20,4},{24,8},{28,12},{1,17},{... | collective-permute-start | bytes 3145736 | tf_op jit(solution)/shard_map/ppermute | solution.py:383
  33.7 1.1 shard_map.78.refs_2_
  34.9 1.1 shard_map.79.refs_3_
  36.0 0.1 copy-done.10
  36.1 1.7 %shard_map.80 = (bf16[256,1024]{1,0:T(8,128)(2,1)S(1)}, bf16[256,1024]{1,0:T(8,128)(2,1)S(1)}, f32[4,128]{1,0:T(4,128)S(1)}) custom-call(s32[2]{0:T(128)S(1)} %pad_add_fusion.1.place_ref, bf16[512,1024]{1,0:T(8,128)(2,1)S(1)} %copy-done.4, bf16[512,1024]{1,0:T(8,128)(2,1)S(1)} %copy-done.5, f32[32,1,128]{2,1,0:T(1,128)S(1)} %bitcast.16, ...), custom_call_target="tpu_custom_call" | custom-call | flops 268435456 | bytes 6178816 | tf_op jit(solution)/shard_map/pallas_call | solution.py:49
  37.9 0.6 collective-permute-start.7
  38.5 1.5 %collective-permute-start.8 = (bf16[256,1024]{1,0:T(8,128)(2,1)S(1)}, bf16[256,1024]{1,0:T(8,128)(2,1)S(1)}, u32[]{:S(2)}, u32[]{:S(2)}) collective-permute-start(bf16[256,1024]{1,0:T(8,128)(2,1)S(1)} %get-tuple-element.48.refs_1_), channel_id=1, source_target_pairs={{0,4},{4,0},{8,12},{12,8},{16,20},{20,16},{24,28},{28,24},{1,5},{5... | collective-permute-start | bytes 1572872 | tf_op jit(solution)/shard_map/ppermute | solution.py:405
  40.0 1.1 collective-permute-done.5
  41.1 1.5 %collective-permute-start.6 = (f32[1,128]{1,0:T(1,128)S(1)}, f32[1,128]{1,0:T(1,128)S(1)}, u32[]{:S(2)}, u32[]{:S(2)}) collective-permute-start(f32[1,128]{1,0:T(1,128)S(1)} %slice.15), channel_id=1, source_target_pairs={{0,2},{1,3},{2,0},{3,1},{4,6},{5,7},{6,4},{7,5},{8,10},{9,11},{10,... | collective-permute-start | bytes 1544 | tf_op jit(solution)/shard_map/ppermute | solution.py:410
  42.6 1.9 %shard_map.81 = (bf16[256,512]{1,0:T(8,128)(2,1)S(1)}, f32[256,512]{1,0:T(8,128)S(1)}) custom-call(s32[1]{0:T(128)} %bitcast.9.flag_ref, bf16[256,1024]{1,0:T(8,128)(2,1)S(1)} %get-tuple-element.47.refs_0_, bf16[256,1024]{1,0:T(8,128)(2,1)S(1)} %get-tuple-element.48.refs_1_, bf16[1024,512]{1,0:T(8,128)(2,1)} %refs_2_.3), custom_call_target="tpu_custom_call" | custom-call | flops 536870912 | bytes 2883584 | tf_op jit(solution)/shard_map/pallas_call | solution.py:49
  44.7 8.1 %collective-permute-done.7.refs_0_.refs_2_ = bf16[256,1024]{1,0:T(8,128)(2,1)S(1)} collective-permute-done((bf16[256,1024]{1,0:T(8,128)(2,1)S(1)}, bf16[256,1024]{1,0:T(8,128)(2,1)S(1)}, u32[]{:S(2)}, u32[]{:S(2)}) %collective-permute-start.7) | collective-permute-done | bytes 524320 | tf_op jit(solution)/shard_map/ppermute | solution.py:405
  52.8 6.5 %collective-permute-done.8.refs_1_.refs_3_ = bf16[256,1024]{1,0:T(8,128)(2,1)S(1)} collective-permute-done((bf16[256,1024]{1,0:T(8,128)(2,1)S(1)}, bf16[256,1024]{1,0:T(8,128)(2,1)S(1)}, u32[]{:S(2)}, u32[]{:S(2)}) %collective-permute-start.8) | collective-permute-done | bytes 524320 | tf_op jit(solution)/shard_map/ppermute | solution.py:405
  59.3 1.9 %shard_map.82 = (bf16[256,512]{1,0:T(8,128)(2,1)S(1)}, f32[256,512]{1,0:T(8,128)S(1)}) custom-call(s32[1]{0:T(128)} %bitcast.9.flag_ref, bf16[256,1024]{1,0:T(8,128)(2,1)S(1)} %collective-permute-done.7.refs_0_.refs_2_, bf16[256,1024]{1,0:T(8,128)(2,1)S(1)} %collective-permute-done.8.refs_1_.refs_3_, bf16[1024,512]{1,0:T(8,128)(2,1)} %refs_2_.3), custom_call_target="tpu_custom_call" | custom-call | flops 536870912 | bytes 2883584 | tf_op jit(solution)/shard_map/pallas_call | solution.py:49
  61.3 1.6 %collective-permute-start.12 = (bf16[128,512]{1,0:T(8,128)(2,1)S(1)}, bf16[128,512]{1,0:T(8,128)(2,1)S(1)}, u32[]{:S(2)}, u32[]{:S(2)}) collective-permute-start(bf16[128,512]{1,0:T(8,128)(2,1)S(1)} %get-tuple-element.62), channel_id=1, source_target_pairs={{0,2},{1,3},{2,0},{3,1},{4,6},{5,7},{6,4},{7,5},{8,10},{9,11},{10,... | collective-permute-start | bytes 393224 | tf_op jit(solution)/shard_map/ppermute | solution.py:432
  63.0 1.4 %collective-permute-start.14 = (bf16[128,512]{1,0:T(8,128)(2,1)S(1)}, bf16[128,512]{1,0:T(8,128)(2,1)S(1)}, u32[]{:S(2)}, u32[]{:S(2)}) collective-permute-start(bf16[128,512]{1,0:T(8,128)(2,1)S(1)} %get-tuple-element.65), channel_id=1, source_target_pairs={{0,2},{1,3},{2,0},{3,1},{4,6},{5,7},{6,4},{7,5},{8,10},{9,11},{10,... | collective-permute-start | bytes 393224 | tf_op jit(solution)/shard_map/ppermute | solution.py:432
  64.4 0.7 collective-permute-start.24
  65.2 2.5 %collective-permute-done.12.got_ref = bf16[128,512]{1,0:T(8,128)(2,1)S(1)} collective-permute-done((bf16[128,512]{1,0:T(8,128)(2,1)S(1)}, bf16[128,512]{1,0:T(8,128)(2,1)S(1)}, u32[]{:S(2)}, u32[]{:S(2)}) %collective-permute-start.12) | collective-permute-done | bytes 131104 | tf_op jit(solution)/shard_map/ppermute | solution.py:432
  67.7 2.4 %collective-permute-done.14.got_ref = bf16[128,512]{1,0:T(8,128)(2,1)S(1)} collective-permute-done((bf16[128,512]{1,0:T(8,128)(2,1)S(1)}, bf16[128,512]{1,0:T(8,128)(2,1)S(1)}, u32[]{:S(2)}, u32[]{:S(2)}) %collective-permute-start.14) | collective-permute-done | bytes 131104 | tf_op jit(solution)/shard_map/ppermute | solution.py:432
  70.1 6.9 %collective-permute-done.9.refs_2_.refs_3_ = bf16[1024,512]{1,0:T(8,128)(2,1)} collective-permute-done((bf16[1024,512]{1,0:T(8,128)(2,1)}, bf16[1024,512]{1,0:T(8,128)(2,1)}, u32[]{:S(2)}, u32[]{:S(2)}) %collective-permute-start.9) | collective-permute-done | bytes 1048608 | tf_op jit(solution)/shard_map/ppermute | solution.py:383
  77.0 1.9 %shard_map.83 = (bf16[256,512]{1,0:T(8,128)(2,1)S(1)}, f32[256,512]{1,0:T(8,128)S(1)}) custom-call(s32[1]{0:T(128)} %bitcast.9.flag_ref, bf16[256,1024]{1,0:T(8,128)(2,1)S(1)} %collective-permute-done.7.refs_0_.refs_2_, bf16[256,1024]{1,0:T(8,128)(2,1)S(1)} %collective-permute-done.8.refs_1_.refs_3_, bf16[1024,512]{1,0:T(8,128)(2,1)} %collective-permute-done.9.refs_2_.refs_3_), custom_call_target="tpu_custom_call" | custom-call | flops 536870912 | bytes 2883584 | tf_op jit(solution)/shard_map/pallas_call | solution.py:49
  78.9 1.3 collective-permute-start.25
  80.2 1.9 %shard_map.84 = (bf16[256,512]{1,0:T(8,128)(2,1)S(1)}, f32[256,512]{1,0:T(8,128)S(1)}) custom-call(s32[1]{0:T(128)} %bitcast.9.flag_ref, bf16[256,1024]{1,0:T(8,128)(2,1)S(1)} %collective-permute-done.7.refs_0_.refs_2_, bf16[256,1024]{1,0:T(8,128)(2,1)S(1)} %collective-permute-done.8.refs_1_.refs_3_, bf16[1024,512]{1,0:T(8,128)(2,1)} %collective-permute-done.10.refs_2_), custom_call_target="tpu_custom_call" | custom-call | flops 536870912 | bytes 2883584 | tf_op jit(solution)/shard_map/pallas_call | solution.py:49
  82.1 2.8 %shard_map.85 = (bf16[256,1024]{1,0:T(8,128)(2,1)S(1)}, f32[256,1024]{1,0:T(8,128)S(1)}) custom-call(s32[1]{0:T(128)} %bitcast.9.flag_ref, bf16[256,1024]{1,0:T(8,128)(2,1)S(1)} %get-tuple-element.47.refs_0_, bf16[256,1024]{1,0:T(8,128)(2,1)S(1)} %get-tuple-element.48.refs_1_, bf16[1024,512]{1,0:T(8,128)(2,1)} %collective-permute-done.10.refs_2_, ...), custom_call_target="tpu_custom_call" | custom-call | flops 1073741824 | bytes 4718592 | tf_op jit(solution)/shard_map/pallas_call | solution.py:49
  85.0 0.5 collective-permute-start.16
  85.6 1.3 collective-permute-done.22.got_ref
  87.0 0.8 copy-done.6
  87.8 1.5 %collective-permute-start.23 = (bf16[128,1024]{1,0:T(8,128)(2,1)S(1)}, bf16[128,1024]{1,0:T(8,128)(2,1)S(1)}, u32[]{:S(2)}, u32[]{:S(2)}) collective-permute-start(bf16[128,1024]{1,0:T(8,128)(2,1)S(1)} %get-tuple-element.74), channel_id=1, source_target_pairs={{0,2},{1,3},{2,0},{3,1},{4,6},{5,7},{6,4},{7,5},{8,10},{9,11},{10,... | collective-permute-start | bytes 786440 | tf_op jit(solution)/shard_map/ppermute | solution.py:432
  89.4 0.6 collective-permute-start.17
  90.0 1.6 %collective-permute-start.20 = (bf16[128,512]{1,0:T(8,128)(2,1)S(1)}, bf16[128,512]{1,0:T(8,128)(2,1)S(1)}, u32[]{:S(2)}, u32[]{:S(2)}) collective-permute-start(bf16[128,512]{1,0:T(8,128)(2,1)S(1)} %get-tuple-element.71), channel_id=1, source_target_pairs={{0,2},{1,3},{2,0},{3,1},{4,6},{5,7},{6,4},{7,5},{8,10},{9,11},{10,... | collective-permute-start | bytes 393224 | tf_op jit(solution)/shard_map/ppermute | solution.py:432
  91.6 0.7 shard_map.89
  92.2 7.5 %collective-permute-done.17.got_ref = bf16[128,512]{1,0:T(8,128)(2,1)S(1)} collective-permute-done((bf16[128,512]{1,0:T(8,128)(2,1)S(1)}, bf16[128,512]{1,0:T(8,128)(2,1)S(1)}, u32[]{:S(2)}, u32[]{:S(2)}) %collective-permute-start.17) | collective-permute-done | bytes 131104 | tf_op jit(solution)/shard_map/ppermute | solution.py:432
  99.8 0.5 collective-permute-start.15
  100.3 0.7 shard_map.91
  101.0 0.8 collective-permute-done.20.got_ref
  101.8 0.7 collective-permute-start.18
  102.5 0.7 shard_map.93
  103.1 0.7 copy-done.11
  103.8 1.3 %collective-permute-start.21 = (bf16[128,512]{1,0:T(8,128)(2,1)}, bf16[128,512]{1,0:T(8,128)(2,1)}, u32[]{:S(2)}, u32[]{:S(2)}) collective-permute-start(bf16[128,512]{1,0:T(8,128)(2,1)} %shard_map.93), channel_id=1, source_target_pairs={{0,4},{4,0},{8,12},{12,8},{16,20},{20,16},{24,28},{28,24},{1,5},{5... | collective-permute-start | bytes 393224 | tf_op jit(solution)/shard_map/ppermute | solution.py:442
  105.3 1.0 copy-done.7
  106.3 0.9 copy-done.12
  107.3 1.5 %collective-permute-done.18.refs_2_ = bf16[128,512]{1,0:T(8,128)(2,1)} collective-permute-done((bf16[128,512]{1,0:T(8,128)(2,1)}, bf16[128,512]{1,0:T(8,128)(2,1)}, u32[]{:S(2)}, u32[]{:S(2)}) %collective-permute-start.18) | collective-permute-done | bytes 131104 | tf_op jit(solution)/shard_map/ppermute | solution.py:442
  108.9 1.8 %collective-permute-done.21.refs_3_ = bf16[128,512]{1,0:T(8,128)(2,1)} collective-permute-done((bf16[128,512]{1,0:T(8,128)(2,1)}, bf16[128,512]{1,0:T(8,128)(2,1)}, u32[]{:S(2)}, u32[]{:S(2)}) %collective-permute-start.21) | collective-permute-done | bytes 131104 | tf_op jit(solution)/shard_map/ppermute | solution.py:442
  110.7 2.3 %shard_map.96.refs_2_ = bf16[128,4096]{1,0:T(8,128)(2,1)} custom-call(s32[6]{0:T(128)S(1)} %stack.86.starts_ref, f32[1,128]{1,0:T(1,128)S(1)} %slice_add_fusion.1.squares_ref, bf16[128,512]{1,0:T(8,128)(2,1)S(1)} %shard_map.87.refs_0_, bf16[128,512]{1,0:T(8,128)(2,1)} %collective-permute-done.15.refs_1_, bf16[128,512]{1,0:T(8,128)(2,1)} %collective-permute-done.18.refs_2_, ...), custom_call_target="tpu_custom_call" | custom-call | bytes 1835520 | tf_op jit(solution)/shard_map/pallas_call | solution.py:49
  113.0 2.5 %shard_map.97 = (bf16[256,1024]{1,0:T(8,128)(2,1)S(1)}, f32[256,1024]{1,0:T(8,128)S(1)}) custom-call(s32[1]{0:T(128)} %bitcast.9.flag_ref, bf16[256,1024]{1,0:T(8,128)(2,1)S(1)} %get-tuple-element.47.refs_0_, bf16[256,1024]{1,0:T(8,128)(2,1)S(1)} %get-tuple-element.48.refs_1_, bf16[256,1024]{1,0:T(8,128)(2,1)S(1)} %collective-permute-done.7.refs_0_.refs_2_, ...), custom_call_target="tpu_custom_call" | custom-call | flops 1073741824 | bytes 5767168 | tf_op jit(solution)/shard_map/pallas_call | solution.py:49
  115.5 1.9 %collective-permute-done.26.got_ref = bf16[256,1024]{1,0:T(8,128)(2,1)S(1)} collective-permute-done((bf16[256,1024]{1,0:T(8,128)(2,1)S(1)}, bf16[256,1024]{1,0:T(8,128)(2,1)S(1)}, u32[]{:S(2)}, u32[]{:S(2)}) %collective-permute-start.26) | collective-permute-done | bytes 524320 | tf_op jit(solution)/shard_map/ppermute | solution.py:432
  117.5 1.6 %collective-permute-start.27 = (bf16[128,1024]{1,0:T(8,128)(2,1)S(1)}, bf16[128,1024]{1,0:T(8,128)(2,1)S(1)}, u32[]{:S(2)}, u32[]{:S(2)}) collective-permute-start(bf16[128,1024]{1,0:T(8,128)(2,1)S(1)} %get-tuple-element.80), channel_id=1, source_target_pairs={{0,2},{1,3},{2,0},{3,1},{4,6},{5,7},{6,4},{7,5},{8,10},{9,11},{10,... | collective-permute-start | bytes 786440 | tf_op jit(solution)/shard_map/ppermute | solution.py:432
  119.1 6.8 %collective-permute-done.27.got_ref = bf16[128,1024]{1,0:T(8,128)(2,1)S(1)} collective-permute-done((bf16[128,1024]{1,0:T(8,128)(2,1)S(1)}, bf16[128,1024]{1,0:T(8,128)(2,1)S(1)}, u32[]{:S(2)}, u32[]{:S(2)}) %collective-permute-start.27) | collective-permute-done | bytes 262176 | tf_op jit(solution)/shard_map/ppermute | solution.py:432
  126.0 0.6 collective-permute-start.28
  126.7 4.3 %collective-permute-done.28.refs_1_ = bf16[128,512]{1,0:T(8,128)(2,1)S(1)} collective-permute-done((bf16[128,512]{1,0:T(8,128)(2,1)S(1)}, bf16[128,512]{1,0:T(8,128)(2,1)S(1)}, u32[]{:S(2)}, u32[]{:S(2)}) %collective-permute-start.28) | collective-permute-done | bytes 131104 | tf_op jit(solution)/shard_map/ppermute | solution.py:442
  131.0 1.4 %shard_map.100 = bf16[128,4096]{1,0:T(8,128)(2,1)} custom-call(s32[2]{0:T(128)S(1)} %pad_add_fusion.starts_ref, f32[1,128]{1,0:T(1,128)S(1)} %slice_add_fusion.1.squares_ref, bf16[128,512]{1,0:T(8,128)(2,1)S(1)} %get-tuple-element.81.refs_0_, bf16[128,512]{1,0:T(8,128)(2,1)S(1)} %collective-permute-done.28.refs_1_, ...), custom_call_target="tpu_custom_call", output_to_operand_aliasing={{}: (4, {})} | custom-call | bytes 524288 | tf_op jit(solution)/shard_map/pallas_call | solution.py:352
  (58 shorter events, 1.4 us)
Async XLA Ops:
  0.0 1.2 copy-start
  1.2 1.2 copy-start.2
  2.5 3.5 %copy-start.1 = (bf16[512,1024]{1,0:T(8,128)(2,1)S(1)}, bf16[512,1024]{1,0:T(8,128)(2,1)}, u32[]{:S(2)}) copy-start(bf16[512,1024]{1,0:T(8,128)(2,1)} %k_ref.7) | copy-start | bytes 3145732
  2.9 6.5 %collective-permute-start = (bf16[4,128,128]{2,1,0:T(8,128)(2,1)S(1)}, bf16[4,128,128]{2,1,0:T(8,128)(2,1)S(1)}, u32[]{:S(2)}, u32[]{:S(2)}) collective-permute-start(bf16[4,128,128]{2,1,0:T(8,128)(2,1)S(1)} %shard_map.74), channel_id=1, source_target_pairs={{0,4},{4,0},{8,12},{12,8},{16,20},{20,16},{24,28},{28,24},{1,5},{5... | collective-permute-start | bytes 393224 | tf_op jit(solution)/shard_map/ppermute | solution.py:124
  5.9 27.7 %copy-start.4 = (bf16[512,1024]{1,0:T(8,128)(2,1)S(1)}, bf16[512,1024]{1,0:T(8,128)(2,1)}, u32[]{:S(2)}) copy-start(bf16[512,1024]{1,0:T(8,128)(2,1)} %q_ref.5) | copy-start | bytes 3145732
  6.4 27.2 %copy-start.3 = (bf16[512,1024]{1,0:T(8,128)(2,1)S(1)}, bf16[512,1024]{1,0:T(8,128)(2,1)}, u32[]{:S(2)}) copy-start(bf16[512,1024]{1,0:T(8,128)(2,1)} %v_ref.7) | copy-start | bytes 3145732
  9.5 6.2 %collective-permute-start.1 = (bf16[4,128,128]{2,1,0:T(8,128)(2,1)S(1)}, bf16[4,128,128]{2,1,0:T(8,128)(2,1)S(1)}, u32[]{:S(2)}, u32[]{:S(2)}) collective-permute-start(bf16[4,128,128]{2,1,0:T(8,128)(2,1)S(1)} %shard_map.75), channel_id=1, source_target_pairs={{0,8},{4,12},{16,24},{20,28},{1,9},{5,13},{17,25},{21,29},{2,10},{... | collective-permute-start | bytes 393224 | tf_op jit(solution)/shard_map/ppermute | solution.py:127
  15.7 0.7 copy-start.8
  16.4 2.7 %collective-permute-start.3 = (bf16[4,128,128]{2,1,0:T(8,128)(2,1)}, bf16[4,128,128]{2,1,0:T(8,128)(2,1)}, u32[]{:S(2)}, u32[]{:S(2)}) collective-permute-start(bf16[4,128,128]{2,1,0:T(8,128)(2,1)} %shard_map.76), channel_id=1, source_target_pairs={{8,24},{12,28},{9,25},{13,29},{10,26},{14,30},{11,27},{15,31}} | collective-permute-start | bytes 393224 | tf_op jit(solution)/shard_map/ppermute | solution.py:130
  17.7 1.4 %collective-permute-start.2 = (bf16[4,128,128]{2,1,0:T(8,128)(2,1)}, bf16[4,128,128]{2,1,0:T(8,128)(2,1)}, u32[]{:S(2)}, u32[]{:S(2)}) collective-permute-start(bf16[4,128,128]{2,1,0:T(8,128)(2,1)} %shard_map.76), channel_id=1, source_target_pairs={{8,16},{12,20},{9,17},{13,21},{10,18},{14,22},{11,19},{15,23}} | collective-permute-start | bytes 393224 | tf_op jit(solution)/shard_map/ppermute | solution.py:129
  19.1 0.9 copy-start.9
  21.1 14.8 %collective-permute-start.4 = (bf16[4,128,128]{2,1,0:T(8,128)(2,1)S(1)}, bf16[4,128,128]{2,1,0:T(8,128)(2,1)S(1)}, u32[]{:S(2)}, u32[]{:S(2)}) collective-permute-start(bf16[4,128,128]{2,1,0:T(8,128)(2,1)S(1)} %get-tuple-element.45), channel_id=1, source_target_pairs={{0,4},{4,0},{8,12},{12,8},{16,20},{20,16},{24,28},{28,24},{1,5},{5... | collective-permute-start | bytes 393224 | tf_op jit(solution)/shard_map/ppermute | solution.py:137
  22.8 54.2 %collective-permute-start.9 = (bf16[1024,512]{1,0:T(8,128)(2,1)}, bf16[1024,512]{1,0:T(8,128)(2,1)}, u32[]{:S(2)}, u32[]{:S(2)}) collective-permute-start(bf16[1024,512]{1,0:T(8,128)(2,1)} %refs_2_.3), channel_id=1, source_target_pairs={{0,16},{4,20},{8,24},{12,28},{16,0},{20,4},{24,8},{28,12},{1,17},{... | collective-permute-start | bytes 3145736 | tf_op jit(solution)/shard_map/ppermute | solution.py:383
  34.8 1.2 copy-start.5
  34.8 1.3 %copy-start.10 = (f32[8,128,128]{2,1,0:T(8,128)S(1)}, f32[8,128,128]{2,1,0:T(8,128)}, u32[]{:S(2)}) copy-start(f32[8,128,128]{2,1,0:T(8,128)} %kv_ref.1) | copy-start | bytes 1572868
  34.8 1.3 %copy-start.13 = (f32[4096]{0:T(1024)S(1)}, f32[4096]{0:T(1024)}, u32[]{:S(2)}) copy-start(f32[4096]{0:T(1024)} %param.12) | copy-start | bytes 49156
  34.8 45.4 %collective-permute-start.10 = (bf16[1024,512]{1,0:T(8,128)(2,1)}, bf16[1024,512]{1,0:T(8,128)(2,1)}, u32[]{:S(2)}, u32[]{:S(2)}) collective-permute-start(bf16[1024,512]{1,0:T(8,128)(2,1)} %refs_2_.3), channel_id=1, source_target_pairs={{0,8},{4,12},{8,0},{12,4},{16,24},{20,28},{24,16},{28,20},{1,9},{5... | collective-permute-start | bytes 3145736 | tf_op jit(solution)/shard_map/ppermute | solution.py:383
  37.9 14.9 %collective-permute-start.7 = (bf16[256,1024]{1,0:T(8,128)(2,1)S(1)}, bf16[256,1024]{1,0:T(8,128)(2,1)S(1)}, u32[]{:S(2)}, u32[]{:S(2)}) collective-permute-start(bf16[256,1024]{1,0:T(8,128)(2,1)S(1)} %get-tuple-element.47.refs_0_), channel_id=1, source_target_pairs={{0,4},{4,0},{8,12},{12,8},{16,20},{20,16},{24,28},{28,24},{1,5},{5... | collective-permute-start | bytes 1572872 | tf_op jit(solution)/shard_map/ppermute | solution.py:405
  38.5 20.8 %collective-permute-start.8 = (bf16[256,1024]{1,0:T(8,128)(2,1)S(1)}, bf16[256,1024]{1,0:T(8,128)(2,1)S(1)}, u32[]{:S(2)}, u32[]{:S(2)}) collective-permute-start(bf16[256,1024]{1,0:T(8,128)(2,1)S(1)} %get-tuple-element.48.refs_1_), channel_id=1, source_target_pairs={{0,4},{4,0},{8,12},{12,8},{16,20},{20,16},{24,28},{28,24},{1,5},{5... | collective-permute-start | bytes 1572872 | tf_op jit(solution)/shard_map/ppermute | solution.py:405
  40.0 1.1 collective-permute-start.5
  41.1 3.5 %collective-permute-start.6 = (f32[1,128]{1,0:T(1,128)S(1)}, f32[1,128]{1,0:T(1,128)S(1)}, u32[]{:S(2)}, u32[]{:S(2)}) collective-permute-start(f32[1,128]{1,0:T(1,128)S(1)} %slice.15), channel_id=1, source_target_pairs={{0,2},{1,3},{2,0},{3,1},{4,6},{5,7},{6,4},{7,5},{8,10},{9,11},{10,... | collective-permute-start | bytes 1544 | tf_op jit(solution)/shard_map/ppermute | solution.py:410
  44.6 16.6 %collective-permute-start.11 = (bf16[256,512]{1,0:T(8,128)(2,1)S(1)}, bf16[256,512]{1,0:T(8,128)(2,1)S(1)}, u32[]{:S(2)}, u32[]{:S(2)}) collective-permute-start(bf16[256,512]{1,0:T(8,128)(2,1)S(1)} %get-tuple-element.49), channel_id=1, source_target_pairs={{0,1},{1,0},{2,3},{3,2},{4,5},{5,4},{6,7},{7,6},{8,9},{9,8},{10,11... | collective-permute-start | bytes 786440 | tf_op jit(solution)/shard_map/ppermute | solution.py:432
  61.2 1.7 %collective-permute-start.13 = (bf16[256,512]{1,0:T(8,128)(2,1)S(1)}, bf16[256,512]{1,0:T(8,128)(2,1)S(1)}, u32[]{:S(2)}, u32[]{:S(2)}) collective-permute-start(bf16[256,512]{1,0:T(8,128)(2,1)S(1)} %get-tuple-element.51), channel_id=1, source_target_pairs={{0,1},{1,0},{2,3},{3,2},{4,5},{5,4},{6,7},{7,6},{8,9},{9,8},{10,11... | collective-permute-start | bytes 786440 | tf_op jit(solution)/shard_map/ppermute | solution.py:432
  61.3 6.4 %collective-permute-start.12 = (bf16[128,512]{1,0:T(8,128)(2,1)S(1)}, bf16[128,512]{1,0:T(8,128)(2,1)S(1)}, u32[]{:S(2)}, u32[]{:S(2)}) collective-permute-start(bf16[128,512]{1,0:T(8,128)(2,1)S(1)} %get-tuple-element.62), channel_id=1, source_target_pairs={{0,2},{1,3},{2,0},{3,1},{4,6},{5,7},{6,4},{7,5},{8,10},{9,11},{10,... | collective-permute-start | bytes 393224 | tf_op jit(solution)/shard_map/ppermute | solution.py:432
  63.0 7.1 %collective-permute-start.14 = (bf16[128,512]{1,0:T(8,128)(2,1)S(1)}, bf16[128,512]{1,0:T(8,128)(2,1)S(1)}, u32[]{:S(2)}, u32[]{:S(2)}) collective-permute-start(bf16[128,512]{1,0:T(8,128)(2,1)S(1)} %get-tuple-element.65), channel_id=1, source_target_pairs={{0,2},{1,3},{2,0},{3,1},{4,6},{5,7},{6,4},{7,5},{8,10},{9,11},{10,... | collective-permute-start | bytes 393224 | tf_op jit(solution)/shard_map/ppermute | solution.py:432
  64.4 48.6 %collective-permute-start.24 = (bf16[1024,512]{1,0:T(8,128)(2,1)}, bf16[1024,512]{1,0:T(8,128)(2,1)S(1)}, u32[]{:S(2)}, u32[]{:S(2)}) collective-permute-start(bf16[1024,512]{1,0:T(8,128)(2,1)} %refs_2_.3), channel_id=1, source_target_pairs={{8,16},{12,20},{16,8},{20,12},{9,17},{13,21},{17,9},{21,13},{10,18... | collective-permute-start | bytes 3145736 | tf_op jit(solution)/shard_map/ppermute | solution.py:383
  78.9 34.1 %collective-permute-start.25 = (bf16[1024,512]{1,0:T(8,128)(2,1)}, bf16[1024,512]{1,0:T(8,128)(2,1)}, u32[]{:S(2)}, u32[]{:S(2)}) collective-permute-start(bf16[1024,512]{1,0:T(8,128)(2,1)} %collective-permute-done.9.refs_2_.refs_3_), channel_id=1, source_target_pairs={{8,0},{12,4},{16,24},{20,28},{9,1},{13,5},{17,25},{21,29},{10,2},{... | collective-permute-start | bytes 3145736 | tf_op jit(solution)/shard_map/ppermute | solution.py:383
  84.9 2.0 %collective-permute-start.22 = (bf16[256,1024]{1,0:T(8,128)(2,1)S(1)}, bf16[256,1024]{1,0:T(8,128)(2,1)S(1)}, u32[]{:S(2)}, u32[]{:S(2)}) collective-permute-start(bf16[256,1024]{1,0:T(8,128)(2,1)S(1)} %get-tuple-element.59), channel_id=1, source_target_pairs={{0,1},{1,0},{2,3},{3,2},{4,5},{5,4},{6,7},{7,6},{8,9},{9,8},{10,11... | collective-permute-start | bytes 1572872 | tf_op jit(solution)/shard_map/ppermute | solution.py:432
  85.0 4.3 %collective-permute-start.16 = (bf16[256,512]{1,0:T(8,128)(2,1)S(1)}, bf16[256,512]{1,0:T(8,128)(2,1)S(1)}, u32[]{:S(2)}, u32[]{:S(2)}) collective-permute-start(bf16[256,512]{1,0:T(8,128)(2,1)S(1)} %get-tuple-element.54), channel_id=1, source_target_pairs={{0,1},{1,0},{2,3},{3,2},{4,5},{5,4},{6,7},{7,6},{8,9},{9,8},{10,11... | collective-permute-start | bytes 786440 | tf_op jit(solution)/shard_map/ppermute | solution.py:432
  85.5 4.4 %collective-permute-start.19 = (bf16[256,512]{1,0:T(8,128)(2,1)S(1)}, bf16[256,512]{1,0:T(8,128)(2,1)S(1)}, u32[]{:S(2)}, u32[]{:S(2)}) collective-permute-start(bf16[256,512]{1,0:T(8,128)(2,1)S(1)} %get-tuple-element.57), channel_id=1, source_target_pairs={{0,1},{1,0},{2,3},{3,2},{4,5},{5,4},{6,7},{7,6},{8,9},{9,8},{10,11... | collective-permute-start | bytes 786440 | tf_op jit(solution)/shard_map/ppermute | solution.py:432
  87.0 0.8 copy-start.6
  87.8 15.3 %collective-permute-start.23 = (bf16[128,1024]{1,0:T(8,128)(2,1)S(1)}, bf16[128,1024]{1,0:T(8,128)(2,1)S(1)}, u32[]{:S(2)}, u32[]{:S(2)}) collective-permute-start(bf16[128,1024]{1,0:T(8,128)(2,1)S(1)} %get-tuple-element.74), channel_id=1, source_target_pairs={{0,2},{1,3},{2,0},{3,1},{4,6},{5,7},{6,4},{7,5},{8,10},{9,11},{10,... | collective-permute-start | bytes 786440 | tf_op jit(solution)/shard_map/ppermute | solution.py:432
  89.4 10.4 %collective-permute-start.17 = (bf16[128,512]{1,0:T(8,128)(2,1)S(1)}, bf16[128,512]{1,0:T(8,128)(2,1)S(1)}, u32[]{:S(2)}, u32[]{:S(2)}) collective-permute-start(bf16[128,512]{1,0:T(8,128)(2,1)S(1)} %get-tuple-element.68), channel_id=1, source_target_pairs={{0,2},{1,3},{2,0},{3,1},{4,6},{5,7},{6,4},{7,5},{8,10},{9,11},{10,... | collective-permute-start | bytes 393224 | tf_op jit(solution)/shard_map/ppermute | solution.py:432
  90.0 11.8 %collective-permute-start.20 = (bf16[128,512]{1,0:T(8,128)(2,1)S(1)}, bf16[128,512]{1,0:T(8,128)(2,1)S(1)}, u32[]{:S(2)}, u32[]{:S(2)}) collective-permute-start(bf16[128,512]{1,0:T(8,128)(2,1)S(1)} %get-tuple-element.71), channel_id=1, source_target_pairs={{0,2},{1,3},{2,0},{3,1},{4,6},{5,7},{6,4},{7,5},{8,10},{9,11},{10,... | collective-permute-start | bytes 393224 | tf_op jit(solution)/shard_map/ppermute | solution.py:432
  99.8 7.6 %collective-permute-start.15 = (bf16[128,512]{1,0:T(8,128)(2,1)}, bf16[128,512]{1,0:T(8,128)(2,1)}, u32[]{:S(2)}, u32[]{:S(2)}) collective-permute-start(bf16[128,512]{1,0:T(8,128)(2,1)} %shard_map.89), channel_id=1, source_target_pairs={{0,4},{4,0},{8,12},{12,8},{16,20},{20,16},{24,28},{28,24},{1,5},{5... | collective-permute-start | bytes 393224 | tf_op jit(solution)/shard_map/ppermute | solution.py:442
  101.8 7.1 %collective-permute-start.18 = (bf16[128,512]{1,0:T(8,128)(2,1)}, bf16[128,512]{1,0:T(8,128)(2,1)}, u32[]{:S(2)}, u32[]{:S(2)}) collective-permute-start(bf16[128,512]{1,0:T(8,128)(2,1)} %shard_map.91), channel_id=1, source_target_pairs={{0,4},{4,0},{8,12},{12,8},{16,20},{20,16},{24,28},{28,24},{1,5},{5... | collective-permute-start | bytes 393224 | tf_op jit(solution)/shard_map/ppermute | solution.py:442
  103.1 0.7 copy-start.11
  103.8 6.8 %collective-permute-start.21 = (bf16[128,512]{1,0:T(8,128)(2,1)}, bf16[128,512]{1,0:T(8,128)(2,1)}, u32[]{:S(2)}, u32[]{:S(2)}) collective-permute-start(bf16[128,512]{1,0:T(8,128)(2,1)} %shard_map.93), channel_id=1, source_target_pairs={{0,4},{4,0},{8,12},{12,8},{16,20},{20,16},{24,28},{28,24},{1,5},{5... | collective-permute-start | bytes 393224 | tf_op jit(solution)/shard_map/ppermute | solution.py:442
  105.3 1.0 copy-start.7
  106.3 0.9 copy-start.12
  115.5 2.0 %collective-permute-start.26 = (bf16[256,1024]{1,0:T(8,128)(2,1)S(1)}, bf16[256,1024]{1,0:T(8,128)(2,1)S(1)}, u32[]{:S(2)}, u32[]{:S(2)}) collective-permute-start(bf16[256,1024]{1,0:T(8,128)(2,1)S(1)} %get-tuple-element.78), channel_id=1, source_target_pairs={{0,1},{1,0},{2,3},{3,2},{4,5},{5,4},{6,7},{7,6},{8,9},{9,8},{10,11... | collective-permute-start | bytes 1572872 | tf_op jit(solution)/shard_map/ppermute | solution.py:432
  117.5 8.4 %collective-permute-start.27 = (bf16[128,1024]{1,0:T(8,128)(2,1)S(1)}, bf16[128,1024]{1,0:T(8,128)(2,1)S(1)}, u32[]{:S(2)}, u32[]{:S(2)}) collective-permute-start(bf16[128,1024]{1,0:T(8,128)(2,1)S(1)} %get-tuple-element.80), channel_id=1, source_target_pairs={{0,2},{1,3},{2,0},{3,1},{4,6},{5,7},{6,4},{7,5},{8,10},{9,11},{10,... | collective-permute-start | bytes 786440 | tf_op jit(solution)/shard_map/ppermute | solution.py:432
  126.0 5.0 %collective-permute-start.28 = (bf16[128,512]{1,0:T(8,128)(2,1)S(1)}, bf16[128,512]{1,0:T(8,128)(2,1)S(1)}, u32[]{:S(2)}, u32[]{:S(2)}) collective-permute-start(bf16[128,512]{1,0:T(8,128)(2,1)S(1)} %get-tuple-element.82), channel_id=1, source_target_pairs={{0,4},{4,0},{8,12},{12,8},{16,20},{20,16},{24,28},{28,24},{1,5},{5... | collective-permute-start | bytes 393224 | tf_op jit(solution)/shard_map/ppermute | solution.py:442

commit v14 on v12

--- a/solution.py
+++ b/solution.py
@@ -124,18 +124,18 @@
         values.append(lax.ppermute(sends[turn - 1], "seq", turn_pairs(n_seq, turn)))
         members.append((i - turn) % inner)
     (first,) = combine(values, [jnp.bfloat16])
-    from_left = lax.ppermute(first, "seq", line_pairs(n_seq, [(0, 1), (2, 3)]))
-    (second,) = combine(values + [from_left], [jnp.bfloat16])
-    near = lax.ppermute(second, "seq", line_pairs(n_seq, [(1, 2)]))
-    far = lax.ppermute(second, "seq", line_pairs(n_seq, [(1, 3)]))
+    from_pair = lax.ppermute(first, "seq", line_pairs(n_seq, SWAP_NEXT))
+    (second,) = combine(values + [from_pair], [jnp.bfloat16])
+    from_half = lax.ppermute(second, "seq", line_pairs(n_seq, [(0, 2), (1, 3)]))
     targets = [i] + [(i + turn) % inner for turn in range(1, inner)] if split else [i]
-    masks = [owner < target for target in targets for owner in members]
+    later = (place // inner) % 2 == 1
+    masks = [mask for target in targets for mask in [later] + [owner < target for owner in members]]
     dtypes = [jnp.float32] + [jnp.bfloat16] * (len(targets) - 1)
-    befores = combine([from_left, near, far], dtypes, values, masks)
+    befores = combine([from_half], dtypes, [from_pair] + values, masks)
     terms = [befores[0]]
     for turn in range(1, len(targets)):
         terms.append(lax.ppermute(befores[turn], "seq", turn_pairs(n_seq, turn)))
-    return terms, [near, far]
+    return terms, from_half
 
 
 def causal_kernel(first_head, place_ref, q_ref, k_ref, v_ref, out_ref):
@@ -389,7 +389,7 @@
         causal_part(queries, key_input, value_input, some, heads - some),
     ]
 
-    own_columns = hold(out_weight, *stepped)
+    own_columns = hold(out_weight, stepped)
     w_halves = along(own_columns, SWAP_HALVES)
     w_next = along(own_columns, SWAP_NEXT)
     w_middle = along(own_columns, SWAP_MIDDLE)
@@ -418,7 +418,7 @@
     owners = [z ^ block for block in range(LINE)]
     blocks = [(out_weight,), (w_next,), (w_halves,)]
 
-    def summed(parts, pins, pin_end=None):
+    def summed(parts, pins):
         weights = sorted({block for _, own in parts for block in own})
         jobs = [(p, weights.index(block)) for p, (_, own) in enumerate(parts) for block in own]
         sent, kept = project(
@@ -434,7 +434,6 @@
             if bit < n_head:
                 sent, kept = fold(kept, got)
             else:
-                got = got if pin_end is None else hold(got, pin_end)
                 kept = fold(kept, got, [width * len(own) for _, own in parts])
         pieces = []
         for piece, (turn, own) in zip(kept, parts):
@@ -466,7 +465,7 @@
         group(turns[1:], [1, 2])
     filled = placed(None, pieces, squares, width, shape, total_width) if in_kernel else None
     last, _, _ = summed(
-        [(turn, [3]) for turn in turns], [*pins, *ends, *returned], filled
+        [(turn, [3]) for turn in turns], [*pins, *ends, *returned]
     )
     if in_kernel:
         return placed(filled, last, squares, width, shape, total_width)

time: 118 us -> 117 us (level)
  starting transfers between devices: 39.3 us -> 34 us
  waiting for transfers between devices: 52.8 us -> 57 us
    ppermute x3, waiting for transfers between devices: 14.5 us -> 7.32 us  [summed(): piece = lax.ppermute(piece, 'seq', turn_pairs(n_seq, -turn))]
    ppermute x10, waiting for transfers between devices: 8.8 us -> 15.8 us  [summed(): got = lax.ppermute(sent, 'head', flip_pairs(n_head, bit))]
    ppermute x4, starting transfers between devices: 13.8 us -> 8.28 us  [along(): return lax.ppermute(value, 'seq', line_pairs(n_seq, hops))]
    ppermute x4, waiting for transfers between devices: 7.26 us -> 10.3 us  [along(): return lax.ppermute(value, 'seq', line_pairs(n_seq, hops))]
    ppermute x3 -> x2, waiting for transfers between devices: 2.5 us -> 5.2 us  [the longest x1 3.14 us: state_prefix(): from_pair = lax.ppermute(first, 'seq', line_pairs(n_seq, SWAP_NEXT))]
    ppermute x1, waiting for transfers between devices: 7.38 us -> 6.02 us  [shards(): lax.ppermute(sent_rows, 'seq', pairs)]
    ppermute x3 -> x2, starting transfers between devices: 6.36 us -> 7.28 us  [the longest x1 5.39 us: state_prefix(): from_half = lax.ppermute(second, 'seq', line_pairs(n_seq, [(0, 2), (1, 3)]))]
  transfers between devices with their start and end apart: 26 -> 25, of which waited for: 14 -> 17; matrix products, arithmetic and copies ran while one was open for 0% -> 0% of each run, Pallas kernels for 14% -> 14%
where the time goes in v14:
time: 117 us; the launch traced here: 116 us
  waiting for transfers between devices  57 us (49%)
  starting transfers between devices  34 us (29%)
  Pallas kernels  21.2 us (18%)
  local copies, waits for them, and re-layouts  3.59 us (3%)
    pallas_call x24, Pallas kernels, local_call(): pl.pallas_call(kernel, in_specs=[pl.BlockSpec(memory_space=pltpu.SMEM)] +...  19.8 us
    ppermute x10, waiting for transfers between devices, summed(): got = lax.ppermute(sent, 'head', flip_pairs(n_head, bit))  15.8 us
    ppermute x4, waiting for transfers between devices, along(): return lax.ppermute(value, 'seq', line_pairs(n_seq, hops))  10.3 us
    ppermute x10, starting transfers between devices, summed(): got = lax.ppermute(sent, 'head', flip_pairs(n_head, bit))  8.44 us
    ppermute x4, starting transfers between devices, along(): return lax.ppermute(value, 'seq', line_pairs(n_seq, hops))  8.28 us
    ppermute x1, waiting for transfers between devices, shards(): lax.ppermute(kept_rows, 'seq', pairs)  8.12 us
    ppermute x3, waiting for transfers between devices, summed(): piece = lax.ppermute(piece, 'seq', turn_pairs(n_seq, -turn))  7.32 us
    ppermute x1, waiting for transfers between devices, shards(): lax.ppermute(sent_rows, 'seq', pairs)  6.02 us
  transfers between devices with their start and end apart: 25, of which 17 were waited for; matrix products, arithmetic and copies ran while one was open for 0% of the time, Pallas kernels for 14%

profile of v14, /device:TPU:0, one launch (start us, length us, event | category | flops | bytes accessed | tf_op | source)
XLA Modules:
  0.0 116.2 jit_solution(2954803552588415507)
XLA Ops:
  0.0 1.2 %copy-done = bf16[512,1024]{1,0:T(8,128)(2,1)S(1)} copy-done((bf16[512,1024]{1,0:T(8,128)(2,1)S(1)}, bf16[512,1024]{1,0:T(8,128)(2,1)}, u32[]{:S(2)}) %copy-start) | copy-done | bytes 1048600
  1.2 1.2 %copy-done.2 = bf16[512,1024]{1,0:T(8,128)(2,1)S(1)} copy-done((bf16[512,1024]{1,0:T(8,128)(2,1)S(1)}, bf16[512,1024]{1,0:T(8,128)(2,1)}, u32[]{:S(2)}) %copy-start.2) | copy-done | bytes 1048600
  2.5 0.5 shard_map.74
  2.9 3.0 %collective-permute-start = (bf16[4,128,128]{2,1,0:T(8,128)(2,1)S(1)}, bf16[4,128,128]{2,1,0:T(8,128)(2,1)S(1)}, u32[]{:S(2)}, u32[]{:S(2)}) collective-permute-start(bf16[4,128,128]{2,1,0:T(8,128)(2,1)S(1)} %shard_map.74), channel_id=1, source_target_pairs={{0,4},{4,0},{8,12},{12,8},{16,20},{20,16},{24,28},{28,24},{1,5},{5... | collective-permute-start | bytes 393224 | tf_op jit(solution)/shard_map/ppermute | solution.py:124
  6.0 0.5 shard_map.73.refs_0_.refs_2_
  6.4 3.0 %collective-permute-done.refs_1_.refs_3_ = bf16[4,128,128]{2,1,0:T(8,128)(2,1)S(1)} collective-permute-done((bf16[4,128,128]{2,1,0:T(8,128)(2,1)S(1)}, bf16[4,128,128]{2,1,0:T(8,128)(2,1)S(1)}, u32[]{:S(2)}, u32[]{:S(2)}) %collective-permute-start) | collective-permute-done | bytes 131104 | tf_op jit(solution)/shard_map/ppermute | solution.py:124
  9.5 1.9 %collective-permute-start.1 = (bf16[4,128,128]{2,1,0:T(8,128)(2,1)S(1)}, bf16[4,128,128]{2,1,0:T(8,128)(2,1)S(1)}, u32[]{:S(2)}, u32[]{:S(2)}) collective-permute-start(bf16[4,128,128]{2,1,0:T(8,128)(2,1)S(1)} %shard_map.75), channel_id=1, source_target_pairs={{0,8},{4,12},{8,0},{12,4},{16,24},{20,28},{24,16},{28,20},{1,9},{5... | collective-permute-start | bytes 393224 | tf_op jit(solution)/shard_map/ppermute | solution.py:127
  11.4 3.1 %collective-permute-done.1.refs_2_.refs_1_ = bf16[4,128,128]{2,1,0:T(8,128)(2,1)S(1)} collective-permute-done((bf16[4,128,128]{2,1,0:T(8,128)(2,1)S(1)}, bf16[4,128,128]{2,1,0:T(8,128)(2,1)S(1)}, u32[]{:S(2)}, u32[]{:S(2)}) %collective-permute-start.1) | collective-permute-done | bytes 131104 | tf_op jit(solution)/shard_map/ppermute | solution.py:127
  14.5 0.7 shard_map.76
  15.2 5.4 %collective-permute-start.2 = (bf16[4,128,128]{2,1,0:T(8,128)(2,1)}, bf16[4,128,128]{2,1,0:T(8,128)(2,1)}, u32[]{:S(2)}, u32[]{:S(2)}) collective-permute-start(bf16[4,128,128]{2,1,0:T(8,128)(2,1)} %shard_map.76), channel_id=1, source_target_pairs={{0,16},{4,20},{8,24},{12,28},{1,17},{5,21},{9,25},{13,29},{2,18},{... | collective-permute-start | bytes 393224 | tf_op jit(solution)/shard_map/ppermute | solution.py:129
  20.6 0.1 stack.81
  20.7 2.1 %collective-permute-done.2.refs_0_ = bf16[4,128,128]{2,1,0:T(8,128)(2,1)} collective-permute-done((bf16[4,128,128]{2,1,0:T(8,128)(2,1)}, bf16[4,128,128]{2,1,0:T(8,128)(2,1)}, u32[]{:S(2)}, u32[]{:S(2)}) %collective-permute-start.2) | collective-permute-done | bytes 131104 | tf_op jit(solution)/shard_map/ppermute | solution.py:129
  22.8 0.9 copy-done.7
  23.7 1.1 shard_map.77
  24.8 1.6 %collective-permute-start.3 = (bf16[4,128,128]{2,1,0:T(8,128)(2,1)S(1)}, bf16[4,128,128]{2,1,0:T(8,128)(2,1)S(1)}, u32[]{:S(2)}, u32[]{:S(2)}) collective-permute-start(bf16[4,128,128]{2,1,0:T(8,128)(2,1)S(1)} %get-tuple-element.39), channel_id=1, source_target_pairs={{0,4},{4,0},{8,12},{12,8},{16,20},{20,16},{24,28},{28,24},{1,5},{5... | collective-permute-start | bytes 393224 | tf_op jit(solution)/shard_map/ppermute | solution.py:137
  26.3 0.1 pad_add_fusion.1.place_ref
  26.4 3.4 %collective-permute-start.9 = (bf16[1024,512]{1,0:T(8,128)(2,1)}, bf16[1024,512]{1,0:T(8,128)(2,1)}, u32[]{:S(2)}, u32[]{:S(2)}) collective-permute-start(bf16[1024,512]{1,0:T(8,128)(2,1)} %refs_2_.3), channel_id=1, source_target_pairs={{0,16},{4,20},{8,24},{12,28},{16,0},{20,4},{24,8},{28,12},{1,17},{... | collective-permute-start | bytes 3145736 | tf_op jit(solution)/shard_map/ppermute | solution.py:383
  29.8 1.1 shard_map.78.refs_2_
  31.0 1.1 shard_map.79.refs_3_
  32.1 2.8 %collective-permute-start.8 = (bf16[1024,512]{1,0:T(8,128)(2,1)}, bf16[1024,512]{1,0:T(8,128)(2,1)}, u32[]{:S(2)}, u32[]{:S(2)}) collective-permute-start(bf16[1024,512]{1,0:T(8,128)(2,1)} %refs_2_.3), channel_id=1, source_target_pairs={{0,8},{4,12},{8,0},{12,4},{16,24},{20,28},{24,16},{28,20},{1,9},{5... | collective-permute-start | bytes 3145736 | tf_op jit(solution)/shard_map/ppermute | solution.py:383
  34.9 1.7 %shard_map.80 = (bf16[256,1024]{1,0:T(8,128)(2,1)S(1)}, bf16[256,1024]{1,0:T(8,128)(2,1)S(1)}, f32[4,128]{1,0:T(4,128)S(1)}) custom-call(s32[2]{0:T(128)S(1)} %pad_add_fusion.1.place_ref, bf16[512,1024]{1,0:T(8,128)(2,1)S(1)} %copy-done.4, bf16[512,1024]{1,0:T(8,128)(2,1)S(1)} %copy-done.5, f32[32,1,128]{2,1,0:T(1,128)S(1)} %bitcast.17, ...), custom_call_target="tpu_custom_call" | custom-call | flops 268435456 | bytes 6178816 | tf_op jit(solution)/shard_map/pallas_call | solution.py:49
  36.7 0.6 collective-permute-start.6
  37.3 1.5 %collective-permute-start.7 = (bf16[256,1024]{1,0:T(8,128)(2,1)S(1)}, bf16[256,1024]{1,0:T(8,128)(2,1)S(1)}, u32[]{:S(2)}, u32[]{:S(2)}) collective-permute-start(bf16[256,1024]{1,0:T(8,128)(2,1)S(1)} %get-tuple-element.42.refs_1_), channel_id=1, source_target_pairs={{0,4},{4,0},{8,12},{12,8},{16,20},{20,16},{24,28},{28,24},{1,5},{5... | collective-permute-start | bytes 1572872 | tf_op jit(solution)/shard_map/ppermute | solution.py:405
  38.8 1.1 collective-permute-done.4
  39.9 1.5 %collective-permute-start.5 = (f32[1,128]{1,0:T(1,128)S(1)}, f32[1,128]{1,0:T(1,128)S(1)}, u32[]{:S(2)}, u32[]{:S(2)}) collective-permute-start(f32[1,128]{1,0:T(1,128)S(1)} %slice.15), channel_id=1, source_target_pairs={{0,2},{1,3},{2,0},{3,1},{4,6},{5,7},{6,4},{7,5},{8,10},{9,11},{10,... | collective-permute-start | bytes 1544 | tf_op jit(solution)/shard_map/ppermute | solution.py:410
  41.4 1.9 %shard_map.81 = (bf16[256,512]{1,0:T(8,128)(2,1)S(1)}, f32[256,512]{1,0:T(8,128)S(1)}) custom-call(s32[1]{0:T(128)} %bitcast.10.flag_ref, bf16[256,1024]{1,0:T(8,128)(2,1)S(1)} %get-tuple-element.41.refs_0_, bf16[256,1024]{1,0:T(8,128)(2,1)S(1)} %get-tuple-element.42.refs_1_, bf16[1024,512]{1,0:T(8,128)(2,1)} %refs_2_.3), custom_call_target="tpu_custom_call" | custom-call | flops 536870912 | bytes 2883584 | tf_op jit(solution)/shard_map/pallas_call | solution.py:49
  43.4 0.1 collective-permute-done.5
  43.5 8.1 %collective-permute-done.6.refs_0_.refs_2_ = bf16[256,1024]{1,0:T(8,128)(2,1)S(1)} collective-permute-done((bf16[256,1024]{1,0:T(8,128)(2,1)S(1)}, bf16[256,1024]{1,0:T(8,128)(2,1)S(1)}, u32[]{:S(2)}, u32[]{:S(2)}) %collective-permute-start.6) | collective-permute-done | bytes 524320 | tf_op jit(solution)/shard_map/ppermute | solution.py:405
  51.6 6.0 %collective-permute-done.7.refs_1_.refs_3_ = bf16[256,1024]{1,0:T(8,128)(2,1)S(1)} collective-permute-done((bf16[256,1024]{1,0:T(8,128)(2,1)S(1)}, bf16[256,1024]{1,0:T(8,128)(2,1)S(1)}, u32[]{:S(2)}, u32[]{:S(2)}) %collective-permute-start.7) | collective-permute-done | bytes 524320 | tf_op jit(solution)/shard_map/ppermute | solution.py:405
  57.6 1.9 %shard_map.82 = (bf16[256,512]{1,0:T(8,128)(2,1)S(1)}, f32[256,512]{1,0:T(8,128)S(1)}) custom-call(s32[1]{0:T(128)} %bitcast.10.flag_ref, bf16[256,1024]{1,0:T(8,128)(2,1)S(1)} %collective-permute-done.6.refs_0_.refs_2_, bf16[256,1024]{1,0:T(8,128)(2,1)S(1)} %collective-permute-done.7.refs_1_.refs_3_, bf16[1024,512]{1,0:T(8,128)(2,1)} %refs_2_.3), custom_call_target="tpu_custom_call" | custom-call | flops 536870912 | bytes 2883584 | tf_op jit(solution)/shard_map/pallas_call | solution.py:49
  59.5 0.1 collective-permute-start.12
  59.7 1.6 %collective-permute-start.11 = (bf16[128,512]{1,0:T(8,128)(2,1)S(1)}, bf16[128,512]{1,0:T(8,128)(2,1)S(1)}, u32[]{:S(2)}, u32[]{:S(2)}) collective-permute-start(bf16[128,512]{1,0:T(8,128)(2,1)S(1)} %get-tuple-element.52), channel_id=1, source_target_pairs={{0,2},{1,3},{2,0},{3,1},{4,6},{5,7},{6,4},{7,5},{8,10},{9,11},{10,... | collective-permute-start | bytes 393224 | tf_op jit(solution)/shard_map/ppermute | solution.py:432
  61.4 1.4 %collective-permute-start.13 = (bf16[128,512]{1,0:T(8,128)(2,1)S(1)}, bf16[128,512]{1,0:T(8,128)(2,1)S(1)}, u32[]{:S(2)}, u32[]{:S(2)}) collective-permute-start(bf16[128,512]{1,0:T(8,128)(2,1)S(1)} %get-tuple-element.54), channel_id=1, source_target_pairs={{0,2},{1,3},{2,0},{3,1},{4,6},{5,7},{6,4},{7,5},{8,10},{9,11},{10,... | collective-permute-start | bytes 393224 | tf_op jit(solution)/shard_map/ppermute | solution.py:432
  62.8 0.7 collective-permute-start.19
  63.5 2.5 %collective-permute-done.11.got_ref = bf16[128,512]{1,0:T(8,128)(2,1)S(1)} collective-permute-done((bf16[128,512]{1,0:T(8,128)(2,1)S(1)}, bf16[128,512]{1,0:T(8,128)(2,1)S(1)}, u32[]{:S(2)}, u32[]{:S(2)}) %collective-permute-start.11) | collective-permute-done | bytes 131104 | tf_op jit(solution)/shard_map/ppermute | solution.py:432
  66.1 8.7 %collective-permute-done.9.refs_3_ = bf16[1024,512]{1,0:T(8,128)(2,1)} collective-permute-done((bf16[1024,512]{1,0:T(8,128)(2,1)}, bf16[1024,512]{1,0:T(8,128)(2,1)}, u32[]{:S(2)}, u32[]{:S(2)}) %collective-permute-start.9) | collective-permute-done | bytes 1048608 | tf_op jit(solution)/shard_map/ppermute | solution.py:383
  74.7 1.3 %collective-permute-start.20 = (bf16[1024,512]{1,0:T(8,128)(2,1)}, bf16[1024,512]{1,0:T(8,128)(2,1)S(1)}, u32[]{:S(2)}, u32[]{:S(2)}) collective-permute-start(bf16[1024,512]{1,0:T(8,128)(2,1)} %collective-permute-done.9.refs_3_), channel_id=1, source_target_pairs={{8,0},{12,4},{16,24},{20,28},{9,1},{13,5},{17,25},{21,29},{10,2},{... | collective-permute-start | bytes 3145736 | tf_op jit(solution)/shard_map/ppermute | solution.py:383
  76.0 2.8 %shard_map.83 = (bf16[256,1024]{1,0:T(8,128)(2,1)S(1)}, f32[256,1024]{1,0:T(8,128)S(1)}) custom-call(s32[1]{0:T(128)} %bitcast.10.flag_ref, bf16[256,1024]{1,0:T(8,128)(2,1)S(1)} %get-tuple-element.41.refs_0_, bf16[256,1024]{1,0:T(8,128)(2,1)S(1)} %get-tuple-element.42.refs_1_, bf16[1024,512]{1,0:T(8,128)(2,1)} %collective-permute-done.8.refs_2_, ...), custom_call_target="tpu_custom_call" | custom-call | flops 1073741824 | bytes 4718592 | tf_op jit(solution)/shard_map/pallas_call | solution.py:49
  78.8 0.1 collective-permute-start.14
  78.9 2.8 %shard_map.84 = (bf16[256,1024]{1,0:T(8,128)(2,1)S(1)}, f32[256,1024]{1,0:T(8,128)S(1)}) custom-call(s32[1]{0:T(128)} %bitcast.10.flag_ref, bf16[256,1024]{1,0:T(8,128)(2,1)S(1)} %collective-permute-done.6.refs_0_.refs_2_, bf16[256,1024]{1,0:T(8,128)(2,1)S(1)} %collective-permute-done.7.refs_1_.refs_3_, bf16[1024,512]{1,0:T(8,128)(2,1)} %collective-permute-done.8.refs_2_, ...), custom_call_target="tpu_custom_call" | custom-call | flops 1073741824 | bytes 4718592 | tf_op jit(solution)/shard_map/pallas_call | solution.py:49
  81.7 0.6 collective-permute-start.16
  82.3 0.1 shard_map.87
  82.4 1.6 %collective-permute-start.15 = (bf16[128,1024]{1,0:T(8,128)(2,1)S(1)}, bf16[128,1024]{1,0:T(8,128)(2,1)S(1)}, u32[]{:S(2)}, u32[]{:S(2)}) collective-permute-start(bf16[128,1024]{1,0:T(8,128)(2,1)S(1)} %get-tuple-element.56), channel_id=1, source_target_pairs={{0,2},{1,3},{2,0},{3,1},{4,6},{5,7},{6,4},{7,5},{8,10},{9,11},{10,... | collective-permute-start | bytes 786440 | tf_op jit(solution)/shard_map/ppermute | solution.py:432
  84.0 0.1 shard_map.88
  84.0 1.5 %collective-permute-start.17 = (bf16[128,1024]{1,0:T(8,128)(2,1)S(1)}, bf16[128,1024]{1,0:T(8,128)(2,1)S(1)}, u32[]{:S(2)}, u32[]{:S(2)}) collective-permute-start(bf16[128,1024]{1,0:T(8,128)(2,1)S(1)} %get-tuple-element.58), channel_id=1, source_target_pairs={{0,2},{1,3},{2,0},{3,1},{4,6},{5,7},{6,4},{7,5},{8,10},{9,11},{10,... | collective-permute-start | bytes 786440 | tf_op jit(solution)/shard_map/ppermute | solution.py:432
  85.5 0.6 collective-permute-start.18
  86.1 5.0 %collective-permute-done.18.refs_1_ = bf16[128,512]{1,0:T(8,128)(2,1)S(1)} collective-permute-done((bf16[128,512]{1,0:T(8,128)(2,1)S(1)}, bf16[128,512]{1,0:T(8,128)(2,1)S(1)}, u32[]{:S(2)}, u32[]{:S(2)}) %collective-permute-start.18) | collective-permute-done | bytes 131104 | tf_op jit(solution)/shard_map/ppermute | solution.py:441
  91.1 0.5 collective-permute-done.15.got_ref
  91.6 4.7 %collective-permute-done.17.got_ref = bf16[128,1024]{1,0:T(8,128)(2,1)S(1)} collective-permute-done((bf16[128,1024]{1,0:T(8,128)(2,1)S(1)}, bf16[128,1024]{1,0:T(8,128)(2,1)S(1)}, u32[]{:S(2)}, u32[]{:S(2)}) %collective-permute-start.17) | collective-permute-done | bytes 262176 | tf_op jit(solution)/shard_map/ppermute | solution.py:432
  96.3 1.6 %collective-permute-done.20.refs_5_ = bf16[1024,512]{1,0:T(8,128)(2,1)S(1)} collective-permute-done((bf16[1024,512]{1,0:T(8,128)(2,1)}, bf16[1024,512]{1,0:T(8,128)(2,1)S(1)}, u32[]{:S(2)}, u32[]{:S(2)}) %collective-permute-start.20) | collective-permute-done | bytes 1048608 | tf_op jit(solution)/shard_map/ppermute | solution.py:383
  97.9 1.3 %shard_map.90 = (bf16[256,1024]{1,0:T(8,128)(2,1)S(1)}, f32[256,1024]{1,0:T(8,128)S(1)}) custom-call(s32[1]{0:T(128)} %bitcast.10.flag_ref, bf16[256,1024]{1,0:T(8,128)(2,1)S(1)} %get-tuple-element.41.refs_0_, bf16[256,1024]{1,0:T(8,128)(2,1)S(1)} %get-tuple-element.42.refs_1_, bf16[256,1024]{1,0:T(8,128)(2,1)S(1)} %collective-permute-done.6.refs_0_.refs_2_, ...), custom_call_target="tpu_custom_call" | custom-call | flops 1073741824 | bytes 5767168 | tf_op jit(solution)/shard_map/pallas_call | solution.py:49
  99.2 0.1 collective-permute-start.21
  99.3 1.9 %collective-permute-done.21.got_ref = bf16[256,1024]{1,0:T(8,128)(2,1)S(1)} collective-permute-done((bf16[256,1024]{1,0:T(8,128)(2,1)S(1)}, bf16[256,1024]{1,0:T(8,128)(2,1)S(1)}, u32[]{:S(2)}, u32[]{:S(2)}) %collective-permute-start.21) | collective-permute-done | bytes 524320 | tf_op jit(solution)/shard_map/ppermute | solution.py:432
  101.2 0.1 shard_map.91
  101.3 1.6 %collective-permute-start.22 = (bf16[128,1024]{1,0:T(8,128)(2,1)S(1)}, bf16[128,1024]{1,0:T(8,128)(2,1)S(1)}, u32[]{:S(2)}, u32[]{:S(2)}) collective-permute-start(bf16[128,1024]{1,0:T(8,128)(2,1)S(1)} %get-tuple-element.65), channel_id=1, source_target_pairs={{0,2},{1,3},{2,0},{3,1},{4,6},{5,7},{6,4},{7,5},{8,10},{9,11},{10,... | collective-permute-start | bytes 786440 | tf_op jit(solution)/shard_map/ppermute | solution.py:432
  102.9 0.6 collective-permute-start.24
  103.5 6.2 %collective-permute-done.22.got_ref = bf16[128,1024]{1,0:T(8,128)(2,1)S(1)} collective-permute-done((bf16[128,1024]{1,0:T(8,128)(2,1)S(1)}, bf16[128,1024]{1,0:T(8,128)(2,1)S(1)}, u32[]{:S(2)}, u32[]{:S(2)}) %collective-permute-start.22) | collective-permute-done | bytes 262176 | tf_op jit(solution)/shard_map/ppermute | solution.py:432
  109.7 0.6 collective-permute-start.23
  110.3 0.1 stack.92.starts_ref
  110.4 0.1 pad_add_fusion.starts_ref
  110.6 0.5 collective-permute-done.24.refs_3_
  111.1 1.8 %shard_map.96.refs_2_ = bf16[128,4096]{1,0:T(8,128)(2,1)} custom-call(s32[6]{0:T(128)S(1)} %stack.92.starts_ref, f32[1,128]{1,0:T(1,128)S(1)} %slice_add_fusion.1.squares_ref, bf16[128,512]{1,0:T(8,128)(2,1)S(1)} %shard_map.93.refs_0_, bf16[128,512]{1,0:T(8,128)(2,1)S(1)} %collective-permute-done.18.refs_1_, bf16[128,1024]{1,0:T(8,128)(2,1)S(1)} %shard_map.94.refs_2_, ...), custom_call_target="tpu_custom_call" | custom-call | bytes 1835520 | tf_op jit(solution)/shard_map/pallas_call | solution.py:49
  112.9 1.9 %collective-permute-done.23.refs_1_ = bf16[128,512]{1,0:T(8,128)(2,1)S(1)} collective-permute-done((bf16[128,512]{1,0:T(8,128)(2,1)S(1)}, bf16[128,512]{1,0:T(8,128)(2,1)S(1)}, u32[]{:S(2)}, u32[]{:S(2)}) %collective-permute-start.23) | collective-permute-done | bytes 131104 | tf_op jit(solution)/shard_map/ppermute | solution.py:441
  114.8 1.4 %shard_map.97 = bf16[128,4096]{1,0:T(8,128)(2,1)} custom-call(s32[2]{0:T(128)S(1)} %pad_add_fusion.starts_ref, f32[1,128]{1,0:T(1,128)S(1)} %slice_add_fusion.1.squares_ref, bf16[128,512]{1,0:T(8,128)(2,1)S(1)} %get-tuple-element.66.refs_0_, bf16[128,512]{1,0:T(8,128)(2,1)S(1)} %collective-permute-done.23.refs_1_, ...), custom_call_target="tpu_custom_call", output_to_operand_aliasing={{}: (4, {})} | custom-call | bytes 524288 | tf_op jit(solution)/shard_map/pallas_call | solution.py:352
  (40 shorter events, 0.4 us)
Async XLA Ops:
  0.0 1.2 %copy-start = (bf16[512,1024]{1,0:T(8,128)(2,1)S(1)}, bf16[512,1024]{1,0:T(8,128)(2,1)}, u32[]{:S(2)}) copy-start(bf16[512,1024]{1,0:T(8,128)(2,1)} %k_ref.7) | copy-start | bytes 3145732
  1.2 1.2 %copy-start.2 = (bf16[512,1024]{1,0:T(8,128)(2,1)S(1)}, bf16[512,1024]{1,0:T(8,128)(2,1)}, u32[]{:S(2)}) copy-start(bf16[512,1024]{1,0:T(8,128)(2,1)} %v_ref.7) | copy-start | bytes 3145732
  2.5 3.5 %copy-start.1 = (bf16[512,1024]{1,0:T(8,128)(2,1)S(1)}, bf16[512,1024]{1,0:T(8,128)(2,1)}, u32[]{:S(2)}) copy-start(bf16[512,1024]{1,0:T(8,128)(2,1)} %k_ref.7) | copy-start | bytes 3145732
  2.9 6.5 %collective-permute-start = (bf16[4,128,128]{2,1,0:T(8,128)(2,1)S(1)}, bf16[4,128,128]{2,1,0:T(8,128)(2,1)S(1)}, u32[]{:S(2)}, u32[]{:S(2)}) collective-permute-start(bf16[4,128,128]{2,1,0:T(8,128)(2,1)S(1)} %shard_map.74), channel_id=1, source_target_pairs={{0,4},{4,0},{8,12},{12,8},{16,20},{20,16},{24,28},{28,24},{1,5},{5... | collective-permute-start | bytes 393224 | tf_op jit(solution)/shard_map/ppermute | solution.py:124
  5.9 23.9 %copy-start.4 = (bf16[512,1024]{1,0:T(8,128)(2,1)S(1)}, bf16[512,1024]{1,0:T(8,128)(2,1)}, u32[]{:S(2)}) copy-start(bf16[512,1024]{1,0:T(8,128)(2,1)} %q_ref.5) | copy-start | bytes 3145732
  6.4 23.4 %copy-start.3 = (bf16[512,1024]{1,0:T(8,128)(2,1)S(1)}, bf16[512,1024]{1,0:T(8,128)(2,1)}, u32[]{:S(2)}) copy-start(bf16[512,1024]{1,0:T(8,128)(2,1)} %v_ref.7) | copy-start | bytes 3145732
  9.5 5.0 %collective-permute-start.1 = (bf16[4,128,128]{2,1,0:T(8,128)(2,1)S(1)}, bf16[4,128,128]{2,1,0:T(8,128)(2,1)S(1)}, u32[]{:S(2)}, u32[]{:S(2)}) collective-permute-start(bf16[4,128,128]{2,1,0:T(8,128)(2,1)S(1)} %shard_map.75), channel_id=1, source_target_pairs={{0,8},{4,12},{8,0},{12,4},{16,24},{20,28},{24,16},{28,20},{1,9},{5... | collective-permute-start | bytes 393224 | tf_op jit(solution)/shard_map/ppermute | solution.py:127
  14.5 0.7 copy-start.6
  15.2 7.6 %collective-permute-start.2 = (bf16[4,128,128]{2,1,0:T(8,128)(2,1)}, bf16[4,128,128]{2,1,0:T(8,128)(2,1)}, u32[]{:S(2)}, u32[]{:S(2)}) collective-permute-start(bf16[4,128,128]{2,1,0:T(8,128)(2,1)} %shard_map.76), channel_id=1, source_target_pairs={{0,16},{4,20},{8,24},{12,28},{1,17},{5,21},{9,25},{13,29},{2,18},{... | collective-permute-start | bytes 393224 | tf_op jit(solution)/shard_map/ppermute | solution.py:129
  22.8 0.9 copy-start.7
  24.8 10.1 %collective-permute-start.3 = (bf16[4,128,128]{2,1,0:T(8,128)(2,1)S(1)}, bf16[4,128,128]{2,1,0:T(8,128)(2,1)S(1)}, u32[]{:S(2)}, u32[]{:S(2)}) collective-permute-start(bf16[4,128,128]{2,1,0:T(8,128)(2,1)S(1)} %get-tuple-element.39), channel_id=1, source_target_pairs={{0,4},{4,0},{8,12},{12,8},{16,20},{20,16},{24,28},{28,24},{1,5},{5... | collective-permute-start | bytes 393224 | tf_op jit(solution)/shard_map/ppermute | solution.py:137
  26.4 48.3 %collective-permute-start.9 = (bf16[1024,512]{1,0:T(8,128)(2,1)}, bf16[1024,512]{1,0:T(8,128)(2,1)}, u32[]{:S(2)}, u32[]{:S(2)}) collective-permute-start(bf16[1024,512]{1,0:T(8,128)(2,1)} %refs_2_.3), channel_id=1, source_target_pairs={{0,16},{4,20},{8,24},{12,28},{16,0},{20,4},{24,8},{28,12},{1,17},{... | collective-permute-start | bytes 3145736 | tf_op jit(solution)/shard_map/ppermute | solution.py:383
  30.9 4.0 %copy-start.5 = (bf16[512,1024]{1,0:T(8,128)(2,1)S(1)}, bf16[512,1024]{1,0:T(8,128)(2,1)}, u32[]{:S(2)}) copy-start(bf16[512,1024]{1,0:T(8,128)(2,1)} %gate_ref.1) | copy-start | bytes 3145732
  30.9 4.0 %copy-start.8 = (f32[8,128,128]{2,1,0:T(8,128)S(1)}, f32[8,128,128]{2,1,0:T(8,128)}, u32[]{:S(2)}) copy-start(f32[8,128,128]{2,1,0:T(8,128)} %kv_ref.1) | copy-start | bytes 1572868
  31.0 4.0 %copy-start.9 = (f32[4096]{0:T(1024)S(1)}, f32[4096]{0:T(1024)}, u32[]{:S(2)}) copy-start(f32[4096]{0:T(1024)} %param.12) | copy-start | bytes 49156
  32.1 44.0 %collective-permute-start.8 = (bf16[1024,512]{1,0:T(8,128)(2,1)}, bf16[1024,512]{1,0:T(8,128)(2,1)}, u32[]{:S(2)}, u32[]{:S(2)}) collective-permute-start(bf16[1024,512]{1,0:T(8,128)(2,1)} %refs_2_.3), channel_id=1, source_target_pairs={{0,8},{4,12},{8,0},{12,4},{16,24},{20,28},{24,16},{28,20},{1,9},{5... | collective-permute-start | bytes 3145736 | tf_op jit(solution)/shard_map/ppermute | solution.py:383
  36.7 14.9 %collective-permute-start.6 = (bf16[256,1024]{1,0:T(8,128)(2,1)S(1)}, bf16[256,1024]{1,0:T(8,128)(2,1)S(1)}, u32[]{:S(2)}, u32[]{:S(2)}) collective-permute-start(bf16[256,1024]{1,0:T(8,128)(2,1)S(1)} %get-tuple-element.41.refs_0_), channel_id=1, source_target_pairs={{0,4},{4,0},{8,12},{12,8},{16,20},{20,16},{24,28},{28,24},{1,5},{5... | collective-permute-start | bytes 1572872 | tf_op jit(solution)/shard_map/ppermute | solution.py:405
  37.3 20.4 %collective-permute-start.7 = (bf16[256,1024]{1,0:T(8,128)(2,1)S(1)}, bf16[256,1024]{1,0:T(8,128)(2,1)S(1)}, u32[]{:S(2)}, u32[]{:S(2)}) collective-permute-start(bf16[256,1024]{1,0:T(8,128)(2,1)S(1)} %get-tuple-element.42.refs_1_), channel_id=1, source_target_pairs={{0,4},{4,0},{8,12},{12,8},{16,20},{20,16},{24,28},{28,24},{1,5},{5... | collective-permute-start | bytes 1572872 | tf_op jit(solution)/shard_map/ppermute | solution.py:405
  38.8 1.1 collective-permute-start.4
  39.9 3.5 %collective-permute-start.5 = (f32[1,128]{1,0:T(1,128)S(1)}, f32[1,128]{1,0:T(1,128)S(1)}, u32[]{:S(2)}, u32[]{:S(2)}) collective-permute-start(f32[1,128]{1,0:T(1,128)S(1)} %slice.15), channel_id=1, source_target_pairs={{0,2},{1,3},{2,0},{3,1},{4,6},{5,7},{6,4},{7,5},{8,10},{9,11},{10,... | collective-permute-start | bytes 1544 | tf_op jit(solution)/shard_map/ppermute | solution.py:410
  43.4 16.2 %collective-permute-start.10 = (bf16[256,512]{1,0:T(8,128)(2,1)S(1)}, bf16[256,512]{1,0:T(8,128)(2,1)S(1)}, u32[]{:S(2)}, u32[]{:S(2)}) collective-permute-start(bf16[256,512]{1,0:T(8,128)(2,1)S(1)} %get-tuple-element.43), channel_id=1, source_target_pairs={{0,1},{1,0},{2,3},{3,2},{4,5},{5,4},{6,7},{7,6},{8,9},{9,8},{10,11... | collective-permute-start | bytes 786440 | tf_op jit(solution)/shard_map/ppermute | solution.py:432
  59.5 1.7 %collective-permute-start.12 = (bf16[256,512]{1,0:T(8,128)(2,1)S(1)}, bf16[256,512]{1,0:T(8,128)(2,1)S(1)}, u32[]{:S(2)}, u32[]{:S(2)}) collective-permute-start(bf16[256,512]{1,0:T(8,128)(2,1)S(1)} %get-tuple-element.45), channel_id=1, source_target_pairs={{0,1},{1,0},{2,3},{3,2},{4,5},{5,4},{6,7},{7,6},{8,9},{9,8},{10,11... | collective-permute-start | bytes 786440 | tf_op jit(solution)/shard_map/ppermute | solution.py:432
  59.7 6.4 %collective-permute-start.11 = (bf16[128,512]{1,0:T(8,128)(2,1)S(1)}, bf16[128,512]{1,0:T(8,128)(2,1)S(1)}, u32[]{:S(2)}, u32[]{:S(2)}) collective-permute-start(bf16[128,512]{1,0:T(8,128)(2,1)S(1)} %get-tuple-element.52), channel_id=1, source_target_pairs={{0,2},{1,3},{2,0},{3,1},{4,6},{5,7},{6,4},{7,5},{8,10},{9,11},{10,... | collective-permute-start | bytes 393224 | tf_op jit(solution)/shard_map/ppermute | solution.py:432
  61.4 13.4 %collective-permute-start.13 = (bf16[128,512]{1,0:T(8,128)(2,1)S(1)}, bf16[128,512]{1,0:T(8,128)(2,1)S(1)}, u32[]{:S(2)}, u32[]{:S(2)}) collective-permute-start(bf16[128,512]{1,0:T(8,128)(2,1)S(1)} %get-tuple-element.54), channel_id=1, source_target_pairs={{0,2},{1,3},{2,0},{3,1},{4,6},{5,7},{6,4},{7,5},{8,10},{9,11},{10,... | collective-permute-start | bytes 393224 | tf_op jit(solution)/shard_map/ppermute | solution.py:432
  62.8 33.5 %collective-permute-start.19 = (bf16[1024,512]{1,0:T(8,128)(2,1)}, bf16[1024,512]{1,0:T(8,128)(2,1)S(1)}, u32[]{:S(2)}, u32[]{:S(2)}) collective-permute-start(bf16[1024,512]{1,0:T(8,128)(2,1)} %refs_2_.3), channel_id=1, source_target_pairs={{8,16},{12,20},{16,8},{20,12},{9,17},{13,21},{17,9},{21,13},{10,18... | collective-permute-start | bytes 3145736 | tf_op jit(solution)/shard_map/ppermute | solution.py:383
  74.7 23.2 %collective-permute-start.20 = (bf16[1024,512]{1,0:T(8,128)(2,1)}, bf16[1024,512]{1,0:T(8,128)(2,1)S(1)}, u32[]{:S(2)}, u32[]{:S(2)}) collective-permute-start(bf16[1024,512]{1,0:T(8,128)(2,1)} %collective-permute-done.9.refs_3_), channel_id=1, source_target_pairs={{8,0},{12,4},{16,24},{20,28},{9,1},{13,5},{17,25},{21,29},{10,2},{... | collective-permute-start | bytes 3145736 | tf_op jit(solution)/shard_map/ppermute | solution.py:383
  78.8 3.4 %collective-permute-start.14 = (bf16[256,1024]{1,0:T(8,128)(2,1)S(1)}, bf16[256,1024]{1,0:T(8,128)(2,1)S(1)}, u32[]{:S(2)}, u32[]{:S(2)}) collective-permute-start(bf16[256,1024]{1,0:T(8,128)(2,1)S(1)} %get-tuple-element.48), channel_id=1, source_target_pairs={{0,1},{1,0},{2,3},{3,2},{4,5},{5,4},{6,7},{7,6},{8,9},{9,8},{10,11... | collective-permute-start | bytes 1572872 | tf_op jit(solution)/shard_map/ppermute | solution.py:432
  81.7 2.2 %collective-permute-start.16 = (bf16[256,1024]{1,0:T(8,128)(2,1)S(1)}, bf16[256,1024]{1,0:T(8,128)(2,1)S(1)}, u32[]{:S(2)}, u32[]{:S(2)}) collective-permute-start(bf16[256,1024]{1,0:T(8,128)(2,1)S(1)} %get-tuple-element.50), channel_id=1, source_target_pairs={{0,1},{1,0},{2,3},{3,2},{4,5},{5,4},{6,7},{7,6},{8,9},{9,8},{10,11... | collective-permute-start | bytes 1572872 | tf_op jit(solution)/shard_map/ppermute | solution.py:432
  82.4 9.2 %collective-permute-start.15 = (bf16[128,1024]{1,0:T(8,128)(2,1)S(1)}, bf16[128,1024]{1,0:T(8,128)(2,1)S(1)}, u32[]{:S(2)}, u32[]{:S(2)}) collective-permute-start(bf16[128,1024]{1,0:T(8,128)(2,1)S(1)} %get-tuple-element.56), channel_id=1, source_target_pairs={{0,2},{1,3},{2,0},{3,1},{4,6},{5,7},{6,4},{7,5},{8,10},{9,11},{10,... | collective-permute-start | bytes 786440 | tf_op jit(solution)/shard_map/ppermute | solution.py:432
  84.0 12.2 %collective-permute-start.17 = (bf16[128,1024]{1,0:T(8,128)(2,1)S(1)}, bf16[128,1024]{1,0:T(8,128)(2,1)S(1)}, u32[]{:S(2)}, u32[]{:S(2)}) collective-permute-start(bf16[128,1024]{1,0:T(8,128)(2,1)S(1)} %get-tuple-element.58), channel_id=1, source_target_pairs={{0,2},{1,3},{2,0},{3,1},{4,6},{5,7},{6,4},{7,5},{8,10},{9,11},{10,... | collective-permute-start | bytes 786440 | tf_op jit(solution)/shard_map/ppermute | solution.py:432
  85.5 5.5 %collective-permute-start.18 = (bf16[128,512]{1,0:T(8,128)(2,1)S(1)}, bf16[128,512]{1,0:T(8,128)(2,1)S(1)}, u32[]{:S(2)}, u32[]{:S(2)}) collective-permute-start(bf16[128,512]{1,0:T(8,128)(2,1)S(1)} %shard_map.89), channel_id=1, source_target_pairs={{0,4},{4,0},{8,12},{12,8},{16,20},{20,16},{24,28},{28,24},{1,5},{5... | collective-permute-start | bytes 393224 | tf_op jit(solution)/shard_map/ppermute | solution.py:441
  99.2 2.0 %collective-permute-start.21 = (bf16[256,1024]{1,0:T(8,128)(2,1)S(1)}, bf16[256,1024]{1,0:T(8,128)(2,1)S(1)}, u32[]{:S(2)}, u32[]{:S(2)}) collective-permute-start(bf16[256,1024]{1,0:T(8,128)(2,1)S(1)} %get-tuple-element.63), channel_id=1, source_target_pairs={{0,1},{1,0},{2,3},{3,2},{4,5},{5,4},{6,7},{7,6},{8,9},{9,8},{10,11... | collective-permute-start | bytes 1572872 | tf_op jit(solution)/shard_map/ppermute | solution.py:432
  101.3 8.4 %collective-permute-start.22 = (bf16[128,1024]{1,0:T(8,128)(2,1)S(1)}, bf16[128,1024]{1,0:T(8,128)(2,1)S(1)}, u32[]{:S(2)}, u32[]{:S(2)}) collective-permute-start(bf16[128,1024]{1,0:T(8,128)(2,1)S(1)} %get-tuple-element.65), channel_id=1, source_target_pairs={{0,2},{1,3},{2,0},{3,1},{4,6},{5,7},{6,4},{7,5},{8,10},{9,11},{10,... | collective-permute-start | bytes 786440 | tf_op jit(solution)/shard_map/ppermute | solution.py:432
  102.9 8.1 %collective-permute-start.24 = (bf16[128,1024]{1,0:T(8,128)(2,1)S(1)}, bf16[128,1024]{1,0:T(8,128)(2,1)S(1)}, u32[]{:S(2)}, u32[]{:S(2)}) collective-permute-start(bf16[128,1024]{1,0:T(8,128)(2,1)S(1)} %shard_map.95), channel_id=1, source_target_pairs={{0,4},{4,0},{8,12},{12,8},{16,20},{20,16},{24,28},{28,24},{1,5},{5... | collective-permute-start | bytes 786440 | tf_op jit(solution)/shard_map/ppermute | solution.py:441
  109.7 5.0 %collective-permute-start.23 = (bf16[128,512]{1,0:T(8,128)(2,1)S(1)}, bf16[128,512]{1,0:T(8,128)(2,1)S(1)}, u32[]{:S(2)}, u32[]{:S(2)}) collective-permute-start(bf16[128,512]{1,0:T(8,128)(2,1)S(1)} %get-tuple-element.67), channel_id=1, source_target_pairs={{0,4},{4,0},{8,12},{12,8},{16,20},{20,16},{24,28},{28,24},{1,5},{5... | collective-permute-start | bytes 393224 | tf_op jit(solution)/shard_map/ppermute | solution.py:441

commit v15 on v14

--- a/solution.py
+++ b/solution.py
@@ -104,7 +104,7 @@
     )[0]
 
 
-def state_prefix(key_input, value_input, n_seq, place):
+def state_prefix(key_input, value_input, n_seq, place, beside):
     inner = n_seq // LINE
     i = place % inner
     heads = key_input.shape[1] // DH
@@ -131,7 +131,7 @@
     later = (place // inner) % 2 == 1
     masks = [mask for target in targets for mask in [later] + [owner < target for owner in members]]
     dtypes = [jnp.float32] + [jnp.bfloat16] * (len(targets) - 1)
-    befores = combine([from_half], dtypes, [from_pair] + values, masks)
+    befores = combine([hold(from_half, *beside)], dtypes, [from_pair] + values, masks)
     terms = [befores[0]]
     for turn in range(1, len(targets)):
         terms.append(lax.ppermute(befores[turn], "seq", turn_pairs(n_seq, turn)))
@@ -382,12 +382,12 @@
     def along(value, hops):
         return lax.ppermute(value, "seq", line_pairs(n_seq, hops))
 
-    terms, stepped = state_prefix(key_input, value_input, n_seq, place)
     some = heads // 2
     inners = [
         causal_part(queries, key_input, value_input, 0, some),
         causal_part(queries, key_input, value_input, some, heads - some),
     ]
+    terms, stepped = state_prefix(key_input, value_input, n_seq, place, inners)
 
     own_columns = hold(out_weight, stepped)
     w_halves = along(own_columns, SWAP_HALVES)
@@ -427,9 +427,10 @@
             [blocks[block] for block in weights],
             hold(flag, *pins),
         )
-        first_sent, bit = sent, 1
+        first_sent, steps, bit = sent, [], 1
         while bit < n_head:
             got = lax.ppermute(sent, "head", flip_pairs(n_head, bit))
+            steps.append(got)
             bit *= 2
             if bit < n_head:
                 sent, kept = fold(kept, got)
@@ -441,24 +442,25 @@
                 piece = lax.ppermute(piece, "seq", turn_pairs(n_seq, -turn))
             starts = [(owners[block] * inner + (i + turn) % inner) * width for block in own]
             pieces.append((piece, starts))
-        return pieces, first_sent, got
+        return pieces, first_sent, steps
 
     turns = list(range(inner))
     shape = (out_rows, width * n_seq)
     in_kernel = width % DH == 0 and out_rows == DH
 
-    pieces, pins, ends = [], [], []
+    pieces, pins, firsts, ends = [], [], [], []
 
     def group(members, some):
-        more, sent, end = summed([(turn, some) for turn in members], pins)
+        more, sent, steps = summed([(turn, some) for turn in members], pins)
         pieces.extend(more)
-        ends.append(end)
+        firsts.append(steps[0])
+        ends.append(steps[-1])
         pins[:] = [sent, squares]
         return [piece for piece, _ in more]
 
     group(turns[:1], [0])
     returned = group(turns[1:], [0]) if inner > 1 else []
-    w_ends = along(hold(w_halves, *ends), TO_ENDS)
+    w_ends = along(hold(w_halves, ends[0], *firsts), TO_ENDS)
     blocks.append((w_middle, w_ends))
     group(turns[:1], [1, 2])
     if inner > 1:

time: 117 us -> 130 us (1.11)
  starting transfers between devices: 34 us -> 53.1 us
  waiting for transfers between devices: 57 us -> 45.9 us
  local copies, waits for them, and re-layouts: 3.59 us -> 9.52 us
    ppermute x4, starting transfers between devices: 8.28 us -> 26.8 us  [along(): return lax.ppermute(value, 'seq', line_pairs(n_seq, hops))]
    ppermute x4, waiting for transfers between devices: 10.3 us -> 3.6 us  [along(): return lax.ppermute(value, 'seq', line_pairs(n_seq, hops))]
    unnamed x20 -> x32, local copies, waits for them, and re-layouts: 3.39 us -> 9.32 us
    ppermute x1, waiting for transfers between devices: 8.12 us -> 2.45 us  [shards(): lax.ppermute(kept_rows, 'seq', pairs)]
    ppermute x10, waiting for transfers between devices: 15.8 us -> 18.5 us  [summed(): got = lax.ppermute(sent, 'head', flip_pairs(n_head, bit))]
    ppermute x3, starting transfers between devices: 1.79 us -> 3.71 us  [summed(): piece = lax.ppermute(piece, 'seq', turn_pairs(n_seq, -turn))]
    ppermute x3, waiting for transfers between devices: 7.32 us -> 5.83 us  [summed(): piece = lax.ppermute(piece, 'seq', turn_pairs(n_seq, -turn))]
  transfers between devices with their start and end apart: 25 -> 25, of which waited for: 17 -> 16; matrix products, arithmetic and copies ran while one was open for 0% -> 0% of each run, Pallas kernels for 14% -> 13%
where the time goes in v15:
time: 130 us; the launch traced here: 129 us
  starting transfers between devices  53.1 us (41%)
  waiting for transfers between devices  45.9 us (35%)
  Pallas kernels  20.1 us (15%)
  local copies, waits for them, and re-layouts  9.52 us (7%)
    ppermute x4, starting transfers between devices, along(): return lax.ppermute(value, 'seq', line_pairs(n_seq, hops))  26.8 us
    pallas_call x24, Pallas kernels, local_call(): pl.pallas_call(kernel, in_specs=[pl.BlockSpec(memory_space=pltpu.SMEM)] +...  18.7 us
    ppermute x10, waiting for transfers between devices, summed(): got = lax.ppermute(sent, 'head', flip_pairs(n_head, bit))  18.5 us
    unnamed x32, local copies, waits for them, and re-layouts  9.32 us
    ppermute x10, starting transfers between devices, summed(): got = lax.ppermute(sent, 'head', flip_pairs(n_head, bit))  7.68 us
    ppermute x3, waiting for transfers between devices, summed(): piece = lax.ppermute(piece, 'seq', turn_pairs(n_seq, -turn))  5.83 us
    ppermute x1, waiting for transfers between devices, shards(): lax.ppermute(sent_rows, 'seq', pairs)  5.62 us
    ppermute x1, starting transfers between devices, state_prefix(): from_half = lax.ppermute(second, 'seq', line_pairs(n_seq, [(0, 2), (1, 3)]))  4.87 us
  transfers between devices with their start and end apart: 25, of which 16 were waited for; matrix products, arithmetic and copies ran while one was open for 0% of the time, Pallas kernels for 13%

profile of v15, /device:TPU:0, one launch (start us, length us, event | category | flops | bytes accessed | tf_op | source)
XLA Modules:
  0.0 129.1 jit_solution(11560948998157553672)
XLA Ops:
  0.0 1.2 copy-done
  1.2 1.2 copy-done.2
  2.5 0.5 shard_map.74
  2.9 3.0 %collective-permute-start = (bf16[4,128,128]{2,1,0:T(8,128)(2,1)S(1)}, bf16[4,128,128]{2,1,0:T(8,128)(2,1)S(1)}, u32[]{:S(2)}, u32[]{:S(2)}) collective-permute-start(bf16[4,128,128]{2,1,0:T(8,128)(2,1)S(1)} %shard_map.74), channel_id=1, source_target_pairs={{0,4},{4,0},{8,12},{12,8},{16,20},{20,16},{24,28},{28,24},{1,5},{5... | collective-permute-start | bytes 393224 | tf_op jit(solution)/shard_map/ppermute | solution.py:124
  5.9 0.5 shard_map.73.refs_0_.refs_2_
  6.4 3.0 %collective-permute-done.refs_1_.refs_3_ = bf16[4,128,128]{2,1,0:T(8,128)(2,1)S(1)} collective-permute-done((bf16[4,128,128]{2,1,0:T(8,128)(2,1)S(1)}, bf16[4,128,128]{2,1,0:T(8,128)(2,1)S(1)}, u32[]{:S(2)}, u32[]{:S(2)}) %collective-permute-start) | collective-permute-done | bytes 131104 | tf_op jit(solution)/shard_map/ppermute | solution.py:124
  9.5 1.9 %collective-permute-start.1 = (bf16[4,128,128]{2,1,0:T(8,128)(2,1)S(1)}, bf16[4,128,128]{2,1,0:T(8,128)(2,1)S(1)}, u32[]{:S(2)}, u32[]{:S(2)}) collective-permute-start(bf16[4,128,128]{2,1,0:T(8,128)(2,1)S(1)} %shard_map.75), channel_id=1, source_target_pairs={{0,8},{4,12},{8,0},{12,4},{16,24},{20,28},{24,16},{28,20},{1,9},{5... | collective-permute-start | bytes 393224 | tf_op jit(solution)/shard_map/ppermute | solution.py:127
  11.4 3.1 %collective-permute-done.1.refs_2_.refs_1_ = bf16[4,128,128]{2,1,0:T(8,128)(2,1)S(1)} collective-permute-done((bf16[4,128,128]{2,1,0:T(8,128)(2,1)S(1)}, bf16[4,128,128]{2,1,0:T(8,128)(2,1)S(1)}, u32[]{:S(2)}, u32[]{:S(2)}) %collective-permute-start.1) | collective-permute-done | bytes 131104 | tf_op jit(solution)/shard_map/ppermute | solution.py:127
  14.6 0.6 copy-done.10
  15.2 4.9 %collective-permute-start.2 = (bf16[4,128,128]{2,1,0:T(8,128)(2,1)S(1)}, bf16[4,128,128]{2,1,0:T(8,128)(2,1)S(1)}, u32[]{:S(2)}, u32[]{:S(2)}) collective-permute-start(bf16[4,128,128]{2,1,0:T(8,128)(2,1)S(1)} %shard_map.76), channel_id=1, source_target_pairs={{0,16},{4,20},{8,24},{12,28},{1,17},{5,21},{9,25},{13,29},{2,18},{... | collective-permute-start | bytes 393224 | tf_op jit(solution)/shard_map/ppermute | solution.py:129
  20.0 2.5 %collective-permute-done.2.refs_0_ = bf16[4,128,128]{2,1,0:T(8,128)(2,1)S(1)} collective-permute-done((bf16[4,128,128]{2,1,0:T(8,128)(2,1)S(1)}, bf16[4,128,128]{2,1,0:T(8,128)(2,1)S(1)}, u32[]{:S(2)}, u32[]{:S(2)}) %collective-permute-start.2) | collective-permute-done | bytes 131104 | tf_op jit(solution)/shard_map/ppermute | solution.py:129
  22.5 0.7 copy-done.13
  23.2 3.4 %collective-permute-start.9 = (bf16[1024,512]{1,0:T(8,128)(2,1)}, bf16[1024,512]{1,0:T(8,128)(2,1)}, u32[]{:S(2)}, u32[]{:S(2)}) collective-permute-start(bf16[1024,512]{1,0:T(8,128)(2,1)} %refs_2_.3), channel_id=1, source_target_pairs={{0,16},{4,20},{8,24},{12,28},{16,0},{20,4},{24,8},{28,12},{1,17},{... | collective-permute-start | bytes 3145736 | tf_op jit(solution)/shard_map/ppermute | solution.py:383
  26.6 1.1 shard_map.77.refs_2_
  27.7 1.0 copy-done.5
  28.7 0.1 stack.81
  28.8 1.1 shard_map.78.refs_3_
  29.9 1.0 copy-done.7
  30.9 0.7 shard_map.79
  31.6 1.6 %collective-permute-start.3 = (bf16[4,128,128]{2,1,0:T(8,128)(2,1)S(1)}, bf16[4,128,128]{2,1,0:T(8,128)(2,1)S(1)}, u32[]{:S(2)}, u32[]{:S(2)}) collective-permute-start(bf16[4,128,128]{2,1,0:T(8,128)(2,1)S(1)} %get-tuple-element.41), channel_id=1, source_target_pairs={{0,4},{4,0},{8,12},{12,8},{16,20},{20,16},{24,28},{28,24},{1,5},{5... | collective-permute-start | bytes 393224 | tf_op jit(solution)/shard_map/ppermute | solution.py:137
  33.2 21.4 %collective-permute-start.8 = (bf16[1024,512]{1,0:T(8,128)(2,1)}, bf16[1024,512]{1,0:T(8,128)(2,1)}, u32[]{:S(2)}, u32[]{:S(2)}) collective-permute-start(bf16[1024,512]{1,0:T(8,128)(2,1)} %refs_2_.3), channel_id=1, source_target_pairs={{0,8},{4,12},{8,0},{12,4},{16,24},{20,28},{24,16},{28,20},{1,9},{5... | collective-permute-start | bytes 3145736 | tf_op jit(solution)/shard_map/ppermute | solution.py:383
  54.6 0.1 pad_add_fusion.1.place_ref
  54.7 1.2 copy-done.6
  55.9 1.2 copy-done.8
  57.1 1.2 copy-done.9
  58.3 1.7 %shard_map.80 = (bf16[256,1024]{1,0:T(8,128)(2,1)S(1)}, bf16[256,1024]{1,0:T(8,128)(2,1)S(1)}, f32[4,128]{1,0:T(4,128)S(1)}) custom-call(s32[2]{0:T(128)S(1)} %pad_add_fusion.1.place_ref, bf16[512,1024]{1,0:T(8,128)(2,1)S(1)} %copy-done.4, bf16[512,1024]{1,0:T(8,128)(2,1)S(1)} %copy-done.9, f32[32,1,128]{2,1,0:T(1,128)S(1)} %bitcast.17, ...), custom_call_target="tpu_custom_call" | custom-call | flops 268435456 | bytes 6178816 | tf_op jit(solution)/shard_map/pallas_call | solution.py:49
  60.0 0.6 collective-permute-start.6
  60.6 1.5 %collective-permute-start.7 = (bf16[256,1024]{1,0:T(8,128)(2,1)S(1)}, bf16[256,1024]{1,0:T(8,128)(2,1)S(1)}, u32[]{:S(2)}, u32[]{:S(2)}) collective-permute-start(bf16[256,1024]{1,0:T(8,128)(2,1)S(1)} %get-tuple-element.44.refs_1_), channel_id=1, source_target_pairs={{0,4},{4,0},{8,12},{12,8},{16,20},{20,16},{24,28},{28,24},{1,5},{5... | collective-permute-start | bytes 1572872 | tf_op jit(solution)/shard_map/ppermute | solution.py:405
  62.1 1.1 collective-permute-done.4
  63.2 1.5 %collective-permute-start.5 = (f32[1,128]{1,0:T(1,128)S(1)}, f32[1,128]{1,0:T(1,128)S(1)}, u32[]{:S(2)}, u32[]{:S(2)}) collective-permute-start(f32[1,128]{1,0:T(1,128)S(1)} %slice.15), channel_id=1, source_target_pairs={{0,2},{1,3},{2,0},{3,1},{4,6},{5,7},{6,4},{7,5},{8,10},{9,11},{10,... | collective-permute-start | bytes 1544 | tf_op jit(solution)/shard_map/ppermute | solution.py:410
  64.8 1.9 %shard_map.81 = (bf16[256,512]{1,0:T(8,128)(2,1)S(1)}, f32[256,512]{1,0:T(8,128)S(1)}) custom-call(s32[1]{0:T(128)} %bitcast.10.flag_ref, bf16[256,1024]{1,0:T(8,128)(2,1)S(1)} %get-tuple-element.43.refs_0_, bf16[256,1024]{1,0:T(8,128)(2,1)S(1)} %get-tuple-element.44.refs_1_, bf16[1024,512]{1,0:T(8,128)(2,1)} %refs_2_.3), custom_call_target="tpu_custom_call" | custom-call | flops 536870912 | bytes 2883584 | tf_op jit(solution)/shard_map/pallas_call | solution.py:49
  66.7 0.1 collective-permute-done.5
  66.8 2.5 %collective-permute-done.6.refs_0_.refs_2_ = bf16[256,1024]{1,0:T(8,128)(2,1)S(1)} collective-permute-done((bf16[256,1024]{1,0:T(8,128)(2,1)S(1)}, bf16[256,1024]{1,0:T(8,128)(2,1)S(1)}, u32[]{:S(2)}, u32[]{:S(2)}) %collective-permute-start.6) | collective-permute-done | bytes 524320 | tf_op jit(solution)/shard_map/ppermute | solution.py:405
  69.2 5.6 %collective-permute-done.7.refs_1_.refs_3_ = bf16[256,1024]{1,0:T(8,128)(2,1)S(1)} collective-permute-done((bf16[256,1024]{1,0:T(8,128)(2,1)S(1)}, bf16[256,1024]{1,0:T(8,128)(2,1)S(1)}, u32[]{:S(2)}, u32[]{:S(2)}) %collective-permute-start.7) | collective-permute-done | bytes 524320 | tf_op jit(solution)/shard_map/ppermute | solution.py:405
  74.9 1.9 %shard_map.82 = (bf16[256,512]{1,0:T(8,128)(2,1)S(1)}, f32[256,512]{1,0:T(8,128)S(1)}) custom-call(s32[1]{0:T(128)} %bitcast.10.flag_ref, bf16[256,1024]{1,0:T(8,128)(2,1)S(1)} %collective-permute-done.6.refs_0_.refs_2_, bf16[256,1024]{1,0:T(8,128)(2,1)S(1)} %collective-permute-done.7.refs_1_.refs_3_, bf16[1024,512]{1,0:T(8,128)(2,1)} %refs_2_.3), custom_call_target="tpu_custom_call" | custom-call | flops 536870912 | bytes 2883584 | tf_op jit(solution)/shard_map/pallas_call | solution.py:49
  76.9 1.6 %collective-permute-start.11 = (bf16[128,512]{1,0:T(8,128)(2,1)S(1)}, bf16[128,512]{1,0:T(8,128)(2,1)S(1)}, u32[]{:S(2)}, u32[]{:S(2)}) collective-permute-start(bf16[128,512]{1,0:T(8,128)(2,1)S(1)} %get-tuple-element.54), channel_id=1, source_target_pairs={{0,2},{1,3},{2,0},{3,1},{4,6},{5,7},{6,4},{7,5},{8,10},{9,11},{10,... | collective-permute-start | bytes 393224 | tf_op jit(solution)/shard_map/ppermute | solution.py:432
  78.5 0.7 collective-permute-start.19
  79.2 3.7 %collective-permute-done.11.got_ref = bf16[128,512]{1,0:T(8,128)(2,1)S(1)} collective-permute-done((bf16[128,512]{1,0:T(8,128)(2,1)S(1)}, bf16[128,512]{1,0:T(8,128)(2,1)S(1)}, u32[]{:S(2)}, u32[]{:S(2)}) %collective-permute-start.11) | collective-permute-done | bytes 131104 | tf_op jit(solution)/shard_map/ppermute | solution.py:432
  82.9 1.3 collective-permute-start.20
  84.2 2.8 %shard_map.83 = (bf16[256,1024]{1,0:T(8,128)(2,1)S(1)}, f32[256,1024]{1,0:T(8,128)S(1)}) custom-call(s32[1]{0:T(128)} %bitcast.10.flag_ref, bf16[256,1024]{1,0:T(8,128)(2,1)S(1)} %get-tuple-element.43.refs_0_, bf16[256,1024]{1,0:T(8,128)(2,1)S(1)} %get-tuple-element.44.refs_1_, bf16[1024,512]{1,0:T(8,128)(2,1)} %collective-permute-done.8.refs_2_, ...), custom_call_target="tpu_custom_call" | custom-call | flops 1073741824 | bytes 4718592 | tf_op jit(solution)/shard_map/pallas_call | solution.py:49
  87.1 2.8 %shard_map.84 = (bf16[256,1024]{1,0:T(8,128)(2,1)S(1)}, f32[256,1024]{1,0:T(8,128)S(1)}) custom-call(s32[1]{0:T(128)} %bitcast.10.flag_ref, bf16[256,1024]{1,0:T(8,128)(2,1)S(1)} %collective-permute-done.6.refs_0_.refs_2_, bf16[256,1024]{1,0:T(8,128)(2,1)S(1)} %collective-permute-done.7.refs_1_.refs_3_, bf16[1024,512]{1,0:T(8,128)(2,1)} %collective-permute-done.8.refs_2_, ...), custom_call_target="tpu_custom_call" | custom-call | flops 1073741824 | bytes 4718592 | tf_op jit(solution)/shard_map/pallas_call | solution.py:49
  89.9 0.6 collective-permute-start.16
  90.5 1.6 %collective-permute-start.13 = (bf16[128,512]{1,0:T(8,128)(2,1)S(1)}, bf16[128,512]{1,0:T(8,128)(2,1)S(1)}, u32[]{:S(2)}, u32[]{:S(2)}) collective-permute-start(bf16[128,512]{1,0:T(8,128)(2,1)S(1)} %get-tuple-element.56), channel_id=1, source_target_pairs={{0,2},{1,3},{2,0},{3,1},{4,6},{5,7},{6,4},{7,5},{8,10},{9,11},{10,... | collective-permute-start | bytes 393224 | tf_op jit(solution)/shard_map/ppermute | solution.py:432
  92.1 0.1 shard_map.87
  92.2 0.6 collective-permute-start.15
  92.7 0.1 shard_map.88
  92.8 1.6 %collective-permute-start.17 = (bf16[128,1024]{1,0:T(8,128)(2,1)S(1)}, bf16[128,1024]{1,0:T(8,128)(2,1)S(1)}, u32[]{:S(2)}, u32[]{:S(2)}) collective-permute-start(bf16[128,1024]{1,0:T(8,128)(2,1)S(1)} %get-tuple-element.60), channel_id=1, source_target_pairs={{0,2},{1,3},{2,0},{3,1},{4,6},{5,7},{6,4},{7,5},{8,10},{9,11},{10,... | collective-permute-start | bytes 786440 | tf_op jit(solution)/shard_map/ppermute | solution.py:432
  94.4 2.5 %collective-permute-done.13.got_ref = bf16[128,512]{1,0:T(8,128)(2,1)S(1)} collective-permute-done((bf16[128,512]{1,0:T(8,128)(2,1)S(1)}, bf16[128,512]{1,0:T(8,128)(2,1)S(1)}, u32[]{:S(2)}, u32[]{:S(2)}) %collective-permute-start.13) | collective-permute-done | bytes 131104 | tf_op jit(solution)/shard_map/ppermute | solution.py:432
  96.9 0.6 collective-permute-start.18
  97.5 4.4 %collective-permute-done.18.refs_1_ = bf16[128,512]{1,0:T(8,128)(2,1)S(1)} collective-permute-done((bf16[128,512]{1,0:T(8,128)(2,1)S(1)}, bf16[128,512]{1,0:T(8,128)(2,1)S(1)}, u32[]{:S(2)}, u32[]{:S(2)}) %collective-permute-start.18) | collective-permute-done | bytes 131104 | tf_op jit(solution)/shard_map/ppermute | solution.py:442
  102.0 0.6 collective-permute-done.15.got_ref
  102.5 4.7 %collective-permute-done.17.got_ref = bf16[128,1024]{1,0:T(8,128)(2,1)S(1)} collective-permute-done((bf16[128,1024]{1,0:T(8,128)(2,1)S(1)}, bf16[128,1024]{1,0:T(8,128)(2,1)S(1)}, u32[]{:S(2)}, u32[]{:S(2)}) %collective-permute-start.17) | collective-permute-done | bytes 262176 | tf_op jit(solution)/shard_map/ppermute | solution.py:432
  107.2 3.6 %collective-permute-done.20.refs_5_ = bf16[1024,512]{1,0:T(8,128)(2,1)S(1)} collective-permute-done((bf16[1024,512]{1,0:T(8,128)(2,1)}, bf16[1024,512]{1,0:T(8,128)(2,1)S(1)}, u32[]{:S(2)}, u32[]{:S(2)}) %collective-permute-start.20) | collective-permute-done | bytes 1048608 | tf_op jit(solution)/shard_map/ppermute | solution.py:383
  110.8 1.3 shard_map.90
  112.2 1.9 %collective-permute-done.21.got_ref = bf16[256,1024]{1,0:T(8,128)(2,1)S(1)} collective-permute-done((bf16[256,1024]{1,0:T(8,128)(2,1)S(1)}, bf16[256,1024]{1,0:T(8,128)(2,1)S(1)}, u32[]{:S(2)}, u32[]{:S(2)}) %collective-permute-start.21) | collective-permute-done | bytes 524320 | tf_op jit(solution)/shard_map/ppermute | solution.py:432
  114.1 0.1 shard_map.91
  114.2 1.6 %collective-permute-start.22 = (bf16[128,1024]{1,0:T(8,128)(2,1)S(1)}, bf16[128,1024]{1,0:T(8,128)(2,1)S(1)}, u32[]{:S(2)}, u32[]{:S(2)}) collective-permute-start(bf16[128,1024]{1,0:T(8,128)(2,1)S(1)} %get-tuple-element.67), channel_id=1, source_target_pairs={{0,2},{1,3},{2,0},{3,1},{4,6},{5,7},{6,4},{7,5},{8,10},{9,11},{10,... | collective-permute-start | bytes 786440 | tf_op jit(solution)/shard_map/ppermute | solution.py:432
  115.8 1.5 %collective-permute-start.24 = (bf16[128,1024]{1,0:T(8,128)(2,1)S(1)}, bf16[128,1024]{1,0:T(8,128)(2,1)S(1)}, u32[]{:S(2)}, u32[]{:S(2)}) collective-permute-start(bf16[128,1024]{1,0:T(8,128)(2,1)S(1)} %shard_map.95), channel_id=1, source_target_pairs={{0,4},{4,0},{8,12},{12,8},{16,20},{20,16},{24,28},{28,24},{1,5},{5... | collective-permute-start | bytes 786440 | tf_op jit(solution)/shard_map/ppermute | solution.py:442
  117.4 5.2 %collective-permute-done.22.got_ref = bf16[128,1024]{1,0:T(8,128)(2,1)S(1)} collective-permute-done((bf16[128,1024]{1,0:T(8,128)(2,1)S(1)}, bf16[128,1024]{1,0:T(8,128)(2,1)S(1)}, u32[]{:S(2)}, u32[]{:S(2)}) %collective-permute-start.22) | collective-permute-done | bytes 262176 | tf_op jit(solution)/shard_map/ppermute | solution.py:432
  122.6 1.6 %collective-permute-start.23 = (bf16[128,512]{1,0:T(8,128)(2,1)S(1)}, bf16[128,512]{1,0:T(8,128)(2,1)S(1)}, u32[]{:S(2)}, u32[]{:S(2)}) collective-permute-start(bf16[128,512]{1,0:T(8,128)(2,1)S(1)} %get-tuple-element.69), channel_id=1, source_target_pairs={{0,4},{4,0},{8,12},{12,8},{16,20},{20,16},{24,28},{28,24},{1,5},{5... | collective-permute-start | bytes 393224 | tf_op jit(solution)/shard_map/ppermute | solution.py:442
  124.2 0.1 stack.92.starts_ref
  124.4 1.8 %shard_map.96.refs_2_ = bf16[128,4096]{1,0:T(8,128)(2,1)} custom-call(s32[6]{0:T(128)S(1)} %stack.92.starts_ref, f32[1,128]{1,0:T(1,128)S(1)} %slice_add_fusion.1.squares_ref, bf16[128,512]{1,0:T(8,128)(2,1)S(1)} %shard_map.93.refs_0_, bf16[128,512]{1,0:T(8,128)(2,1)S(1)} %collective-permute-done.18.refs_1_, bf16[128,1024]{1,0:T(8,128)(2,1)S(1)} %shard_map.94.refs_2_, ...), custom_call_target="tpu_custom_call" | custom-call | bytes 1835520 | tf_op jit(solution)/shard_map/pallas_call | solution.py:49
  126.3 1.4 %collective-permute-done.23.refs_1_ = bf16[128,512]{1,0:T(8,128)(2,1)S(1)} collective-permute-done((bf16[128,512]{1,0:T(8,128)(2,1)S(1)}, bf16[128,512]{1,0:T(8,128)(2,1)S(1)}, u32[]{:S(2)}, u32[]{:S(2)}) %collective-permute-start.23) | collective-permute-done | bytes 131104 | tf_op jit(solution)/shard_map/ppermute | solution.py:442
  127.7 1.4 %shard_map.97 = bf16[128,4096]{1,0:T(8,128)(2,1)} custom-call(s32[2]{0:T(128)S(1)} %pad_add_fusion.starts_ref, f32[1,128]{1,0:T(1,128)S(1)} %slice_add_fusion.1.squares_ref, bf16[128,512]{1,0:T(8,128)(2,1)S(1)} %get-tuple-element.68.refs_0_, bf16[128,512]{1,0:T(8,128)(2,1)S(1)} %collective-permute-done.23.refs_1_, ...), custom_call_target="tpu_custom_call", output_to_operand_aliasing={{}: (4, {})} | custom-call | bytes 524288 | tf_op jit(solution)/shard_map/pallas_call | solution.py:352
  (52 shorter events, 0.8 us)
Async XLA Ops:
  0.0 1.2 copy-start
  1.2 1.2 copy-start.2
  2.5 3.5 %copy-start.1 = (bf16[512,1024]{1,0:T(8,128)(2,1)S(1)}, bf16[512,1024]{1,0:T(8,128)(2,1)}, u32[]{:S(2)}) copy-start(bf16[512,1024]{1,0:T(8,128)(2,1)} %k_ref.7) | copy-start | bytes 3145732
  2.9 6.5 %collective-permute-start = (bf16[4,128,128]{2,1,0:T(8,128)(2,1)S(1)}, bf16[4,128,128]{2,1,0:T(8,128)(2,1)S(1)}, u32[]{:S(2)}, u32[]{:S(2)}) collective-permute-start(bf16[4,128,128]{2,1,0:T(8,128)(2,1)S(1)} %shard_map.74), channel_id=1, source_target_pairs={{0,4},{4,0},{8,12},{12,8},{16,20},{20,16},{24,28},{28,24},{1,5},{5... | collective-permute-start | bytes 393224 | tf_op jit(solution)/shard_map/ppermute | solution.py:124
  6.4 20.2 %copy-start.4 = (bf16[512,1024]{1,0:T(8,128)(2,1)S(1)}, bf16[512,1024]{1,0:T(8,128)(2,1)}, u32[]{:S(2)}) copy-start(bf16[512,1024]{1,0:T(8,128)(2,1)} %q_ref.5) | copy-start | bytes 3145732
  9.5 5.0 %collective-permute-start.1 = (bf16[4,128,128]{2,1,0:T(8,128)(2,1)S(1)}, bf16[4,128,128]{2,1,0:T(8,128)(2,1)S(1)}, u32[]{:S(2)}, u32[]{:S(2)}) collective-permute-start(bf16[4,128,128]{2,1,0:T(8,128)(2,1)S(1)} %shard_map.75), channel_id=1, source_target_pairs={{0,8},{4,12},{8,0},{12,4},{16,24},{20,28},{24,16},{28,20},{1,9},{5... | collective-permute-start | bytes 393224 | tf_op jit(solution)/shard_map/ppermute | solution.py:127
  14.5 0.6 copy-start.10
  15.2 13.6 %copy-start.3 = (bf16[512,1024]{1,0:T(8,128)(2,1)S(1)}, bf16[512,1024]{1,0:T(8,128)(2,1)}, u32[]{:S(2)}) copy-start(bf16[512,1024]{1,0:T(8,128)(2,1)} %v_ref.7) | copy-start | bytes 3145732
  15.2 7.4 %collective-permute-start.2 = (bf16[4,128,128]{2,1,0:T(8,128)(2,1)S(1)}, bf16[4,128,128]{2,1,0:T(8,128)(2,1)S(1)}, u32[]{:S(2)}, u32[]{:S(2)}) collective-permute-start(bf16[4,128,128]{2,1,0:T(8,128)(2,1)S(1)} %shard_map.76), channel_id=1, source_target_pairs={{0,16},{4,20},{8,24},{12,28},{1,17},{5,21},{9,25},{13,29},{2,18},{... | collective-permute-start | bytes 393224 | tf_op jit(solution)/shard_map/ppermute | solution.py:129
  22.5 0.7 copy-start.13
  23.2 59.7 %collective-permute-start.9 = (bf16[1024,512]{1,0:T(8,128)(2,1)}, bf16[1024,512]{1,0:T(8,128)(2,1)}, u32[]{:S(2)}, u32[]{:S(2)}) collective-permute-start(bf16[1024,512]{1,0:T(8,128)(2,1)} %refs_2_.3), channel_id=1, source_target_pairs={{0,16},{4,20},{8,24},{12,28},{16,0},{20,4},{24,8},{28,12},{1,17},{... | collective-permute-start | bytes 3145736 | tf_op jit(solution)/shard_map/ppermute | solution.py:383
  27.7 1.0 copy-start.5
  28.8 2.1 %copy-start.11 = (bf16[4,128,128]{2,1,0:T(8,128)(2,1)S(1)}, bf16[4,128,128]{2,1,0:T(8,128)(2,1)}, u32[]{:S(2)}) copy-start(bf16[4,128,128]{2,1,0:T(8,128)(2,1)} %copy-done.10) | copy-start | bytes 393220
  28.8 2.1 %copy-start.14 = (bf16[4,128,128]{2,1,0:T(8,128)(2,1)S(1)}, bf16[4,128,128]{2,1,0:T(8,128)(2,1)}, u32[]{:S(2)}) copy-start(bf16[4,128,128]{2,1,0:T(8,128)(2,1)} %copy-done.13) | copy-start | bytes 393220
  29.9 1.0 copy-start.7
  30.9 23.7 %copy-start.12 = (f32[8,128,128]{2,1,0:T(8,128)S(1)}, f32[8,128,128]{2,1,0:T(8,128)}, u32[]{:S(2)}) copy-start(f32[8,128,128]{2,1,0:T(8,128)} %kv_ref.1) | copy-start | bytes 1572868
  30.9 23.7 %copy-start.15 = (f32[4096]{0:T(1024)S(1)}, f32[4096]{0:T(1024)}, u32[]{:S(2)}) copy-start(f32[4096]{0:T(1024)} %param.12) | copy-start | bytes 49156
  31.6 23.0 %collective-permute-start.3 = (bf16[4,128,128]{2,1,0:T(8,128)(2,1)S(1)}, bf16[4,128,128]{2,1,0:T(8,128)(2,1)S(1)}, u32[]{:S(2)}, u32[]{:S(2)}) collective-permute-start(bf16[4,128,128]{2,1,0:T(8,128)(2,1)S(1)} %get-tuple-element.41), channel_id=1, source_target_pairs={{0,4},{4,0},{8,12},{12,8},{16,20},{20,16},{24,28},{28,24},{1,5},{5... | collective-permute-start | bytes 393224 | tf_op jit(solution)/shard_map/ppermute | solution.py:137
  33.2 51.0 %collective-permute-start.8 = (bf16[1024,512]{1,0:T(8,128)(2,1)}, bf16[1024,512]{1,0:T(8,128)(2,1)}, u32[]{:S(2)}, u32[]{:S(2)}) collective-permute-start(bf16[1024,512]{1,0:T(8,128)(2,1)} %refs_2_.3), channel_id=1, source_target_pairs={{0,8},{4,12},{8,0},{12,4},{16,24},{20,28},{24,16},{28,20},{1,9},{5... | collective-permute-start | bytes 3145736 | tf_op jit(solution)/shard_map/ppermute | solution.py:383
  54.6 1.2 copy-start.6
  55.9 1.2 copy-start.8
  57.1 1.2 copy-start.9
  60.0 9.2 %collective-permute-start.6 = (bf16[256,1024]{1,0:T(8,128)(2,1)S(1)}, bf16[256,1024]{1,0:T(8,128)(2,1)S(1)}, u32[]{:S(2)}, u32[]{:S(2)}) collective-permute-start(bf16[256,1024]{1,0:T(8,128)(2,1)S(1)} %get-tuple-element.43.refs_0_), channel_id=1, source_target_pairs={{0,4},{4,0},{8,12},{12,8},{16,20},{20,16},{24,28},{28,24},{1,5},{5... | collective-permute-start | bytes 1572872 | tf_op jit(solution)/shard_map/ppermute | solution.py:405
  60.6 14.3 %collective-permute-start.7 = (bf16[256,1024]{1,0:T(8,128)(2,1)S(1)}, bf16[256,1024]{1,0:T(8,128)(2,1)S(1)}, u32[]{:S(2)}, u32[]{:S(2)}) collective-permute-start(bf16[256,1024]{1,0:T(8,128)(2,1)S(1)} %get-tuple-element.44.refs_1_), channel_id=1, source_target_pairs={{0,4},{4,0},{8,12},{12,8},{16,20},{20,16},{24,28},{28,24},{1,5},{5... | collective-permute-start | bytes 1572872 | tf_op jit(solution)/shard_map/ppermute | solution.py:405
  62.1 1.1 collective-permute-start.4
  63.2 3.5 %collective-permute-start.5 = (f32[1,128]{1,0:T(1,128)S(1)}, f32[1,128]{1,0:T(1,128)S(1)}, u32[]{:S(2)}, u32[]{:S(2)}) collective-permute-start(f32[1,128]{1,0:T(1,128)S(1)} %slice.15), channel_id=1, source_target_pairs={{0,2},{1,3},{2,0},{3,1},{4,6},{5,7},{6,4},{7,5},{8,10},{9,11},{10,... | collective-permute-start | bytes 1544 | tf_op jit(solution)/shard_map/ppermute | solution.py:410
  66.8 10.1 %collective-permute-start.10 = (bf16[256,512]{1,0:T(8,128)(2,1)S(1)}, bf16[256,512]{1,0:T(8,128)(2,1)S(1)}, u32[]{:S(2)}, u32[]{:S(2)}) collective-permute-start(bf16[256,512]{1,0:T(8,128)(2,1)S(1)} %get-tuple-element.45), channel_id=1, source_target_pairs={{0,1},{1,0},{2,3},{3,2},{4,5},{5,4},{6,7},{7,6},{8,9},{9,8},{10,11... | collective-permute-start | bytes 786440 | tf_op jit(solution)/shard_map/ppermute | solution.py:432
  76.8 6.1 %collective-permute-start.12 = (bf16[256,512]{1,0:T(8,128)(2,1)S(1)}, bf16[256,512]{1,0:T(8,128)(2,1)S(1)}, u32[]{:S(2)}, u32[]{:S(2)}) collective-permute-start(bf16[256,512]{1,0:T(8,128)(2,1)S(1)} %get-tuple-element.47), channel_id=1, source_target_pairs={{0,1},{1,0},{2,3},{3,2},{4,5},{5,4},{6,7},{7,6},{8,9},{9,8},{10,11... | collective-permute-start | bytes 786440 | tf_op jit(solution)/shard_map/ppermute | solution.py:432
  76.9 6.0 %collective-permute-start.11 = (bf16[128,512]{1,0:T(8,128)(2,1)S(1)}, bf16[128,512]{1,0:T(8,128)(2,1)S(1)}, u32[]{:S(2)}, u32[]{:S(2)}) collective-permute-start(bf16[128,512]{1,0:T(8,128)(2,1)S(1)} %get-tuple-element.54), channel_id=1, source_target_pairs={{0,2},{1,3},{2,0},{3,1},{4,6},{5,7},{6,4},{7,5},{8,10},{9,11},{10,... | collective-permute-start | bytes 393224 | tf_op jit(solution)/shard_map/ppermute | solution.py:432
  78.5 28.7 %collective-permute-start.19 = (bf16[1024,512]{1,0:T(8,128)(2,1)}, bf16[1024,512]{1,0:T(8,128)(2,1)S(1)}, u32[]{:S(2)}, u32[]{:S(2)}) collective-permute-start(bf16[1024,512]{1,0:T(8,128)(2,1)} %refs_2_.3), channel_id=1, source_target_pairs={{8,16},{12,20},{16,8},{20,12},{9,17},{13,21},{17,9},{21,13},{10,18... | collective-permute-start | bytes 3145736 | tf_op jit(solution)/shard_map/ppermute | solution.py:383
  82.9 27.9 %collective-permute-start.20 = (bf16[1024,512]{1,0:T(8,128)(2,1)}, bf16[1024,512]{1,0:T(8,128)(2,1)S(1)}, u32[]{:S(2)}, u32[]{:S(2)}) collective-permute-start(bf16[1024,512]{1,0:T(8,128)(2,1)} %collective-permute-done.9.refs_3_), channel_id=1, source_target_pairs={{8,0},{12,4},{16,24},{20,28},{9,1},{13,5},{17,25},{21,29},{10,2},{... | collective-permute-start | bytes 3145736 | tf_op jit(solution)/shard_map/ppermute | solution.py:383
  87.0 5.1 %collective-permute-start.14 = (bf16[256,1024]{1,0:T(8,128)(2,1)S(1)}, bf16[256,1024]{1,0:T(8,128)(2,1)S(1)}, u32[]{:S(2)}, u32[]{:S(2)}) collective-permute-start(bf16[256,1024]{1,0:T(8,128)(2,1)S(1)} %get-tuple-element.50), channel_id=1, source_target_pairs={{0,1},{1,0},{2,3},{3,2},{4,5},{5,4},{6,7},{7,6},{8,9},{9,8},{10,11... | collective-permute-start | bytes 1572872 | tf_op jit(solution)/shard_map/ppermute | solution.py:432
  89.9 2.9 %collective-permute-start.16 = (bf16[256,1024]{1,0:T(8,128)(2,1)S(1)}, bf16[256,1024]{1,0:T(8,128)(2,1)S(1)}, u32[]{:S(2)}, u32[]{:S(2)}) collective-permute-start(bf16[256,1024]{1,0:T(8,128)(2,1)S(1)} %get-tuple-element.52), channel_id=1, source_target_pairs={{0,1},{1,0},{2,3},{3,2},{4,5},{5,4},{6,7},{7,6},{8,9},{9,8},{10,11... | collective-permute-start | bytes 1572872 | tf_op jit(solution)/shard_map/ppermute | solution.py:432
  90.5 6.4 %collective-permute-start.13 = (bf16[128,512]{1,0:T(8,128)(2,1)S(1)}, bf16[128,512]{1,0:T(8,128)(2,1)S(1)}, u32[]{:S(2)}, u32[]{:S(2)}) collective-permute-start(bf16[128,512]{1,0:T(8,128)(2,1)S(1)} %get-tuple-element.56), channel_id=1, source_target_pairs={{0,2},{1,3},{2,0},{3,1},{4,6},{5,7},{6,4},{7,5},{8,10},{9,11},{10,... | collective-permute-start | bytes 393224 | tf_op jit(solution)/shard_map/ppermute | solution.py:432
  92.2 10.4 %collective-permute-start.15 = (bf16[128,1024]{1,0:T(8,128)(2,1)S(1)}, bf16[128,1024]{1,0:T(8,128)(2,1)S(1)}, u32[]{:S(2)}, u32[]{:S(2)}) collective-permute-start(bf16[128,1024]{1,0:T(8,128)(2,1)S(1)} %get-tuple-element.58), channel_id=1, source_target_pairs={{0,2},{1,3},{2,0},{3,1},{4,6},{5,7},{6,4},{7,5},{8,10},{9,11},{10,... | collective-permute-start | bytes 786440 | tf_op jit(solution)/shard_map/ppermute | solution.py:432
  92.8 14.4 %collective-permute-start.17 = (bf16[128,1024]{1,0:T(8,128)(2,1)S(1)}, bf16[128,1024]{1,0:T(8,128)(2,1)S(1)}, u32[]{:S(2)}, u32[]{:S(2)}) collective-permute-start(bf16[128,1024]{1,0:T(8,128)(2,1)S(1)} %get-tuple-element.60), channel_id=1, source_target_pairs={{0,2},{1,3},{2,0},{3,1},{4,6},{5,7},{6,4},{7,5},{8,10},{9,11},{10,... | collective-permute-start | bytes 786440 | tf_op jit(solution)/shard_map/ppermute | solution.py:432
  96.9 5.0 %collective-permute-start.18 = (bf16[128,512]{1,0:T(8,128)(2,1)S(1)}, bf16[128,512]{1,0:T(8,128)(2,1)S(1)}, u32[]{:S(2)}, u32[]{:S(2)}) collective-permute-start(bf16[128,512]{1,0:T(8,128)(2,1)S(1)} %shard_map.89), channel_id=1, source_target_pairs={{0,4},{4,0},{8,12},{12,8},{16,20},{20,16},{24,28},{28,24},{1,5},{5... | collective-permute-start | bytes 393224 | tf_op jit(solution)/shard_map/ppermute | solution.py:442
  112.1 2.0 %collective-permute-start.21 = (bf16[256,1024]{1,0:T(8,128)(2,1)S(1)}, bf16[256,1024]{1,0:T(8,128)(2,1)S(1)}, u32[]{:S(2)}, u32[]{:S(2)}) collective-permute-start(bf16[256,1024]{1,0:T(8,128)(2,1)S(1)} %get-tuple-element.65), channel_id=1, source_target_pairs={{0,1},{1,0},{2,3},{3,2},{4,5},{5,4},{6,7},{7,6},{8,9},{9,8},{10,11... | collective-permute-start | bytes 1572872 | tf_op jit(solution)/shard_map/ppermute | solution.py:432
  114.2 8.4 %collective-permute-start.22 = (bf16[128,1024]{1,0:T(8,128)(2,1)S(1)}, bf16[128,1024]{1,0:T(8,128)(2,1)S(1)}, u32[]{:S(2)}, u32[]{:S(2)}) collective-permute-start(bf16[128,1024]{1,0:T(8,128)(2,1)S(1)} %get-tuple-element.67), channel_id=1, source_target_pairs={{0,2},{1,3},{2,0},{3,1},{4,6},{5,7},{6,4},{7,5},{8,10},{9,11},{10,... | collective-permute-start | bytes 786440 | tf_op jit(solution)/shard_map/ppermute | solution.py:432
  115.8 8.6 %collective-permute-start.24 = (bf16[128,1024]{1,0:T(8,128)(2,1)S(1)}, bf16[128,1024]{1,0:T(8,128)(2,1)S(1)}, u32[]{:S(2)}, u32[]{:S(2)}) collective-permute-start(bf16[128,1024]{1,0:T(8,128)(2,1)S(1)} %shard_map.95), channel_id=1, source_target_pairs={{0,4},{4,0},{8,12},{12,8},{16,20},{20,16},{24,28},{28,24},{1,5},{5... | collective-permute-start | bytes 786440 | tf_op jit(solution)/shard_map/ppermute | solution.py:442
  122.6 5.0 %collective-permute-start.23 = (bf16[128,512]{1,0:T(8,128)(2,1)S(1)}, bf16[128,512]{1,0:T(8,128)(2,1)S(1)}, u32[]{:S(2)}, u32[]{:S(2)}) collective-permute-start(bf16[128,512]{1,0:T(8,128)(2,1)S(1)} %get-tuple-element.69), channel_id=1, source_target_pairs={{0,4},{4,0},{8,12},{12,8},{16,20},{20,16},{24,28},{28,24},{1,5},{5... | collective-permute-start | bytes 393224 | tf_op jit(solution)/shard_map/ppermute | solution.py:442

commit v16 on v14

--- a/solution.py
+++ b/solution.py
@@ -104,7 +104,7 @@
     )[0]
 
 
-def state_prefix(key_input, value_input, n_seq, place):
+def state_prefix(key_input, value_input, n_seq, place, beside):
     inner = n_seq // LINE
     i = place % inner
     heads = key_input.shape[1] // DH
@@ -131,7 +131,7 @@
     later = (place // inner) % 2 == 1
     masks = [mask for target in targets for mask in [later] + [owner < target for owner in members]]
     dtypes = [jnp.float32] + [jnp.bfloat16] * (len(targets) - 1)
-    befores = combine([from_half], dtypes, [from_pair] + values, masks)
+    befores = combine([hold(from_half, *beside)], dtypes, [from_pair] + values, masks)
     terms = [befores[0]]
     for turn in range(1, len(targets)):
         terms.append(lax.ppermute(befores[turn], "seq", turn_pairs(n_seq, turn)))
@@ -382,12 +382,12 @@
     def along(value, hops):
         return lax.ppermute(value, "seq", line_pairs(n_seq, hops))
 
-    terms, stepped = state_prefix(key_input, value_input, n_seq, place)
     some = heads // 2
     inners = [
         causal_part(queries, key_input, value_input, 0, some),
         causal_part(queries, key_input, value_input, some, heads - some),
     ]
+    terms, stepped = state_prefix(key_input, value_input, n_seq, place, inners)
 
     own_columns = hold(out_weight, stepped)
     w_halves = along(own_columns, SWAP_HALVES)

time: 117 us -> 119 us (1.017)
  local copies, waits for them, and re-layouts: 3.59 us -> 12.8 us
  Pallas kernels: 21.2 us -> 18.7 us
  starting transfers between devices: 34 us -> 31.7 us
  waiting for transfers between devices: 57 us -> 54.9 us
    unnamed x20 -> x46, local copies, waits for them, and re-layouts: 3.39 us -> 12.6 us
    pallas_call x24, Pallas kernels: 19.8 us -> 17.3 us  [local_call(): pl.pallas_call(kernel, in_specs=[pl.BlockSpec(memory_space=pltpu.SMEM)] +...]
    ppermute x4, starting transfers between devices: 8.28 us -> 6.09 us  [along(): return lax.ppermute(value, 'seq', line_pairs(n_seq, hops))]
    ppermute x1, waiting for transfers between devices: 2.06 us -> 0.01 us  [state_prefix(): from_half = lax.ppermute(second, 'seq', line_pairs(n_seq, [(0, 2), (1, 3)]))]
    ppermute x3, waiting for transfers between devices: 7.32 us -> 5.52 us  [summed(): piece = lax.ppermute(piece, 'seq', turn_pairs(n_seq, -turn))]
    ppermute x2, waiting for transfers between devices: 1.22 us -> 2.45 us  [shards(): lax.ppermute(squares[half:], 'head', flip_pairs(n_head, bit))]
  transfers between devices with their start and end apart: 25 -> 25, of which waited for: 17 -> 15; matrix products, arithmetic and copies ran while one was open for 0% -> 0% of each run, Pallas kernels for 14% -> 11%
where the time goes in v16:
time: 119 us
  waiting for transfers between devices  54.9 us (46%)
  starting transfers between devices  31.7 us (27%)
  Pallas kernels  18.7 us (16%)
  local copies, waits for them, and re-layouts  12.8 us (11%)
    pallas_call x24, Pallas kernels, local_call(): pl.pallas_call(kernel, in_specs=[pl.BlockSpec(memory_space=pltpu.SMEM)] +...  17.3 us
    ppermute x10, waiting for transfers between devices, summed(): got = lax.ppermute(sent, 'head', flip_pairs(n_head, bit))  15.8 us
    unnamed x46, local copies, waits for them, and re-layouts  12.6 us
    ppermute x4, waiting for transfers between devices, along(): return lax.ppermute(value, 'seq', line_pairs(n_seq, hops))  10.9 us
    ppermute x10, starting transfers between devices, summed(): got = lax.ppermute(sent, 'head', flip_pairs(n_head, bit))  8.44 us
    ppermute x1, waiting for transfers between devices, shards(): lax.ppermute(kept_rows, 'seq', pairs)  8.13 us
    ppermute x4, starting transfers between devices, along(): return lax.ppermute(value, 'seq', line_pairs(n_seq, hops))  6.09 us
    ppermute x1, waiting for transfers between devices, shards(): lax.ppermute(sent_rows, 'seq', pairs)  6.02 us
  transfers between devices with their start and end apart: 25, of which 15 were waited for; matrix products, arithmetic and copies ran while one was open for 0% of the time, Pallas kernels for 11%

profile of v16, /device:TPU:0, one launch (start us, length us, event | category | flops | bytes accessed | tf_op | source)
XLA Modules:
  0.0 118.6 jit_solution(11526491661761423228)
XLA Ops:
  0.0 1.2 %copy-done = bf16[512,1024]{1,0:T(8,128)(2,1)S(1)} copy-done((bf16[512,1024]{1,0:T(8,128)(2,1)S(1)}, bf16[512,1024]{1,0:T(8,128)(2,1)}, u32[]{:S(2)}) %copy-start) | copy-done | bytes 1048600
  1.2 1.2 %copy-done.2 = bf16[512,1024]{1,0:T(8,128)(2,1)S(1)} copy-done((bf16[512,1024]{1,0:T(8,128)(2,1)S(1)}, bf16[512,1024]{1,0:T(8,128)(2,1)}, u32[]{:S(2)}) %copy-start.2) | copy-done | bytes 1048600
  2.5 0.5 shard_map.74
  2.9 3.0 %collective-permute-start = (bf16[4,128,128]{2,1,0:T(8,128)(2,1)S(1)}, bf16[4,128,128]{2,1,0:T(8,128)(2,1)S(1)}, u32[]{:S(2)}, u32[]{:S(2)}) collective-permute-start(bf16[4,128,128]{2,1,0:T(8,128)(2,1)S(1)} %shard_map.74), channel_id=1, source_target_pairs={{0,4},{4,0},{8,12},{12,8},{16,20},{20,16},{24,28},{28,24},{1,5},{5... | collective-permute-start | bytes 393224 | tf_op jit(solution)/shard_map/ppermute | solution.py:124
  6.0 0.5 shard_map.73.refs_0_.refs_2_
  6.4 3.0 %collective-permute-done.refs_1_.refs_3_ = bf16[4,128,128]{2,1,0:T(8,128)(2,1)S(1)} collective-permute-done((bf16[4,128,128]{2,1,0:T(8,128)(2,1)S(1)}, bf16[4,128,128]{2,1,0:T(8,128)(2,1)S(1)}, u32[]{:S(2)}, u32[]{:S(2)}) %collective-permute-start) | collective-permute-done | bytes 131104 | tf_op jit(solution)/shard_map/ppermute | solution.py:124
  9.5 1.9 %collective-permute-start.1 = (bf16[4,128,128]{2,1,0:T(8,128)(2,1)S(1)}, bf16[4,128,128]{2,1,0:T(8,128)(2,1)S(1)}, u32[]{:S(2)}, u32[]{:S(2)}) collective-permute-start(bf16[4,128,128]{2,1,0:T(8,128)(2,1)S(1)} %shard_map.75), channel_id=1, source_target_pairs={{0,8},{4,12},{8,0},{12,4},{16,24},{20,28},{24,16},{28,20},{1,9},{5... | collective-permute-start | bytes 393224 | tf_op jit(solution)/shard_map/ppermute | solution.py:127
  11.4 3.1 %collective-permute-done.1.refs_2_.refs_1_ = bf16[4,128,128]{2,1,0:T(8,128)(2,1)S(1)} collective-permute-done((bf16[4,128,128]{2,1,0:T(8,128)(2,1)S(1)}, bf16[4,128,128]{2,1,0:T(8,128)(2,1)S(1)}, u32[]{:S(2)}, u32[]{:S(2)}) %collective-permute-start.1) | collective-permute-done | bytes 131104 | tf_op jit(solution)/shard_map/ppermute | solution.py:127
  14.5 0.7 shard_map.76
  15.2 5.4 %collective-permute-start.2 = (bf16[4,128,128]{2,1,0:T(8,128)(2,1)}, bf16[4,128,128]{2,1,0:T(8,128)(2,1)}, u32[]{:S(2)}, u32[]{:S(2)}) collective-permute-start(bf16[4,128,128]{2,1,0:T(8,128)(2,1)} %shard_map.76), channel_id=1, source_target_pairs={{0,16},{4,20},{8,24},{12,28},{1,17},{5,21},{9,25},{13,29},{2,18},{... | collective-permute-start | bytes 393224 | tf_op jit(solution)/shard_map/ppermute | solution.py:129
  20.7 1.1 shard_map.77.refs_2_
  21.8 1.0 copy-done.6
  22.8 1.1 shard_map.78.refs_3_
  23.9 1.0 copy-done.8
  24.9 1.1 shard_map.79
  26.0 0.7 copy-done.18
  26.7 1.5 %collective-permute-start.3 = (bf16[4,128,128]{2,1,0:T(8,128)(2,1)S(1)}, bf16[4,128,128]{2,1,0:T(8,128)(2,1)S(1)}, u32[]{:S(2)}, u32[]{:S(2)}) collective-permute-start(bf16[4,128,128]{2,1,0:T(8,128)(2,1)S(1)} %get-tuple-element.41), channel_id=1, source_target_pairs={{0,4},{4,0},{8,12},{12,8},{16,20},{20,16},{24,28},{28,24},{1,5},{5... | collective-permute-start | bytes 393224 | tf_op jit(solution)/shard_map/ppermute | solution.py:137
  28.2 1.3 %collective-permute-start.9 = (bf16[1024,512]{1,0:T(8,128)(2,1)}, bf16[1024,512]{1,0:T(8,128)(2,1)}, u32[]{:S(2)}, u32[]{:S(2)}) collective-permute-start(bf16[1024,512]{1,0:T(8,128)(2,1)} %refs_2_.3), channel_id=1, source_target_pairs={{0,16},{4,20},{8,24},{12,28},{16,0},{20,4},{24,8},{28,12},{1,17},{... | collective-permute-start | bytes 3145736 | tf_op jit(solution)/shard_map/ppermute | solution.py:383
  29.6 2.8 %collective-permute-start.8 = (bf16[1024,512]{1,0:T(8,128)(2,1)}, bf16[1024,512]{1,0:T(8,128)(2,1)}, u32[]{:S(2)}, u32[]{:S(2)}) collective-permute-start(bf16[1024,512]{1,0:T(8,128)(2,1)} %refs_2_.3), channel_id=1, source_target_pairs={{0,8},{4,12},{8,0},{12,4},{16,24},{20,28},{24,16},{28,20},{1,9},{5... | collective-permute-start | bytes 3145736 | tf_op jit(solution)/shard_map/ppermute | solution.py:383
  32.4 1.2 %copy-done.7 = f32[512,512]{1,0:T(8,128)S(1)} copy-done((f32[512,512]{1,0:T(8,128)S(1)}, f32[512,512]{1,0:T(8,128)}, u32[]{:S(2)}) %copy-start.7) | copy-done | bytes 1048600
  33.6 1.2 %copy-done.9 = f32[512,512]{1,0:T(8,128)S(1)} copy-done((f32[512,512]{1,0:T(8,128)S(1)}, f32[512,512]{1,0:T(8,128)}, u32[]{:S(2)}) %copy-start.9) | copy-done | bytes 1048600
  34.8 1.2 %copy-done.10 = bf16[512,1024]{1,0:T(8,128)(2,1)S(1)} copy-done((bf16[512,1024]{1,0:T(8,128)(2,1)S(1)}, bf16[512,1024]{1,0:T(8,128)(2,1)}, u32[]{:S(2)}) %copy-start.10) | copy-done | bytes 1048600
  36.0 1.0 copy-done.15
  37.1 0.9 copy-done.19
  38.0 1.7 %shard_map.80 = (bf16[256,1024]{1,0:T(8,128)(2,1)S(1)}, bf16[256,1024]{1,0:T(8,128)(2,1)S(1)}, f32[4,128]{1,0:T(4,128)S(1)}) custom-call(s32[2]{0:T(128)S(1)} %pad_add_fusion.1.place_ref, bf16[512,1024]{1,0:T(8,128)(2,1)S(1)} %copy-done.4, bf16[512,1024]{1,0:T(8,128)(2,1)S(1)} %copy-done.10, f32[32,1,128]{2,1,0:T(1,128)S(1)} %bitcast.17, ...), custom_call_target="tpu_custom_call" | custom-call | flops 268435456 | bytes 6178816 | tf_op jit(solution)/shard_map/pallas_call | solution.py:49
  39.7 0.9 collective-permute-start.6
  40.6 1.2 %collective-permute-start.7 = (bf16[256,1024]{1,0:T(8,128)(2,1)S(1)}, bf16[256,1024]{1,0:T(8,128)(2,1)S(1)}, u32[]{:S(2)}, u32[]{:S(2)}) collective-permute-start(bf16[256,1024]{1,0:T(8,128)(2,1)S(1)} %get-tuple-element.44.refs_1_), channel_id=1, source_target_pairs={{0,4},{4,0},{8,12},{12,8},{16,20},{20,16},{24,28},{28,24},{1,5},{5... | collective-permute-start | bytes 1572872 | tf_op jit(solution)/shard_map/ppermute | solution.py:405
  41.8 1.1 collective-permute-done.4
  42.9 1.5 %collective-permute-start.5 = (f32[1,128]{1,0:T(1,128)S(1)}, f32[1,128]{1,0:T(1,128)S(1)}, u32[]{:S(2)}, u32[]{:S(2)}) collective-permute-start(f32[1,128]{1,0:T(1,128)S(1)} %slice.15), channel_id=1, source_target_pairs={{0,2},{1,3},{2,0},{3,1},{4,6},{5,7},{6,4},{7,5},{8,10},{9,11},{10,... | collective-permute-start | bytes 1544 | tf_op jit(solution)/shard_map/ppermute | solution.py:410
  44.5 0.7 shard_map.81
  45.2 1.3 %collective-permute-done.5 = f32[1,128]{1,0:T(1,128)S(1)} collective-permute-done((f32[1,128]{1,0:T(1,128)S(1)}, f32[1,128]{1,0:T(1,128)S(1)}, u32[]{:S(2)}, u32[]{:S(2)}) %collective-permute-start.5) | collective-permute-done | bytes 544 | tf_op jit(solution)/shard_map/ppermute | solution.py:410
  46.5 8.1 %collective-permute-done.6.refs_0_.refs_2_ = bf16[256,1024]{1,0:T(8,128)(2,1)S(1)} collective-permute-done((bf16[256,1024]{1,0:T(8,128)(2,1)S(1)}, bf16[256,1024]{1,0:T(8,128)(2,1)S(1)}, u32[]{:S(2)}, u32[]{:S(2)}) %collective-permute-start.6) | collective-permute-done | bytes 524320 | tf_op jit(solution)/shard_map/ppermute | solution.py:405
  54.6 6.0 %collective-permute-done.7.refs_1_.refs_3_ = bf16[256,1024]{1,0:T(8,128)(2,1)S(1)} collective-permute-done((bf16[256,1024]{1,0:T(8,128)(2,1)S(1)}, bf16[256,1024]{1,0:T(8,128)(2,1)S(1)}, u32[]{:S(2)}, u32[]{:S(2)}) %collective-permute-start.7) | collective-permute-done | bytes 524320 | tf_op jit(solution)/shard_map/ppermute | solution.py:405
  60.6 0.7 shard_map.82
  61.5 1.6 %collective-permute-start.11 = (bf16[128,512]{1,0:T(8,128)(2,1)S(1)}, bf16[128,512]{1,0:T(8,128)(2,1)S(1)}, u32[]{:S(2)}, u32[]{:S(2)}) collective-permute-start(bf16[128,512]{1,0:T(8,128)(2,1)S(1)} %get-tuple-element.54), channel_id=1, source_target_pairs={{0,2},{1,3},{2,0},{3,1},{4,6},{5,7},{6,4},{7,5},{8,10},{9,11},{10,... | collective-permute-start | bytes 393224 | tf_op jit(solution)/shard_map/ppermute | solution.py:432
  63.1 1.5 %collective-permute-start.13 = (bf16[128,512]{1,0:T(8,128)(2,1)S(1)}, bf16[128,512]{1,0:T(8,128)(2,1)S(1)}, u32[]{:S(2)}, u32[]{:S(2)}) collective-permute-start(bf16[128,512]{1,0:T(8,128)(2,1)S(1)} %get-tuple-element.56), channel_id=1, source_target_pairs={{0,2},{1,3},{2,0},{3,1},{4,6},{5,7},{6,4},{7,5},{8,10},{9,11},{10,... | collective-permute-start | bytes 393224 | tf_op jit(solution)/shard_map/ppermute | solution.py:432
  64.6 0.7 collective-permute-start.19
  65.3 2.5 %collective-permute-done.11.got_ref = bf16[128,512]{1,0:T(8,128)(2,1)S(1)} collective-permute-done((bf16[128,512]{1,0:T(8,128)(2,1)S(1)}, bf16[128,512]{1,0:T(8,128)(2,1)S(1)}, u32[]{:S(2)}, u32[]{:S(2)}) %collective-permute-start.11) | collective-permute-done | bytes 131104 | tf_op jit(solution)/shard_map/ppermute | solution.py:432
  67.9 7.5 %collective-permute-done.9.refs_3_ = bf16[1024,512]{1,0:T(8,128)(2,1)} collective-permute-done((bf16[1024,512]{1,0:T(8,128)(2,1)}, bf16[1024,512]{1,0:T(8,128)(2,1)}, u32[]{:S(2)}, u32[]{:S(2)}) %collective-permute-start.9) | collective-permute-done | bytes 1048608 | tf_op jit(solution)/shard_map/ppermute | solution.py:383
  75.4 1.3 %collective-permute-start.20 = (bf16[1024,512]{1,0:T(8,128)(2,1)}, bf16[1024,512]{1,0:T(8,128)(2,1)S(1)}, u32[]{:S(2)}, u32[]{:S(2)}) collective-permute-start(bf16[1024,512]{1,0:T(8,128)(2,1)} %collective-permute-done.9.refs_3_), channel_id=1, source_target_pairs={{8,0},{12,4},{16,24},{20,28},{9,1},{13,5},{17,25},{21,29},{10,2},{... | collective-permute-start | bytes 3145736 | tf_op jit(solution)/shard_map/ppermute | solution.py:383
  76.7 2.8 %shard_map.83 = (bf16[256,1024]{1,0:T(8,128)(2,1)S(1)}, f32[256,1024]{1,0:T(8,128)S(1)}) custom-call(s32[1]{0:T(128)} %bitcast.10.flag_ref, bf16[256,1024]{1,0:T(8,128)(2,1)S(1)} %get-tuple-element.43.refs_0_, bf16[256,1024]{1,0:T(8,128)(2,1)S(1)} %get-tuple-element.44.refs_1_, bf16[1024,512]{1,0:T(8,128)(2,1)} %collective-permute-done.8.refs_2_, ...), custom_call_target="tpu_custom_call" | custom-call | flops 1073741824 | bytes 4718592 | tf_op jit(solution)/shard_map/pallas_call | solution.py:49
  79.5 2.8 %shard_map.84 = (bf16[256,1024]{1,0:T(8,128)(2,1)S(1)}, f32[256,1024]{1,0:T(8,128)S(1)}) custom-call(s32[1]{0:T(128)} %bitcast.10.flag_ref, bf16[256,1024]{1,0:T(8,128)(2,1)S(1)} %collective-permute-done.6.refs_0_.refs_2_, bf16[256,1024]{1,0:T(8,128)(2,1)S(1)} %collective-permute-done.7.refs_1_.refs_3_, bf16[1024,512]{1,0:T(8,128)(2,1)} %collective-permute-done.8.refs_2_, ...), custom_call_target="tpu_custom_call" | custom-call | flops 1073741824 | bytes 4718592 | tf_op jit(solution)/shard_map/pallas_call | solution.py:49
  82.3 0.6 collective-permute-start.16
  83.0 1.6 %collective-permute-start.15 = (bf16[128,1024]{1,0:T(8,128)(2,1)S(1)}, bf16[128,1024]{1,0:T(8,128)(2,1)S(1)}, u32[]{:S(2)}, u32[]{:S(2)}) collective-permute-start(bf16[128,1024]{1,0:T(8,128)(2,1)S(1)} %get-tuple-element.58), channel_id=1, source_target_pairs={{0,2},{1,3},{2,0},{3,1},{4,6},{5,7},{6,4},{7,5},{8,10},{9,11},{10,... | collective-permute-start | bytes 786440 | tf_op jit(solution)/shard_map/ppermute | solution.py:432
  84.6 0.1 shard_map.88
  84.7 1.4 %collective-permute-start.17 = (bf16[128,1024]{1,0:T(8,128)(2,1)S(1)}, bf16[128,1024]{1,0:T(8,128)(2,1)S(1)}, u32[]{:S(2)}, u32[]{:S(2)}) collective-permute-start(bf16[128,1024]{1,0:T(8,128)(2,1)S(1)} %get-tuple-element.60), channel_id=1, source_target_pairs={{0,2},{1,3},{2,0},{3,1},{4,6},{5,7},{6,4},{7,5},{8,10},{9,11},{10,... | collective-permute-start | bytes 786440 | tf_op jit(solution)/shard_map/ppermute | solution.py:432
  86.2 0.6 collective-permute-start.18
  86.8 4.9 %collective-permute-done.18.refs_1_ = bf16[128,512]{1,0:T(8,128)(2,1)S(1)} collective-permute-done((bf16[128,512]{1,0:T(8,128)(2,1)S(1)}, bf16[128,512]{1,0:T(8,128)(2,1)S(1)}, u32[]{:S(2)}, u32[]{:S(2)}) %collective-permute-start.18) | collective-permute-done | bytes 131104 | tf_op jit(solution)/shard_map/ppermute | solution.py:441
  91.7 0.5 collective-permute-done.15.got_ref
  92.2 4.7 %collective-permute-done.17.got_ref = bf16[128,1024]{1,0:T(8,128)(2,1)S(1)} collective-permute-done((bf16[128,1024]{1,0:T(8,128)(2,1)S(1)}, bf16[128,1024]{1,0:T(8,128)(2,1)S(1)}, u32[]{:S(2)}, u32[]{:S(2)}) %collective-permute-start.17) | collective-permute-done | bytes 262176 | tf_op jit(solution)/shard_map/ppermute | solution.py:432
  96.9 3.4 %collective-permute-done.20.refs_5_ = bf16[1024,512]{1,0:T(8,128)(2,1)S(1)} collective-permute-done((bf16[1024,512]{1,0:T(8,128)(2,1)}, bf16[1024,512]{1,0:T(8,128)(2,1)S(1)}, u32[]{:S(2)}, u32[]{:S(2)}) %collective-permute-start.20) | collective-permute-done | bytes 1048608 | tf_op jit(solution)/shard_map/ppermute | solution.py:383
  100.3 1.3 %shard_map.90 = (bf16[256,1024]{1,0:T(8,128)(2,1)S(1)}, f32[256,1024]{1,0:T(8,128)S(1)}) custom-call(s32[1]{0:T(128)} %bitcast.10.flag_ref, bf16[256,1024]{1,0:T(8,128)(2,1)S(1)} %get-tuple-element.43.refs_0_, bf16[256,1024]{1,0:T(8,128)(2,1)S(1)} %get-tuple-element.44.refs_1_, bf16[256,1024]{1,0:T(8,128)(2,1)S(1)} %collective-permute-done.6.refs_0_.refs_2_, ...), custom_call_target="tpu_custom_call" | custom-call | flops 1073741824 | bytes 5767168 | tf_op jit(solution)/shard_map/pallas_call | solution.py:49
  101.7 1.9 %collective-permute-done.21.got_ref = bf16[256,1024]{1,0:T(8,128)(2,1)S(1)} collective-permute-done((bf16[256,1024]{1,0:T(8,128)(2,1)S(1)}, bf16[256,1024]{1,0:T(8,128)(2,1)S(1)}, u32[]{:S(2)}, u32[]{:S(2)}) %collective-permute-start.21) | collective-permute-done | bytes 524320 | tf_op jit(solution)/shard_map/ppermute | solution.py:432
  103.6 0.1 shard_map.91
  103.7 1.6 %collective-permute-start.22 = (bf16[128,1024]{1,0:T(8,128)(2,1)S(1)}, bf16[128,1024]{1,0:T(8,128)(2,1)S(1)}, u32[]{:S(2)}, u32[]{:S(2)}) collective-permute-start(bf16[128,1024]{1,0:T(8,128)(2,1)S(1)} %get-tuple-element.67), channel_id=1, source_target_pairs={{0,2},{1,3},{2,0},{3,1},{4,6},{5,7},{6,4},{7,5},{8,10},{9,11},{10,... | collective-permute-start | bytes 786440 | tf_op jit(solution)/shard_map/ppermute | solution.py:432
  105.3 0.6 collective-permute-start.24
  105.9 6.2 %collective-permute-done.22.got_ref = bf16[128,1024]{1,0:T(8,128)(2,1)S(1)} collective-permute-done((bf16[128,1024]{1,0:T(8,128)(2,1)S(1)}, bf16[128,1024]{1,0:T(8,128)(2,1)S(1)}, u32[]{:S(2)}, u32[]{:S(2)}) %collective-permute-start.22) | collective-permute-done | bytes 262176 | tf_op jit(solution)/shard_map/ppermute | solution.py:432
  112.2 0.6 collective-permute-start.23
  112.9 0.2 copy-done.12
  113.1 0.8 copy-done.17
  114.0 0.8 copy-done.21
  114.8 1.8 %shard_map.96.refs_2_ = bf16[128,4096]{1,0:T(8,128)(2,1)} custom-call(s32[6]{0:T(128)S(1)} %stack.92.starts_ref, f32[1,128]{1,0:T(1,128)S(1)} %slice_add_fusion.1.squares_ref, bf16[128,512]{1,0:T(8,128)(2,1)S(1)} %shard_map.93.refs_0_, bf16[128,512]{1,0:T(8,128)(2,1)S(1)} %copy-done.21, bf16[128,1024]{1,0:T(8,128)(2,1)S(1)} %shard_map.94.refs_2_, ...), custom_call_target="tpu_custom_call" | custom-call | bytes 1835520 | tf_op jit(solution)/shard_map/pallas_call | solution.py:49
  116.6 0.6 collective-permute-done.23.refs_1_
  117.2 1.4 %shard_map.97 = bf16[128,4096]{1,0:T(8,128)(2,1)} custom-call(s32[2]{0:T(128)S(1)} %pad_add_fusion.starts_ref, f32[1,128]{1,0:T(1,128)S(1)} %slice_add_fusion.1.squares_ref, bf16[128,512]{1,0:T(8,128)(2,1)S(1)} %get-tuple-element.68.refs_0_, bf16[128,512]{1,0:T(8,128)(2,1)S(1)} %collective-permute-done.23.refs_1_, ...), custom_call_target="tpu_custom_call", output_to_operand_aliasing={{}: (4, {})} | custom-call | bytes 524288 | tf_op jit(solution)/shard_map/pallas_call | solution.py:352
  (66 shorter events, 1.1 us)
Async XLA Ops:
  0.0 1.2 %copy-start = (bf16[512,1024]{1,0:T(8,128)(2,1)S(1)}, bf16[512,1024]{1,0:T(8,128)(2,1)}, u32[]{:S(2)}) copy-start(bf16[512,1024]{1,0:T(8,128)(2,1)} %k_ref.7) | copy-start | bytes 3145732
  1.2 1.2 %copy-start.2 = (bf16[512,1024]{1,0:T(8,128)(2,1)S(1)}, bf16[512,1024]{1,0:T(8,128)(2,1)}, u32[]{:S(2)}) copy-start(bf16[512,1024]{1,0:T(8,128)(2,1)} %v_ref.7) | copy-start | bytes 3145732
  2.5 3.5 %copy-start.1 = (bf16[512,1024]{1,0:T(8,128)(2,1)S(1)}, bf16[512,1024]{1,0:T(8,128)(2,1)}, u32[]{:S(2)}) copy-start(bf16[512,1024]{1,0:T(8,128)(2,1)} %k_ref.7) | copy-start | bytes 3145732
  2.9 6.5 %collective-permute-start = (bf16[4,128,128]{2,1,0:T(8,128)(2,1)S(1)}, bf16[4,128,128]{2,1,0:T(8,128)(2,1)S(1)}, u32[]{:S(2)}, u32[]{:S(2)}) collective-permute-start(bf16[4,128,128]{2,1,0:T(8,128)(2,1)S(1)} %shard_map.74), channel_id=1, source_target_pairs={{0,4},{4,0},{8,12},{12,8},{16,20},{20,16},{24,28},{28,24},{1,5},{5... | collective-permute-start | bytes 393224 | tf_op jit(solution)/shard_map/ppermute | solution.py:124
  5.9 14.8 %copy-start.4 = (bf16[512,1024]{1,0:T(8,128)(2,1)S(1)}, bf16[512,1024]{1,0:T(8,128)(2,1)}, u32[]{:S(2)}) copy-start(bf16[512,1024]{1,0:T(8,128)(2,1)} %q_ref.5) | copy-start | bytes 3145732
  6.4 14.3 %copy-start.3 = (bf16[512,1024]{1,0:T(8,128)(2,1)S(1)}, bf16[512,1024]{1,0:T(8,128)(2,1)}, u32[]{:S(2)}) copy-start(bf16[512,1024]{1,0:T(8,128)(2,1)} %v_ref.7) | copy-start | bytes 3145732
  9.5 5.0 %collective-permute-start.1 = (bf16[4,128,128]{2,1,0:T(8,128)(2,1)S(1)}, bf16[4,128,128]{2,1,0:T(8,128)(2,1)S(1)}, u32[]{:S(2)}, u32[]{:S(2)}) collective-permute-start(bf16[4,128,128]{2,1,0:T(8,128)(2,1)S(1)} %shard_map.75), channel_id=1, source_target_pairs={{0,8},{4,12},{8,0},{12,4},{16,24},{20,28},{24,16},{28,20},{1,9},{5... | collective-permute-start | bytes 393224 | tf_op jit(solution)/shard_map/ppermute | solution.py:127
  14.5 0.7 copy-start.13
  15.2 9.7 %collective-permute-start.2 = (bf16[4,128,128]{2,1,0:T(8,128)(2,1)}, bf16[4,128,128]{2,1,0:T(8,128)(2,1)}, u32[]{:S(2)}, u32[]{:S(2)}) collective-permute-start(bf16[4,128,128]{2,1,0:T(8,128)(2,1)} %shard_map.76), channel_id=1, source_target_pairs={{0,16},{4,20},{8,24},{12,28},{1,17},{5,21},{9,25},{13,29},{2,18},{... | collective-permute-start | bytes 393224 | tf_op jit(solution)/shard_map/ppermute | solution.py:129
  21.8 1.0 copy-start.6
  22.8 2.1 %copy-start.14 = (bf16[4,128,128]{2,1,0:T(8,128)(2,1)S(1)}, bf16[4,128,128]{2,1,0:T(8,128)(2,1)}, u32[]{:S(2)}) copy-start(bf16[4,128,128]{2,1,0:T(8,128)(2,1)} %copy-done.13) | copy-start | bytes 393220
  23.9 1.0 copy-start.8
  24.9 7.5 %copy-start.22 = (f32[4096]{0:T(1024)S(1)}, f32[4096]{0:T(1024)}, u32[]{:S(2)}) copy-start(f32[4096]{0:T(1024)} %param.12) | copy-start | bytes 49156
  26.0 0.7 copy-start.18
  26.7 5.7 %collective-permute-start.3 = (bf16[4,128,128]{2,1,0:T(8,128)(2,1)S(1)}, bf16[4,128,128]{2,1,0:T(8,128)(2,1)S(1)}, u32[]{:S(2)}, u32[]{:S(2)}) collective-permute-start(bf16[4,128,128]{2,1,0:T(8,128)(2,1)S(1)} %get-tuple-element.41), channel_id=1, source_target_pairs={{0,4},{4,0},{8,12},{12,8},{16,20},{20,16},{24,28},{28,24},{1,5},{5... | collective-permute-start | bytes 393224 | tf_op jit(solution)/shard_map/ppermute | solution.py:137
  28.2 47.2 %collective-permute-start.9 = (bf16[1024,512]{1,0:T(8,128)(2,1)}, bf16[1024,512]{1,0:T(8,128)(2,1)}, u32[]{:S(2)}, u32[]{:S(2)}) collective-permute-start(bf16[1024,512]{1,0:T(8,128)(2,1)} %refs_2_.3), channel_id=1, source_target_pairs={{0,16},{4,20},{8,24},{12,28},{16,0},{20,4},{24,8},{28,12},{1,17},{... | collective-permute-start | bytes 3145736 | tf_op jit(solution)/shard_map/ppermute | solution.py:383
  29.6 47.1 %collective-permute-start.8 = (bf16[1024,512]{1,0:T(8,128)(2,1)}, bf16[1024,512]{1,0:T(8,128)(2,1)}, u32[]{:S(2)}, u32[]{:S(2)}) collective-permute-start(bf16[1024,512]{1,0:T(8,128)(2,1)} %refs_2_.3), channel_id=1, source_target_pairs={{0,8},{4,12},{8,0},{12,4},{16,24},{20,28},{24,16},{28,20},{1,9},{5... | collective-permute-start | bytes 3145736 | tf_op jit(solution)/shard_map/ppermute | solution.py:383
  32.4 1.2 %copy-start.7 = (f32[512,512]{1,0:T(8,128)S(1)}, f32[512,512]{1,0:T(8,128)}, u32[]{:S(2)}) copy-start(f32[512,512]{1,0:T(8,128)} %copy-done.6) | copy-start | bytes 3145732
  33.6 1.2 %copy-start.9 = (f32[512,512]{1,0:T(8,128)S(1)}, f32[512,512]{1,0:T(8,128)}, u32[]{:S(2)}) copy-start(f32[512,512]{1,0:T(8,128)} %copy-done.8) | copy-start | bytes 3145732
  34.8 1.2 %copy-start.10 = (bf16[512,1024]{1,0:T(8,128)(2,1)S(1)}, bf16[512,1024]{1,0:T(8,128)(2,1)}, u32[]{:S(2)}) copy-start(bf16[512,1024]{1,0:T(8,128)(2,1)} %gate_ref.1) | copy-start | bytes 3145732
  36.0 1.0 copy-start.15
  37.1 0.9 copy-start.19
  38.0 6.4 %copy-start.5 = (bf16[1024,512]{1,0:T(8,128)(2,1)S(1)}, bf16[1024,512]{1,0:T(8,128)(2,1)}, u32[]{:S(2)}) copy-start(bf16[1024,512]{1,0:T(8,128)(2,1)} %refs_2_.3) | copy-start | bytes 3145732
  39.7 14.9 %collective-permute-start.6 = (bf16[256,1024]{1,0:T(8,128)(2,1)S(1)}, bf16[256,1024]{1,0:T(8,128)(2,1)S(1)}, u32[]{:S(2)}, u32[]{:S(2)}) collective-permute-start(bf16[256,1024]{1,0:T(8,128)(2,1)S(1)} %get-tuple-element.43.refs_0_), channel_id=1, source_target_pairs={{0,4},{4,0},{8,12},{12,8},{16,20},{20,16},{24,28},{28,24},{1,5},{5... | collective-permute-start | bytes 1572872 | tf_op jit(solution)/shard_map/ppermute | solution.py:405
  40.6 20.1 %collective-permute-start.7 = (bf16[256,1024]{1,0:T(8,128)(2,1)S(1)}, bf16[256,1024]{1,0:T(8,128)(2,1)S(1)}, u32[]{:S(2)}, u32[]{:S(2)}) collective-permute-start(bf16[256,1024]{1,0:T(8,128)(2,1)S(1)} %get-tuple-element.44.refs_1_), channel_id=1, source_target_pairs={{0,4},{4,0},{8,12},{12,8},{16,20},{20,16},{24,28},{28,24},{1,5},{5... | collective-permute-start | bytes 1572872 | tf_op jit(solution)/shard_map/ppermute | solution.py:405
  41.8 1.1 collective-permute-start.4
  42.9 3.5 %collective-permute-start.5 = (f32[1,128]{1,0:T(1,128)S(1)}, f32[1,128]{1,0:T(1,128)S(1)}, u32[]{:S(2)}, u32[]{:S(2)}) collective-permute-start(f32[1,128]{1,0:T(1,128)S(1)} %slice.15), channel_id=1, source_target_pairs={{0,2},{1,3},{2,0},{3,1},{4,6},{5,7},{6,4},{7,5},{8,10},{9,11},{10,... | collective-permute-start | bytes 1544 | tf_op jit(solution)/shard_map/ppermute | solution.py:410
  46.5 14.9 %collective-permute-start.10 = (bf16[256,512]{1,0:T(8,128)(2,1)S(1)}, bf16[256,512]{1,0:T(8,128)(2,1)S(1)}, u32[]{:S(2)}, u32[]{:S(2)}) collective-permute-start(bf16[256,512]{1,0:T(8,128)(2,1)S(1)} %get-tuple-element.45), channel_id=1, source_target_pairs={{0,1},{1,0},{2,3},{3,2},{4,5},{5,4},{6,7},{7,6},{8,9},{9,8},{10,11... | collective-permute-start | bytes 786440 | tf_op jit(solution)/shard_map/ppermute | solution.py:432
  61.4 1.7 %collective-permute-start.12 = (bf16[256,512]{1,0:T(8,128)(2,1)S(1)}, bf16[256,512]{1,0:T(8,128)(2,1)S(1)}, u32[]{:S(2)}, u32[]{:S(2)}) collective-permute-start(bf16[256,512]{1,0:T(8,128)(2,1)S(1)} %get-tuple-element.47), channel_id=1, source_target_pairs={{0,1},{1,0},{2,3},{3,2},{4,5},{5,4},{6,7},{7,6},{8,9},{9,8},{10,11... | collective-permute-start | bytes 786440 | tf_op jit(solution)/shard_map/ppermute | solution.py:432
  61.5 6.4 %collective-permute-start.11 = (bf16[128,512]{1,0:T(8,128)(2,1)S(1)}, bf16[128,512]{1,0:T(8,128)(2,1)S(1)}, u32[]{:S(2)}, u32[]{:S(2)}) collective-permute-start(bf16[128,512]{1,0:T(8,128)(2,1)S(1)} %get-tuple-element.54), channel_id=1, source_target_pairs={{0,2},{1,3},{2,0},{3,1},{4,6},{5,7},{6,4},{7,5},{8,10},{9,11},{10,... | collective-permute-start | bytes 393224 | tf_op jit(solution)/shard_map/ppermute | solution.py:432
  63.1 12.2 %collective-permute-start.13 = (bf16[128,512]{1,0:T(8,128)(2,1)S(1)}, bf16[128,512]{1,0:T(8,128)(2,1)S(1)}, u32[]{:S(2)}, u32[]{:S(2)}) collective-permute-start(bf16[128,512]{1,0:T(8,128)(2,1)S(1)} %get-tuple-element.56), channel_id=1, source_target_pairs={{0,2},{1,3},{2,0},{3,1},{4,6},{5,7},{6,4},{7,5},{8,10},{9,11},{10,... | collective-permute-start | bytes 393224 | tf_op jit(solution)/shard_map/ppermute | solution.py:432
  64.6 32.3 %collective-permute-start.19 = (bf16[1024,512]{1,0:T(8,128)(2,1)S(1)}, bf16[1024,512]{1,0:T(8,128)(2,1)S(1)}, u32[]{:S(2)}, u32[]{:S(2)}) collective-permute-start(bf16[1024,512]{1,0:T(8,128)(2,1)S(1)} %copy-done.5), channel_id=1, source_target_pairs={{8,16},{12,20},{16,8},{20,12},{9,17},{13,21},{17,9},{21,13},{10,18... | collective-permute-start | bytes 3145736 | tf_op jit(solution)/shard_map/ppermute | solution.py:383
  75.4 24.9 %collective-permute-start.20 = (bf16[1024,512]{1,0:T(8,128)(2,1)}, bf16[1024,512]{1,0:T(8,128)(2,1)S(1)}, u32[]{:S(2)}, u32[]{:S(2)}) collective-permute-start(bf16[1024,512]{1,0:T(8,128)(2,1)} %collective-permute-done.9.refs_3_), channel_id=1, source_target_pairs={{8,0},{12,4},{16,24},{20,28},{9,1},{13,5},{17,25},{21,29},{10,2},{... | collective-permute-start | bytes 3145736 | tf_op jit(solution)/shard_map/ppermute | solution.py:383
  79.4 3.4 %collective-permute-start.14 = (bf16[256,1024]{1,0:T(8,128)(2,1)S(1)}, bf16[256,1024]{1,0:T(8,128)(2,1)S(1)}, u32[]{:S(2)}, u32[]{:S(2)}) collective-permute-start(bf16[256,1024]{1,0:T(8,128)(2,1)S(1)} %get-tuple-element.50), channel_id=1, source_target_pairs={{0,1},{1,0},{2,3},{3,2},{4,5},{5,4},{6,7},{7,6},{8,9},{9,8},{10,11... | collective-permute-start | bytes 1572872 | tf_op jit(solution)/shard_map/ppermute | solution.py:432
  82.3 2.3 %collective-permute-start.16 = (bf16[256,1024]{1,0:T(8,128)(2,1)S(1)}, bf16[256,1024]{1,0:T(8,128)(2,1)S(1)}, u32[]{:S(2)}, u32[]{:S(2)}) collective-permute-start(bf16[256,1024]{1,0:T(8,128)(2,1)S(1)} %get-tuple-element.52), channel_id=1, source_target_pairs={{0,1},{1,0},{2,3},{3,2},{4,5},{5,4},{6,7},{7,6},{8,9},{9,8},{10,11... | collective-permute-start | bytes 1572872 | tf_op jit(solution)/shard_map/ppermute | solution.py:432
  83.0 1.7 %copy-start.11 = (f32[128,1024]{1,0:T(8,128)}, f32[128,1024]{1,0:T(8,128)S(1)}, u32[]{:S(2)}) copy-start(f32[128,1024]{1,0:T(8,128)S(1)} %get-tuple-element.71.kept_ref) | copy-start | bytes 1572868
  83.0 9.2 %collective-permute-start.15 = (bf16[128,1024]{1,0:T(8,128)(2,1)S(1)}, bf16[128,1024]{1,0:T(8,128)(2,1)S(1)}, u32[]{:S(2)}, u32[]{:S(2)}) collective-permute-start(bf16[128,1024]{1,0:T(8,128)(2,1)S(1)} %get-tuple-element.58), channel_id=1, source_target_pairs={{0,2},{1,3},{2,0},{3,1},{4,6},{5,7},{6,4},{7,5},{8,10},{9,11},{10,... | collective-permute-start | bytes 786440 | tf_op jit(solution)/shard_map/ppermute | solution.py:432
  84.7 12.2 %collective-permute-start.17 = (bf16[128,1024]{1,0:T(8,128)(2,1)S(1)}, bf16[128,1024]{1,0:T(8,128)(2,1)S(1)}, u32[]{:S(2)}, u32[]{:S(2)}) collective-permute-start(bf16[128,1024]{1,0:T(8,128)(2,1)S(1)} %get-tuple-element.60), channel_id=1, source_target_pairs={{0,2},{1,3},{2,0},{3,1},{4,6},{5,7},{6,4},{7,5},{8,10},{9,11},{10,... | collective-permute-start | bytes 786440 | tf_op jit(solution)/shard_map/ppermute | solution.py:432
  86.2 5.5 %collective-permute-start.18 = (bf16[128,512]{1,0:T(8,128)(2,1)S(1)}, bf16[128,512]{1,0:T(8,128)(2,1)S(1)}, u32[]{:S(2)}, u32[]{:S(2)}) collective-permute-start(bf16[128,512]{1,0:T(8,128)(2,1)S(1)} %shard_map.89), channel_id=1, source_target_pairs={{0,4},{4,0},{8,12},{12,8},{16,20},{20,16},{24,28},{28,24},{1,5},{5... | collective-permute-start | bytes 393224 | tf_op jit(solution)/shard_map/ppermute | solution.py:441
  91.7 9.9 %copy-start.20 = (bf16[128,512]{1,0:T(8,128)(2,1)}, bf16[128,512]{1,0:T(8,128)(2,1)S(1)}, u32[]{:S(2)}) copy-start(bf16[128,512]{1,0:T(8,128)(2,1)S(1)} %collective-permute-done.18.refs_1_) | copy-start | bytes 393220
  92.2 9.4 %copy-start.16 = (bf16[128,1024]{1,0:T(8,128)(2,1)}, bf16[128,1024]{1,0:T(8,128)(2,1)S(1)}, u32[]{:S(2)}) copy-start(bf16[128,1024]{1,0:T(8,128)(2,1)S(1)} %collective-permute-done.15.got_ref) | copy-start | bytes 786436
  101.6 2.0 %collective-permute-start.21 = (bf16[256,1024]{1,0:T(8,128)(2,1)S(1)}, bf16[256,1024]{1,0:T(8,128)(2,1)S(1)}, u32[]{:S(2)}, u32[]{:S(2)}) collective-permute-start(bf16[256,1024]{1,0:T(8,128)(2,1)S(1)} %get-tuple-element.65), channel_id=1, source_target_pairs={{0,1},{1,0},{2,3},{3,2},{4,5},{5,4},{6,7},{7,6},{8,9},{9,8},{10,11... | collective-permute-start | bytes 1572872 | tf_op jit(solution)/shard_map/ppermute | solution.py:432
  103.7 8.4 %collective-permute-start.22 = (bf16[128,1024]{1,0:T(8,128)(2,1)S(1)}, bf16[128,1024]{1,0:T(8,128)(2,1)S(1)}, u32[]{:S(2)}, u32[]{:S(2)}) collective-permute-start(bf16[128,1024]{1,0:T(8,128)(2,1)S(1)} %get-tuple-element.67), channel_id=1, source_target_pairs={{0,2},{1,3},{2,0},{3,1},{4,6},{5,7},{6,4},{7,5},{8,10},{9,11},{10,... | collective-permute-start | bytes 786440 | tf_op jit(solution)/shard_map/ppermute | solution.py:432
  105.3 8.6 %collective-permute-start.24 = (bf16[128,1024]{1,0:T(8,128)(2,1)S(1)}, bf16[128,1024]{1,0:T(8,128)(2,1)S(1)}, u32[]{:S(2)}, u32[]{:S(2)}) collective-permute-start(bf16[128,1024]{1,0:T(8,128)(2,1)S(1)} %shard_map.95), channel_id=1, source_target_pairs={{0,4},{4,0},{8,12},{12,8},{16,20},{20,16},{24,28},{28,24},{1,5},{5... | collective-permute-start | bytes 786440 | tf_op jit(solution)/shard_map/ppermute | solution.py:441
  112.1 1.0 copy-start.12
  112.2 5.0 %collective-permute-start.23 = (bf16[128,512]{1,0:T(8,128)(2,1)S(1)}, bf16[128,512]{1,0:T(8,128)(2,1)S(1)}, u32[]{:S(2)}, u32[]{:S(2)}) collective-permute-start(bf16[128,512]{1,0:T(8,128)(2,1)S(1)} %get-tuple-element.69), channel_id=1, source_target_pairs={{0,4},{4,0},{8,12},{12,8},{16,20},{20,16},{24,28},{28,24},{1,5},{5... | collective-permute-start | bytes 393224 | tf_op jit(solution)/shard_map/ppermute | solution.py:441
  112.9 1.0 copy-start.17
  113.9 0.9 copy-start.21

commit v17 on v14

--- a/solution.py
+++ b/solution.py
@@ -104,7 +104,7 @@
     )[0]
 
 
-def state_prefix(key_input, value_input, n_seq, place):
+def state_prefix(key_input, value_input, n_seq, place, ahead):
     inner = n_seq // LINE
     i = place % inner
     heads = key_input.shape[1] // DH
@@ -125,8 +125,10 @@
         members.append((i - turn) % inner)
     (first,) = combine(values, [jnp.bfloat16])
     from_pair = lax.ppermute(first, "seq", line_pairs(n_seq, SWAP_NEXT))
+    from_pair = hold(from_pair, ahead[0])
     (second,) = combine(values + [from_pair], [jnp.bfloat16])
     from_half = lax.ppermute(second, "seq", line_pairs(n_seq, [(0, 2), (1, 3)]))
+    from_half = hold(from_half, ahead[1])
     targets = [i] + [(i + turn) % inner for turn in range(1, inner)] if split else [i]
     later = (place // inner) % 2 == 1
     masks = [mask for target in targets for mask in [later] + [owner < target for owner in members]]
@@ -135,7 +137,7 @@
     terms = [befores[0]]
     for turn in range(1, len(targets)):
         terms.append(lax.ppermute(befores[turn], "seq", turn_pairs(n_seq, turn)))
-    return terms, from_half
+    return terms
 
 
 def causal_kernel(first_head, place_ref, q_ref, k_ref, v_ref, out_ref):
@@ -382,17 +384,16 @@
     def along(value, hops):
         return lax.ppermute(value, "seq", line_pairs(n_seq, hops))
 
-    terms, stepped = state_prefix(key_input, value_input, n_seq, place)
+    w_halves = along(out_weight, SWAP_HALVES)
+    w_next = along(out_weight, SWAP_NEXT)
+    terms = state_prefix(key_input, value_input, n_seq, place, (w_halves, w_next))
+    w_middle = along(hold(out_weight, *terms), SWAP_MIDDLE)
+    w_ends = along(hold(w_halves, *terms), TO_ENDS)
     some = heads // 2
     inners = [
         causal_part(queries, key_input, value_input, 0, some),
         causal_part(queries, key_input, value_input, some, heads - some),
     ]
-
-    own_columns = hold(out_weight, stepped)
-    w_halves = along(own_columns, SWAP_HALVES)
-    w_next = along(own_columns, SWAP_NEXT)
-    w_middle = along(own_columns, SWAP_MIDDLE)
 
     bits = n_head.bit_length() - 1
     order = [int(format(j, "b").zfill(bits)[::-1], 2) for j in range(n_head)] if bits else [0]
@@ -416,7 +417,7 @@
 
 
     owners = [z ^ block for block in range(LINE)]
-    blocks = [(out_weight,), (w_next,), (w_halves,)]
+    blocks = [(out_weight,), (w_next,), (w_halves,), (w_middle, w_ends)]
 
     def summed(parts, pins):
         weights = sorted({block for _, own in parts for block in own})
@@ -447,26 +448,15 @@
     shape = (out_rows, width * n_seq)
     in_kernel = width % DH == 0 and out_rows == DH
 
-    pieces, pins, ends = [], [], []
-
-    def group(members, some):
-        more, sent, end = summed([(turn, some) for turn in members], pins)
-        pieces.extend(more)
-        ends.append(end)
-        pins[:] = [sent, squares]
-        return [piece for piece, _ in more]
-
-    group(turns[:1], [0])
-    returned = group(turns[1:], [0]) if inner > 1 else []
-    w_ends = along(hold(w_halves, *ends), TO_ENDS)
-    blocks.append((w_middle, w_ends))
-    group(turns[:1], [1, 2])
-    if inner > 1:
-        group(turns[1:], [1, 2])
+    groups = [(turns[:1], [0, 1, 2]), (turns[:1], [3])]
+    groups += [(turns[1:], [block]) for block in range(LINE)] if inner > 1 else []
+    pieces, pins = [], []
+    for members, some in groups:
+        last, sent, _ = summed([(turn, some) for turn in members], pins)
+        pieces += last
+        pins = [sent, squares]
+    pieces = pieces[: len(pieces) - len(last)]
     filled = placed(None, pieces, squares, width, shape, total_width) if in_kernel else None
-    last, _, _ = summed(
-        [(turn, [3]) for turn in turns], [*pins, *ends, *returned]
-    )
     if in_kernel:
         return placed(filled, last, squares, width, shape, total_width)
     scale = lax.rsqrt(squares.reshape(out_rows, 1) / total_width + epsilon)

time: 117 us -> 147 us (1.26)
  the two profiles are of different devices: /device:TPU:0 before, /device:TPU:22 now
where the time goes in v17:
time: 147 us; the launch traced here: 146 us
  waiting for transfers between devices  92.5 us (63%)
  starting transfers between devices  25.5 us (17%)
  Pallas kernels  22.3 us (15%)
  local copies, waits for them, and re-layouts  5.28 us (4%)
    ppermute x1, waiting for transfers between devices, state_prefix(): from_pair = lax.ppermute(first, 'seq', line_pairs(n_seq, SWAP_NEXT))  39.9 us
    pallas_call x27, Pallas kernels, local_call(): pl.pallas_call(kernel, in_specs=[pl.BlockSpec(memory_space=pltpu.SMEM)] +...  21.5 us
    ppermute x12, waiting for transfers between devices, summed(): got = lax.ppermute(sent, 'head', flip_pairs(n_head, bit))  16.5 us
    ppermute x4, starting transfers between devices, along(): return lax.ppermute(value, 'seq', line_pairs(n_seq, hops))  10 us
    ppermute x4, waiting for transfers between devices, along(): return lax.ppermute(value, 'seq', line_pairs(n_seq, hops))  9.7 us
    ppermute x1, waiting for transfers between devices, shards(): lax.ppermute(sent_rows, 'seq', pairs)  7.5 us
    ppermute x1, waiting for transfers between devices, state_prefix(): from_half = lax.ppermute(second, 'seq', line_pairs(n_seq, [(0, 2), (1, 3)]))  6.7 us
    ppermute x12, starting transfers between devices, summed(): got = lax.ppermute(sent, 'head', flip_pairs(n_head, bit))  6.68 us
  transfers between devices with their start and end apart: 28, of which 14 were waited for; matrix products, arithmetic and copies ran while one was open for 0% of the time, Pallas kernels for 14%

profile of v17, /device:TPU:22, one launch (start us, length us, event | category | flops | bytes accessed | tf_op | source)
XLA Modules:
  0.0 146.0 jit_solution(6054630025283947897)
XLA Ops:
  0.0 0.3 collective-permute-start.2
  0.3 1.6 %collective-permute-start.4 = (bf16[1024,512]{1,0:T(8,128)(2,1)}, bf16[1024,512]{1,0:T(8,128)(2,1)}, u32[]{:S(2)}, u32[]{:S(2)}) collective-permute-start(bf16[1024,512]{1,0:T(8,128)(2,1)} %refs_2_.3), channel_id=1, source_target_pairs={{0,8},{4,12},{8,0},{12,4},{16,24},{20,28},{24,16},{28,20},{1,9},{5... | collective-permute-start | bytes 3145736 | tf_op jit(solution)/shard_map/ppermute | solution.py:385
  1.9 1.2 copy-done
  3.1 1.2 copy-done.2
  4.4 0.5 shard_map.74
  4.9 0.6 collective-permute-start
  5.5 0.1 copy-done.1
  5.6 0.5 shard_map.73.refs_0_.refs_2_
  6.1 3.8 %collective-permute-done.refs_1_.refs_3_ = bf16[4,128,128]{2,1,0:T(8,128)(2,1)S(1)} collective-permute-done((bf16[4,128,128]{2,1,0:T(8,128)(2,1)S(1)}, bf16[4,128,128]{2,1,0:T(8,128)(2,1)S(1)}, u32[]{:S(2)}, u32[]{:S(2)}) %collective-permute-start) | collective-permute-done | bytes 131104 | tf_op jit(solution)/shard_map/ppermute | solution.py:124
  9.9 0.5 collective-permute-start.1
  10.4 39.9 %collective-permute-done.1.refs_2_.refs_1_ = bf16[4,128,128]{2,1,0:T(8,128)(2,1)S(1)} collective-permute-done((bf16[4,128,128]{2,1,0:T(8,128)(2,1)S(1)}, bf16[4,128,128]{2,1,0:T(8,128)(2,1)S(1)}, u32[]{:S(2)}, u32[]{:S(2)}) %collective-permute-start.1) | collective-permute-done | bytes 131104 | tf_op jit(solution)/shard_map/ppermute | solution.py:127
  50.3 0.7 shard_map.76
  51.0 0.7 copy-done.7
  51.7 1.3 collective-permute-start.3
  53.0 0.1 stack.76
  53.2 6.7 %collective-permute-done.3.refs_0_ = bf16[4,128,128]{2,1,0:T(8,128)(2,1)} collective-permute-done((bf16[4,128,128]{2,1,0:T(8,128)(2,1)}, bf16[4,128,128]{2,1,0:T(8,128)(2,1)}, u32[]{:S(2)}, u32[]{:S(2)}) %collective-permute-start.3) | collective-permute-done | bytes 131104 | tf_op jit(solution)/shard_map/ppermute | solution.py:130
  59.9 0.9 copy-done.8
  60.8 1.1 shard_map.77
  61.9 0.7 copy-done.10
  62.6 0.5 collective-permute-start.5
  63.1 4.4 %collective-permute-done.5.refs_1_ = bf16[4,128,128]{2,1,0:T(8,128)(2,1)S(1)} collective-permute-done((bf16[4,128,128]{2,1,0:T(8,128)(2,1)S(1)}, bf16[4,128,128]{2,1,0:T(8,128)(2,1)S(1)}, u32[]{:S(2)}, u32[]{:S(2)}) %collective-permute-start.5) | collective-permute-done | bytes 131104 | tf_op jit(solution)/shard_map/ppermute | solution.py:139
  67.5 3.6 %collective-permute-start.8 = (bf16[1024,512]{1,0:T(8,128)(2,1)}, bf16[1024,512]{1,0:T(8,128)(2,1)}, u32[]{:S(2)}, u32[]{:S(2)}) collective-permute-start(bf16[1024,512]{1,0:T(8,128)(2,1)} %refs_2_.3), channel_id=1, source_target_pairs={{8,16},{12,20},{16,8},{20,12},{9,17},{13,21},{17,9},{21,13},{10,18... | collective-permute-start | bytes 3145736 | tf_op jit(solution)/shard_map/ppermute | solution.py:385
  71.1 4.5 %collective-permute-start.9 = (bf16[1024,512]{1,0:T(8,128)(2,1)}, bf16[1024,512]{1,0:T(8,128)(2,1)}, u32[]{:S(2)}, u32[]{:S(2)}) collective-permute-start(bf16[1024,512]{1,0:T(8,128)(2,1)} %collective-permute-done.2.refs_4_.refs_2_), channel_id=1, source_target_pairs={{8,0},{12,4},{16,24},{20,28},{9,1},{13,5},{17,25},{21,29},{10,2},{... | collective-permute-start | bytes 3145736 | tf_op jit(solution)/shard_map/ppermute | solution.py:385
  75.6 1.1 shard_map.78.refs_2_
  76.8 1.1 shard_map.79.refs_3_
  77.9 0.1 pad_add_fusion.place_ref
  78.0 0.1 copy-done.9
  78.2 1.7 %shard_map.80 = (bf16[256,1024]{1,0:T(8,128)(2,1)S(1)}, bf16[256,1024]{1,0:T(8,128)(2,1)S(1)}, f32[4,128]{1,0:T(4,128)S(1)}) custom-call(s32[2]{0:T(128)S(1)} %pad_add_fusion.place_ref, bf16[512,1024]{1,0:T(8,128)(2,1)S(1)} %copy-done.4, bf16[512,1024]{1,0:T(8,128)(2,1)S(1)} %copy-done.6, f32[32,1,128]{2,1,0:T(1,128)S(1)} %bitcast.17, ...), custom_call_target="tpu_custom_call" | custom-call | flops 268435456 | bytes 6178816 | tf_op jit(solution)/shard_map/pallas_call | solution.py:49
  80.0 0.6 collective-permute-start.10
  80.6 1.5 %collective-permute-start.11 = (bf16[256,1024]{1,0:T(8,128)(2,1)S(1)}, bf16[256,1024]{1,0:T(8,128)(2,1)S(1)}, u32[]{:S(2)}, u32[]{:S(2)}) collective-permute-start(bf16[256,1024]{1,0:T(8,128)(2,1)S(1)} %get-tuple-element.49.refs_1_), channel_id=1, source_target_pairs={{0,4},{4,0},{8,12},{12,8},{16,20},{20,16},{24,28},{28,24},{1,5},{5... | collective-permute-start | bytes 1572872 | tf_op jit(solution)/shard_map/ppermute | solution.py:406
  82.1 0.6 collective-permute-start.7
  82.7 3.3 %shard_map.81 = (bf16[256,1536]{1,0:T(8,128)(2,1)S(1)}, f32[256,1536]{1,0:T(8,128)S(1)}) custom-call(s32[1]{0:T(128)} %bitcast.9.flag_ref, bf16[256,1024]{1,0:T(8,128)(2,1)S(1)} %get-tuple-element.48.refs_0_, bf16[256,1024]{1,0:T(8,128)(2,1)S(1)} %get-tuple-element.49.refs_1_, bf16[1024,512]{1,0:T(8,128)(2,1)S(1)} %copy-done.5, ...), custom_call_target="tpu_custom_call" | custom-call | flops 1610612736 | bytes 6553600 | tf_op jit(solution)/shard_map/pallas_call | solution.py:49
  86.1 6.9 %collective-permute-done.8.refs_2_ = bf16[1024,512]{1,0:T(8,128)(2,1)} collective-permute-done((bf16[1024,512]{1,0:T(8,128)(2,1)}, bf16[1024,512]{1,0:T(8,128)(2,1)}, u32[]{:S(2)}, u32[]{:S(2)}) %collective-permute-start.8) | collective-permute-done | bytes 1048608 | tf_op jit(solution)/shard_map/ppermute | solution.py:385
  93.0 2.8 %collective-permute-done.9.refs_3_ = bf16[1024,512]{1,0:T(8,128)(2,1)} collective-permute-done((bf16[1024,512]{1,0:T(8,128)(2,1)}, bf16[1024,512]{1,0:T(8,128)(2,1)}, u32[]{:S(2)}, u32[]{:S(2)}) %collective-permute-start.9) | collective-permute-done | bytes 1048608 | tf_op jit(solution)/shard_map/ppermute | solution.py:385
  95.8 2.2 %shard_map.82 = (bf16[256,512]{1,0:T(8,128)(2,1)S(1)}, f32[256,512]{1,0:T(8,128)S(1)}) custom-call(s32[1]{0:T(128)} %bitcast.9.flag_ref, bf16[256,1024]{1,0:T(8,128)(2,1)S(1)} %get-tuple-element.48.refs_0_, bf16[256,1024]{1,0:T(8,128)(2,1)S(1)} %get-tuple-element.49.refs_1_, bf16[1024,512]{1,0:T(8,128)(2,1)} %collective-permute-done.8.refs_2_, ...), custom_call_target="tpu_custom_call" | custom-call | flops 536870912 | bytes 3932160 | tf_op jit(solution)/shard_map/pallas_call | solution.py:49
  98.0 7.5 %collective-permute-done.11.refs_1_ = bf16[256,1024]{1,0:T(8,128)(2,1)S(1)} collective-permute-done((bf16[256,1024]{1,0:T(8,128)(2,1)S(1)}, bf16[256,1024]{1,0:T(8,128)(2,1)S(1)}, u32[]{:S(2)}, u32[]{:S(2)}) %collective-permute-start.11) | collective-permute-done | bytes 524320 | tf_op jit(solution)/shard_map/ppermute | solution.py:406
  105.5 0.7 shard_map.83
  106.2 1.9 %shard_map.84 = (bf16[256,512]{1,0:T(8,128)(2,1)S(1)}, f32[256,512]{1,0:T(8,128)S(1)}) custom-call(s32[1]{0:T(128)} %bitcast.9.flag_ref, bf16[256,1024]{1,0:T(8,128)(2,1)S(1)} %collective-permute-done.10.refs_0_, bf16[256,1024]{1,0:T(8,128)(2,1)S(1)} %collective-permute-done.11.refs_1_, bf16[1024,512]{1,0:T(8,128)(2,1)} %collective-permute-done.4.refs_3_.refs_2_), custom_call_target="tpu_custom_call" | custom-call | flops 536870912 | bytes 2883584 | tf_op jit(solution)/shard_map/pallas_call | solution.py:49
  108.2 1.9 %shard_map.85 = (bf16[256,512]{1,0:T(8,128)(2,1)S(1)}, f32[256,512]{1,0:T(8,128)S(1)}) custom-call(s32[1]{0:T(128)} %bitcast.9.flag_ref, bf16[256,1024]{1,0:T(8,128)(2,1)S(1)} %collective-permute-done.10.refs_0_, bf16[256,1024]{1,0:T(8,128)(2,1)S(1)} %collective-permute-done.11.refs_1_, bf16[1024,512]{1,0:T(8,128)(2,1)} %collective-permute-done.2.refs_4_.refs_2_), custom_call_target="tpu_custom_call" | custom-call | flops 536870912 | bytes 2883584 | tf_op jit(solution)/shard_map/pallas_call | solution.py:49
  110.2 0.5 collective-permute-start.22
  110.7 0.1 collective-permute-start.19
  110.8 2.2 %shard_map.86 = (bf16[256,512]{1,0:T(8,128)(2,1)S(1)}, f32[256,512]{1,0:T(8,128)S(1)}) custom-call(s32[1]{0:T(128)} %bitcast.9.flag_ref, bf16[256,1024]{1,0:T(8,128)(2,1)S(1)} %collective-permute-done.10.refs_0_, bf16[256,1024]{1,0:T(8,128)(2,1)S(1)} %collective-permute-done.11.refs_1_, bf16[1024,512]{1,0:T(8,128)(2,1)} %collective-permute-done.8.refs_2_, ...), custom_call_target="tpu_custom_call" | custom-call | flops 536870912 | bytes 3932160 | tf_op jit(solution)/shard_map/pallas_call | solution.py:49
  113.0 0.5 collective-permute-start.12
  113.5 0.1 collective-permute-start.17
  113.6 0.2 shard_map.89
  113.8 0.6 collective-permute-start.16
  114.4 1.6 %collective-permute-start.26 = (bf16[128,512]{1,0:T(8,128)(2,1)S(1)}, bf16[128,512]{1,0:T(8,128)(2,1)S(1)}, u32[]{:S(2)}, u32[]{:S(2)}) collective-permute-start(bf16[128,512]{1,0:T(8,128)(2,1)S(1)} %get-tuple-element.80), channel_id=1, source_target_pairs={{0,2},{1,3},{2,0},{3,1},{4,6},{5,7},{6,4},{7,5},{8,10},{9,11},{10,... | collective-permute-start | bytes 393224 | tf_op jit(solution)/shard_map/ppermute | solution.py:433
  116.1 0.6 collective-permute-start.23
  116.7 1.6 %collective-permute-start.20 = (bf16[128,512]{1,0:T(8,128)(2,1)S(1)}, bf16[128,512]{1,0:T(8,128)(2,1)S(1)}, u32[]{:S(2)}, u32[]{:S(2)}) collective-permute-start(bf16[128,512]{1,0:T(8,128)(2,1)S(1)} %get-tuple-element.74), channel_id=1, source_target_pairs={{0,2},{1,3},{2,0},{3,1},{4,6},{5,7},{6,4},{7,5},{8,10},{9,11},{10,... | collective-permute-start | bytes 393224 | tf_op jit(solution)/shard_map/ppermute | solution.py:433
  118.3 0.6 collective-permute-start.13
  119.0 9.6 %collective-permute-done.26.got_ref = bf16[128,512]{1,0:T(8,128)(2,1)S(1)} collective-permute-done((bf16[128,512]{1,0:T(8,128)(2,1)S(1)}, bf16[128,512]{1,0:T(8,128)(2,1)S(1)}, u32[]{:S(2)}, u32[]{:S(2)}) %collective-permute-start.26) | collective-permute-done | bytes 131104 | tf_op jit(solution)/shard_map/ppermute | solution.py:433
  128.6 0.5 collective-permute-start.18
  129.1 2.3 %collective-permute-done.23.got_ref = bf16[128,512]{1,0:T(8,128)(2,1)S(1)} collective-permute-done((bf16[128,512]{1,0:T(8,128)(2,1)S(1)}, bf16[128,512]{1,0:T(8,128)(2,1)S(1)}, u32[]{:S(2)}, u32[]{:S(2)}) %collective-permute-start.23) | collective-permute-done | bytes 131104 | tf_op jit(solution)/shard_map/ppermute | solution.py:433
  131.4 0.5 collective-permute-start.27
  132.0 2.2 %collective-permute-done.20.got_ref = bf16[128,512]{1,0:T(8,128)(2,1)S(1)} collective-permute-done((bf16[128,512]{1,0:T(8,128)(2,1)S(1)}, bf16[128,512]{1,0:T(8,128)(2,1)S(1)}, u32[]{:S(2)}, u32[]{:S(2)}) %collective-permute-start.20) | collective-permute-done | bytes 131104 | tf_op jit(solution)/shard_map/ppermute | solution.py:433
  134.2 0.5 collective-permute-start.24
  134.8 2.2 %collective-permute-done.13.got_ref = bf16[128,512]{1,0:T(8,128)(2,1)S(1)} collective-permute-done((bf16[128,512]{1,0:T(8,128)(2,1)S(1)}, bf16[128,512]{1,0:T(8,128)(2,1)S(1)}, u32[]{:S(2)}, u32[]{:S(2)}) %collective-permute-start.13) | collective-permute-done | bytes 131104 | tf_op jit(solution)/shard_map/ppermute | solution.py:433
  137.0 0.5 collective-permute-start.21
  137.6 1.6 %collective-permute-start.14 = (bf16[128,512]{1,0:T(8,128)(2,1)S(1)}, bf16[128,512]{1,0:T(8,128)(2,1)S(1)}, u32[]{:S(2)}, u32[]{:S(2)}) collective-permute-start(bf16[128,512]{1,0:T(8,128)(2,1)S(1)} %shard_map.88), channel_id=1, source_target_pairs={{0,4},{4,0},{8,12},{12,8},{16,20},{20,16},{24,28},{28,24},{1,5},{5... | collective-permute-start | bytes 393224 | tf_op jit(solution)/shard_map/ppermute | solution.py:442
  139.2 0.1 stack.88.starts_ref
  139.4 0.1 collective-permute-done.24.refs_3_
  139.5 3.8 %collective-permute-done.21.refs_2_ = bf16[128,512]{1,0:T(8,128)(2,1)S(1)} collective-permute-done((bf16[128,512]{1,0:T(8,128)(2,1)S(1)}, bf16[128,512]{1,0:T(8,128)(2,1)S(1)}, u32[]{:S(2)}, u32[]{:S(2)}) %collective-permute-start.21) | collective-permute-done | bytes 131104 | tf_op jit(solution)/shard_map/ppermute | solution.py:442
  143.4 1.8 %shard_map.99.refs_1_ = bf16[128,4096]{1,0:T(8,128)(2,1)} custom-call(s32[7]{0:T(128)S(1)} %stack.88.starts_ref, f32[1,128]{1,0:T(1,128)S(1)} %slice_add_fusion.1.squares_ref, bf16[128,1536]{1,0:T(8,128)(2,1)S(1)} %shard_map.90.refs_0_, bf16[128,512]{1,0:T(8,128)(2,1)S(1)} %shard_map.92.refs_1_, bf16[128,512]{1,0:T(8,128)(2,1)S(1)} %collective-permute-done.21.refs_2_, ...), custom_call_target="tpu_custom_call" | custom-call | bytes 1966592 | tf_op jit(solution)/shard_map/pallas_call | solution.py:49
  145.2 0.8 shard_map.100
  (54 shorter events, 0.9 us)
Async XLA Ops:
  0.0 50.3 %collective-permute-start.2 = (bf16[1024,512]{1,0:T(8,128)(2,1)}, bf16[1024,512]{1,0:T(8,128)(2,1)}, u32[]{:S(2)}, u32[]{:S(2)}) collective-permute-start(bf16[1024,512]{1,0:T(8,128)(2,1)} %refs_2_.3), channel_id=1, source_target_pairs={{0,16},{4,20},{8,24},{12,28},{16,0},{20,4},{24,8},{28,12},{1,17},{... | collective-permute-start | bytes 3145736 | tf_op jit(solution)/shard_map/ppermute | solution.py:385
  0.3 52.8 %collective-permute-start.4 = (bf16[1024,512]{1,0:T(8,128)(2,1)}, bf16[1024,512]{1,0:T(8,128)(2,1)}, u32[]{:S(2)}, u32[]{:S(2)}) collective-permute-start(bf16[1024,512]{1,0:T(8,128)(2,1)} %refs_2_.3), channel_id=1, source_target_pairs={{0,8},{4,12},{8,0},{12,4},{16,24},{20,28},{24,16},{28,20},{1,9},{5... | collective-permute-start | bytes 3145736 | tf_op jit(solution)/shard_map/ppermute | solution.py:385
  1.9 1.2 copy-start
  3.1 1.2 copy-start.2
  4.4 1.2 copy-start.1
  4.9 5.0 %collective-permute-start = (bf16[4,128,128]{2,1,0:T(8,128)(2,1)S(1)}, bf16[4,128,128]{2,1,0:T(8,128)(2,1)S(1)}, u32[]{:S(2)}, u32[]{:S(2)}) collective-permute-start(bf16[4,128,128]{2,1,0:T(8,128)(2,1)S(1)} %shard_map.74), channel_id=1, source_target_pairs={{0,4},{4,0},{8,12},{12,8},{16,20},{20,16},{24,28},{28,24},{1,5},{5... | collective-permute-start | bytes 393224 | tf_op jit(solution)/shard_map/ppermute | solution.py:124
  5.6 70.0 %copy-start.3 = (bf16[512,1024]{1,0:T(8,128)(2,1)S(1)}, bf16[512,1024]{1,0:T(8,128)(2,1)}, u32[]{:S(2)}) copy-start(bf16[512,1024]{1,0:T(8,128)(2,1)} %v_ref.7) | copy-start | bytes 3145732
  5.6 70.0 %copy-start.4 = (bf16[512,1024]{1,0:T(8,128)(2,1)S(1)}, bf16[512,1024]{1,0:T(8,128)(2,1)}, u32[]{:S(2)}) copy-start(bf16[512,1024]{1,0:T(8,128)(2,1)} %q_ref.5) | copy-start | bytes 3145732
  9.9 40.4 %collective-permute-start.1 = (bf16[4,128,128]{2,1,0:T(8,128)(2,1)S(1)}, bf16[4,128,128]{2,1,0:T(8,128)(2,1)S(1)}, u32[]{:S(2)}, u32[]{:S(2)}) collective-permute-start(bf16[4,128,128]{2,1,0:T(8,128)(2,1)S(1)} %shard_map.75), channel_id=1, source_target_pairs={{0,8},{4,12},{8,0},{12,4},{16,24},{20,28},{24,16},{28,20},{1,9},{5... | collective-permute-start | bytes 393224 | tf_op jit(solution)/shard_map/ppermute | solution.py:127
  51.0 0.7 copy-start.7
  51.7 8.2 %collective-permute-start.3 = (bf16[4,128,128]{2,1,0:T(8,128)(2,1)}, bf16[4,128,128]{2,1,0:T(8,128)(2,1)}, u32[]{:S(2)}, u32[]{:S(2)}) collective-permute-start(bf16[4,128,128]{2,1,0:T(8,128)(2,1)} %shard_map.76), channel_id=1, source_target_pairs={{0,16},{4,20},{8,24},{12,28},{1,17},{5,21},{9,25},{13,29},{2,18},{... | collective-permute-start | bytes 393224 | tf_op jit(solution)/shard_map/ppermute | solution.py:130
  59.9 0.9 copy-start.8
  61.8 0.7 copy-start.10
  62.6 5.0 %collective-permute-start.5 = (bf16[4,128,128]{2,1,0:T(8,128)(2,1)S(1)}, bf16[4,128,128]{2,1,0:T(8,128)(2,1)S(1)}, u32[]{:S(2)}, u32[]{:S(2)}) collective-permute-start(bf16[4,128,128]{2,1,0:T(8,128)(2,1)S(1)} %get-tuple-element.46), channel_id=1, source_target_pairs={{0,4},{4,0},{8,12},{12,8},{16,20},{20,16},{24,28},{28,24},{1,5},{5... | collective-permute-start | bytes 393224 | tf_op jit(solution)/shard_map/ppermute | solution.py:139
  67.5 25.5 %collective-permute-start.8 = (bf16[1024,512]{1,0:T(8,128)(2,1)}, bf16[1024,512]{1,0:T(8,128)(2,1)}, u32[]{:S(2)}, u32[]{:S(2)}) collective-permute-start(bf16[1024,512]{1,0:T(8,128)(2,1)} %refs_2_.3), channel_id=1, source_target_pairs={{8,16},{12,20},{16,8},{20,12},{9,17},{13,21},{17,9},{21,13},{10,18... | collective-permute-start | bytes 3145736 | tf_op jit(solution)/shard_map/ppermute | solution.py:385
  71.1 24.7 %collective-permute-start.9 = (bf16[1024,512]{1,0:T(8,128)(2,1)}, bf16[1024,512]{1,0:T(8,128)(2,1)}, u32[]{:S(2)}, u32[]{:S(2)}) collective-permute-start(bf16[1024,512]{1,0:T(8,128)(2,1)} %collective-permute-done.2.refs_4_.refs_2_), channel_id=1, source_target_pairs={{8,0},{12,4},{16,24},{20,28},{9,1},{13,5},{17,25},{21,29},{10,2},{... | collective-permute-start | bytes 3145736 | tf_op jit(solution)/shard_map/ppermute | solution.py:385
  76.7 1.2 copy-start.6
  76.7 1.3 copy-start.9
  76.7 1.4 copy-start.11
  76.8 1.4 copy-start.12
  78.2 4.5 %copy-start.5 = (bf16[1024,512]{1,0:T(8,128)(2,1)S(1)}, bf16[1024,512]{1,0:T(8,128)(2,1)}, u32[]{:S(2)}) copy-start(bf16[1024,512]{1,0:T(8,128)(2,1)} %refs_2_.3) | copy-start | bytes 3145732
  79.9 2.2 %collective-permute-start.6 = (f32[2,128]{1,0:T(2,128)S(1)}, f32[2,128]{1,0:T(2,128)S(1)}, u32[]{:S(2)}, u32[]{:S(2)}) collective-permute-start(f32[2,128]{1,0:T(2,128)S(1)} %slice.13), channel_id=1, source_target_pairs={{0,1},{1,0},{2,3},{3,2},{4,5},{5,4},{6,7},{7,6},{8,9},{9,8},{10,11... | collective-permute-start | bytes 3080 | tf_op jit(solution)/shard_map/ppermute | solution.py:411
  80.0 18.1 %collective-permute-start.10 = (bf16[256,1024]{1,0:T(8,128)(2,1)S(1)}, bf16[256,1024]{1,0:T(8,128)(2,1)S(1)}, u32[]{:S(2)}, u32[]{:S(2)}) collective-permute-start(bf16[256,1024]{1,0:T(8,128)(2,1)S(1)} %get-tuple-element.48.refs_0_), channel_id=1, source_target_pairs={{0,4},{4,0},{8,12},{12,8},{16,20},{20,16},{24,28},{28,24},{1,5},{5... | collective-permute-start | bytes 1572872 | tf_op jit(solution)/shard_map/ppermute | solution.py:406
  80.6 25.0 %collective-permute-start.11 = (bf16[256,1024]{1,0:T(8,128)(2,1)S(1)}, bf16[256,1024]{1,0:T(8,128)(2,1)S(1)}, u32[]{:S(2)}, u32[]{:S(2)}) collective-permute-start(bf16[256,1024]{1,0:T(8,128)(2,1)S(1)} %get-tuple-element.49.refs_1_), channel_id=1, source_target_pairs={{0,4},{4,0},{8,12},{12,8},{16,20},{20,16},{24,28},{28,24},{1,5},{5... | collective-permute-start | bytes 1572872 | tf_op jit(solution)/shard_map/ppermute | solution.py:406
  82.1 3.9 %collective-permute-start.7 = (f32[1,128]{1,0:T(1,128)S(1)}, f32[1,128]{1,0:T(1,128)S(1)}, u32[]{:S(2)}, u32[]{:S(2)}) collective-permute-start(f32[1,128]{1,0:T(1,128)S(1)} %slice.15), channel_id=1, source_target_pairs={{0,2},{1,3},{2,0},{3,1},{4,6},{5,7},{6,4},{7,5},{8,10},{9,11},{10,... | collective-permute-start | bytes 1544 | tf_op jit(solution)/shard_map/ppermute | solution.py:411
  86.0 27.5 %collective-permute-start.15 = (bf16[256,1536]{1,0:T(8,128)(2,1)S(1)}, bf16[256,1536]{1,0:T(8,128)(2,1)S(1)}, u32[]{:S(2)}, u32[]{:S(2)}) collective-permute-start(bf16[256,1536]{1,0:T(8,128)(2,1)S(1)} %get-tuple-element.50), channel_id=1, source_target_pairs={{0,1},{1,0},{2,3},{3,2},{4,5},{5,4},{6,7},{7,6},{8,9},{9,8},{10,11... | collective-permute-start | bytes 2359304 | tf_op jit(solution)/shard_map/ppermute | solution.py:433
  110.1 3.7 %collective-permute-start.25 = (bf16[256,512]{1,0:T(8,128)(2,1)S(1)}, bf16[256,512]{1,0:T(8,128)(2,1)S(1)}, u32[]{:S(2)}, u32[]{:S(2)}) collective-permute-start(bf16[256,512]{1,0:T(8,128)(2,1)S(1)} %get-tuple-element.60), channel_id=1, source_target_pairs={{0,1},{1,0},{2,3},{3,2},{4,5},{5,4},{6,7},{7,6},{8,9},{9,8},{10,11... | collective-permute-start | bytes 786440 | tf_op jit(solution)/shard_map/ppermute | solution.py:433
  110.2 4.2 %collective-permute-start.22 = (bf16[256,512]{1,0:T(8,128)(2,1)S(1)}, bf16[256,512]{1,0:T(8,128)(2,1)S(1)}, u32[]{:S(2)}, u32[]{:S(2)}) collective-permute-start(bf16[256,512]{1,0:T(8,128)(2,1)S(1)} %get-tuple-element.58), channel_id=1, source_target_pairs={{0,1},{1,0},{2,3},{3,2},{4,5},{5,4},{6,7},{7,6},{8,9},{9,8},{10,11... | collective-permute-start | bytes 786440 | tf_op jit(solution)/shard_map/ppermute | solution.py:433
  110.7 5.4 %collective-permute-start.19 = (bf16[256,512]{1,0:T(8,128)(2,1)S(1)}, bf16[256,512]{1,0:T(8,128)(2,1)S(1)}, u32[]{:S(2)}, u32[]{:S(2)}) collective-permute-start(bf16[256,512]{1,0:T(8,128)(2,1)S(1)} %get-tuple-element.56), channel_id=1, source_target_pairs={{0,1},{1,0},{2,3},{3,2},{4,5},{5,4},{6,7},{7,6},{8,9},{9,8},{10,11... | collective-permute-start | bytes 786440 | tf_op jit(solution)/shard_map/ppermute | solution.py:433
  113.0 3.7 %collective-permute-start.12 = (bf16[256,512]{1,0:T(8,128)(2,1)S(1)}, bf16[256,512]{1,0:T(8,128)(2,1)S(1)}, u32[]{:S(2)}, u32[]{:S(2)}) collective-permute-start(bf16[256,512]{1,0:T(8,128)(2,1)S(1)} %get-tuple-element.63), channel_id=1, source_target_pairs={{0,1},{1,0},{2,3},{3,2},{4,5},{5,4},{6,7},{7,6},{8,9},{9,8},{10,11... | collective-permute-start | bytes 786440 | tf_op jit(solution)/shard_map/ppermute | solution.py:433
  113.5 4.8 %collective-permute-start.17 = (bf16[256,512]{1,0:T(8,128)(2,1)S(1)}, bf16[256,512]{1,0:T(8,128)(2,1)S(1)}, u32[]{:S(2)}, u32[]{:S(2)}) collective-permute-start(bf16[256,512]{1,0:T(8,128)(2,1)S(1)} %get-tuple-element.54), channel_id=1, source_target_pairs={{0,1},{1,0},{2,3},{3,2},{4,5},{5,4},{6,7},{7,6},{8,9},{9,8},{10,11... | collective-permute-start | bytes 786440 | tf_op jit(solution)/shard_map/ppermute | solution.py:433
  113.8 23.8 %collective-permute-start.16 = (bf16[128,1536]{1,0:T(8,128)(2,1)S(1)}, bf16[128,1536]{1,0:T(8,128)(2,1)S(1)}, u32[]{:S(2)}, u32[]{:S(2)}) collective-permute-start(bf16[128,1536]{1,0:T(8,128)(2,1)S(1)} %get-tuple-element.68), channel_id=1, source_target_pairs={{0,2},{1,3},{2,0},{3,1},{4,6},{5,7},{6,4},{7,5},{8,10},{9,11},{10,... | collective-permute-start | bytes 1179656 | tf_op jit(solution)/shard_map/ppermute | solution.py:433
  114.4 14.2 %collective-permute-start.26 = (bf16[128,512]{1,0:T(8,128)(2,1)S(1)}, bf16[128,512]{1,0:T(8,128)(2,1)S(1)}, u32[]{:S(2)}, u32[]{:S(2)}) collective-permute-start(bf16[128,512]{1,0:T(8,128)(2,1)S(1)} %get-tuple-element.80), channel_id=1, source_target_pairs={{0,2},{1,3},{2,0},{3,1},{4,6},{5,7},{6,4},{7,5},{8,10},{9,11},{10,... | collective-permute-start | bytes 393224 | tf_op jit(solution)/shard_map/ppermute | solution.py:433
  116.1 15.3 %collective-permute-start.23 = (bf16[128,512]{1,0:T(8,128)(2,1)S(1)}, bf16[128,512]{1,0:T(8,128)(2,1)S(1)}, u32[]{:S(2)}, u32[]{:S(2)}) collective-permute-start(bf16[128,512]{1,0:T(8,128)(2,1)S(1)} %get-tuple-element.77), channel_id=1, source_target_pairs={{0,2},{1,3},{2,0},{3,1},{4,6},{5,7},{6,4},{7,5},{8,10},{9,11},{10,... | collective-permute-start | bytes 393224 | tf_op jit(solution)/shard_map/ppermute | solution.py:433
  116.7 17.5 %collective-permute-start.20 = (bf16[128,512]{1,0:T(8,128)(2,1)S(1)}, bf16[128,512]{1,0:T(8,128)(2,1)S(1)}, u32[]{:S(2)}, u32[]{:S(2)}) collective-permute-start(bf16[128,512]{1,0:T(8,128)(2,1)S(1)} %get-tuple-element.74), channel_id=1, source_target_pairs={{0,2},{1,3},{2,0},{3,1},{4,6},{5,7},{6,4},{7,5},{8,10},{9,11},{10,... | collective-permute-start | bytes 393224 | tf_op jit(solution)/shard_map/ppermute | solution.py:433
  118.3 18.7 %collective-permute-start.13 = (bf16[128,512]{1,0:T(8,128)(2,1)S(1)}, bf16[128,512]{1,0:T(8,128)(2,1)S(1)}, u32[]{:S(2)}, u32[]{:S(2)}) collective-permute-start(bf16[128,512]{1,0:T(8,128)(2,1)S(1)} %get-tuple-element.65), channel_id=1, source_target_pairs={{0,2},{1,3},{2,0},{3,1},{4,6},{5,7},{6,4},{7,5},{8,10},{9,11},{10,... | collective-permute-start | bytes 393224 | tf_op jit(solution)/shard_map/ppermute | solution.py:433
  128.6 10.8 %collective-permute-start.18 = (bf16[128,512]{1,0:T(8,128)(2,1)S(1)}, bf16[128,512]{1,0:T(8,128)(2,1)S(1)}, u32[]{:S(2)}, u32[]{:S(2)}) collective-permute-start(bf16[128,512]{1,0:T(8,128)(2,1)S(1)} %get-tuple-element.71), channel_id=1, source_target_pairs={{0,2},{1,3},{2,0},{3,1},{4,6},{5,7},{6,4},{7,5},{8,10},{9,11},{10,... | collective-permute-start | bytes 393224 | tf_op jit(solution)/shard_map/ppermute | solution.py:433
  131.4 8.0 %collective-permute-start.27 = (bf16[128,512]{1,0:T(8,128)(2,1)S(1)}, bf16[128,512]{1,0:T(8,128)(2,1)S(1)}, u32[]{:S(2)}, u32[]{:S(2)}) collective-permute-start(bf16[128,512]{1,0:T(8,128)(2,1)S(1)} %shard_map.98), channel_id=1, source_target_pairs={{0,4},{4,0},{8,12},{12,8},{16,20},{20,16},{24,28},{28,24},{1,5},{5... | collective-permute-start | bytes 393224 | tf_op jit(solution)/shard_map/ppermute | solution.py:442
  134.2 5.3 %collective-permute-start.24 = (bf16[128,512]{1,0:T(8,128)(2,1)S(1)}, bf16[128,512]{1,0:T(8,128)(2,1)S(1)}, u32[]{:S(2)}, u32[]{:S(2)}) collective-permute-start(bf16[128,512]{1,0:T(8,128)(2,1)S(1)} %shard_map.96), channel_id=1, source_target_pairs={{0,4},{4,0},{8,12},{12,8},{16,20},{20,16},{24,28},{28,24},{1,5},{5... | collective-permute-start | bytes 393224 | tf_op jit(solution)/shard_map/ppermute | solution.py:442
  137.0 6.4 %collective-permute-start.21 = (bf16[128,512]{1,0:T(8,128)(2,1)S(1)}, bf16[128,512]{1,0:T(8,128)(2,1)S(1)}, u32[]{:S(2)}, u32[]{:S(2)}) collective-permute-start(bf16[128,512]{1,0:T(8,128)(2,1)S(1)} %shard_map.94), channel_id=1, source_target_pairs={{0,4},{4,0},{8,12},{12,8},{16,20},{20,16},{24,28},{28,24},{1,5},{5... | collective-permute-start | bytes 393224 | tf_op jit(solution)/shard_map/ppermute | solution.py:442
  137.6 7.6 %collective-permute-start.14 = (bf16[128,512]{1,0:T(8,128)(2,1)S(1)}, bf16[128,512]{1,0:T(8,128)(2,1)S(1)}, u32[]{:S(2)}, u32[]{:S(2)}) collective-permute-start(bf16[128,512]{1,0:T(8,128)(2,1)S(1)} %shard_map.88), channel_id=1, source_target_pairs={{0,4},{4,0},{8,12},{12,8},{16,20},{20,16},{24,28},{28,24},{1,5},{5... | collective-permute-start | bytes 393224 | tf_op jit(solution)/shard_map/ppermute | solution.py:442

commit v18 on v14

--- a/solution.py
+++ b/solution.py
@@ -464,9 +464,13 @@
     if inner > 1:
         group(turns[1:], [1, 2])
     filled = placed(None, pieces, squares, width, shape, total_width) if in_kernel else None
-    last, _, _ = summed(
-        [(turn, [3]) for turn in turns], [*pins, *ends, *returned]
-    )
+    pins += [*ends, *returned]
+    last = []
+    for members in (turns[1:], turns[:1]):
+        if members:
+            more, sent, _ = summed([(turn, [3]) for turn in members], pins)
+            last += more
+            pins = [sent]
     if in_kernel:
         return placed(filled, last, squares, width, shape, total_width)
     scale = lax.rsqrt(squares.reshape(out_rows, 1) / total_width + epsilon)

time: 117 us -> 114 us (0.974)
  waiting for transfers between devices: 57 us -> 52.2 us
  starting transfers between devices: 34 us -> 36 us
    ppermute x10 -> x12, waiting for transfers between devices: 15.8 us -> 12 us  [summed(): got = lax.ppermute(sent, 'head', flip_pairs(n_head, bit))]
    ppermute x10 -> x12, starting transfers between devices: 8.44 us -> 9.55 us  [summed(): got = lax.ppermute(sent, 'head', flip_pairs(n_head, bit))]
    pallas_call x24 -> x27, Pallas kernels: 19.8 us -> 20 us  [local_call(): pl.pallas_call(kernel, in_specs=[pl.BlockSpec(memory_space=pltpu.SMEM)] +...]
  transfers between devices with their start and end apart: 25 -> 27, of which waited for: 17 -> 16; matrix products, arithmetic and copies ran while one was open for 0% -> 0% of each run, Pallas kernels for 14% -> 15%
where the time goes in v18:
time: 114 us
  waiting for transfers between devices  52.2 us (46%)
  starting transfers between devices  36 us (32%)
  Pallas kernels  21.4 us (19%)
  local copies, waits for them, and re-layouts  3.59 us (3%)
    pallas_call x27, Pallas kernels, local_call(): pl.pallas_call(kernel, in_specs=[pl.BlockSpec(memory_space=pltpu.SMEM)] +...  20 us
    ppermute x12, waiting for transfers between devices, summed(): got = lax.ppermute(sent, 'head', flip_pairs(n_head, bit))  12 us
    ppermute x4, waiting for transfers between devices, along(): return lax.ppermute(value, 'seq', line_pairs(n_seq, hops))  10.3 us
    ppermute x12, starting transfers between devices, summed(): got = lax.ppermute(sent, 'head', flip_pairs(n_head, bit))  9.55 us
    ppermute x4, starting transfers between devices, along(): return lax.ppermute(value, 'seq', line_pairs(n_seq, hops))  8.27 us
    ppermute x1, waiting for transfers between devices, shards(): lax.ppermute(kept_rows, 'seq', pairs)  8.12 us
    ppermute x3, waiting for transfers between devices, summed(): piece = lax.ppermute(piece, 'seq', turn_pairs(n_seq, -turn))  6.33 us
    ppermute x1, waiting for transfers between devices, shards(): lax.ppermute(sent_rows, 'seq', pairs)  6.02 us
  transfers between devices with their start and end apart: 27, of which 16 were waited for; matrix products, arithmetic and copies ran while one was open for 0% of the time, Pallas kernels for 15%

profile of v18, /device:TPU:0, one launch (start us, length us, event | category | flops | bytes accessed | tf_op | source)
XLA Modules:
  0.0 113.7 jit_solution(423247243653243616)
XLA Ops:
  0.0 1.2 %copy-done = bf16[512,1024]{1,0:T(8,128)(2,1)S(1)} copy-done((bf16[512,1024]{1,0:T(8,128)(2,1)S(1)}, bf16[512,1024]{1,0:T(8,128)(2,1)}, u32[]{:S(2)}) %copy-start) | copy-done | bytes 1048600
  1.2 1.2 %copy-done.2 = bf16[512,1024]{1,0:T(8,128)(2,1)S(1)} copy-done((bf16[512,1024]{1,0:T(8,128)(2,1)S(1)}, bf16[512,1024]{1,0:T(8,128)(2,1)}, u32[]{:S(2)}) %copy-start.2) | copy-done | bytes 1048600
  2.5 0.5 shard_map.74
  2.9 3.0 %collective-permute-start = (bf16[4,128,128]{2,1,0:T(8,128)(2,1)S(1)}, bf16[4,128,128]{2,1,0:T(8,128)(2,1)S(1)}, u32[]{:S(2)}, u32[]{:S(2)}) collective-permute-start(bf16[4,128,128]{2,1,0:T(8,128)(2,1)S(1)} %shard_map.74), channel_id=1, source_target_pairs={{0,4},{4,0},{8,12},{12,8},{16,20},{20,16},{24,28},{28,24},{1,5},{5... | collective-permute-start | bytes 393224 | tf_op jit(solution)/shard_map/ppermute | solution.py:124
  6.0 0.5 shard_map.73.refs_0_.refs_2_
  6.4 3.0 %collective-permute-done.refs_1_.refs_3_ = bf16[4,128,128]{2,1,0:T(8,128)(2,1)S(1)} collective-permute-done((bf16[4,128,128]{2,1,0:T(8,128)(2,1)S(1)}, bf16[4,128,128]{2,1,0:T(8,128)(2,1)S(1)}, u32[]{:S(2)}, u32[]{:S(2)}) %collective-permute-start) | collective-permute-done | bytes 131104 | tf_op jit(solution)/shard_map/ppermute | solution.py:124
  9.5 1.9 %collective-permute-start.1 = (bf16[4,128,128]{2,1,0:T(8,128)(2,1)S(1)}, bf16[4,128,128]{2,1,0:T(8,128)(2,1)S(1)}, u32[]{:S(2)}, u32[]{:S(2)}) collective-permute-start(bf16[4,128,128]{2,1,0:T(8,128)(2,1)S(1)} %shard_map.75), channel_id=1, source_target_pairs={{0,8},{4,12},{8,0},{12,4},{16,24},{20,28},{24,16},{28,20},{1,9},{5... | collective-permute-start | bytes 393224 | tf_op jit(solution)/shard_map/ppermute | solution.py:127
  11.4 3.1 %collective-permute-done.1.refs_2_.refs_1_ = bf16[4,128,128]{2,1,0:T(8,128)(2,1)S(1)} collective-permute-done((bf16[4,128,128]{2,1,0:T(8,128)(2,1)S(1)}, bf16[4,128,128]{2,1,0:T(8,128)(2,1)S(1)}, u32[]{:S(2)}, u32[]{:S(2)}) %collective-permute-start.1) | collective-permute-done | bytes 131104 | tf_op jit(solution)/shard_map/ppermute | solution.py:127
  14.5 0.7 shard_map.76
  15.2 5.4 %collective-permute-start.2 = (bf16[4,128,128]{2,1,0:T(8,128)(2,1)}, bf16[4,128,128]{2,1,0:T(8,128)(2,1)}, u32[]{:S(2)}, u32[]{:S(2)}) collective-permute-start(bf16[4,128,128]{2,1,0:T(8,128)(2,1)} %shard_map.76), channel_id=1, source_target_pairs={{0,16},{4,20},{8,24},{12,28},{1,17},{5,21},{9,25},{13,29},{2,18},{... | collective-permute-start | bytes 393224 | tf_op jit(solution)/shard_map/ppermute | solution.py:129
  20.6 0.1 stack.81
  20.7 2.1 %collective-permute-done.2.refs_0_ = bf16[4,128,128]{2,1,0:T(8,128)(2,1)} collective-permute-done((bf16[4,128,128]{2,1,0:T(8,128)(2,1)}, bf16[4,128,128]{2,1,0:T(8,128)(2,1)}, u32[]{:S(2)}, u32[]{:S(2)}) %collective-permute-start.2) | collective-permute-done | bytes 131104 | tf_op jit(solution)/shard_map/ppermute | solution.py:129
  22.8 0.9 copy-done.7
  23.7 1.1 shard_map.77
  24.8 1.6 %collective-permute-start.3 = (bf16[4,128,128]{2,1,0:T(8,128)(2,1)S(1)}, bf16[4,128,128]{2,1,0:T(8,128)(2,1)S(1)}, u32[]{:S(2)}, u32[]{:S(2)}) collective-permute-start(bf16[4,128,128]{2,1,0:T(8,128)(2,1)S(1)} %get-tuple-element.42), channel_id=1, source_target_pairs={{0,4},{4,0},{8,12},{12,8},{16,20},{20,16},{24,28},{28,24},{1,5},{5... | collective-permute-start | bytes 393224 | tf_op jit(solution)/shard_map/ppermute | solution.py:137
  26.3 0.1 pad_add_fusion.1.place_ref
  26.4 3.4 %collective-permute-start.9 = (bf16[1024,512]{1,0:T(8,128)(2,1)}, bf16[1024,512]{1,0:T(8,128)(2,1)}, u32[]{:S(2)}, u32[]{:S(2)}) collective-permute-start(bf16[1024,512]{1,0:T(8,128)(2,1)} %refs_2_.3), channel_id=1, source_target_pairs={{0,16},{4,20},{8,24},{12,28},{16,0},{20,4},{24,8},{28,12},{1,17},{... | collective-permute-start | bytes 3145736 | tf_op jit(solution)/shard_map/ppermute | solution.py:383
  29.9 1.1 shard_map.78.refs_2_
  31.0 1.1 shard_map.79.refs_3_
  32.1 2.8 %collective-permute-start.8 = (bf16[1024,512]{1,0:T(8,128)(2,1)}, bf16[1024,512]{1,0:T(8,128)(2,1)}, u32[]{:S(2)}, u32[]{:S(2)}) collective-permute-start(bf16[1024,512]{1,0:T(8,128)(2,1)} %refs_2_.3), channel_id=1, source_target_pairs={{0,8},{4,12},{8,0},{12,4},{16,24},{20,28},{24,16},{28,20},{1,9},{5... | collective-permute-start | bytes 3145736 | tf_op jit(solution)/shard_map/ppermute | solution.py:383
  34.9 1.7 %shard_map.80 = (bf16[256,1024]{1,0:T(8,128)(2,1)S(1)}, bf16[256,1024]{1,0:T(8,128)(2,1)S(1)}, f32[4,128]{1,0:T(4,128)S(1)}) custom-call(s32[2]{0:T(128)S(1)} %pad_add_fusion.1.place_ref, bf16[512,1024]{1,0:T(8,128)(2,1)S(1)} %copy-done.4, bf16[512,1024]{1,0:T(8,128)(2,1)S(1)} %copy-done.5, f32[32,1,128]{2,1,0:T(1,128)S(1)} %bitcast.17, ...), custom_call_target="tpu_custom_call" | custom-call | flops 268435456 | bytes 6178816 | tf_op jit(solution)/shard_map/pallas_call | solution.py:49
  36.7 0.6 collective-permute-start.6
  37.3 1.5 %collective-permute-start.7 = (bf16[256,1024]{1,0:T(8,128)(2,1)S(1)}, bf16[256,1024]{1,0:T(8,128)(2,1)S(1)}, u32[]{:S(2)}, u32[]{:S(2)}) collective-permute-start(bf16[256,1024]{1,0:T(8,128)(2,1)S(1)} %get-tuple-element.45.refs_1_), channel_id=1, source_target_pairs={{0,4},{4,0},{8,12},{12,8},{16,20},{20,16},{24,28},{28,24},{1,5},{5... | collective-permute-start | bytes 1572872 | tf_op jit(solution)/shard_map/ppermute | solution.py:405
  38.8 1.1 collective-permute-done.4
  39.9 1.5 %collective-permute-start.5 = (f32[1,128]{1,0:T(1,128)S(1)}, f32[1,128]{1,0:T(1,128)S(1)}, u32[]{:S(2)}, u32[]{:S(2)}) collective-permute-start(f32[1,128]{1,0:T(1,128)S(1)} %slice.15), channel_id=1, source_target_pairs={{0,2},{1,3},{2,0},{3,1},{4,6},{5,7},{6,4},{7,5},{8,10},{9,11},{10,... | collective-permute-start | bytes 1544 | tf_op jit(solution)/shard_map/ppermute | solution.py:410
  41.4 1.9 %shard_map.81 = (bf16[256,512]{1,0:T(8,128)(2,1)S(1)}, f32[256,512]{1,0:T(8,128)S(1)}) custom-call(s32[1]{0:T(128)} %bitcast.10.flag_ref, bf16[256,1024]{1,0:T(8,128)(2,1)S(1)} %get-tuple-element.44.refs_0_, bf16[256,1024]{1,0:T(8,128)(2,1)S(1)} %get-tuple-element.45.refs_1_, bf16[1024,512]{1,0:T(8,128)(2,1)} %refs_2_.3), custom_call_target="tpu_custom_call" | custom-call | flops 536870912 | bytes 2883584 | tf_op jit(solution)/shard_map/pallas_call | solution.py:49
  43.4 0.1 collective-permute-done.5
  43.5 8.1 %collective-permute-done.6.refs_0_ = bf16[256,1024]{1,0:T(8,128)(2,1)S(1)} collective-permute-done((bf16[256,1024]{1,0:T(8,128)(2,1)S(1)}, bf16[256,1024]{1,0:T(8,128)(2,1)S(1)}, u32[]{:S(2)}, u32[]{:S(2)}) %collective-permute-start.6) | collective-permute-done | bytes 524320 | tf_op jit(solution)/shard_map/ppermute | solution.py:405
  51.6 6.0 %collective-permute-done.7.refs_1_ = bf16[256,1024]{1,0:T(8,128)(2,1)S(1)} collective-permute-done((bf16[256,1024]{1,0:T(8,128)(2,1)S(1)}, bf16[256,1024]{1,0:T(8,128)(2,1)S(1)}, u32[]{:S(2)}, u32[]{:S(2)}) %collective-permute-start.7) | collective-permute-done | bytes 524320 | tf_op jit(solution)/shard_map/ppermute | solution.py:405
  57.6 1.9 %shard_map.82 = (bf16[256,512]{1,0:T(8,128)(2,1)S(1)}, f32[256,512]{1,0:T(8,128)S(1)}) custom-call(s32[1]{0:T(128)} %bitcast.10.flag_ref, bf16[256,1024]{1,0:T(8,128)(2,1)S(1)} %collective-permute-done.6.refs_0_, bf16[256,1024]{1,0:T(8,128)(2,1)S(1)} %collective-permute-done.7.refs_1_, bf16[1024,512]{1,0:T(8,128)(2,1)} %refs_2_.3), custom_call_target="tpu_custom_call" | custom-call | flops 536870912 | bytes 2883584 | tf_op jit(solution)/shard_map/pallas_call | solution.py:49
  59.5 0.1 collective-permute-start.12
  59.7 1.6 %collective-permute-start.11 = (bf16[128,512]{1,0:T(8,128)(2,1)S(1)}, bf16[128,512]{1,0:T(8,128)(2,1)S(1)}, u32[]{:S(2)}, u32[]{:S(2)}) collective-permute-start(bf16[128,512]{1,0:T(8,128)(2,1)S(1)} %get-tuple-element.55), channel_id=1, source_target_pairs={{0,2},{1,3},{2,0},{3,1},{4,6},{5,7},{6,4},{7,5},{8,10},{9,11},{10,... | collective-permute-start | bytes 393224 | tf_op jit(solution)/shard_map/ppermute | solution.py:432
  61.4 1.4 %collective-permute-start.13 = (bf16[128,512]{1,0:T(8,128)(2,1)S(1)}, bf16[128,512]{1,0:T(8,128)(2,1)S(1)}, u32[]{:S(2)}, u32[]{:S(2)}) collective-permute-start(bf16[128,512]{1,0:T(8,128)(2,1)S(1)} %get-tuple-element.57), channel_id=1, source_target_pairs={{0,2},{1,3},{2,0},{3,1},{4,6},{5,7},{6,4},{7,5},{8,10},{9,11},{10,... | collective-permute-start | bytes 393224 | tf_op jit(solution)/shard_map/ppermute | solution.py:432
  62.8 0.7 collective-permute-start.19
  63.5 2.5 %collective-permute-done.11.got_ref = bf16[128,512]{1,0:T(8,128)(2,1)S(1)} collective-permute-done((bf16[128,512]{1,0:T(8,128)(2,1)S(1)}, bf16[128,512]{1,0:T(8,128)(2,1)S(1)}, u32[]{:S(2)}, u32[]{:S(2)}) %collective-permute-start.11) | collective-permute-done | bytes 131104 | tf_op jit(solution)/shard_map/ppermute | solution.py:432
  66.1 8.7 %collective-permute-done.9.refs_3_ = bf16[1024,512]{1,0:T(8,128)(2,1)} collective-permute-done((bf16[1024,512]{1,0:T(8,128)(2,1)}, bf16[1024,512]{1,0:T(8,128)(2,1)}, u32[]{:S(2)}, u32[]{:S(2)}) %collective-permute-start.9) | collective-permute-done | bytes 1048608 | tf_op jit(solution)/shard_map/ppermute | solution.py:383
  74.7 1.3 %collective-permute-start.20 = (bf16[1024,512]{1,0:T(8,128)(2,1)}, bf16[1024,512]{1,0:T(8,128)(2,1)S(1)}, u32[]{:S(2)}, u32[]{:S(2)}) collective-permute-start(bf16[1024,512]{1,0:T(8,128)(2,1)} %collective-permute-done.9.refs_3_), channel_id=1, source_target_pairs={{8,0},{12,4},{16,24},{20,28},{9,1},{13,5},{17,25},{21,29},{10,2},{... | collective-permute-start | bytes 3145736 | tf_op jit(solution)/shard_map/ppermute | solution.py:383
  76.0 2.8 %shard_map.83 = (bf16[256,1024]{1,0:T(8,128)(2,1)S(1)}, f32[256,1024]{1,0:T(8,128)S(1)}) custom-call(s32[1]{0:T(128)} %bitcast.10.flag_ref, bf16[256,1024]{1,0:T(8,128)(2,1)S(1)} %get-tuple-element.44.refs_0_, bf16[256,1024]{1,0:T(8,128)(2,1)S(1)} %get-tuple-element.45.refs_1_, bf16[1024,512]{1,0:T(8,128)(2,1)} %collective-permute-done.8.refs_2_, ...), custom_call_target="tpu_custom_call" | custom-call | flops 1073741824 | bytes 4718592 | tf_op jit(solution)/shard_map/pallas_call | solution.py:49
  78.8 0.1 collective-permute-start.14
  78.9 2.8 %shard_map.84 = (bf16[256,1024]{1,0:T(8,128)(2,1)S(1)}, f32[256,1024]{1,0:T(8,128)S(1)}) custom-call(s32[1]{0:T(128)} %bitcast.10.flag_ref, bf16[256,1024]{1,0:T(8,128)(2,1)S(1)} %collective-permute-done.6.refs_0_, bf16[256,1024]{1,0:T(8,128)(2,1)S(1)} %collective-permute-done.7.refs_1_, bf16[1024,512]{1,0:T(8,128)(2,1)} %collective-permute-done.8.refs_2_, ...), custom_call_target="tpu_custom_call" | custom-call | flops 1073741824 | bytes 4718592 | tf_op jit(solution)/shard_map/pallas_call | solution.py:49
  81.7 0.6 collective-permute-start.16
  82.3 0.1 shard_map.87
  82.4 1.6 %collective-permute-start.15 = (bf16[128,1024]{1,0:T(8,128)(2,1)S(1)}, bf16[128,1024]{1,0:T(8,128)(2,1)S(1)}, u32[]{:S(2)}, u32[]{:S(2)}) collective-permute-start(bf16[128,1024]{1,0:T(8,128)(2,1)S(1)} %get-tuple-element.59), channel_id=1, source_target_pairs={{0,2},{1,3},{2,0},{3,1},{4,6},{5,7},{6,4},{7,5},{8,10},{9,11},{10,... | collective-permute-start | bytes 786440 | tf_op jit(solution)/shard_map/ppermute | solution.py:432
  84.0 0.1 shard_map.88
  84.1 1.5 %collective-permute-start.17 = (bf16[128,1024]{1,0:T(8,128)(2,1)S(1)}, bf16[128,1024]{1,0:T(8,128)(2,1)S(1)}, u32[]{:S(2)}, u32[]{:S(2)}) collective-permute-start(bf16[128,1024]{1,0:T(8,128)(2,1)S(1)} %get-tuple-element.61), channel_id=1, source_target_pairs={{0,2},{1,3},{2,0},{3,1},{4,6},{5,7},{6,4},{7,5},{8,10},{9,11},{10,... | collective-permute-start | bytes 786440 | tf_op jit(solution)/shard_map/ppermute | solution.py:432
  85.5 0.6 collective-permute-start.18
  86.1 4.9 %collective-permute-done.18.refs_1_ = bf16[128,512]{1,0:T(8,128)(2,1)S(1)} collective-permute-done((bf16[128,512]{1,0:T(8,128)(2,1)S(1)}, bf16[128,512]{1,0:T(8,128)(2,1)S(1)}, u32[]{:S(2)}, u32[]{:S(2)}) %collective-permute-start.18) | collective-permute-done | bytes 131104 | tf_op jit(solution)/shard_map/ppermute | solution.py:441
  91.1 0.5 collective-permute-done.15.got_ref
  91.6 4.7 %collective-permute-done.17.got_ref = bf16[128,1024]{1,0:T(8,128)(2,1)S(1)} collective-permute-done((bf16[128,1024]{1,0:T(8,128)(2,1)S(1)}, bf16[128,1024]{1,0:T(8,128)(2,1)S(1)}, u32[]{:S(2)}, u32[]{:S(2)}) %collective-permute-start.17) | collective-permute-done | bytes 262176 | tf_op jit(solution)/shard_map/ppermute | solution.py:432
  96.3 1.6 %collective-permute-done.20.refs_3_ = bf16[1024,512]{1,0:T(8,128)(2,1)S(1)} collective-permute-done((bf16[1024,512]{1,0:T(8,128)(2,1)}, bf16[1024,512]{1,0:T(8,128)(2,1)S(1)}, u32[]{:S(2)}, u32[]{:S(2)}) %collective-permute-start.20) | collective-permute-done | bytes 1048608 | tf_op jit(solution)/shard_map/ppermute | solution.py:383
  97.9 0.7 shard_map.90
  98.7 0.7 shard_map.93
  99.5 0.5 collective-permute-start.24
  100.1 0.6 collective-permute-start.26
  100.7 1.6 %collective-permute-start.22 = (bf16[128,512]{1,0:T(8,128)(2,1)S(1)}, bf16[128,512]{1,0:T(8,128)(2,1)S(1)}, u32[]{:S(2)}, u32[]{:S(2)}) collective-permute-start(bf16[128,512]{1,0:T(8,128)(2,1)S(1)} %get-tuple-element.68), channel_id=1, source_target_pairs={{0,2},{1,3},{2,0},{3,1},{4,6},{5,7},{6,4},{7,5},{8,10},{9,11},{10,... | collective-permute-start | bytes 393224 | tf_op jit(solution)/shard_map/ppermute | solution.py:432
  102.4 0.6 collective-permute-start.25
  102.9 4.2 %collective-permute-done.22.got_ref = bf16[128,512]{1,0:T(8,128)(2,1)S(1)} collective-permute-done((bf16[128,512]{1,0:T(8,128)(2,1)S(1)}, bf16[128,512]{1,0:T(8,128)(2,1)S(1)}, u32[]{:S(2)}, u32[]{:S(2)}) %collective-permute-start.22) | collective-permute-done | bytes 131104 | tf_op jit(solution)/shard_map/ppermute | solution.py:432
  107.2 1.6 %collective-permute-start.23 = (bf16[128,512]{1,0:T(8,128)(2,1)S(1)}, bf16[128,512]{1,0:T(8,128)(2,1)S(1)}, u32[]{:S(2)}, u32[]{:S(2)}) collective-permute-start(bf16[128,512]{1,0:T(8,128)(2,1)S(1)} %shard_map.92), channel_id=1, source_target_pairs={{0,4},{4,0},{8,12},{12,8},{16,20},{20,16},{24,28},{28,24},{1,5},{5... | collective-permute-start | bytes 393224 | tf_op jit(solution)/shard_map/ppermute | solution.py:441
  108.8 0.1 stack.92.starts_ref
  108.9 0.1 pad_add_fusion.starts_ref
  109.0 0.2 collective-permute-done.26.refs_3_
  109.2 1.8 %shard_map.99.refs_2_ = bf16[128,4096]{1,0:T(8,128)(2,1)} custom-call(s32[6]{0:T(128)S(1)} %stack.92.starts_ref, f32[1,128]{1,0:T(1,128)S(1)} %slice_add_fusion.1.squares_ref, bf16[128,512]{1,0:T(8,128)(2,1)S(1)} %shard_map.96.refs_0_, bf16[128,512]{1,0:T(8,128)(2,1)S(1)} %collective-permute-done.18.refs_1_, bf16[128,1024]{1,0:T(8,128)(2,1)S(1)} %shard_map.97.refs_2_, ...), custom_call_target="tpu_custom_call" | custom-call | bytes 1835520 | tf_op jit(solution)/shard_map/pallas_call | solution.py:49
  111.0 1.2 %collective-permute-done.23.refs_0_ = bf16[128,512]{1,0:T(8,128)(2,1)S(1)} collective-permute-done((bf16[128,512]{1,0:T(8,128)(2,1)S(1)}, bf16[128,512]{1,0:T(8,128)(2,1)S(1)}, u32[]{:S(2)}, u32[]{:S(2)}) %collective-permute-start.23) | collective-permute-done | bytes 131104 | tf_op jit(solution)/shard_map/ppermute | solution.py:441
  112.3 1.4 %shard_map.100 = bf16[128,4096]{1,0:T(8,128)(2,1)} custom-call(s32[2]{0:T(128)S(1)} %pad_add_fusion.starts_ref, f32[1,128]{1,0:T(1,128)S(1)} %slice_add_fusion.1.squares_ref, bf16[128,512]{1,0:T(8,128)(2,1)S(1)} %collective-permute-done.23.refs_0_, bf16[128,512]{1,0:T(8,128)(2,1)S(1)} %shard_map.95.refs_1_, ...), custom_call_target="tpu_custom_call", output_to_operand_aliasing={{}: (4, {})} | custom-call | bytes 524288 | tf_op jit(solution)/shard_map/pallas_call | solution.py:352
  (47 shorter events, 0.6 us)
Async XLA Ops:
  0.0 1.2 %copy-start = (bf16[512,1024]{1,0:T(8,128)(2,1)S(1)}, bf16[512,1024]{1,0:T(8,128)(2,1)}, u32[]{:S(2)}) copy-start(bf16[512,1024]{1,0:T(8,128)(2,1)} %k_ref.7) | copy-start | bytes 3145732
  1.2 1.2 %copy-start.2 = (bf16[512,1024]{1,0:T(8,128)(2,1)S(1)}, bf16[512,1024]{1,0:T(8,128)(2,1)}, u32[]{:S(2)}) copy-start(bf16[512,1024]{1,0:T(8,128)(2,1)} %v_ref.7) | copy-start | bytes 3145732
  2.5 3.5 %copy-start.1 = (bf16[512,1024]{1,0:T(8,128)(2,1)S(1)}, bf16[512,1024]{1,0:T(8,128)(2,1)}, u32[]{:S(2)}) copy-start(bf16[512,1024]{1,0:T(8,128)(2,1)} %k_ref.7) | copy-start | bytes 3145732
  2.9 6.5 %collective-permute-start = (bf16[4,128,128]{2,1,0:T(8,128)(2,1)S(1)}, bf16[4,128,128]{2,1,0:T(8,128)(2,1)S(1)}, u32[]{:S(2)}, u32[]{:S(2)}) collective-permute-start(bf16[4,128,128]{2,1,0:T(8,128)(2,1)S(1)} %shard_map.74), channel_id=1, source_target_pairs={{0,4},{4,0},{8,12},{12,8},{16,20},{20,16},{24,28},{28,24},{1,5},{5... | collective-permute-start | bytes 393224 | tf_op jit(solution)/shard_map/ppermute | solution.py:124
  5.9 23.9 %copy-start.4 = (bf16[512,1024]{1,0:T(8,128)(2,1)S(1)}, bf16[512,1024]{1,0:T(8,128)(2,1)}, u32[]{:S(2)}) copy-start(bf16[512,1024]{1,0:T(8,128)(2,1)} %q_ref.5) | copy-start | bytes 3145732
  6.4 23.4 %copy-start.3 = (bf16[512,1024]{1,0:T(8,128)(2,1)S(1)}, bf16[512,1024]{1,0:T(8,128)(2,1)}, u32[]{:S(2)}) copy-start(bf16[512,1024]{1,0:T(8,128)(2,1)} %v_ref.7) | copy-start | bytes 3145732
  9.5 5.0 %collective-permute-start.1 = (bf16[4,128,128]{2,1,0:T(8,128)(2,1)S(1)}, bf16[4,128,128]{2,1,0:T(8,128)(2,1)S(1)}, u32[]{:S(2)}, u32[]{:S(2)}) collective-permute-start(bf16[4,128,128]{2,1,0:T(8,128)(2,1)S(1)} %shard_map.75), channel_id=1, source_target_pairs={{0,8},{4,12},{8,0},{12,4},{16,24},{20,28},{24,16},{28,20},{1,9},{5... | collective-permute-start | bytes 393224 | tf_op jit(solution)/shard_map/ppermute | solution.py:127
  14.5 0.7 copy-start.6
  15.2 7.6 %collective-permute-start.2 = (bf16[4,128,128]{2,1,0:T(8,128)(2,1)}, bf16[4,128,128]{2,1,0:T(8,128)(2,1)}, u32[]{:S(2)}, u32[]{:S(2)}) collective-permute-start(bf16[4,128,128]{2,1,0:T(8,128)(2,1)} %shard_map.76), channel_id=1, source_target_pairs={{0,16},{4,20},{8,24},{12,28},{1,17},{5,21},{9,25},{13,29},{2,18},{... | collective-permute-start | bytes 393224 | tf_op jit(solution)/shard_map/ppermute | solution.py:129
  22.8 0.9 copy-start.7
  24.8 10.1 %collective-permute-start.3 = (bf16[4,128,128]{2,1,0:T(8,128)(2,1)S(1)}, bf16[4,128,128]{2,1,0:T(8,128)(2,1)S(1)}, u32[]{:S(2)}, u32[]{:S(2)}) collective-permute-start(bf16[4,128,128]{2,1,0:T(8,128)(2,1)S(1)} %get-tuple-element.42), channel_id=1, source_target_pairs={{0,4},{4,0},{8,12},{12,8},{16,20},{20,16},{24,28},{28,24},{1,5},{5... | collective-permute-start | bytes 393224 | tf_op jit(solution)/shard_map/ppermute | solution.py:137
  26.4 48.3 %collective-permute-start.9 = (bf16[1024,512]{1,0:T(8,128)(2,1)}, bf16[1024,512]{1,0:T(8,128)(2,1)}, u32[]{:S(2)}, u32[]{:S(2)}) collective-permute-start(bf16[1024,512]{1,0:T(8,128)(2,1)} %refs_2_.3), channel_id=1, source_target_pairs={{0,16},{4,20},{8,24},{12,28},{16,0},{20,4},{24,8},{28,12},{1,17},{... | collective-permute-start | bytes 3145736 | tf_op jit(solution)/shard_map/ppermute | solution.py:383
  30.9 4.0 %copy-start.5 = (bf16[512,1024]{1,0:T(8,128)(2,1)S(1)}, bf16[512,1024]{1,0:T(8,128)(2,1)}, u32[]{:S(2)}) copy-start(bf16[512,1024]{1,0:T(8,128)(2,1)} %gate_ref.1) | copy-start | bytes 3145732
  31.0 4.0 %copy-start.8 = (f32[8,128,128]{2,1,0:T(8,128)S(1)}, f32[8,128,128]{2,1,0:T(8,128)}, u32[]{:S(2)}) copy-start(f32[8,128,128]{2,1,0:T(8,128)} %kv_ref.1) | copy-start | bytes 1572868
  31.0 4.0 %copy-start.9 = (f32[4096]{0:T(1024)S(1)}, f32[4096]{0:T(1024)}, u32[]{:S(2)}) copy-start(f32[4096]{0:T(1024)} %param.12) | copy-start | bytes 49156
  32.1 44.0 %collective-permute-start.8 = (bf16[1024,512]{1,0:T(8,128)(2,1)}, bf16[1024,512]{1,0:T(8,128)(2,1)}, u32[]{:S(2)}, u32[]{:S(2)}) collective-permute-start(bf16[1024,512]{1,0:T(8,128)(2,1)} %refs_2_.3), channel_id=1, source_target_pairs={{0,8},{4,12},{8,0},{12,4},{16,24},{20,28},{24,16},{28,20},{1,9},{5... | collective-permute-start | bytes 3145736 | tf_op jit(solution)/shard_map/ppermute | solution.py:383
  36.7 14.9 %collective-permute-start.6 = (bf16[256,1024]{1,0:T(8,128)(2,1)S(1)}, bf16[256,1024]{1,0:T(8,128)(2,1)S(1)}, u32[]{:S(2)}, u32[]{:S(2)}) collective-permute-start(bf16[256,1024]{1,0:T(8,128)(2,1)S(1)} %get-tuple-element.44.refs_0_), channel_id=1, source_target_pairs={{0,4},{4,0},{8,12},{12,8},{16,20},{20,16},{24,28},{28,24},{1,5},{5... | collective-permute-start | bytes 1572872 | tf_op jit(solution)/shard_map/ppermute | solution.py:405
  37.3 20.3 %collective-permute-start.7 = (bf16[256,1024]{1,0:T(8,128)(2,1)S(1)}, bf16[256,1024]{1,0:T(8,128)(2,1)S(1)}, u32[]{:S(2)}, u32[]{:S(2)}) collective-permute-start(bf16[256,1024]{1,0:T(8,128)(2,1)S(1)} %get-tuple-element.45.refs_1_), channel_id=1, source_target_pairs={{0,4},{4,0},{8,12},{12,8},{16,20},{20,16},{24,28},{28,24},{1,5},{5... | collective-permute-start | bytes 1572872 | tf_op jit(solution)/shard_map/ppermute | solution.py:405
  38.8 1.1 %collective-permute-start.4 = (f32[2,128]{1,0:T(2,128)S(1)}, f32[2,128]{1,0:T(2,128)S(1)}, u32[]{:S(2)}, u32[]{:S(2)}) collective-permute-start(f32[2,128]{1,0:T(2,128)S(1)} %slice.13), channel_id=1, source_target_pairs={{0,1},{1,0},{2,3},{3,2},{4,5},{5,4},{6,7},{7,6},{8,9},{9,8},{10,11... | collective-permute-start | bytes 3080 | tf_op jit(solution)/shard_map/ppermute | solution.py:410
  39.9 3.5 %collective-permute-start.5 = (f32[1,128]{1,0:T(1,128)S(1)}, f32[1,128]{1,0:T(1,128)S(1)}, u32[]{:S(2)}, u32[]{:S(2)}) collective-permute-start(f32[1,128]{1,0:T(1,128)S(1)} %slice.15), channel_id=1, source_target_pairs={{0,2},{1,3},{2,0},{3,1},{4,6},{5,7},{6,4},{7,5},{8,10},{9,11},{10,... | collective-permute-start | bytes 1544 | tf_op jit(solution)/shard_map/ppermute | solution.py:410
  43.5 16.2 %collective-permute-start.10 = (bf16[256,512]{1,0:T(8,128)(2,1)S(1)}, bf16[256,512]{1,0:T(8,128)(2,1)S(1)}, u32[]{:S(2)}, u32[]{:S(2)}) collective-permute-start(bf16[256,512]{1,0:T(8,128)(2,1)S(1)} %get-tuple-element.46), channel_id=1, source_target_pairs={{0,1},{1,0},{2,3},{3,2},{4,5},{5,4},{6,7},{7,6},{8,9},{9,8},{10,11... | collective-permute-start | bytes 786440 | tf_op jit(solution)/shard_map/ppermute | solution.py:432
  59.5 1.8 %collective-permute-start.12 = (bf16[256,512]{1,0:T(8,128)(2,1)S(1)}, bf16[256,512]{1,0:T(8,128)(2,1)S(1)}, u32[]{:S(2)}, u32[]{:S(2)}) collective-permute-start(bf16[256,512]{1,0:T(8,128)(2,1)S(1)} %get-tuple-element.48), channel_id=1, source_target_pairs={{0,1},{1,0},{2,3},{3,2},{4,5},{5,4},{6,7},{7,6},{8,9},{9,8},{10,11... | collective-permute-start | bytes 786440 | tf_op jit(solution)/shard_map/ppermute | solution.py:432
  59.7 6.4 %collective-permute-start.11 = (bf16[128,512]{1,0:T(8,128)(2,1)S(1)}, bf16[128,512]{1,0:T(8,128)(2,1)S(1)}, u32[]{:S(2)}, u32[]{:S(2)}) collective-permute-start(bf16[128,512]{1,0:T(8,128)(2,1)S(1)} %get-tuple-element.55), channel_id=1, source_target_pairs={{0,2},{1,3},{2,0},{3,1},{4,6},{5,7},{6,4},{7,5},{8,10},{9,11},{10,... | collective-permute-start | bytes 393224 | tf_op jit(solution)/shard_map/ppermute | solution.py:432
  61.4 13.4 %collective-permute-start.13 = (bf16[128,512]{1,0:T(8,128)(2,1)S(1)}, bf16[128,512]{1,0:T(8,128)(2,1)S(1)}, u32[]{:S(2)}, u32[]{:S(2)}) collective-permute-start(bf16[128,512]{1,0:T(8,128)(2,1)S(1)} %get-tuple-element.57), channel_id=1, source_target_pairs={{0,2},{1,3},{2,0},{3,1},{4,6},{5,7},{6,4},{7,5},{8,10},{9,11},{10,... | collective-permute-start | bytes 393224 | tf_op jit(solution)/shard_map/ppermute | solution.py:432
  62.8 33.5 %collective-permute-start.19 = (bf16[1024,512]{1,0:T(8,128)(2,1)}, bf16[1024,512]{1,0:T(8,128)(2,1)S(1)}, u32[]{:S(2)}, u32[]{:S(2)}) collective-permute-start(bf16[1024,512]{1,0:T(8,128)(2,1)} %refs_2_.3), channel_id=1, source_target_pairs={{8,16},{12,20},{16,8},{20,12},{9,17},{13,21},{17,9},{21,13},{10,18... | collective-permute-start | bytes 3145736 | tf_op jit(solution)/shard_map/ppermute | solution.py:383
  74.7 23.2 %collective-permute-start.20 = (bf16[1024,512]{1,0:T(8,128)(2,1)}, bf16[1024,512]{1,0:T(8,128)(2,1)S(1)}, u32[]{:S(2)}, u32[]{:S(2)}) collective-permute-start(bf16[1024,512]{1,0:T(8,128)(2,1)} %collective-permute-done.9.refs_3_), channel_id=1, source_target_pairs={{8,0},{12,4},{16,24},{20,28},{9,1},{13,5},{17,25},{21,29},{10,2},{... | collective-permute-start | bytes 3145736 | tf_op jit(solution)/shard_map/ppermute | solution.py:383
  78.8 3.4 %collective-permute-start.14 = (bf16[256,1024]{1,0:T(8,128)(2,1)S(1)}, bf16[256,1024]{1,0:T(8,128)(2,1)S(1)}, u32[]{:S(2)}, u32[]{:S(2)}) collective-permute-start(bf16[256,1024]{1,0:T(8,128)(2,1)S(1)} %get-tuple-element.51), channel_id=1, source_target_pairs={{0,1},{1,0},{2,3},{3,2},{4,5},{5,4},{6,7},{7,6},{8,9},{9,8},{10,11... | collective-permute-start | bytes 1572872 | tf_op jit(solution)/shard_map/ppermute | solution.py:432
  81.7 2.2 %collective-permute-start.16 = (bf16[256,1024]{1,0:T(8,128)(2,1)S(1)}, bf16[256,1024]{1,0:T(8,128)(2,1)S(1)}, u32[]{:S(2)}, u32[]{:S(2)}) collective-permute-start(bf16[256,1024]{1,0:T(8,128)(2,1)S(1)} %get-tuple-element.53), channel_id=1, source_target_pairs={{0,1},{1,0},{2,3},{3,2},{4,5},{5,4},{6,7},{7,6},{8,9},{9,8},{10,11... | collective-permute-start | bytes 1572872 | tf_op jit(solution)/shard_map/ppermute | solution.py:432
  82.4 9.2 %collective-permute-start.15 = (bf16[128,1024]{1,0:T(8,128)(2,1)S(1)}, bf16[128,1024]{1,0:T(8,128)(2,1)S(1)}, u32[]{:S(2)}, u32[]{:S(2)}) collective-permute-start(bf16[128,1024]{1,0:T(8,128)(2,1)S(1)} %get-tuple-element.59), channel_id=1, source_target_pairs={{0,2},{1,3},{2,0},{3,1},{4,6},{5,7},{6,4},{7,5},{8,10},{9,11},{10,... | collective-permute-start | bytes 786440 | tf_op jit(solution)/shard_map/ppermute | solution.py:432
  84.1 12.2 %collective-permute-start.17 = (bf16[128,1024]{1,0:T(8,128)(2,1)S(1)}, bf16[128,1024]{1,0:T(8,128)(2,1)S(1)}, u32[]{:S(2)}, u32[]{:S(2)}) collective-permute-start(bf16[128,1024]{1,0:T(8,128)(2,1)S(1)} %get-tuple-element.61), channel_id=1, source_target_pairs={{0,2},{1,3},{2,0},{3,1},{4,6},{5,7},{6,4},{7,5},{8,10},{9,11},{10,... | collective-permute-start | bytes 786440 | tf_op jit(solution)/shard_map/ppermute | solution.py:432
  85.5 5.5 %collective-permute-start.18 = (bf16[128,512]{1,0:T(8,128)(2,1)S(1)}, bf16[128,512]{1,0:T(8,128)(2,1)S(1)}, u32[]{:S(2)}, u32[]{:S(2)}) collective-permute-start(bf16[128,512]{1,0:T(8,128)(2,1)S(1)} %shard_map.89), channel_id=1, source_target_pairs={{0,4},{4,0},{8,12},{12,8},{16,20},{20,16},{24,28},{28,24},{1,5},{5... | collective-permute-start | bytes 393224 | tf_op jit(solution)/shard_map/ppermute | solution.py:441
  98.7 2.0 %collective-permute-start.21 = (bf16[256,512]{1,0:T(8,128)(2,1)S(1)}, bf16[256,512]{1,0:T(8,128)(2,1)S(1)}, u32[]{:S(2)}, u32[]{:S(2)}) collective-permute-start(bf16[256,512]{1,0:T(8,128)(2,1)S(1)} %get-tuple-element.66), channel_id=1, source_target_pairs={{0,1},{1,0},{2,3},{3,2},{4,5},{5,4},{6,7},{7,6},{8,9},{9,8},{10,11... | collective-permute-start | bytes 786440 | tf_op jit(solution)/shard_map/ppermute | solution.py:432
  99.5 2.8 %collective-permute-start.24 = (bf16[256,512]{1,0:T(8,128)(2,1)S(1)}, bf16[256,512]{1,0:T(8,128)(2,1)S(1)}, u32[]{:S(2)}, u32[]{:S(2)}) collective-permute-start(bf16[256,512]{1,0:T(8,128)(2,1)S(1)} %get-tuple-element.71), channel_id=1, source_target_pairs={{0,1},{1,0},{2,3},{3,2},{4,5},{5,4},{6,7},{7,6},{8,9},{9,8},{10,11... | collective-permute-start | bytes 786440 | tf_op jit(solution)/shard_map/ppermute | solution.py:432
  100.1 9.1 %collective-permute-start.26 = (bf16[128,1024]{1,0:T(8,128)(2,1)S(1)}, bf16[128,1024]{1,0:T(8,128)(2,1)S(1)}, u32[]{:S(2)}, u32[]{:S(2)}) collective-permute-start(bf16[128,1024]{1,0:T(8,128)(2,1)S(1)} %shard_map.98), channel_id=1, source_target_pairs={{0,4},{4,0},{8,12},{12,8},{16,20},{20,16},{24,28},{28,24},{1,5},{5... | collective-permute-start | bytes 786440 | tf_op jit(solution)/shard_map/ppermute | solution.py:441
  100.7 6.5 %collective-permute-start.22 = (bf16[128,512]{1,0:T(8,128)(2,1)S(1)}, bf16[128,512]{1,0:T(8,128)(2,1)S(1)}, u32[]{:S(2)}, u32[]{:S(2)}) collective-permute-start(bf16[128,512]{1,0:T(8,128)(2,1)S(1)} %get-tuple-element.68), channel_id=1, source_target_pairs={{0,2},{1,3},{2,0},{3,1},{4,6},{5,7},{6,4},{7,5},{8,10},{9,11},{10,... | collective-permute-start | bytes 393224 | tf_op jit(solution)/shard_map/ppermute | solution.py:432
  102.4 8.6 %collective-permute-start.25 = (bf16[128,512]{1,0:T(8,128)(2,1)S(1)}, bf16[128,512]{1,0:T(8,128)(2,1)S(1)}, u32[]{:S(2)}, u32[]{:S(2)}) collective-permute-start(bf16[128,512]{1,0:T(8,128)(2,1)S(1)} %get-tuple-element.73), channel_id=1, source_target_pairs={{0,2},{1,3},{2,0},{3,1},{4,6},{5,7},{6,4},{7,5},{8,10},{9,11},{10,... | collective-permute-start | bytes 393224 | tf_op jit(solution)/shard_map/ppermute | solution.py:432
  107.2 5.0 %collective-permute-start.23 = (bf16[128,512]{1,0:T(8,128)(2,1)S(1)}, bf16[128,512]{1,0:T(8,128)(2,1)S(1)}, u32[]{:S(2)}, u32[]{:S(2)}) collective-permute-start(bf16[128,512]{1,0:T(8,128)(2,1)S(1)} %shard_map.92), channel_id=1, source_target_pairs={{0,4},{4,0},{8,12},{12,8},{16,20},{20,16},{24,28},{28,24},{1,5},{5... | collective-permute-start | bytes 393224 | tf_op jit(solution)/shard_map/ppermute | solution.py:441

commit v19 on v18

--- a/solution.py
+++ b/solution.py
@@ -332,10 +332,15 @@
     out_ref, buf, sem = refs[-3:]
     copies = []
     parts = scaled_parts(counts, width, starts_ref, squares_ref, refs[: len(counts)], total_width)
-    for at, (part, start) in enumerate(parts):
-        buf[at] = part.astype(out_ref.dtype)
-        copies.append(pltpu.make_async_copy(buf.at[at], out_ref.at[:, pl.ds(start, DH)], sem.at[at]))
-        copies[-1].start()
+    steps = width // DH
+    for at, (part, _) in enumerate(parts):
+        where = at // steps
+        buf[where, :, pl.ds(at % steps * DH, DH)] = part.astype(out_ref.dtype)
+        if at % steps == steps - 1:
+            start = pl.multiple_of(starts_ref[where], DH)
+            target = out_ref.at[:, pl.ds(start, width)]
+            copies.append(pltpu.make_async_copy(buf.at[where], target, sem.at[where]))
+            copies[-1].start()
     for copy in copies:
         copy.wait()
 
@@ -357,8 +362,8 @@
         out_specs=pl.BlockSpec(memory_space=pl.ANY),
         out_shape=out_shape,
         scratch_shapes=[
-            pltpu.VMEM((columns // DH, shape[0], DH), jnp.bfloat16),
-            pltpu.SemaphoreType.DMA((columns // DH,)),
+            pltpu.VMEM((columns // width, shape[0], width), jnp.bfloat16),
+            pltpu.SemaphoreType.DMA((columns // width,)),
         ],
         input_output_aliases={len(operands) + 1: 0},
         compiler_params=pltpu.CompilerParams(vmem_limit_bytes=VMEM_BYTES),
@@ -460,9 +465,8 @@
     returned = group(turns[1:], [0]) if inner > 1 else []
     w_ends = along(hold(w_halves, *ends), TO_ENDS)
     blocks.append((w_middle, w_ends))
+    late = group(turns[1:], [1, 2]) if inner > 1 else []
     group(turns[:1], [1, 2])
-    if inner > 1:
-        group(turns[1:], [1, 2])
     filled = placed(None, pieces, squares, width, shape, total_width) if in_kernel else None
     pins += [*ends, *returned]
     last = []
@@ -470,7 +474,7 @@
         if members:
             more, sent, _ = summed([(turn, [3]) for turn in members], pins)
             last += more
-            pins = [sent]
+            pins = [sent, *late]
     if in_kernel:
         return placed(filled, last, squares, width, shape, total_width)
     scale = lax.rsqrt(squares.reshape(out_rows, 1) / total_width + epsilon)

time: 114 us -> 114 us (level)
    ppermute x3, waiting for transfers between devices: 6.33 us -> 1.48 us  [summed(): piece = lax.ppermute(piece, 'seq', turn_pairs(n_seq, -turn))]
    ppermute x12, waiting for transfers between devices: 12 us -> 16.1 us  [summed(): got = lax.ppermute(sent, 'head', flip_pairs(n_head, bit))]
    unnamed x20 -> x24, local copies, waits for them, and re-layouts: 3.39 us -> 4.24 us
  transfers between devices with their start and end apart: 27 -> 27, of which waited for: 16 -> 15; matrix products, arithmetic and copies ran while one was open for 0% -> 0% of each run, Pallas kernels for 15% -> 16%
where the time goes in v19:
time: 114 us; the launch traced here: 113 us
  waiting for transfers between devices  51.5 us (45%)
  starting transfers between devices  35.4 us (31%)
  Pallas kernels  21.4 us (19%)
  local copies, waits for them, and re-layouts  4.43 us (4%)
    pallas_call x27, Pallas kernels, local_call(): pl.pallas_call(kernel, in_specs=[pl.BlockSpec(memory_space=pltpu.SMEM)] +...  20 us
    ppermute x12, waiting for transfers between devices, summed(): got = lax.ppermute(sent, 'head', flip_pairs(n_head, bit))  16.1 us
    ppermute x4, waiting for transfers between devices, along(): return lax.ppermute(value, 'seq', line_pairs(n_seq, hops))  10.3 us
    ppermute x12, starting transfers between devices, summed(): got = lax.ppermute(sent, 'head', flip_pairs(n_head, bit))  9.86 us
    ppermute x4, starting transfers between devices, along(): return lax.ppermute(value, 'seq', line_pairs(n_seq, hops))  8.27 us
    ppermute x1, waiting for transfers between devices, shards(): lax.ppermute(kept_rows, 'seq', pairs)  8.13 us
    ppermute x1, waiting for transfers between devices, shards(): lax.ppermute(sent_rows, 'seq', pairs)  6.03 us
    ppermute x1, starting transfers between devices, state_prefix(): from_half = lax.ppermute(second, 'seq', line_pairs(n_seq, [(0, 2), (1, 3)]))  5.39 us
  transfers between devices with their start and end apart: 27, of which 15 were waited for; matrix products, arithmetic and copies ran while one was open for 0% of the time, Pallas kernels for 16%

profile of v19, /device:TPU:0, one launch (start us, length us, event | category | flops | bytes accessed | tf_op | source)
XLA Modules:
  0.0 113.2 jit_solution(7138119647978478964)
XLA Ops:
  0.0 1.2 %copy-done = bf16[512,1024]{1,0:T(8,128)(2,1)S(1)} copy-done((bf16[512,1024]{1,0:T(8,128)(2,1)S(1)}, bf16[512,1024]{1,0:T(8,128)(2,1)}, u32[]{:S(2)}) %copy-start) | copy-done | bytes 1048600
  1.2 1.2 %copy-done.2 = bf16[512,1024]{1,0:T(8,128)(2,1)S(1)} copy-done((bf16[512,1024]{1,0:T(8,128)(2,1)S(1)}, bf16[512,1024]{1,0:T(8,128)(2,1)}, u32[]{:S(2)}) %copy-start.2) | copy-done | bytes 1048600
  2.5 0.5 shard_map.74
  2.9 3.0 %collective-permute-start = (bf16[4,128,128]{2,1,0:T(8,128)(2,1)S(1)}, bf16[4,128,128]{2,1,0:T(8,128)(2,1)S(1)}, u32[]{:S(2)}, u32[]{:S(2)}) collective-permute-start(bf16[4,128,128]{2,1,0:T(8,128)(2,1)S(1)} %shard_map.74), channel_id=1, source_target_pairs={{0,4},{4,0},{8,12},{12,8},{16,20},{20,16},{24,28},{28,24},{1,5},{5... | collective-permute-start | bytes 393224 | tf_op jit(solution)/shard_map/ppermute | solution.py:124
  6.0 0.5 shard_map.73.refs_0_.refs_2_
  6.4 3.0 %collective-permute-done.refs_1_.refs_3_ = bf16[4,128,128]{2,1,0:T(8,128)(2,1)S(1)} collective-permute-done((bf16[4,128,128]{2,1,0:T(8,128)(2,1)S(1)}, bf16[4,128,128]{2,1,0:T(8,128)(2,1)S(1)}, u32[]{:S(2)}, u32[]{:S(2)}) %collective-permute-start) | collective-permute-done | bytes 131104 | tf_op jit(solution)/shard_map/ppermute | solution.py:124
  9.5 1.9 %collective-permute-start.1 = (bf16[4,128,128]{2,1,0:T(8,128)(2,1)S(1)}, bf16[4,128,128]{2,1,0:T(8,128)(2,1)S(1)}, u32[]{:S(2)}, u32[]{:S(2)}) collective-permute-start(bf16[4,128,128]{2,1,0:T(8,128)(2,1)S(1)} %shard_map.75), channel_id=1, source_target_pairs={{0,8},{4,12},{8,0},{12,4},{16,24},{20,28},{24,16},{28,20},{1,9},{5... | collective-permute-start | bytes 393224 | tf_op jit(solution)/shard_map/ppermute | solution.py:127
  11.4 3.1 %collective-permute-done.1.refs_2_.refs_1_ = bf16[4,128,128]{2,1,0:T(8,128)(2,1)S(1)} collective-permute-done((bf16[4,128,128]{2,1,0:T(8,128)(2,1)S(1)}, bf16[4,128,128]{2,1,0:T(8,128)(2,1)S(1)}, u32[]{:S(2)}, u32[]{:S(2)}) %collective-permute-start.1) | collective-permute-done | bytes 131104 | tf_op jit(solution)/shard_map/ppermute | solution.py:127
  14.5 0.7 shard_map.76
  15.2 5.4 %collective-permute-start.2 = (bf16[4,128,128]{2,1,0:T(8,128)(2,1)}, bf16[4,128,128]{2,1,0:T(8,128)(2,1)}, u32[]{:S(2)}, u32[]{:S(2)}) collective-permute-start(bf16[4,128,128]{2,1,0:T(8,128)(2,1)} %shard_map.76), channel_id=1, source_target_pairs={{0,16},{4,20},{8,24},{12,28},{1,17},{5,21},{9,25},{13,29},{2,18},{... | collective-permute-start | bytes 393224 | tf_op jit(solution)/shard_map/ppermute | solution.py:129
  20.6 0.1 stack.81
  20.7 2.1 %collective-permute-done.2.refs_0_ = bf16[4,128,128]{2,1,0:T(8,128)(2,1)} collective-permute-done((bf16[4,128,128]{2,1,0:T(8,128)(2,1)}, bf16[4,128,128]{2,1,0:T(8,128)(2,1)}, u32[]{:S(2)}, u32[]{:S(2)}) %collective-permute-start.2) | collective-permute-done | bytes 131104 | tf_op jit(solution)/shard_map/ppermute | solution.py:129
  22.8 0.9 copy-done.7
  23.7 1.1 shard_map.77
  24.8 1.6 %collective-permute-start.3 = (bf16[4,128,128]{2,1,0:T(8,128)(2,1)S(1)}, bf16[4,128,128]{2,1,0:T(8,128)(2,1)S(1)}, u32[]{:S(2)}, u32[]{:S(2)}) collective-permute-start(bf16[4,128,128]{2,1,0:T(8,128)(2,1)S(1)} %get-tuple-element.42), channel_id=1, source_target_pairs={{0,4},{4,0},{8,12},{12,8},{16,20},{20,16},{24,28},{28,24},{1,5},{5... | collective-permute-start | bytes 393224 | tf_op jit(solution)/shard_map/ppermute | solution.py:137
  26.3 0.1 pad_add_fusion.1.place_ref
  26.4 3.4 %collective-permute-start.9 = (bf16[1024,512]{1,0:T(8,128)(2,1)}, bf16[1024,512]{1,0:T(8,128)(2,1)}, u32[]{:S(2)}, u32[]{:S(2)}) collective-permute-start(bf16[1024,512]{1,0:T(8,128)(2,1)} %refs_2_.3), channel_id=1, source_target_pairs={{0,16},{4,20},{8,24},{12,28},{16,0},{20,4},{24,8},{28,12},{1,17},{... | collective-permute-start | bytes 3145736 | tf_op jit(solution)/shard_map/ppermute | solution.py:388
  29.9 1.1 shard_map.78.refs_2_
  31.0 2.8 %collective-permute-start.8 = (bf16[1024,512]{1,0:T(8,128)(2,1)}, bf16[1024,512]{1,0:T(8,128)(2,1)}, u32[]{:S(2)}, u32[]{:S(2)}) collective-permute-start(bf16[1024,512]{1,0:T(8,128)(2,1)} %refs_2_.3), channel_id=1, source_target_pairs={{0,8},{4,12},{8,0},{12,4},{16,24},{20,28},{24,16},{28,20},{1,9},{5... | collective-permute-start | bytes 3145736 | tf_op jit(solution)/shard_map/ppermute | solution.py:388
  33.8 1.1 shard_map.79.refs_3_
  34.9 1.8 %shard_map.80 = (bf16[256,1024]{1,0:T(8,128)(2,1)S(1)}, bf16[256,1024]{1,0:T(8,128)(2,1)S(1)}, f32[4,128]{1,0:T(4,128)S(1)}) custom-call(s32[2]{0:T(128)S(1)} %pad_add_fusion.1.place_ref, bf16[512,1024]{1,0:T(8,128)(2,1)S(1)} %copy-done.4, bf16[512,1024]{1,0:T(8,128)(2,1)S(1)} %copy-done.5, f32[32,1,128]{2,1,0:T(1,128)S(1)} %bitcast.17, ...), custom_call_target="tpu_custom_call" | custom-call | flops 268435456 | bytes 6178816 | tf_op jit(solution)/shard_map/pallas_call | solution.py:49
  36.7 0.6 collective-permute-start.6
  37.3 1.5 %collective-permute-start.7 = (bf16[256,1024]{1,0:T(8,128)(2,1)S(1)}, bf16[256,1024]{1,0:T(8,128)(2,1)S(1)}, u32[]{:S(2)}, u32[]{:S(2)}) collective-permute-start(bf16[256,1024]{1,0:T(8,128)(2,1)S(1)} %get-tuple-element.45.refs_1_), channel_id=1, source_target_pairs={{0,4},{4,0},{8,12},{12,8},{16,20},{20,16},{24,28},{28,24},{1,5},{5... | collective-permute-start | bytes 1572872 | tf_op jit(solution)/shard_map/ppermute | solution.py:410
  38.8 1.1 %collective-permute-done.4 = f32[2,128]{1,0:T(2,128)S(1)} collective-permute-done((f32[2,128]{1,0:T(2,128)S(1)}, f32[2,128]{1,0:T(2,128)S(1)}, u32[]{:S(2)}, u32[]{:S(2)}) %collective-permute-start.4) | collective-permute-done | bytes 1056 | tf_op jit(solution)/shard_map/ppermute | solution.py:415
  39.9 1.5 %collective-permute-start.5 = (f32[1,128]{1,0:T(1,128)S(1)}, f32[1,128]{1,0:T(1,128)S(1)}, u32[]{:S(2)}, u32[]{:S(2)}) collective-permute-start(f32[1,128]{1,0:T(1,128)S(1)} %slice.15), channel_id=1, source_target_pairs={{0,2},{1,3},{2,0},{3,1},{4,6},{5,7},{6,4},{7,5},{8,10},{9,11},{10,... | collective-permute-start | bytes 1544 | tf_op jit(solution)/shard_map/ppermute | solution.py:415
  41.5 1.9 %shard_map.81 = (bf16[256,512]{1,0:T(8,128)(2,1)S(1)}, f32[256,512]{1,0:T(8,128)S(1)}) custom-call(s32[1]{0:T(128)} %bitcast.10.flag_ref, bf16[256,1024]{1,0:T(8,128)(2,1)S(1)} %get-tuple-element.44.refs_0_, bf16[256,1024]{1,0:T(8,128)(2,1)S(1)} %get-tuple-element.45.refs_1_, bf16[1024,512]{1,0:T(8,128)(2,1)} %refs_2_.3), custom_call_target="tpu_custom_call" | custom-call | flops 536870912 | bytes 2883584 | tf_op jit(solution)/shard_map/pallas_call | solution.py:49
  43.4 0.1 collective-permute-done.5
  43.5 8.1 %collective-permute-done.6.refs_0_ = bf16[256,1024]{1,0:T(8,128)(2,1)S(1)} collective-permute-done((bf16[256,1024]{1,0:T(8,128)(2,1)S(1)}, bf16[256,1024]{1,0:T(8,128)(2,1)S(1)}, u32[]{:S(2)}, u32[]{:S(2)}) %collective-permute-start.6) | collective-permute-done | bytes 524320 | tf_op jit(solution)/shard_map/ppermute | solution.py:410
  51.6 6.0 %collective-permute-done.7.refs_1_ = bf16[256,1024]{1,0:T(8,128)(2,1)S(1)} collective-permute-done((bf16[256,1024]{1,0:T(8,128)(2,1)S(1)}, bf16[256,1024]{1,0:T(8,128)(2,1)S(1)}, u32[]{:S(2)}, u32[]{:S(2)}) %collective-permute-start.7) | collective-permute-done | bytes 524320 | tf_op jit(solution)/shard_map/ppermute | solution.py:410
  57.6 1.9 %shard_map.82 = (bf16[256,512]{1,0:T(8,128)(2,1)S(1)}, f32[256,512]{1,0:T(8,128)S(1)}) custom-call(s32[1]{0:T(128)} %bitcast.10.flag_ref, bf16[256,1024]{1,0:T(8,128)(2,1)S(1)} %collective-permute-done.6.refs_0_, bf16[256,1024]{1,0:T(8,128)(2,1)S(1)} %collective-permute-done.7.refs_1_, bf16[1024,512]{1,0:T(8,128)(2,1)} %refs_2_.3), custom_call_target="tpu_custom_call" | custom-call | flops 536870912 | bytes 2883584 | tf_op jit(solution)/shard_map/pallas_call | solution.py:49
  59.7 1.6 %collective-permute-start.11 = (bf16[128,512]{1,0:T(8,128)(2,1)S(1)}, bf16[128,512]{1,0:T(8,128)(2,1)S(1)}, u32[]{:S(2)}, u32[]{:S(2)}) collective-permute-start(bf16[128,512]{1,0:T(8,128)(2,1)S(1)} %get-tuple-element.55), channel_id=1, source_target_pairs={{0,2},{1,3},{2,0},{3,1},{4,6},{5,7},{6,4},{7,5},{8,10},{9,11},{10,... | collective-permute-start | bytes 393224 | tf_op jit(solution)/shard_map/ppermute | solution.py:437
  61.4 1.4 %collective-permute-start.13 = (bf16[128,512]{1,0:T(8,128)(2,1)S(1)}, bf16[128,512]{1,0:T(8,128)(2,1)S(1)}, u32[]{:S(2)}, u32[]{:S(2)}) collective-permute-start(bf16[128,512]{1,0:T(8,128)(2,1)S(1)} %get-tuple-element.57), channel_id=1, source_target_pairs={{0,2},{1,3},{2,0},{3,1},{4,6},{5,7},{6,4},{7,5},{8,10},{9,11},{10,... | collective-permute-start | bytes 393224 | tf_op jit(solution)/shard_map/ppermute | solution.py:437
  62.8 0.7 collective-permute-start.19
  63.5 2.5 %collective-permute-done.11.got_ref = bf16[128,512]{1,0:T(8,128)(2,1)S(1)} collective-permute-done((bf16[128,512]{1,0:T(8,128)(2,1)S(1)}, bf16[128,512]{1,0:T(8,128)(2,1)S(1)}, u32[]{:S(2)}, u32[]{:S(2)}) %collective-permute-start.11) | collective-permute-done | bytes 131104 | tf_op jit(solution)/shard_map/ppermute | solution.py:437
  66.1 8.7 %collective-permute-done.9.refs_3_ = bf16[1024,512]{1,0:T(8,128)(2,1)} collective-permute-done((bf16[1024,512]{1,0:T(8,128)(2,1)}, bf16[1024,512]{1,0:T(8,128)(2,1)}, u32[]{:S(2)}, u32[]{:S(2)}) %collective-permute-start.9) | collective-permute-done | bytes 1048608 | tf_op jit(solution)/shard_map/ppermute | solution.py:388
  74.8 1.3 %collective-permute-start.20 = (bf16[1024,512]{1,0:T(8,128)(2,1)}, bf16[1024,512]{1,0:T(8,128)(2,1)S(1)}, u32[]{:S(2)}, u32[]{:S(2)}) collective-permute-start(bf16[1024,512]{1,0:T(8,128)(2,1)} %collective-permute-done.9.refs_3_), channel_id=1, source_target_pairs={{8,0},{12,4},{16,24},{20,28},{9,1},{13,5},{17,25},{21,29},{10,2},{... | collective-permute-start | bytes 3145736 | tf_op jit(solution)/shard_map/ppermute | solution.py:388
  76.1 2.8 %shard_map.83 = (bf16[256,1024]{1,0:T(8,128)(2,1)S(1)}, f32[256,1024]{1,0:T(8,128)S(1)}) custom-call(s32[1]{0:T(128)} %bitcast.10.flag_ref, bf16[256,1024]{1,0:T(8,128)(2,1)S(1)} %collective-permute-done.6.refs_0_, bf16[256,1024]{1,0:T(8,128)(2,1)S(1)} %collective-permute-done.7.refs_1_, bf16[1024,512]{1,0:T(8,128)(2,1)} %collective-permute-done.8.refs_2_, ...), custom_call_target="tpu_custom_call" | custom-call | flops 1073741824 | bytes 4718592 | tf_op jit(solution)/shard_map/pallas_call | solution.py:49
  78.8 0.1 collective-permute-start.14
  78.9 2.8 %shard_map.84 = (bf16[256,1024]{1,0:T(8,128)(2,1)S(1)}, f32[256,1024]{1,0:T(8,128)S(1)}) custom-call(s32[1]{0:T(128)} %bitcast.10.flag_ref, bf16[256,1024]{1,0:T(8,128)(2,1)S(1)} %get-tuple-element.44.refs_0_, bf16[256,1024]{1,0:T(8,128)(2,1)S(1)} %get-tuple-element.45.refs_1_, bf16[1024,512]{1,0:T(8,128)(2,1)} %collective-permute-done.8.refs_2_, ...), custom_call_target="tpu_custom_call" | custom-call | flops 1073741824 | bytes 4718592 | tf_op jit(solution)/shard_map/pallas_call | solution.py:49
  81.7 0.6 collective-permute-start.16
  82.3 0.1 shard_map.87
  82.4 1.6 %collective-permute-start.15 = (bf16[128,1024]{1,0:T(8,128)(2,1)S(1)}, bf16[128,1024]{1,0:T(8,128)(2,1)S(1)}, u32[]{:S(2)}, u32[]{:S(2)}) collective-permute-start(bf16[128,1024]{1,0:T(8,128)(2,1)S(1)} %get-tuple-element.59), channel_id=1, source_target_pairs={{0,2},{1,3},{2,0},{3,1},{4,6},{5,7},{6,4},{7,5},{8,10},{9,11},{10,... | collective-permute-start | bytes 786440 | tf_op jit(solution)/shard_map/ppermute | solution.py:437
  84.0 0.1 shard_map.88
  84.1 1.5 %collective-permute-start.17 = (bf16[128,1024]{1,0:T(8,128)(2,1)S(1)}, bf16[128,1024]{1,0:T(8,128)(2,1)S(1)}, u32[]{:S(2)}, u32[]{:S(2)}) collective-permute-start(bf16[128,1024]{1,0:T(8,128)(2,1)S(1)} %get-tuple-element.61), channel_id=1, source_target_pairs={{0,2},{1,3},{2,0},{3,1},{4,6},{5,7},{6,4},{7,5},{8,10},{9,11},{10,... | collective-permute-start | bytes 786440 | tf_op jit(solution)/shard_map/ppermute | solution.py:437
  85.5 0.6 collective-permute-start.18
  86.1 5.5 %collective-permute-done.15.got_ref = bf16[128,1024]{1,0:T(8,128)(2,1)S(1)} collective-permute-done((bf16[128,1024]{1,0:T(8,128)(2,1)S(1)}, bf16[128,1024]{1,0:T(8,128)(2,1)S(1)}, u32[]{:S(2)}, u32[]{:S(2)}) %collective-permute-start.15) | collective-permute-done | bytes 262176 | tf_op jit(solution)/shard_map/ppermute | solution.py:437
  91.7 0.6 collective-permute-start.24
  92.3 4.0 %collective-permute-done.17.got_ref = bf16[128,1024]{1,0:T(8,128)(2,1)S(1)} collective-permute-done((bf16[128,1024]{1,0:T(8,128)(2,1)S(1)}, bf16[128,1024]{1,0:T(8,128)(2,1)S(1)}, u32[]{:S(2)}, u32[]{:S(2)}) %collective-permute-start.17) | collective-permute-done | bytes 262176 | tf_op jit(solution)/shard_map/ppermute | solution.py:437
  96.3 1.6 %collective-permute-done.20.refs_3_ = bf16[1024,512]{1,0:T(8,128)(2,1)S(1)} collective-permute-done((bf16[1024,512]{1,0:T(8,128)(2,1)}, bf16[1024,512]{1,0:T(8,128)(2,1)S(1)}, u32[]{:S(2)}, u32[]{:S(2)}) %collective-permute-start.20) | collective-permute-done | bytes 1048608 | tf_op jit(solution)/shard_map/ppermute | solution.py:388
  97.9 0.7 shard_map.90
  98.7 0.1 collective-permute-start.21
  98.8 0.7 shard_map.94
  99.5 0.5 collective-permute-start.25
  100.0 0.2 collective-permute-done.21.got_ref
  100.3 1.6 %collective-permute-start.22 = (bf16[128,512]{1,0:T(8,128)(2,1)S(1)}, bf16[128,512]{1,0:T(8,128)(2,1)S(1)}, u32[]{:S(2)}, u32[]{:S(2)}) collective-permute-start(bf16[128,512]{1,0:T(8,128)(2,1)S(1)} %get-tuple-element.68), channel_id=1, source_target_pairs={{0,2},{1,3},{2,0},{3,1},{4,6},{5,7},{6,4},{7,5},{8,10},{9,11},{10,... | collective-permute-start | bytes 393224 | tf_op jit(solution)/shard_map/ppermute | solution.py:437
  102.0 0.9 collective-permute-start.26
  102.9 3.9 %collective-permute-done.22.got_ref = bf16[128,512]{1,0:T(8,128)(2,1)S(1)} collective-permute-done((bf16[128,512]{1,0:T(8,128)(2,1)S(1)}, bf16[128,512]{1,0:T(8,128)(2,1)S(1)}, u32[]{:S(2)}, u32[]{:S(2)}) %collective-permute-start.22) | collective-permute-done | bytes 131104 | tf_op jit(solution)/shard_map/ppermute | solution.py:437
  106.8 0.6 collective-permute-start.23
  107.4 0.1 stack.92.starts_ref
  107.4 0.1 pad_add_fusion.starts_ref
  107.6 0.8 copy-done.10
  108.5 1.8 %shard_map.99.refs_2_ = bf16[128,4096]{1,0:T(8,128)(2,1)} custom-call(s32[6]{0:T(128)S(1)} %stack.92.starts_ref, f32[1,128]{1,0:T(1,128)S(1)} %slice_add_fusion.1.squares_ref, bf16[128,512]{1,0:T(8,128)(2,1)S(1)} %shard_map.97.refs_0_, bf16[128,512]{1,0:T(8,128)(2,1)S(1)} %copy-done.10, bf16[128,1024]{1,0:T(8,128)(2,1)S(1)} %collective-permute-done.24.refs_2_, ...), custom_call_target="tpu_custom_call" | custom-call | bytes 1835520 | tf_op jit(solution)/shard_map/pallas_call | solution.py:49
  110.3 1.5 %collective-permute-done.23.refs_0_ = bf16[128,512]{1,0:T(8,128)(2,1)S(1)} collective-permute-done((bf16[128,512]{1,0:T(8,128)(2,1)S(1)}, bf16[128,512]{1,0:T(8,128)(2,1)S(1)}, u32[]{:S(2)}, u32[]{:S(2)}) %collective-permute-start.23) | collective-permute-done | bytes 131104 | tf_op jit(solution)/shard_map/ppermute | solution.py:446
  111.8 1.4 %shard_map.100 = bf16[128,4096]{1,0:T(8,128)(2,1)} custom-call(s32[2]{0:T(128)S(1)} %pad_add_fusion.starts_ref, f32[1,128]{1,0:T(1,128)S(1)} %slice_add_fusion.1.squares_ref, bf16[128,512]{1,0:T(8,128)(2,1)S(1)} %collective-permute-done.23.refs_0_, bf16[128,512]{1,0:T(8,128)(2,1)S(1)} %shard_map.96.refs_1_, ...), custom_call_target="tpu_custom_call", output_to_operand_aliasing={{}: (4, {})} | custom-call | bytes 524288 | tf_op jit(solution)/shard_map/pallas_call | solution.py:357
  (51 shorter events, 0.6 us)
Async XLA Ops:
  0.0 1.2 %copy-start = (bf16[512,1024]{1,0:T(8,128)(2,1)S(1)}, bf16[512,1024]{1,0:T(8,128)(2,1)}, u32[]{:S(2)}) copy-start(bf16[512,1024]{1,0:T(8,128)(2,1)} %k_ref.7) | copy-start | bytes 3145732
  1.2 1.2 %copy-start.2 = (bf16[512,1024]{1,0:T(8,128)(2,1)S(1)}, bf16[512,1024]{1,0:T(8,128)(2,1)}, u32[]{:S(2)}) copy-start(bf16[512,1024]{1,0:T(8,128)(2,1)} %v_ref.7) | copy-start | bytes 3145732
  2.5 3.5 %copy-start.1 = (bf16[512,1024]{1,0:T(8,128)(2,1)S(1)}, bf16[512,1024]{1,0:T(8,128)(2,1)}, u32[]{:S(2)}) copy-start(bf16[512,1024]{1,0:T(8,128)(2,1)} %k_ref.7) | copy-start | bytes 3145732
  2.9 6.5 %collective-permute-start = (bf16[4,128,128]{2,1,0:T(8,128)(2,1)S(1)}, bf16[4,128,128]{2,1,0:T(8,128)(2,1)S(1)}, u32[]{:S(2)}, u32[]{:S(2)}) collective-permute-start(bf16[4,128,128]{2,1,0:T(8,128)(2,1)S(1)} %shard_map.74), channel_id=1, source_target_pairs={{0,4},{4,0},{8,12},{12,8},{16,20},{20,16},{24,28},{28,24},{1,5},{5... | collective-permute-start | bytes 393224 | tf_op jit(solution)/shard_map/ppermute | solution.py:124
  5.9 23.9 %copy-start.4 = (bf16[512,1024]{1,0:T(8,128)(2,1)S(1)}, bf16[512,1024]{1,0:T(8,128)(2,1)}, u32[]{:S(2)}) copy-start(bf16[512,1024]{1,0:T(8,128)(2,1)} %q_ref.5) | copy-start | bytes 3145732
  6.4 23.4 %copy-start.3 = (bf16[512,1024]{1,0:T(8,128)(2,1)S(1)}, bf16[512,1024]{1,0:T(8,128)(2,1)}, u32[]{:S(2)}) copy-start(bf16[512,1024]{1,0:T(8,128)(2,1)} %v_ref.7) | copy-start | bytes 3145732
  9.5 5.0 %collective-permute-start.1 = (bf16[4,128,128]{2,1,0:T(8,128)(2,1)S(1)}, bf16[4,128,128]{2,1,0:T(8,128)(2,1)S(1)}, u32[]{:S(2)}, u32[]{:S(2)}) collective-permute-start(bf16[4,128,128]{2,1,0:T(8,128)(2,1)S(1)} %shard_map.75), channel_id=1, source_target_pairs={{0,8},{4,12},{8,0},{12,4},{16,24},{20,28},{24,16},{28,20},{1,9},{5... | collective-permute-start | bytes 393224 | tf_op jit(solution)/shard_map/ppermute | solution.py:127
  14.5 0.7 copy-start.6
  15.2 7.6 %collective-permute-start.2 = (bf16[4,128,128]{2,1,0:T(8,128)(2,1)}, bf16[4,128,128]{2,1,0:T(8,128)(2,1)}, u32[]{:S(2)}, u32[]{:S(2)}) collective-permute-start(bf16[4,128,128]{2,1,0:T(8,128)(2,1)} %shard_map.76), channel_id=1, source_target_pairs={{0,16},{4,20},{8,24},{12,28},{1,17},{5,21},{9,25},{13,29},{2,18},{... | collective-permute-start | bytes 393224 | tf_op jit(solution)/shard_map/ppermute | solution.py:129
  22.8 0.9 copy-start.7
  24.8 10.1 %collective-permute-start.3 = (bf16[4,128,128]{2,1,0:T(8,128)(2,1)S(1)}, bf16[4,128,128]{2,1,0:T(8,128)(2,1)S(1)}, u32[]{:S(2)}, u32[]{:S(2)}) collective-permute-start(bf16[4,128,128]{2,1,0:T(8,128)(2,1)S(1)} %get-tuple-element.42), channel_id=1, source_target_pairs={{0,4},{4,0},{8,12},{12,8},{16,20},{20,16},{24,28},{28,24},{1,5},{5... | collective-permute-start | bytes 393224 | tf_op jit(solution)/shard_map/ppermute | solution.py:137
  26.4 48.3 %collective-permute-start.9 = (bf16[1024,512]{1,0:T(8,128)(2,1)}, bf16[1024,512]{1,0:T(8,128)(2,1)}, u32[]{:S(2)}, u32[]{:S(2)}) collective-permute-start(bf16[1024,512]{1,0:T(8,128)(2,1)} %refs_2_.3), channel_id=1, source_target_pairs={{0,16},{4,20},{8,24},{12,28},{16,0},{20,4},{24,8},{28,12},{1,17},{... | collective-permute-start | bytes 3145736 | tf_op jit(solution)/shard_map/ppermute | solution.py:388
  30.9 4.0 %copy-start.5 = (bf16[512,1024]{1,0:T(8,128)(2,1)S(1)}, bf16[512,1024]{1,0:T(8,128)(2,1)}, u32[]{:S(2)}) copy-start(bf16[512,1024]{1,0:T(8,128)(2,1)} %gate_ref.1) | copy-start | bytes 3145732
  31.0 4.0 %copy-start.8 = (f32[8,128,128]{2,1,0:T(8,128)S(1)}, f32[8,128,128]{2,1,0:T(8,128)}, u32[]{:S(2)}) copy-start(f32[8,128,128]{2,1,0:T(8,128)} %kv_ref.1) | copy-start | bytes 1572868
  31.0 4.0 %copy-start.11 = (f32[4096]{0:T(1024)S(1)}, f32[4096]{0:T(1024)}, u32[]{:S(2)}) copy-start(f32[4096]{0:T(1024)} %param.12) | copy-start | bytes 49156
  31.0 45.1 %collective-permute-start.8 = (bf16[1024,512]{1,0:T(8,128)(2,1)}, bf16[1024,512]{1,0:T(8,128)(2,1)}, u32[]{:S(2)}, u32[]{:S(2)}) collective-permute-start(bf16[1024,512]{1,0:T(8,128)(2,1)} %refs_2_.3), channel_id=1, source_target_pairs={{0,8},{4,12},{8,0},{12,4},{16,24},{20,28},{24,16},{28,20},{1,9},{5... | collective-permute-start | bytes 3145736 | tf_op jit(solution)/shard_map/ppermute | solution.py:388
  36.7 14.9 %collective-permute-start.6 = (bf16[256,1024]{1,0:T(8,128)(2,1)S(1)}, bf16[256,1024]{1,0:T(8,128)(2,1)S(1)}, u32[]{:S(2)}, u32[]{:S(2)}) collective-permute-start(bf16[256,1024]{1,0:T(8,128)(2,1)S(1)} %get-tuple-element.44.refs_0_), channel_id=1, source_target_pairs={{0,4},{4,0},{8,12},{12,8},{16,20},{20,16},{24,28},{28,24},{1,5},{5... | collective-permute-start | bytes 1572872 | tf_op jit(solution)/shard_map/ppermute | solution.py:410
  37.3 20.4 %collective-permute-start.7 = (bf16[256,1024]{1,0:T(8,128)(2,1)S(1)}, bf16[256,1024]{1,0:T(8,128)(2,1)S(1)}, u32[]{:S(2)}, u32[]{:S(2)}) collective-permute-start(bf16[256,1024]{1,0:T(8,128)(2,1)S(1)} %get-tuple-element.45.refs_1_), channel_id=1, source_target_pairs={{0,4},{4,0},{8,12},{12,8},{16,20},{20,16},{24,28},{28,24},{1,5},{5... | collective-permute-start | bytes 1572872 | tf_op jit(solution)/shard_map/ppermute | solution.py:410
  38.8 1.1 %collective-permute-start.4 = (f32[2,128]{1,0:T(2,128)S(1)}, f32[2,128]{1,0:T(2,128)S(1)}, u32[]{:S(2)}, u32[]{:S(2)}) collective-permute-start(f32[2,128]{1,0:T(2,128)S(1)} %slice.13), channel_id=1, source_target_pairs={{0,1},{1,0},{2,3},{3,2},{4,5},{5,4},{6,7},{7,6},{8,9},{9,8},{10,11... | collective-permute-start | bytes 3080 | tf_op jit(solution)/shard_map/ppermute | solution.py:415
  39.9 3.5 %collective-permute-start.5 = (f32[1,128]{1,0:T(1,128)S(1)}, f32[1,128]{1,0:T(1,128)S(1)}, u32[]{:S(2)}, u32[]{:S(2)}) collective-permute-start(f32[1,128]{1,0:T(1,128)S(1)} %slice.15), channel_id=1, source_target_pairs={{0,2},{1,3},{2,0},{3,1},{4,6},{5,7},{6,4},{7,5},{8,10},{9,11},{10,... | collective-permute-start | bytes 1544 | tf_op jit(solution)/shard_map/ppermute | solution.py:415
  43.5 16.2 %collective-permute-start.10 = (bf16[256,512]{1,0:T(8,128)(2,1)S(1)}, bf16[256,512]{1,0:T(8,128)(2,1)S(1)}, u32[]{:S(2)}, u32[]{:S(2)}) collective-permute-start(bf16[256,512]{1,0:T(8,128)(2,1)S(1)} %get-tuple-element.46), channel_id=1, source_target_pairs={{0,1},{1,0},{2,3},{3,2},{4,5},{5,4},{6,7},{7,6},{8,9},{9,8},{10,11... | collective-permute-start | bytes 786440 | tf_op jit(solution)/shard_map/ppermute | solution.py:437
  59.6 1.7 %collective-permute-start.12 = (bf16[256,512]{1,0:T(8,128)(2,1)S(1)}, bf16[256,512]{1,0:T(8,128)(2,1)S(1)}, u32[]{:S(2)}, u32[]{:S(2)}) collective-permute-start(bf16[256,512]{1,0:T(8,128)(2,1)S(1)} %get-tuple-element.48), channel_id=1, source_target_pairs={{0,1},{1,0},{2,3},{3,2},{4,5},{5,4},{6,7},{7,6},{8,9},{9,8},{10,11... | collective-permute-start | bytes 786440 | tf_op jit(solution)/shard_map/ppermute | solution.py:437
  59.7 6.4 %collective-permute-start.11 = (bf16[128,512]{1,0:T(8,128)(2,1)S(1)}, bf16[128,512]{1,0:T(8,128)(2,1)S(1)}, u32[]{:S(2)}, u32[]{:S(2)}) collective-permute-start(bf16[128,512]{1,0:T(8,128)(2,1)S(1)} %get-tuple-element.55), channel_id=1, source_target_pairs={{0,2},{1,3},{2,0},{3,1},{4,6},{5,7},{6,4},{7,5},{8,10},{9,11},{10,... | collective-permute-start | bytes 393224 | tf_op jit(solution)/shard_map/ppermute | solution.py:437
  61.4 13.4 %collective-permute-start.13 = (bf16[128,512]{1,0:T(8,128)(2,1)S(1)}, bf16[128,512]{1,0:T(8,128)(2,1)S(1)}, u32[]{:S(2)}, u32[]{:S(2)}) collective-permute-start(bf16[128,512]{1,0:T(8,128)(2,1)S(1)} %get-tuple-element.57), channel_id=1, source_target_pairs={{0,2},{1,3},{2,0},{3,1},{4,6},{5,7},{6,4},{7,5},{8,10},{9,11},{10,... | collective-permute-start | bytes 393224 | tf_op jit(solution)/shard_map/ppermute | solution.py:437
  62.8 33.5 %collective-permute-start.19 = (bf16[1024,512]{1,0:T(8,128)(2,1)}, bf16[1024,512]{1,0:T(8,128)(2,1)S(1)}, u32[]{:S(2)}, u32[]{:S(2)}) collective-permute-start(bf16[1024,512]{1,0:T(8,128)(2,1)} %refs_2_.3), channel_id=1, source_target_pairs={{8,16},{12,20},{16,8},{20,12},{9,17},{13,21},{17,9},{21,13},{10,18... | collective-permute-start | bytes 3145736 | tf_op jit(solution)/shard_map/ppermute | solution.py:388
  74.8 23.2 %collective-permute-start.20 = (bf16[1024,512]{1,0:T(8,128)(2,1)}, bf16[1024,512]{1,0:T(8,128)(2,1)S(1)}, u32[]{:S(2)}, u32[]{:S(2)}) collective-permute-start(bf16[1024,512]{1,0:T(8,128)(2,1)} %collective-permute-done.9.refs_3_), channel_id=1, source_target_pairs={{8,0},{12,4},{16,24},{20,28},{9,1},{13,5},{17,25},{21,29},{10,2},{... | collective-permute-start | bytes 3145736 | tf_op jit(solution)/shard_map/ppermute | solution.py:388
  78.8 3.4 %collective-permute-start.14 = (bf16[256,1024]{1,0:T(8,128)(2,1)S(1)}, bf16[256,1024]{1,0:T(8,128)(2,1)S(1)}, u32[]{:S(2)}, u32[]{:S(2)}) collective-permute-start(bf16[256,1024]{1,0:T(8,128)(2,1)S(1)} %get-tuple-element.51), channel_id=1, source_target_pairs={{0,1},{1,0},{2,3},{3,2},{4,5},{5,4},{6,7},{7,6},{8,9},{9,8},{10,11... | collective-permute-start | bytes 1572872 | tf_op jit(solution)/shard_map/ppermute | solution.py:437
  81.7 2.2 %collective-permute-start.16 = (bf16[256,1024]{1,0:T(8,128)(2,1)S(1)}, bf16[256,1024]{1,0:T(8,128)(2,1)S(1)}, u32[]{:S(2)}, u32[]{:S(2)}) collective-permute-start(bf16[256,1024]{1,0:T(8,128)(2,1)S(1)} %get-tuple-element.53), channel_id=1, source_target_pairs={{0,1},{1,0},{2,3},{3,2},{4,5},{5,4},{6,7},{7,6},{8,9},{9,8},{10,11... | collective-permute-start | bytes 1572872 | tf_op jit(solution)/shard_map/ppermute | solution.py:437
  82.4 9.2 %collective-permute-start.15 = (bf16[128,1024]{1,0:T(8,128)(2,1)S(1)}, bf16[128,1024]{1,0:T(8,128)(2,1)S(1)}, u32[]{:S(2)}, u32[]{:S(2)}) collective-permute-start(bf16[128,1024]{1,0:T(8,128)(2,1)S(1)} %get-tuple-element.59), channel_id=1, source_target_pairs={{0,2},{1,3},{2,0},{3,1},{4,6},{5,7},{6,4},{7,5},{8,10},{9,11},{10,... | collective-permute-start | bytes 786440 | tf_op jit(solution)/shard_map/ppermute | solution.py:437
  84.1 12.2 %collective-permute-start.17 = (bf16[128,1024]{1,0:T(8,128)(2,1)S(1)}, bf16[128,1024]{1,0:T(8,128)(2,1)S(1)}, u32[]{:S(2)}, u32[]{:S(2)}) collective-permute-start(bf16[128,1024]{1,0:T(8,128)(2,1)S(1)} %get-tuple-element.61), channel_id=1, source_target_pairs={{0,2},{1,3},{2,0},{3,1},{4,6},{5,7},{6,4},{7,5},{8,10},{9,11},{10,... | collective-permute-start | bytes 786440 | tf_op jit(solution)/shard_map/ppermute | solution.py:437
  85.5 6.7 %collective-permute-start.18 = (bf16[128,512]{1,0:T(8,128)(2,1)S(1)}, bf16[128,512]{1,0:T(8,128)(2,1)S(1)}, u32[]{:S(2)}, u32[]{:S(2)}) collective-permute-start(bf16[128,512]{1,0:T(8,128)(2,1)S(1)} %shard_map.89), channel_id=1, source_target_pairs={{0,4},{4,0},{8,12},{12,8},{16,20},{20,16},{24,28},{28,24},{1,5},{5... | collective-permute-start | bytes 393224 | tf_op jit(solution)/shard_map/ppermute | solution.py:446
  91.7 7.1 %collective-permute-start.24 = (bf16[128,1024]{1,0:T(8,128)(2,1)S(1)}, bf16[128,1024]{1,0:T(8,128)(2,1)S(1)}, u32[]{:S(2)}, u32[]{:S(2)}) collective-permute-start(bf16[128,1024]{1,0:T(8,128)(2,1)S(1)} %shard_map.93), channel_id=1, source_target_pairs={{0,4},{4,0},{8,12},{12,8},{16,20},{20,16},{24,28},{28,24},{1,5},{5... | collective-permute-start | bytes 786440 | tf_op jit(solution)/shard_map/ppermute | solution.py:446
  92.3 6.4 %copy-start.9 = (bf16[128,512]{1,0:T(8,128)(2,1)}, bf16[128,512]{1,0:T(8,128)(2,1)S(1)}, u32[]{:S(2)}) copy-start(bf16[128,512]{1,0:T(8,128)(2,1)S(1)} %collective-permute-done.18.refs_1_) | copy-start | bytes 393220
  98.7 1.6 %collective-permute-start.21 = (bf16[256,512]{1,0:T(8,128)(2,1)S(1)}, bf16[256,512]{1,0:T(8,128)(2,1)S(1)}, u32[]{:S(2)}, u32[]{:S(2)}) collective-permute-start(bf16[256,512]{1,0:T(8,128)(2,1)S(1)} %get-tuple-element.66), channel_id=1, source_target_pairs={{0,1},{1,0},{2,3},{3,2},{4,5},{5,4},{6,7},{7,6},{8,9},{9,8},{10,11... | collective-permute-start | bytes 786440 | tf_op jit(solution)/shard_map/ppermute | solution.py:437
  99.5 2.4 %collective-permute-start.25 = (bf16[256,512]{1,0:T(8,128)(2,1)S(1)}, bf16[256,512]{1,0:T(8,128)(2,1)S(1)}, u32[]{:S(2)}, u32[]{:S(2)}) collective-permute-start(bf16[256,512]{1,0:T(8,128)(2,1)S(1)} %get-tuple-element.72), channel_id=1, source_target_pairs={{0,1},{1,0},{2,3},{3,2},{4,5},{5,4},{6,7},{7,6},{8,9},{9,8},{10,11... | collective-permute-start | bytes 786440 | tf_op jit(solution)/shard_map/ppermute | solution.py:437
  100.3 6.4 %collective-permute-start.22 = (bf16[128,512]{1,0:T(8,128)(2,1)S(1)}, bf16[128,512]{1,0:T(8,128)(2,1)S(1)}, u32[]{:S(2)}, u32[]{:S(2)}) collective-permute-start(bf16[128,512]{1,0:T(8,128)(2,1)S(1)} %get-tuple-element.68), channel_id=1, source_target_pairs={{0,2},{1,3},{2,0},{3,1},{4,6},{5,7},{6,4},{7,5},{8,10},{9,11},{10,... | collective-permute-start | bytes 393224 | tf_op jit(solution)/shard_map/ppermute | solution.py:437
  102.0 8.3 %collective-permute-start.26 = (bf16[128,512]{1,0:T(8,128)(2,1)S(1)}, bf16[128,512]{1,0:T(8,128)(2,1)S(1)}, u32[]{:S(2)}, u32[]{:S(2)}) collective-permute-start(bf16[128,512]{1,0:T(8,128)(2,1)S(1)} %get-tuple-element.74), channel_id=1, source_target_pairs={{0,2},{1,3},{2,0},{3,1},{4,6},{5,7},{6,4},{7,5},{8,10},{9,11},{10,... | collective-permute-start | bytes 393224 | tf_op jit(solution)/shard_map/ppermute | solution.py:437
  106.8 5.0 %collective-permute-start.23 = (bf16[128,512]{1,0:T(8,128)(2,1)S(1)}, bf16[128,512]{1,0:T(8,128)(2,1)S(1)}, u32[]{:S(2)}, u32[]{:S(2)}) collective-permute-start(bf16[128,512]{1,0:T(8,128)(2,1)S(1)} %shard_map.92), channel_id=1, source_target_pairs={{0,4},{4,0},{8,12},{12,8},{16,20},{20,16},{24,28},{28,24},{1,5},{5... | collective-permute-start | bytes 393224 | tf_op jit(solution)/shard_map/ppermute | solution.py:446
  107.5 0.9 copy-start.10
